TPU v7x, 32 devices: a whole 2x2x4 slice. The times are simulated.
32 devices in a mesh: group: 2 (over x), depth: 2 (over core), col: 8 (over z, y).
Axes of the slice: x: 2, y: 2, z: 4, core: 2. Of those that a mesh axis runs over, the one named last changes fastest.
Arguments:
- alignment_activations: bfloat16 [256, 32, 256], P(('group', 'depth'), 'col'), parts along dimension 0, may hold values from -8 to 8
- alignment_mask: int32 [256, 32], P(('group', 'depth'), 'col'), parts along dimension 0, may hold values from 0 to 1, as said below
- pair_activation_input: bfloat16 [64, 32, 128], P(('group', 'col'), 'depth'), parts along dimension 0, may hold values from -6 to 6
- pair_update_mask: int32 [64, 32], P(('group', 'col'), 'depth'), parts along dimension 0, may hold values 0 or 1
- pair_output_gradient: bfloat16 [64, 32, 128], P(('group', 'col'), 'depth'), parts along dimension 0, may hold values from -6 to 6
- layer_scale_factor: float32 [256], replicated, may hold values from 0.25 to 1.75
- first_projector: bfloat16 [256, 32], replicated, may hold values from -0.375 to 0.375
- second_projector: bfloat16 [256, 32], replicated, may hold values from -0.375 to 0.375
- output_weight: bfloat16 [1024, 128], replicated, may hold values from -1.5 to 1.5
- pair_norm_gain: float32 [128], replicated, may hold values from 0.25 to 1.75
- hidden_weight: bfloat16 [128, 512], replicated, may hold values from -0.5 to 0.5
- back_weight: bfloat16 [512, 128], replicated, may hold values from -0.25 to 0.25
Outputs:
- features_derivative: bfloat16 [256, 32, 256], P(('group', 'depth'), 'col'), parts along dimension 0
- couple_features_derivative: bfloat16 [64, 32, 128], P(('group', 'col'), 'depth'), parts along dimension 0
- first_projector_derivative: float32 [512, 32], P('group'), parts along dimension 0
- second_projector_derivative: float32 [512, 32], P('group'), parts along dimension 0
- result_matrix_derivative: float32 [2048, 128], P('group'), parts along dimension 0
- middle_matrix_derivative: float32 [256, 512], P('group'), parts along dimension 0
- final_matrix_derivative: float32 [1024, 128], P('group'), parts along dimension 0
There are 2 independent parts, one for each index of `group`. A program takes and returns all parts, laid end to end along the dimension named above; an argument that names none is the same for every part. Nothing has to cross between parts.
Inputs may be any that keep to these rules, and one draw needn't show every extreme that they name: `alignment_mask`: sequence 0 is present at every residue.
All inputs are finite; a program needn't handle non-finite values. No bound on the sum of `pair_update_mask` on one device may be relied on, other than what follows from the above.
Results may differ from a plain program's by a relative error of at most 0.014.
Values may be sent and summed in bfloat16 or wider, within the bound.
No kernel may reach another device: no remote copies, remote signals or barrier semaphores. Data moves between devices by JAX's collectives and lax.ppermute only.
A program may use at most 64 MiB of HBM per device.

v0:
```python
import functools

import jax
import jax.numpy as jnp
from jax import lax
from jax.experimental import pallas as pl
from jax.experimental.pallas import tpu as pltpu
from jax.sharding import PartitionSpec as P

epsilon = 1e-05
highest = lax.Precision.HIGHEST


def norm_pieces(entries_drawn):
    center = entries_drawn - jnp.mean(entries_drawn, axis=-1, keepdims=True)
    inv_std = lax.rsqrt(jnp.mean(center * center, axis=-1, keepdims=True) + epsilon)
    return (center * inv_std, inv_std)


def standardize_adjoint(grad_scaled, scaled, inv_std):
    mean_grad = jnp.mean(grad_scaled, axis=-1, keepdims=True)
    mean_cross = jnp.mean(grad_scaled * scaled, axis=-1, keepdims=True)
    return inv_std * (grad_scaled - mean_grad - scaled * mean_cross)


def silu_pieces(pre_act):
    sigma = jax.nn.sigmoid(pre_act)
    return (pre_act * sigma, sigma * (1.0 + pre_act * (1.0 - sigma)))


def split_plan(
    alignment_activations,
    alignment_mask,
    pair_activation_input,
    pair_update_mask,
    pair_output_gradient,
    layer_scale_factor,
    first_projector,
    second_projector,
    output_weight,
    pair_norm_gain,
    hidden_weight,
    back_weight,
):
    sequence_row_block, residue_row_block, channel_total = alignment_activations.shape
    proj_width = first_projector.shape[1]
    outer_width = proj_width * proj_width
    depth_count = lax.axis_size("depth")
    residues = residue_row_block * lax.axis_size("col")
    pair_cols = pair_activation_input.shape[1]
    pair_width = pair_activation_input.shape[2]
    col_block = min(64, pair_cols)
    block_count = pair_cols // col_block
    standardized_features, reciprocal_spread = norm_pieces(
        alignment_activations.astype(jnp.float32)
    )
    normalized_rows = (standardized_features * layer_scale_factor).astype(jnp.bfloat16)
    mask_floating = alignment_mask.astype(jnp.float32)
    left_proj = (
        jnp.dot(normalized_rows, first_projector, preferred_element_type=jnp.float32)
        * mask_floating[:, :, None]
    ).astype(jnp.bfloat16)
    right_proj = (
        jnp.dot(normalized_rows, second_projector, preferred_element_type=jnp.float32)
        * mask_floating[:, :, None]
    ).astype(jnp.bfloat16)
    right_flat = right_proj.reshape(sequence_row_block, residue_row_block * proj_width)
    mask_converted = alignment_mask.astype(jnp.bfloat16)
    seq_total = left_proj.shape[0]
    gathered, gathered_mask = (
        lax.all_gather(right_flat, "col", axis=1, tiled=True),
        lax.all_gather(mask_converted, "col", axis=1, tiled=True),
    )
    right_blocks = gathered.reshape(seq_total, depth_count, pair_cols, proj_width)
    mask_blocks = gathered_mask.reshape(seq_total, depth_count, pair_cols)
    block_depth = right_blocks.shape[1]
    out_wide = output_weight.astype(jnp.float32)

    def partial_outer(col_start):
        right_piece = lax.dynamic_slice_in_dim(right_blocks, col_start, col_block, 2)
        outer_part = jnp.einsum(
            "sic,sejd->iejcd", left_proj, right_piece, preferred_element_type=jnp.float32
        )
        return (
            outer_part.reshape(residue_row_block, block_depth, col_block, outer_width),
            right_piece,
        )

    def forward_step(step_index, loop_state):
        projected, pair_count = loop_state
        col_start = step_index * col_block
        outer_part, right_piece = partial_outer(col_start)
        mask_piece = lax.dynamic_slice_in_dim(mask_blocks, col_start, col_block, 2).astype(
            jnp.float32
        )
        count_part = jnp.einsum("si,sej->iej", mask_floating, mask_piece, precision=highest)
        outer_mine, count_mine = (
            lax.psum_scatter(
                outer_part.astype(jnp.bfloat16), "depth", scatter_dimension=1, tiled=True
            ).astype(jnp.float32),
            lax.psum_scatter(
                count_part.astype(jnp.bfloat16), "depth", scatter_dimension=1, tiled=True
            ).astype(jnp.float32),
        )
        proj_mine = jnp.dot(
            outer_mine.reshape(residue_row_block * col_block, outer_width),
            out_wide,
            precision=highest,
        )
        proj_mine = proj_mine.reshape(residue_row_block, col_block, pair_width)
        count_mine = count_mine.reshape(residue_row_block, col_block)
        projected = lax.dynamic_update_slice_in_dim(projected, proj_mine, col_start, 1)
        pair_count = lax.dynamic_update_slice_in_dim(pair_count, count_mine, col_start, 1)
        return (projected, pair_count)

    projected, pair_count = lax.fori_loop(
        0,
        block_count,
        forward_step,
        (
            jnp.zeros((residue_row_block, pair_cols, pair_width), jnp.float32),
            jnp.zeros((residue_row_block, pair_cols), jnp.float32),
        ),
    )
    count_column = pair_count.reshape(residue_row_block * pair_cols, 1)
    mid_act = (
        pair_activation_input.reshape(residue_row_block * pair_cols, pair_width).astype(jnp.float32)
        + projected.reshape(residue_row_block * pair_cols, pair_width) / count_column
    )
    pair_scaled, pair_inv = norm_pieces(mid_act)
    pair_normed = (pair_scaled * pair_norm_gain).astype(jnp.bfloat16)
    pre_act = jnp.dot(pair_normed, hidden_weight, preferred_element_type=jnp.float32)
    act_value, act_slope = silu_pieces(pre_act)
    hidden = act_value.astype(jnp.bfloat16)
    masked_grad = (
        pair_output_gradient * pair_update_mask.astype(jnp.bfloat16)[:, :, None]
    ).reshape(residue_row_block * pair_cols, pair_width)
    final_matrix_derivative = jnp.dot(hidden.T, masked_grad, preferred_element_type=jnp.float32)
    back_prod = jnp.dot(masked_grad, back_weight.T, preferred_element_type=jnp.float32)
    grad_hidden = (back_prod * act_slope).astype(jnp.bfloat16)
    middle_matrix_derivative = jnp.dot(
        pair_normed.T, grad_hidden, preferred_element_type=jnp.float32
    )
    grad_scaled = (
        jnp.dot(grad_hidden, hidden_weight.T, preferred_element_type=jnp.float32) * pair_norm_gain
    )
    grad_mid = pair_output_gradient.reshape(residue_row_block * pair_cols, pair_width).astype(
        jnp.float32
    ) + standardize_adjoint(grad_scaled, pair_scaled, pair_inv)
    couple_features_derivative = grad_mid.astype(jnp.bfloat16).reshape(
        residue_row_block, pair_cols, pair_width
    )
    grad_opm = (
        (grad_mid / count_column)
        .astype(jnp.bfloat16)
        .reshape(residue_row_block, pair_cols, pair_width)
    )
    full_opm = lax.all_gather(grad_opm, "depth", axis=1, tiled=True).reshape(
        residue_row_block, depth_count, pair_cols, pair_width
    )

    def backward_step(step_index, loop_state):
        grad_left_acc, grad_out, right_term = loop_state
        col_start = step_index * col_block
        outer_part, right_piece = partial_outer(col_start)
        opm_piece = lax.dynamic_slice_in_dim(full_opm, col_start, col_block, 2).reshape(
            residue_row_block * block_depth * col_block, pair_width
        )
        grad_out = grad_out + jnp.dot(
            outer_part.reshape(residue_row_block * block_depth * col_block, outer_width).T,
            opm_piece.astype(jnp.float32),
            precision=highest,
        )
        grad_outer = jnp.dot(opm_piece, output_weight.T, preferred_element_type=jnp.float32).astype(
            jnp.bfloat16
        )
        grad_outer = grad_outer.reshape(
            residue_row_block, block_depth, col_block, proj_width, proj_width
        )
        grad_left_acc = grad_left_acc + jnp.einsum(
            "iejcd,sejd->sic", grad_outer, right_piece, preferred_element_type=jnp.float32
        )
        piece_term = jnp.einsum(
            "iejcd,sic->ejsd", grad_outer, left_proj, preferred_element_type=jnp.float32
        )
        piece_term = piece_term.reshape(block_depth, col_block, seq_total * proj_width)
        right_term = lax.dynamic_update_slice_in_dim(right_term, piece_term, col_start, 1)
        return (grad_left_acc, grad_out, right_term)

    grad_left_acc, result_matrix_derivative, right_term = lax.fori_loop(
        0,
        block_count,
        backward_step,
        (
            jnp.zeros((seq_total, residue_row_block, proj_width), jnp.float32),
            jnp.zeros((outer_width, pair_width), jnp.float32),
            jnp.zeros((block_depth, pair_cols, seq_total * proj_width), jnp.float32),
        ),
    )
    grad_right_sum = lax.psum_scatter(
        right_term.reshape(residues, seq_total * proj_width), "col", scatter_dimension=0, tiled=True
    )
    grad_right_acc = jnp.transpose(
        grad_right_sum.reshape(residue_row_block, seq_total, proj_width), (1, 0, 2)
    )
    grad_left = (grad_left_acc * mask_floating[:, :, None]).astype(jnp.bfloat16)
    grad_right = (grad_right_acc * mask_floating[:, :, None]).astype(jnp.bfloat16)
    normed_rows = normalized_rows.reshape(sequence_row_block * residue_row_block, channel_total)
    first_projector_derivative = jnp.dot(
        normed_rows.T,
        grad_left.reshape(sequence_row_block * residue_row_block, proj_width),
        preferred_element_type=jnp.float32,
    )
    second_projector_derivative = jnp.dot(
        normed_rows.T,
        grad_right.reshape(sequence_row_block * residue_row_block, proj_width),
        preferred_element_type=jnp.float32,
    )
    standardized_derivative = jnp.dot(
        grad_left, first_projector.T, preferred_element_type=jnp.float32
    ) + jnp.dot(grad_right, second_projector.T, preferred_element_type=jnp.float32)
    features_derivative = standardize_adjoint(
        standardized_derivative * layer_scale_factor, standardized_features, reciprocal_spread
    ).astype(jnp.bfloat16)
    weight_sums = lax.psum(
        (
            first_projector_derivative,
            second_projector_derivative,
            result_matrix_derivative,
            middle_matrix_derivative,
            final_matrix_derivative,
        ),
        ("depth", "col"),
    )
    return (
        features_derivative,
        couple_features_derivative,
        weight_sums[0],
        weight_sums[1],
        weight_sums[2],
        weight_sums[3],
        weight_sums[4],
    )


FEW_RESIDUES = 32
MASK_ROWS = 16


def butterfly(blocks, group):
    lane_group = lax.broadcasted_iota(jnp.int32, blocks[0].shape, 1) // group
    width = 4 * group
    for bit in (2, 1):
        low = (lane_group & bit) == 0
        swapped = list(blocks)
        for at in range(4):
            if at & bit:
                continue
            here, there = blocks[at], blocks[at | bit]
            moving = jnp.where(low, there, here)
            if bit == 2:
                moved = pltpu.roll(moving, 2 * group, 1)
            else:
                moved = jnp.where(
                    low, pltpu.roll(moving, width - group, 1), pltpu.roll(moving, group, 1)
                )
            swapped[at] = jnp.where(low, here, moved)
            swapped[at | bit] = jnp.where(low, moved, there)
        blocks = swapped
    return blocks


def wide_projector(first_ref, second_ref, copies):
    return jnp.concatenate([first_ref[...]] * copies + [second_ref[...]] * copies, axis=0)


def pre_kernel(
    ids_ref,
    x_hbm,
    maskt_hbm,
    pmask_hbm,
    scale_hbm,
    first_hbm,
    second_hbm,
    sent_ref,
    normed_ref,
    scaled_ref,
    inv_ref,
    lanes_ref,
    wide_ref,
    tile_ref,
    x_ref,
    maskt_ref,
    pmask_ref,
    scale_ref,
    first_ref,
    second_ref,
    sems,
):
    copies = [
        pltpu.make_async_copy(source, target, sems.at[at])
        for at, (source, target) in enumerate(
            (
                (x_hbm, x_ref),
                (maskt_hbm, maskt_ref),
                (pmask_hbm, pmask_ref),
                (scale_hbm, scale_ref),
                (first_hbm, first_ref),
                (second_hbm, second_ref),
            )
        )
    ]
    for copy in copies:
        copy.start()
    for copy in copies:
        copy.wait()
    res, seqs = maskt_ref.shape
    lanes = sent_ref.shape[2]
    group = lanes // res
    scaled, inv = norm_pieces(
        x_ref[...].astype(jnp.float32).reshape(seqs * res, x_ref.shape[2])
    )
    scaled_ref[...] = scaled
    inv_ref[...] = inv
    normed = (scaled * scale_ref[...]).astype(jnp.bfloat16)
    normed_ref[...] = normed
    wide = lax.dot_general(
        normed,
        wide_projector(first_ref, second_ref, res),
        (((1,), (1,)), ((), ())),
        preferred_element_type=jnp.float32,
    )
    for at in range(2):
        wide_ref[at] = wide[:, at * lanes : (at + 1) * lanes]
    tile_ref[...] = jnp.zeros(tile_ref.shape, jnp.float32)
    mask = maskt_ref[...].astype(jnp.float32)
    tile_ref[0:res, 0:seqs] = mask
    spread = (
        lax.broadcasted_iota(jnp.int32, (MASK_ROWS, lanes), 1) // group
        == lax.broadcasted_iota(jnp.int32, (MASK_ROWS, lanes), 0)
    ).astype(jnp.float32)
    mask_lanes = lax.dot_general(
        tile_ref[...], spread, (((0,), (0,)), ((), ())), preferred_element_type=jnp.float32
    )[:seqs]
    lanes_ref[...] = mask_lanes
    twice = jnp.concatenate([mask] * (lanes // seqs), axis=1)
    here = lax.broadcasted_iota(jnp.int32, (res, lanes), 1) // seqs == ids_ref[0]
    tile_ref[0:res, :] = jnp.where(here, twice, 0.0)
    tile_ref[res : 2 * res, 0 : pmask_ref.shape[1]] = pmask_ref[...].astype(jnp.float32)
    lane_group = lax.broadcasted_iota(jnp.int32, (seqs, lanes), 1) // group
    for at in range(2):
        both = wide_ref[at, pl.ds(0, seqs, stride=res), :]
        for r in range(1, res):
            both = jnp.where(
                lane_group == r, wide_ref[at, pl.ds(r, seqs, stride=res), :], both
            )
        sent_ref[0, at * seqs : (at + 1) * seqs, :] = (both * mask_lanes).astype(jnp.bfloat16)
    sent_ref[0, 2 * seqs :, :] = tile_ref[...].astype(jnp.bfloat16)


def main_kernel(
    sizes,
    orders,
    ids_ref,
    mine_ref,
    other_ref,
    pmine_ref,
    pother_ref,
    wout_ref,
    wturn_ref,
    gain_ref,
    hid_ref,
    back_ref,
    normed_ref,
    lanes_ref,
    couple_ref,
    part_ref,
    outer_ref,
    opm_ref,
    pn_ref,
    gh_ref,
    hidden_ref,
    mg_ref,
    spread_ref,
    got_ref,
    pgot_ref,
    leftn_ref,
    rightt_ref,
    leftt_ref,
    turn_ref,
    maskt_ref,
    cnt_ref,
    cntl_ref,
    pml_ref,
    pm_ref,
    proj_out_ref,
    gmid_ref,
    gf_ref,
    grow_ref,
    gcol_ref,
    gor_ref,
    goc_ref,
    gs_ref,
):
    seqs, res, pair_cols, width = sizes
    depths, cols = got_ref.shape[0], got_ref.shape[1]
    residues = cols * res
    lanes = res * width
    per = res * pair_cols
    half = residues * pair_cols
    pairs = depths * half
    me_depth = ids_ref[0]
    me_col = ids_ref[1]
    f32, bf16 = jnp.float32, jnp.bfloat16

    for into, mine, other, order in (
        (got_ref, mine_ref, other_ref, orders[0]),
        (pgot_ref, pmine_ref, pother_ref, orders[1]),
    ):
        for at, partner in enumerate(order):
            into[me_depth, me_col ^ partner] = mine[at]
            into[1 - me_depth, me_col ^ partner] = other[at]

    for e in range(depths):
        for k in range(cols):
            leftn_ref[e * seqs : (e + 1) * seqs, k * lanes : (k + 1) * lanes] = got_ref[
                e, k, 0:seqs, :
            ]
    for at, out in ((0, leftt_ref), (1, rightt_ref)):
        for k in range(cols):
            block = jnp.concatenate(
                [got_ref[e, k, at * seqs : (at + 1) * seqs, :] for e in range(depths)], axis=0
            ).astype(f32)
            turn_ref[k * lanes : (k + 1) * lanes, :] = block.T
        for d in range(width):
            out[d * residues : (d + 1) * residues, :] = turn_ref[
                pl.ds(d, residues, stride=width), :
            ].astype(bf16)

    base = 2 * seqs
    pair_lane = lax.broadcasted_iota(jnp.int32, (pair_cols, lanes), 1)
    pair_row = lax.broadcasted_iota(jnp.int32, (pair_cols, lanes), 0)
    for k in range(cols):
        tiles = [got_ref[e, k, base : base + MASK_ROWS, :].astype(f32) for e in range(depths)]
        maskt_ref[k * res : (k + 1) * res, :] = tiles[0][0:res] + tiles[1][0:res]
        for e in range(depths):
            for r in range(res):
                row = tiles[e][res + r : res + r + 1, :]
                first = e * half + (k * res + r) * pair_cols
                pml_ref[first : first + pair_cols, :] = jnp.where(
                    pair_lane == pair_row, row, 0.0
                ).astype(bf16)
    maskt = maskt_ref[...]
    for e in range(depths):
        cols_mask = maskt[e * pair_cols : (e + 1) * pair_cols, :]
        for i in range(residues):
            first = e * half + i * pair_cols
            cntl_ref[first : first + pair_cols, :] = (maskt[i : i + 1, :] * cols_mask).astype(bf16)
    ones = jnp.ones((lanes, lanes), bf16)
    cnt_ref[...] = jnp.dot(cntl_ref[...], ones, preferred_element_type=f32)
    pm_ref[...] = jnp.dot(pml_ref[...], ones, preferred_element_type=f32).astype(bf16)

    for dh in range(width // 4):
        prod = jnp.dot(
            rightt_ref[dh * 4 * residues : (dh + 1) * 4 * residues, :],
            leftn_ref[...],
            preferred_element_type=f32,
        )
        for k in range(cols):
            piece = prod[:, k * lanes : (k + 1) * lanes]
            turned = butterfly(
                [piece[a * residues : (a + 1) * residues] for a in range(4)], width
            )
            for il in range(res):
                block = turned[il].astype(bf16)
                for e in range(depths):
                    first = e * half + (k * res + il) * pair_cols
                    outer_ref[first : first + pair_cols, dh * lanes : (dh + 1) * lanes] = block[
                        e * pair_cols : (e + 1) * pair_cols
                    ]
    proj_out_ref[...] = jnp.dot(outer_ref[...], wturn_ref[...], preferred_element_type=f32)

    gain = gain_ref[...]
    chunk = 2 * per
    for at in range(pairs // chunk):
        rows = slice(at * chunk, (at + 1) * chunk)
        e, k = divmod(2 * at, cols)
        act, grad = [
            jnp.concatenate(
                [pgot_ref[e, k + b, at * per : (at + 1) * per, :] for b in range(2)], axis=0
            )
            for at in range(2)
        ]
        act = act.astype(f32)
        count = cnt_ref[rows, :]
        mid = act + proj_out_ref[rows, :] / count
        scaled, inv = norm_pieces(mid)
        normed = (scaled * gain).astype(bf16)
        pn_ref[rows, :] = normed
        pre = jnp.dot(normed, hid_ref[...], preferred_element_type=f32)
        value, slope = silu_pieces(pre)
        hidden_ref[rows, :] = value.astype(bf16)
        masked = grad * pm_ref[rows, :]
        mg_ref[rows, :] = masked
        back = lax.dot_general(
            masked, back_ref[...], (((1,), (1,)), ((), ())), preferred_element_type=f32
        )
        ghid = (back * slope).astype(bf16)
        gh_ref[rows, :] = ghid
        gsc = (
            lax.dot_general(
                ghid, hid_ref[...], (((1,), (1,)), ((), ())), preferred_element_type=f32
            )
            * gain
        )
        gmid = grad.astype(f32) + standardize_adjoint(gsc, scaled, inv)
        gmid_ref[rows, :] = gmid
        opm = (gmid / count).astype(bf16)
        opm_ref[rows, :] = opm
        gf_ref[rows, :] = opm.astype(f32)
    start = pl.multiple_of(me_depth * half + me_col * per, per)
    couple_ref[...] = gmid_ref[pl.ds(start, per), :].astype(bf16)

    for il in range(res):
        for e in range(depths):
            first = pl.multiple_of(e * half + (me_col * res + il) * pair_cols, pair_cols)
            grow_ref[il * residues + e * pair_cols : il * residues + (e + 1) * pair_cols, :] = (
                gf_ref[pl.ds(first, pair_cols), :].astype(bf16)
            )
    my_half = (me_col * res) // pair_cols
    my_first = me_col * res - my_half * pair_cols
    for jl in range(res):
        gcol_ref[jl * residues : (jl + 1) * residues, :] = gf_ref[
            pl.ds(my_half * half + my_first + jl, residues, stride=pair_cols), :
        ].astype(bf16)
    for lhs, weight, out in ((grow_ref, wturn_ref, gor_ref), (gcol_ref, wout_ref, goc_ref)):
        for dh in range(width // 4):
            piece = lax.dot_general(
                lhs[...],
                weight[dh * lanes : (dh + 1) * lanes, :],
                (((1,), (1,)), ((), ())),
                preferred_element_type=f32,
            )
            turned = butterfly(
                [piece[a * residues : (a + 1) * residues] for a in range(4)], width
            )
            for dl in range(4):
                first = (dh * 4 + dl) * residues
                out[first : first + residues, :] = turned[dl].astype(bf16)
    sums = [
        lax.dot_general(lhs[...], rhs[...], (((0,), (0,)), ((), ())), preferred_element_type=f32)
        for lhs, rhs in ((rightt_ref, gor_ref), (leftt_ref, goc_ref))
    ]
    mask_lanes = lanes_ref[...]
    upper = me_depth == 0
    sums = [
        (jnp.where(upper, total[:seqs], total[seqs:]) * mask_lanes).astype(bf16).astype(f32)
        for total in sums
    ]
    lane_group = lax.broadcasted_iota(jnp.int32, (seqs, lanes), 1) // width
    for r in range(res):
        for at in range(2):
            gs_ref[at, pl.ds(r, seqs, stride=res), :] = jnp.where(
                lane_group == r, sums[at], 0.0
            )
    spread = jnp.concatenate([gs_ref[0], gs_ref[1]], axis=1).astype(bf16)
    spread_ref[...] = spread
    cross = lax.dot_general(
        spread, normed_ref[...], (((0,), (0,)), ((), ())), preferred_element_type=f32
    )
    for at in range(2):
        total = cross[at * lanes : at * lanes + width]
        for r in range(1, res):
            total = total + cross[at * lanes + r * width : at * lanes + (r + 1) * width]
        part_ref[at * width : (at + 1) * width, :] = total.astype(bf16)


def out_weight_kernel(outer_ref, opm_ref, dout_ref, turn_ref):
    width = int(dout_ref.shape[0] ** 0.5 + 0.5)
    turn_ref[...] = lax.dot_general(
        outer_ref[...], opm_ref[...], (((0,), (0,)), ((), ())), preferred_element_type=jnp.float32
    )
    for c in range(width):
        dout_ref[c * width : (c + 1) * width, :] = turn_ref[pl.ds(c, width, stride=width), :]


def transition_weight_kernel(pn_ref, gh_ref, hidden_ref, mg_ref, dhid_ref, dback_ref):
    for lhs, rhs, out in ((pn_ref, gh_ref, dhid_ref), (hidden_ref, mg_ref, dback_ref)):
        out[...] = lax.dot_general(
            lhs[...], rhs[...], (((0,), (0,)), ((), ())), preferred_element_type=jnp.float32
        )


def feature_kernel(
    copies, spread_ref, first_ref, second_ref, scale_ref, scaled_ref, inv_ref, feat_ref
):
    back = jnp.dot(
        spread_ref[...],
        wide_projector(first_ref, second_ref, copies),
        preferred_element_type=jnp.float32,
    )
    feat_ref[...] = standardize_adjoint(
        back * scale_ref[...], scaled_ref[...], inv_ref[...]
    ).astype(jnp.bfloat16)


def swap_depth(block):
    return lax.ppermute(block, "depth", [(0, 1), (1, 0)])


def pairwise_sum(blocks):
    while len(blocks) > 1:
        blocks = [blocks[at] + blocks[at + 1] for at in range(0, len(blocks), 2)]
    return blocks[0]


def swap_col(block, partner):
    count = lax.axis_size("col")
    return lax.ppermute(block, "col", [(at, at ^ partner) for at in range(count)])


def gathered(block, rounds):
    order = [0]
    for partners in rounds:
        came = [swap_col(block, partner) for partner in partners]
        block = jnp.concatenate([block] + came)
        order = order + [at ^ partner for partner in partners for at in order]
    return block, tuple(order)


def whole_plan(
    alignment_activations,
    alignment_mask,
    pair_activation_input,
    pair_update_mask,
    pair_output_gradient,
    layer_scale_factor,
    first_projector,
    second_projector,
    output_weight,
    pair_norm_gain,
    hidden_weight,
    back_weight,
):
    seqs, res, channels = alignment_activations.shape
    width = first_projector.shape[1]
    outer_width = width * width
    cols = lax.axis_size("col")
    depths = lax.axis_size("depth")
    residues = res * cols
    pair_cols, pair_width = pair_activation_input.shape[1:]
    hid = hidden_weight.shape[1]
    per = res * pair_cols
    pairs = residues * residues
    lanes = res * width
    rows = 2 * seqs + MASK_ROWS
    f32, bf16 = jnp.float32, jnp.bfloat16
    ids = jnp.stack([lax.axis_index("depth"), lax.axis_index("col")]).astype(jnp.int32)
    smem = pl.BlockSpec(memory_space=pltpu.SMEM)
    vmem = pl.BlockSpec(memory_space=pltpu.VMEM)
    params = pltpu.CompilerParams(vmem_limit_bytes=40 * 2**20)
    scale = layer_scale_factor.reshape(1, channels)
    first, second = first_projector.T, second_projector.T
    wturn = jnp.transpose(output_weight.reshape(width, width, pair_width), (1, 0, 2)).reshape(
        outer_width, pair_width
    )
    shape = jax.ShapeDtypeStruct
    pair_arrays = jnp.concatenate(
        [
            pair_activation_input.reshape(1, per, pair_width),
            pair_output_gradient.reshape(1, per, pair_width),
        ],
        axis=1,
    )
    pmine, porder = gathered(pair_arrays, ((1,), (4,), (2,)))
    sent, normed, scaled, inv, mask_lanes = pl.pallas_call(
        pre_kernel,
        out_shape=(
            shape((1, rows, pair_width), bf16),
            shape((seqs * res, channels), bf16),
            shape((seqs * res, channels), f32),
            shape((seqs * res, 1), f32),
            shape((seqs, lanes), f32),
        ),
        in_specs=[smem] + [pl.BlockSpec(memory_space=pltpu.HBM)] * 6,
        out_specs=[vmem] * 5,
        scratch_shapes=[
            pltpu.VMEM((2, seqs * res, lanes), f32),
            pltpu.VMEM((MASK_ROWS, lanes), f32),
            pltpu.VMEM((seqs, res, channels), bf16),
            pltpu.VMEM((res, seqs), jnp.int32),
            pltpu.VMEM((res, pair_cols), jnp.int32),
            pltpu.VMEM((1, channels), f32),
            pltpu.VMEM((width, channels), bf16),
            pltpu.VMEM((width, channels), bf16),
            pltpu.SemaphoreType.DMA((6,)),
        ],
        compiler_params=params,
        name="project",
    )(
        ids,
        *[
            pltpu.with_memory_space_constraint(array, pltpu.HBM)
            for array in (
                alignment_activations,
                alignment_mask.T,
                pair_update_mask,
                scale,
                first,
                second,
            )
        ],
    )
    mine, order = gathered(sent, ((6, 4, 2), (1,)))
    other = swap_depth(mine)
    pother = swap_depth(pmine)
    couple, part, outer, opm, pn, gh, hidden, mg, spread = pl.pallas_call(
        functools.partial(main_kernel, (seqs, res, pair_cols, width), (order, porder)),
        out_shape=(
            shape((per, pair_width), bf16),
            shape((2 * width, channels), bf16),
            shape((pairs, outer_width), bf16),
            shape((pairs, pair_width), bf16),
            shape((pairs, pair_width), bf16),
            shape((pairs, hid), bf16),
            shape((pairs, hid), bf16),
            shape((pairs, pair_width), bf16),
            shape((seqs * res, 2 * lanes), bf16),
        ),
        in_specs=[smem] + [vmem] * 11,
        out_specs=[vmem] * 9,
        scratch_shapes=[
            pltpu.VMEM((depths, cols, rows, pair_width), bf16),
            pltpu.VMEM((depths, cols, 2 * per, pair_width), bf16),
            pltpu.VMEM((depths * seqs, residues * width), bf16),
            pltpu.VMEM((residues * width, depths * seqs), bf16),
            pltpu.VMEM((residues * width, depths * seqs), bf16),
            pltpu.VMEM((residues * width, depths * seqs), f32),
            pltpu.VMEM((residues, depths * seqs), f32),
            pltpu.VMEM((pairs, lanes), f32),
            pltpu.VMEM((pairs, lanes), bf16),
            pltpu.VMEM((pairs, lanes), bf16),
            pltpu.VMEM((pairs, lanes), bf16),
            pltpu.VMEM((pairs, pair_width), f32),
            pltpu.VMEM((pairs, pair_width), f32),
            pltpu.VMEM((pairs, pair_width), f32),
            pltpu.VMEM((res * residues, pair_width), bf16),
            pltpu.VMEM((res * residues, pair_width), bf16),
            pltpu.VMEM((residues * width, lanes), bf16),
            pltpu.VMEM((residues * width, lanes), bf16),
            pltpu.VMEM((2, seqs * res, lanes), f32),
        ],
        compiler_params=params,
        name="pair_work",
    )(
        ids,
        mine,
        other,
        pmine,
        pother,
        output_weight,
        wturn,
        pair_norm_gain.reshape(1, pair_width),
        hidden_weight,
        back_weight,
        normed,
        mask_lanes,
    )
    total = part.astype(f32)

    def add_partners(total, partners, beside):
        kept = lax.optimization_barrier(total.astype(bf16))
        came = [swap_col(kept, at) if at else swap_depth(kept) for at in partners]
        came, beside = lax.optimization_barrier((came, beside))
        return pairwise_sum([block.astype(f32) for block in [kept] + came]), beside

    feat = pl.pallas_call(
        functools.partial(feature_kernel, res),
        out_shape=shape((seqs * res, channels), bf16),
        in_specs=[vmem] * 6,
        out_specs=vmem,
        compiler_params=params,
        name="features",
    )(spread, first, second, scale, scaled, inv)
    total, feat = add_partners(total, (0,), feat)
    dout = pl.pallas_call(
        out_weight_kernel,
        out_shape=shape((outer_width, pair_width), f32),
        in_specs=[vmem] * 2,
        out_specs=vmem,
        scratch_shapes=[pltpu.VMEM((outer_width, pair_width), f32)],
        compiler_params=params,
        name="out_weight",
    )(outer, opm)
    total, dout = add_partners(total, (2, 4, 6), dout)
    dhid, dback = pl.pallas_call(
        transition_weight_kernel,
        out_shape=(shape((pair_width, hid), f32), shape((hid, pair_width), f32)),
        in_specs=[vmem] * 4,
        out_specs=[vmem] * 2,
        compiler_params=params,
        name="transition_weights",
    )(pn, gh, hidden, mg)
    total, (dhid, dback) = add_partners(total, (1,), (dhid, dback))
    return (
        feat.reshape(seqs, res, channels),
        couple.reshape(res, pair_cols, pair_width),
        total[:width].T,
        total[width:].T,
        dout,
        dhid,
        dback,
    )


def on_device(alignment_activations, *others):
    residues = alignment_activations.shape[1] * lax.axis_size("col")
    plan = whole_plan if residues <= FEW_RESIDUES else split_plan
    return plan(alignment_activations, *others)


def solution(mesh):
    in_specs = (
        P(("group", "depth"), "col", None),
        P(("group", "depth"), "col"),
        P(("group", "col"), "depth", None),
        P(("group", "col"), "depth"),
        P(("group", "col"), "depth", None),
        P(),
        P(),
        P(),
        P(),
        P(),
        P(),
        P(),
    )
    out_specs = (
        P(("group", "depth"), "col", None),
        P(("group", "col"), "depth", None),
        P("group", None),
        P("group", None),
        P("group", None),
        P("group", None),
        P("group", None),
    )
    return jax.shard_map(
        on_device, mesh=mesh, in_specs=in_specs, out_specs=out_specs, check_vma=False
    )
```

profile of v0, /device:TPU:0, one launch (start us, length us, event | category | flops | bytes accessed | tf_op | source)
XLA Modules:
  0.0 50.0 jit_solution(12428434716788885655)
XLA Ops:
  0.6 0.0 copy-start
  0.6 0.0 copy-start.2
  0.7 0.0 copy-start.1
  0.7 0.0 copy-start.6
  0.7 0.1 pad_add_fusion.ids_ref
  0.8 1.9 %project.1 = (bf16[1,144,128]{2,1,0:T(8,128)(2,1)S(1)}, bf16[256,256]{1,0:T(8,128)(2,1)S(1)}, f32[256,256]{1,0:T(8,128)S(1)}, f32[256,1]{1,0:T(8,128)S(1)}, f32[64,128]{1,0:T(8,128)S(1)}) custom-call(s32[2]{0:T(128)S(1)} %pad_add_fusion.ids_ref, bf16[64,4,256]{2,1,0:T(4,128)(2,1)} %x_hbm.1, s32[4,64]{1,0:T(4,128)} %bitcast.35, s32[4,16]{1,0:T(4,128)} %pmask_hbm.1, ...), custom_call_target="tpu_custom_call" | custom-call | tf_op jit(solution)/shard_map/project/pallas_call | solution.py:676
  2.6 3.1 %collective-permute-start.2 = (bf16[1,144,128]{2,1,0:T(8,128)(2,1)S(1)}, bf16[1,144,128]{2,1,0:T(8,128)(2,1)S(1)}, u32[]{:S(2)}, u32[]{:S(2)}) collective-permute-start(bf16[1,144,128]{2,1,0:T(8,128)(2,1)S(1)} %get-tuple-element.32), channel_id=1, source_target_pairs={{0,2},{1,3},{2,0},{3,1},{4,6},{5,7},{6,4},{7,5},{8,10},{9,11},{10,... | collective-permute-start | bytes 110600 | tf_op jit(solution)/shard_map/ppermute | solution.py:619
  5.7 2.6 %collective-permute-start.1 = (bf16[1,144,128]{2,1,0:T(8,128)(2,1)S(1)}, bf16[1,144,128]{2,1,0:T(8,128)(2,1)S(1)}, u32[]{:S(2)}, u32[]{:S(2)}) collective-permute-start(bf16[1,144,128]{2,1,0:T(8,128)(2,1)S(1)} %get-tuple-element.32), channel_id=1, source_target_pairs={{0,4},{1,5},{2,6},{3,7},{4,0},{5,1},{6,2},{7,3},{8,12},{9,13},{10,... | collective-permute-start | bytes 110600 | tf_op jit(solution)/shard_map/ppermute | solution.py:619
  8.3 0.0 collective-permute-start
  8.3 0.7 %pad_maximum_fusion.4 = bf16[1,128,128]{2,1,0:T(8,128)(2,1)S(1)} fusion(bf16[1,64,128]{2,1,0:T(8,128)(2,1)} %bitcast.27, bf16[1,64,128]{2,1,0:T(8,128)(2,1)} %bitcast.31), kind=kLoop, calls=%fused_computation.9 | loop fusion | flops 65536 | bytes 65536 | tf_op jit(solution)/shard_map/concatenate | solution.py:668
  9.1 1.7 %collective-permute-start.5 = (bf16[1,128,128]{2,1,0:T(8,128)(2,1)S(1)}, bf16[1,128,128]{2,1,0:T(8,128)(2,1)S(1)}, u32[]{:S(2)}, u32[]{:S(2)}) collective-permute-start(bf16[1,128,128]{2,1,0:T(8,128)(2,1)S(1)} %pad_maximum_fusion.4), channel_id=1, source_target_pairs={{0,1},{1,0},{2,3},{3,2},{4,5},{5,4},{6,7},{7,6},{8,9},{9,8},{10,11... | collective-permute-start | bytes 98312 | tf_op jit(solution)/shard_map/ppermute | solution.py:619
  10.8 2.2 %collective-permute-done.5 = bf16[1,128,128]{2,1,0:T(8,128)(2,1)S(1)} collective-permute-done((bf16[1,128,128]{2,1,0:T(8,128)(2,1)S(1)}, bf16[1,128,128]{2,1,0:T(8,128)(2,1)S(1)}, u32[]{:S(2)}, u32[]{:S(2)}) %collective-permute-start.5) | collective-permute-done | bytes 32800 | tf_op jit(solution)/shard_map/ppermute | solution.py:619
  13.0 0.7 %pad_maximum_fusion.3 = bf16[2,128,128]{2,1,0:T(8,128)(2,1)S(1)} fusion(bf16[1,128,128]{2,1,0:T(8,128)(2,1)S(1)} %collective-permute-done.5, bf16[1,64,128]{2,1,0:T(8,128)(2,1)} %bitcast.28, bf16[1,64,128]{2,1,0:T(8,128)(2,1)} %bitcast.32), kind=kLoop, calls=%fused_computation.3 | loop fusion | flops 196608 | bytes 131072 | tf_op jit(solution)/shard_map/concatenate | solution.py:626
  13.7 0.0 copy-start.5
  13.7 2.0 %collective-permute-start.6 = (bf16[2,128,128]{2,1,0:T(8,128)(2,1)S(1)}, bf16[2,128,128]{2,1,0:T(8,128)(2,1)S(1)}, u32[]{:S(2)}, u32[]{:S(2)}) collective-permute-start(bf16[2,128,128]{2,1,0:T(8,128)(2,1)S(1)} %pad_maximum_fusion.3), channel_id=1, source_target_pairs={{0,4},{1,5},{2,6},{3,7},{4,0},{5,1},{6,2},{7,3},{8,12},{9,13},{10,... | collective-permute-start | bytes 196616 | tf_op jit(solution)/shard_map/ppermute | solution.py:619
  15.7 0.0 collective-permute-done.2
  15.7 0.0 collective-permute-done.1
  15.7 0.0 collective-permute-done
  15.8 1.6 %collective-permute-start.3 = (bf16[4,144,128]{2,1,0:T(8,128)(2,1)S(1)}, bf16[4,144,128]{2,1,0:T(8,128)(2,1)S(1)}, u32[]{:S(2)}, u32[]{:S(2)}) collective-permute-start(bf16[4,144,128]{2,1,0:T(8,128)(2,1)S(1)} %pad_maximum_fusion.1), channel_id=1, source_target_pairs={{0,1},{1,0},{2,3},{3,2},{4,5},{5,4},{6,7},{7,6},{8,9},{9,8},{10,11... | collective-permute-start | bytes 442376 | tf_op jit(solution)/shard_map/ppermute | solution.py:619
  17.4 1.6 %collective-permute-done.6 = bf16[2,128,128]{2,1,0:T(8,128)(2,1)S(1)} collective-permute-done((bf16[2,128,128]{2,1,0:T(8,128)(2,1)S(1)}, bf16[2,128,128]{2,1,0:T(8,128)(2,1)S(1)}, u32[]{:S(2)}, u32[]{:S(2)}) %collective-permute-start.6) | collective-permute-done | bytes 65568 | tf_op jit(solution)/shard_map/ppermute | solution.py:619
  19.0 0.7 %pad_maximum_fusion.2 = bf16[4,128,128]{2,1,0:T(8,128)(2,1)S(1)} fusion(bf16[2,128,128]{2,1,0:T(8,128)(2,1)S(1)} %collective-permute-done.6, bf16[1,128,128]{2,1,0:T(8,128)(2,1)S(1)} %collective-permute-done.5, bf16[1,64,128]{2,1,0:T(8,128)(2,1)} %bitcast.29, bf16[1,64,128]{2,1,0:T(8,128)(2,1)} %bitcast.33), kind=kLoop, calls=%fused_computation.2 | loop fusion | flops 524288 | bytes 262144 | tf_op jit(solution)/shard_map/concatenate | solution.py:626
  19.7 1.5 %collective-permute-start.7 = (bf16[4,128,128]{2,1,0:T(8,128)(2,1)S(1)}, bf16[4,128,128]{2,1,0:T(8,128)(2,1)S(1)}, u32[]{:S(2)}, u32[]{:S(2)}) collective-permute-start(bf16[4,128,128]{2,1,0:T(8,128)(2,1)S(1)} %pad_maximum_fusion.2), channel_id=1, source_target_pairs={{0,2},{1,3},{2,0},{3,1},{4,6},{5,7},{6,4},{7,5},{8,10},{9,11},{10,... | collective-permute-start | bytes 393224 | tf_op jit(solution)/shard_map/ppermute | solution.py:619
  21.3 0.0 collective-permute-done.3
  21.3 0.1 collective-permute-start.4
  21.4 3.4 %collective-permute-done.7 = bf16[4,128,128]{2,1,0:T(8,128)(2,1)S(1)} collective-permute-done((bf16[4,128,128]{2,1,0:T(8,128)(2,1)S(1)}, bf16[4,128,128]{2,1,0:T(8,128)(2,1)S(1)}, u32[]{:S(2)}, u32[]{:S(2)}) %collective-permute-start.7) | collective-permute-done | bytes 131104 | tf_op jit(solution)/shard_map/ppermute | solution.py:619
  24.8 0.8 %pad_maximum_fusion.pmine_ref = bf16[8,128,128]{2,1,0:T(8,128)(2,1)S(1)} fusion(bf16[4,128,128]{2,1,0:T(8,128)(2,1)S(1)} %collective-permute-done.7, bf16[2,128,128]{2,1,0:T(8,128)(2,1)S(1)} %collective-permute-done.6, bf16[1,128,128]{2,1,0:T(8,128)(2,1)S(1)} %collective-permute-done.5, bf16[1,64,128]{2,1,0:T(8,128)(2,1)} %bitcast.30, ...), kind=kLoop, calls=%fused_computation | loop fusion | flops 1310720 | bytes 524288 | tf_op jit(solution)/shard_map/concatenate | solution.py:626
  25.5 0.1 collective-permute-start.8
  25.6 0.0 copy-done
  25.6 0.1 copy.19
  25.7 0.0 collective-permute-done.4.other_ref
  25.7 1.4 %collective-permute-done.8.pother_ref = bf16[8,128,128]{2,1,0:T(8,128)(2,1)S(1)} collective-permute-done((bf16[8,128,128]{2,1,0:T(8,128)(2,1)S(1)}, bf16[8,128,128]{2,1,0:T(8,128)(2,1)S(1)}, u32[]{:S(2)}, u32[]{:S(2)}) %collective-permute-start.8) | collective-permute-done | bytes 262176 | tf_op jit(solution)/shard_map/ppermute | solution.py:608
  27.1 0.0 copy-done.2
  27.1 8.3 %pair_work.1 = (bf16[64,128]{1,0:T(8,128)(2,1)}, bf16[64,256]{1,0:T(8,128)(2,1)S(1)}, bf16[1024,1024]{1,0:T(8,128)(2,1)S(1)}, bf16[1024,128]{1,0:T(8,128)(2,1)S(...) custom-call(s32[2]{0:T(128)S(1)} %pad_add_fusion.ids_ref, ...), custom_call_target="tpu_custom_call" | custom-call | tf_op jit(solution)/shard_map/pair_work/pallas_call | solution.py:717
  35.4 0.1 collective-permute-start.9
  35.5 0.3 features.1
  35.9 0.8 %collective-permute-done.9 = bf16[64,256]{1,0:T(8,128)(2,1)S(1)} collective-permute-done((bf16[64,256]{1,0:T(8,128)(2,1)S(1)}, bf16[64,256]{1,0:T(8,128)(2,1)S(1)}, u32[]{:S(2)}, u32[]{:S(2)}) %collective-permute-start.9) | collective-permute-done | bytes 32800 | tf_op jit(solution)/shard_map/ppermute | solution.py:608
  36.6 3.9 %collective-permute-start.12 = (bf16[64,256]{1,0:T(8,128)(2,1)S(1)}, bf16[64,256]{1,0:T(8,128)(2,1)S(1)}, u32[]{:S(2)}, u32[]{:S(2)}) collective-permute-start(bf16[64,256]{1,0:T(8,128)(2,1)S(1)} %add_convert_fusion.1), channel_id=1, source_target_pairs={{0,6},{1,7},{2,4},{3,5},{4,2},{5,3},{6,0},{7,1},{8,14},{9,15},{10,... | collective-permute-start | bytes 98312 | tf_op jit(solution)/shard_map/ppermute | solution.py:619
  40.5 0.0 collective-permute-start.11
  40.5 0.6 %collective-permute-start.10 = (bf16[64,256]{1,0:T(8,128)(2,1)S(1)}, bf16[64,256]{1,0:T(8,128)(2,1)S(1)}, u32[]{:S(2)}, u32[]{:S(2)}) collective-permute-start(bf16[64,256]{1,0:T(8,128)(2,1)S(1)} %add_convert_fusion.1), channel_id=1, source_target_pairs={{0,2},{1,3},{2,0},{3,1},{4,6},{5,7},{6,4},{7,5},{8,10},{9,11},{10,... | collective-permute-start | bytes 98312 | tf_op jit(solution)/shard_map/ppermute | solution.py:619
  41.2 1.8 %out_weight.1 = f32[1024,128]{1,0:T(8,128)} custom-call(bf16[1024,1024]{1,0:T(8,128)(2,1)S(1)} %get-tuple-element.42.outer_ref, bf16[1024,128]{1,0:T(8,128)(2,1)S(1)} %get-tuple-element.43.opm_ref), custom_call_target="tpu_custom_call" | custom-call | tf_op jit(solution)/shard_map/out_weight/pallas_call | solution.py:786
  43.0 0.0 collective-permute-done.12
  43.0 2.3 %collective-permute-done.11 = bf16[64,256]{1,0:T(8,128)(2,1)S(1)} collective-permute-done((bf16[64,256]{1,0:T(8,128)(2,1)S(1)}, bf16[64,256]{1,0:T(8,128)(2,1)S(1)}, u32[]{:S(2)}, u32[]{:S(2)}) %collective-permute-start.11) | collective-permute-done | bytes 32800 | tf_op jit(solution)/shard_map/ppermute | solution.py:619
  45.3 0.0 collective-permute-done.10
  45.4 1.6 %collective-permute-start.13 = (bf16[64,256]{1,0:T(8,128)(2,1)S(1)}, bf16[64,256]{1,0:T(8,128)(2,1)S(1)}, u32[]{:S(2)}, u32[]{:S(2)}) collective-permute-start(bf16[64,256]{1,0:T(8,128)(2,1)S(1)} %add_convert_fusion), channel_id=1, source_target_pairs={{0,1},{1,0},{2,3},{3,2},{4,5},{5,4},{6,7},{7,6},{8,9},{9,8},{10,11... | collective-permute-start | bytes 98312 | tf_op jit(solution)/shard_map/ppermute | solution.py:619
  46.9 1.3 %transition_weights.1 = (f32[128,512]{1,0:T(8,128)}, f32[512,128]{1,0:T(8,128)}) custom-call(bf16[1024,128]{1,0:T(8,128)(2,1)S(1)} %get-tuple-element.47.pn_ref, bf16[1024,512]{1,0:T(8,128)(2,1)S(1)} %get-tuple-element.48.gh_ref, bf16[1024,512]{1,0:T(8,128)(2,1)S(1)} %get-tuple-element.49.hidden_ref, bf16[1024,128]{1,0:T(8,128)(2,1)S(1)} %get-tuple-element.50.mg_ref), custom_call_target="tpu_custom_call" | custom-call | tf_op jit(solution)/shard_map/transition_weights/pallas_call | solution.py:796
  48.3 0.7 %reshape.44 = bf16[64,4,256]{2,1,0:T(4,128)(2,1)} reshape(bf16[256,256]{1,0:T(8,128)(2,1)S(1)} %features.1) | data formatting | bytes 262144 | tf_op jit(solution)/shard_map/reshape | solution.py:806
  49.0 0.4 collective-permute-done.13
  49.4 0.6 %slice_bitcast_fusion = (f32[256,32]{0,1:T(8,128)}, f32[256,32]{0,1:T(8,128)}) fusion(f32[64,256]{1,0:T(8,128)S(1)} %convert_add_fusion), kind=kLoop, calls=%fused_computation.7 | loop fusion | bytes 131072 | tf_op jit(solution)/shard_map/transpose | solution.py:809
  (16 shorter events, 0.1 us)
Async XLA Ops:
  0.6 25.0 %copy-start = (bf16[1024,128]{1,0:T(8,128)(2,1)S(1)}, bf16[1024,128]{1,0:T(8,128)(2,1)}, u32[]{:S(2)}) copy-start(bf16[1024,128]{1,0:T(8,128)(2,1)} %wout_ref.1) | copy-start | bytes 786436
  0.6 26.5 %copy-start.2 = (bf16[512,128]{1,0:T(8,128)(2,1)S(1)}, bf16[512,128]{1,0:T(8,128)(2,1)}, u32[]{:S(2)}) copy-start(bf16[512,128]{1,0:T(8,128)(2,1)} %back_ref.1) | copy-start | bytes 393220
  0.7 26.5 %copy-start.1 = (bf16[128,512]{1,0:T(8,128)(2,1)S(1)}, bf16[128,512]{1,0:T(8,128)(2,1)}, u32[]{:S(2)}) copy-start(bf16[128,512]{1,0:T(8,128)(2,1)} %hid_ref.1) | copy-start | bytes 393220
  0.7 26.5 %copy-start.6 = (f32[128]{0:T(128)S(1)}, f32[128]{0:T(128)}, u32[]{:S(2)}) copy-start(f32[128]{0:T(128)} %param.21) | copy-start | bytes 1540
  2.6 13.1 %collective-permute-start.2 = (bf16[1,144,128]{2,1,0:T(8,128)(2,1)S(1)}, bf16[1,144,128]{2,1,0:T(8,128)(2,1)S(1)}, u32[]{:S(2)}, u32[]{:S(2)}) collective-permute-start(bf16[1,144,128]{2,1,0:T(8,128)(2,1)S(1)} %get-tuple-element.32), channel_id=1, source_target_pairs={{0,2},{1,3},{2,0},{3,1},{4,6},{5,7},{6,4},{7,5},{8,10},{9,11},{10,... | collective-permute-start | bytes 110600 | tf_op jit(solution)/shard_map/ppermute | solution.py:619
  5.7 10.0 %collective-permute-start.1 = (bf16[1,144,128]{2,1,0:T(8,128)(2,1)S(1)}, bf16[1,144,128]{2,1,0:T(8,128)(2,1)S(1)}, u32[]{:S(2)}, u32[]{:S(2)}) collective-permute-start(bf16[1,144,128]{2,1,0:T(8,128)(2,1)S(1)} %get-tuple-element.32), channel_id=1, source_target_pairs={{0,4},{1,5},{2,6},{3,7},{4,0},{5,1},{6,2},{7,3},{8,12},{9,13},{10,... | collective-permute-start | bytes 110600 | tf_op jit(solution)/shard_map/ppermute | solution.py:619
  8.3 7.4 %collective-permute-start = (bf16[1,144,128]{2,1,0:T(8,128)(2,1)S(1)}, bf16[1,144,128]{2,1,0:T(8,128)(2,1)S(1)}, u32[]{:S(2)}, u32[]{:S(2)}) collective-permute-start(bf16[1,144,128]{2,1,0:T(8,128)(2,1)S(1)} %get-tuple-element.32), channel_id=1, source_target_pairs={{0,6},{1,7},{2,4},{3,5},{4,2},{5,3},{6,0},{7,1},{8,14},{9,15},{10,... | collective-permute-start | bytes 110600 | tf_op jit(solution)/shard_map/ppermute | solution.py:619
  9.1 3.9 %collective-permute-start.5 = (bf16[1,128,128]{2,1,0:T(8,128)(2,1)S(1)}, bf16[1,128,128]{2,1,0:T(8,128)(2,1)S(1)}, u32[]{:S(2)}, u32[]{:S(2)}) collective-permute-start(bf16[1,128,128]{2,1,0:T(8,128)(2,1)S(1)} %pad_maximum_fusion.4), channel_id=1, source_target_pairs={{0,1},{1,0},{2,3},{3,2},{4,5},{5,4},{6,7},{7,6},{8,9},{9,8},{10,11... | collective-permute-start | bytes 98312 | tf_op jit(solution)/shard_map/ppermute | solution.py:619
  13.7 21.8 %copy-start.3 = (bf16[256,32]{0,1:T(8,128)(2,1)S(1)}, bf16[256,32]{0,1:T(8,128)(2,1)}, u32[]{:S(2)}) copy-start(bf16[256,32]{0,1:T(8,128)(2,1)} %param.18) | copy-start | bytes 49156
  13.7 21.8 %copy-start.4 = (bf16[256,32]{0,1:T(8,128)(2,1)S(1)}, bf16[256,32]{0,1:T(8,128)(2,1)}, u32[]{:S(2)}) copy-start(bf16[256,32]{0,1:T(8,128)(2,1)} %param.19) | copy-start | bytes 49156
  13.7 21.8 %copy-start.5 = (f32[256]{0:T(256)S(1)}, f32[256]{0:T(256)}, u32[]{:S(2)}) copy-start(f32[256]{0:T(256)} %param.17) | copy-start | bytes 3076
  13.7 5.2 %collective-permute-start.6 = (bf16[2,128,128]{2,1,0:T(8,128)(2,1)S(1)}, bf16[2,128,128]{2,1,0:T(8,128)(2,1)S(1)}, u32[]{:S(2)}, u32[]{:S(2)}) collective-permute-start(bf16[2,128,128]{2,1,0:T(8,128)(2,1)S(1)} %pad_maximum_fusion.3), channel_id=1, source_target_pairs={{0,4},{1,5},{2,6},{3,7},{4,0},{5,1},{6,2},{7,3},{8,12},{9,13},{10,... | collective-permute-start | bytes 196616 | tf_op jit(solution)/shard_map/ppermute | solution.py:619
  15.8 5.5 %collective-permute-start.3 = (bf16[4,144,128]{2,1,0:T(8,128)(2,1)S(1)}, bf16[4,144,128]{2,1,0:T(8,128)(2,1)S(1)}, u32[]{:S(2)}, u32[]{:S(2)}) collective-permute-start(bf16[4,144,128]{2,1,0:T(8,128)(2,1)S(1)} %pad_maximum_fusion.1), channel_id=1, source_target_pairs={{0,1},{1,0},{2,3},{3,2},{4,5},{5,4},{6,7},{7,6},{8,9},{9,8},{10,11... | collective-permute-start | bytes 442376 | tf_op jit(solution)/shard_map/ppermute | solution.py:619
  19.7 5.0 %collective-permute-start.7 = (bf16[4,128,128]{2,1,0:T(8,128)(2,1)S(1)}, bf16[4,128,128]{2,1,0:T(8,128)(2,1)S(1)}, u32[]{:S(2)}, u32[]{:S(2)}) collective-permute-start(bf16[4,128,128]{2,1,0:T(8,128)(2,1)S(1)} %pad_maximum_fusion.2), channel_id=1, source_target_pairs={{0,2},{1,3},{2,0},{3,1},{4,6},{5,7},{6,4},{7,5},{8,10},{9,11},{10,... | collective-permute-start | bytes 393224 | tf_op jit(solution)/shard_map/ppermute | solution.py:619
  21.3 4.4 %collective-permute-start.4 = (bf16[8,144,128]{2,1,0:T(8,128)(2,1)S(1)}, bf16[8,144,128]{2,1,0:T(8,128)(2,1)S(1)}, u32[]{:S(2)}, u32[]{:S(2)}) collective-permute-start(bf16[8,144,128]{2,1,0:T(8,128)(2,1)S(1)} %constant_dynamic-update-slice_fusion.mine_ref), channel_id=1, source_target_pairs={{0,8},{8,0},{1,9},{9,1},{2,10},{10,2},{3,11},{11,3},{4,12},{12,4},... | collective-permute-start | bytes 884744 | tf_op jit(solution)/shard_map/ppermute | solution.py:608
  25.5 1.6 %collective-permute-start.8 = (bf16[8,128,128]{2,1,0:T(8,128)(2,1)S(1)}, bf16[8,128,128]{2,1,0:T(8,128)(2,1)S(1)}, u32[]{:S(2)}, u32[]{:S(2)}) collective-permute-start(bf16[8,128,128]{2,1,0:T(8,128)(2,1)S(1)} %pad_maximum_fusion.pmine_ref), channel_id=1, source_target_pairs={{0,8},{8,0},{1,9},{9,1},{2,10},{10,2},{3,11},{11,3},{4,12},{12,4},... | collective-permute-start | bytes 786440 | tf_op jit(solution)/shard_map/ppermute | solution.py:608
  35.4 1.2 %collective-permute-start.9 = (bf16[64,256]{1,0:T(8,128)(2,1)S(1)}, bf16[64,256]{1,0:T(8,128)(2,1)S(1)}, u32[]{:S(2)}, u32[]{:S(2)}) collective-permute-start(bf16[64,256]{1,0:T(8,128)(2,1)S(1)} %get-tuple-element.35), channel_id=1, source_target_pairs={{0,8},{8,0},{1,9},{9,1},{2,10},{10,2},{3,11},{11,3},{4,12},{12,4},... | collective-permute-start | bytes 98312 | tf_op jit(solution)/shard_map/ppermute | solution.py:608
  36.6 6.4 %collective-permute-start.12 = (bf16[64,256]{1,0:T(8,128)(2,1)S(1)}, bf16[64,256]{1,0:T(8,128)(2,1)S(1)}, u32[]{:S(2)}, u32[]{:S(2)}) collective-permute-start(bf16[64,256]{1,0:T(8,128)(2,1)S(1)} %add_convert_fusion.1), channel_id=1, source_target_pairs={{0,6},{1,7},{2,4},{3,5},{4,2},{5,3},{6,0},{7,1},{8,14},{9,15},{10,... | collective-permute-start | bytes 98312 | tf_op jit(solution)/shard_map/ppermute | solution.py:619
  40.5 4.8 %collective-permute-start.11 = (bf16[64,256]{1,0:T(8,128)(2,1)S(1)}, bf16[64,256]{1,0:T(8,128)(2,1)S(1)}, u32[]{:S(2)}, u32[]{:S(2)}) collective-permute-start(bf16[64,256]{1,0:T(8,128)(2,1)S(1)} %add_convert_fusion.1), channel_id=1, source_target_pairs={{0,4},{1,5},{2,6},{3,7},{4,0},{5,1},{6,2},{7,3},{8,12},{9,13},{10,... | collective-permute-start | bytes 98312 | tf_op jit(solution)/shard_map/ppermute | solution.py:619
  40.5 4.8 %collective-permute-start.10 = (bf16[64,256]{1,0:T(8,128)(2,1)S(1)}, bf16[64,256]{1,0:T(8,128)(2,1)S(1)}, u32[]{:S(2)}, u32[]{:S(2)}) collective-permute-start(bf16[64,256]{1,0:T(8,128)(2,1)S(1)} %add_convert_fusion.1), channel_id=1, source_target_pairs={{0,2},{1,3},{2,0},{3,1},{4,6},{5,7},{6,4},{7,5},{8,10},{9,11},{10,... | collective-permute-start | bytes 98312 | tf_op jit(solution)/shard_map/ppermute | solution.py:619
  45.4 4.0 %collective-permute-start.13 = (bf16[64,256]{1,0:T(8,128)(2,1)S(1)}, bf16[64,256]{1,0:T(8,128)(2,1)S(1)}, u32[]{:S(2)}, u32[]{:S(2)}) collective-permute-start(bf16[64,256]{1,0:T(8,128)(2,1)S(1)} %add_convert_fusion), channel_id=1, source_target_pairs={{0,1},{1,0},{2,3},{3,2},{4,5},{5,4},{6,7},{7,6},{8,9},{9,8},{10,11... | collective-permute-start | bytes 98312 | tf_op jit(solution)/shard_map/ppermute | solution.py:619
where the time goes:
time: 50.8 us; the launch traced here: 50 us
  starting transfers between devices  18.9 us (37%)
  Pallas kernels  13.6 us (27%)
  waiting for transfers between devices  12.1 us (24%)
  other arithmetic  3.12 us (6%)
  local copies, waits for them, and re-layouts  1.51 us (3%)
  between operations  0.79 us (2%)
    ppermute x11, starting transfers between devices, swap_col(): lax.ppermute(block, 'col', [(at, at ^ partner) for at in range(count)])  18.6 us
    ppermute x11, waiting for transfers between devices, swap_col(): lax.ppermute(block, 'col', [(at, at ^ partner) for at in range(count)])  9.91 us
    pallas_call x1, Pallas kernels, whole_plan(): pl.pallas_call(functools.partial(main_kernel, (seqs, res, pair_cols, widt...  8.3 us
    concatenate x4, other arithmetic, gathered(): block = jnp.concatenate([block] + came)  2.26 us
    ppermute x3, waiting for transfers between devices, swap_depth(): return lax.ppermute(block, 'depth', [(0, 1), (1, 0)])  2.17 us
    pallas_call x1, Pallas kernels, whole_plan(): pl.pallas_call(pre_kernel, out_shape=(shape((1, rows, pair_width), bf16),...  1.88 us
    pallas_call x1, Pallas kernels, whole_plan(): pl.pallas_call(out_weight_kernel, out_shape=shape((outer_width, pair_widt...  1.82 us
    pallas_call x1, Pallas kernels, whole_plan(): pl.pallas_call(transition_weight_kernel, out_shape=(shape((pair_width, hi...  1.32 us
  transfers between devices with their start and end apart: 14, of which 7 were waited for; matrix products, arithmetic and copies ran while one was open for 8% of the time, Pallas kernels for 7%

commit v1 on v0

--- a/solution.py
+++ b/solution.py
@@ -245,6 +245,8 @@
 
 FEW_RESIDUES = 32
 MASK_ROWS = 16
+Z_PARTNERS = (2, 4, 6)
+Y_PARTNER = 1
 
 
 def butterfly(blocks, group):
@@ -282,6 +284,8 @@
     scale_hbm,
     first_hbm,
     second_hbm,
+    act_hbm,
+    grad_hbm,
     sent_ref,
     normed_ref,
     scaled_ref,
@@ -297,6 +301,9 @@
     second_ref,
     sems,
 ):
+    res, seqs = maskt_ref.shape
+    pairs = act_hbm.shape[0]
+    first_pair = 2 * seqs + MASK_ROWS
     copies = [
         pltpu.make_async_copy(source, target, sems.at[at])
         for at, (source, target) in enumerate(
@@ -307,6 +314,8 @@
                 (scale_hbm, scale_ref),
                 (first_hbm, first_ref),
                 (second_hbm, second_ref),
+                (act_hbm, sent_ref.at[0, pl.ds(first_pair, pairs), :]),
+                (grad_hbm, sent_ref.at[0, pl.ds(first_pair + pairs, pairs), :]),
             )
         )
     ]
@@ -314,7 +323,6 @@
         copy.start()
     for copy in copies:
         copy.wait()
-    res, seqs = maskt_ref.shape
     lanes = sent_ref.shape[2]
     group = lanes // res
     scaled, inv = norm_pieces(
@@ -355,71 +363,45 @@
                 lane_group == r, wide_ref[at, pl.ds(r, seqs, stride=res), :], both
             )
         sent_ref[0, at * seqs : (at + 1) * seqs, :] = (both * mask_lanes).astype(jnp.bfloat16)
-    sent_ref[0, 2 * seqs :, :] = tile_ref[...].astype(jnp.bfloat16)
-
-
-def main_kernel(
+    sent_ref[0, 2 * seqs : first_pair, :] = tile_ref[...].astype(jnp.bfloat16)
+
+
+def outer_kernel(
     sizes,
     orders,
     ids_ref,
-    mine_ref,
-    other_ref,
-    pmine_ref,
-    pother_ref,
-    wout_ref,
+    near_ref,
+    far_ref,
+    other_near_ref,
+    other_far_ref,
     wturn_ref,
-    gain_ref,
-    hid_ref,
-    back_ref,
-    normed_ref,
-    lanes_ref,
-    couple_ref,
-    part_ref,
     outer_ref,
-    opm_ref,
-    pn_ref,
-    gh_ref,
-    hidden_ref,
-    mg_ref,
-    spread_ref,
-    got_ref,
-    pgot_ref,
-    leftn_ref,
+    proj_out_ref,
+    cnt_ref,
+    pm_ref,
     rightt_ref,
     leftt_ref,
+    got_ref,
+    leftn_ref,
+    mine_ref,
     turn_ref,
     maskt_ref,
-    cnt_ref,
     cntl_ref,
     pml_ref,
-    pm_ref,
-    proj_out_ref,
-    gmid_ref,
-    gf_ref,
-    grow_ref,
-    gcol_ref,
-    gor_ref,
-    goc_ref,
-    gs_ref,
 ):
     seqs, res, pair_cols, width = sizes
     depths, cols = got_ref.shape[0], got_ref.shape[1]
     residues = cols * res
     lanes = res * width
-    per = res * pair_cols
-    half = residues * pair_cols
-    pairs = depths * half
+    half_cols = pair_cols // res
     me_depth = ids_ref[0]
     me_col = ids_ref[1]
     f32, bf16 = jnp.float32, jnp.bfloat16
 
-    for into, mine, other, order in (
-        (got_ref, mine_ref, other_ref, orders[0]),
-        (pgot_ref, pmine_ref, pother_ref, orders[1]),
-    ):
+    for order, mine, other in zip(orders, (near_ref, far_ref), (other_near_ref, other_far_ref)):
         for at, partner in enumerate(order):
-            into[me_depth, me_col ^ partner] = mine[at]
-            into[1 - me_depth, me_col ^ partner] = other[at]
+            got_ref[me_depth, me_col ^ partner] = mine[at]
+            got_ref[1 - me_depth, me_col ^ partner] = other[at]
 
     for e in range(depths):
         for k in range(cols):
@@ -428,14 +410,25 @@
             ]
     for at, out in ((0, leftt_ref), (1, rightt_ref)):
         for k in range(cols):
-            block = jnp.concatenate(
-                [got_ref[e, k, at * seqs : (at + 1) * seqs, :] for e in range(depths)], axis=0
-            ).astype(f32)
-            turn_ref[k * lanes : (k + 1) * lanes, :] = block.T
+            block = got_ref[me_depth, k, at * seqs : (at + 1) * seqs, :].astype(f32)
+            turn_ref[k * lanes : (k + 1) * lanes, 0:seqs] = block.T
         for d in range(width):
             out[d * residues : (d + 1) * residues, :] = turn_ref[
                 pl.ds(d, residues, stride=width), :
             ].astype(bf16)
+    for k in range(half_cols):
+        block = jnp.concatenate(
+            [
+                got_ref[e, me_depth * half_cols + k, seqs : 2 * seqs, :]
+                for e in range(depths)
+            ],
+            axis=0,
+        ).astype(f32)
+        turn_ref[k * lanes : (k + 1) * lanes, :] = block.T
+    for d in range(width):
+        mine_ref[d * pair_cols : (d + 1) * pair_cols, :] = turn_ref[
+            pl.ds(d, pair_cols, stride=width), :
+        ].astype(bf16)
 
     base = 2 * seqs
     pair_lane = lax.broadcasted_iota(jnp.int32, (pair_cols, lanes), 1)
@@ -443,57 +436,83 @@
     for k in range(cols):
         tiles = [got_ref[e, k, base : base + MASK_ROWS, :].astype(f32) for e in range(depths)]
         maskt_ref[k * res : (k + 1) * res, :] = tiles[0][0:res] + tiles[1][0:res]
-        for e in range(depths):
-            for r in range(res):
-                row = tiles[e][res + r : res + r + 1, :]
-                first = e * half + (k * res + r) * pair_cols
-                pml_ref[first : first + pair_cols, :] = jnp.where(
-                    pair_lane == pair_row, row, 0.0
-                ).astype(bf16)
+        own = got_ref[me_depth, k, base : base + MASK_ROWS, :].astype(f32)
+        for r in range(res):
+            row = own[res + r : res + r + 1, :]
+            first = (k * res + r) * pair_cols
+            pml_ref[first : first + pair_cols, :] = jnp.where(
+                pair_lane == pair_row, row, 0.0
+            ).astype(bf16)
     maskt = maskt_ref[...]
-    for e in range(depths):
-        cols_mask = maskt[e * pair_cols : (e + 1) * pair_cols, :]
-        for i in range(residues):
-            first = e * half + i * pair_cols
-            cntl_ref[first : first + pair_cols, :] = (maskt[i : i + 1, :] * cols_mask).astype(bf16)
+    cols_mask = maskt_ref[pl.ds(pl.multiple_of(me_depth * pair_cols, pair_cols), pair_cols), :]
+    for i in range(residues):
+        cntl_ref[i * pair_cols : (i + 1) * pair_cols, :] = (maskt[i : i + 1, :] * cols_mask).astype(
+            bf16
+        )
     ones = jnp.ones((lanes, lanes), bf16)
     cnt_ref[...] = jnp.dot(cntl_ref[...], ones, preferred_element_type=f32)
     pm_ref[...] = jnp.dot(pml_ref[...], ones, preferred_element_type=f32).astype(bf16)
 
     for dh in range(width // 4):
         prod = jnp.dot(
-            rightt_ref[dh * 4 * residues : (dh + 1) * 4 * residues, :],
+            mine_ref[dh * 4 * pair_cols : (dh + 1) * 4 * pair_cols, :],
             leftn_ref[...],
             preferred_element_type=f32,
         )
         for k in range(cols):
             piece = prod[:, k * lanes : (k + 1) * lanes]
             turned = butterfly(
-                [piece[a * residues : (a + 1) * residues] for a in range(4)], width
+                [piece[a * pair_cols : (a + 1) * pair_cols] for a in range(4)], width
             )
             for il in range(res):
-                block = turned[il].astype(bf16)
-                for e in range(depths):
-                    first = e * half + (k * res + il) * pair_cols
-                    outer_ref[first : first + pair_cols, dh * lanes : (dh + 1) * lanes] = block[
-                        e * pair_cols : (e + 1) * pair_cols
-                    ]
+                first = (k * res + il) * pair_cols
+                outer_ref[first : first + pair_cols, dh * lanes : (dh + 1) * lanes] = turned[
+                    il
+                ].astype(bf16)
     proj_out_ref[...] = jnp.dot(outer_ref[...], wturn_ref[...], preferred_element_type=f32)
 
+
+def transition_kernel(
+    sizes,
+    orders,
+    ids_ref,
+    near_ref,
+    far_ref,
+    proj_out_ref,
+    cnt_ref,
+    pm_ref,
+    gain_ref,
+    hid_ref,
+    back_ref,
+    couple_ref,
+    opm_ref,
+    pn_ref,
+    gh_ref,
+    hidden_ref,
+    mg_ref,
+    pgot_ref,
+    gmid_ref,
+):
+    seqs, res, pair_cols, width = sizes
+    per = res * pair_cols
+    cols = pgot_ref.shape[0]
+    me_col = ids_ref[1]
+    f32, bf16 = jnp.float32, jnp.bfloat16
+    for order, mine in zip(orders, (near_ref, far_ref)):
+        for at, partner in enumerate(order):
+            pgot_ref[me_col ^ partner] = mine[at]
     gain = gain_ref[...]
     chunk = 2 * per
-    for at in range(pairs // chunk):
+    for at in range(cols // 2):
         rows = slice(at * chunk, (at + 1) * chunk)
-        e, k = divmod(2 * at, cols)
         act, grad = [
             jnp.concatenate(
-                [pgot_ref[e, k + b, at * per : (at + 1) * per, :] for b in range(2)], axis=0
+                [pgot_ref[2 * at + b, w * per : (w + 1) * per, :] for b in range(2)], axis=0
             )
-            for at in range(2)
+            for w in range(2)
         ]
-        act = act.astype(f32)
         count = cnt_ref[rows, :]
-        mid = act + proj_out_ref[rows, :] / count
+        mid = act.astype(f32) + proj_out_ref[rows, :] / count
         scaled, inv = norm_pieces(mid)
         normed = (scaled * gain).astype(bf16)
         pn_ref[rows, :] = normed
@@ -515,23 +534,51 @@
         )
         gmid = grad.astype(f32) + standardize_adjoint(gsc, scaled, inv)
         gmid_ref[rows, :] = gmid
-        opm = (gmid / count).astype(bf16)
-        opm_ref[rows, :] = opm
-        gf_ref[rows, :] = opm.astype(f32)
-    start = pl.multiple_of(me_depth * half + me_col * per, per)
-    couple_ref[...] = gmid_ref[pl.ds(start, per), :].astype(bf16)
+        opm_ref[rows, :] = (gmid / count).astype(bf16)
+    couple_ref[...] = gmid_ref[pl.ds(pl.multiple_of(me_col * per, per), per), :].astype(bf16)
+
+
+def projector_kernel(
+    sizes,
+    ids_ref,
+    opm_ref,
+    other_opm_ref,
+    rightt_ref,
+    leftt_ref,
+    wout_ref,
+    wturn_ref,
+    normed_ref,
+    lanes_ref,
+    part_ref,
+    spread_ref,
+    gf_ref,
+    grow_ref,
+    gcol_ref,
+    gor_ref,
+    goc_ref,
+    gs_ref,
+):
+    seqs, res, pair_cols, width = sizes
+    depths, half = gf_ref.shape[0], gf_ref.shape[1]
+    residues = half // pair_cols
+    lanes = res * width
+    me_depth = ids_ref[0]
+    me_col = ids_ref[1]
+    f32, bf16 = jnp.float32, jnp.bfloat16
+    gf_ref[me_depth] = opm_ref[...].astype(f32)
+    gf_ref[1 - me_depth] = other_opm_ref[...].astype(f32)
 
     for il in range(res):
         for e in range(depths):
-            first = pl.multiple_of(e * half + (me_col * res + il) * pair_cols, pair_cols)
+            first = pl.multiple_of((me_col * res + il) * pair_cols, pair_cols)
             grow_ref[il * residues + e * pair_cols : il * residues + (e + 1) * pair_cols, :] = (
-                gf_ref[pl.ds(first, pair_cols), :].astype(bf16)
+                gf_ref[e, pl.ds(first, pair_cols), :].astype(bf16)
             )
     my_half = (me_col * res) // pair_cols
     my_first = me_col * res - my_half * pair_cols
     for jl in range(res):
         gcol_ref[jl * residues : (jl + 1) * residues, :] = gf_ref[
-            pl.ds(my_half * half + my_first + jl, residues, stride=pair_cols), :
+            my_half, pl.ds(my_first + jl, residues, stride=pair_cols), :
         ].astype(bf16)
     for lhs, weight, out in ((grow_ref, wturn_ref, gor_ref), (gcol_ref, wout_ref, goc_ref)):
         for dh in range(width // 4):
@@ -547,22 +594,15 @@
             for dl in range(4):
                 first = (dh * 4 + dl) * residues
                 out[first : first + residues, :] = turned[dl].astype(bf16)
-    sums = [
-        lax.dot_general(lhs[...], rhs[...], (((0,), (0,)), ((), ())), preferred_element_type=f32)
-        for lhs, rhs in ((rightt_ref, gor_ref), (leftt_ref, goc_ref))
-    ]
     mask_lanes = lanes_ref[...]
-    upper = me_depth == 0
-    sums = [
-        (jnp.where(upper, total[:seqs], total[seqs:]) * mask_lanes).astype(bf16).astype(f32)
-        for total in sums
-    ]
     lane_group = lax.broadcasted_iota(jnp.int32, (seqs, lanes), 1) // width
-    for r in range(res):
-        for at in range(2):
-            gs_ref[at, pl.ds(r, seqs, stride=res), :] = jnp.where(
-                lane_group == r, sums[at], 0.0
-            )
+    for at, (lhs, rhs) in enumerate(((rightt_ref, gor_ref), (leftt_ref, goc_ref))):
+        total = lax.dot_general(
+            lhs[...], rhs[...], (((0,), (0,)), ((), ())), preferred_element_type=f32
+        )[:seqs]
+        total = (total * mask_lanes).astype(bf16).astype(f32)
+        for r in range(res):
+            gs_ref[at, pl.ds(r, seqs, stride=res), :] = jnp.where(lane_group == r, total, 0.0)
     spread = jnp.concatenate([gs_ref[0], gs_ref[1]], axis=1).astype(bf16)
     spread_ref[...] = spread
     cross = lax.dot_general(
@@ -581,14 +621,16 @@
         outer_ref[...], opm_ref[...], (((0,), (0,)), ((), ())), preferred_element_type=jnp.float32
     )
     for c in range(width):
-        dout_ref[c * width : (c + 1) * width, :] = turn_ref[pl.ds(c, width, stride=width), :]
+        dout_ref[c * width : (c + 1) * width, :] = turn_ref[
+            pl.ds(c, width, stride=width), :
+        ].astype(jnp.bfloat16)
 
 
 def transition_weight_kernel(pn_ref, gh_ref, hidden_ref, mg_ref, dhid_ref, dback_ref):
     for lhs, rhs, out in ((pn_ref, gh_ref, dhid_ref), (hidden_ref, mg_ref, dback_ref)):
         out[...] = lax.dot_general(
             lhs[...], rhs[...], (((0,), (0,)), ((), ())), preferred_element_type=jnp.float32
-        )
+        ).astype(jnp.bfloat16)
 
 
 def feature_kernel(
@@ -617,15 +659,6 @@
 def swap_col(block, partner):
     count = lax.axis_size("col")
     return lax.ppermute(block, "col", [(at, at ^ partner) for at in range(count)])
-
-
-def gathered(block, rounds):
-    order = [0]
-    for partners in rounds:
-        came = [swap_col(block, partner) for partner in partners]
-        block = jnp.concatenate([block] + came)
-        order = order + [at ^ partner for partner in partners for at in order]
-    return block, tuple(order)
 
 
 def whole_plan(
@@ -651,9 +684,10 @@
     pair_cols, pair_width = pair_activation_input.shape[1:]
     hid = hidden_weight.shape[1]
     per = res * pair_cols
-    pairs = residues * residues
     lanes = res * width
-    rows = 2 * seqs + MASK_ROWS
+    near_rows = 2 * seqs + MASK_ROWS
+    rows = near_rows + 2 * per
+    half = residues * pair_cols
     f32, bf16 = jnp.float32, jnp.bfloat16
     ids = jnp.stack([lax.axis_index("depth"), lax.axis_index("col")]).astype(jnp.int32)
     smem = pl.BlockSpec(memory_space=pltpu.SMEM)
@@ -665,14 +699,6 @@
         outer_width, pair_width
     )
     shape = jax.ShapeDtypeStruct
-    pair_arrays = jnp.concatenate(
-        [
-            pair_activation_input.reshape(1, per, pair_width),
-            pair_output_gradient.reshape(1, per, pair_width),
-        ],
-        axis=1,
-    )
-    pmine, porder = gathered(pair_arrays, ((1,), (4,), (2,)))
     sent, normed, scaled, inv, mask_lanes = pl.pallas_call(
         pre_kernel,
         out_shape=(
@@ -682,7 +708,7 @@
             shape((seqs * res, 1), f32),
             shape((seqs, lanes), f32),
         ),
-        in_specs=[smem] + [pl.BlockSpec(memory_space=pltpu.HBM)] * 6,
+        in_specs=[smem] + [pl.BlockSpec(memory_space=pltpu.HBM)] * 8,
         out_specs=[vmem] * 5,
         scratch_shapes=[
             pltpu.VMEM((2, seqs * res, lanes), f32),
@@ -693,7 +719,7 @@
             pltpu.VMEM((1, channels), f32),
             pltpu.VMEM((width, channels), bf16),
             pltpu.VMEM((width, channels), bf16),
-            pltpu.SemaphoreType.DMA((6,)),
+            pltpu.SemaphoreType.DMA((8,)),
         ],
         compiler_params=params,
         name="project",
@@ -708,42 +734,93 @@
                 scale,
                 first,
                 second,
+                pair_activation_input.reshape(per, pair_width),
+                pair_output_gradient.reshape(per, pair_width),
             )
         ],
     )
-    mine, order = gathered(sent, ((6, 4, 2), (1,)))
-    other = swap_depth(mine)
-    pother = swap_depth(pmine)
-    couple, part, outer, opm, pn, gh, hidden, mg, spread = pl.pallas_call(
-        functools.partial(main_kernel, (seqs, res, pair_cols, width), (order, porder)),
+    near_order = (0,) + Z_PARTNERS
+    far_order = tuple(at ^ Y_PARTNER for at in near_order)
+    blocks = [sent] + [swap_col(sent, partner) for partner in Z_PARTNERS]
+    near = jnp.concatenate([block[:, :near_rows] for block in blocks])
+    pair_near = jnp.concatenate([block[:, near_rows:] for block in blocks])
+    far = swap_col(near, Y_PARTNER)
+    pair_far = swap_col(pair_near, Y_PARTNER)
+    sizes = (seqs, res, pair_cols, width)
+    orders = (near_order, far_order)
+    outer, proj_out, cnt, pm, rightt, leftt = pl.pallas_call(
+        functools.partial(outer_kernel, sizes, orders),
+        out_shape=(
+            shape((half, outer_width), bf16),
+            shape((half, pair_width), f32),
+            shape((half, lanes), f32),
+            shape((half, lanes), bf16),
+            shape((residues * width, depths * seqs), bf16),
+            shape((residues * width, depths * seqs), bf16),
+        ),
+        in_specs=[smem] + [vmem] * 5,
+        out_specs=[vmem] * 6,
+        scratch_shapes=[
+            pltpu.VMEM((depths, cols, near_rows, pair_width), bf16),
+            pltpu.VMEM((depths * seqs, residues * width), bf16),
+            pltpu.VMEM((pair_cols * width, depths * seqs), bf16),
+            pltpu.VMEM((residues * width, depths * seqs), f32),
+            pltpu.VMEM((residues, depths * seqs), f32),
+            pltpu.VMEM((half, lanes), bf16),
+            pltpu.VMEM((half, lanes), bf16),
+        ],
+        compiler_params=params,
+        name="outer_products",
+    )(ids, near, far, swap_depth(near), swap_depth(far), wturn)
+    couple, opm, pn, gh, hidden, mg = pl.pallas_call(
+        functools.partial(transition_kernel, sizes, orders),
         out_shape=(
             shape((per, pair_width), bf16),
+            shape((half, pair_width), bf16),
+            shape((half, pair_width), bf16),
+            shape((half, hid), bf16),
+            shape((half, hid), bf16),
+            shape((half, pair_width), bf16),
+        ),
+        in_specs=[smem] + [vmem] * 8,
+        out_specs=[vmem] * 6,
+        scratch_shapes=[
+            pltpu.VMEM((cols, 2 * per, pair_width), bf16),
+            pltpu.VMEM((half, pair_width), f32),
+        ],
+        compiler_params=params,
+        name="transition",
+    )(
+        ids,
+        pair_near,
+        pair_far,
+        proj_out,
+        cnt,
+        pm,
+        pair_norm_gain.reshape(1, pair_width),
+        hidden_weight,
+        back_weight,
+    )
+    dout = pl.pallas_call(
+        out_weight_kernel,
+        out_shape=shape((outer_width, pair_width), bf16),
+        in_specs=[vmem] * 2,
+        out_specs=vmem,
+        scratch_shapes=[pltpu.VMEM((outer_width, pair_width), f32)],
+        compiler_params=params,
+        name="out_weight",
+    )(outer, opm)
+    other_opm, dout = lax.optimization_barrier((swap_depth(opm), dout))
+    part, spread = pl.pallas_call(
+        functools.partial(projector_kernel, sizes),
+        out_shape=(
             shape((2 * width, channels), bf16),
-            shape((pairs, outer_width), bf16),
-            shape((pairs, pair_width), bf16),
-            shape((pairs, pair_width), bf16),
-            shape((pairs, hid), bf16),
-            shape((pairs, hid), bf16),
-            shape((pairs, pair_width), bf16),
             shape((seqs * res, 2 * lanes), bf16),
         ),
-        in_specs=[smem] + [vmem] * 11,
-        out_specs=[vmem] * 9,
+        in_specs=[smem] + [vmem] * 8,
+        out_specs=[vmem] * 2,
         scratch_shapes=[
-            pltpu.VMEM((depths, cols, rows, pair_width), bf16),
-            pltpu.VMEM((depths, cols, 2 * per, pair_width), bf16),
-            pltpu.VMEM((depths * seqs, residues * width), bf16),
-            pltpu.VMEM((residues * width, depths * seqs), bf16),
-            pltpu.VMEM((residues * width, depths * seqs), bf16),
-            pltpu.VMEM((residues * width, depths * seqs), f32),
-            pltpu.VMEM((residues, depths * seqs), f32),
-            pltpu.VMEM((pairs, lanes), f32),
-            pltpu.VMEM((pairs, lanes), bf16),
-            pltpu.VMEM((pairs, lanes), bf16),
-            pltpu.VMEM((pairs, lanes), bf16),
-            pltpu.VMEM((pairs, pair_width), f32),
-            pltpu.VMEM((pairs, pair_width), f32),
-            pltpu.VMEM((pairs, pair_width), f32),
+            pltpu.VMEM((depths, half, pair_width), f32),
             pltpu.VMEM((res * residues, pair_width), bf16),
             pltpu.VMEM((res * residues, pair_width), bf16),
             pltpu.VMEM((residues * width, lanes), bf16),
@@ -751,29 +828,8 @@
             pltpu.VMEM((2, seqs * res, lanes), f32),
         ],
         compiler_params=params,
-        name="pair_work",
-    )(
-        ids,
-        mine,
-        other,
-        pmine,
-        pother,
-        output_weight,
-        wturn,
-        pair_norm_gain.reshape(1, pair_width),
-        hidden_weight,
-        back_weight,
-        normed,
-        mask_lanes,
-    )
-    total = part.astype(f32)
-
-    def add_partners(total, partners, beside):
-        kept = lax.optimization_barrier(total.astype(bf16))
-        came = [swap_col(kept, at) if at else swap_depth(kept) for at in partners]
-        came, beside = lax.optimization_barrier((came, beside))
-        return pairwise_sum([block.astype(f32) for block in [kept] + came]), beside
-
+        name="projector_parts",
+    )(ids, opm, other_opm, rightt, leftt, output_weight, wturn, normed, mask_lanes)
     feat = pl.pallas_call(
         functools.partial(feature_kernel, res),
         out_shape=shape((seqs * res, channels), bf16),
@@ -782,26 +838,24 @@
         compiler_params=params,
         name="features",
     )(spread, first, second, scale, scaled, inv)
-    total, feat = add_partners(total, (0,), feat)
-    dout = pl.pallas_call(
-        out_weight_kernel,
-        out_shape=shape((outer_width, pair_width), f32),
-        in_specs=[vmem] * 2,
-        out_specs=vmem,
-        scratch_shapes=[pltpu.VMEM((outer_width, pair_width), f32)],
-        compiler_params=params,
-        name="out_weight",
-    )(outer, opm)
-    total, dout = add_partners(total, (2, 4, 6), dout)
     dhid, dback = pl.pallas_call(
         transition_weight_kernel,
-        out_shape=(shape((pair_width, hid), f32), shape((hid, pair_width), f32)),
+        out_shape=(shape((pair_width, hid), bf16), shape((hid, pair_width), bf16)),
         in_specs=[vmem] * 4,
         out_specs=[vmem] * 2,
         compiler_params=params,
         name="transition_weights",
     )(pn, gh, hidden, mg)
-    total, (dhid, dback) = add_partners(total, (1,), (dhid, dback))
+    total = part.astype(f32)
+    for partners in ((0,), Z_PARTNERS, (Y_PARTNER,)):
+        kept = lax.optimization_barrier(total.astype(bf16))
+        came = [swap_col(kept, at) if at else swap_depth(kept) for at in partners]
+        if partners == Z_PARTNERS:
+            came, dhid, dback = lax.optimization_barrier((came, dhid, dback))
+        total = pairwise_sum([block.astype(f32) for block in [kept] + came])
+    dout, dhid, dback = [
+        block.astype(f32) + swap_depth(block).astype(f32) for block in (dout, dhid, dback)
+    ]
     return (
         feat.reshape(seqs, res, channels),
         couple.reshape(res, pair_cols, pair_width),
@@ -814,8 +868,9 @@
 
 
 def on_device(alignment_activations, *others):
-    residues = alignment_activations.shape[1] * lax.axis_size("col")
-    plan = whole_plan if residues <= FEW_RESIDUES else split_plan
+    cols = lax.axis_size("col")
+    residues = alignment_activations.shape[1] * cols
+    plan = whole_plan if cols == 8 and residues <= FEW_RESIDUES else split_plan
     return plan(alignment_activations, *others)
 
 

time: 50.8 us -> 48.9 us (0.963)
  Pallas kernels: 13.6 us -> 10.2 us
  starting transfers between devices: 18.9 us -> 15.9 us
  waiting for transfers between devices: 12.1 us -> 15 us
  local copies, waits for them, and re-layouts: 1.51 us -> 4.21 us
  other arithmetic: 3.12 us -> 2.49 us
    ppermute x11 -> x9, starting transfers between devices: 18.6 us -> 15.2 us  [swap_col(): lax.ppermute(block, 'col', [(at, at ^ partner) for at in range(count)])]
    ppermute x11 -> x9, waiting for transfers between devices: 9.91 us -> 13 us  [swap_col(): lax.ppermute(block, 'col', [(at, at ^ partner) for at in range(count)])]
    concatenate x5 -> x2, other arithmetic: 3 us -> 0.04 us  [the longest x1 0.02 us: whole_plan(): near = jnp.concatenate([block[:, :near_rows] for block in blocks])]
    add x0 -> x3, other arithmetic: none -> 2.34 us  [whole_plan(): block.astype(f32) + swap_depth(block).astype(f32)]
    unnamed x18, local copies, waits for them, and re-layouts: 0.06 us -> 1.98 us
    pallas_call x1 -> x3, Pallas kernels: 8.3 us -> 6.85 us  [the longest x1 2.81 us: whole_plan(): pl.pallas_call(functools.partial(outer_kernel, sizes, orders), out_shape=...]
    pallas_call x1, Pallas kernels: 1.82 us -> 0.76 us  [whole_plan(): pl.pallas_call(out_weight_kernel, out_shape=shape((outer_width, pair_widt...]
    pallas_call x1, Pallas kernels: 1.32 us -> 0.4 us  [whole_plan(): pl.pallas_call(transition_weight_kernel, out_shape=(shape((pair_width, hi...]
  transfers between devices with their start and end apart: 14 -> 16, of which waited for: 7 -> 10; matrix products, arithmetic and copies ran while one was open for 8% -> 6% of each run, Pallas kernels for 7% -> 9%
where the time goes in v1:
time: 48.9 us; the launch traced here: 48.6 us
  starting transfers between devices  15.9 us (33%)
  waiting for transfers between devices  15 us (31%)
  Pallas kernels  10.2 us (21%)
  local copies, waits for them, and re-layouts  4.21 us (9%)
  other arithmetic  2.49 us (5%)
  between operations  0.78 us (2%)
    ppermute x9, starting transfers between devices, swap_col(): lax.ppermute(block, 'col', [(at, at ^ partner) for at in range(count)])  15.2 us
    ppermute x9, waiting for transfers between devices, swap_col(): lax.ppermute(block, 'col', [(at, at ^ partner) for at in range(count)])  13 us
    pallas_call x1, Pallas kernels, whole_plan(): pl.pallas_call(functools.partial(outer_kernel, sizes, orders), out_shape=...  2.81 us
    pallas_call x1, Pallas kernels, whole_plan(): pl.pallas_call(functools.partial(transition_kernel, sizes, orders), out_s...  2.41 us
    add x3, other arithmetic, whole_plan(): block.astype(f32) + swap_depth(block).astype(f32)  2.34 us
    ppermute x7, waiting for transfers between devices, swap_depth(): return lax.ppermute(block, 'depth', [(0, 1), (1, 0)])  2.02 us
    unnamed x18, local copies, waits for them, and re-layouts  1.98 us
    pallas_call x1, Pallas kernels, whole_plan(): pl.pallas_call(pre_kernel, out_shape=(shape((1, rows, pair_width), bf16),...  1.9 us
  transfers between devices with their start and end apart: 16, of which 10 were waited for; matrix products, arithmetic and copies ran while one was open for 6% of the time, Pallas kernels for 9%

profile of v1, /device:TPU:0, one launch (start us, length us, event | category | flops | bytes accessed | tf_op | source)
XLA Modules:
  0.0 48.6 jit_solution(13447642614875671594)
XLA Ops:
  0.6 0.1 pad_add_fusion.ids_ref
  0.7 1.9 %project.1 = (bf16[1,272,128]{2,1,0:T(8,128)(2,1)S(1)}, bf16[256,256]{1,0:T(8,128)(2,1)S(1)}, f32[256,256]{1,0:T(8,128)S(1)}, f32[256,1]{1,0:T(8,128)S(1)}, f32[64,128]{1,0:T(8,128)S(1)}) custom-call(s32[2]{0:T(128)S(1)} %pad_add_fusion.ids_ref, bf16[64,4,256]{2,1,0:T(4,128)(2,1)} %x_hbm.1, s32[4,64]{1,0:T(4,128)} %bitcast.30, s32[4,16]{1,0:T(4,128)} %pmask_hbm.1, ...), custom_call_target="tpu_custom_call" | custom-call | tf_op jit(solution)/shard_map/project/pallas_call | solution.py:702
  2.6 5.1 %collective-permute-start.2 = (bf16[1,272,128]{2,1,0:T(8,128)(2,1)S(1)}, bf16[1,272,128]{2,1,0:T(8,128)(2,1)S(1)}, u32[]{:S(2)}, u32[]{:S(2)}) collective-permute-start(bf16[1,272,128]{2,1,0:T(8,128)(2,1)S(1)} %get-tuple-element.35), channel_id=1, source_target_pairs={{0,6},{1,7},{2,4},{3,5},{4,2},{5,3},{6,0},{7,1},{8,14},{9,15},{10,... | collective-permute-start | bytes 208904 | tf_op jit(solution)/shard_map/ppermute | solution.py:661
  7.7 0.0 collective-permute-start.1
  7.7 0.6 %collective-permute-start = (bf16[1,272,128]{2,1,0:T(8,128)(2,1)S(1)}, bf16[1,272,128]{2,1,0:T(8,128)(2,1)S(1)}, u32[]{:S(2)}, u32[]{:S(2)}) collective-permute-start(bf16[1,272,128]{2,1,0:T(8,128)(2,1)S(1)} %get-tuple-element.35), channel_id=1, source_target_pairs={{0,2},{1,3},{2,0},{3,1},{4,6},{5,7},{6,4},{7,5},{8,10},{9,11},{10,... | collective-permute-start | bytes 208904 | tf_op jit(solution)/shard_map/ppermute | solution.py:661
  8.4 2.0 %collective-permute-done.2 = bf16[1,272,128]{2,1,0:T(8,128)(2,1)S(1)} collective-permute-done((bf16[1,272,128]{2,1,0:T(8,128)(2,1)S(1)}, bf16[1,272,128]{2,1,0:T(8,128)(2,1)S(1)}, u32[]{:S(2)}, u32[]{:S(2)}) %collective-permute-start.2) | collective-permute-done | bytes 69664 | tf_op jit(solution)/shard_map/ppermute | solution.py:661
  10.4 3.2 %collective-permute-done.1 = bf16[1,272,128]{2,1,0:T(8,128)(2,1)S(1)} collective-permute-done((bf16[1,272,128]{2,1,0:T(8,128)(2,1)S(1)}, bf16[1,272,128]{2,1,0:T(8,128)(2,1)S(1)}, u32[]{:S(2)}, u32[]{:S(2)}) %collective-permute-start.1) | collective-permute-done | bytes 69664 | tf_op jit(solution)/shard_map/ppermute | solution.py:661
  13.7 0.6 %copy-done.8 = bf16[1,272,128]{2,1,0:T(8,128)(2,1)} copy-done((bf16[1,272,128]{2,1,0:T(8,128)(2,1)}, bf16[1,272,128]{2,1,0:T(8,128)(2,1)S(1)}, u32[]{:S(2)}) %copy-start.8) | copy-done | bytes 69656
  14.3 0.0 collective-permute-done
  14.3 0.8 %slice-done = bf16[1,144,128]{2,1,0:T(8,128)(2,1)S(1)} async-done(((bf16[1,272,128]{2,1,0:T(8,128)(2,1)}), bf16[1,144,128]{2,1,0:T(8,128)(2,1)S(1)}, s32[]{:S(2)}) %slice-start) | async-done | bytes 36888 | tf_op jit(solution)/shard_map/slice | solution.py:745
  15.1 0.0 slice-done.2
  15.1 0.0 copy-start
  15.1 1.6 %collective-permute-start.4 = (bf16[4,144,128]{2,1,0:T(8,128)(2,1)S(1)}, bf16[4,144,128]{2,1,0:T(8,128)(2,1)S(1)}, u32[]{:S(2)}, u32[]{:S(2)}) collective-permute-start(bf16[4,144,128]{2,1,0:T(8,128)(2,1)S(1)} %pad_maximum_fusion.near_ref), channel_id=1, source_target_pairs={{0,1},{1,0},{2,3},{3,2},{4,5},{5,4},{6,7},{7,6},{8,9},{9,8},{10,11... | collective-permute-start | bytes 442376 | tf_op jit(solution)/shard_map/ppermute | solution.py:661
  16.7 3.8 %collective-permute-done.4.far_ref = bf16[4,144,128]{2,1,0:T(8,128)(2,1)S(1)} collective-permute-done((bf16[4,144,128]{2,1,0:T(8,128)(2,1)S(1)}, bf16[4,144,128]{2,1,0:T(8,128)(2,1)S(1)}, u32[]{:S(2)}, u32[]{:S(2)}) %collective-permute-start.4) | collective-permute-done | bytes 147488 | tf_op jit(solution)/shard_map/ppermute | solution.py:661
  20.5 0.0 collective-permute-start.6
  20.6 1.8 %collective-permute-start.3 = (bf16[4,128,128]{2,1,0:T(8,128)(2,1)S(1)}, bf16[4,128,128]{2,1,0:T(8,128)(2,1)S(1)}, u32[]{:S(2)}, u32[]{:S(2)}) collective-permute-start(bf16[4,128,128]{2,1,0:T(8,128)(2,1)S(1)} %pad_maximum_fusion.1.near_ref), channel_id=1, source_target_pairs={{0,1},{1,0},{2,3},{3,2},{4,5},{5,4},{6,7},{7,6},{8,9},{9,8},{10,11... | collective-permute-start | bytes 393224 | tf_op jit(solution)/shard_map/ppermute | solution.py:661
  22.4 0.1 copy.19
  22.5 0.0 collective-permute-done.5.other_near_ref
  22.5 0.0 collective-permute-done.6.other_far_ref
  22.5 0.0 copy-start.1
  22.5 0.0 copy-start.2
  22.5 2.8 %outer_products.1 = (bf16[512,1024]{1,0:T(8,128)(2,1)S(1)}, f32[512,128]{1,0:T(8,128)S(1)}, f32[512,128]{1,0:T(8,128)S(1)}, bf16[512,128]{1,0:T(8,128)(2,1)S(1)}...) custom-call(s32[2]{0:T(128)S(1)} %pad_add_fusion.ids_ref, ...), custom_call_target="tpu_custom_call" | custom-call | tf_op jit(solution)/shard_map/outer_products/pallas_call | solution.py:751
  25.3 1.2 %collective-permute-done.3.far_ref = bf16[4,128,128]{2,1,0:T(8,128)(2,1)S(1)} collective-permute-done((bf16[4,128,128]{2,1,0:T(8,128)(2,1)S(1)}, bf16[4,128,128]{2,1,0:T(8,128)(2,1)S(1)}, u32[]{:S(2)}, u32[]{:S(2)}) %collective-permute-start.3) | collective-permute-done | bytes 131104 | tf_op jit(solution)/shard_map/ppermute | solution.py:661
  26.5 0.6 %copy-done.6 = f32[128]{0:T(128)S(1)} copy-done((f32[128]{0:T(128)S(1)}, f32[128]{0:T(128)}, u32[]{:S(2)}) %copy-start.6) | copy-done | bytes 536
  27.2 2.4 %transition.1 = (bf16[64,128]{1,0:T(8,128)(2,1)}, bf16[512,128]{1,0:T(8,128)(2,1)S(1)}, bf16[512,128]{1,0:T(8,128)(2,1)S(1)}, bf16[512,512]{1,0:T(8,128)(2,1)S(1...) custom-call(s32[2]{0:T(128)S(1)} %pad_add_fusion.ids_ref, ...), custom_call_target="tpu_custom_call" | custom-call | tf_op jit(solution)/shard_map/transition/pallas_call | solution.py:775
  29.6 0.8 %out_weight.1 = bf16[1024,128]{1,0:T(8,128)(2,1)S(1)} custom-call(bf16[512,1024]{1,0:T(8,128)(2,1)S(1)} %get-tuple-element.40.outer_ref, bf16[512,128]{1,0:T(8,128)(2,1)S(1)} %get-tuple-element.39.opm_ref), custom_call_target="tpu_custom_call" | custom-call | tf_op jit(solution)/shard_map/out_weight/pallas_call | solution.py:804
  30.4 0.6 %collective-permute-done.7.other_opm_ref = bf16[512,128]{1,0:T(8,128)(2,1)S(1)} collective-permute-done((bf16[512,128]{1,0:T(8,128)(2,1)S(1)}, bf16[512,128]{1,0:T(8,128)(2,1)S(1)}, u32[]{:S(2)}, u32[]{:S(2)}) %collective-permute-start.7) | collective-permute-done | bytes 131104 | tf_op jit(solution)/shard_map/ppermute | solution.py:650
  30.9 1.6 %projector_parts.1 = (bf16[64,256]{1,0:T(8,128)(2,1)S(1)}, bf16[256,256]{1,0:T(8,128)(2,1)S(1)}) custom-call(s32[2]{0:T(128)S(1)} %pad_add_fusion.ids_ref, bf16[512,128]{1,0:T(8,128)(2,1)S(1)} %get-tuple-element.39.opm_ref, bf16[512,128]{1,0:T(8,128)(2,1)S(1)} %collective-permute-done.7.other_opm_ref, bf16[1024,128]{1,0:T(8,128)(2,1)S(1)} %get-tuple-element.42.rightt_ref, ...), custom_call_target="tpu_custom_call" | custom-call | tf_op jit(solution)/shard_map/projector_parts/pallas_call | solution.py:814
  32.6 0.2 collective-permute-start.8
  32.7 1.1 %collective-permute-done.8 = bf16[64,256]{1,0:T(8,128)(2,1)S(1)} collective-permute-done((bf16[64,256]{1,0:T(8,128)(2,1)S(1)}, bf16[64,256]{1,0:T(8,128)(2,1)S(1)}, u32[]{:S(2)}, u32[]{:S(2)}) %collective-permute-start.8) | collective-permute-done | bytes 32800 | tf_op jit(solution)/shard_map/ppermute | solution.py:650
  33.8 2.6 %collective-permute-start.11 = (bf16[64,256]{1,0:T(8,128)(2,1)S(1)}, bf16[64,256]{1,0:T(8,128)(2,1)S(1)}, u32[]{:S(2)}, u32[]{:S(2)}) collective-permute-start(bf16[64,256]{1,0:T(8,128)(2,1)S(1)} %add_convert_fusion.1), channel_id=1, source_target_pairs={{0,6},{1,7},{2,4},{3,5},{4,2},{5,3},{6,0},{7,1},{8,14},{9,15},{10,... | collective-permute-start | bytes 98312 | tf_op jit(solution)/shard_map/ppermute | solution.py:661
  36.4 1.9 %collective-permute-start.9 = (bf16[64,256]{1,0:T(8,128)(2,1)S(1)}, bf16[64,256]{1,0:T(8,128)(2,1)S(1)}, u32[]{:S(2)}, u32[]{:S(2)}) collective-permute-start(bf16[64,256]{1,0:T(8,128)(2,1)S(1)} %add_convert_fusion.1), channel_id=1, source_target_pairs={{0,2},{1,3},{2,0},{3,1},{4,6},{5,7},{6,4},{7,5},{8,10},{9,11},{10,... | collective-permute-start | bytes 98312 | tf_op jit(solution)/shard_map/ppermute | solution.py:661
  38.3 0.4 transition_weights.1
  38.7 0.9 %collective-permute-done.11 = bf16[64,256]{1,0:T(8,128)(2,1)S(1)} collective-permute-done((bf16[64,256]{1,0:T(8,128)(2,1)S(1)}, bf16[64,256]{1,0:T(8,128)(2,1)S(1)}, u32[]{:S(2)}, u32[]{:S(2)}) %collective-permute-start.11) | collective-permute-done | bytes 32800 | tf_op jit(solution)/shard_map/ppermute | solution.py:661
  39.6 1.6 %collective-permute-done.10 = bf16[64,256]{1,0:T(8,128)(2,1)S(1)} collective-permute-done((bf16[64,256]{1,0:T(8,128)(2,1)S(1)}, bf16[64,256]{1,0:T(8,128)(2,1)S(1)}, u32[]{:S(2)}, u32[]{:S(2)}) %collective-permute-start.10) | collective-permute-done | bytes 32800 | tf_op jit(solution)/shard_map/ppermute | solution.py:661
  41.2 0.0 collective-permute-done.9
  41.3 1.6 %collective-permute-start.12 = (bf16[64,256]{1,0:T(8,128)(2,1)S(1)}, bf16[64,256]{1,0:T(8,128)(2,1)S(1)}, u32[]{:S(2)}, u32[]{:S(2)}) collective-permute-start(bf16[64,256]{1,0:T(8,128)(2,1)S(1)} %add_convert_fusion), channel_id=1, source_target_pairs={{0,1},{1,0},{2,3},{3,2},{4,5},{5,4},{6,7},{7,6},{8,9},{9,8},{10,11... | collective-permute-start | bytes 98312 | tf_op jit(solution)/shard_map/ppermute | solution.py:661
  42.8 0.7 %copy-done.5 = f32[256]{0:T(256)S(1)} copy-done((f32[256]{0:T(256)S(1)}, f32[256]{0:T(256)}, u32[]{:S(2)}) %copy-start.5) | copy-done | bytes 1048
  43.5 0.3 features.1
  43.8 0.7 %reshape.44 = bf16[64,4,256]{2,1,0:T(4,128)(2,1)} reshape(bf16[256,256]{1,0:T(8,128)(2,1)S(1)} %features.1) | data formatting | bytes 262144 | tf_op jit(solution)/shard_map/reshape | solution.py:860
  44.5 0.5 %collective-permute-start.14 = (bf16[128,512]{1,0:T(8,128)(2,1)S(1)}, bf16[128,512]{1,0:T(8,128)(2,1)S(1)}, u32[]{:S(2)}, u32[]{:S(2)}) collective-permute-start(bf16[128,512]{1,0:T(8,128)(2,1)S(1)} %get-tuple-element.61), channel_id=1, source_target_pairs={{0,8},{8,0},{1,9},{9,1},{2,10},{10,2},{3,11},{11,3},{4,12},{12,4},... | collective-permute-start | bytes 393224 | tf_op jit(solution)/shard_map/ppermute | solution.py:650
  45.0 0.2 collective-permute-done.12
  45.3 0.6 %slice_bitcast_fusion = (f32[256,32]{0,1:T(8,128)}, f32[256,32]{0,1:T(8,128)}) fusion(f32[64,256]{1,0:T(8,128)S(1)} %convert_add_fusion.3), kind=kLoop, calls=%fused_computation.8 | loop fusion | bytes 131072 | tf_op jit(solution)/shard_map/transpose | solution.py:863
  45.9 0.4 collective-permute-done.14
  46.3 0.7 %convert_add_fusion.2 = f32[128,512]{1,0:T(8,128)} fusion(bf16[128,512]{1,0:T(8,128)(2,1)S(1)} %collective-permute-done.14, bf16[128,512]{1,0:T(8,128)(2,1)S(1)} %get-tuple-element.61), kind=kLoop, calls=%fused_computation.2 | loop fusion | flops 196608 | bytes 524288 | tf_op jit(solution)/shard_map/add | solution.py:857
  47.0 0.7 %convert_add_fusion.1 = f32[512,128]{1,0:T(8,128)} fusion(bf16[512,128]{1,0:T(8,128)(2,1)S(1)} %collective-permute-done.15, bf16[512,128]{1,0:T(8,128)(2,1)S(1)} %get-tuple-element.62), kind=kLoop, calls=%fused_computation.1 | loop fusion | flops 196608 | bytes 524288 | tf_op jit(solution)/shard_map/add | solution.py:857
  47.7 0.0 collective-permute-done.13
  47.7 0.9 %convert_add_fusion = f32[1024,128]{1,0:T(8,128)} fusion(bf16[1024,128]{1,0:T(8,128)(2,1)S(1)} %collective-permute-done.13, bf16[1024,128]{1,0:T(8,128)(2,1)S(1)} %out_weight.1), kind=kLoop, calls=%fused_computation | loop fusion | flops 393216 | bytes 1048576 | tf_op jit(solution)/shard_map/add | solution.py:857
  (33 shorter events, 0.1 us)
Async XLA Ops:
  2.6 7.8 %collective-permute-start.2 = (bf16[1,272,128]{2,1,0:T(8,128)(2,1)S(1)}, bf16[1,272,128]{2,1,0:T(8,128)(2,1)S(1)}, u32[]{:S(2)}, u32[]{:S(2)}) collective-permute-start(bf16[1,272,128]{2,1,0:T(8,128)(2,1)S(1)} %get-tuple-element.35), channel_id=1, source_target_pairs={{0,6},{1,7},{2,4},{3,5},{4,2},{5,3},{6,0},{7,1},{8,14},{9,15},{10,... | collective-permute-start | bytes 208904 | tf_op jit(solution)/shard_map/ppermute | solution.py:661
  7.7 5.9 %collective-permute-start.1 = (bf16[1,272,128]{2,1,0:T(8,128)(2,1)S(1)}, bf16[1,272,128]{2,1,0:T(8,128)(2,1)S(1)}, u32[]{:S(2)}, u32[]{:S(2)}) collective-permute-start(bf16[1,272,128]{2,1,0:T(8,128)(2,1)S(1)} %get-tuple-element.35), channel_id=1, source_target_pairs={{0,4},{1,5},{2,6},{3,7},{4,0},{5,1},{6,2},{7,3},{8,12},{9,13},{10,... | collective-permute-start | bytes 208904 | tf_op jit(solution)/shard_map/ppermute | solution.py:661
  7.7 6.5 %collective-permute-start = (bf16[1,272,128]{2,1,0:T(8,128)(2,1)S(1)}, bf16[1,272,128]{2,1,0:T(8,128)(2,1)S(1)}, u32[]{:S(2)}, u32[]{:S(2)}) collective-permute-start(bf16[1,272,128]{2,1,0:T(8,128)(2,1)S(1)} %get-tuple-element.35), channel_id=1, source_target_pairs={{0,2},{1,3},{2,0},{3,1},{4,6},{5,7},{6,4},{7,5},{8,10},{9,11},{10,... | collective-permute-start | bytes 208904 | tf_op jit(solution)/shard_map/ppermute | solution.py:661
  10.4 3.2 %copy-start.7 = (bf16[1,272,128]{2,1,0:T(8,128)(2,1)}, bf16[1,272,128]{2,1,0:T(8,128)(2,1)S(1)}, u32[]{:S(2)}) copy-start(bf16[1,272,128]{2,1,0:T(8,128)(2,1)S(1)} %collective-permute-done.2) | copy-start | bytes 208900
  13.6 0.6 %copy-start.8 = (bf16[1,272,128]{2,1,0:T(8,128)(2,1)}, bf16[1,272,128]{2,1,0:T(8,128)(2,1)S(1)}, u32[]{:S(2)}) copy-start(bf16[1,272,128]{2,1,0:T(8,128)(2,1)S(1)} %collective-permute-done.1) | copy-start | bytes 208900
  14.3 0.8 %slice-start = ((bf16[1,272,128]{2,1,0:T(8,128)(2,1)}), bf16[1,144,128]{2,1,0:T(8,128)(2,1)S(1)}, s32[]{:S(2)}) async-start(bf16[1,272,128]{2,1,0:T(8,128)(2,1)} %copy-done.7), calls=%async_computation | async-start | bytes 73728 | tf_op jit(solution)/shard_map/slice | solution.py:745
  14.3 0.8 %slice-start.2 = ((bf16[1,272,128]{2,1,0:T(8,128)(2,1)}), bf16[1,144,128]{2,1,0:T(8,128)(2,1)S(1)}, s32[]{:S(2)}) async-start(bf16[1,272,128]{2,1,0:T(8,128)(2,1)} %copy-done.8), calls=%async_computation.2 | async-start | bytes 73728 | tf_op jit(solution)/shard_map/slice | solution.py:745
  15.1 5.5 %slice-start.1 = ((bf16[1,272,128]{2,1,0:T(8,128)(2,1)}), bf16[1,128,128]{2,1,0:T(8,128)(2,1)S(1)}, s32[]{:S(2)}) async-start(bf16[1,272,128]{2,1,0:T(8,128)(2,1)} %copy-done.7), calls=%async_computation.1 | async-start | bytes 65536 | tf_op jit(solution)/shard_map/slice | solution.py:746
  15.1 5.5 %slice-start.3 = ((bf16[1,272,128]{2,1,0:T(8,128)(2,1)}), bf16[1,128,128]{2,1,0:T(8,128)(2,1)S(1)}, s32[]{:S(2)}) async-start(bf16[1,272,128]{2,1,0:T(8,128)(2,1)} %copy-done.8), calls=%async_computation.3 | async-start | bytes 65536 | tf_op jit(solution)/shard_map/slice | solution.py:746
  15.1 7.3 %copy-start = (bf16[1024,128]{1,0:T(8,128)(2,1)S(1)}, bf16[1024,128]{1,0:T(8,128)(2,1)}, u32[]{:S(2)}) copy-start(bf16[1024,128]{1,0:T(8,128)(2,1)} %wout_ref.1) | copy-start | bytes 786436
  15.1 5.4 %collective-permute-start.4 = (bf16[4,144,128]{2,1,0:T(8,128)(2,1)S(1)}, bf16[4,144,128]{2,1,0:T(8,128)(2,1)S(1)}, u32[]{:S(2)}, u32[]{:S(2)}) collective-permute-start(bf16[4,144,128]{2,1,0:T(8,128)(2,1)S(1)} %pad_maximum_fusion.near_ref), channel_id=1, source_target_pairs={{0,1},{1,0},{2,3},{3,2},{4,5},{5,4},{6,7},{7,6},{8,9},{9,8},{10,11... | collective-permute-start | bytes 442376 | tf_op jit(solution)/shard_map/ppermute | solution.py:661
  16.7 5.8 %collective-permute-start.5 = (bf16[4,144,128]{2,1,0:T(8,128)(2,1)S(1)}, bf16[4,144,128]{2,1,0:T(8,128)(2,1)S(1)}, u32[]{:S(2)}, u32[]{:S(2)}) collective-permute-start(bf16[4,144,128]{2,1,0:T(8,128)(2,1)S(1)} %pad_maximum_fusion.near_ref), channel_id=1, source_target_pairs={{0,8},{8,0},{1,9},{9,1},{2,10},{10,2},{3,11},{11,3},{4,12},{12,4},... | collective-permute-start | bytes 442376 | tf_op jit(solution)/shard_map/ppermute | solution.py:650
  20.5 2.0 %collective-permute-start.6 = (bf16[4,144,128]{2,1,0:T(8,128)(2,1)S(1)}, bf16[4,144,128]{2,1,0:T(8,128)(2,1)S(1)}, u32[]{:S(2)}, u32[]{:S(2)}) collective-permute-start(bf16[4,144,128]{2,1,0:T(8,128)(2,1)S(1)} %collective-permute-done.4.far_ref), channel_id=1, source_target_pairs={{0,8},{8,0},{1,9},{9,1},{2,10},{10,2},{3,11},{11,3},{4,12},{12,4},... | collective-permute-start | bytes 442376 | tf_op jit(solution)/shard_map/ppermute | solution.py:650
  20.6 6.0 %collective-permute-start.3 = (bf16[4,128,128]{2,1,0:T(8,128)(2,1)S(1)}, bf16[4,128,128]{2,1,0:T(8,128)(2,1)S(1)}, u32[]{:S(2)}, u32[]{:S(2)}) collective-permute-start(bf16[4,128,128]{2,1,0:T(8,128)(2,1)S(1)} %pad_maximum_fusion.1.near_ref), channel_id=1, source_target_pairs={{0,1},{1,0},{2,3},{3,2},{4,5},{5,4},{6,7},{7,6},{8,9},{9,8},{10,11... | collective-permute-start | bytes 393224 | tf_op jit(solution)/shard_map/ppermute | solution.py:661
  22.5 4.0 %copy-start.1 = (bf16[128,512]{1,0:T(8,128)(2,1)S(1)}, bf16[128,512]{1,0:T(8,128)(2,1)}, u32[]{:S(2)}) copy-start(bf16[128,512]{1,0:T(8,128)(2,1)} %hid_ref.1) | copy-start | bytes 393220
  22.5 4.0 %copy-start.2 = (bf16[512,128]{1,0:T(8,128)(2,1)S(1)}, bf16[512,128]{1,0:T(8,128)(2,1)}, u32[]{:S(2)}) copy-start(bf16[512,128]{1,0:T(8,128)(2,1)} %back_ref.1) | copy-start | bytes 393220
  26.5 0.7 %copy-start.6 = (f32[128]{0:T(128)S(1)}, f32[128]{0:T(128)}, u32[]{:S(2)}) copy-start(f32[128]{0:T(128)} %param.21) | copy-start | bytes 1540
  29.6 1.3 %collective-permute-start.7 = (bf16[512,128]{1,0:T(8,128)(2,1)S(1)}, bf16[512,128]{1,0:T(8,128)(2,1)S(1)}, u32[]{:S(2)}, u32[]{:S(2)}) collective-permute-start(bf16[512,128]{1,0:T(8,128)(2,1)S(1)} %get-tuple-element.39.opm_ref), channel_id=1, source_target_pairs={{0,8},{8,0},{1,9},{9,1},{2,10},{10,2},{3,11},{11,3},{4,12},{12,4},... | collective-permute-start | bytes 393224 | tf_op jit(solution)/shard_map/ppermute | solution.py:650
  32.6 1.2 %collective-permute-start.8 = (bf16[64,256]{1,0:T(8,128)(2,1)S(1)}, bf16[64,256]{1,0:T(8,128)(2,1)S(1)}, u32[]{:S(2)}, u32[]{:S(2)}) collective-permute-start(bf16[64,256]{1,0:T(8,128)(2,1)S(1)} %get-tuple-element.50), channel_id=1, source_target_pairs={{0,8},{8,0},{1,9},{9,1},{2,10},{10,2},{3,11},{11,3},{4,12},{12,4},... | collective-permute-start | bytes 98312 | tf_op jit(solution)/shard_map/ppermute | solution.py:650
  33.8 5.8 %collective-permute-start.11 = (bf16[64,256]{1,0:T(8,128)(2,1)S(1)}, bf16[64,256]{1,0:T(8,128)(2,1)S(1)}, u32[]{:S(2)}, u32[]{:S(2)}) collective-permute-start(bf16[64,256]{1,0:T(8,128)(2,1)S(1)} %add_convert_fusion.1), channel_id=1, source_target_pairs={{0,6},{1,7},{2,4},{3,5},{4,2},{5,3},{6,0},{7,1},{8,14},{9,15},{10,... | collective-permute-start | bytes 98312 | tf_op jit(solution)/shard_map/ppermute | solution.py:661
  36.4 4.8 %collective-permute-start.10 = (bf16[64,256]{1,0:T(8,128)(2,1)S(1)}, bf16[64,256]{1,0:T(8,128)(2,1)S(1)}, u32[]{:S(2)}, u32[]{:S(2)}) collective-permute-start(bf16[64,256]{1,0:T(8,128)(2,1)S(1)} %add_convert_fusion.1), channel_id=1, source_target_pairs={{0,4},{1,5},{2,6},{3,7},{4,0},{5,1},{6,2},{7,3},{8,12},{9,13},{10,... | collective-permute-start | bytes 98312 | tf_op jit(solution)/shard_map/ppermute | solution.py:661
  36.4 4.8 %collective-permute-start.9 = (bf16[64,256]{1,0:T(8,128)(2,1)S(1)}, bf16[64,256]{1,0:T(8,128)(2,1)S(1)}, u32[]{:S(2)}, u32[]{:S(2)}) collective-permute-start(bf16[64,256]{1,0:T(8,128)(2,1)S(1)} %add_convert_fusion.1), channel_id=1, source_target_pairs={{0,2},{1,3},{2,0},{3,1},{4,6},{5,7},{6,4},{7,5},{8,10},{9,11},{10,... | collective-permute-start | bytes 98312 | tf_op jit(solution)/shard_map/ppermute | solution.py:661
  41.2 1.6 %copy-start.3 = (bf16[256,32]{0,1:T(8,128)(2,1)S(1)}, bf16[256,32]{0,1:T(8,128)(2,1)}, u32[]{:S(2)}) copy-start(bf16[256,32]{0,1:T(8,128)(2,1)} %param.18) | copy-start | bytes 49156
  41.2 1.6 %copy-start.4 = (bf16[256,32]{0,1:T(8,128)(2,1)S(1)}, bf16[256,32]{0,1:T(8,128)(2,1)}, u32[]{:S(2)}) copy-start(bf16[256,32]{0,1:T(8,128)(2,1)} %param.19) | copy-start | bytes 49156
  41.3 4.0 %collective-permute-start.12 = (bf16[64,256]{1,0:T(8,128)(2,1)S(1)}, bf16[64,256]{1,0:T(8,128)(2,1)S(1)}, u32[]{:S(2)}, u32[]{:S(2)}) collective-permute-start(bf16[64,256]{1,0:T(8,128)(2,1)S(1)} %add_convert_fusion), channel_id=1, source_target_pairs={{0,1},{1,0},{2,3},{3,2},{4,5},{5,4},{6,7},{7,6},{8,9},{9,8},{10,11... | collective-permute-start | bytes 98312 | tf_op jit(solution)/shard_map/ppermute | solution.py:661
  42.8 0.7 %copy-start.5 = (f32[256]{0:T(256)S(1)}, f32[256]{0:T(256)}, u32[]{:S(2)}) copy-start(f32[256]{0:T(256)} %param.17) | copy-start | bytes 3076
  44.5 3.2 %collective-permute-start.13 = (bf16[1024,128]{1,0:T(8,128)(2,1)S(1)}, bf16[1024,128]{1,0:T(8,128)(2,1)S(1)}, u32[]{:S(2)}, u32[]{:S(2)}) collective-permute-start(bf16[1024,128]{1,0:T(8,128)(2,1)S(1)} %out_weight.1), channel_id=1, source_target_pairs={{0,8},{8,0},{1,9},{9,1},{2,10},{10,2},{3,11},{11,3},{4,12},{12,4},... | collective-permute-start | bytes 786440 | tf_op jit(solution)/shard_map/ppermute | solution.py:650
  44.5 1.7 %collective-permute-start.14 = (bf16[128,512]{1,0:T(8,128)(2,1)S(1)}, bf16[128,512]{1,0:T(8,128)(2,1)S(1)}, u32[]{:S(2)}, u32[]{:S(2)}) collective-permute-start(bf16[128,512]{1,0:T(8,128)(2,1)S(1)} %get-tuple-element.61), channel_id=1, source_target_pairs={{0,8},{8,0},{1,9},{9,1},{2,10},{10,2},{3,11},{11,3},{4,12},{12,4},... | collective-permute-start | bytes 393224 | tf_op jit(solution)/shard_map/ppermute | solution.py:650
  45.0 2.0 %collective-permute-start.15 = (bf16[512,128]{1,0:T(8,128)(2,1)S(1)}, bf16[512,128]{1,0:T(8,128)(2,1)S(1)}, u32[]{:S(2)}, u32[]{:S(2)}) collective-permute-start(bf16[512,128]{1,0:T(8,128)(2,1)S(1)} %get-tuple-element.62), channel_id=1, source_target_pairs={{0,8},{8,0},{1,9},{9,1},{2,10},{10,2},{3,11},{11,3},{4,12},{12,4},... | collective-permute-start | bytes 393224 | tf_op jit(solution)/shard_map/ppermute | solution.py:650

commit v2 on v1

--- a/solution.py
+++ b/solution.py
@@ -284,9 +284,15 @@
     scale_hbm,
     first_hbm,
     second_hbm,
+    gain_hbm,
     act_hbm,
     grad_hbm,
     sent_ref,
+    pairs_ref,
+    scale_ref,
+    first_ref,
+    second_ref,
+    gain_ref,
     normed_ref,
     scaled_ref,
     inv_ref,
@@ -296,14 +302,10 @@
     x_ref,
     maskt_ref,
     pmask_ref,
-    scale_ref,
-    first_ref,
-    second_ref,
     sems,
 ):
     res, seqs = maskt_ref.shape
     pairs = act_hbm.shape[0]
-    first_pair = 2 * seqs + MASK_ROWS
     copies = [
         pltpu.make_async_copy(source, target, sems.at[at])
         for at, (source, target) in enumerate(
@@ -314,8 +316,9 @@
                 (scale_hbm, scale_ref),
                 (first_hbm, first_ref),
                 (second_hbm, second_ref),
-                (act_hbm, sent_ref.at[0, pl.ds(first_pair, pairs), :]),
-                (grad_hbm, sent_ref.at[0, pl.ds(first_pair + pairs, pairs), :]),
+                (gain_hbm, gain_ref),
+                (act_hbm, pairs_ref.at[0, pl.ds(0, pairs), :]),
+                (grad_hbm, pairs_ref.at[0, pl.ds(pairs, pairs), :]),
             )
         )
     ]
@@ -363,7 +366,7 @@
                 lane_group == r, wide_ref[at, pl.ds(r, seqs, stride=res), :], both
             )
         sent_ref[0, at * seqs : (at + 1) * seqs, :] = (both * mask_lanes).astype(jnp.bfloat16)
-    sent_ref[0, 2 * seqs : first_pair, :] = tile_ref[...].astype(jnp.bfloat16)
+    sent_ref[0, 2 * seqs :, :] = tile_ref[...].astype(jnp.bfloat16)
 
 
 def outer_kernel(
@@ -379,8 +382,6 @@
     proj_out_ref,
     cnt_ref,
     pm_ref,
-    rightt_ref,
-    leftt_ref,
     got_ref,
     leftn_ref,
     mine_ref,
@@ -408,14 +409,6 @@
             leftn_ref[e * seqs : (e + 1) * seqs, k * lanes : (k + 1) * lanes] = got_ref[
                 e, k, 0:seqs, :
             ]
-    for at, out in ((0, leftt_ref), (1, rightt_ref)):
-        for k in range(cols):
-            block = got_ref[me_depth, k, at * seqs : (at + 1) * seqs, :].astype(f32)
-            turn_ref[k * lanes : (k + 1) * lanes, 0:seqs] = block.T
-        for d in range(width):
-            out[d * residues : (d + 1) * residues, :] = turn_ref[
-                pl.ds(d, residues, stride=width), :
-            ].astype(bf16)
     for k in range(half_cols):
         block = jnp.concatenate(
             [
@@ -470,6 +463,24 @@
                     il
                 ].astype(bf16)
     proj_out_ref[...] = jnp.dot(outer_ref[...], wturn_ref[...], preferred_element_type=f32)
+
+
+def turn_kernel(sizes, orders, ids_ref, near_ref, far_ref, rightt_ref, leftt_ref, turn_ref):
+    seqs, res, _, width = sizes
+    lanes = res * width
+    residues = turn_ref.shape[0] // width
+    me_col = ids_ref[1]
+    for at, out in ((0, leftt_ref), (1, rightt_ref)):
+        for order, blocks in zip(orders, (near_ref, far_ref)):
+            for place, partner in enumerate(order):
+                block = blocks[place, at * seqs : (at + 1) * seqs, :].astype(jnp.float32)
+                block = jnp.concatenate([block] * (lanes // seqs), axis=0)
+                first = pl.multiple_of((me_col ^ partner) * lanes, lanes)
+                turn_ref[pl.ds(first, lanes), :] = block.T
+        for d in range(width):
+            out[d * residues : (d + 1) * residues, :] = turn_ref[
+                pl.ds(d, residues, stride=width), :
+            ].astype(jnp.bfloat16)
 
 
 def transition_kernel(
@@ -633,6 +644,11 @@
         ).astype(jnp.bfloat16)
 
 
+def sum_kernel(*refs):
+    for mine, other, out in zip(refs[0:3], refs[3:6], refs[6:9]):
+        out[...] = mine[...].astype(jnp.float32) + other[...].astype(jnp.float32)
+
+
 def feature_kernel(
     copies, spread_ref, first_ref, second_ref, scale_ref, scaled_ref, inv_ref, feat_ref
 ):
@@ -659,6 +675,16 @@
 def swap_col(block, partner):
     count = lax.axis_size("col")
     return lax.ppermute(block, "col", [(at, at ^ partner) for at in range(count)])
+
+
+def swap_both(block, partner):
+    count = lax.axis_size("col")
+    pairs = [
+        (depth * count + at, (1 - depth) * count + (at ^ partner))
+        for depth in range(2)
+        for at in range(count)
+    ]
+    return lax.ppermute(block, ("depth", "col"), pairs)
 
 
 def whole_plan(
@@ -685,41 +711,42 @@
     hid = hidden_weight.shape[1]
     per = res * pair_cols
     lanes = res * width
-    near_rows = 2 * seqs + MASK_ROWS
-    rows = near_rows + 2 * per
+    rows = 2 * seqs + MASK_ROWS
     half = residues * pair_cols
     f32, bf16 = jnp.float32, jnp.bfloat16
     ids = jnp.stack([lax.axis_index("depth"), lax.axis_index("col")]).astype(jnp.int32)
     smem = pl.BlockSpec(memory_space=pltpu.SMEM)
     vmem = pl.BlockSpec(memory_space=pltpu.VMEM)
-    params = pltpu.CompilerParams(vmem_limit_bytes=40 * 2**20)
+    params = pltpu.CompilerParams(vmem_limit_bytes=16 * 2**20)
     scale = layer_scale_factor.reshape(1, channels)
     first, second = first_projector.T, second_projector.T
     wturn = jnp.transpose(output_weight.reshape(width, width, pair_width), (1, 0, 2)).reshape(
         outer_width, pair_width
     )
     shape = jax.ShapeDtypeStruct
-    sent, normed, scaled, inv, mask_lanes = pl.pallas_call(
+    sent, sent_pairs, scale, first, second, gain, normed, scaled, inv, mask_lanes = pl.pallas_call(
         pre_kernel,
         out_shape=(
             shape((1, rows, pair_width), bf16),
+            shape((1, 2 * per, pair_width), bf16),
+            shape((1, channels), f32),
+            shape((width, channels), bf16),
+            shape((width, channels), bf16),
+            shape((1, pair_width), f32),
             shape((seqs * res, channels), bf16),
             shape((seqs * res, channels), f32),
             shape((seqs * res, 1), f32),
             shape((seqs, lanes), f32),
         ),
-        in_specs=[smem] + [pl.BlockSpec(memory_space=pltpu.HBM)] * 8,
-        out_specs=[vmem] * 5,
+        in_specs=[smem] + [pl.BlockSpec(memory_space=pltpu.HBM)] * 9,
+        out_specs=[vmem] * 10,
         scratch_shapes=[
             pltpu.VMEM((2, seqs * res, lanes), f32),
             pltpu.VMEM((MASK_ROWS, lanes), f32),
             pltpu.VMEM((seqs, res, channels), bf16),
             pltpu.VMEM((res, seqs), jnp.int32),
             pltpu.VMEM((res, pair_cols), jnp.int32),
-            pltpu.VMEM((1, channels), f32),
-            pltpu.VMEM((width, channels), bf16),
-            pltpu.VMEM((width, channels), bf16),
-            pltpu.SemaphoreType.DMA((8,)),
+            pltpu.SemaphoreType.DMA((9,)),
         ],
         compiler_params=params,
         name="project",
@@ -734,6 +761,7 @@
                 scale,
                 first,
                 second,
+                pair_norm_gain.reshape(1, pair_width),
                 pair_activation_input.reshape(per, pair_width),
                 pair_output_gradient.reshape(per, pair_width),
             )
@@ -741,30 +769,31 @@
     )
     near_order = (0,) + Z_PARTNERS
     far_order = tuple(at ^ Y_PARTNER for at in near_order)
-    blocks = [sent] + [swap_col(sent, partner) for partner in Z_PARTNERS]
-    near = jnp.concatenate([block[:, :near_rows] for block in blocks])
-    pair_near = jnp.concatenate([block[:, near_rows:] for block in blocks])
+    came = [swap_col(sent, partner) for partner in Z_PARTNERS]
+    came[0], sent_pairs = lax.optimization_barrier((came[0], sent_pairs))
+    near = jnp.concatenate([sent] + came)
+    pair_near = jnp.concatenate(
+        [sent_pairs] + [swap_col(sent_pairs, partner) for partner in Z_PARTNERS]
+    )
     far = swap_col(near, Y_PARTNER)
     pair_far = swap_col(pair_near, Y_PARTNER)
     sizes = (seqs, res, pair_cols, width)
     orders = (near_order, far_order)
-    outer, proj_out, cnt, pm, rightt, leftt = pl.pallas_call(
+    outer, proj_out, cnt, pm = pl.pallas_call(
         functools.partial(outer_kernel, sizes, orders),
         out_shape=(
             shape((half, outer_width), bf16),
             shape((half, pair_width), f32),
             shape((half, lanes), f32),
             shape((half, lanes), bf16),
-            shape((residues * width, depths * seqs), bf16),
-            shape((residues * width, depths * seqs), bf16),
         ),
         in_specs=[smem] + [vmem] * 5,
-        out_specs=[vmem] * 6,
+        out_specs=[vmem] * 4,
         scratch_shapes=[
-            pltpu.VMEM((depths, cols, near_rows, pair_width), bf16),
+            pltpu.VMEM((depths, cols, rows, pair_width), bf16),
             pltpu.VMEM((depths * seqs, residues * width), bf16),
             pltpu.VMEM((pair_cols * width, depths * seqs), bf16),
-            pltpu.VMEM((residues * width, depths * seqs), f32),
+            pltpu.VMEM((pair_cols * width, depths * seqs), f32),
             pltpu.VMEM((residues, depths * seqs), f32),
             pltpu.VMEM((half, lanes), bf16),
             pltpu.VMEM((half, lanes), bf16),
@@ -772,6 +801,22 @@
         compiler_params=params,
         name="outer_products",
     )(ids, near, far, swap_depth(near), swap_depth(far), wturn)
+    near, far, proj_out = lax.optimization_barrier((near, far, proj_out))
+    rightt, leftt = pl.pallas_call(
+        functools.partial(turn_kernel, sizes, orders),
+        out_shape=(
+            shape((residues * width, depths * seqs), bf16),
+            shape((residues * width, depths * seqs), bf16),
+        ),
+        in_specs=[smem] + [vmem] * 2,
+        out_specs=[vmem] * 2,
+        scratch_shapes=[pltpu.VMEM((residues * width, depths * seqs), f32)],
+        compiler_params=params,
+        name="turned",
+    )(ids, near, far)
+    pair_far, rightt, leftt, proj_out = lax.optimization_barrier(
+        (pair_far, rightt, leftt, proj_out)
+    )
     couple, opm, pn, gh, hidden, mg = pl.pallas_call(
         functools.partial(transition_kernel, sizes, orders),
         out_shape=(
@@ -797,7 +842,7 @@
         proj_out,
         cnt,
         pm,
-        pair_norm_gain.reshape(1, pair_width),
+        gain,
         hidden_weight,
         back_weight,
     )
@@ -810,7 +855,16 @@
         compiler_params=params,
         name="out_weight",
     )(outer, opm)
-    other_opm, dout = lax.optimization_barrier((swap_depth(opm), dout))
+    dhid, dback = pl.pallas_call(
+        transition_weight_kernel,
+        out_shape=(shape((pair_width, hid), bf16), shape((hid, pair_width), bf16)),
+        in_specs=[vmem] * 4,
+        out_specs=[vmem] * 2,
+        compiler_params=params,
+        name="transition_weights",
+    )(pn, gh, hidden, mg)
+    other_opm, dout, dhid, dback = lax.optimization_barrier((swap_depth(opm), dout, dhid, dback))
+    other_weights = [swap_depth(block) for block in (dout, dhid, dback)]
     part, spread = pl.pallas_call(
         functools.partial(projector_kernel, sizes),
         out_shape=(
@@ -838,24 +892,27 @@
         compiler_params=params,
         name="features",
     )(spread, first, second, scale, scaled, inv)
-    dhid, dback = pl.pallas_call(
-        transition_weight_kernel,
-        out_shape=(shape((pair_width, hid), bf16), shape((hid, pair_width), bf16)),
-        in_specs=[vmem] * 4,
-        out_specs=[vmem] * 2,
+    dout, dhid, dback = pl.pallas_call(
+        sum_kernel,
+        out_shape=(
+            shape((outer_width, pair_width), f32),
+            shape((pair_width, hid), f32),
+            shape((hid, pair_width), f32),
+        ),
+        in_specs=[vmem] * 6,
+        out_specs=[vmem] * 3,
         compiler_params=params,
-        name="transition_weights",
-    )(pn, gh, hidden, mg)
+        name="sums_over_depth",
+    )(dout, dhid, dback, *other_weights)
     total = part.astype(f32)
-    for partners in ((0,), Z_PARTNERS, (Y_PARTNER,)):
-        kept = lax.optimization_barrier(total.astype(bf16))
-        came = [swap_col(kept, at) if at else swap_depth(kept) for at in partners]
-        if partners == Z_PARTNERS:
-            came, dhid, dback = lax.optimization_barrier((came, dhid, dback))
-        total = pairwise_sum([block.astype(f32) for block in [kept] + came])
-    dout, dhid, dback = [
-        block.astype(f32) + swap_depth(block).astype(f32) for block in (dout, dhid, dback)
-    ]
+    kept = lax.optimization_barrier(total.astype(bf16))
+    near_ones = [swap_depth(kept), swap_col(kept, Y_PARTNER), swap_both(kept, Y_PARTNER)]
+    near_ones, feat = lax.optimization_barrier((near_ones, feat))
+    total = pairwise_sum([block.astype(f32) for block in [kept] + near_ones])
+    kept = lax.optimization_barrier(total.astype(bf16))
+    far_ones = [swap_col(kept, partner) for partner in Z_PARTNERS]
+    far_ones, dout, dhid, dback = lax.optimization_barrier((far_ones, dout, dhid, dback))
+    total = pairwise_sum([block.astype(f32) for block in [kept] + far_ones])
     return (
         feat.reshape(seqs, res, channels),
         couple.reshape(res, pair_cols, pair_width),

time: 48.9 us -> 47.5 us (0.971)
  starting transfers between devices: 15.9 us -> 20.7 us
  local copies, waits for them, and re-layouts: 4.21 us -> 1.51 us
  waiting for transfers between devices: 15 us -> 12.3 us
  other arithmetic: 2.49 us -> 0.11 us
  Pallas kernels: 10.2 us -> 11.9 us
    ppermute x9 -> x12, starting transfers between devices: 15.2 us -> 18.3 us  [swap_col(): lax.ppermute(block, 'col', [(at, at ^ partner) for at in range(count)])]
    add x3 -> x0, other arithmetic: 2.34 us -> none  [whole_plan(): block.astype(f32) + swap_depth(block).astype(f32)]
    pallas_call x0 -> x2, Pallas kernels: none -> 2.32 us  [the longest x1 1.31 us: whole_plan(): pl.pallas_call(functools.partial(turn_kernel, sizes, orders), out_shape=(...]
    unnamed x18 -> x12, local copies, waits for them, and re-layouts: 1.98 us -> 0.07 us
    ppermute x7, waiting for transfers between devices: 2.02 us -> 0.19 us  [swap_depth(): return lax.ppermute(block, 'depth', [(0, 1), (1, 0)])]
    ppermute x0 -> x1, starting transfers between devices: none -> 1.49 us  [swap_both(): return lax.ppermute(block, ('depth', 'col'), pairs)]
    ppermute x9 -> x12, waiting for transfers between devices: 13 us -> 11.6 us  [swap_col(): lax.ppermute(block, 'col', [(at, at ^ partner) for at in range(count)])]
    slice x12 -> x0, local copies, waits for them, and re-layouts: 0.8 us -> none  [the longest x6 0.79 us: whole_plan(): near = jnp.concatenate([block[:, :near_rows] for block in blocks])]
  transfers between devices with their start and end apart: 16 -> 20, of which waited for: 10 -> 9; matrix products, arithmetic and copies ran while one was open for 6% -> 2% of each run, Pallas kernels for 9% -> 13%
where the time goes in v2:
time: 47.5 us; the launch traced here: 47.3 us
  starting transfers between devices  20.7 us (44%)
  waiting for transfers between devices  12.3 us (26%)
  Pallas kernels  11.9 us (25%)
  local copies, waits for them, and re-layouts  1.51 us (3%)
  between operations  0.79 us (2%)
    ppermute x12, starting transfers between devices, swap_col(): lax.ppermute(block, 'col', [(at, at ^ partner) for at in range(count)])  18.3 us
    ppermute x12, waiting for transfers between devices, swap_col(): lax.ppermute(block, 'col', [(at, at ^ partner) for at in range(count)])  11.6 us
    pallas_call x1, Pallas kernels, whole_plan(): pl.pallas_call(functools.partial(transition_kernel, sizes, orders), out_s...  2.42 us
    pallas_call x1, Pallas kernels, whole_plan(): pl.pallas_call(functools.partial(outer_kernel, sizes, orders), out_shape=...  2.13 us
    pallas_call x1, Pallas kernels, whole_plan(): pl.pallas_call(pre_kernel, out_shape=(shape((1, rows, pair_width), bf16),...  1.91 us
    pallas_call x1, Pallas kernels, whole_plan(): pl.pallas_call(functools.partial(projector_kernel, sizes), out_shape=(sha...  1.64 us
    ppermute x1, starting transfers between devices, swap_both(): return lax.ppermute(block, ('depth', 'col'), pairs)  1.49 us
    pallas_call x1, Pallas kernels, whole_plan(): pl.pallas_call(functools.partial(turn_kernel, sizes, orders), out_shape=(...  1.31 us
  transfers between devices with their start and end apart: 20, of which 9 were waited for; matrix products, arithmetic and copies ran while one was open for 2% of the time, Pallas kernels for 13%

profile of v2, /device:TPU:0, one launch (start us, length us, event | category | flops | bytes accessed | tf_op | source)
XLA Modules:
  0.0 47.3 jit_solution(8706130980937817233)
XLA Ops:
  0.6 0.1 pad_add_fusion.ids_ref
  0.7 1.9 %project.1 = (bf16[1,144,128]{2,1,0:T(8,128)(2,1)S(1)}, bf16[1,128,128]{2,1,0:T(8,128)(2,1)S(1)}, f32[1,256]{1,0:T(1,128)S(1)}, bf16[32,256]{1,0:T(8,128)(2,1)S(...) custom-call(s32[2]{0:T(128)S(1)} %pad_add_fusion.ids_ref, ...), custom_call_target="tpu_custom_call" | custom-call | tf_op jit(solution)/shard_map/project/pallas_call | solution.py:727
  2.6 0.0 copy-start
  2.6 5.1 %collective-permute-start.6 = (bf16[1,144,128]{2,1,0:T(8,128)(2,1)S(1)}, bf16[1,144,128]{2,1,0:T(8,128)(2,1)S(1)}, u32[]{:S(2)}, u32[]{:S(2)}) collective-permute-start(bf16[1,144,128]{2,1,0:T(8,128)(2,1)S(1)} %get-tuple-element.59), channel_id=1, source_target_pairs={{0,6},{1,7},{2,4},{3,5},{4,2},{5,3},{6,0},{7,1},{8,14},{9,15},{10,... | collective-permute-start | bytes 110600 | tf_op jit(solution)/shard_map/ppermute | solution.py:677
  7.8 0.6 %collective-permute-start = (bf16[1,144,128]{2,1,0:T(8,128)(2,1)S(1)}, bf16[1,144,128]{2,1,0:T(8,128)(2,1)S(1)}, u32[]{:S(2)}, u32[]{:S(2)}) collective-permute-start(bf16[1,144,128]{2,1,0:T(8,128)(2,1)S(1)} %get-tuple-element.59), channel_id=1, source_target_pairs={{0,2},{1,3},{2,0},{3,1},{4,6},{5,7},{6,4},{7,5},{8,10},{9,11},{10,... | collective-permute-start | bytes 110600 | tf_op jit(solution)/shard_map/ppermute | solution.py:677
  8.4 3.3 %collective-permute-done = bf16[1,144,128]{2,1,0:T(8,128)(2,1)S(1)} collective-permute-done((bf16[1,144,128]{2,1,0:T(8,128)(2,1)S(1)}, bf16[1,144,128]{2,1,0:T(8,128)(2,1)S(1)}, u32[]{:S(2)}, u32[]{:S(2)}) %collective-permute-start) | collective-permute-done | bytes 36896 | tf_op jit(solution)/shard_map/ppermute | solution.py:677
  11.7 2.4 %collective-permute-start.3 = (bf16[1,128,128]{2,1,0:T(8,128)(2,1)S(1)}, bf16[1,128,128]{2,1,0:T(8,128)(2,1)S(1)}, u32[]{:S(2)}, u32[]{:S(2)}) collective-permute-start(bf16[1,128,128]{2,1,0:T(8,128)(2,1)S(1)} %get-tuple-element.61), channel_id=1, source_target_pairs={{0,6},{1,7},{2,4},{3,5},{4,2},{5,3},{6,0},{7,1},{8,14},{9,15},{10,... | collective-permute-start | bytes 98312 | tf_op jit(solution)/shard_map/ppermute | solution.py:677
  14.1 0.6 %collective-permute-start.2 = (bf16[1,128,128]{2,1,0:T(8,128)(2,1)S(1)}, bf16[1,128,128]{2,1,0:T(8,128)(2,1)S(1)}, u32[]{:S(2)}, u32[]{:S(2)}) collective-permute-start(bf16[1,128,128]{2,1,0:T(8,128)(2,1)S(1)} %get-tuple-element.61), channel_id=1, source_target_pairs={{0,4},{1,5},{2,6},{3,7},{4,0},{5,1},{6,2},{7,3},{8,12},{9,13},{10,... | collective-permute-start | bytes 98312 | tf_op jit(solution)/shard_map/ppermute | solution.py:677
  14.6 1.5 %collective-permute-start.1 = (bf16[1,128,128]{2,1,0:T(8,128)(2,1)S(1)}, bf16[1,128,128]{2,1,0:T(8,128)(2,1)S(1)}, u32[]{:S(2)}, u32[]{:S(2)}) collective-permute-start(bf16[1,128,128]{2,1,0:T(8,128)(2,1)S(1)} %get-tuple-element.61), channel_id=1, source_target_pairs={{0,2},{1,3},{2,0},{3,1},{4,6},{5,7},{6,4},{7,5},{8,10},{9,11},{10,... | collective-permute-start | bytes 98312 | tf_op jit(solution)/shard_map/ppermute | solution.py:677
  16.1 0.0 collective-permute-done.5
  16.1 0.0 collective-permute-done.6
  16.2 0.1 collective-permute-start.8
  16.3 1.6 %collective-permute-start.7 = (bf16[4,144,128]{2,1,0:T(8,128)(2,1)S(1)}, bf16[4,144,128]{2,1,0:T(8,128)(2,1)S(1)}, u32[]{:S(2)}, u32[]{:S(2)}) collective-permute-start(bf16[4,144,128]{2,1,0:T(8,128)(2,1)S(1)} %constant_dynamic-update-slice_fusion.4.near_ref), channel_id=1, source_target_pairs={{0,1},{1,0},{2,3},{3,2},{4,5},{5,4},{6,7},{7,6},{8,9},{9,8},{10,11... | collective-permute-start | bytes 442376 | tf_op jit(solution)/shard_map/ppermute | solution.py:677
  17.8 0.7 %collective-permute-done.1 = bf16[1,128,128]{2,1,0:T(8,128)(2,1)S(1)} collective-permute-done((bf16[1,128,128]{2,1,0:T(8,128)(2,1)S(1)}, bf16[1,128,128]{2,1,0:T(8,128)(2,1)S(1)}, u32[]{:S(2)}, u32[]{:S(2)}) %collective-permute-start.1) | collective-permute-done | bytes 32800 | tf_op jit(solution)/shard_map/ppermute | solution.py:677
  18.6 0.3 collective-permute-done.2
  18.9 3.6 %collective-permute-done.7.far_ref = bf16[4,144,128]{2,1,0:T(8,128)(2,1)S(1)} collective-permute-done((bf16[4,144,128]{2,1,0:T(8,128)(2,1)S(1)}, bf16[4,144,128]{2,1,0:T(8,128)(2,1)S(1)}, u32[]{:S(2)}, u32[]{:S(2)}) %collective-permute-start.7) | collective-permute-done | bytes 147488 | tf_op jit(solution)/shard_map/ppermute | solution.py:677
  22.5 0.0 collective-permute-done.3
  22.5 1.6 %collective-permute-start.4 = (bf16[4,128,128]{2,1,0:T(8,128)(2,1)S(1)}, bf16[4,128,128]{2,1,0:T(8,128)(2,1)S(1)}, u32[]{:S(2)}, u32[]{:S(2)}) collective-permute-start(bf16[4,128,128]{2,1,0:T(8,128)(2,1)S(1)} %constant_dynamic-update-slice_fusion.near_ref), channel_id=1, source_target_pairs={{0,1},{1,0},{2,3},{3,2},{4,5},{5,4},{6,7},{7,6},{8,9},{9,8},{10,11... | collective-permute-start | bytes 393224 | tf_op jit(solution)/shard_map/ppermute | solution.py:677
  24.1 0.1 copy.19
  24.2 0.0 collective-permute-done.8.other_near_ref
  24.3 2.1 %outer_products.1 = (bf16[512,1024]{1,0:T(8,128)(2,1)S(1)}, f32[512,128]{1,0:T(8,128)S(1)}, f32[512,128]{1,0:T(8,128)S(1)}, bf16[512,128]{1,0:T(8,128)(2,1)S(1)}) custom-call(s32[2]{0:T(128)S(1)} %pad_add_fusion.ids_ref, bf16[4,144,128]{2,1,0:T(8,128)(2,1)S(1)} %constant_dynamic-update-slice_fusion.4.near_ref, ...), custom_call_target="tpu_custom_call" | custom-call | tf_op jit(solution)/shard_map/outer_products/pallas_call | solution.py:782
  26.4 0.0 copy-start.1
  26.4 0.0 copy-start.2
  26.4 1.3 %turned.1 = (bf16[1024,128]{1,0:T(8,128)(2,1)S(1)}, bf16[1024,128]{1,0:T(8,128)(2,1)S(1)}) custom-call(s32[2]{0:T(128)S(1)} %pad_add_fusion.ids_ref, bf16[4,144,128]{2,1,0:T(8,128)(2,1)S(1)} %constant_dynamic-update-slice_fusion.4.near_ref, bf16[4,144,128]{2,1,0:T(8,128)(2,1)S(1)} %collective-permute-done.7.far_ref), custom_call_target="tpu_custom_call" | custom-call | tf_op jit(solution)/shard_map/turned/pallas_call | solution.py:805
  27.7 0.8 %collective-permute-done.4.far_ref = bf16[4,128,128]{2,1,0:T(8,128)(2,1)S(1)} collective-permute-done((bf16[4,128,128]{2,1,0:T(8,128)(2,1)S(1)}, bf16[4,128,128]{2,1,0:T(8,128)(2,1)S(1)}, u32[]{:S(2)}, u32[]{:S(2)}) %collective-permute-start.4) | collective-permute-done | bytes 131104 | tf_op jit(solution)/shard_map/ppermute | solution.py:677
  28.5 2.4 %transition.1 = (bf16[64,128]{1,0:T(8,128)(2,1)}, bf16[512,128]{1,0:T(8,128)(2,1)S(1)}, bf16[512,128]{1,0:T(8,128)(2,1)S(1)}, bf16[512,512]{1,0:T(8,128)(2,1)S(1...) custom-call(s32[2]{0:T(128)S(1)} %pad_add_fusion.ids_ref, ...), custom_call_target="tpu_custom_call" | custom-call | tf_op jit(solution)/shard_map/transition/pallas_call | solution.py:820
  30.9 0.8 %out_weight.1.refs_0_ = bf16[1024,128]{1,0:T(8,128)(2,1)S(1)} custom-call(bf16[512,1024]{1,0:T(8,128)(2,1)S(1)} %get-tuple-element.75.outer_ref, bf16[512,128]{1,0:T(8,128)(2,1)S(1)} %get-tuple-element.74.opm_ref), custom_call_target="tpu_custom_call" | custom-call | tf_op jit(solution)/shard_map/out_weight/pallas_call | solution.py:849
  31.7 0.4 transition_weights.1
  32.1 0.2 collective-permute-done.10.other_opm_ref
  32.3 1.6 %projector_parts.1 = (bf16[64,256]{1,0:T(8,128)(2,1)S(1)}, bf16[256,256]{1,0:T(8,128)(2,1)S(1)}) custom-call(s32[2]{0:T(128)S(1)} %pad_add_fusion.ids_ref, bf16[512,128]{1,0:T(8,128)(2,1)S(1)} %get-tuple-element.74.opm_ref, bf16[512,128]{1,0:T(8,128)(2,1)S(1)} %collective-permute-done.10.other_opm_ref, bf16[1024,128]{1,0:T(8,128)(2,1)S(1)} %get-tuple-element.83.rightt_ref, ...), custom_call_target="tpu_custom_call" | custom-call | tf_op jit(solution)/shard_map/projector_parts/pallas_call | solution.py:868
  33.9 1.5 %collective-permute-start.13 = (bf16[64,256]{1,0:T(8,128)(2,1)S(1)}, bf16[64,256]{1,0:T(8,128)(2,1)S(1)}, u32[]{:S(2)}, u32[]{:S(2)}) collective-permute-start(bf16[64,256]{1,0:T(8,128)(2,1)S(1)} %get-tuple-element.87), channel_id=1, source_target_pairs={{0,9},{1,8},{2,11},{3,10},{4,13},{5,12},{6,15},{7,14},{8,1},{9,0},... | collective-permute-start | bytes 98312 | tf_op jit(solution)/shard_map/ppermute | solution.py:687
  35.4 0.5 %collective-permute-start.12 = (bf16[64,256]{1,0:T(8,128)(2,1)S(1)}, bf16[64,256]{1,0:T(8,128)(2,1)S(1)}, u32[]{:S(2)}, u32[]{:S(2)}) collective-permute-start(bf16[64,256]{1,0:T(8,128)(2,1)S(1)} %get-tuple-element.87), channel_id=1, source_target_pairs={{0,1},{1,0},{2,3},{3,2},{4,5},{5,4},{6,7},{7,6},{8,9},{9,8},{10,11... | collective-permute-start | bytes 98312 | tf_op jit(solution)/shard_map/ppermute | solution.py:677
  35.9 0.0 collective-permute-start.11
  35.9 0.5 %collective-permute-start.17 = (bf16[1024,128]{1,0:T(8,128)(2,1)S(1)}, bf16[1024,128]{1,0:T(8,128)(2,1)S(1)}, u32[]{:S(2)}, u32[]{:S(2)}) collective-permute-start(bf16[1024,128]{1,0:T(8,128)(2,1)S(1)} %out_weight.1.refs_0_), channel_id=1, source_target_pairs={{0,8},{8,0},{1,9},{9,1},{2,10},{10,2},{3,11},{11,3},{4,12},{12,4},... | collective-permute-start | bytes 786440 | tf_op jit(solution)/shard_map/ppermute | solution.py:666
  36.4 0.3 features.1
  36.8 0.5 %collective-permute-done.13 = bf16[64,256]{1,0:T(8,128)(2,1)S(1)} collective-permute-done((bf16[64,256]{1,0:T(8,128)(2,1)S(1)}, bf16[64,256]{1,0:T(8,128)(2,1)S(1)}, u32[]{:S(2)}, u32[]{:S(2)}) %collective-permute-start.13) | collective-permute-done | bytes 32800 | tf_op jit(solution)/shard_map/ppermute | solution.py:687
  37.3 0.3 collective-permute-start.19
  37.6 1.7 %collective-permute-done.12 = bf16[64,256]{1,0:T(8,128)(2,1)S(1)} collective-permute-done((bf16[64,256]{1,0:T(8,128)(2,1)S(1)}, bf16[64,256]{1,0:T(8,128)(2,1)S(1)}, u32[]{:S(2)}, u32[]{:S(2)}) %collective-permute-start.12) | collective-permute-done | bytes 32800 | tf_op jit(solution)/shard_map/ppermute | solution.py:677
  39.3 0.0 collective-permute-done.11
  39.4 2.4 %collective-permute-start.16 = (bf16[64,256]{1,0:T(8,128)(2,1)S(1)}, bf16[64,256]{1,0:T(8,128)(2,1)S(1)}, u32[]{:S(2)}, u32[]{:S(2)}) collective-permute-start(bf16[64,256]{1,0:T(8,128)(2,1)S(1)} %add_convert_fusion), channel_id=1, source_target_pairs={{0,6},{1,7},{2,4},{3,5},{4,2},{5,3},{6,0},{7,1},{8,14},{9,15},{10,... | collective-permute-start | bytes 98312 | tf_op jit(solution)/shard_map/ppermute | solution.py:677
  41.8 0.0 collective-permute-start.15
  41.8 0.0 collective-permute-done.18.refs_4_
  41.8 2.0 %collective-permute-start.14 = (bf16[64,256]{1,0:T(8,128)(2,1)S(1)}, bf16[64,256]{1,0:T(8,128)(2,1)S(1)}, u32[]{:S(2)}, u32[]{:S(2)}) collective-permute-start(bf16[64,256]{1,0:T(8,128)(2,1)S(1)} %add_convert_fusion), channel_id=1, source_target_pairs={{0,2},{1,3},{2,0},{3,1},{4,6},{5,7},{6,4},{7,5},{8,10},{9,11},{10,... | collective-permute-start | bytes 98312 | tf_op jit(solution)/shard_map/ppermute | solution.py:677
  43.8 0.7 %reshape.44 = bf16[64,4,256]{2,1,0:T(4,128)(2,1)} reshape(bf16[256,256]{1,0:T(8,128)(2,1)S(1)} %features.1) | data formatting | bytes 262144 | tf_op jit(solution)/shard_map/reshape | solution.py:917
  44.5 0.0 collective-permute-done.19.refs_5_
  44.5 1.0 %sums_over_depth.1 = (f32[1024,128]{1,0:T(8,128)}, f32[128,512]{1,0:T(8,128)}, f32[512,128]{1,0:T(8,128)}) custom-call(bf16[1024,128]{1,0:T(8,128)(2,1)S(1)} %out_weight.1.refs_0_, bf16[128,512]{1,0:T(8,128)(2,1)S(1)} %get-tuple-element.100.refs_1_, bf16[512,128]{1,0:T(8,128)(2,1)S(1)} %get-tuple-element.101.refs_2_, ...), custom_call_target="tpu_custom_call" | custom-call | tf_op jit(solution)/shard_map/sums_over_depth/pallas_call | solution.py:895
  45.5 1.1 %collective-permute-done.15 = bf16[64,256]{1,0:T(8,128)(2,1)S(1)} collective-permute-done((bf16[64,256]{1,0:T(8,128)(2,1)S(1)}, bf16[64,256]{1,0:T(8,128)(2,1)S(1)}, u32[]{:S(2)}, u32[]{:S(2)}) %collective-permute-start.15) | collective-permute-done | bytes 32800 | tf_op jit(solution)/shard_map/ppermute | solution.py:677
  46.6 0.6 %slice_bitcast_fusion = (f32[256,32]{0,1:T(8,128)}, f32[256,32]{0,1:T(8,128)}) fusion(f32[64,256]{1,0:T(8,128)S(1)} %add_add_fusion), kind=kLoop, calls=%fused_computation.2 | loop fusion | bytes 131072 | tf_op jit(solution)/shard_map/transpose | solution.py:920
  (21 shorter events, 0.1 us)
Async XLA Ops:
  2.6 21.5 %copy-start = (bf16[1024,128]{1,0:T(8,128)(2,1)S(1)}, bf16[1024,128]{1,0:T(8,128)(2,1)}, u32[]{:S(2)}) copy-start(bf16[1024,128]{1,0:T(8,128)(2,1)} %wout_ref.1) | copy-start | bytes 786436
  2.6 13.5 %collective-permute-start.6 = (bf16[1,144,128]{2,1,0:T(8,128)(2,1)S(1)}, bf16[1,144,128]{2,1,0:T(8,128)(2,1)S(1)}, u32[]{:S(2)}, u32[]{:S(2)}) collective-permute-start(bf16[1,144,128]{2,1,0:T(8,128)(2,1)S(1)} %get-tuple-element.59), channel_id=1, source_target_pairs={{0,6},{1,7},{2,4},{3,5},{4,2},{5,3},{6,0},{7,1},{8,14},{9,15},{10,... | collective-permute-start | bytes 110600 | tf_op jit(solution)/shard_map/ppermute | solution.py:677
  7.8 8.4 %collective-permute-start.5 = (bf16[1,144,128]{2,1,0:T(8,128)(2,1)S(1)}, bf16[1,144,128]{2,1,0:T(8,128)(2,1)S(1)}, u32[]{:S(2)}, u32[]{:S(2)}) collective-permute-start(bf16[1,144,128]{2,1,0:T(8,128)(2,1)S(1)} %get-tuple-element.59), channel_id=1, source_target_pairs={{0,4},{1,5},{2,6},{3,7},{4,0},{5,1},{6,2},{7,3},{8,12},{9,13},{10,... | collective-permute-start | bytes 110600 | tf_op jit(solution)/shard_map/ppermute | solution.py:677
  7.8 4.0 %collective-permute-start = (bf16[1,144,128]{2,1,0:T(8,128)(2,1)S(1)}, bf16[1,144,128]{2,1,0:T(8,128)(2,1)S(1)}, u32[]{:S(2)}, u32[]{:S(2)}) collective-permute-start(bf16[1,144,128]{2,1,0:T(8,128)(2,1)S(1)} %get-tuple-element.59), channel_id=1, source_target_pairs={{0,2},{1,3},{2,0},{3,1},{4,6},{5,7},{6,4},{7,5},{8,10},{9,11},{10,... | collective-permute-start | bytes 110600 | tf_op jit(solution)/shard_map/ppermute | solution.py:677
  11.7 10.8 %collective-permute-start.3 = (bf16[1,128,128]{2,1,0:T(8,128)(2,1)S(1)}, bf16[1,128,128]{2,1,0:T(8,128)(2,1)S(1)}, u32[]{:S(2)}, u32[]{:S(2)}) collective-permute-start(bf16[1,128,128]{2,1,0:T(8,128)(2,1)S(1)} %get-tuple-element.61), channel_id=1, source_target_pairs={{0,6},{1,7},{2,4},{3,5},{4,2},{5,3},{6,0},{7,1},{8,14},{9,15},{10,... | collective-permute-start | bytes 98312 | tf_op jit(solution)/shard_map/ppermute | solution.py:677
  14.1 4.8 %collective-permute-start.2 = (bf16[1,128,128]{2,1,0:T(8,128)(2,1)S(1)}, bf16[1,128,128]{2,1,0:T(8,128)(2,1)S(1)}, u32[]{:S(2)}, u32[]{:S(2)}) collective-permute-start(bf16[1,128,128]{2,1,0:T(8,128)(2,1)S(1)} %get-tuple-element.61), channel_id=1, source_target_pairs={{0,4},{1,5},{2,6},{3,7},{4,0},{5,1},{6,2},{7,3},{8,12},{9,13},{10,... | collective-permute-start | bytes 98312 | tf_op jit(solution)/shard_map/ppermute | solution.py:677
  14.6 3.9 %collective-permute-start.1 = (bf16[1,128,128]{2,1,0:T(8,128)(2,1)S(1)}, bf16[1,128,128]{2,1,0:T(8,128)(2,1)S(1)}, u32[]{:S(2)}, u32[]{:S(2)}) collective-permute-start(bf16[1,128,128]{2,1,0:T(8,128)(2,1)S(1)} %get-tuple-element.61), channel_id=1, source_target_pairs={{0,2},{1,3},{2,0},{3,1},{4,6},{5,7},{6,4},{7,5},{8,10},{9,11},{10,... | collective-permute-start | bytes 98312 | tf_op jit(solution)/shard_map/ppermute | solution.py:677
  16.2 8.1 %collective-permute-start.8 = (bf16[4,144,128]{2,1,0:T(8,128)(2,1)S(1)}, bf16[4,144,128]{2,1,0:T(8,128)(2,1)S(1)}, u32[]{:S(2)}, u32[]{:S(2)}) collective-permute-start(bf16[4,144,128]{2,1,0:T(8,128)(2,1)S(1)} %constant_dynamic-update-slice_fusion.4.near_ref), channel_id=1, source_target_pairs={{0,8},{8,0},{1,9},{9,1},{2,10},{10,2},{3,11},{11,3},{4,12},{12,4},... | collective-permute-start | bytes 442376 | tf_op jit(solution)/shard_map/ppermute | solution.py:666
  16.3 6.3 %collective-permute-start.7 = (bf16[4,144,128]{2,1,0:T(8,128)(2,1)S(1)}, bf16[4,144,128]{2,1,0:T(8,128)(2,1)S(1)}, u32[]{:S(2)}, u32[]{:S(2)}) collective-permute-start(bf16[4,144,128]{2,1,0:T(8,128)(2,1)S(1)} %constant_dynamic-update-slice_fusion.4.near_ref), channel_id=1, source_target_pairs={{0,1},{1,0},{2,3},{3,2},{4,5},{5,4},{6,7},{7,6},{8,9},{9,8},{10,11... | collective-permute-start | bytes 442376 | tf_op jit(solution)/shard_map/ppermute | solution.py:677
  22.5 1.7 %collective-permute-start.9 = (bf16[4,144,128]{2,1,0:T(8,128)(2,1)S(1)}, bf16[4,144,128]{2,1,0:T(8,128)(2,1)S(1)}, u32[]{:S(2)}, u32[]{:S(2)}) collective-permute-start(bf16[4,144,128]{2,1,0:T(8,128)(2,1)S(1)} %collective-permute-done.7.far_ref), channel_id=1, source_target_pairs={{0,8},{8,0},{1,9},{9,1},{2,10},{10,2},{3,11},{11,3},{4,12},{12,4},... | collective-permute-start | bytes 442376 | tf_op jit(solution)/shard_map/ppermute | solution.py:666
  22.5 6.0 %collective-permute-start.4 = (bf16[4,128,128]{2,1,0:T(8,128)(2,1)S(1)}, bf16[4,128,128]{2,1,0:T(8,128)(2,1)S(1)}, u32[]{:S(2)}, u32[]{:S(2)}) collective-permute-start(bf16[4,128,128]{2,1,0:T(8,128)(2,1)S(1)} %constant_dynamic-update-slice_fusion.near_ref), channel_id=1, source_target_pairs={{0,1},{1,0},{2,3},{3,2},{4,5},{5,4},{6,7},{7,6},{8,9},{9,8},{10,11... | collective-permute-start | bytes 393224 | tf_op jit(solution)/shard_map/ppermute | solution.py:677
  26.4 2.1 %copy-start.1 = (bf16[128,512]{1,0:T(8,128)(2,1)S(1)}, bf16[128,512]{1,0:T(8,128)(2,1)}, u32[]{:S(2)}) copy-start(bf16[128,512]{1,0:T(8,128)(2,1)} %hid_ref.1) | copy-start | bytes 393220
  26.4 2.1 %copy-start.2 = (bf16[512,128]{1,0:T(8,128)(2,1)S(1)}, bf16[512,128]{1,0:T(8,128)(2,1)}, u32[]{:S(2)}) copy-start(bf16[512,128]{1,0:T(8,128)(2,1)} %back_ref.1) | copy-start | bytes 393220
  30.9 1.3 %collective-permute-start.10 = (bf16[512,128]{1,0:T(8,128)(2,1)S(1)}, bf16[512,128]{1,0:T(8,128)(2,1)S(1)}, u32[]{:S(2)}, u32[]{:S(2)}) collective-permute-start(bf16[512,128]{1,0:T(8,128)(2,1)S(1)} %get-tuple-element.74.opm_ref), channel_id=1, source_target_pairs={{0,8},{8,0},{1,9},{9,1},{2,10},{10,2},{3,11},{11,3},{4,12},{12,4},... | collective-permute-start | bytes 393224 | tf_op jit(solution)/shard_map/ppermute | solution.py:666
  33.9 3.4 %collective-permute-start.13 = (bf16[64,256]{1,0:T(8,128)(2,1)S(1)}, bf16[64,256]{1,0:T(8,128)(2,1)S(1)}, u32[]{:S(2)}, u32[]{:S(2)}) collective-permute-start(bf16[64,256]{1,0:T(8,128)(2,1)S(1)} %get-tuple-element.87), channel_id=1, source_target_pairs={{0,9},{1,8},{2,11},{3,10},{4,13},{5,12},{6,15},{7,14},{8,1},{9,0},... | collective-permute-start | bytes 98312 | tf_op jit(solution)/shard_map/ppermute | solution.py:687
  35.4 3.9 %collective-permute-start.12 = (bf16[64,256]{1,0:T(8,128)(2,1)S(1)}, bf16[64,256]{1,0:T(8,128)(2,1)S(1)}, u32[]{:S(2)}, u32[]{:S(2)}) collective-permute-start(bf16[64,256]{1,0:T(8,128)(2,1)S(1)} %get-tuple-element.87), channel_id=1, source_target_pairs={{0,1},{1,0},{2,3},{3,2},{4,5},{5,4},{6,7},{7,6},{8,9},{9,8},{10,11... | collective-permute-start | bytes 98312 | tf_op jit(solution)/shard_map/ppermute | solution.py:677
  35.9 3.4 %collective-permute-start.11 = (bf16[64,256]{1,0:T(8,128)(2,1)S(1)}, bf16[64,256]{1,0:T(8,128)(2,1)S(1)}, u32[]{:S(2)}, u32[]{:S(2)}) collective-permute-start(bf16[64,256]{1,0:T(8,128)(2,1)S(1)} %get-tuple-element.87), channel_id=1, source_target_pairs={{0,8},{8,0},{1,9},{9,1},{2,10},{10,2},{3,11},{11,3},{4,12},{12,4},... | collective-permute-start | bytes 98312 | tf_op jit(solution)/shard_map/ppermute | solution.py:666
  35.9 8.6 %collective-permute-start.17 = (bf16[1024,128]{1,0:T(8,128)(2,1)S(1)}, bf16[1024,128]{1,0:T(8,128)(2,1)S(1)}, u32[]{:S(2)}, u32[]{:S(2)}) collective-permute-start(bf16[1024,128]{1,0:T(8,128)(2,1)S(1)} %out_weight.1.refs_0_), channel_id=1, source_target_pairs={{0,8},{8,0},{1,9},{9,1},{2,10},{10,2},{3,11},{11,3},{4,12},{12,4},... | collective-permute-start | bytes 786440 | tf_op jit(solution)/shard_map/ppermute | solution.py:666
  36.4 5.4 %collective-permute-start.18 = (bf16[128,512]{1,0:T(8,128)(2,1)S(1)}, bf16[128,512]{1,0:T(8,128)(2,1)S(1)}, u32[]{:S(2)}, u32[]{:S(2)}) collective-permute-start(bf16[128,512]{1,0:T(8,128)(2,1)S(1)} %get-tuple-element.100.refs_1_), channel_id=1, source_target_pairs={{0,8},{8,0},{1,9},{9,1},{2,10},{10,2},{3,11},{11,3},{4,12},{12,4},... | collective-permute-start | bytes 393224 | tf_op jit(solution)/shard_map/ppermute | solution.py:666
  37.3 7.2 %collective-permute-start.19 = (bf16[512,128]{1,0:T(8,128)(2,1)S(1)}, bf16[512,128]{1,0:T(8,128)(2,1)S(1)}, u32[]{:S(2)}, u32[]{:S(2)}) collective-permute-start(bf16[512,128]{1,0:T(8,128)(2,1)S(1)} %get-tuple-element.101.refs_2_), channel_id=1, source_target_pairs={{0,8},{8,0},{1,9},{9,1},{2,10},{10,2},{3,11},{11,3},{4,12},{12,4},... | collective-permute-start | bytes 393224 | tf_op jit(solution)/shard_map/ppermute | solution.py:666
  39.4 6.2 %collective-permute-start.16 = (bf16[64,256]{1,0:T(8,128)(2,1)S(1)}, bf16[64,256]{1,0:T(8,128)(2,1)S(1)}, u32[]{:S(2)}, u32[]{:S(2)}) collective-permute-start(bf16[64,256]{1,0:T(8,128)(2,1)S(1)} %add_convert_fusion), channel_id=1, source_target_pairs={{0,6},{1,7},{2,4},{3,5},{4,2},{5,3},{6,0},{7,1},{8,14},{9,15},{10,... | collective-permute-start | bytes 98312 | tf_op jit(solution)/shard_map/ppermute | solution.py:677
  41.8 4.8 %collective-permute-start.15 = (bf16[64,256]{1,0:T(8,128)(2,1)S(1)}, bf16[64,256]{1,0:T(8,128)(2,1)S(1)}, u32[]{:S(2)}, u32[]{:S(2)}) collective-permute-start(bf16[64,256]{1,0:T(8,128)(2,1)S(1)} %add_convert_fusion), channel_id=1, source_target_pairs={{0,4},{1,5},{2,6},{3,7},{4,0},{5,1},{6,2},{7,3},{8,12},{9,13},{10,... | collective-permute-start | bytes 98312 | tf_op jit(solution)/shard_map/ppermute | solution.py:677
  41.8 4.8 %collective-permute-start.14 = (bf16[64,256]{1,0:T(8,128)(2,1)S(1)}, bf16[64,256]{1,0:T(8,128)(2,1)S(1)}, u32[]{:S(2)}, u32[]{:S(2)}) collective-permute-start(bf16[64,256]{1,0:T(8,128)(2,1)S(1)} %add_convert_fusion), channel_id=1, source_target_pairs={{0,2},{1,3},{2,0},{3,1},{4,6},{5,7},{6,4},{7,5},{8,10},{9,11},{10,... | collective-permute-start | bytes 98312 | tf_op jit(solution)/shard_map/ppermute | solution.py:677

commit v3 on v2

--- a/solution.py
+++ b/solution.py
@@ -245,7 +245,6 @@
 
 FEW_RESIDUES = 32
 MASK_ROWS = 16
-Z_PARTNERS = (2, 4, 6)
 Y_PARTNER = 1
 
 
@@ -288,7 +287,6 @@
     act_hbm,
     grad_hbm,
     sent_ref,
-    pairs_ref,
     scale_ref,
     first_ref,
     second_ref,
@@ -302,6 +300,7 @@
     x_ref,
     maskt_ref,
     pmask_ref,
+    pairs_ref,
     sems,
 ):
     res, seqs = maskt_ref.shape
@@ -317,8 +316,8 @@
                 (first_hbm, first_ref),
                 (second_hbm, second_ref),
                 (gain_hbm, gain_ref),
-                (act_hbm, pairs_ref.at[0, pl.ds(0, pairs), :]),
-                (grad_hbm, pairs_ref.at[0, pl.ds(pairs, pairs), :]),
+                (act_hbm, pairs_ref.at[pl.ds(0, pairs), :]),
+                (grad_hbm, pairs_ref.at[pl.ds(pairs, pairs), :]),
             )
         )
     ]
@@ -366,12 +365,15 @@
                 lane_group == r, wide_ref[at, pl.ds(r, seqs, stride=res), :], both
             )
         sent_ref[0, at * seqs : (at + 1) * seqs, :] = (both * mask_lanes).astype(jnp.bfloat16)
-    sent_ref[0, 2 * seqs :, :] = tile_ref[...].astype(jnp.bfloat16)
+    first_pair = 2 * seqs + MASK_ROWS
+    sent_ref[0, 2 * seqs : first_pair, :] = tile_ref[...].astype(jnp.bfloat16)
+    sent_ref[0, first_pair:, :] = pairs_ref[...]
+    for at in range(1, sent_ref.shape[0]):
+        sent_ref[at] = sent_ref[0]
 
 
 def outer_kernel(
     sizes,
-    orders,
     ids_ref,
     near_ref,
     far_ref,
@@ -399,10 +401,13 @@
     me_col = ids_ref[1]
     f32, bf16 = jnp.float32, jnp.bfloat16
 
-    for order, mine, other in zip(orders, (near_ref, far_ref), (other_near_ref, other_far_ref)):
-        for at, partner in enumerate(order):
-            got_ref[me_depth, me_col ^ partner] = mine[at]
-            got_ref[1 - me_depth, me_col ^ partner] = other[at]
+    for mine, other, owner in (
+        (near_ref, other_near_ref, me_col % 2),
+        (far_ref, other_far_ref, 1 - me_col % 2),
+    ):
+        for at in range(cols // 2):
+            got_ref[me_depth, 2 * at + owner] = mine[at]
+            got_ref[1 - me_depth, 2 * at + owner] = other[at]
 
     for e in range(depths):
         for k in range(cols):
@@ -465,17 +470,17 @@
     proj_out_ref[...] = jnp.dot(outer_ref[...], wturn_ref[...], preferred_element_type=f32)
 
 
-def turn_kernel(sizes, orders, ids_ref, near_ref, far_ref, rightt_ref, leftt_ref, turn_ref):
+def turn_kernel(sizes, ids_ref, near_ref, far_ref, rightt_ref, leftt_ref, turn_ref):
     seqs, res, _, width = sizes
     lanes = res * width
     residues = turn_ref.shape[0] // width
     me_col = ids_ref[1]
     for at, out in ((0, leftt_ref), (1, rightt_ref)):
-        for order, blocks in zip(orders, (near_ref, far_ref)):
-            for place, partner in enumerate(order):
+        for blocks, owner in ((near_ref, me_col % 2), (far_ref, 1 - me_col % 2)):
+            for place in range(blocks.shape[0]):
                 block = blocks[place, at * seqs : (at + 1) * seqs, :].astype(jnp.float32)
                 block = jnp.concatenate([block] * (lanes // seqs), axis=0)
-                first = pl.multiple_of((me_col ^ partner) * lanes, lanes)
+                first = pl.multiple_of((2 * place + owner) * lanes, lanes)
                 turn_ref[pl.ds(first, lanes), :] = block.T
         for d in range(width):
             out[d * residues : (d + 1) * residues, :] = turn_ref[
@@ -485,7 +490,6 @@
 
 def transition_kernel(
     sizes,
-    orders,
     ids_ref,
     near_ref,
     far_ref,
@@ -509,9 +513,9 @@
     cols = pgot_ref.shape[0]
     me_col = ids_ref[1]
     f32, bf16 = jnp.float32, jnp.bfloat16
-    for order, mine in zip(orders, (near_ref, far_ref)):
-        for at, partner in enumerate(order):
-            pgot_ref[me_col ^ partner] = mine[at]
+    for mine, owner in ((near_ref, me_col % 2), (far_ref, 1 - me_col % 2)):
+        for at in range(cols // 2):
+            pgot_ref[2 * at + owner] = mine[at]
     gain = gain_ref[...]
     chunk = 2 * per
     for at in range(cols // 2):
@@ -712,6 +716,7 @@
     per = res * pair_cols
     lanes = res * width
     rows = 2 * seqs + MASK_ROWS
+    line = cols // 2
     half = residues * pair_cols
     f32, bf16 = jnp.float32, jnp.bfloat16
     ids = jnp.stack([lax.axis_index("depth"), lax.axis_index("col")]).astype(jnp.int32)
@@ -724,11 +729,10 @@
         outer_width, pair_width
     )
     shape = jax.ShapeDtypeStruct
-    sent, sent_pairs, scale, first, second, gain, normed, scaled, inv, mask_lanes = pl.pallas_call(
+    sent, scale, first, second, gain, normed, scaled, inv, mask_lanes = pl.pallas_call(
         pre_kernel,
         out_shape=(
-            shape((1, rows, pair_width), bf16),
-            shape((1, 2 * per, pair_width), bf16),
+            shape((line, rows + 2 * per, pair_width), bf16),
             shape((1, channels), f32),
             shape((width, channels), bf16),
             shape((width, channels), bf16),
@@ -739,13 +743,14 @@
             shape((seqs, lanes), f32),
         ),
         in_specs=[smem] + [pl.BlockSpec(memory_space=pltpu.HBM)] * 9,
-        out_specs=[vmem] * 10,
+        out_specs=[vmem] * 9,
         scratch_shapes=[
             pltpu.VMEM((2, seqs * res, lanes), f32),
             pltpu.VMEM((MASK_ROWS, lanes), f32),
             pltpu.VMEM((seqs, res, channels), bf16),
             pltpu.VMEM((res, seqs), jnp.int32),
             pltpu.VMEM((res, pair_cols), jnp.int32),
+            pltpu.VMEM((2 * per, pair_width), bf16),
             pltpu.SemaphoreType.DMA((9,)),
         ],
         compiler_params=params,
@@ -767,20 +772,18 @@
             )
         ],
     )
-    near_order = (0,) + Z_PARTNERS
-    far_order = tuple(at ^ Y_PARTNER for at in near_order)
-    came = [swap_col(sent, partner) for partner in Z_PARTNERS]
-    came[0], sent_pairs = lax.optimization_barrier((came[0], sent_pairs))
-    near = jnp.concatenate([sent] + came)
-    pair_near = jnp.concatenate(
-        [sent_pairs] + [swap_col(sent_pairs, partner) for partner in Z_PARTNERS]
-    )
+    lines = [list(range(at, cols, 2)) for at in range(2)]
+
+    def along_z(copies):
+        return lax.all_to_all(copies, "col", 0, 0, axis_index_groups=lines)
+
+    blocks = along_z(sent)
+    near, pair_near = blocks[:, :rows], blocks[:, rows:]
     far = swap_col(near, Y_PARTNER)
     pair_far = swap_col(pair_near, Y_PARTNER)
     sizes = (seqs, res, pair_cols, width)
-    orders = (near_order, far_order)
     outer, proj_out, cnt, pm = pl.pallas_call(
-        functools.partial(outer_kernel, sizes, orders),
+        functools.partial(outer_kernel, sizes),
         out_shape=(
             shape((half, outer_width), bf16),
             shape((half, pair_width), f32),
@@ -803,7 +806,7 @@
     )(ids, near, far, swap_depth(near), swap_depth(far), wturn)
     near, far, proj_out = lax.optimization_barrier((near, far, proj_out))
     rightt, leftt = pl.pallas_call(
-        functools.partial(turn_kernel, sizes, orders),
+        functools.partial(turn_kernel, sizes),
         out_shape=(
             shape((residues * width, depths * seqs), bf16),
             shape((residues * width, depths * seqs), bf16),
@@ -818,7 +821,7 @@
         (pair_far, rightt, leftt, proj_out)
     )
     couple, opm, pn, gh, hidden, mg = pl.pallas_call(
-        functools.partial(transition_kernel, sizes, orders),
+        functools.partial(transition_kernel, sizes),
         out_shape=(
             shape((per, pair_width), bf16),
             shape((half, pair_width), bf16),
@@ -910,9 +913,9 @@
     near_ones, feat = lax.optimization_barrier((near_ones, feat))
     total = pairwise_sum([block.astype(f32) for block in [kept] + near_ones])
     kept = lax.optimization_barrier(total.astype(bf16))
-    far_ones = [swap_col(kept, partner) for partner in Z_PARTNERS]
+    far_ones = along_z(jnp.broadcast_to(kept, (line,) + kept.shape))
     far_ones, dout, dhid, dback = lax.optimization_barrier((far_ones, dout, dhid, dback))
-    total = pairwise_sum([block.astype(f32) for block in [kept] + far_ones])
+    total = pairwise_sum([far_ones[at].astype(f32) for at in range(line)])
     return (
         feat.reshape(seqs, res, channels),
         couple.reshape(res, pair_cols, pair_width),

time: 47.5 us -> 50.8 us (1.069)
  blocking collectives: 0 us -> 15.3 us
  starting transfers between devices: 20.7 us -> 9.57 us
  waiting for transfers between devices: 12.3 us -> 10.7 us
  local copies, waits for them, and re-layouts: 1.51 us -> 2.12 us
    all_to_all x0 -> x1, blocking collectives: none -> 15.3 us  [along_z(): return lax.all_to_all(copies, 'col', 0, 0, axis_index_groups=lines)]
    ppermute x12 -> x3, starting transfers between devices: 18.3 us -> 3.67 us  [swap_col(): lax.ppermute(block, 'col', [(at, at ^ partner) for at in range(count)])]
    ppermute x12 -> x3, waiting for transfers between devices: 11.6 us -> 6.33 us  [swap_col(): lax.ppermute(block, 'col', [(at, at ^ partner) for at in range(count)])]
    all_to_all x0 -> x1, starting transfers between devices: none -> 3.32 us  [along_z(): return lax.all_to_all(copies, 'col', 0, 0, axis_index_groups=lines)]
    all_to_all x0 -> x1, waiting for transfers between devices: none -> 3.27 us  [along_z(): return lax.all_to_all(copies, 'col', 0, 0, axis_index_groups=lines)]
    broadcast_in_dim x0 -> x1, local copies, waits for them, and re-layouts: none -> 0.66 us  [whole_plan(): far_ones = along_z(jnp.broadcast_to(kept, (line,) + kept.shape))]
  transfers between devices with their start and end apart: 20 -> 12, of which waited for: 9 -> 8; matrix products, arithmetic and copies ran while one was open for 2% -> 3% of each run, Pallas kernels for 13% -> 12%
where the time goes in v3:
time: 50.8 us; the launch traced here: 50.6 us
  blocking collectives  15.3 us (30%)
  Pallas kernels  12 us (24%)
  waiting for transfers between devices  10.7 us (21%)
  starting transfers between devices  9.57 us (19%)
  local copies, waits for them, and re-layouts  2.12 us (4%)
  between operations  0.76 us (1%)
    all_to_all x1, blocking collectives, along_z(): return lax.all_to_all(copies, 'col', 0, 0, axis_index_groups=lines)  15.3 us
    ppermute x3, waiting for transfers between devices, swap_col(): lax.ppermute(block, 'col', [(at, at ^ partner) for at in range(count)])  6.33 us
    ppermute x3, starting transfers between devices, swap_col(): lax.ppermute(block, 'col', [(at, at ^ partner) for at in range(count)])  3.67 us
    all_to_all x1, starting transfers between devices, along_z(): return lax.all_to_all(copies, 'col', 0, 0, axis_index_groups=lines)  3.32 us
    all_to_all x1, waiting for transfers between devices, along_z(): return lax.all_to_all(copies, 'col', 0, 0, axis_index_groups=lines)  3.27 us
    pallas_call x1, Pallas kernels, whole_plan(): pl.pallas_call(functools.partial(transition_kernel, sizes), out_shape=(sh...  2.4 us
    pallas_call x1, Pallas kernels, whole_plan(): pl.pallas_call(functools.partial(outer_kernel, sizes), out_shape=(shape((...  2.14 us
    pallas_call x1, Pallas kernels, whole_plan(): pl.pallas_call(pre_kernel, out_shape=(shape((line, rows + 2 * per, pair_w...  1.93 us
  transfers between devices with their start and end apart: 12, of which 8 were waited for; matrix products, arithmetic and copies ran while one was open for 3% of the time, Pallas kernels for 12%

profile of v3, /device:TPU:0, one launch (start us, length us, event | category | flops | bytes accessed | tf_op | source)
XLA Modules:
  0.0 50.6 jit_solution(210628840389799634)
XLA Ops:
  0.6 0.1 pad_add_fusion.ids_ref
  0.7 1.9 %project.1 = (bf16[4,272,128]{2,1,0:T(8,128)(2,1)S(1)}, f32[1,256]{1,0:T(1,128)S(1)}, bf16[32,256]{1,0:T(8,128)(2,1)S(1)}, bf16[32,256]{1,0:T(8,128)(2,1)S(1)}, ...) custom-call(s32[2]{0:T(128)S(1)} %pad_add_fusion.ids_ref, ...), custom_call_target="tpu_custom_call" | custom-call | tf_op jit(solution)/shard_map/project/pallas_call | solution.py:732
  2.6 15.3 %all_to_all.10 = bf16[4,272,128]{2,1,0:T(8,128)(2,1)S(1)} all-to-all(bf16[4,272,128]{2,1,0:T(8,128)(2,1)S(1)} %get-tuple-element.54), channel_id=1, replica_groups={{0,2,4,6},{1,3,5,7},{8,10,12,14},{9,11,13,15},{16,18,20,22},{17,19,21,2..., dimensions={0} | all-to-all | bytes 557056 | tf_op jit(solution)/shard_map/all_to_all | solution.py:778
  18.0 0.0 copy-start
  18.0 1.6 %collective-permute-start.1 = (bf16[4,144,128]{2,1,0:T(8,128)(2,1)S(1)}, bf16[4,144,128]{2,1,0:T(8,128)(2,1)S(1)}, u32[]{:S(2)}, u32[]{:S(2)}) collective-permute-start(bf16[4,144,128]{2,1,0:T(8,128)(2,1)S(1)} %slice.41.near_ref), channel_id=1, source_target_pairs={{0,1},{1,0},{2,3},{3,2},{4,5},{5,4},{6,7},{7,6},{8,9},{9,8},{10,11... | collective-permute-start | bytes 442376 | tf_op jit(solution)/shard_map/ppermute | solution.py:681
  19.6 0.0 collective-permute-start.2
  19.6 3.6 %collective-permute-done.1.far_ref = bf16[4,144,128]{2,1,0:T(8,128)(2,1)S(1)} collective-permute-done((bf16[4,144,128]{2,1,0:T(8,128)(2,1)S(1)}, bf16[4,144,128]{2,1,0:T(8,128)(2,1)S(1)}, u32[]{:S(2)}, u32[]{:S(2)}) %collective-permute-start.1) | collective-permute-done | bytes 147488 | tf_op jit(solution)/shard_map/ppermute | solution.py:681
  23.2 0.0 collective-permute-start.3
  23.2 1.6 %collective-permute-start = (bf16[4,128,128]{2,1,0:T(8,128)(2,1)S(1)}, bf16[4,128,128]{2,1,0:T(8,128)(2,1)S(1)}, u32[]{:S(2)}, u32[]{:S(2)}) collective-permute-start(bf16[4,128,128]{2,1,0:T(8,128)(2,1)S(1)} %slice.40.near_ref), channel_id=1, source_target_pairs={{0,1},{1,0},{2,3},{3,2},{4,5},{5,4},{6,7},{7,6},{8,9},{9,8},{10,11... | collective-permute-start | bytes 393224 | tf_op jit(solution)/shard_map/ppermute | solution.py:681
  24.8 0.0 copy-done
  24.8 0.1 copy.19
  24.9 0.0 collective-permute-done.2.other_near_ref
  24.9 0.0 collective-permute-done.3.other_far_ref
  24.9 2.1 %outer_products.1 = (bf16[512,1024]{1,0:T(8,128)(2,1)S(1)}, f32[512,128]{1,0:T(8,128)S(1)}, f32[512,128]{1,0:T(8,128)S(1)}, bf16[512,128]{1,0:T(8,128)(2,1)S(1)}) custom-call(s32[2]{0:T(128)S(1)} %pad_add_fusion.ids_ref, bf16[4,144,128]{2,1,0:T(8,128)(2,1)S(1)} %slice.41.near_ref, bf16[4,144,128]{2,1,0:T(8,128)(2,1)S(1)} %collective-permute-done.1.far_ref, ...), custom_call_target="tpu_custom_call" | custom-call | tf_op jit(solution)/shard_map/outer_products/pallas_call | solution.py:785
  27.1 0.0 copy-start.1
  27.1 0.0 copy-start.2
  27.1 1.4 %turned.1 = (bf16[1024,128]{1,0:T(8,128)(2,1)S(1)}, bf16[1024,128]{1,0:T(8,128)(2,1)S(1)}) custom-call(s32[2]{0:T(128)S(1)} %pad_add_fusion.ids_ref, bf16[4,144,128]{2,1,0:T(8,128)(2,1)S(1)} %slice.41.near_ref, bf16[4,144,128]{2,1,0:T(8,128)(2,1)S(1)} %collective-permute-done.1.far_ref), custom_call_target="tpu_custom_call" | custom-call | tf_op jit(solution)/shard_map/turned/pallas_call | solution.py:808
  28.5 0.7 %collective-permute-done.far_ref = bf16[4,128,128]{2,1,0:T(8,128)(2,1)S(1)} collective-permute-done((bf16[4,128,128]{2,1,0:T(8,128)(2,1)S(1)}, bf16[4,128,128]{2,1,0:T(8,128)(2,1)S(1)}, u32[]{:S(2)}, u32[]{:S(2)}) %collective-permute-start) | collective-permute-done | bytes 131104 | tf_op jit(solution)/shard_map/ppermute | solution.py:681
  29.2 0.0 copy-done.1
  29.2 0.0 copy-done.2
  29.2 2.4 %transition.1 = (bf16[64,128]{1,0:T(8,128)(2,1)}, bf16[512,128]{1,0:T(8,128)(2,1)S(1)}, bf16[512,128]{1,0:T(8,128)(2,1)S(1)}, bf16[512,512]{1,0:T(8,128)(2,1)S(1...) custom-call(s32[2]{0:T(128)S(1)} %pad_add_fusion.ids_ref, bf16[4,128,128]{2,1,0:T(8,128)(2,1)S(1)} %slice.40.near_ref, ...), custom_call_target="tpu_custom_call" | custom-call | tf_op jit(solution)/shard_map/transition/pallas_call | solution.py:823
  31.6 0.0 collective-permute-start.4
  31.6 0.8 %out_weight.1.refs_0_ = bf16[1024,128]{1,0:T(8,128)(2,1)S(1)} custom-call(bf16[512,1024]{1,0:T(8,128)(2,1)S(1)} %get-tuple-element.67.outer_ref, bf16[512,128]{1,0:T(8,128)(2,1)S(1)} %get-tuple-element.66.opm_ref), custom_call_target="tpu_custom_call" | custom-call | tf_op jit(solution)/shard_map/out_weight/pallas_call | solution.py:852
  32.4 0.4 transition_weights.1
  32.8 0.2 collective-permute-done.4.other_opm_ref
  33.0 1.6 %projector_parts.1 = (bf16[64,256]{1,0:T(8,128)(2,1)S(1)}, bf16[256,256]{1,0:T(8,128)(2,1)S(1)}) custom-call(s32[2]{0:T(128)S(1)} %pad_add_fusion.ids_ref, bf16[512,128]{1,0:T(8,128)(2,1)S(1)} %get-tuple-element.66.opm_ref, bf16[512,128]{1,0:T(8,128)(2,1)S(1)} %collective-permute-done.4.other_opm_ref, bf16[1024,128]{1,0:T(8,128)(2,1)S(1)} %get-tuple-element.75.rightt_ref, ...), custom_call_target="tpu_custom_call" | custom-call | tf_op jit(solution)/shard_map/projector_parts/pallas_call | solution.py:871
  34.6 1.5 %collective-permute-start.7 = (bf16[64,256]{1,0:T(8,128)(2,1)S(1)}, bf16[64,256]{1,0:T(8,128)(2,1)S(1)}, u32[]{:S(2)}, u32[]{:S(2)}) collective-permute-start(bf16[64,256]{1,0:T(8,128)(2,1)S(1)} %get-tuple-element.79), channel_id=1, source_target_pairs={{0,9},{1,8},{2,11},{3,10},{4,13},{5,12},{6,15},{7,14},{8,1},{9,0},... | collective-permute-start | bytes 98312 | tf_op jit(solution)/shard_map/ppermute | solution.py:691
  36.1 0.5 collective-permute-start.6
  36.6 0.0 collective-permute-start.5
  36.6 0.5 %collective-permute-start.8 = (bf16[1024,128]{1,0:T(8,128)(2,1)S(1)}, bf16[1024,128]{1,0:T(8,128)(2,1)S(1)}, u32[]{:S(2)}, u32[]{:S(2)}) collective-permute-start(bf16[1024,128]{1,0:T(8,128)(2,1)S(1)} %out_weight.1.refs_0_), channel_id=1, source_target_pairs={{0,8},{8,0},{1,9},{9,1},{2,10},{10,2},{3,11},{11,3},{4,12},{12,4},... | collective-permute-start | bytes 786440 | tf_op jit(solution)/shard_map/ppermute | solution.py:670
  37.1 0.3 features.1
  37.4 0.5 %collective-permute-done.7 = bf16[64,256]{1,0:T(8,128)(2,1)S(1)} collective-permute-done((bf16[64,256]{1,0:T(8,128)(2,1)S(1)}, bf16[64,256]{1,0:T(8,128)(2,1)S(1)}, u32[]{:S(2)}, u32[]{:S(2)}) %collective-permute-start.7) | collective-permute-done | bytes 32800 | tf_op jit(solution)/shard_map/ppermute | solution.py:691
  38.0 2.0 %collective-permute-done.6 = bf16[64,256]{1,0:T(8,128)(2,1)S(1)} collective-permute-done((bf16[64,256]{1,0:T(8,128)(2,1)S(1)}, bf16[64,256]{1,0:T(8,128)(2,1)S(1)}, u32[]{:S(2)}, u32[]{:S(2)}) %collective-permute-start.6) | collective-permute-done | bytes 32800 | tf_op jit(solution)/shard_map/ppermute | solution.py:681
  40.0 0.0 collective-permute-done.5
  40.0 0.7 %broadcast_in_dim.3 = bf16[4,64,256]{2,1,0:T(8,128)(2,1)} broadcast(bf16[64,256]{1,0:T(8,128)(2,1)S(1)} %add_convert_fusion), dimensions={1,2} | broadcast | bytes 163840 | tf_op jit(solution)/shard_map/broadcast_in_dim | solution.py:916
  40.7 3.3 %all-to-all-start.1 = ((bf16[4,64,256]{2,1,0:T(8,128)(2,1)}), bf16[4,64,256]{2,1,0:T(8,128)(2,1)S(1)}, u32[]{:S(2)}, u32[]{:S(2)}) async-start(bf16[4,64,256]{2,1,0:T(8,128)(2,1)} %broadcast_in_dim.3), calls=%async_computation.1 | async-start | bytes 262144 | tf_op jit(solution)/shard_map/all_to_all | solution.py:778
  44.0 0.1 collective-permute-start.9
  44.1 0.5 collective-permute-start.10
  44.6 0.7 %reshape.53 = bf16[64,4,256]{2,1,0:T(4,128)(2,1)} reshape(bf16[256,256]{1,0:T(8,128)(2,1)S(1)} %features.1) | data formatting | bytes 262144 | tf_op jit(solution)/shard_map/reshape | solution.py:920
  45.3 0.1 collective-permute-done.9.refs_4_
  45.4 0.2 collective-permute-done.10.refs_5_
  45.6 0.0 collective-permute-done.8.refs_3_
  45.6 1.0 %sums_over_depth.1 = (f32[1024,128]{1,0:T(8,128)}, f32[128,512]{1,0:T(8,128)}, f32[512,128]{1,0:T(8,128)}) custom-call(bf16[1024,128]{1,0:T(8,128)(2,1)S(1)} %out_weight.1.refs_0_, bf16[128,512]{1,0:T(8,128)(2,1)S(1)} %get-tuple-element.92.refs_1_, bf16[512,128]{1,0:T(8,128)(2,1)S(1)} %get-tuple-element.93.refs_2_, ...), custom_call_target="tpu_custom_call" | custom-call | tf_op jit(solution)/shard_map/sums_over_depth/pallas_call | solution.py:898
  46.6 3.3 %all-to-all-done.1 = bf16[4,64,256]{2,1,0:T(8,128)(2,1)S(1)} async-done(((bf16[4,64,256]{2,1,0:T(8,128)(2,1)}), bf16[4,64,256]{2,1,0:T(8,128)(2,1)S(1)}, u32[]{:S(2)}, u32[]{:S(2)}) %all-to-all-start.1) | async-done | bytes 131104 | tf_op jit(solution)/shard_map/all_to_all | solution.py:778
  49.9 0.6 %slice_bitcast_fusion = (f32[256,32]{0,1:T(8,128)}, f32[256,32]{0,1:T(8,128)}) fusion(f32[1,64,256]{2,1,0:T(8,128)S(1)} %add_add_fusion), kind=kLoop, calls=%fused_computation.2 | loop fusion | bytes 131072 | tf_op jit(solution)/shard_map/transpose | solution.py:923
  (4 shorter events, 0.1 us)
Async XLA Ops:
  18.0 6.8 %copy-start = (bf16[1024,128]{1,0:T(8,128)(2,1)S(1)}, bf16[1024,128]{1,0:T(8,128)(2,1)}, u32[]{:S(2)}) copy-start(bf16[1024,128]{1,0:T(8,128)(2,1)} %wout_ref.1) | copy-start | bytes 786436
  18.0 5.2 %collective-permute-start.1 = (bf16[4,144,128]{2,1,0:T(8,128)(2,1)S(1)}, bf16[4,144,128]{2,1,0:T(8,128)(2,1)S(1)}, u32[]{:S(2)}, u32[]{:S(2)}) collective-permute-start(bf16[4,144,128]{2,1,0:T(8,128)(2,1)S(1)} %slice.41.near_ref), channel_id=1, source_target_pairs={{0,1},{1,0},{2,3},{3,2},{4,5},{5,4},{6,7},{7,6},{8,9},{9,8},{10,11... | collective-permute-start | bytes 442376 | tf_op jit(solution)/shard_map/ppermute | solution.py:681
  19.6 5.3 %collective-permute-start.2 = (bf16[4,144,128]{2,1,0:T(8,128)(2,1)S(1)}, bf16[4,144,128]{2,1,0:T(8,128)(2,1)S(1)}, u32[]{:S(2)}, u32[]{:S(2)}) collective-permute-start(bf16[4,144,128]{2,1,0:T(8,128)(2,1)S(1)} %slice.41.near_ref), channel_id=1, source_target_pairs={{0,8},{8,0},{1,9},{9,1},{2,10},{10,2},{3,11},{11,3},{4,12},{12,4},... | collective-permute-start | bytes 442376 | tf_op jit(solution)/shard_map/ppermute | solution.py:670
  23.2 1.7 %collective-permute-start.3 = (bf16[4,144,128]{2,1,0:T(8,128)(2,1)S(1)}, bf16[4,144,128]{2,1,0:T(8,128)(2,1)S(1)}, u32[]{:S(2)}, u32[]{:S(2)}) collective-permute-start(bf16[4,144,128]{2,1,0:T(8,128)(2,1)S(1)} %collective-permute-done.1.far_ref), channel_id=1, source_target_pairs={{0,8},{8,0},{1,9},{9,1},{2,10},{10,2},{3,11},{11,3},{4,12},{12,4},... | collective-permute-start | bytes 442376 | tf_op jit(solution)/shard_map/ppermute | solution.py:670
  23.2 6.0 %collective-permute-start = (bf16[4,128,128]{2,1,0:T(8,128)(2,1)S(1)}, bf16[4,128,128]{2,1,0:T(8,128)(2,1)S(1)}, u32[]{:S(2)}, u32[]{:S(2)}) collective-permute-start(bf16[4,128,128]{2,1,0:T(8,128)(2,1)S(1)} %slice.40.near_ref), channel_id=1, source_target_pairs={{0,1},{1,0},{2,3},{3,2},{4,5},{5,4},{6,7},{7,6},{8,9},{9,8},{10,11... | collective-permute-start | bytes 393224 | tf_op jit(solution)/shard_map/ppermute | solution.py:681
  27.1 2.1 %copy-start.1 = (bf16[128,512]{1,0:T(8,128)(2,1)S(1)}, bf16[128,512]{1,0:T(8,128)(2,1)}, u32[]{:S(2)}) copy-start(bf16[128,512]{1,0:T(8,128)(2,1)} %hid_ref.1) | copy-start | bytes 393220
  27.1 2.1 %copy-start.2 = (bf16[512,128]{1,0:T(8,128)(2,1)S(1)}, bf16[512,128]{1,0:T(8,128)(2,1)}, u32[]{:S(2)}) copy-start(bf16[512,128]{1,0:T(8,128)(2,1)} %back_ref.1) | copy-start | bytes 393220
  31.6 1.3 %collective-permute-start.4 = (bf16[512,128]{1,0:T(8,128)(2,1)S(1)}, bf16[512,128]{1,0:T(8,128)(2,1)S(1)}, u32[]{:S(2)}, u32[]{:S(2)}) collective-permute-start(bf16[512,128]{1,0:T(8,128)(2,1)S(1)} %get-tuple-element.66.opm_ref), channel_id=1, source_target_pairs={{0,8},{8,0},{1,9},{9,1},{2,10},{10,2},{3,11},{11,3},{4,12},{12,4},... | collective-permute-start | bytes 393224 | tf_op jit(solution)/shard_map/ppermute | solution.py:670
  34.6 3.4 %collective-permute-start.7 = (bf16[64,256]{1,0:T(8,128)(2,1)S(1)}, bf16[64,256]{1,0:T(8,128)(2,1)S(1)}, u32[]{:S(2)}, u32[]{:S(2)}) collective-permute-start(bf16[64,256]{1,0:T(8,128)(2,1)S(1)} %get-tuple-element.79), channel_id=1, source_target_pairs={{0,9},{1,8},{2,11},{3,10},{4,13},{5,12},{6,15},{7,14},{8,1},{9,0},... | collective-permute-start | bytes 98312 | tf_op jit(solution)/shard_map/ppermute | solution.py:691
  36.1 3.9 %collective-permute-start.6 = (bf16[64,256]{1,0:T(8,128)(2,1)S(1)}, bf16[64,256]{1,0:T(8,128)(2,1)S(1)}, u32[]{:S(2)}, u32[]{:S(2)}) collective-permute-start(bf16[64,256]{1,0:T(8,128)(2,1)S(1)} %get-tuple-element.79), channel_id=1, source_target_pairs={{0,1},{1,0},{2,3},{3,2},{4,5},{5,4},{6,7},{7,6},{8,9},{9,8},{10,11... | collective-permute-start | bytes 98312 | tf_op jit(solution)/shard_map/ppermute | solution.py:681
  36.6 3.4 %collective-permute-start.5 = (bf16[64,256]{1,0:T(8,128)(2,1)S(1)}, bf16[64,256]{1,0:T(8,128)(2,1)S(1)}, u32[]{:S(2)}, u32[]{:S(2)}) collective-permute-start(bf16[64,256]{1,0:T(8,128)(2,1)S(1)} %get-tuple-element.79), channel_id=1, source_target_pairs={{0,8},{8,0},{1,9},{9,1},{2,10},{10,2},{3,11},{11,3},{4,12},{12,4},... | collective-permute-start | bytes 98312 | tf_op jit(solution)/shard_map/ppermute | solution.py:670
  36.6 9.0 %collective-permute-start.8 = (bf16[1024,128]{1,0:T(8,128)(2,1)S(1)}, bf16[1024,128]{1,0:T(8,128)(2,1)S(1)}, u32[]{:S(2)}, u32[]{:S(2)}) collective-permute-start(bf16[1024,128]{1,0:T(8,128)(2,1)S(1)} %out_weight.1.refs_0_), channel_id=1, source_target_pairs={{0,8},{8,0},{1,9},{9,1},{2,10},{10,2},{3,11},{11,3},{4,12},{12,4},... | collective-permute-start | bytes 786440 | tf_op jit(solution)/shard_map/ppermute | solution.py:670
  40.7 9.2 %all-to-all-start.1 = ((bf16[4,64,256]{2,1,0:T(8,128)(2,1)}), bf16[4,64,256]{2,1,0:T(8,128)(2,1)S(1)}, u32[]{:S(2)}, u32[]{:S(2)}) async-start(bf16[4,64,256]{2,1,0:T(8,128)(2,1)} %broadcast_in_dim.3), calls=%async_computation.1 | async-start | bytes 262144 | tf_op jit(solution)/shard_map/all_to_all | solution.py:778
  44.0 1.4 %collective-permute-start.9 = (bf16[128,512]{1,0:T(8,128)(2,1)S(1)}, bf16[128,512]{1,0:T(8,128)(2,1)S(1)}, u32[]{:S(2)}, u32[]{:S(2)}) collective-permute-start(bf16[128,512]{1,0:T(8,128)(2,1)S(1)} %get-tuple-element.92.refs_1_), channel_id=1, source_target_pairs={{0,8},{8,0},{1,9},{9,1},{2,10},{10,2},{3,11},{11,3},{4,12},{12,4},... | collective-permute-start | bytes 393224 | tf_op jit(solution)/shard_map/ppermute | solution.py:670
  44.1 1.5 %collective-permute-start.10 = (bf16[512,128]{1,0:T(8,128)(2,1)S(1)}, bf16[512,128]{1,0:T(8,128)(2,1)S(1)}, u32[]{:S(2)}, u32[]{:S(2)}) collective-permute-start(bf16[512,128]{1,0:T(8,128)(2,1)S(1)} %get-tuple-element.93.refs_2_), channel_id=1, source_target_pairs={{0,8},{8,0},{1,9},{9,1},{2,10},{10,2},{3,11},{11,3},{4,12},{12,4},... | collective-permute-start | bytes 393224 | tf_op jit(solution)/shard_map/ppermute | solution.py:670

commit v4 on v2

--- a/solution.py
+++ b/solution.py
@@ -288,7 +288,6 @@
     act_hbm,
     grad_hbm,
     sent_ref,
-    pairs_ref,
     scale_ref,
     first_ref,
     second_ref,
@@ -296,7 +295,6 @@
     normed_ref,
     scaled_ref,
     inv_ref,
-    lanes_ref,
     wide_ref,
     tile_ref,
     x_ref,
@@ -306,6 +304,7 @@
 ):
     res, seqs = maskt_ref.shape
     pairs = act_hbm.shape[0]
+    first_pair = 2 * seqs + MASK_ROWS
     copies = [
         pltpu.make_async_copy(source, target, sems.at[at])
         for at, (source, target) in enumerate(
@@ -317,8 +316,8 @@
                 (first_hbm, first_ref),
                 (second_hbm, second_ref),
                 (gain_hbm, gain_ref),
-                (act_hbm, pairs_ref.at[0, pl.ds(0, pairs), :]),
-                (grad_hbm, pairs_ref.at[0, pl.ds(pairs, pairs), :]),
+                (act_hbm, sent_ref.at[0, pl.ds(first_pair, pairs), :]),
+                (grad_hbm, sent_ref.at[0, pl.ds(first_pair + pairs, pairs), :]),
             )
         )
     ]
@@ -353,7 +352,6 @@
     mask_lanes = lax.dot_general(
         tile_ref[...], spread, (((0,), (0,)), ((), ())), preferred_element_type=jnp.float32
     )[:seqs]
-    lanes_ref[...] = mask_lanes
     twice = jnp.concatenate([mask] * (lanes // seqs), axis=1)
     here = lax.broadcasted_iota(jnp.int32, (res, lanes), 1) // seqs == ids_ref[0]
     tile_ref[0:res, :] = jnp.where(here, twice, 0.0)
@@ -366,7 +364,7 @@
                 lane_group == r, wide_ref[at, pl.ds(r, seqs, stride=res), :], both
             )
         sent_ref[0, at * seqs : (at + 1) * seqs, :] = (both * mask_lanes).astype(jnp.bfloat16)
-    sent_ref[0, 2 * seqs :, :] = tile_ref[...].astype(jnp.bfloat16)
+    sent_ref[0, 2 * seqs : first_pair, :] = tile_ref[...].astype(jnp.bfloat16)
 
 
 def outer_kernel(
@@ -382,11 +380,11 @@
     proj_out_ref,
     cnt_ref,
     pm_ref,
+    maskt_ref,
     got_ref,
     leftn_ref,
     mine_ref,
     turn_ref,
-    maskt_ref,
     cntl_ref,
     pml_ref,
 ):
@@ -465,18 +463,35 @@
     proj_out_ref[...] = jnp.dot(outer_ref[...], wturn_ref[...], preferred_element_type=f32)
 
 
-def turn_kernel(sizes, orders, ids_ref, near_ref, far_ref, rightt_ref, leftt_ref, turn_ref):
+def turn_kernel(
+    sizes,
+    orders,
+    ids_ref,
+    near_ref,
+    far_ref,
+    other_near_ref,
+    other_far_ref,
+    rightt_ref,
+    leftt_ref,
+    got_ref,
+    turn_ref,
+):
     seqs, res, _, width = sizes
+    depths, cols = got_ref.shape[0], got_ref.shape[1]
     lanes = res * width
-    residues = turn_ref.shape[0] // width
+    residues = res * cols
+    me_depth = ids_ref[0]
     me_col = ids_ref[1]
+    for order, mine, other in zip(orders, (near_ref, far_ref), (other_near_ref, other_far_ref)):
+        for at, partner in enumerate(order):
+            got_ref[me_depth, me_col ^ partner] = mine[at, 0 : 2 * seqs, :]
+            got_ref[1 - me_depth, me_col ^ partner] = other[at, 0 : 2 * seqs, :]
     for at, out in ((0, leftt_ref), (1, rightt_ref)):
-        for order, blocks in zip(orders, (near_ref, far_ref)):
-            for place, partner in enumerate(order):
-                block = blocks[place, at * seqs : (at + 1) * seqs, :].astype(jnp.float32)
-                block = jnp.concatenate([block] * (lanes // seqs), axis=0)
-                first = pl.multiple_of((me_col ^ partner) * lanes, lanes)
-                turn_ref[pl.ds(first, lanes), :] = block.T
+        for k in range(cols):
+            block = jnp.concatenate(
+                [got_ref[e, k, at * seqs : (at + 1) * seqs, :] for e in range(depths)], axis=0
+            ).astype(jnp.float32)
+            turn_ref[k * lanes : (k + 1) * lanes, :] = block.T
         for d in range(width):
             out[d * residues : (d + 1) * residues, :] = turn_ref[
                 pl.ds(d, residues, stride=width), :
@@ -558,8 +573,11 @@
     leftt_ref,
     wout_ref,
     wturn_ref,
+    maskt_ref,
     normed_ref,
-    lanes_ref,
+    far_normed_ref,
+    other_normed_ref,
+    other_far_normed_ref,
     part_ref,
     spread_ref,
     gf_ref,
@@ -568,26 +586,37 @@
     gor_ref,
     goc_ref,
     gs_ref,
+    rows_ref,
 ):
     seqs, res, pair_cols, width = sizes
     depths, half = gf_ref.shape[0], gf_ref.shape[1]
     residues = half // pair_cols
     lanes = res * width
+    here = 2 * res
     me_depth = ids_ref[0]
     me_col = ids_ref[1]
+    me_y = me_col % 2
+    first_here = (me_col // 2) * here
     f32, bf16 = jnp.float32, jnp.bfloat16
     gf_ref[me_depth] = opm_ref[...].astype(f32)
     gf_ref[1 - me_depth] = other_opm_ref[...].astype(f32)
-
-    for il in range(res):
+    for y, e, block in (
+        (me_y, me_depth, normed_ref),
+        (1 - me_y, me_depth, far_normed_ref),
+        (me_y, 1 - me_depth, other_normed_ref),
+        (1 - me_y, 1 - me_depth, other_far_normed_ref),
+    ):
+        rows_ref[y, e] = block[...]
+
+    for il in range(here):
         for e in range(depths):
-            first = pl.multiple_of((me_col * res + il) * pair_cols, pair_cols)
+            first = pl.multiple_of((first_here + il) * pair_cols, pair_cols)
             grow_ref[il * residues + e * pair_cols : il * residues + (e + 1) * pair_cols, :] = (
                 gf_ref[e, pl.ds(first, pair_cols), :].astype(bf16)
             )
-    my_half = (me_col * res) // pair_cols
-    my_first = me_col * res - my_half * pair_cols
-    for jl in range(res):
+    my_half = first_here // pair_cols
+    my_first = first_here - my_half * pair_cols
+    for jl in range(here):
         gcol_ref[jl * residues : (jl + 1) * residues, :] = gf_ref[
             my_half, pl.ds(my_first + jl, residues, stride=pair_cols), :
         ].astype(bf16)
@@ -599,30 +628,54 @@
                 (((1,), (1,)), ((), ())),
                 preferred_element_type=f32,
             )
-            turned = butterfly(
-                [piece[a * residues : (a + 1) * residues] for a in range(4)], width
-            )
-            for dl in range(4):
-                first = (dh * 4 + dl) * residues
-                out[first : first + residues, :] = turned[dl].astype(bf16)
-    mask_lanes = lanes_ref[...]
+            for y in range(2):
+                turned = butterfly(
+                    [
+                        piece[(y * res + a) * residues : (y * res + a + 1) * residues]
+                        for a in range(4)
+                    ],
+                    width,
+                )
+                for dl in range(4):
+                    first = (dh * 4 + dl) * residues
+                    out[first : first + residues, y * lanes : (y + 1) * lanes] = turned[dl].astype(
+                        bf16
+                    )
+    group = lax.broadcasted_iota(jnp.int32, (here, here * width), 1) // width
+    spread = (group == lax.broadcasted_iota(jnp.int32, (here, here * width), 0)).astype(f32)
+    mask_lanes = lax.dot_general(
+        maskt_ref[pl.ds(pl.multiple_of(first_here, here), here), :],
+        spread,
+        (((0,), (0,)), ((), ())),
+        preferred_element_type=f32,
+    )
     lane_group = lax.broadcasted_iota(jnp.int32, (seqs, lanes), 1) // width
     for at, (lhs, rhs) in enumerate(((rightt_ref, gor_ref), (leftt_ref, goc_ref))):
         total = lax.dot_general(
             lhs[...], rhs[...], (((0,), (0,)), ((), ())), preferred_element_type=f32
-        )[:seqs]
+        )
         total = (total * mask_lanes).astype(bf16).astype(f32)
-        for r in range(res):
-            gs_ref[at, pl.ds(r, seqs, stride=res), :] = jnp.where(lane_group == r, total, 0.0)
-    spread = jnp.concatenate([gs_ref[0], gs_ref[1]], axis=1).astype(bf16)
-    spread_ref[...] = spread
-    cross = lax.dot_general(
-        spread, normed_ref[...], (((0,), (0,)), ((), ())), preferred_element_type=f32
-    )
+        for y in range(2):
+            for e in range(depths):
+                block = total[e * seqs : (e + 1) * seqs, y * lanes : (y + 1) * lanes]
+                for r in range(res):
+                    gs_ref[at, y, e, pl.ds(r, seqs, stride=res), :] = jnp.where(
+                        lane_group == r, block, 0.0
+                    )
+    spread_ref[...] = jnp.concatenate(
+        [gs_ref[0, me_y, me_depth], gs_ref[1, me_y, me_depth]], axis=1
+    ).astype(bf16)
+    rows = rows_ref.shape[2]
     for at in range(2):
-        total = cross[at * lanes : at * lanes + width]
+        cross = lax.dot_general(
+            gs_ref[at].reshape(2 * depths * rows, lanes).astype(bf16),
+            rows_ref[...].reshape(2 * depths * rows, rows_ref.shape[3]),
+            (((0,), (0,)), ((), ())),
+            preferred_element_type=f32,
+        )
+        total = cross[:width]
         for r in range(1, res):
-            total = total + cross[at * lanes + r * width : at * lanes + (r + 1) * width]
+            total = total + cross[r * width : (r + 1) * width]
         part_ref[at * width : (at + 1) * width, :] = total.astype(bf16)
 
 
@@ -675,16 +728,6 @@
 def swap_col(block, partner):
     count = lax.axis_size("col")
     return lax.ppermute(block, "col", [(at, at ^ partner) for at in range(count)])
-
-
-def swap_both(block, partner):
-    count = lax.axis_size("col")
-    pairs = [
-        (depth * count + at, (1 - depth) * count + (at ^ partner))
-        for depth in range(2)
-        for at in range(count)
-    ]
-    return lax.ppermute(block, ("depth", "col"), pairs)
 
 
 def whole_plan(
@@ -724,11 +767,10 @@
         outer_width, pair_width
     )
     shape = jax.ShapeDtypeStruct
-    sent, sent_pairs, scale, first, second, gain, normed, scaled, inv, mask_lanes = pl.pallas_call(
+    sent, scale, first, second, gain, normed, scaled, inv = pl.pallas_call(
         pre_kernel,
         out_shape=(
-            shape((1, rows, pair_width), bf16),
-            shape((1, 2 * per, pair_width), bf16),
+            shape((1, rows + 2 * per, pair_width), bf16),
             shape((1, channels), f32),
             shape((width, channels), bf16),
             shape((width, channels), bf16),
@@ -736,10 +778,9 @@
             shape((seqs * res, channels), bf16),
             shape((seqs * res, channels), f32),
             shape((seqs * res, 1), f32),
-            shape((seqs, lanes), f32),
         ),
         in_specs=[smem] + [pl.BlockSpec(memory_space=pltpu.HBM)] * 9,
-        out_specs=[vmem] * 10,
+        out_specs=[vmem] * 8,
         scratch_shapes=[
             pltpu.VMEM((2, seqs * res, lanes), f32),
             pltpu.VMEM((MASK_ROWS, lanes), f32),
@@ -769,53 +810,58 @@
     )
     near_order = (0,) + Z_PARTNERS
     far_order = tuple(at ^ Y_PARTNER for at in near_order)
-    came = [swap_col(sent, partner) for partner in Z_PARTNERS]
-    came[0], sent_pairs = lax.optimization_barrier((came[0], sent_pairs))
-    near = jnp.concatenate([sent] + came)
-    pair_near = jnp.concatenate(
-        [sent_pairs] + [swap_col(sent_pairs, partner) for partner in Z_PARTNERS]
-    )
+    blocks = lax.optimization_barrier(
+        jnp.concatenate([sent] + [swap_col(sent, partner) for partner in Z_PARTNERS])
+    )
+    near, pair_near = blocks[:, :rows], blocks[:, rows:]
+    far_normed = swap_col(normed, Y_PARTNER)
+    other_normed, other_far_normed = swap_depth(normed), swap_depth(far_normed)
+    near, far_normed, other_normed = lax.optimization_barrier((near, far_normed, other_normed))
     far = swap_col(near, Y_PARTNER)
     pair_far = swap_col(pair_near, Y_PARTNER)
+    other_near, other_far = swap_depth(near), swap_depth(far)
     sizes = (seqs, res, pair_cols, width)
     orders = (near_order, far_order)
-    outer, proj_out, cnt, pm = pl.pallas_call(
+    outer, proj_out, cnt, pm, maskt = pl.pallas_call(
         functools.partial(outer_kernel, sizes, orders),
         out_shape=(
             shape((half, outer_width), bf16),
             shape((half, pair_width), f32),
             shape((half, lanes), f32),
             shape((half, lanes), bf16),
+            shape((residues, depths * seqs), f32),
         ),
         in_specs=[smem] + [vmem] * 5,
-        out_specs=[vmem] * 4,
+        out_specs=[vmem] * 5,
         scratch_shapes=[
             pltpu.VMEM((depths, cols, rows, pair_width), bf16),
             pltpu.VMEM((depths * seqs, residues * width), bf16),
             pltpu.VMEM((pair_cols * width, depths * seqs), bf16),
             pltpu.VMEM((pair_cols * width, depths * seqs), f32),
-            pltpu.VMEM((residues, depths * seqs), f32),
             pltpu.VMEM((half, lanes), bf16),
             pltpu.VMEM((half, lanes), bf16),
         ],
         compiler_params=params,
         name="outer_products",
-    )(ids, near, far, swap_depth(near), swap_depth(far), wturn)
-    near, far, proj_out = lax.optimization_barrier((near, far, proj_out))
+    )(ids, near, far, other_near, other_far, wturn)
+    other_near, other_far, proj_out = lax.optimization_barrier((other_near, other_far, proj_out))
     rightt, leftt = pl.pallas_call(
         functools.partial(turn_kernel, sizes, orders),
         out_shape=(
             shape((residues * width, depths * seqs), bf16),
             shape((residues * width, depths * seqs), bf16),
         ),
-        in_specs=[smem] + [vmem] * 2,
+        in_specs=[smem] + [vmem] * 4,
         out_specs=[vmem] * 2,
-        scratch_shapes=[pltpu.VMEM((residues * width, depths * seqs), f32)],
+        scratch_shapes=[
+            pltpu.VMEM((depths, cols, 2 * seqs, pair_width), bf16),
+            pltpu.VMEM((residues * width, depths * seqs), f32),
+        ],
         compiler_params=params,
         name="turned",
-    )(ids, near, far)
-    pair_far, rightt, leftt, proj_out = lax.optimization_barrier(
-        (pair_far, rightt, leftt, proj_out)
+    )(ids, near, far, other_near, other_far)
+    pair_far, rightt, leftt, proj_out, other_far_normed = lax.optimization_barrier(
+        (pair_far, rightt, leftt, proj_out, other_far_normed)
     )
     couple, opm, pn, gh, hidden, mg = pl.pallas_call(
         functools.partial(transition_kernel, sizes, orders),
@@ -871,19 +917,33 @@
             shape((2 * width, channels), bf16),
             shape((seqs * res, 2 * lanes), bf16),
         ),
-        in_specs=[smem] + [vmem] * 8,
+        in_specs=[smem] + [vmem] * 11,
         out_specs=[vmem] * 2,
         scratch_shapes=[
             pltpu.VMEM((depths, half, pair_width), f32),
-            pltpu.VMEM((res * residues, pair_width), bf16),
-            pltpu.VMEM((res * residues, pair_width), bf16),
-            pltpu.VMEM((residues * width, lanes), bf16),
-            pltpu.VMEM((residues * width, lanes), bf16),
-            pltpu.VMEM((2, seqs * res, lanes), f32),
+            pltpu.VMEM((2 * res * residues, pair_width), bf16),
+            pltpu.VMEM((2 * res * residues, pair_width), bf16),
+            pltpu.VMEM((residues * width, 2 * lanes), bf16),
+            pltpu.VMEM((residues * width, 2 * lanes), bf16),
+            pltpu.VMEM((2, 2, depths, seqs * res, lanes), f32),
+            pltpu.VMEM((2, depths, seqs * res, channels), bf16),
         ],
         compiler_params=params,
         name="projector_parts",
-    )(ids, opm, other_opm, rightt, leftt, output_weight, wturn, normed, mask_lanes)
+    )(
+        ids,
+        opm,
+        other_opm,
+        rightt,
+        leftt,
+        output_weight,
+        wturn,
+        maskt,
+        normed,
+        far_normed,
+        other_normed,
+        other_far_normed,
+    )
     feat = pl.pallas_call(
         functools.partial(feature_kernel, res),
         out_shape=shape((seqs * res, channels), bf16),
@@ -904,15 +964,9 @@
         compiler_params=params,
         name="sums_over_depth",
     )(dout, dhid, dback, *other_weights)
-    total = part.astype(f32)
-    kept = lax.optimization_barrier(total.astype(bf16))
-    near_ones = [swap_depth(kept), swap_col(kept, Y_PARTNER), swap_both(kept, Y_PARTNER)]
-    near_ones, feat = lax.optimization_barrier((near_ones, feat))
-    total = pairwise_sum([block.astype(f32) for block in [kept] + near_ones])
-    kept = lax.optimization_barrier(total.astype(bf16))
-    far_ones = [swap_col(kept, partner) for partner in Z_PARTNERS]
-    far_ones, dout, dhid, dback = lax.optimization_barrier((far_ones, dout, dhid, dback))
-    total = pairwise_sum([block.astype(f32) for block in [kept] + far_ones])
+    came = [swap_col(part, partner) for partner in Z_PARTNERS]
+    came, feat, dout, dhid, dback = lax.optimization_barrier((came, feat, dout, dhid, dback))
+    total = pairwise_sum([block.astype(f32) for block in [part] + came])
     return (
         feat.reshape(seqs, res, channels),
         couple.reshape(res, pair_cols, pair_width),

time: 47.5 us -> 42.8 us (0.901)
  starting transfers between devices: 20.7 us -> 16.4 us
  waiting for transfers between devices: 12.3 us -> 11.3 us
  Pallas kernels: 11.9 us -> 12.4 us
    ppermute x12 -> x9, starting transfers between devices: 18.3 us -> 15.3 us  [swap_col(): lax.ppermute(block, 'col', [(at, at ^ partner) for at in range(count)])]
    ppermute x1 -> x0, starting transfers between devices: 1.49 us -> none  [swap_both(): return lax.ppermute(block, ('depth', 'col'), pairs)]
    ppermute x1 -> x0, waiting for transfers between devices: 0.54 us -> none  [swap_both(): return lax.ppermute(block, ('depth', 'col'), pairs)]
    ppermute x12 -> x9, waiting for transfers between devices: 11.6 us -> 11.1 us  [swap_col(): lax.ppermute(block, 'col', [(at, at ^ partner) for at in range(count)])]
    ppermute x7 -> x8, starting transfers between devices: 0.93 us -> 1.16 us  [swap_depth(): return lax.ppermute(block, 'depth', [(0, 1), (1, 0)])]
  transfers between devices with their start and end apart: 20 -> 17, of which waited for: 9 -> 8; matrix products, arithmetic and copies ran while one was open for 2% -> 0% of each run, Pallas kernels for 13% -> 19%
where the time goes in v4:
time: 42.8 us; the launch traced here: 42.5 us
  starting transfers between devices  16.4 us (38%)
  Pallas kernels  12.4 us (29%)
  waiting for transfers between devices  11.3 us (26%)
  local copies, waits for them, and re-layouts  1.47 us (3%)
  between operations  0.79 us (2%)
    ppermute x9, starting transfers between devices, swap_col(): lax.ppermute(block, 'col', [(at, at ^ partner) for at in range(count)])  15.3 us
    ppermute x9, waiting for transfers between devices, swap_col(): lax.ppermute(block, 'col', [(at, at ^ partner) for at in range(count)])  11.1 us
    pallas_call x1, Pallas kernels, whole_plan(): pl.pallas_call(functools.partial(transition_kernel, sizes, orders), out_s...  2.41 us
    pallas_call x1, Pallas kernels, whole_plan(): pl.pallas_call(functools.partial(outer_kernel, sizes, orders), out_shape=...  2.13 us
    pallas_call x1, Pallas kernels, whole_plan(): pl.pallas_call(functools.partial(projector_kernel, sizes), out_shape=(sha...  2.04 us
    pallas_call x1, Pallas kernels, whole_plan(): pl.pallas_call(pre_kernel, out_shape=(shape((1, rows + 2 * per, pair_widt...  1.91 us
    pallas_call x1, Pallas kernels, whole_plan(): pl.pallas_call(functools.partial(turn_kernel, sizes, orders), out_shape=(...  1.39 us
    ppermute x8, starting transfers between devices, swap_depth(): return lax.ppermute(block, 'depth', [(0, 1), (1, 0)])  1.16 us
  transfers between devices with their start and end apart: 17, of which 8 were waited for; matrix products, arithmetic and copies ran while one was open for 0% of the time, Pallas kernels for 19%

profile of v4, /device:TPU:0, one launch (start us, length us, event | category | flops | bytes accessed | tf_op | source)
XLA Modules:
  0.0 42.5 jit_solution(13394182221764130862)
XLA Ops:
  0.6 0.1 pad_add_fusion.ids_ref
  0.7 1.9 %project.1 = (bf16[1,272,128]{2,1,0:T(8,128)(2,1)S(1)}, f32[1,256]{1,0:T(1,128)S(1)}, bf16[32,256]{1,0:T(8,128)(2,1)S(1)}, bf16[32,256]{1,0:T(8,128)(2,1)S(1)}, ...) custom-call(s32[2]{0:T(128)S(1)} %pad_add_fusion.ids_ref, ...), custom_call_target="tpu_custom_call" | custom-call | tf_op jit(solution)/shard_map/project/pallas_call | solution.py:770
  2.6 5.1 %collective-permute-start.2 = (bf16[1,272,128]{2,1,0:T(8,128)(2,1)S(1)}, bf16[1,272,128]{2,1,0:T(8,128)(2,1)S(1)}, u32[]{:S(2)}, u32[]{:S(2)}) collective-permute-start(bf16[1,272,128]{2,1,0:T(8,128)(2,1)S(1)} %get-tuple-element.57), channel_id=1, source_target_pairs={{0,6},{1,7},{2,4},{3,5},{4,2},{5,3},{6,0},{7,1},{8,14},{9,15},{10,... | collective-permute-start | bytes 208904 | tf_op jit(solution)/shard_map/ppermute | solution.py:730
  7.7 0.0 collective-permute-start.1
  7.8 0.6 %collective-permute-start = (bf16[1,272,128]{2,1,0:T(8,128)(2,1)S(1)}, bf16[1,272,128]{2,1,0:T(8,128)(2,1)S(1)}, u32[]{:S(2)}, u32[]{:S(2)}) collective-permute-start(bf16[1,272,128]{2,1,0:T(8,128)(2,1)S(1)} %get-tuple-element.57), channel_id=1, source_target_pairs={{0,2},{1,3},{2,0},{3,1},{4,6},{5,7},{6,4},{7,5},{8,10},{9,11},{10,... | collective-permute-start | bytes 208904 | tf_op jit(solution)/shard_map/ppermute | solution.py:730
  8.4 0.0 collective-permute-start.5
  8.4 1.7 %collective-permute-start.4 = (bf16[256,256]{1,0:T(8,128)(2,1)S(1)}, bf16[256,256]{1,0:T(8,128)(2,1)S(1)}, u32[]{:S(2)}, u32[]{:S(2)}) collective-permute-start(bf16[256,256]{1,0:T(8,128)(2,1)S(1)} %get-tuple-element.58.normed_ref), channel_id=1, source_target_pairs={{0,1},{1,0},{2,3},{3,2},{4,5},{5,4},{6,7},{7,6},{8,9},{9,8},{10,11... | collective-permute-start | bytes 393224 | tf_op jit(solution)/shard_map/ppermute | solution.py:730
  10.1 0.4 collective-permute-done.2
  10.4 3.2 %collective-permute-done.1 = bf16[1,272,128]{2,1,0:T(8,128)(2,1)S(1)} collective-permute-done((bf16[1,272,128]{2,1,0:T(8,128)(2,1)S(1)}, bf16[1,272,128]{2,1,0:T(8,128)(2,1)S(1)}, u32[]{:S(2)}, u32[]{:S(2)}) %collective-permute-start.1) | collective-permute-done | bytes 69664 | tf_op jit(solution)/shard_map/ppermute | solution.py:730
  13.7 0.0 collective-permute-done
  13.7 0.0 copy-start
  13.7 0.0 collective-permute-done.5.other_normed_ref
  13.7 0.6 %collective-permute-done.4.far_normed_ref = bf16[256,256]{1,0:T(8,128)(2,1)S(1)} collective-permute-done((bf16[256,256]{1,0:T(8,128)(2,1)S(1)}, bf16[256,256]{1,0:T(8,128)(2,1)S(1)}, u32[]{:S(2)}, u32[]{:S(2)}) %collective-permute-start.4) | collective-permute-done | bytes 131104 | tf_op jit(solution)/shard_map/ppermute | solution.py:730
  14.3 1.7 %collective-permute-start.6 = (bf16[4,144,128]{2,1,0:T(8,128)(2,1)S(1)}, bf16[4,144,128]{2,1,0:T(8,128)(2,1)S(1)}, u32[]{:S(2)}, u32[]{:S(2)}) collective-permute-start(bf16[4,144,128]{2,1,0:T(8,128)(2,1)S(1)} %slice.17.near_ref), channel_id=1, source_target_pairs={{0,1},{1,0},{2,3},{3,2},{4,5},{5,4},{6,7},{7,6},{8,9},{9,8},{10,11... | collective-permute-start | bytes 442376 | tf_op jit(solution)/shard_map/ppermute | solution.py:730
  16.0 0.0 collective-permute-start.7
  16.0 3.8 %collective-permute-done.6.far_ref = bf16[4,144,128]{2,1,0:T(8,128)(2,1)S(1)} collective-permute-done((bf16[4,144,128]{2,1,0:T(8,128)(2,1)S(1)}, bf16[4,144,128]{2,1,0:T(8,128)(2,1)S(1)}, u32[]{:S(2)}, u32[]{:S(2)}) %collective-permute-start.6) | collective-permute-done | bytes 147488 | tf_op jit(solution)/shard_map/ppermute | solution.py:730
  19.8 0.0 collective-permute-start.8
  19.8 1.7 %collective-permute-start.3 = (bf16[4,128,128]{2,1,0:T(8,128)(2,1)S(1)}, bf16[4,128,128]{2,1,0:T(8,128)(2,1)S(1)}, u32[]{:S(2)}, u32[]{:S(2)}) collective-permute-start(bf16[4,128,128]{2,1,0:T(8,128)(2,1)S(1)} %slice.16.near_ref), channel_id=1, source_target_pairs={{0,1},{1,0},{2,3},{3,2},{4,5},{5,4},{6,7},{7,6},{8,9},{9,8},{10,11... | collective-permute-start | bytes 393224 | tf_op jit(solution)/shard_map/ppermute | solution.py:730
  21.5 0.2 collective-permute-start.9
  21.8 0.1 copy.19
  21.9 0.0 collective-permute-done.8.other_far_ref
  21.9 2.1 %outer_products.1 = (bf16[512,1024]{1,0:T(8,128)(2,1)S(1)}, f32[512,128]{1,0:T(8,128)S(1)}, f32[512,128]{1,0:T(8,128)S(1)}, bf16[512,128]{1,0:T(8,128)(2,1)S(1)}, f32[32,128]{1,0:T(8,128)S(1)}) custom-call(s32[2]{0:T(128)S(1)} %pad_add_fusion.ids_ref, bf16[4,144,128]{2,1,0:T(8,128)(2,1)S(1)} %slice.17.near_ref, ...), custom_call_target="tpu_custom_call" | custom-call | tf_op jit(solution)/shard_map/outer_products/pallas_call | solution.py:825
  24.0 0.0 copy-start.1
  24.0 0.0 copy-start.2
  24.0 1.4 %turned.1 = (bf16[1024,128]{1,0:T(8,128)(2,1)S(1)}, bf16[1024,128]{1,0:T(8,128)(2,1)S(1)}) custom-call(s32[2]{0:T(128)S(1)} %pad_add_fusion.ids_ref, bf16[4,144,128]{2,1,0:T(8,128)(2,1)S(1)} %slice.17.near_ref, bf16[4,144,128]{2,1,0:T(8,128)(2,1)S(1)} %collective-permute-done.6.far_ref, bf16[4,144,128]{2,1,0:T(8,128)(2,1)S(1)} %collective-permute-done.7.other_near_ref, ...), custom_call_target="tpu_custom_call" | custom-call | tf_op jit(solution)/shard_map/turned/pallas_call | solution.py:848
  25.4 0.3 collective-permute-done.3.far_ref
  25.8 0.0 collective-permute-done.9.other_far_normed_ref
  25.8 2.4 %transition.1 = (bf16[64,128]{1,0:T(8,128)(2,1)}, bf16[512,128]{1,0:T(8,128)(2,1)S(1)}, bf16[512,128]{1,0:T(8,128)(2,1)S(1)}, bf16[512,512]{1,0:T(8,128)(2,1)S(1...) custom-call(s32[2]{0:T(128)S(1)} %pad_add_fusion.ids_ref, bf16[4,128,128]{2,1,0:T(8,128)(2,1)S(1)} %slice.16.near_ref, ...), custom_call_target="tpu_custom_call" | custom-call | tf_op jit(solution)/shard_map/transition/pallas_call | solution.py:866
  28.2 0.8 %out_weight.1.refs_0_ = bf16[1024,128]{1,0:T(8,128)(2,1)S(1)} custom-call(bf16[512,1024]{1,0:T(8,128)(2,1)S(1)} %get-tuple-element.72.outer_ref, bf16[512,128]{1,0:T(8,128)(2,1)S(1)} %get-tuple-element.71.opm_ref), custom_call_target="tpu_custom_call" | custom-call | tf_op jit(solution)/shard_map/out_weight/pallas_call | solution.py:895
  29.0 0.4 transition_weights.1
  29.4 0.2 collective-permute-done.10.other_opm_ref
  29.5 0.4 collective-permute-start.14
  30.0 0.1 collective-permute-start.15
  30.1 0.4 collective-permute-start.16
  30.5 2.0 %projector_parts.1 = (bf16[64,256]{1,0:T(8,128)(2,1)S(1)}, bf16[256,256]{1,0:T(8,128)(2,1)S(1)}) custom-call(s32[2]{0:T(128)S(1)} %pad_add_fusion.ids_ref, bf16[512,128]{1,0:T(8,128)(2,1)S(1)} %get-tuple-element.71.opm_ref, bf16[512,128]{1,0:T(8,128)(2,1)S(1)} %collective-permute-done.10.other_opm_ref, bf16[1024,128]{1,0:T(8,128)(2,1)S(1)} %get-tuple-element.80.rightt_ref, ...), custom_call_target="tpu_custom_call" | custom-call | tf_op jit(solution)/shard_map/projector_parts/pallas_call | solution.py:914
  32.5 3.8 %collective-permute-start.13 = (bf16[64,256]{1,0:T(8,128)(2,1)S(1)}, bf16[64,256]{1,0:T(8,128)(2,1)S(1)}, u32[]{:S(2)}, u32[]{:S(2)}) collective-permute-start(bf16[64,256]{1,0:T(8,128)(2,1)S(1)} %get-tuple-element.86), channel_id=1, source_target_pairs={{0,6},{1,7},{2,4},{3,5},{4,2},{5,3},{6,0},{7,1},{8,14},{9,15},{10,... | collective-permute-start | bytes 98312 | tf_op jit(solution)/shard_map/ppermute | solution.py:730
  36.3 0.0 collective-permute-start.12
  36.3 0.0 collective-permute-done.15.refs_4_
  36.3 0.6 %collective-permute-start.11 = (bf16[64,256]{1,0:T(8,128)(2,1)S(1)}, bf16[64,256]{1,0:T(8,128)(2,1)S(1)}, u32[]{:S(2)}, u32[]{:S(2)}) collective-permute-start(bf16[64,256]{1,0:T(8,128)(2,1)S(1)} %get-tuple-element.86), channel_id=1, source_target_pairs={{0,2},{1,3},{2,0},{3,1},{4,6},{5,7},{6,4},{7,5},{8,10},{9,11},{10,... | collective-permute-start | bytes 98312 | tf_op jit(solution)/shard_map/ppermute | solution.py:730
  37.0 0.3 features.1
  37.3 0.0 collective-permute-done.16.refs_5_
  37.3 0.0 collective-permute-done.14.refs_3_
  37.3 1.0 %sums_over_depth.1 = (f32[1024,128]{1,0:T(8,128)}, f32[128,512]{1,0:T(8,128)}, f32[512,128]{1,0:T(8,128)}) custom-call(bf16[1024,128]{1,0:T(8,128)(2,1)S(1)} %out_weight.1.refs_0_, bf16[128,512]{1,0:T(8,128)(2,1)S(1)} %get-tuple-element.94.refs_1_, bf16[512,128]{1,0:T(8,128)(2,1)S(1)} %get-tuple-element.95.refs_2_, ...), custom_call_target="tpu_custom_call" | custom-call | tf_op jit(solution)/shard_map/sums_over_depth/pallas_call | solution.py:955
  38.3 0.1 collective-permute-done.13
  38.4 2.7 %collective-permute-done.12 = bf16[64,256]{1,0:T(8,128)(2,1)S(1)} collective-permute-done((bf16[64,256]{1,0:T(8,128)(2,1)S(1)}, bf16[64,256]{1,0:T(8,128)(2,1)S(1)}, u32[]{:S(2)}, u32[]{:S(2)}) %collective-permute-start.12) | collective-permute-done | bytes 32800 | tf_op jit(solution)/shard_map/ppermute | solution.py:730
  41.2 0.0 collective-permute-done.11
  41.2 0.7 %reshape.44 = bf16[64,4,256]{2,1,0:T(4,128)(2,1)} reshape(bf16[256,256]{1,0:T(8,128)(2,1)S(1)} %features.1) | data formatting | bytes 262144 | tf_op jit(solution)/shard_map/reshape | solution.py:971
  41.9 0.6 %slice_bitcast_fusion = (f32[256,32]{0,1:T(8,128)}, f32[256,32]{0,1:T(8,128)}) fusion(f32[64,256]{1,0:T(8,128)S(1)} %add_add_fusion), kind=kLoop, calls=%fused_computation.2 | loop fusion | bytes 131072 | tf_op jit(solution)/shard_map/transpose | solution.py:974
  (9 shorter events, 0.1 us)
Async XLA Ops:
  2.6 7.8 %collective-permute-start.2 = (bf16[1,272,128]{2,1,0:T(8,128)(2,1)S(1)}, bf16[1,272,128]{2,1,0:T(8,128)(2,1)S(1)}, u32[]{:S(2)}, u32[]{:S(2)}) collective-permute-start(bf16[1,272,128]{2,1,0:T(8,128)(2,1)S(1)} %get-tuple-element.57), channel_id=1, source_target_pairs={{0,6},{1,7},{2,4},{3,5},{4,2},{5,3},{6,0},{7,1},{8,14},{9,15},{10,... | collective-permute-start | bytes 208904 | tf_op jit(solution)/shard_map/ppermute | solution.py:730
  7.7 5.9 %collective-permute-start.1 = (bf16[1,272,128]{2,1,0:T(8,128)(2,1)S(1)}, bf16[1,272,128]{2,1,0:T(8,128)(2,1)S(1)}, u32[]{:S(2)}, u32[]{:S(2)}) collective-permute-start(bf16[1,272,128]{2,1,0:T(8,128)(2,1)S(1)} %get-tuple-element.57), channel_id=1, source_target_pairs={{0,4},{1,5},{2,6},{3,7},{4,0},{5,1},{6,2},{7,3},{8,12},{9,13},{10,... | collective-permute-start | bytes 208904 | tf_op jit(solution)/shard_map/ppermute | solution.py:730
  7.8 5.9 %collective-permute-start = (bf16[1,272,128]{2,1,0:T(8,128)(2,1)S(1)}, bf16[1,272,128]{2,1,0:T(8,128)(2,1)S(1)}, u32[]{:S(2)}, u32[]{:S(2)}) collective-permute-start(bf16[1,272,128]{2,1,0:T(8,128)(2,1)S(1)} %get-tuple-element.57), channel_id=1, source_target_pairs={{0,2},{1,3},{2,0},{3,1},{4,6},{5,7},{6,4},{7,5},{8,10},{9,11},{10,... | collective-permute-start | bytes 208904 | tf_op jit(solution)/shard_map/ppermute | solution.py:730
  8.4 5.3 %collective-permute-start.5 = (bf16[256,256]{1,0:T(8,128)(2,1)S(1)}, bf16[256,256]{1,0:T(8,128)(2,1)S(1)}, u32[]{:S(2)}, u32[]{:S(2)}) collective-permute-start(bf16[256,256]{1,0:T(8,128)(2,1)S(1)} %get-tuple-element.58.normed_ref), channel_id=1, source_target_pairs={{0,8},{8,0},{1,9},{9,1},{2,10},{10,2},{3,11},{11,3},{4,12},{12,4},... | collective-permute-start | bytes 393224 | tf_op jit(solution)/shard_map/ppermute | solution.py:719
  8.4 5.9 %collective-permute-start.4 = (bf16[256,256]{1,0:T(8,128)(2,1)S(1)}, bf16[256,256]{1,0:T(8,128)(2,1)S(1)}, u32[]{:S(2)}, u32[]{:S(2)}) collective-permute-start(bf16[256,256]{1,0:T(8,128)(2,1)S(1)} %get-tuple-element.58.normed_ref), channel_id=1, source_target_pairs={{0,1},{1,0},{2,3},{3,2},{4,5},{5,4},{6,7},{7,6},{8,9},{9,8},{10,11... | collective-permute-start | bytes 393224 | tf_op jit(solution)/shard_map/ppermute | solution.py:730
  13.7 8.1 %copy-start = (bf16[1024,128]{1,0:T(8,128)(2,1)S(1)}, bf16[1024,128]{1,0:T(8,128)(2,1)}, u32[]{:S(2)}) copy-start(bf16[1024,128]{1,0:T(8,128)(2,1)} %wout_ref.1) | copy-start | bytes 786436
  14.3 5.5 %collective-permute-start.6 = (bf16[4,144,128]{2,1,0:T(8,128)(2,1)S(1)}, bf16[4,144,128]{2,1,0:T(8,128)(2,1)S(1)}, u32[]{:S(2)}, u32[]{:S(2)}) collective-permute-start(bf16[4,144,128]{2,1,0:T(8,128)(2,1)S(1)} %slice.17.near_ref), channel_id=1, source_target_pairs={{0,1},{1,0},{2,3},{3,2},{4,5},{5,4},{6,7},{7,6},{8,9},{9,8},{10,11... | collective-permute-start | bytes 442376 | tf_op jit(solution)/shard_map/ppermute | solution.py:730
  16.0 5.9 %collective-permute-start.7 = (bf16[4,144,128]{2,1,0:T(8,128)(2,1)S(1)}, bf16[4,144,128]{2,1,0:T(8,128)(2,1)S(1)}, u32[]{:S(2)}, u32[]{:S(2)}) collective-permute-start(bf16[4,144,128]{2,1,0:T(8,128)(2,1)S(1)} %slice.17.near_ref), channel_id=1, source_target_pairs={{0,8},{8,0},{1,9},{9,1},{2,10},{10,2},{3,11},{11,3},{4,12},{12,4},... | collective-permute-start | bytes 442376 | tf_op jit(solution)/shard_map/ppermute | solution.py:719
  19.8 2.1 %collective-permute-start.8 = (bf16[4,144,128]{2,1,0:T(8,128)(2,1)S(1)}, bf16[4,144,128]{2,1,0:T(8,128)(2,1)S(1)}, u32[]{:S(2)}, u32[]{:S(2)}) collective-permute-start(bf16[4,144,128]{2,1,0:T(8,128)(2,1)S(1)} %collective-permute-done.6.far_ref), channel_id=1, source_target_pairs={{0,8},{8,0},{1,9},{9,1},{2,10},{10,2},{3,11},{11,3},{4,12},{12,4},... | collective-permute-start | bytes 442376 | tf_op jit(solution)/shard_map/ppermute | solution.py:719
  19.8 6.0 %collective-permute-start.3 = (bf16[4,128,128]{2,1,0:T(8,128)(2,1)S(1)}, bf16[4,128,128]{2,1,0:T(8,128)(2,1)S(1)}, u32[]{:S(2)}, u32[]{:S(2)}) collective-permute-start(bf16[4,128,128]{2,1,0:T(8,128)(2,1)S(1)} %slice.16.near_ref), channel_id=1, source_target_pairs={{0,1},{1,0},{2,3},{3,2},{4,5},{5,4},{6,7},{7,6},{8,9},{9,8},{10,11... | collective-permute-start | bytes 393224 | tf_op jit(solution)/shard_map/ppermute | solution.py:730
  21.5 4.2 %collective-permute-start.9 = (bf16[256,256]{1,0:T(8,128)(2,1)S(1)}, bf16[256,256]{1,0:T(8,128)(2,1)S(1)}, u32[]{:S(2)}, u32[]{:S(2)}) collective-permute-start(bf16[256,256]{1,0:T(8,128)(2,1)S(1)} %collective-permute-done.4.far_normed_ref), channel_id=1, source_target_pairs={{0,8},{8,0},{1,9},{9,1},{2,10},{10,2},{3,11},{11,3},{4,12},{12,4},... | collective-permute-start | bytes 393224 | tf_op jit(solution)/shard_map/ppermute | solution.py:719
  24.0 1.8 %copy-start.1 = (bf16[128,512]{1,0:T(8,128)(2,1)S(1)}, bf16[128,512]{1,0:T(8,128)(2,1)}, u32[]{:S(2)}) copy-start(bf16[128,512]{1,0:T(8,128)(2,1)} %hid_ref.1) | copy-start | bytes 393220
  24.0 1.7 %copy-start.2 = (bf16[512,128]{1,0:T(8,128)(2,1)S(1)}, bf16[512,128]{1,0:T(8,128)(2,1)}, u32[]{:S(2)}) copy-start(bf16[512,128]{1,0:T(8,128)(2,1)} %back_ref.1) | copy-start | bytes 393220
  28.2 1.3 %collective-permute-start.10 = (bf16[512,128]{1,0:T(8,128)(2,1)S(1)}, bf16[512,128]{1,0:T(8,128)(2,1)S(1)}, u32[]{:S(2)}, u32[]{:S(2)}) collective-permute-start(bf16[512,128]{1,0:T(8,128)(2,1)S(1)} %get-tuple-element.71.opm_ref), channel_id=1, source_target_pairs={{0,8},{8,0},{1,9},{9,1},{2,10},{10,2},{3,11},{11,3},{4,12},{12,4},... | collective-permute-start | bytes 393224 | tf_op jit(solution)/shard_map/ppermute | solution.py:719
  29.5 7.8 %collective-permute-start.14 = (bf16[1024,128]{1,0:T(8,128)(2,1)S(1)}, bf16[1024,128]{1,0:T(8,128)(2,1)S(1)}, u32[]{:S(2)}, u32[]{:S(2)}) collective-permute-start(bf16[1024,128]{1,0:T(8,128)(2,1)S(1)} %out_weight.1.refs_0_), channel_id=1, source_target_pairs={{0,8},{8,0},{1,9},{9,1},{2,10},{10,2},{3,11},{11,3},{4,12},{12,4},... | collective-permute-start | bytes 786440 | tf_op jit(solution)/shard_map/ppermute | solution.py:719
  30.0 6.4 %collective-permute-start.15 = (bf16[128,512]{1,0:T(8,128)(2,1)S(1)}, bf16[128,512]{1,0:T(8,128)(2,1)S(1)}, u32[]{:S(2)}, u32[]{:S(2)}) collective-permute-start(bf16[128,512]{1,0:T(8,128)(2,1)S(1)} %get-tuple-element.94.refs_1_), channel_id=1, source_target_pairs={{0,8},{8,0},{1,9},{9,1},{2,10},{10,2},{3,11},{11,3},{4,12},{12,4},... | collective-permute-start | bytes 393224 | tf_op jit(solution)/shard_map/ppermute | solution.py:719
  30.1 7.2 %collective-permute-start.16 = (bf16[512,128]{1,0:T(8,128)(2,1)S(1)}, bf16[512,128]{1,0:T(8,128)(2,1)S(1)}, u32[]{:S(2)}, u32[]{:S(2)}) collective-permute-start(bf16[512,128]{1,0:T(8,128)(2,1)S(1)} %get-tuple-element.95.refs_2_), channel_id=1, source_target_pairs={{0,8},{8,0},{1,9},{9,1},{2,10},{10,2},{3,11},{11,3},{4,12},{12,4},... | collective-permute-start | bytes 393224 | tf_op jit(solution)/shard_map/ppermute | solution.py:719
  32.5 5.9 %collective-permute-start.13 = (bf16[64,256]{1,0:T(8,128)(2,1)S(1)}, bf16[64,256]{1,0:T(8,128)(2,1)S(1)}, u32[]{:S(2)}, u32[]{:S(2)}) collective-permute-start(bf16[64,256]{1,0:T(8,128)(2,1)S(1)} %get-tuple-element.86), channel_id=1, source_target_pairs={{0,6},{1,7},{2,4},{3,5},{4,2},{5,3},{6,0},{7,1},{8,14},{9,15},{10,... | collective-permute-start | bytes 98312 | tf_op jit(solution)/shard_map/ppermute | solution.py:730
  36.3 4.8 %collective-permute-start.12 = (bf16[64,256]{1,0:T(8,128)(2,1)S(1)}, bf16[64,256]{1,0:T(8,128)(2,1)S(1)}, u32[]{:S(2)}, u32[]{:S(2)}) collective-permute-start(bf16[64,256]{1,0:T(8,128)(2,1)S(1)} %get-tuple-element.86), channel_id=1, source_target_pairs={{0,4},{1,5},{2,6},{3,7},{4,0},{5,1},{6,2},{7,3},{8,12},{9,13},{10,... | collective-permute-start | bytes 98312 | tf_op jit(solution)/shard_map/ppermute | solution.py:730
  36.3 4.8 %collective-permute-start.11 = (bf16[64,256]{1,0:T(8,128)(2,1)S(1)}, bf16[64,256]{1,0:T(8,128)(2,1)S(1)}, u32[]{:S(2)}, u32[]{:S(2)}) collective-permute-start(bf16[64,256]{1,0:T(8,128)(2,1)S(1)} %get-tuple-element.86), channel_id=1, source_target_pairs={{0,2},{1,3},{2,0},{3,1},{4,6},{5,7},{6,4},{7,5},{8,10},{9,11},{10,... | collective-permute-start | bytes 98312 | tf_op jit(solution)/shard_map/ppermute | solution.py:730

commit v5 on v4

--- a/solution.py
+++ b/solution.py
@@ -363,17 +363,33 @@
             both = jnp.where(
                 lane_group == r, wide_ref[at, pl.ds(r, seqs, stride=res), :], both
             )
-        sent_ref[0, at * seqs : (at + 1) * seqs, :] = (both * mask_lanes).astype(jnp.bfloat16)
-    sent_ref[0, 2 * seqs : first_pair, :] = tile_ref[...].astype(jnp.bfloat16)
+        first = (seqs + MASK_ROWS, 0)[at]
+        sent_ref[0, first : first + seqs, :] = (both * mask_lanes).astype(jnp.bfloat16)
+    sent_ref[0, seqs : seqs + MASK_ROWS, :] = tile_ref[...].astype(jnp.bfloat16)
+
+
+def place_projections(ids_ref, blocks, right_ref, left_ref, seqs):
+    near_ref, other_near_ref, far_ref, other_far_ref = blocks
+    me_depth = ids_ref[0]
+    me_z, me_y = ids_ref[1] // 2, ids_ref[1] % 2
+    rights = seqs + MASK_ROWS
+    for at in range(near_ref.shape[0]):
+        z = me_z ^ at
+        right_ref[me_depth, 2 * z + me_y] = near_ref[at, 0:rights, :]
+        right_ref[1 - me_depth, 2 * z + me_y] = other_near_ref[at, 0:rights, :]
+        right_ref[me_depth, 2 * z + 1 - me_y] = far_ref[at]
+        right_ref[1 - me_depth, 2 * z + 1 - me_y] = other_far_ref[at]
+        if left_ref is not None:
+            left_ref[me_depth, z] = near_ref[at, rights : rights + seqs, :]
+            left_ref[1 - me_depth, z] = other_near_ref[at, rights : rights + seqs, :]
 
 
 def outer_kernel(
     sizes,
-    orders,
     ids_ref,
     near_ref,
+    other_near_ref,
     far_ref,
-    other_near_ref,
     other_far_ref,
     wturn_ref,
     outer_ref,
@@ -381,7 +397,8 @@
     cnt_ref,
     pm_ref,
     maskt_ref,
-    got_ref,
+    right_ref,
+    left_ref,
     leftn_ref,
     mine_ref,
     turn_ref,
@@ -389,31 +406,22 @@
     pml_ref,
 ):
     seqs, res, pair_cols, width = sizes
-    depths, cols = got_ref.shape[0], got_ref.shape[1]
-    residues = cols * res
+    depths, cols = right_ref.shape[0], right_ref.shape[1]
+    line = left_ref.shape[1]
     lanes = res * width
     half_cols = pair_cols // res
     me_depth = ids_ref[0]
-    me_col = ids_ref[1]
+    me_z, me_y = ids_ref[1] // 2, ids_ref[1] % 2
     f32, bf16 = jnp.float32, jnp.bfloat16
-
-    for order, mine, other in zip(orders, (near_ref, far_ref), (other_near_ref, other_far_ref)):
-        for at, partner in enumerate(order):
-            got_ref[me_depth, me_col ^ partner] = mine[at]
-            got_ref[1 - me_depth, me_col ^ partner] = other[at]
-
+    place_projections(
+        ids_ref, (near_ref, other_near_ref, far_ref, other_far_ref), right_ref, left_ref, seqs
+    )
     for e in range(depths):
-        for k in range(cols):
-            leftn_ref[e * seqs : (e + 1) * seqs, k * lanes : (k + 1) * lanes] = got_ref[
-                e, k, 0:seqs, :
-            ]
+        for z in range(line):
+            leftn_ref[e * seqs : (e + 1) * seqs, z * lanes : (z + 1) * lanes] = left_ref[e, z]
     for k in range(half_cols):
         block = jnp.concatenate(
-            [
-                got_ref[e, me_depth * half_cols + k, seqs : 2 * seqs, :]
-                for e in range(depths)
-            ],
-            axis=0,
+            [right_ref[e, me_depth * half_cols + k, 0:seqs, :] for e in range(depths)], axis=0
         ).astype(f32)
         turn_ref[k * lanes : (k + 1) * lanes, :] = block.T
     for d in range(width):
@@ -421,89 +429,77 @@
             pl.ds(d, pair_cols, stride=width), :
         ].astype(bf16)
 
-    base = 2 * seqs
+    for k in range(cols):
+        tiles = [
+            right_ref[e, k, seqs : seqs + MASK_ROWS, :].astype(f32) for e in range(depths)
+        ]
+        maskt_ref[k * res : (k + 1) * res, :] = tiles[0][0:res] + tiles[1][0:res]
     pair_lane = lax.broadcasted_iota(jnp.int32, (pair_cols, lanes), 1)
     pair_row = lax.broadcasted_iota(jnp.int32, (pair_cols, lanes), 0)
-    for k in range(cols):
-        tiles = [got_ref[e, k, base : base + MASK_ROWS, :].astype(f32) for e in range(depths)]
-        maskt_ref[k * res : (k + 1) * res, :] = tiles[0][0:res] + tiles[1][0:res]
-        own = got_ref[me_depth, k, base : base + MASK_ROWS, :].astype(f32)
+    cols_mask = maskt_ref[pl.ds(pl.multiple_of(me_depth * pair_cols, pair_cols), pair_cols), :]
+    for z in range(line):
+        tile = right_ref[me_depth, 2 * z + me_y, seqs : seqs + MASK_ROWS, :].astype(f32)
+        other = right_ref[1 - me_depth, 2 * z + me_y, seqs : seqs + MASK_ROWS, :].astype(f32)
         for r in range(res):
-            row = own[res + r : res + r + 1, :]
-            first = (k * res + r) * pair_cols
+            first = (z * res + r) * pair_cols
             pml_ref[first : first + pair_cols, :] = jnp.where(
-                pair_lane == pair_row, row, 0.0
+                pair_lane == pair_row, tile[res + r : res + r + 1, :], 0.0
             ).astype(bf16)
-    maskt = maskt_ref[...]
-    cols_mask = maskt_ref[pl.ds(pl.multiple_of(me_depth * pair_cols, pair_cols), pair_cols), :]
-    for i in range(residues):
-        cntl_ref[i * pair_cols : (i + 1) * pair_cols, :] = (maskt[i : i + 1, :] * cols_mask).astype(
-            bf16
-        )
+            cntl_ref[first : first + pair_cols, :] = (
+                (tile[r : r + 1, :] + other[r : r + 1, :]) * cols_mask
+            ).astype(bf16)
     ones = jnp.ones((lanes, lanes), bf16)
     cnt_ref[...] = jnp.dot(cntl_ref[...], ones, preferred_element_type=f32)
     pm_ref[...] = jnp.dot(pml_ref[...], ones, preferred_element_type=f32).astype(bf16)
 
-    for dh in range(width // 4):
+    for z2 in range(line // 2):
         prod = jnp.dot(
-            mine_ref[dh * 4 * pair_cols : (dh + 1) * 4 * pair_cols, :],
-            leftn_ref[...],
+            mine_ref[...],
+            leftn_ref[:, 2 * z2 * lanes : 2 * (z2 + 1) * lanes],
             preferred_element_type=f32,
         )
-        for k in range(cols):
-            piece = prod[:, k * lanes : (k + 1) * lanes]
-            turned = butterfly(
-                [piece[a * pair_cols : (a + 1) * pair_cols] for a in range(4)], width
-            )
-            for il in range(res):
-                first = (k * res + il) * pair_cols
-                outer_ref[first : first + pair_cols, dh * lanes : (dh + 1) * lanes] = turned[
-                    il
-                ].astype(bf16)
+        for dh in range(width // 4):
+            for b in range(2):
+                piece = prod[
+                    dh * 4 * pair_cols : (dh + 1) * 4 * pair_cols, b * lanes : (b + 1) * lanes
+                ]
+                turned = butterfly(
+                    [piece[a * pair_cols : (a + 1) * pair_cols] for a in range(4)], width
+                )
+                for il in range(res):
+                    first = ((2 * z2 + b) * res + il) * pair_cols
+                    outer_ref[first : first + pair_cols, dh * lanes : (dh + 1) * lanes] = turned[
+                        il
+                    ].astype(bf16)
     proj_out_ref[...] = jnp.dot(outer_ref[...], wturn_ref[...], preferred_element_type=f32)
 
 
-def turn_kernel(
+def turn_kernel(sizes, firsts, ids_ref, mine_ref, other_ref, *refs):
+    seqs, res, _, width = sizes
+    outs, got_ref, turn_ref = refs[:-2], refs[-2], refs[-1]
+    line = mine_ref.shape[0]
+    lanes = res * width
+    me_depth = ids_ref[0]
+    me_z = ids_ref[1] // 2
+    for first, out in zip(firsts, outs):
+        for at in range(line):
+            got_ref[me_depth, me_z ^ at] = mine_ref[at, first : first + seqs, :]
+            got_ref[1 - me_depth, me_z ^ at] = other_ref[at, first : first + seqs, :]
+        for z in range(line):
+            block = jnp.concatenate(
+                [got_ref[e, z] for e in range(got_ref.shape[0])], axis=0
+            ).astype(jnp.float32)
+            turn_ref[z * lanes : (z + 1) * lanes, :] = block.T
+        for d in range(width):
+            out[d * line * res : (d + 1) * line * res, :] = turn_ref[
+                pl.ds(d, line * res, stride=width), :
+            ].astype(jnp.bfloat16)
+
+
+def transition_kernel(
     sizes,
-    orders,
     ids_ref,
     near_ref,
-    far_ref,
-    other_near_ref,
-    other_far_ref,
-    rightt_ref,
-    leftt_ref,
-    got_ref,
-    turn_ref,
-):
-    seqs, res, _, width = sizes
-    depths, cols = got_ref.shape[0], got_ref.shape[1]
-    lanes = res * width
-    residues = res * cols
-    me_depth = ids_ref[0]
-    me_col = ids_ref[1]
-    for order, mine, other in zip(orders, (near_ref, far_ref), (other_near_ref, other_far_ref)):
-        for at, partner in enumerate(order):
-            got_ref[me_depth, me_col ^ partner] = mine[at, 0 : 2 * seqs, :]
-            got_ref[1 - me_depth, me_col ^ partner] = other[at, 0 : 2 * seqs, :]
-    for at, out in ((0, leftt_ref), (1, rightt_ref)):
-        for k in range(cols):
-            block = jnp.concatenate(
-                [got_ref[e, k, at * seqs : (at + 1) * seqs, :] for e in range(depths)], axis=0
-            ).astype(jnp.float32)
-            turn_ref[k * lanes : (k + 1) * lanes, :] = block.T
-        for d in range(width):
-            out[d * residues : (d + 1) * residues, :] = turn_ref[
-                pl.ds(d, residues, stride=width), :
-            ].astype(jnp.bfloat16)
-
-
-def transition_kernel(
-    sizes,
-    orders,
-    ids_ref,
-    near_ref,
-    far_ref,
     proj_out_ref,
     cnt_ref,
     pm_ref,
@@ -516,52 +512,90 @@
     gh_ref,
     hidden_ref,
     mg_ref,
-    pgot_ref,
+    pairs_ref,
     gmid_ref,
 ):
     seqs, res, pair_cols, width = sizes
     per = res * pair_cols
-    cols = pgot_ref.shape[0]
-    me_col = ids_ref[1]
+    line = pairs_ref.shape[0]
+    me_z = ids_ref[1] // 2
+    first_pair = 2 * seqs + MASK_ROWS
     f32, bf16 = jnp.float32, jnp.bfloat16
-    for order, mine in zip(orders, (near_ref, far_ref)):
-        for at, partner in enumerate(order):
-            pgot_ref[me_col ^ partner] = mine[at]
+    for at in range(line):
+        pairs_ref[me_z ^ at] = near_ref[at, first_pair:, :]
     gain = gain_ref[...]
-    chunk = 2 * per
-    for at in range(cols // 2):
-        rows = slice(at * chunk, (at + 1) * chunk)
-        act, grad = [
-            jnp.concatenate(
-                [pgot_ref[2 * at + b, w * per : (w + 1) * per, :] for b in range(2)], axis=0
-            )
-            for w in range(2)
+    act, grad = [
+        jnp.concatenate([pairs_ref[z, w * per : (w + 1) * per, :] for z in range(line)], axis=0)
+        for w in range(2)
+    ]
+    count = cnt_ref[...]
+    mid = act.astype(f32) + proj_out_ref[...] / count
+    scaled, inv = norm_pieces(mid)
+    normed = (scaled * gain).astype(bf16)
+    pn_ref[...] = normed
+    pre = jnp.dot(normed, hid_ref[...], preferred_element_type=f32)
+    value, slope = silu_pieces(pre)
+    hidden_ref[...] = value.astype(bf16)
+    masked = grad * pm_ref[...]
+    mg_ref[...] = masked
+    back = lax.dot_general(
+        masked, back_ref[...], (((1,), (1,)), ((), ())), preferred_element_type=f32
+    )
+    ghid = (back * slope).astype(bf16)
+    gh_ref[...] = ghid
+    gsc = (
+        lax.dot_general(ghid, hid_ref[...], (((1,), (1,)), ((), ())), preferred_element_type=f32)
+        * gain
+    )
+    gmid = grad.astype(f32) + standardize_adjoint(gsc, scaled, inv)
+    gmid_ref[...] = gmid
+    opm_ref[...] = (gmid / count).astype(bf16)
+    couple_ref[...] = gmid_ref[pl.ds(pl.multiple_of(me_z * per, per), per), :].astype(bf16)
+
+
+def weights_kernel(
+    ids_ref, outer_ref, opm_ref, pn_ref, gh_ref, hidden_ref, mg_ref, keep_ref, give_ref, turn_ref, both_ref
+):
+    pair_width, hid = pn_ref.shape[1], gh_ref.shape[1]
+    outer_width = outer_ref.shape[1]
+    width = int(outer_width**0.5 + 0.5)
+
+    def contract(lhs, rhs):
+        return lax.dot_general(
+            lhs[...], rhs[...], (((0,), (0,)), ((), ())), preferred_element_type=jnp.float32
+        )
+
+    turn_ref[...] = contract(outer_ref, opm_ref)
+    for c in range(width):
+        both_ref[0, c * width : (c + 1) * width, :] = turn_ref[
+            pl.ds(c, width, stride=width), :
+        ].astype(jnp.bfloat16)
+    dhid = contract(pn_ref, gh_ref).astype(jnp.bfloat16)
+    for at in range(hid // pair_width):
+        both_ref[1, at * pair_width : (at + 1) * pair_width, :] = dhid[
+            :, at * pair_width : (at + 1) * pair_width
         ]
-        count = cnt_ref[rows, :]
-        mid = act.astype(f32) + proj_out_ref[rows, :] / count
-        scaled, inv = norm_pieces(mid)
-        normed = (scaled * gain).astype(bf16)
-        pn_ref[rows, :] = normed
-        pre = jnp.dot(normed, hid_ref[...], preferred_element_type=f32)
-        value, slope = silu_pieces(pre)
-        hidden_ref[rows, :] = value.astype(bf16)
-        masked = grad * pm_ref[rows, :]
-        mg_ref[rows, :] = masked
-        back = lax.dot_general(
-            masked, back_ref[...], (((1,), (1,)), ((), ())), preferred_element_type=f32
-        )
-        ghid = (back * slope).astype(bf16)
-        gh_ref[rows, :] = ghid
-        gsc = (
-            lax.dot_general(
-                ghid, hid_ref[...], (((1,), (1,)), ((), ())), preferred_element_type=f32
-            )
-            * gain
-        )
-        gmid = grad.astype(f32) + standardize_adjoint(gsc, scaled, inv)
-        gmid_ref[rows, :] = gmid
-        opm_ref[rows, :] = (gmid / count).astype(bf16)
-    couple_ref[...] = gmid_ref[pl.ds(pl.multiple_of(me_col * per, per), per), :].astype(bf16)
+    both_ref[1, hid:, :] = contract(hidden_ref, mg_ref).astype(jnp.bfloat16)
+    keep_ref[...] = both_ref[ids_ref[0]]
+    give_ref[...] = both_ref[1 - ids_ref[0]]
+
+
+def weights_out_kernel(ids_ref, mine_ref, other_ref, dout_ref, dhid_ref, dback_ref, both_ref):
+    pair_width, hid = dhid_ref.shape
+    both_ref[ids_ref[0]] = mine_ref[...]
+    both_ref[1 - ids_ref[0]] = other_ref[...]
+    dout_ref[...] = both_ref[0].astype(jnp.float32)
+    for at in range(hid // pair_width):
+        dhid_ref[:, at * pair_width : (at + 1) * pair_width] = both_ref[
+            1, at * pair_width : (at + 1) * pair_width, :
+        ].astype(jnp.float32)
+    dback_ref[...] = both_ref[1, hid:, :].astype(jnp.float32)
+
+
+def spread_rows(block, res, width, out_ref):
+    lane_group = lax.broadcasted_iota(jnp.int32, block.shape, 1) // width
+    for r in range(res):
+        out_ref[pl.ds(r, block.shape[0], stride=res), :] = jnp.where(lane_group == r, block, 0.0)
 
 
 def projector_kernel(
@@ -569,7 +603,8 @@
     ids_ref,
     opm_ref,
     other_opm_ref,
-    rightt_ref,
+    right_near_ref,
+    right_far_ref,
     leftt_ref,
     wout_ref,
     wturn_ref,
@@ -579,24 +614,28 @@
     other_normed_ref,
     other_far_normed_ref,
     part_ref,
-    spread_ref,
+    gleft_ref,
+    gright_ref,
+    gright_far_ref,
     gf_ref,
     grow_ref,
     gcol_ref,
-    gor_ref,
+    gon_ref,
+    gof_ref,
     goc_ref,
-    gs_ref,
+    gl_ref,
+    gr_ref,
     rows_ref,
+    tot_ref,
 ):
     seqs, res, pair_cols, width = sizes
     depths, half = gf_ref.shape[0], gf_ref.shape[1]
-    residues = half // pair_cols
+    rows_here = half // pair_cols
+    residues = depths * pair_cols
     lanes = res * width
     here = 2 * res
     me_depth = ids_ref[0]
-    me_col = ids_ref[1]
-    me_y = me_col % 2
-    first_here = (me_col // 2) * here
+    me_z, me_y = ids_ref[1] // 2, ids_ref[1] % 2
     f32, bf16 = jnp.float32, jnp.bfloat16
     gf_ref[me_depth] = opm_ref[...].astype(f32)
     gf_ref[1 - me_depth] = other_opm_ref[...].astype(f32)
@@ -608,68 +647,81 @@
     ):
         rows_ref[y, e] = block[...]
 
-    for il in range(here):
-        for e in range(depths):
-            first = pl.multiple_of((first_here + il) * pair_cols, pair_cols)
-            grow_ref[il * residues + e * pair_cols : il * residues + (e + 1) * pair_cols, :] = (
-                gf_ref[e, pl.ds(first, pair_cols), :].astype(bf16)
+    line = rows_here // res
+    for il in range(res):
+        for at, y in enumerate((me_y, 1 - me_y)):
+            for z in range(line):
+                e, z_low = divmod(z, line // depths)
+                first = (me_z * res + il) * pair_cols + z_low * here + y * res
+                to = il * residues + at * rows_here + z * res
+                grow_ref[to : to + res, :] = gf_ref[e, pl.ds(first, res), :]
+    my_half = (me_z * here) // pair_cols
+    my_first = me_z * here - my_half * pair_cols
+    for jl in range(here):
+        gcol_ref[jl * rows_here : (jl + 1) * rows_here, :] = gf_ref[
+            my_half, pl.ds(my_first + jl, rows_here, stride=pair_cols), :
+        ].astype(bf16)
+    for dh in range(width // 4):
+        piece = lax.dot_general(
+            grow_ref[...].astype(bf16),
+            wturn_ref[dh * lanes : (dh + 1) * lanes, :],
+            (((1,), (1,)), ((), ())),
+            preferred_element_type=f32,
+        )
+        turned = butterfly([piece[a * residues : (a + 1) * residues] for a in range(4)], width)
+        for dl in range(4):
+            rows = slice((dh * 4 + dl) * rows_here, (dh * 4 + dl + 1) * rows_here)
+            gon_ref[rows, :] = turned[dl][:rows_here].astype(bf16)
+            gof_ref[rows, :] = turned[dl][rows_here:].astype(bf16)
+        piece = lax.dot_general(
+            gcol_ref[...],
+            wout_ref[dh * lanes : (dh + 1) * lanes, :],
+            (((1,), (1,)), ((), ())),
+            preferred_element_type=f32,
+        )
+        for y in range(2):
+            turned = butterfly(
+                [
+                    piece[(y * res + a) * rows_here : (y * res + a + 1) * rows_here]
+                    for a in range(4)
+                ],
+                width,
             )
-    my_half = first_here // pair_cols
-    my_first = first_here - my_half * pair_cols
-    for jl in range(here):
-        gcol_ref[jl * residues : (jl + 1) * residues, :] = gf_ref[
-            my_half, pl.ds(my_first + jl, residues, stride=pair_cols), :
-        ].astype(bf16)
-    for lhs, weight, out in ((grow_ref, wturn_ref, gor_ref), (gcol_ref, wout_ref, goc_ref)):
-        for dh in range(width // 4):
-            piece = lax.dot_general(
-                lhs[...],
-                weight[dh * lanes : (dh + 1) * lanes, :],
-                (((1,), (1,)), ((), ())),
-                preferred_element_type=f32,
-            )
-            for y in range(2):
-                turned = butterfly(
-                    [
-                        piece[(y * res + a) * residues : (y * res + a + 1) * residues]
-                        for a in range(4)
-                    ],
-                    width,
-                )
-                for dl in range(4):
-                    first = (dh * 4 + dl) * residues
-                    out[first : first + residues, y * lanes : (y + 1) * lanes] = turned[dl].astype(
-                        bf16
-                    )
+            for dl in range(4):
+                rows = slice((dh * 4 + dl) * rows_here, (dh * 4 + dl + 1) * rows_here)
+                goc_ref[rows, y * lanes : (y + 1) * lanes] = turned[dl].astype(bf16)
     group = lax.broadcasted_iota(jnp.int32, (here, here * width), 1) // width
     spread = (group == lax.broadcasted_iota(jnp.int32, (here, here * width), 0)).astype(f32)
     mask_lanes = lax.dot_general(
-        maskt_ref[pl.ds(pl.multiple_of(first_here, here), here), :],
+        maskt_ref[pl.ds(pl.multiple_of(me_z * here, here), here), :],
         spread,
         (((0,), (0,)), ((), ())),
         preferred_element_type=f32,
     )
-    lane_group = lax.broadcasted_iota(jnp.int32, (seqs, lanes), 1) // width
-    for at, (lhs, rhs) in enumerate(((rightt_ref, gor_ref), (leftt_ref, goc_ref))):
-        total = lax.dot_general(
-            lhs[...], rhs[...], (((0,), (0,)), ((), ())), preferred_element_type=f32
-        )
-        total = (total * mask_lanes).astype(bf16).astype(f32)
+    mask_own = jnp.where(me_y == 0, mask_lanes[:, :lanes], mask_lanes[:, lanes:])
+    left_near, left_far, right = [
+        lax.dot_general(lhs[...], rhs[...], (((0,), (0,)), ((), ())), preferred_element_type=f32)
+        for lhs, rhs in ((right_near_ref, gon_ref), (right_far_ref, gof_ref), (leftt_ref, goc_ref))
+    ]
+    left = ((left_near + left_far) * mask_own).astype(bf16).astype(f32)
+    right = right * mask_lanes
+    for e in range(depths):
+        tot_ref[0, e] = left[e * seqs : (e + 1) * seqs]
+        spread_rows(left[e * seqs : (e + 1) * seqs], res, width, gl_ref.at[e])
         for y in range(2):
-            for e in range(depths):
-                block = total[e * seqs : (e + 1) * seqs, y * lanes : (y + 1) * lanes]
-                for r in range(res):
-                    gs_ref[at, y, e, pl.ds(r, seqs, stride=res), :] = jnp.where(
-                        lane_group == r, block, 0.0
-                    )
-    spread_ref[...] = jnp.concatenate(
-        [gs_ref[0, me_y, me_depth], gs_ref[1, me_y, me_depth]], axis=1
-    ).astype(bf16)
+            block = right[e * seqs : (e + 1) * seqs, y * lanes : (y + 1) * lanes]
+            tot_ref[1 + y, e] = block
+            spread_rows(block, res, width, gr_ref.at[y, e])
+    gleft_ref[...] = tot_ref[0, me_depth]
+    gright_ref[...] = tot_ref[1 + me_y, me_depth]
+    gright_far_ref[...] = tot_ref[2 - me_y, me_depth]
     rows = rows_ref.shape[2]
-    for at in range(2):
+    for at, (lhs, rhs, blocks) in enumerate(
+        ((gl_ref[...], rows_ref[me_y], depths), (gr_ref[...], rows_ref[...], 2 * depths))
+    ):
         cross = lax.dot_general(
-            gs_ref[at].reshape(2 * depths * rows, lanes).astype(bf16),
-            rows_ref[...].reshape(2 * depths * rows, rows_ref.shape[3]),
+            lhs.reshape(blocks * rows, lanes).astype(bf16),
+            rhs.reshape(blocks * rows, rows_ref.shape[3]),
             (((0,), (0,)), ((), ())),
             preferred_element_type=f32,
         )
@@ -679,35 +731,25 @@
         part_ref[at * width : (at + 1) * width, :] = total.astype(bf16)
 
 
-def out_weight_kernel(outer_ref, opm_ref, dout_ref, turn_ref):
-    width = int(dout_ref.shape[0] ** 0.5 + 0.5)
-    turn_ref[...] = lax.dot_general(
-        outer_ref[...], opm_ref[...], (((0,), (0,)), ((), ())), preferred_element_type=jnp.float32
-    )
-    for c in range(width):
-        dout_ref[c * width : (c + 1) * width, :] = turn_ref[
-            pl.ds(c, width, stride=width), :
-        ].astype(jnp.bfloat16)
-
-
-def transition_weight_kernel(pn_ref, gh_ref, hidden_ref, mg_ref, dhid_ref, dback_ref):
-    for lhs, rhs, out in ((pn_ref, gh_ref, dhid_ref), (hidden_ref, mg_ref, dback_ref)):
-        out[...] = lax.dot_general(
-            lhs[...], rhs[...], (((0,), (0,)), ((), ())), preferred_element_type=jnp.float32
-        ).astype(jnp.bfloat16)
-
-
-def sum_kernel(*refs):
-    for mine, other, out in zip(refs[0:3], refs[3:6], refs[6:9]):
-        out[...] = mine[...].astype(jnp.float32) + other[...].astype(jnp.float32)
-
-
 def feature_kernel(
-    copies, spread_ref, first_ref, second_ref, scale_ref, scaled_ref, inv_ref, feat_ref
+    sizes,
+    gleft_ref,
+    gright_ref,
+    gright_came_ref,
+    first_ref,
+    second_ref,
+    scale_ref,
+    scaled_ref,
+    inv_ref,
+    feat_ref,
+    gs_ref,
 ):
+    res, width = sizes[1], sizes[3]
+    spread_rows(gleft_ref[...], res, width, gs_ref.at[0])
+    spread_rows(gright_ref[...] + gright_came_ref[...], res, width, gs_ref.at[1])
     back = jnp.dot(
-        spread_ref[...],
-        wide_projector(first_ref, second_ref, copies),
+        jnp.concatenate([gs_ref[0], gs_ref[1]], axis=1).astype(jnp.bfloat16),
+        wide_projector(first_ref, second_ref, res),
         preferred_element_type=jnp.float32,
     )
     feat_ref[...] = standardize_adjoint(
@@ -754,8 +796,10 @@
     hid = hidden_weight.shape[1]
     per = res * pair_cols
     lanes = res * width
-    rows = 2 * seqs + MASK_ROWS
-    half = residues * pair_cols
+    rights = seqs + MASK_ROWS
+    rows = rights + seqs
+    line = cols // 2
+    half = line * res * pair_cols
     f32, bf16 = jnp.float32, jnp.bfloat16
     ids = jnp.stack([lax.axis_index("depth"), lax.axis_index("col")]).astype(jnp.int32)
     smem = pl.BlockSpec(memory_space=pltpu.SMEM)
@@ -808,22 +852,36 @@
             )
         ],
     )
-    near_order = (0,) + Z_PARTNERS
-    far_order = tuple(at ^ Y_PARTNER for at in near_order)
-    blocks = lax.optimization_barrier(
+    near = lax.optimization_barrier(
         jnp.concatenate([sent] + [swap_col(sent, partner) for partner in Z_PARTNERS])
     )
-    near, pair_near = blocks[:, :rows], blocks[:, rows:]
     far_normed = swap_col(normed, Y_PARTNER)
     other_normed, other_far_normed = swap_depth(normed), swap_depth(far_normed)
     near, far_normed, other_normed = lax.optimization_barrier((near, far_normed, other_normed))
-    far = swap_col(near, Y_PARTNER)
-    pair_far = swap_col(pair_near, Y_PARTNER)
-    other_near, other_far = swap_depth(near), swap_depth(far)
     sizes = (seqs, res, pair_cols, width)
-    orders = (near_order, far_order)
+    far = swap_col(near[:, :rights], Y_PARTNER)
+    other_near = swap_depth(near[:, :rows])
+
+    def turned(firsts, mine, other):
+        return pl.pallas_call(
+            functools.partial(turn_kernel, sizes, firsts),
+            out_shape=(shape((line * res * width, depths * seqs), bf16),) * len(firsts),
+            in_specs=[smem] + [vmem] * 2,
+            out_specs=[vmem] * len(firsts),
+            scratch_shapes=[
+                pltpu.VMEM((depths, line, seqs, lanes), bf16),
+                pltpu.VMEM((line * res * width, depths * seqs), f32),
+            ],
+            compiler_params=params,
+            name="turned",
+        )(ids, mine, other)
+
+    right_near, leftt = turned((0, rights), near, other_near)
+    far, right_near, leftt = lax.optimization_barrier((far, right_near, leftt))
+    other_far = swap_depth(far)
+    other_far, other_far_normed = lax.optimization_barrier((other_far, other_far_normed))
     outer, proj_out, cnt, pm, maskt = pl.pallas_call(
-        functools.partial(outer_kernel, sizes, orders),
+        functools.partial(outer_kernel, sizes),
         out_shape=(
             shape((half, outer_width), bf16),
             shape((half, pair_width), f32),
@@ -834,8 +892,9 @@
         in_specs=[smem] + [vmem] * 5,
         out_specs=[vmem] * 5,
         scratch_shapes=[
-            pltpu.VMEM((depths, cols, rows, pair_width), bf16),
-            pltpu.VMEM((depths * seqs, residues * width), bf16),
+            pltpu.VMEM((depths, cols, rights, lanes), bf16),
+            pltpu.VMEM((depths, line, seqs, lanes), bf16),
+            pltpu.VMEM((depths * seqs, line * lanes), bf16),
             pltpu.VMEM((pair_cols * width, depths * seqs), bf16),
             pltpu.VMEM((pair_cols * width, depths * seqs), f32),
             pltpu.VMEM((half, lanes), bf16),
@@ -843,28 +902,9 @@
         ],
         compiler_params=params,
         name="outer_products",
-    )(ids, near, far, other_near, other_far, wturn)
-    other_near, other_far, proj_out = lax.optimization_barrier((other_near, other_far, proj_out))
-    rightt, leftt = pl.pallas_call(
-        functools.partial(turn_kernel, sizes, orders),
-        out_shape=(
-            shape((residues * width, depths * seqs), bf16),
-            shape((residues * width, depths * seqs), bf16),
-        ),
-        in_specs=[smem] + [vmem] * 4,
-        out_specs=[vmem] * 2,
-        scratch_shapes=[
-            pltpu.VMEM((depths, cols, 2 * seqs, pair_width), bf16),
-            pltpu.VMEM((residues * width, depths * seqs), f32),
-        ],
-        compiler_params=params,
-        name="turned",
-    )(ids, near, far, other_near, other_far)
-    pair_far, rightt, leftt, proj_out, other_far_normed = lax.optimization_barrier(
-        (pair_far, rightt, leftt, proj_out, other_far_normed)
-    )
+    )(ids, near, other_near, far, other_far, wturn)
     couple, opm, pn, gh, hidden, mg = pl.pallas_call(
-        functools.partial(transition_kernel, sizes, orders),
+        functools.partial(transition_kernel, sizes),
         out_shape=(
             shape((per, pair_width), bf16),
             shape((half, pair_width), bf16),
@@ -873,60 +913,53 @@
             shape((half, hid), bf16),
             shape((half, pair_width), bf16),
         ),
-        in_specs=[smem] + [vmem] * 8,
+        in_specs=[smem] + [vmem] * 7,
         out_specs=[vmem] * 6,
         scratch_shapes=[
-            pltpu.VMEM((cols, 2 * per, pair_width), bf16),
+            pltpu.VMEM((line, 2 * per, pair_width), bf16),
             pltpu.VMEM((half, pair_width), f32),
         ],
         compiler_params=params,
         name="transition",
-    )(
-        ids,
-        pair_near,
-        pair_far,
-        proj_out,
-        cnt,
-        pm,
-        gain,
-        hidden_weight,
-        back_weight,
-    )
-    dout = pl.pallas_call(
-        out_weight_kernel,
-        out_shape=shape((outer_width, pair_width), bf16),
-        in_specs=[vmem] * 2,
-        out_specs=vmem,
-        scratch_shapes=[pltpu.VMEM((outer_width, pair_width), f32)],
+    )(ids, near, proj_out, cnt, pm, gain, hidden_weight, back_weight)
+    other_opm = swap_depth(opm)
+    other_far, opm = lax.optimization_barrier((other_far, opm))
+    (right_far,) = turned((0,), far, other_far)
+    weight_rows = outer_width
+    keep, give = pl.pallas_call(
+        weights_kernel,
+        out_shape=(shape((weight_rows, pair_width), bf16),) * 2,
+        in_specs=[smem] + [vmem] * 6,
+        out_specs=[vmem] * 2,
+        scratch_shapes=[
+            pltpu.VMEM((outer_width, pair_width), f32),
+            pltpu.VMEM((2, weight_rows, pair_width), bf16),
+        ],
         compiler_params=params,
-        name="out_weight",
-    )(outer, opm)
-    dhid, dback = pl.pallas_call(
-        transition_weight_kernel,
-        out_shape=(shape((pair_width, hid), bf16), shape((hid, pair_width), bf16)),
-        in_specs=[vmem] * 4,
-        out_specs=[vmem] * 2,
-        compiler_params=params,
-        name="transition_weights",
-    )(pn, gh, hidden, mg)
-    other_opm, dout, dhid, dback = lax.optimization_barrier((swap_depth(opm), dout, dhid, dback))
-    other_weights = [swap_depth(block) for block in (dout, dhid, dback)]
-    part, spread = pl.pallas_call(
+        name="weight_gradients",
+    )(ids, outer, opm, pn, gh, hidden, mg)
+    other_opm, right_far, keep, give = lax.optimization_barrier((other_opm, right_far, keep, give))
+    part, gleft, gright, gright_far = pl.pallas_call(
         functools.partial(projector_kernel, sizes),
         out_shape=(
             shape((2 * width, channels), bf16),
-            shape((seqs * res, 2 * lanes), bf16),
+            shape((seqs, lanes), f32),
+            shape((seqs, lanes), f32),
+            shape((seqs, lanes), f32),
         ),
-        in_specs=[smem] + [vmem] * 11,
-        out_specs=[vmem] * 2,
+        in_specs=[smem] + [vmem] * 12,
+        out_specs=[vmem] * 4,
         scratch_shapes=[
             pltpu.VMEM((depths, half, pair_width), f32),
-            pltpu.VMEM((2 * res * residues, pair_width), bf16),
-            pltpu.VMEM((2 * res * residues, pair_width), bf16),
-            pltpu.VMEM((residues * width, 2 * lanes), bf16),
-            pltpu.VMEM((residues * width, 2 * lanes), bf16),
-            pltpu.VMEM((2, 2, depths, seqs * res, lanes), f32),
+            pltpu.VMEM((res * residues, pair_width), f32),
+            pltpu.VMEM((2 * res * line * res, pair_width), bf16),
+            pltpu.VMEM((line * res * width, lanes), bf16),
+            pltpu.VMEM((line * res * width, lanes), bf16),
+            pltpu.VMEM((line * res * width, 2 * lanes), bf16),
+            pltpu.VMEM((depths, seqs * res, lanes), f32),
+            pltpu.VMEM((2, depths, seqs * res, lanes), f32),
             pltpu.VMEM((2, depths, seqs * res, channels), bf16),
+            pltpu.VMEM((3, depths, seqs, lanes), f32),
         ],
         compiler_params=params,
         name="projector_parts",
@@ -934,7 +967,8 @@
         ids,
         opm,
         other_opm,
-        rightt,
+        right_near,
+        right_far,
         leftt,
         output_weight,
         wturn,
@@ -944,29 +978,41 @@
         other_normed,
         other_far_normed,
     )
+
+    given, part = lax.optimization_barrier((swap_depth(give), part))
+
+    def rounded_sum(block, came):
+        return (block.astype(f32) + came.astype(f32)).astype(bf16)
+
+    came = [swap_col(part, partner) for partner in Z_PARTNERS]
+    came[2], gright_far = lax.optimization_barrier((came[2], gright_far))
+    weights = rounded_sum(keep, given)
+    weights = rounded_sum(weights, swap_col(weights, Y_PARTNER))
+    total = pairwise_sum([block.astype(f32) for block in [part] + came])
+    part = lax.optimization_barrier(total.astype(bf16))
+    total = part.astype(f32) + swap_col(part, Y_PARTNER).astype(f32)
     feat = pl.pallas_call(
-        functools.partial(feature_kernel, res),
+        functools.partial(feature_kernel, sizes),
         out_shape=shape((seqs * res, channels), bf16),
-        in_specs=[vmem] * 6,
+        in_specs=[vmem] * 8,
         out_specs=vmem,
+        scratch_shapes=[pltpu.VMEM((2, seqs * res, lanes), f32)],
         compiler_params=params,
         name="features",
-    )(spread, first, second, scale, scaled, inv)
+    )(gleft, gright, swap_col(gright_far, Y_PARTNER), first, second, scale, scaled, inv)
     dout, dhid, dback = pl.pallas_call(
-        sum_kernel,
+        weights_out_kernel,
         out_shape=(
             shape((outer_width, pair_width), f32),
             shape((pair_width, hid), f32),
             shape((hid, pair_width), f32),
         ),
-        in_specs=[vmem] * 6,
+        in_specs=[smem] + [vmem] * 2,
         out_specs=[vmem] * 3,
+        scratch_shapes=[pltpu.VMEM((2, weight_rows, pair_width), bf16)],
         compiler_params=params,
-        name="sums_over_depth",
-    )(dout, dhid, dback, *other_weights)
-    came = [swap_col(part, partner) for partner in Z_PARTNERS]
-    came, feat, dout, dhid, dback = lax.optimization_barrier((came, feat, dout, dhid, dback))
-    total = pairwise_sum([block.astype(f32) for block in [part] + came])
+        name="weights_out",
+    )(ids, weights, swap_depth(weights))
     return (
         feat.reshape(seqs, res, channels),
         couple.reshape(res, pair_cols, pair_width),

time: 42.8 us -> 47 us (1.098)
  waiting for transfers between devices: 11.3 us -> 13.6 us
  starting transfers between devices: 16.4 us -> 18.2 us
    ppermute x9 -> x11, starting transfers between devices: 15.3 us -> 17.4 us  [swap_col(): lax.ppermute(block, 'col', [(at, at ^ partner) for at in range(count)])]
    ppermute x9 -> x11, waiting for transfers between devices: 11.1 us -> 12.4 us  [swap_col(): lax.ppermute(block, 'col', [(at, at ^ partner) for at in range(count)])]
    ppermute x8 -> x7, waiting for transfers between devices: 0.19 us -> 1.18 us  [swap_depth(): return lax.ppermute(block, 'depth', [(0, 1), (1, 0)])]
    ppermute x8 -> x7, starting transfers between devices: 1.16 us -> 0.88 us  [swap_depth(): return lax.ppermute(block, 'depth', [(0, 1), (1, 0)])]
  transfers between devices with their start and end apart: 17 -> 18, of which waited for: 8 -> 9; matrix products, arithmetic and copies ran while one was open for 0% -> 3% of each run, Pallas kernels for 19% -> 12%
where the time goes in v5:
time: 47 us; the launch traced here: 46.8 us
  starting transfers between devices  18.2 us (39%)
  waiting for transfers between devices  13.6 us (29%)
  Pallas kernels  12.4 us (26%)
  local copies, waits for them, and re-layouts  1.46 us (3%)
  between operations  0.82 us (2%)
    ppermute x11, starting transfers between devices, swap_col(): lax.ppermute(block, 'col', [(at, at ^ partner) for at in range(count)])  17.4 us
    ppermute x11, waiting for transfers between devices, swap_col(): lax.ppermute(block, 'col', [(at, at ^ partner) for at in range(count)])  12.4 us
    pallas_call x1, Pallas kernels, whole_plan(): pl.pallas_call(functools.partial(projector_kernel, sizes), out_shape=(sha...  1.99 us
    pallas_call x1, Pallas kernels, whole_plan(): pl.pallas_call(functools.partial(transition_kernel, sizes), out_shape=(sh...  1.95 us
    pallas_call x1, Pallas kernels, whole_plan(): pl.pallas_call(pre_kernel, out_shape=(shape((1, rows + 2 * per, pair_widt...  1.91 us
    pallas_call x2, Pallas kernels, turned(): pl.pallas_call(functools.partial(turn_kernel, sizes, firsts), out_shape=(...  1.83 us
    pallas_call x1, Pallas kernels, whole_plan(): pl.pallas_call(functools.partial(outer_kernel, sizes), out_shape=(shape((...  1.59 us
    pallas_call x1, Pallas kernels, whole_plan(): pl.pallas_call(weights_out_kernel, out_shape=(shape((outer_width, pair_wi...  1.57 us
  transfers between devices with their start and end apart: 18, of which 9 were waited for; matrix products, arithmetic and copies ran while one was open for 3% of the time, Pallas kernels for 12%

profile of v5, /device:TPU:0, one launch (start us, length us, event | category | flops | bytes accessed | tf_op | source)
XLA Modules:
  0.0 46.8 jit_solution(14973284501859561624)
XLA Ops:
  0.6 0.1 pad_add_fusion.ids_ref
  0.7 1.9 %project.1 = (bf16[1,272,128]{2,1,0:T(8,128)(2,1)S(1)}, f32[1,256]{1,0:T(1,128)S(1)}, bf16[32,256]{1,0:T(8,128)(2,1)S(1)}, bf16[32,256]{1,0:T(8,128)(2,1)S(1)}, ...) custom-call(s32[2]{0:T(128)S(1)} %pad_add_fusion.ids_ref, ...), custom_call_target="tpu_custom_call" | custom-call | tf_op jit(solution)/shard_map/project/pallas_call | solution.py:814
  2.6 5.1 %collective-permute-start.2 = (bf16[1,272,128]{2,1,0:T(8,128)(2,1)S(1)}, bf16[1,272,128]{2,1,0:T(8,128)(2,1)S(1)}, u32[]{:S(2)}, u32[]{:S(2)}) collective-permute-start(bf16[1,272,128]{2,1,0:T(8,128)(2,1)S(1)} %get-tuple-element.55), channel_id=1, source_target_pairs={{0,6},{1,7},{2,4},{3,5},{4,2},{5,3},{6,0},{7,1},{8,14},{9,15},{10,... | collective-permute-start | bytes 208904 | tf_op jit(solution)/shard_map/ppermute | solution.py:772
  7.7 0.0 collective-permute-start.1
  7.8 0.6 %collective-permute-start = (bf16[1,272,128]{2,1,0:T(8,128)(2,1)S(1)}, bf16[1,272,128]{2,1,0:T(8,128)(2,1)S(1)}, u32[]{:S(2)}, u32[]{:S(2)}) collective-permute-start(bf16[1,272,128]{2,1,0:T(8,128)(2,1)S(1)} %get-tuple-element.55), channel_id=1, source_target_pairs={{0,2},{1,3},{2,0},{3,1},{4,6},{5,7},{6,4},{7,5},{8,10},{9,11},{10,... | collective-permute-start | bytes 208904 | tf_op jit(solution)/shard_map/ppermute | solution.py:772
  8.4 1.7 %collective-permute-start.3 = (bf16[256,256]{1,0:T(8,128)(2,1)S(1)}, bf16[256,256]{1,0:T(8,128)(2,1)S(1)}, u32[]{:S(2)}, u32[]{:S(2)}) collective-permute-start(bf16[256,256]{1,0:T(8,128)(2,1)S(1)} %get-tuple-element.56.normed_ref), channel_id=1, source_target_pairs={{0,1},{1,0},{2,3},{3,2},{4,5},{5,4},{6,7},{7,6},{8,9},{9,8},{10,11... | collective-permute-start | bytes 393224 | tf_op jit(solution)/shard_map/ppermute | solution.py:772
  10.1 0.4 collective-permute-done.2
  10.4 3.2 %collective-permute-done.1 = bf16[1,272,128]{2,1,0:T(8,128)(2,1)S(1)} collective-permute-done((bf16[1,272,128]{2,1,0:T(8,128)(2,1)S(1)}, bf16[1,272,128]{2,1,0:T(8,128)(2,1)S(1)}, u32[]{:S(2)}, u32[]{:S(2)}) %collective-permute-start.1) | collective-permute-done | bytes 69664 | tf_op jit(solution)/shard_map/ppermute | solution.py:772
  13.7 0.0 collective-permute-done
  13.7 0.0 collective-permute-done.4.other_normed_ref
  13.7 0.6 %collective-permute-done.3.far_normed_ref = bf16[256,256]{1,0:T(8,128)(2,1)S(1)} collective-permute-done((bf16[256,256]{1,0:T(8,128)(2,1)S(1)}, bf16[256,256]{1,0:T(8,128)(2,1)S(1)}, u32[]{:S(2)}, u32[]{:S(2)}) %collective-permute-start.3) | collective-permute-done | bytes 131104 | tf_op jit(solution)/shard_map/ppermute | solution.py:772
  14.3 0.0 copy-start
  14.3 0.1 collective-permute-start.6
  14.4 1.7 %collective-permute-start.5 = (bf16[4,80,128]{2,1,0:T(8,128)(2,1)S(1)}, bf16[4,80,128]{2,1,0:T(8,128)(2,1)S(1)}, u32[]{:S(2)}, u32[]{:S(2)}) collective-permute-start(bf16[4,80,128]{2,1,0:T(8,128)(2,1)S(1)} %slice.12), channel_id=1, source_target_pairs={{0,1},{1,0},{2,3},{3,2},{4,5},{5,4},{6,7},{7,6},{8,9},{9,8},{10,11... | collective-permute-start | bytes 245768 | tf_op jit(solution)/shard_map/ppermute | solution.py:772
  16.2 0.2 collective-permute-start.8
  16.3 0.0 collective-permute-done.6.other_ref.other_near_ref
  16.3 1.0 %turned.2 = (bf16[512,128]{1,0:T(8,128)(2,1)S(1)}, bf16[512,128]{1,0:T(8,128)(2,1)S(1)}) custom-call(s32[2]{0:T(128)S(1)} %pad_add_fusion.ids_ref, bf16[4,272,128]{2,1,0:T(8,128)(2,1)S(1)} %pad_maximum_fusion.mine_ref.near_ref, bf16[4,144,128]{2,1,0:T(8,128)(2,1)S(1)} %collective-permute-done.6.other_ref.other_near_ref), custom_call_target="tpu_custom_call" | custom-call | tf_op jit(solution)/shard_map/turned/pallas_call | solution.py:866
  17.3 1.9 %collective-permute-done.5.far_ref.mine_ref = bf16[4,80,128]{2,1,0:T(8,128)(2,1)S(1)} collective-permute-done((bf16[4,80,128]{2,1,0:T(8,128)(2,1)S(1)}, bf16[4,80,128]{2,1,0:T(8,128)(2,1)S(1)}, u32[]{:S(2)}, u32[]{:S(2)}) %collective-permute-start.5) | collective-permute-done | bytes 81952 | tf_op jit(solution)/shard_map/ppermute | solution.py:772
  19.3 0.0 collective-permute-start.7
  19.3 0.1 copy.19
  19.4 0.0 collective-permute-done.8.other_far_normed_ref
  19.4 1.2 %collective-permute-done.7.other_far_ref.other_ref = bf16[4,80,128]{2,1,0:T(8,128)(2,1)S(1)} collective-permute-done((bf16[4,80,128]{2,1,0:T(8,128)(2,1)S(1)}, bf16[4,80,128]{2,1,0:T(8,128)(2,1)S(1)}, u32[]{:S(2)}, u32[]{:S(2)}) %collective-permute-start.7) | collective-permute-done | bytes 81952 | tf_op jit(solution)/shard_map/ppermute | solution.py:761
  20.6 1.6 %outer_products.1 = (bf16[256,1024]{1,0:T(8,128)(2,1)S(1)}, f32[256,128]{1,0:T(8,128)S(1)}, f32[256,128]{1,0:T(8,128)S(1)}, bf16[256,128]{1,0:T(8,128)(2,1)S(1)}, f32[32,128]{1,0:T(8,128)S(1)}) custom-call(s32[2]{0:T(128)S(1)} %pad_add_fusion.ids_ref, bf16[4,272,128]{2,1,0:T(8,128)(2,1)S(1)} %pad_maximum_fusion.mine_ref.near_ref, ...), custom_call_target="tpu_custom_call" | custom-call | tf_op jit(solution)/shard_map/outer_products/pallas_call | solution.py:883
  22.2 1.9 %transition.1 = (bf16[64,128]{1,0:T(8,128)(2,1)}, bf16[256,128]{1,0:T(8,128)(2,1)S(1)}, bf16[256,128]{1,0:T(8,128)(2,1)S(1)}, bf16[256,512]{1,0:T(8,128)(2,1)S(1...) custom-call(s32[2]{0:T(128)S(1)} %pad_add_fusion.ids_ref, ...), custom_call_target="tpu_custom_call" | custom-call | tf_op jit(solution)/shard_map/transition/pallas_call | solution.py:906
  24.1 0.2 collective-permute-start.9
  24.3 0.8 %turned.3.right_far_ref = bf16[512,128]{1,0:T(8,128)(2,1)S(1)} custom-call(s32[2]{0:T(128)S(1)} %pad_add_fusion.ids_ref, bf16[4,80,128]{2,1,0:T(8,128)(2,1)S(1)} %collective-permute-done.5.far_ref.mine_ref, bf16[4,80,128]{2,1,0:T(8,128)(2,1)S(1)} %collective-permute-done.7.other_far_ref.other_ref), custom_call_target="tpu_custom_call" | custom-call | tf_op jit(solution)/shard_map/turned/pallas_call | solution.py:866
  25.1 1.3 %weight_gradients.1 = (bf16[1024,128]{1,0:T(8,128)(2,1)S(1)}, bf16[1024,128]{1,0:T(8,128)(2,1)S(1)}) custom-call(s32[2]{0:T(128)S(1)} %pad_add_fusion.ids_ref, bf16[256,1024]{1,0:T(8,128)(2,1)S(1)} %get-tuple-element.69.outer_ref, bf16[256,128]{1,0:T(8,128)(2,1)S(1)} %get-tuple-element.67.opm_ref, bf16[256,128]{1,0:T(8,128)(2,1)S(1)} %get-tuple-element.70.pn_ref, ...), custom_call_target="tpu_custom_call" | custom-call | tf_op jit(solution)/shard_map/weight_gradients/pallas_call | solution.py:929
  26.4 0.4 collective-permute-start.10
  26.8 2.0 %projector_parts.1 = (bf16[64,256]{1,0:T(8,128)(2,1)S(1)}, f32[64,128]{1,0:T(8,128)S(1)}, f32[64,128]{1,0:T(8,128)S(1)}, f32[64,128]{1,0:T(8,128)S(1)}) custom-call(s32[2]{0:T(128)S(1)} %pad_add_fusion.ids_ref, bf16[256,128]{1,0:T(8,128)(2,1)S(1)} %get-tuple-element.67.opm_ref, bf16[256,128]{1,0:T(8,128)(2,1)S(1)} %collective-permute-done.9.other_opm_ref, ...), custom_call_target="tpu_custom_call" | custom-call | tf_op jit(solution)/shard_map/projector_parts/pallas_call | solution.py:942
  28.8 0.0 collective-permute-done.10
  28.8 0.1 add_convert_fusion.1
  28.9 1.7 %collective-permute-start.16 = (bf16[1024,128]{1,0:T(8,128)(2,1)S(1)}, bf16[1024,128]{1,0:T(8,128)(2,1)S(1)}, u32[]{:S(2)}, u32[]{:S(2)}) collective-permute-start(bf16[1024,128]{1,0:T(8,128)(2,1)S(1)} %add_convert_fusion.1), channel_id=1, source_target_pairs={{0,1},{1,0},{2,3},{3,2},{4,5},{5,4},{6,7},{7,6},{8,9},{9,8},{10,11... | collective-permute-start | bytes 786440 | tf_op jit(solution)/shard_map/ppermute | solution.py:772
  30.7 3.6 %collective-permute-start.11 = (bf16[64,256]{1,0:T(8,128)(2,1)S(1)}, bf16[64,256]{1,0:T(8,128)(2,1)S(1)}, u32[]{:S(2)}, u32[]{:S(2)}) collective-permute-start(bf16[64,256]{1,0:T(8,128)(2,1)S(1)} %get-tuple-element.88), channel_id=1, source_target_pairs={{0,6},{1,7},{2,4},{3,5},{4,2},{5,3},{6,0},{7,1},{8,14},{9,15},{10,... | collective-permute-start | bytes 98312 | tf_op jit(solution)/shard_map/ppermute | solution.py:772
  34.3 0.0 collective-permute-start.14
  34.3 0.8 %collective-permute-start.13 = (bf16[64,256]{1,0:T(8,128)(2,1)S(1)}, bf16[64,256]{1,0:T(8,128)(2,1)S(1)}, u32[]{:S(2)}, u32[]{:S(2)}) collective-permute-start(bf16[64,256]{1,0:T(8,128)(2,1)S(1)} %get-tuple-element.88), channel_id=1, source_target_pairs={{0,2},{1,3},{2,0},{3,1},{4,6},{5,7},{6,4},{7,5},{8,10},{9,11},{10,... | collective-permute-start | bytes 98312 | tf_op jit(solution)/shard_map/ppermute | solution.py:772
  35.0 1.5 %collective-permute-done.11 = bf16[64,256]{1,0:T(8,128)(2,1)S(1)} collective-permute-done((bf16[64,256]{1,0:T(8,128)(2,1)S(1)}, bf16[64,256]{1,0:T(8,128)(2,1)S(1)}, u32[]{:S(2)}, u32[]{:S(2)}) %collective-permute-start.11) | collective-permute-done | bytes 32800 | tf_op jit(solution)/shard_map/ppermute | solution.py:772
  36.6 2.5 %collective-permute-done.14 = bf16[64,256]{1,0:T(8,128)(2,1)S(1)} collective-permute-done((bf16[64,256]{1,0:T(8,128)(2,1)S(1)}, bf16[64,256]{1,0:T(8,128)(2,1)S(1)}, u32[]{:S(2)}, u32[]{:S(2)}) %collective-permute-start.14) | collective-permute-done | bytes 32800 | tf_op jit(solution)/shard_map/ppermute | solution.py:772
  39.1 0.6 %collective-permute-start.15 = (bf16[64,256]{1,0:T(8,128)(2,1)S(1)}, bf16[64,256]{1,0:T(8,128)(2,1)S(1)}, u32[]{:S(2)}, u32[]{:S(2)}) collective-permute-start(bf16[64,256]{1,0:T(8,128)(2,1)S(1)} %add_convert_fusion.2), channel_id=1, source_target_pairs={{0,1},{1,0},{2,3},{3,2},{4,5},{5,4},{6,7},{7,6},{8,9},{9,8},{10,11... | collective-permute-start | bytes 98312 | tf_op jit(solution)/shard_map/ppermute | solution.py:772
  39.7 1.5 %collective-permute-start.12 = (f32[64,128]{1,0:T(8,128)S(1)}, f32[64,128]{1,0:T(8,128)S(1)}, u32[]{:S(2)}, u32[]{:S(2)}) collective-permute-start(f32[64,128]{1,0:T(8,128)S(1)} %get-tuple-element.90), channel_id=1, source_target_pairs={{0,1},{1,0},{2,3},{3,2},{4,5},{5,4},{6,7},{7,6},{8,9},{9,8},{10,11... | collective-permute-start | bytes 98312 | tf_op jit(solution)/shard_map/ppermute | solution.py:772
  41.2 0.0 collective-permute-done.16
  41.2 0.1 add_convert_fusion.mine_ref
  41.3 0.1 collective-permute-start.17
  41.4 1.7 %collective-permute-done.15 = bf16[64,256]{1,0:T(8,128)(2,1)S(1)} collective-permute-done((bf16[64,256]{1,0:T(8,128)(2,1)S(1)}, bf16[64,256]{1,0:T(8,128)(2,1)S(1)}, u32[]{:S(2)}, u32[]{:S(2)}) %collective-permute-start.15) | collective-permute-done | bytes 32800 | tf_op jit(solution)/shard_map/ppermute | solution.py:772
  43.1 0.5 %collective-permute-done.12.gright_came_ref = f32[64,128]{1,0:T(8,128)S(1)} collective-permute-done((f32[64,128]{1,0:T(8,128)S(1)}, f32[64,128]{1,0:T(8,128)S(1)}, u32[]{:S(2)}, u32[]{:S(2)}) %collective-permute-start.12) | collective-permute-done | bytes 32800 | tf_op jit(solution)/shard_map/ppermute | solution.py:772
  43.6 0.3 features.1
  43.9 0.7 %reshape.44 = bf16[64,4,256]{2,1,0:T(4,128)(2,1)} reshape(bf16[256,256]{1,0:T(8,128)(2,1)S(1)} %features.1) | data formatting | bytes 262144 | tf_op jit(solution)/shard_map/reshape | solution.py:1017
  44.6 0.6 %slice_bitcast_fusion = (f32[256,32]{0,1:T(8,128)}, f32[256,32]{0,1:T(8,128)}) fusion(f32[64,256]{1,0:T(8,128)S(1)} %convert_add_fusion), kind=kLoop, calls=%fused_computation.5 | loop fusion | bytes 131072 | tf_op jit(solution)/shard_map/transpose | solution.py:1020
  45.2 1.6 %weights_out.1 = (f32[1024,128]{1,0:T(8,128)}, f32[128,512]{1,0:T(8,128)}, f32[512,128]{1,0:T(8,128)}) custom-call(s32[2]{0:T(128)S(1)} %pad_add_fusion.ids_ref, bf16[1024,128]{1,0:T(8,128)(2,1)S(1)} %add_convert_fusion.mine_ref, bf16[1024,128]{1,0:T(8,128)(2,1)S(1)} %collective-permute-done.17.other_ref), custom_call_target="tpu_custom_call" | custom-call | tf_op jit(solution)/shard_map/weights_out/pallas_call | solution.py:1003
  (14 shorter events, 0.1 us)
Async XLA Ops:
  2.6 7.8 %collective-permute-start.2 = (bf16[1,272,128]{2,1,0:T(8,128)(2,1)S(1)}, bf16[1,272,128]{2,1,0:T(8,128)(2,1)S(1)}, u32[]{:S(2)}, u32[]{:S(2)}) collective-permute-start(bf16[1,272,128]{2,1,0:T(8,128)(2,1)S(1)} %get-tuple-element.55), channel_id=1, source_target_pairs={{0,6},{1,7},{2,4},{3,5},{4,2},{5,3},{6,0},{7,1},{8,14},{9,15},{10,... | collective-permute-start | bytes 208904 | tf_op jit(solution)/shard_map/ppermute | solution.py:772
  7.7 5.9 %collective-permute-start.1 = (bf16[1,272,128]{2,1,0:T(8,128)(2,1)S(1)}, bf16[1,272,128]{2,1,0:T(8,128)(2,1)S(1)}, u32[]{:S(2)}, u32[]{:S(2)}) collective-permute-start(bf16[1,272,128]{2,1,0:T(8,128)(2,1)S(1)} %get-tuple-element.55), channel_id=1, source_target_pairs={{0,4},{1,5},{2,6},{3,7},{4,0},{5,1},{6,2},{7,3},{8,12},{9,13},{10,... | collective-permute-start | bytes 208904 | tf_op jit(solution)/shard_map/ppermute | solution.py:772
  7.8 5.9 %collective-permute-start = (bf16[1,272,128]{2,1,0:T(8,128)(2,1)S(1)}, bf16[1,272,128]{2,1,0:T(8,128)(2,1)S(1)}, u32[]{:S(2)}, u32[]{:S(2)}) collective-permute-start(bf16[1,272,128]{2,1,0:T(8,128)(2,1)S(1)} %get-tuple-element.55), channel_id=1, source_target_pairs={{0,2},{1,3},{2,0},{3,1},{4,6},{5,7},{6,4},{7,5},{8,10},{9,11},{10,... | collective-permute-start | bytes 208904 | tf_op jit(solution)/shard_map/ppermute | solution.py:772
  8.4 5.3 %collective-permute-start.4 = (bf16[256,256]{1,0:T(8,128)(2,1)S(1)}, bf16[256,256]{1,0:T(8,128)(2,1)S(1)}, u32[]{:S(2)}, u32[]{:S(2)}) collective-permute-start(bf16[256,256]{1,0:T(8,128)(2,1)S(1)} %get-tuple-element.56.normed_ref), channel_id=1, source_target_pairs={{0,8},{8,0},{1,9},{9,1},{2,10},{10,2},{3,11},{11,3},{4,12},{12,4},... | collective-permute-start | bytes 393224 | tf_op jit(solution)/shard_map/ppermute | solution.py:761
  8.4 5.9 %collective-permute-start.3 = (bf16[256,256]{1,0:T(8,128)(2,1)S(1)}, bf16[256,256]{1,0:T(8,128)(2,1)S(1)}, u32[]{:S(2)}, u32[]{:S(2)}) collective-permute-start(bf16[256,256]{1,0:T(8,128)(2,1)S(1)} %get-tuple-element.56.normed_ref), channel_id=1, source_target_pairs={{0,1},{1,0},{2,3},{3,2},{4,5},{5,4},{6,7},{7,6},{8,9},{9,8},{10,11... | collective-permute-start | bytes 393224 | tf_op jit(solution)/shard_map/ppermute | solution.py:772
  14.3 5.0 %copy-start = (bf16[1024,128]{1,0:T(8,128)(2,1)S(1)}, bf16[1024,128]{1,0:T(8,128)(2,1)}, u32[]{:S(2)}) copy-start(bf16[1024,128]{1,0:T(8,128)(2,1)} %wout_ref.1) | copy-start | bytes 786436
  14.3 2.0 %collective-permute-start.6 = (bf16[4,144,128]{2,1,0:T(8,128)(2,1)S(1)}, bf16[4,144,128]{2,1,0:T(8,128)(2,1)S(1)}, u32[]{:S(2)}, u32[]{:S(2)}) collective-permute-start(bf16[4,144,128]{2,1,0:T(8,128)(2,1)S(1)} %slice.13), channel_id=1, source_target_pairs={{0,8},{8,0},{1,9},{9,1},{2,10},{10,2},{3,11},{11,3},{4,12},{12,4},... | collective-permute-start | bytes 442376 | tf_op jit(solution)/shard_map/ppermute | solution.py:761
  14.4 4.9 %collective-permute-start.5 = (bf16[4,80,128]{2,1,0:T(8,128)(2,1)S(1)}, bf16[4,80,128]{2,1,0:T(8,128)(2,1)S(1)}, u32[]{:S(2)}, u32[]{:S(2)}) collective-permute-start(bf16[4,80,128]{2,1,0:T(8,128)(2,1)S(1)} %slice.12), channel_id=1, source_target_pairs={{0,1},{1,0},{2,3},{3,2},{4,5},{5,4},{6,7},{7,6},{8,9},{9,8},{10,11... | collective-permute-start | bytes 245768 | tf_op jit(solution)/shard_map/ppermute | solution.py:772
  16.2 3.2 %collective-permute-start.8 = (bf16[256,256]{1,0:T(8,128)(2,1)S(1)}, bf16[256,256]{1,0:T(8,128)(2,1)S(1)}, u32[]{:S(2)}, u32[]{:S(2)}) collective-permute-start(bf16[256,256]{1,0:T(8,128)(2,1)S(1)} %collective-permute-done.3.far_normed_ref), channel_id=1, source_target_pairs={{0,8},{8,0},{1,9},{9,1},{2,10},{10,2},{3,11},{11,3},{4,12},{12,4},... | collective-permute-start | bytes 393224 | tf_op jit(solution)/shard_map/ppermute | solution.py:761
  19.3 1.3 %collective-permute-start.7 = (bf16[4,80,128]{2,1,0:T(8,128)(2,1)S(1)}, bf16[4,80,128]{2,1,0:T(8,128)(2,1)S(1)}, u32[]{:S(2)}, u32[]{:S(2)}) collective-permute-start(bf16[4,80,128]{2,1,0:T(8,128)(2,1)S(1)} %collective-permute-done.5.far_ref.mine_ref), channel_id=1, source_target_pairs={{0,8},{8,0},{1,9},{9,1},{2,10},{10,2},{3,11},{11,3},{4,12},{12,4},... | collective-permute-start | bytes 245768 | tf_op jit(solution)/shard_map/ppermute | solution.py:761
  20.6 1.6 %copy-start.1 = (bf16[128,512]{1,0:T(8,128)(2,1)S(1)}, bf16[128,512]{1,0:T(8,128)(2,1)}, u32[]{:S(2)}) copy-start(bf16[128,512]{1,0:T(8,128)(2,1)} %hid_ref.1) | copy-start | bytes 393220
  20.6 1.6 %copy-start.2 = (bf16[512,128]{1,0:T(8,128)(2,1)S(1)}, bf16[512,128]{1,0:T(8,128)(2,1)}, u32[]{:S(2)}) copy-start(bf16[512,128]{1,0:T(8,128)(2,1)} %back_ref.1) | copy-start | bytes 393220
  24.1 2.3 %collective-permute-start.9 = (bf16[256,128]{1,0:T(8,128)(2,1)S(1)}, bf16[256,128]{1,0:T(8,128)(2,1)S(1)}, u32[]{:S(2)}, u32[]{:S(2)}) collective-permute-start(bf16[256,128]{1,0:T(8,128)(2,1)S(1)} %get-tuple-element.67.opm_ref), channel_id=1, source_target_pairs={{0,8},{8,0},{1,9},{9,1},{2,10},{10,2},{3,11},{11,3},{4,12},{12,4},... | collective-permute-start | bytes 196616 | tf_op jit(solution)/shard_map/ppermute | solution.py:761
  26.4 2.4 %collective-permute-start.10 = (bf16[1024,128]{1,0:T(8,128)(2,1)S(1)}, bf16[1024,128]{1,0:T(8,128)(2,1)S(1)}, u32[]{:S(2)}, u32[]{:S(2)}) collective-permute-start(bf16[1024,128]{1,0:T(8,128)(2,1)S(1)} %get-tuple-element.86), channel_id=1, source_target_pairs={{0,8},{8,0},{1,9},{9,1},{2,10},{10,2},{3,11},{11,3},{4,12},{12,4},... | collective-permute-start | bytes 786440 | tf_op jit(solution)/shard_map/ppermute | solution.py:761
  28.9 12.3 %collective-permute-start.16 = (bf16[1024,128]{1,0:T(8,128)(2,1)S(1)}, bf16[1024,128]{1,0:T(8,128)(2,1)S(1)}, u32[]{:S(2)}, u32[]{:S(2)}) collective-permute-start(bf16[1024,128]{1,0:T(8,128)(2,1)S(1)} %add_convert_fusion.1), channel_id=1, source_target_pairs={{0,1},{1,0},{2,3},{3,2},{4,5},{5,4},{6,7},{7,6},{8,9},{9,8},{10,11... | collective-permute-start | bytes 786440 | tf_op jit(solution)/shard_map/ppermute | solution.py:772
  30.7 5.9 %collective-permute-start.11 = (bf16[64,256]{1,0:T(8,128)(2,1)S(1)}, bf16[64,256]{1,0:T(8,128)(2,1)S(1)}, u32[]{:S(2)}, u32[]{:S(2)}) collective-permute-start(bf16[64,256]{1,0:T(8,128)(2,1)S(1)} %get-tuple-element.88), channel_id=1, source_target_pairs={{0,6},{1,7},{2,4},{3,5},{4,2},{5,3},{6,0},{7,1},{8,14},{9,15},{10,... | collective-permute-start | bytes 98312 | tf_op jit(solution)/shard_map/ppermute | solution.py:772
  34.3 4.8 %collective-permute-start.14 = (bf16[64,256]{1,0:T(8,128)(2,1)S(1)}, bf16[64,256]{1,0:T(8,128)(2,1)S(1)}, u32[]{:S(2)}, u32[]{:S(2)}) collective-permute-start(bf16[64,256]{1,0:T(8,128)(2,1)S(1)} %get-tuple-element.88), channel_id=1, source_target_pairs={{0,4},{1,5},{2,6},{3,7},{4,0},{5,1},{6,2},{7,3},{8,12},{9,13},{10,... | collective-permute-start | bytes 98312 | tf_op jit(solution)/shard_map/ppermute | solution.py:772
  34.3 4.8 %collective-permute-start.13 = (bf16[64,256]{1,0:T(8,128)(2,1)S(1)}, bf16[64,256]{1,0:T(8,128)(2,1)S(1)}, u32[]{:S(2)}, u32[]{:S(2)}) collective-permute-start(bf16[64,256]{1,0:T(8,128)(2,1)S(1)} %get-tuple-element.88), channel_id=1, source_target_pairs={{0,2},{1,3},{2,0},{3,1},{4,6},{5,7},{6,4},{7,5},{8,10},{9,11},{10,... | collective-permute-start | bytes 98312 | tf_op jit(solution)/shard_map/ppermute | solution.py:772
  39.1 4.0 %collective-permute-start.15 = (bf16[64,256]{1,0:T(8,128)(2,1)S(1)}, bf16[64,256]{1,0:T(8,128)(2,1)S(1)}, u32[]{:S(2)}, u32[]{:S(2)}) collective-permute-start(bf16[64,256]{1,0:T(8,128)(2,1)S(1)} %add_convert_fusion.2), channel_id=1, source_target_pairs={{0,1},{1,0},{2,3},{3,2},{4,5},{5,4},{6,7},{7,6},{8,9},{9,8},{10,11... | collective-permute-start | bytes 98312 | tf_op jit(solution)/shard_map/ppermute | solution.py:772
  39.7 3.9 %collective-permute-start.12 = (f32[64,128]{1,0:T(8,128)S(1)}, f32[64,128]{1,0:T(8,128)S(1)}, u32[]{:S(2)}, u32[]{:S(2)}) collective-permute-start(f32[64,128]{1,0:T(8,128)S(1)} %get-tuple-element.90), channel_id=1, source_target_pairs={{0,1},{1,0},{2,3},{3,2},{4,5},{5,4},{6,7},{7,6},{8,9},{9,8},{10,11... | collective-permute-start | bytes 98312 | tf_op jit(solution)/shard_map/ppermute | solution.py:772
  41.3 3.9 %collective-permute-start.17 = (bf16[1024,128]{1,0:T(8,128)(2,1)S(1)}, bf16[1024,128]{1,0:T(8,128)(2,1)S(1)}, u32[]{:S(2)}, u32[]{:S(2)}) collective-permute-start(bf16[1024,128]{1,0:T(8,128)(2,1)S(1)} %add_convert_fusion.mine_ref), channel_id=1, source_target_pairs={{0,8},{8,0},{1,9},{9,1},{2,10},{10,2},{3,11},{11,3},{4,12},{12,4},... | collective-permute-start | bytes 786440 | tf_op jit(solution)/shard_map/ppermute | solution.py:761

commit v6 on v4

--- a/solution.py
+++ b/solution.py
@@ -444,22 +444,25 @@
     cnt_ref[...] = jnp.dot(cntl_ref[...], ones, preferred_element_type=f32)
     pm_ref[...] = jnp.dot(pml_ref[...], ones, preferred_element_type=f32).astype(bf16)
 
-    for dh in range(width // 4):
+    for k2 in range(cols // 2):
         prod = jnp.dot(
-            mine_ref[dh * 4 * pair_cols : (dh + 1) * 4 * pair_cols, :],
-            leftn_ref[...],
+            mine_ref[...],
+            leftn_ref[:, 2 * k2 * lanes : 2 * (k2 + 1) * lanes],
             preferred_element_type=f32,
         )
-        for k in range(cols):
-            piece = prod[:, k * lanes : (k + 1) * lanes]
-            turned = butterfly(
-                [piece[a * pair_cols : (a + 1) * pair_cols] for a in range(4)], width
-            )
-            for il in range(res):
-                first = (k * res + il) * pair_cols
-                outer_ref[first : first + pair_cols, dh * lanes : (dh + 1) * lanes] = turned[
-                    il
-                ].astype(bf16)
+        for dh in range(width // 4):
+            for b in range(2):
+                piece = prod[
+                    dh * 4 * pair_cols : (dh + 1) * 4 * pair_cols, b * lanes : (b + 1) * lanes
+                ]
+                turned = butterfly(
+                    [piece[a * pair_cols : (a + 1) * pair_cols] for a in range(4)], width
+                )
+                for il in range(res):
+                    first = ((2 * k2 + b) * res + il) * pair_cols
+                    outer_ref[first : first + pair_cols, dh * lanes : (dh + 1) * lanes] = turned[
+                        il
+                    ].astype(bf16)
     proj_out_ref[...] = jnp.dot(outer_ref[...], wturn_ref[...], preferred_element_type=f32)
 
 
@@ -679,27 +682,42 @@
         part_ref[at * width : (at + 1) * width, :] = total.astype(bf16)
 
 
-def out_weight_kernel(outer_ref, opm_ref, dout_ref, turn_ref):
-    width = int(dout_ref.shape[0] ** 0.5 + 0.5)
-    turn_ref[...] = lax.dot_general(
-        outer_ref[...], opm_ref[...], (((0,), (0,)), ((), ())), preferred_element_type=jnp.float32
-    )
+def weights_kernel(outer_ref, opm_ref, pn_ref, gh_ref, hidden_ref, mg_ref, out_ref, turn_ref):
+    pair_width, hid = pn_ref.shape[1], gh_ref.shape[1]
+    outer_width = outer_ref.shape[1]
+    width = int(outer_width**0.5 + 0.5)
+
+    def contract(lhs, rhs):
+        return lax.dot_general(
+            lhs[...], rhs[...], (((0,), (0,)), ((), ())), preferred_element_type=jnp.float32
+        )
+
+    turn_ref[...] = contract(outer_ref, opm_ref)
     for c in range(width):
-        dout_ref[c * width : (c + 1) * width, :] = turn_ref[
+        out_ref[c * width : (c + 1) * width, :] = turn_ref[
             pl.ds(c, width, stride=width), :
         ].astype(jnp.bfloat16)
-
-
-def transition_weight_kernel(pn_ref, gh_ref, hidden_ref, mg_ref, dhid_ref, dback_ref):
-    for lhs, rhs, out in ((pn_ref, gh_ref, dhid_ref), (hidden_ref, mg_ref, dback_ref)):
-        out[...] = lax.dot_general(
-            lhs[...], rhs[...], (((0,), (0,)), ((), ())), preferred_element_type=jnp.float32
-        ).astype(jnp.bfloat16)
-
-
-def sum_kernel(*refs):
-    for mine, other, out in zip(refs[0:3], refs[3:6], refs[6:9]):
-        out[...] = mine[...].astype(jnp.float32) + other[...].astype(jnp.float32)
+    dhid = contract(pn_ref, gh_ref).astype(jnp.bfloat16)
+    for at in range(hid // pair_width):
+        first = outer_width + at * pair_width
+        out_ref[first : first + pair_width, :] = dhid[:, at * pair_width : (at + 1) * pair_width]
+    out_ref[outer_width + hid :, :] = contract(hidden_ref, mg_ref).astype(jnp.bfloat16)
+
+
+def weights_sum_kernel(mine_ref, other_ref, dout_ref, dhid_ref, dback_ref):
+    pair_width, hid = dhid_ref.shape
+    outer_width = dout_ref.shape[0]
+
+    def added(first, count):
+        rows = slice(first, first + count)
+        return mine_ref[rows, :].astype(jnp.float32) + other_ref[rows, :].astype(jnp.float32)
+
+    dout_ref[...] = added(0, outer_width)
+    for at in range(hid // pair_width):
+        dhid_ref[:, at * pair_width : (at + 1) * pair_width] = added(
+            outer_width + at * pair_width, pair_width
+        )
+    dback_ref[...] = added(outer_width + hid, hid)
 
 
 def feature_kernel(
@@ -814,11 +832,10 @@
         jnp.concatenate([sent] + [swap_col(sent, partner) for partner in Z_PARTNERS])
     )
     near, pair_near = blocks[:, :rows], blocks[:, rows:]
-    far_normed = swap_col(normed, Y_PARTNER)
-    other_normed, other_far_normed = swap_depth(normed), swap_depth(far_normed)
-    near, far_normed, other_normed = lax.optimization_barrier((near, far_normed, other_normed))
     far = swap_col(near, Y_PARTNER)
     pair_far = swap_col(pair_near, Y_PARTNER)
+    far, normed = lax.optimization_barrier((far, normed))
+    far_normed = swap_col(normed, Y_PARTNER)
     other_near, other_far = swap_depth(near), swap_depth(far)
     sizes = (seqs, res, pair_cols, width)
     orders = (near_order, far_order)
@@ -860,8 +877,8 @@
         compiler_params=params,
         name="turned",
     )(ids, near, far, other_near, other_far)
-    pair_far, rightt, leftt, proj_out, other_far_normed = lax.optimization_barrier(
-        (pair_far, rightt, leftt, proj_out, other_far_normed)
+    pair_far, rightt, leftt, proj_out = lax.optimization_barrier(
+        (pair_far, rightt, leftt, proj_out)
     )
     couple, opm, pn, gh, hidden, mg = pl.pallas_call(
         functools.partial(transition_kernel, sizes, orders),
@@ -892,25 +909,19 @@
         hidden_weight,
         back_weight,
     )
-    dout = pl.pallas_call(
-        out_weight_kernel,
-        out_shape=shape((outer_width, pair_width), bf16),
-        in_specs=[vmem] * 2,
+    opm, far_normed = lax.optimization_barrier((opm, far_normed))
+    weights = pl.pallas_call(
+        weights_kernel,
+        out_shape=shape((outer_width + 2 * hid, pair_width), bf16),
+        in_specs=[vmem] * 6,
         out_specs=vmem,
         scratch_shapes=[pltpu.VMEM((outer_width, pair_width), f32)],
         compiler_params=params,
-        name="out_weight",
-    )(outer, opm)
-    dhid, dback = pl.pallas_call(
-        transition_weight_kernel,
-        out_shape=(shape((pair_width, hid), bf16), shape((hid, pair_width), bf16)),
-        in_specs=[vmem] * 4,
-        out_specs=[vmem] * 2,
-        compiler_params=params,
-        name="transition_weights",
-    )(pn, gh, hidden, mg)
-    other_opm, dout, dhid, dback = lax.optimization_barrier((swap_depth(opm), dout, dhid, dback))
-    other_weights = [swap_depth(block) for block in (dout, dhid, dback)]
+        name="weight_gradients",
+    )(outer, opm, pn, gh, hidden, mg)
+    other_opm, other_normed, other_far_normed, weights = lax.optimization_barrier(
+        (swap_depth(opm), swap_depth(normed), swap_depth(far_normed), weights)
+    )
     part, spread = pl.pallas_call(
         functools.partial(projector_kernel, sizes),
         out_shape=(
@@ -952,19 +963,20 @@
         compiler_params=params,
         name="features",
     )(spread, first, second, scale, scaled, inv)
+    came = [swap_col(part, partner) for partner in Z_PARTNERS]
+    came[2], weights = lax.optimization_barrier((came[2], weights))
     dout, dhid, dback = pl.pallas_call(
-        sum_kernel,
+        weights_sum_kernel,
         out_shape=(
             shape((outer_width, pair_width), f32),
             shape((pair_width, hid), f32),
             shape((hid, pair_width), f32),
         ),
-        in_specs=[vmem] * 6,
+        in_specs=[vmem] * 2,
         out_specs=[vmem] * 3,
         compiler_params=params,
         name="sums_over_depth",
-    )(dout, dhid, dback, *other_weights)
-    came = [swap_col(part, partner) for partner in Z_PARTNERS]
+    )(weights, swap_depth(weights))
     came, feat, dout, dhid, dback = lax.optimization_barrier((came, feat, dout, dhid, dback))
     total = pairwise_sum([block.astype(f32) for block in [part] + came])
     return (

time: 42.8 us -> 44.5 us (1.040)
  waiting for transfers between devices: 11.3 us -> 15 us
  starting transfers between devices: 16.4 us -> 14.5 us
    ppermute x9, waiting for transfers between devices: 11.1 us -> 14.8 us  [swap_col(): lax.ppermute(block, 'col', [(at, at ^ partner) for at in range(count)])]
    ppermute x9, starting transfers between devices: 15.3 us -> 13.9 us  [swap_col(): lax.ppermute(block, 'col', [(at, at ^ partner) for at in range(count)])]
    ppermute x8 -> x6, starting transfers between devices: 1.16 us -> 0.59 us  [swap_depth(): return lax.ppermute(block, 'depth', [(0, 1), (1, 0)])]
    pallas_call x3 -> x2, Pallas kernels: 2.17 us -> 1.93 us  [the longest x1 1.02 us: whole_plan(): pl.pallas_call(weights_sum_kernel, out_shape=(shape((outer_width, pair_wi...]
  transfers between devices with their start and end apart: 17 -> 15, of which waited for: 8 -> 8; matrix products, arithmetic and copies ran while one was open for 0% -> 0% of each run, Pallas kernels for 19% -> 19%
where the time goes in v6:
time: 44.5 us; the launch traced here: 44.2 us
  waiting for transfers between devices  15 us (34%)
  starting transfers between devices  14.5 us (33%)
  Pallas kernels  12.4 us (28%)
  local copies, waits for them, and re-layouts  1.47 us (3%)
  between operations  0.79 us (2%)
    ppermute x9, waiting for transfers between devices, swap_col(): lax.ppermute(block, 'col', [(at, at ^ partner) for at in range(count)])  14.8 us
    ppermute x9, starting transfers between devices, swap_col(): lax.ppermute(block, 'col', [(at, at ^ partner) for at in range(count)])  13.9 us
    pallas_call x1, Pallas kernels, whole_plan(): pl.pallas_call(functools.partial(transition_kernel, sizes, orders), out_s...  2.41 us
    pallas_call x1, Pallas kernels, whole_plan(): pl.pallas_call(functools.partial(outer_kernel, sizes, orders), out_shape=...  2.4 us
    pallas_call x1, Pallas kernels, whole_plan(): pl.pallas_call(functools.partial(projector_kernel, sizes), out_shape=(sha...  2.03 us
    pallas_call x1, Pallas kernels, whole_plan(): pl.pallas_call(pre_kernel, out_shape=(shape((1, rows + 2 * per, pair_widt...  1.91 us
    pallas_call x1, Pallas kernels, whole_plan(): pl.pallas_call(functools.partial(turn_kernel, sizes, orders), out_shape=(...  1.39 us
    pallas_call x1, Pallas kernels, whole_plan(): pl.pallas_call(weights_sum_kernel, out_shape=(shape((outer_width, pair_wi...  1.02 us
  transfers between devices with their start and end apart: 15, of which 8 were waited for; matrix products, arithmetic and copies ran while one was open for 0% of the time, Pallas kernels for 19%

profile of v6, /device:TPU:0, one launch (start us, length us, event | category | flops | bytes accessed | tf_op | source)
XLA Modules:
  0.0 44.2 jit_solution(14211727331999734868)
XLA Ops:
  0.6 0.1 pad_add_fusion.ids_ref
  0.7 1.9 %project.1 = (bf16[1,272,128]{2,1,0:T(8,128)(2,1)S(1)}, f32[1,256]{1,0:T(1,128)S(1)}, bf16[32,256]{1,0:T(8,128)(2,1)S(1)}, bf16[32,256]{1,0:T(8,128)(2,1)S(1)}, ...) custom-call(s32[2]{0:T(128)S(1)} %pad_add_fusion.ids_ref, ...), custom_call_target="tpu_custom_call" | custom-call | tf_op jit(solution)/shard_map/project/pallas_call | solution.py:788
  2.6 3.1 %collective-permute-start = (bf16[1,272,128]{2,1,0:T(8,128)(2,1)S(1)}, bf16[1,272,128]{2,1,0:T(8,128)(2,1)S(1)}, u32[]{:S(2)}, u32[]{:S(2)}) collective-permute-start(bf16[1,272,128]{2,1,0:T(8,128)(2,1)S(1)} %get-tuple-element.57), channel_id=1, source_target_pairs={{0,2},{1,3},{2,0},{3,1},{4,6},{5,7},{6,4},{7,5},{8,10},{9,11},{10,... | collective-permute-start | bytes 208904 | tf_op jit(solution)/shard_map/ppermute | solution.py:748
  5.7 2.6 %collective-permute-start.1 = (bf16[1,272,128]{2,1,0:T(8,128)(2,1)S(1)}, bf16[1,272,128]{2,1,0:T(8,128)(2,1)S(1)}, u32[]{:S(2)}, u32[]{:S(2)}) collective-permute-start(bf16[1,272,128]{2,1,0:T(8,128)(2,1)S(1)} %get-tuple-element.57), channel_id=1, source_target_pairs={{0,4},{1,5},{2,6},{3,7},{4,0},{5,1},{6,2},{7,3},{8,12},{9,13},{10,... | collective-permute-start | bytes 208904 | tf_op jit(solution)/shard_map/ppermute | solution.py:748
  8.3 0.0 collective-permute-start.2
  8.3 0.0 collective-permute-done
  8.3 4.9 %collective-permute-done.1 = bf16[1,272,128]{2,1,0:T(8,128)(2,1)S(1)} collective-permute-done((bf16[1,272,128]{2,1,0:T(8,128)(2,1)S(1)}, bf16[1,272,128]{2,1,0:T(8,128)(2,1)S(1)}, u32[]{:S(2)}, u32[]{:S(2)}) %collective-permute-start.1) | collective-permute-done | bytes 69664 | tf_op jit(solution)/shard_map/ppermute | solution.py:748
  13.2 1.3 %collective-permute-done.2 = bf16[1,272,128]{2,1,0:T(8,128)(2,1)S(1)} collective-permute-done((bf16[1,272,128]{2,1,0:T(8,128)(2,1)S(1)}, bf16[1,272,128]{2,1,0:T(8,128)(2,1)S(1)}, u32[]{:S(2)}, u32[]{:S(2)}) %collective-permute-start.2) | collective-permute-done | bytes 69664 | tf_op jit(solution)/shard_map/ppermute | solution.py:748
  14.6 0.0 copy-start
  14.6 1.6 %collective-permute-start.4 = (bf16[4,144,128]{2,1,0:T(8,128)(2,1)S(1)}, bf16[4,144,128]{2,1,0:T(8,128)(2,1)S(1)}, u32[]{:S(2)}, u32[]{:S(2)}) collective-permute-start(bf16[4,144,128]{2,1,0:T(8,128)(2,1)S(1)} %slice.17.near_ref), channel_id=1, source_target_pairs={{0,1},{1,0},{2,3},{3,2},{4,5},{5,4},{6,7},{7,6},{8,9},{9,8},{10,11... | collective-permute-start | bytes 442376 | tf_op jit(solution)/shard_map/ppermute | solution.py:748
  16.2 0.0 collective-permute-start.5
  16.2 3.6 %collective-permute-done.4.far_ref = bf16[4,144,128]{2,1,0:T(8,128)(2,1)S(1)} collective-permute-done((bf16[4,144,128]{2,1,0:T(8,128)(2,1)S(1)}, bf16[4,144,128]{2,1,0:T(8,128)(2,1)S(1)}, u32[]{:S(2)}, u32[]{:S(2)}) %collective-permute-start.4) | collective-permute-done | bytes 147488 | tf_op jit(solution)/shard_map/ppermute | solution.py:748
  19.8 0.0 collective-permute-start.6
  19.8 1.6 %collective-permute-start.3 = (bf16[4,128,128]{2,1,0:T(8,128)(2,1)S(1)}, bf16[4,128,128]{2,1,0:T(8,128)(2,1)S(1)}, u32[]{:S(2)}, u32[]{:S(2)}) collective-permute-start(bf16[4,128,128]{2,1,0:T(8,128)(2,1)S(1)} %slice.16.near_ref), channel_id=1, source_target_pairs={{0,1},{1,0},{2,3},{3,2},{4,5},{5,4},{6,7},{7,6},{8,9},{9,8},{10,11... | collective-permute-start | bytes 393224 | tf_op jit(solution)/shard_map/ppermute | solution.py:748
  21.4 0.5 %collective-permute-start.7 = (bf16[256,256]{1,0:T(8,128)(2,1)S(1)}, bf16[256,256]{1,0:T(8,128)(2,1)S(1)}, u32[]{:S(2)}, u32[]{:S(2)}) collective-permute-start(bf16[256,256]{1,0:T(8,128)(2,1)S(1)} %get-tuple-element.72.normed_ref), channel_id=1, source_target_pairs={{0,1},{1,0},{2,3},{3,2},{4,5},{5,4},{6,7},{7,6},{8,9},{9,8},{10,11... | collective-permute-start | bytes 393224 | tf_op jit(solution)/shard_map/ppermute | solution.py:748
  21.9 0.0 copy-done
  21.9 0.1 copy.19
  22.0 0.1 collective-permute-start.9
  22.1 0.0 collective-permute-done.5.other_near_ref
  22.1 0.0 collective-permute-done.6.other_far_ref
  22.1 2.4 %outer_products.1 = (bf16[512,1024]{1,0:T(8,128)(2,1)S(1)}, f32[512,128]{1,0:T(8,128)S(1)}, f32[512,128]{1,0:T(8,128)S(1)}, bf16[512,128]{1,0:T(8,128)(2,1)S(1)}, f32[32,128]{1,0:T(8,128)S(1)}) custom-call(s32[2]{0:T(128)S(1)} %pad_add_fusion.ids_ref, bf16[4,144,128]{2,1,0:T(8,128)(2,1)S(1)} %slice.17.near_ref, ...), custom_call_target="tpu_custom_call" | custom-call | tf_op jit(solution)/shard_map/outer_products/pallas_call | solution.py:842
  24.5 0.0 copy-start.1
  24.5 0.0 copy-start.2
  24.6 1.4 %turned.1 = (bf16[1024,128]{1,0:T(8,128)(2,1)S(1)}, bf16[1024,128]{1,0:T(8,128)(2,1)S(1)}) custom-call(s32[2]{0:T(128)S(1)} %pad_add_fusion.ids_ref, bf16[4,144,128]{2,1,0:T(8,128)(2,1)S(1)} %slice.17.near_ref, bf16[4,144,128]{2,1,0:T(8,128)(2,1)S(1)} %collective-permute-done.4.far_ref, bf16[4,144,128]{2,1,0:T(8,128)(2,1)S(1)} %collective-permute-done.5.other_near_ref, ...), custom_call_target="tpu_custom_call" | custom-call | tf_op jit(solution)/shard_map/turned/pallas_call | solution.py:865
  26.0 0.2 collective-permute-done.3.far_ref
  26.2 0.0 copy-done.1
  26.2 0.0 copy-done.2
  26.2 2.4 %transition.1 = (bf16[64,128]{1,0:T(8,128)(2,1)}, bf16[512,128]{1,0:T(8,128)(2,1)S(1)}, bf16[512,128]{1,0:T(8,128)(2,1)S(1)}, bf16[512,512]{1,0:T(8,128)(2,1)S(1...) custom-call(s32[2]{0:T(128)S(1)} %pad_add_fusion.ids_ref, bf16[4,128,128]{2,1,0:T(8,128)(2,1)S(1)} %slice.16.near_ref, ...), custom_call_target="tpu_custom_call" | custom-call | tf_op jit(solution)/shard_map/transition/pallas_call | solution.py:883
  28.6 0.0 collective-permute-done.7.far_normed_ref
  28.6 0.3 collective-permute-start.10
  28.9 0.2 collective-permute-start.8
  29.1 0.9 %weight_gradients.1.mine_ref = bf16[2048,128]{1,0:T(8,128)(2,1)S(1)} custom-call(bf16[512,1024]{1,0:T(8,128)(2,1)S(1)} %get-tuple-element.75.outer_ref, bf16[512,128]{1,0:T(8,128)(2,1)S(1)} %get-tuple-element.73.opm_ref, bf16[512,128]{1,0:T(8,128)(2,1)S(1)} %get-tuple-element.76.pn_ref, bf16[512,512]{1,0:T(8,128)(2,1)S(1)} %get-tuple-element.77.gh_ref, ...), custom_call_target="tpu_custom_call" | custom-call | tf_op jit(solution)/shard_map/weight_gradients/pallas_call | solution.py:913
  30.0 0.0 collective-permute-done.9.other_normed_ref
  30.1 0.0 collective-permute-done.10.other_far_normed_ref
  30.1 0.2 collective-permute-done.8.other_opm_ref
  30.2 2.0 %projector_parts.1 = (bf16[64,256]{1,0:T(8,128)(2,1)S(1)}, bf16[256,256]{1,0:T(8,128)(2,1)S(1)}) custom-call(s32[2]{0:T(128)S(1)} %pad_add_fusion.ids_ref, bf16[512,128]{1,0:T(8,128)(2,1)S(1)} %get-tuple-element.73.opm_ref, bf16[512,128]{1,0:T(8,128)(2,1)S(1)} %collective-permute-done.8.other_opm_ref, bf16[1024,128]{1,0:T(8,128)(2,1)S(1)} %get-tuple-element.81.rightt_ref, ...), custom_call_target="tpu_custom_call" | custom-call | tf_op jit(solution)/shard_map/projector_parts/pallas_call | solution.py:925
  32.3 2.0 %collective-permute-start.13 = (bf16[64,256]{1,0:T(8,128)(2,1)S(1)}, bf16[64,256]{1,0:T(8,128)(2,1)S(1)}, u32[]{:S(2)}, u32[]{:S(2)}) collective-permute-start(bf16[64,256]{1,0:T(8,128)(2,1)S(1)} %get-tuple-element.86), channel_id=1, source_target_pairs={{0,6},{1,7},{2,4},{3,5},{4,2},{5,3},{6,0},{7,1},{8,14},{9,15},{10,... | collective-permute-start | bytes 98312 | tf_op jit(solution)/shard_map/ppermute | solution.py:748
  34.3 3.8 %collective-permute-done.13 = bf16[64,256]{1,0:T(8,128)(2,1)S(1)} collective-permute-done((bf16[64,256]{1,0:T(8,128)(2,1)S(1)}, bf16[64,256]{1,0:T(8,128)(2,1)S(1)}, u32[]{:S(2)}, u32[]{:S(2)}) %collective-permute-start.13) | collective-permute-done | bytes 32800 | tf_op jit(solution)/shard_map/ppermute | solution.py:748
  38.1 0.0 collective-permute-start.14
  38.1 0.0 collective-permute-start.11
  38.1 2.5 %collective-permute-start.12 = (bf16[64,256]{1,0:T(8,128)(2,1)S(1)}, bf16[64,256]{1,0:T(8,128)(2,1)S(1)}, u32[]{:S(2)}, u32[]{:S(2)}) collective-permute-start(bf16[64,256]{1,0:T(8,128)(2,1)S(1)} %get-tuple-element.86), channel_id=1, source_target_pairs={{0,4},{1,5},{2,6},{3,7},{4,0},{5,1},{6,2},{7,3},{8,12},{9,13},{10,... | collective-permute-start | bytes 98312 | tf_op jit(solution)/shard_map/ppermute | solution.py:748
  40.6 0.3 features.1
  40.9 0.0 collective-permute-done.14.other_ref
  40.9 1.0 %sums_over_depth.1 = (f32[1024,128]{1,0:T(8,128)}, f32[128,512]{1,0:T(8,128)}, f32[512,128]{1,0:T(8,128)}) custom-call(bf16[2048,128]{1,0:T(8,128)(2,1)S(1)} %weight_gradients.1.mine_ref, bf16[2048,128]{1,0:T(8,128)(2,1)S(1)} %collective-permute-done.14.other_ref), custom_call_target="tpu_custom_call" | custom-call | tf_op jit(solution)/shard_map/sums_over_depth/pallas_call | solution.py:968
  41.9 0.1 collective-permute-done.11
  42.0 0.9 %collective-permute-done.12 = bf16[64,256]{1,0:T(8,128)(2,1)S(1)} collective-permute-done((bf16[64,256]{1,0:T(8,128)(2,1)S(1)}, bf16[64,256]{1,0:T(8,128)(2,1)S(1)}, u32[]{:S(2)}, u32[]{:S(2)}) %collective-permute-start.12) | collective-permute-done | bytes 32800 | tf_op jit(solution)/shard_map/ppermute | solution.py:748
  42.9 0.6 %slice_bitcast_fusion = (f32[256,32]{0,1:T(8,128)}, f32[256,32]{0,1:T(8,128)}) fusion(f32[64,256]{1,0:T(8,128)S(1)} %add_add_fusion), kind=kLoop, calls=%fused_computation.2 | loop fusion | bytes 131072 | tf_op jit(solution)/shard_map/transpose | solution.py:986
  43.5 0.7 %reshape.44 = bf16[64,4,256]{2,1,0:T(4,128)(2,1)} reshape(bf16[256,256]{1,0:T(8,128)(2,1)S(1)} %features.1) | data formatting | bytes 262144 | tf_op jit(solution)/shard_map/reshape | solution.py:983
  (4 shorter events, 0.1 us)
Async XLA Ops:
  2.6 5.7 %collective-permute-start = (bf16[1,272,128]{2,1,0:T(8,128)(2,1)S(1)}, bf16[1,272,128]{2,1,0:T(8,128)(2,1)S(1)}, u32[]{:S(2)}, u32[]{:S(2)}) collective-permute-start(bf16[1,272,128]{2,1,0:T(8,128)(2,1)S(1)} %get-tuple-element.57), channel_id=1, source_target_pairs={{0,2},{1,3},{2,0},{3,1},{4,6},{5,7},{6,4},{7,5},{8,10},{9,11},{10,... | collective-permute-start | bytes 208904 | tf_op jit(solution)/shard_map/ppermute | solution.py:748
  5.7 7.5 %collective-permute-start.1 = (bf16[1,272,128]{2,1,0:T(8,128)(2,1)S(1)}, bf16[1,272,128]{2,1,0:T(8,128)(2,1)S(1)}, u32[]{:S(2)}, u32[]{:S(2)}) collective-permute-start(bf16[1,272,128]{2,1,0:T(8,128)(2,1)S(1)} %get-tuple-element.57), channel_id=1, source_target_pairs={{0,4},{1,5},{2,6},{3,7},{4,0},{5,1},{6,2},{7,3},{8,12},{9,13},{10,... | collective-permute-start | bytes 208904 | tf_op jit(solution)/shard_map/ppermute | solution.py:748
  8.3 6.2 %collective-permute-start.2 = (bf16[1,272,128]{2,1,0:T(8,128)(2,1)S(1)}, bf16[1,272,128]{2,1,0:T(8,128)(2,1)S(1)}, u32[]{:S(2)}, u32[]{:S(2)}) collective-permute-start(bf16[1,272,128]{2,1,0:T(8,128)(2,1)S(1)} %get-tuple-element.57), channel_id=1, source_target_pairs={{0,6},{1,7},{2,4},{3,5},{4,2},{5,3},{6,0},{7,1},{8,14},{9,15},{10,... | collective-permute-start | bytes 208904 | tf_op jit(solution)/shard_map/ppermute | solution.py:748
  14.6 7.4 %copy-start = (bf16[1024,128]{1,0:T(8,128)(2,1)S(1)}, bf16[1024,128]{1,0:T(8,128)(2,1)}, u32[]{:S(2)}) copy-start(bf16[1024,128]{1,0:T(8,128)(2,1)} %wout_ref.1) | copy-start | bytes 786436
  14.6 5.2 %collective-permute-start.4 = (bf16[4,144,128]{2,1,0:T(8,128)(2,1)S(1)}, bf16[4,144,128]{2,1,0:T(8,128)(2,1)S(1)}, u32[]{:S(2)}, u32[]{:S(2)}) collective-permute-start(bf16[4,144,128]{2,1,0:T(8,128)(2,1)S(1)} %slice.17.near_ref), channel_id=1, source_target_pairs={{0,1},{1,0},{2,3},{3,2},{4,5},{5,4},{6,7},{7,6},{8,9},{9,8},{10,11... | collective-permute-start | bytes 442376 | tf_op jit(solution)/shard_map/ppermute | solution.py:748
  16.2 5.9 %collective-permute-start.5 = (bf16[4,144,128]{2,1,0:T(8,128)(2,1)S(1)}, bf16[4,144,128]{2,1,0:T(8,128)(2,1)S(1)}, u32[]{:S(2)}, u32[]{:S(2)}) collective-permute-start(bf16[4,144,128]{2,1,0:T(8,128)(2,1)S(1)} %slice.17.near_ref), channel_id=1, source_target_pairs={{0,8},{8,0},{1,9},{9,1},{2,10},{10,2},{3,11},{11,3},{4,12},{12,4},... | collective-permute-start | bytes 442376 | tf_op jit(solution)/shard_map/ppermute | solution.py:737
  19.8 2.3 %collective-permute-start.6 = (bf16[4,144,128]{2,1,0:T(8,128)(2,1)S(1)}, bf16[4,144,128]{2,1,0:T(8,128)(2,1)S(1)}, u32[]{:S(2)}, u32[]{:S(2)}) collective-permute-start(bf16[4,144,128]{2,1,0:T(8,128)(2,1)S(1)} %collective-permute-done.4.far_ref), channel_id=1, source_target_pairs={{0,8},{8,0},{1,9},{9,1},{2,10},{10,2},{3,11},{11,3},{4,12},{12,4},... | collective-permute-start | bytes 442376 | tf_op jit(solution)/shard_map/ppermute | solution.py:737
  19.8 6.4 %collective-permute-start.3 = (bf16[4,128,128]{2,1,0:T(8,128)(2,1)S(1)}, bf16[4,128,128]{2,1,0:T(8,128)(2,1)S(1)}, u32[]{:S(2)}, u32[]{:S(2)}) collective-permute-start(bf16[4,128,128]{2,1,0:T(8,128)(2,1)S(1)} %slice.16.near_ref), channel_id=1, source_target_pairs={{0,1},{1,0},{2,3},{3,2},{4,5},{5,4},{6,7},{7,6},{8,9},{9,8},{10,11... | collective-permute-start | bytes 393224 | tf_op jit(solution)/shard_map/ppermute | solution.py:748
  21.4 7.2 %collective-permute-start.7 = (bf16[256,256]{1,0:T(8,128)(2,1)S(1)}, bf16[256,256]{1,0:T(8,128)(2,1)S(1)}, u32[]{:S(2)}, u32[]{:S(2)}) collective-permute-start(bf16[256,256]{1,0:T(8,128)(2,1)S(1)} %get-tuple-element.72.normed_ref), channel_id=1, source_target_pairs={{0,1},{1,0},{2,3},{3,2},{4,5},{5,4},{6,7},{7,6},{8,9},{9,8},{10,11... | collective-permute-start | bytes 393224 | tf_op jit(solution)/shard_map/ppermute | solution.py:748
  22.0 8.0 %collective-permute-start.9 = (bf16[256,256]{1,0:T(8,128)(2,1)S(1)}, bf16[256,256]{1,0:T(8,128)(2,1)S(1)}, u32[]{:S(2)}, u32[]{:S(2)}) collective-permute-start(bf16[256,256]{1,0:T(8,128)(2,1)S(1)} %get-tuple-element.72.normed_ref), channel_id=1, source_target_pairs={{0,8},{8,0},{1,9},{9,1},{2,10},{10,2},{3,11},{11,3},{4,12},{12,4},... | collective-permute-start | bytes 393224 | tf_op jit(solution)/shard_map/ppermute | solution.py:737
  24.5 1.6 %copy-start.1 = (bf16[128,512]{1,0:T(8,128)(2,1)S(1)}, bf16[128,512]{1,0:T(8,128)(2,1)}, u32[]{:S(2)}) copy-start(bf16[128,512]{1,0:T(8,128)(2,1)} %hid_ref.1) | copy-start | bytes 393220
  24.5 1.6 %copy-start.2 = (bf16[512,128]{1,0:T(8,128)(2,1)S(1)}, bf16[512,128]{1,0:T(8,128)(2,1)}, u32[]{:S(2)}) copy-start(bf16[512,128]{1,0:T(8,128)(2,1)} %back_ref.1) | copy-start | bytes 393220
  28.6 1.4 %collective-permute-start.10 = (bf16[256,256]{1,0:T(8,128)(2,1)S(1)}, bf16[256,256]{1,0:T(8,128)(2,1)S(1)}, u32[]{:S(2)}, u32[]{:S(2)}) collective-permute-start(bf16[256,256]{1,0:T(8,128)(2,1)S(1)} %collective-permute-done.7.far_normed_ref), channel_id=1, source_target_pairs={{0,8},{8,0},{1,9},{9,1},{2,10},{10,2},{3,11},{11,3},{4,12},{12,4},... | collective-permute-start | bytes 393224 | tf_op jit(solution)/shard_map/ppermute | solution.py:737
  28.9 1.3 %collective-permute-start.8 = (bf16[512,128]{1,0:T(8,128)(2,1)S(1)}, bf16[512,128]{1,0:T(8,128)(2,1)S(1)}, u32[]{:S(2)}, u32[]{:S(2)}) collective-permute-start(bf16[512,128]{1,0:T(8,128)(2,1)S(1)} %get-tuple-element.73.opm_ref), channel_id=1, source_target_pairs={{0,8},{8,0},{1,9},{9,1},{2,10},{10,2},{3,11},{11,3},{4,12},{12,4},... | collective-permute-start | bytes 393224 | tf_op jit(solution)/shard_map/ppermute | solution.py:737
  32.3 5.8 %collective-permute-start.13 = (bf16[64,256]{1,0:T(8,128)(2,1)S(1)}, bf16[64,256]{1,0:T(8,128)(2,1)S(1)}, u32[]{:S(2)}, u32[]{:S(2)}) collective-permute-start(bf16[64,256]{1,0:T(8,128)(2,1)S(1)} %get-tuple-element.86), channel_id=1, source_target_pairs={{0,6},{1,7},{2,4},{3,5},{4,2},{5,3},{6,0},{7,1},{8,14},{9,15},{10,... | collective-permute-start | bytes 98312 | tf_op jit(solution)/shard_map/ppermute | solution.py:748
  38.1 2.8 %collective-permute-start.14 = (bf16[2048,128]{1,0:T(8,128)(2,1)S(1)}, bf16[2048,128]{1,0:T(8,128)(2,1)S(1)}, u32[]{:S(2)}, u32[]{:S(2)}) collective-permute-start(bf16[2048,128]{1,0:T(8,128)(2,1)S(1)} %weight_gradients.1.mine_ref), channel_id=1, source_target_pairs={{0,8},{8,0},{1,9},{9,1},{2,10},{10,2},{3,11},{11,3},{4,12},{12,4},... | collective-permute-start | bytes 1572872 | tf_op jit(solution)/shard_map/ppermute | solution.py:737
  38.1 3.9 %collective-permute-start.11 = (bf16[64,256]{1,0:T(8,128)(2,1)S(1)}, bf16[64,256]{1,0:T(8,128)(2,1)S(1)}, u32[]{:S(2)}, u32[]{:S(2)}) collective-permute-start(bf16[64,256]{1,0:T(8,128)(2,1)S(1)} %get-tuple-element.86), channel_id=1, source_target_pairs={{0,2},{1,3},{2,0},{3,1},{4,6},{5,7},{6,4},{7,5},{8,10},{9,11},{10,... | collective-permute-start | bytes 98312 | tf_op jit(solution)/shard_map/ppermute | solution.py:748
  38.1 4.8 %collective-permute-start.12 = (bf16[64,256]{1,0:T(8,128)(2,1)S(1)}, bf16[64,256]{1,0:T(8,128)(2,1)S(1)}, u32[]{:S(2)}, u32[]{:S(2)}) collective-permute-start(bf16[64,256]{1,0:T(8,128)(2,1)S(1)} %get-tuple-element.86), channel_id=1, source_target_pairs={{0,4},{1,5},{2,6},{3,7},{4,0},{5,1},{6,2},{7,3},{8,12},{9,13},{10,... | collective-permute-start | bytes 98312 | tf_op jit(solution)/shard_map/ppermute | solution.py:748

commit v7 on v6

--- a/solution.py
+++ b/solution.py
@@ -245,7 +245,7 @@
 
 FEW_RESIDUES = 32
 MASK_ROWS = 16
-Z_PARTNERS = (2, 4, 6)
+Z_PARTNERS = (6, 4, 2)
 Y_PARTNER = 1
 
 
@@ -444,25 +444,22 @@
     cnt_ref[...] = jnp.dot(cntl_ref[...], ones, preferred_element_type=f32)
     pm_ref[...] = jnp.dot(pml_ref[...], ones, preferred_element_type=f32).astype(bf16)
 
-    for k2 in range(cols // 2):
+    for dh in range(width // 4):
         prod = jnp.dot(
-            mine_ref[...],
-            leftn_ref[:, 2 * k2 * lanes : 2 * (k2 + 1) * lanes],
+            mine_ref[dh * 4 * pair_cols : (dh + 1) * 4 * pair_cols, :],
+            leftn_ref[...],
             preferred_element_type=f32,
         )
-        for dh in range(width // 4):
-            for b in range(2):
-                piece = prod[
-                    dh * 4 * pair_cols : (dh + 1) * 4 * pair_cols, b * lanes : (b + 1) * lanes
-                ]
-                turned = butterfly(
-                    [piece[a * pair_cols : (a + 1) * pair_cols] for a in range(4)], width
-                )
-                for il in range(res):
-                    first = ((2 * k2 + b) * res + il) * pair_cols
-                    outer_ref[first : first + pair_cols, dh * lanes : (dh + 1) * lanes] = turned[
-                        il
-                    ].astype(bf16)
+        for k in range(cols):
+            piece = prod[:, k * lanes : (k + 1) * lanes]
+            turned = butterfly(
+                [piece[a * pair_cols : (a + 1) * pair_cols] for a in range(4)], width
+            )
+            for il in range(res):
+                first = (k * res + il) * pair_cols
+                outer_ref[first : first + pair_cols, dh * lanes : (dh + 1) * lanes] = turned[
+                    il
+                ].astype(bf16)
     proj_out_ref[...] = jnp.dot(outer_ref[...], wturn_ref[...], preferred_element_type=f32)
 
 
@@ -963,8 +960,8 @@
         compiler_params=params,
         name="features",
     )(spread, first, second, scale, scaled, inv)
+    part, weights = lax.optimization_barrier((part, weights))
     came = [swap_col(part, partner) for partner in Z_PARTNERS]
-    came[2], weights = lax.optimization_barrier((came[2], weights))
     dout, dhid, dback = pl.pallas_call(
         weights_sum_kernel,
         out_shape=(

time: 44.5 us -> 40.8 us (0.917)
  waiting for transfers between devices: 15 us -> 11.3 us
    ppermute x9, waiting for transfers between devices: 14.8 us -> 11.2 us  [swap_col(): lax.ppermute(block, 'col', [(at, at ^ partner) for at in range(count)])]
  transfers between devices with their start and end apart: 15 -> 15, of which waited for: 8 -> 6; matrix products, arithmetic and copies ran while one was open for 0% -> 0% of each run, Pallas kernels for 19% -> 20%
where the time goes in v7:
time: 40.8 us; the launch traced here: 40.6 us
  starting transfers between devices  14.8 us (36%)
  Pallas kernels  12.1 us (30%)
  waiting for transfers between devices  11.3 us (28%)
  local copies, waits for them, and re-layouts  1.47 us (4%)
  between operations  0.78 us (2%)
    ppermute x9, starting transfers between devices, swap_col(): lax.ppermute(block, 'col', [(at, at ^ partner) for at in range(count)])  13.8 us
    ppermute x9, waiting for transfers between devices, swap_col(): lax.ppermute(block, 'col', [(at, at ^ partner) for at in range(count)])  11.2 us
    pallas_call x1, Pallas kernels, whole_plan(): pl.pallas_call(functools.partial(transition_kernel, sizes, orders), out_s...  2.41 us
    pallas_call x1, Pallas kernels, whole_plan(): pl.pallas_call(functools.partial(outer_kernel, sizes, orders), out_shape=...  2.11 us
    pallas_call x1, Pallas kernels, whole_plan(): pl.pallas_call(functools.partial(projector_kernel, sizes), out_shape=(sha...  2.03 us
    pallas_call x1, Pallas kernels, whole_plan(): pl.pallas_call(pre_kernel, out_shape=(shape((1, rows + 2 * per, pair_widt...  1.91 us
    pallas_call x1, Pallas kernels, whole_plan(): pl.pallas_call(functools.partial(turn_kernel, sizes, orders), out_shape=(...  1.39 us
    pallas_call x1, Pallas kernels, whole_plan(): pl.pallas_call(weights_sum_kernel, out_shape=(shape((outer_width, pair_wi...  1.02 us
  transfers between devices with their start and end apart: 15, of which 6 were waited for; matrix products, arithmetic and copies ran while one was open for 0% of the time, Pallas kernels for 20%

profile of v7, /device:TPU:0, one launch (start us, length us, event | category | flops | bytes accessed | tf_op | source)
XLA Modules:
  0.0 40.6 jit_solution(11138443694563777229)
XLA Ops:
  0.6 0.1 pad_add_fusion.ids_ref
  0.7 1.9 %project.1 = (bf16[1,272,128]{2,1,0:T(8,128)(2,1)S(1)}, f32[1,256]{1,0:T(1,128)S(1)}, bf16[32,256]{1,0:T(8,128)(2,1)S(1)}, bf16[32,256]{1,0:T(8,128)(2,1)S(1)}, ...) custom-call(s32[2]{0:T(128)S(1)} %pad_add_fusion.ids_ref, ...), custom_call_target="tpu_custom_call" | custom-call | tf_op jit(solution)/shard_map/project/pallas_call | solution.py:785
  2.6 5.1 %collective-permute-start = (bf16[1,272,128]{2,1,0:T(8,128)(2,1)S(1)}, bf16[1,272,128]{2,1,0:T(8,128)(2,1)S(1)}, u32[]{:S(2)}, u32[]{:S(2)}) collective-permute-start(bf16[1,272,128]{2,1,0:T(8,128)(2,1)S(1)} %get-tuple-element.57), channel_id=1, source_target_pairs={{0,6},{1,7},{2,4},{3,5},{4,2},{5,3},{6,0},{7,1},{8,14},{9,15},{10,... | collective-permute-start | bytes 208904 | tf_op jit(solution)/shard_map/ppermute | solution.py:745
  7.7 0.0 collective-permute-start.1
  7.8 0.6 %collective-permute-start.2 = (bf16[1,272,128]{2,1,0:T(8,128)(2,1)S(1)}, bf16[1,272,128]{2,1,0:T(8,128)(2,1)S(1)}, u32[]{:S(2)}, u32[]{:S(2)}) collective-permute-start(bf16[1,272,128]{2,1,0:T(8,128)(2,1)S(1)} %get-tuple-element.57), channel_id=1, source_target_pairs={{0,2},{1,3},{2,0},{3,1},{4,6},{5,7},{6,4},{7,5},{8,10},{9,11},{10,... | collective-permute-start | bytes 208904 | tf_op jit(solution)/shard_map/ppermute | solution.py:745
  8.4 2.0 %collective-permute-done = bf16[1,272,128]{2,1,0:T(8,128)(2,1)S(1)} collective-permute-done((bf16[1,272,128]{2,1,0:T(8,128)(2,1)S(1)}, bf16[1,272,128]{2,1,0:T(8,128)(2,1)S(1)}, u32[]{:S(2)}, u32[]{:S(2)}) %collective-permute-start) | collective-permute-done | bytes 69664 | tf_op jit(solution)/shard_map/ppermute | solution.py:745
  10.4 3.2 %collective-permute-done.1 = bf16[1,272,128]{2,1,0:T(8,128)(2,1)S(1)} collective-permute-done((bf16[1,272,128]{2,1,0:T(8,128)(2,1)S(1)}, bf16[1,272,128]{2,1,0:T(8,128)(2,1)S(1)}, u32[]{:S(2)}, u32[]{:S(2)}) %collective-permute-start.1) | collective-permute-done | bytes 69664 | tf_op jit(solution)/shard_map/ppermute | solution.py:745
  13.7 0.0 collective-permute-done.2
  13.7 0.0 copy-start
  13.7 1.6 %collective-permute-start.4 = (bf16[4,144,128]{2,1,0:T(8,128)(2,1)S(1)}, bf16[4,144,128]{2,1,0:T(8,128)(2,1)S(1)}, u32[]{:S(2)}, u32[]{:S(2)}) collective-permute-start(bf16[4,144,128]{2,1,0:T(8,128)(2,1)S(1)} %slice.17.near_ref), channel_id=1, source_target_pairs={{0,1},{1,0},{2,3},{3,2},{4,5},{5,4},{6,7},{7,6},{8,9},{9,8},{10,11... | collective-permute-start | bytes 442376 | tf_op jit(solution)/shard_map/ppermute | solution.py:745
  15.3 0.0 collective-permute-start.5
  15.3 3.8 %collective-permute-done.4.far_ref = bf16[4,144,128]{2,1,0:T(8,128)(2,1)S(1)} collective-permute-done((bf16[4,144,128]{2,1,0:T(8,128)(2,1)S(1)}, bf16[4,144,128]{2,1,0:T(8,128)(2,1)S(1)}, u32[]{:S(2)}, u32[]{:S(2)}) %collective-permute-start.4) | collective-permute-done | bytes 147488 | tf_op jit(solution)/shard_map/ppermute | solution.py:745
  19.1 0.0 collective-permute-start.6
  19.2 1.8 %collective-permute-start.3 = (bf16[4,128,128]{2,1,0:T(8,128)(2,1)S(1)}, bf16[4,128,128]{2,1,0:T(8,128)(2,1)S(1)}, u32[]{:S(2)}, u32[]{:S(2)}) collective-permute-start(bf16[4,128,128]{2,1,0:T(8,128)(2,1)S(1)} %slice.16.near_ref), channel_id=1, source_target_pairs={{0,1},{1,0},{2,3},{3,2},{4,5},{5,4},{6,7},{7,6},{8,9},{9,8},{10,11... | collective-permute-start | bytes 393224 | tf_op jit(solution)/shard_map/ppermute | solution.py:745
  21.0 0.3 collective-permute-start.7
  21.3 0.0 copy-done
  21.3 0.1 copy.19
  21.4 0.1 collective-permute-start.9
  21.4 0.0 collective-permute-done.5.other_near_ref
  21.4 0.0 collective-permute-done.6.other_far_ref
  21.5 2.1 %outer_products.1 = (bf16[512,1024]{1,0:T(8,128)(2,1)S(1)}, f32[512,128]{1,0:T(8,128)S(1)}, f32[512,128]{1,0:T(8,128)S(1)}, bf16[512,128]{1,0:T(8,128)(2,1)S(1)}, f32[32,128]{1,0:T(8,128)S(1)}) custom-call(s32[2]{0:T(128)S(1)} %pad_add_fusion.ids_ref, bf16[4,144,128]{2,1,0:T(8,128)(2,1)S(1)} %slice.17.near_ref, ...), custom_call_target="tpu_custom_call" | custom-call | tf_op jit(solution)/shard_map/outer_products/pallas_call | solution.py:839
  23.6 0.0 copy-start.1
  23.6 0.0 copy-start.2
  23.6 1.4 %turned.1 = (bf16[1024,128]{1,0:T(8,128)(2,1)S(1)}, bf16[1024,128]{1,0:T(8,128)(2,1)S(1)}) custom-call(s32[2]{0:T(128)S(1)} %pad_add_fusion.ids_ref, bf16[4,144,128]{2,1,0:T(8,128)(2,1)S(1)} %slice.17.near_ref, bf16[4,144,128]{2,1,0:T(8,128)(2,1)S(1)} %collective-permute-done.4.far_ref, bf16[4,144,128]{2,1,0:T(8,128)(2,1)S(1)} %collective-permute-done.5.other_near_ref, ...), custom_call_target="tpu_custom_call" | custom-call | tf_op jit(solution)/shard_map/turned/pallas_call | solution.py:862
  25.0 0.5 %collective-permute-done.3.far_ref = bf16[4,128,128]{2,1,0:T(8,128)(2,1)S(1)} collective-permute-done((bf16[4,128,128]{2,1,0:T(8,128)(2,1)S(1)}, bf16[4,128,128]{2,1,0:T(8,128)(2,1)S(1)}, u32[]{:S(2)}, u32[]{:S(2)}) %collective-permute-start.3) | collective-permute-done | bytes 131104 | tf_op jit(solution)/shard_map/ppermute | solution.py:745
  25.5 0.0 copy-done.1
  25.5 0.0 copy-done.2
  25.5 2.4 %transition.1 = (bf16[64,128]{1,0:T(8,128)(2,1)}, bf16[512,128]{1,0:T(8,128)(2,1)S(1)}, bf16[512,128]{1,0:T(8,128)(2,1)S(1)}, bf16[512,512]{1,0:T(8,128)(2,1)S(1...) custom-call(s32[2]{0:T(128)S(1)} %pad_add_fusion.ids_ref, bf16[4,128,128]{2,1,0:T(8,128)(2,1)S(1)} %slice.16.near_ref, ...), custom_call_target="tpu_custom_call" | custom-call | tf_op jit(solution)/shard_map/transition/pallas_call | solution.py:880
  27.9 0.0 collective-permute-done.7.far_normed_ref
  27.9 0.0 collective-permute-start.10
  27.9 0.5 %collective-permute-start.8 = (bf16[512,128]{1,0:T(8,128)(2,1)S(1)}, bf16[512,128]{1,0:T(8,128)(2,1)S(1)}, u32[]{:S(2)}, u32[]{:S(2)}) collective-permute-start(bf16[512,128]{1,0:T(8,128)(2,1)S(1)} %get-tuple-element.73.opm_ref), channel_id=1, source_target_pairs={{0,8},{8,0},{1,9},{9,1},{2,10},{10,2},{3,11},{11,3},{4,12},{12,4},... | collective-permute-start | bytes 393224 | tf_op jit(solution)/shard_map/ppermute | solution.py:734
  28.5 0.9 %weight_gradients.1.mine_ref = bf16[2048,128]{1,0:T(8,128)(2,1)S(1)} custom-call(bf16[512,1024]{1,0:T(8,128)(2,1)S(1)} %get-tuple-element.75.outer_ref, bf16[512,128]{1,0:T(8,128)(2,1)S(1)} %get-tuple-element.73.opm_ref, bf16[512,128]{1,0:T(8,128)(2,1)S(1)} %get-tuple-element.76.pn_ref, bf16[512,512]{1,0:T(8,128)(2,1)S(1)} %get-tuple-element.77.gh_ref, ...), custom_call_target="tpu_custom_call" | custom-call | tf_op jit(solution)/shard_map/weight_gradients/pallas_call | solution.py:910
  29.4 0.0 collective-permute-done.9.other_normed_ref
  29.4 0.0 collective-permute-done.10.other_far_normed_ref
  29.4 0.1 collective-permute-done.8.other_opm_ref
  29.5 2.0 %projector_parts.1 = (bf16[64,256]{1,0:T(8,128)(2,1)S(1)}, bf16[256,256]{1,0:T(8,128)(2,1)S(1)}) custom-call(s32[2]{0:T(128)S(1)} %pad_add_fusion.ids_ref, bf16[512,128]{1,0:T(8,128)(2,1)S(1)} %get-tuple-element.73.opm_ref, bf16[512,128]{1,0:T(8,128)(2,1)S(1)} %collective-permute-done.8.other_opm_ref, bf16[1024,128]{1,0:T(8,128)(2,1)S(1)} %get-tuple-element.81.rightt_ref, ...), custom_call_target="tpu_custom_call" | custom-call | tf_op jit(solution)/shard_map/projector_parts/pallas_call | solution.py:922
  31.5 0.4 collective-permute-start.14
  31.9 2.5 %collective-permute-start.11 = (bf16[64,256]{1,0:T(8,128)(2,1)S(1)}, bf16[64,256]{1,0:T(8,128)(2,1)S(1)}, u32[]{:S(2)}, u32[]{:S(2)}) collective-permute-start(bf16[64,256]{1,0:T(8,128)(2,1)S(1)} %get-tuple-element.88), channel_id=1, source_target_pairs={{0,6},{1,7},{2,4},{3,5},{4,2},{5,3},{6,0},{7,1},{8,14},{9,15},{10,... | collective-permute-start | bytes 98312 | tf_op jit(solution)/shard_map/ppermute | solution.py:745
  34.4 0.0 collective-permute-start.12
  34.4 1.9 %collective-permute-start.13 = (bf16[64,256]{1,0:T(8,128)(2,1)S(1)}, bf16[64,256]{1,0:T(8,128)(2,1)S(1)}, u32[]{:S(2)}, u32[]{:S(2)}) collective-permute-start(bf16[64,256]{1,0:T(8,128)(2,1)S(1)} %get-tuple-element.88), channel_id=1, source_target_pairs={{0,2},{1,3},{2,0},{3,1},{4,6},{5,7},{6,4},{7,5},{8,10},{9,11},{10,... | collective-permute-start | bytes 98312 | tf_op jit(solution)/shard_map/ppermute | solution.py:745
  36.3 0.3 features.1
  36.6 0.0 collective-permute-done.14.other_ref
  36.6 1.0 %sums_over_depth.1 = (f32[1024,128]{1,0:T(8,128)}, f32[128,512]{1,0:T(8,128)}, f32[512,128]{1,0:T(8,128)}) custom-call(bf16[2048,128]{1,0:T(8,128)(2,1)S(1)} %weight_gradients.1.mine_ref, bf16[2048,128]{1,0:T(8,128)(2,1)S(1)} %collective-permute-done.14.other_ref), custom_call_target="tpu_custom_call" | custom-call | tf_op jit(solution)/shard_map/sums_over_depth/pallas_call | solution.py:965
  37.6 0.0 collective-permute-done.11
  37.6 1.6 %collective-permute-done.12 = bf16[64,256]{1,0:T(8,128)(2,1)S(1)} collective-permute-done((bf16[64,256]{1,0:T(8,128)(2,1)S(1)}, bf16[64,256]{1,0:T(8,128)(2,1)S(1)}, u32[]{:S(2)}, u32[]{:S(2)}) %collective-permute-start.12) | collective-permute-done | bytes 32800 | tf_op jit(solution)/shard_map/ppermute | solution.py:745
  39.2 0.0 collective-permute-done.13
  39.3 0.6 %slice_bitcast_fusion = (f32[256,32]{0,1:T(8,128)}, f32[256,32]{0,1:T(8,128)}) fusion(f32[64,256]{1,0:T(8,128)S(1)} %add_add_fusion), kind=kLoop, calls=%fused_computation.2 | loop fusion | bytes 131072 | tf_op jit(solution)/shard_map/transpose | solution.py:983
  39.9 0.7 %reshape.44 = bf16[64,4,256]{2,1,0:T(4,128)(2,1)} reshape(bf16[256,256]{1,0:T(8,128)(2,1)S(1)} %features.1) | data formatting | bytes 262144 | tf_op jit(solution)/shard_map/reshape | solution.py:980
  (4 shorter events, 0.1 us)
Async XLA Ops:
  2.6 7.8 %collective-permute-start = (bf16[1,272,128]{2,1,0:T(8,128)(2,1)S(1)}, bf16[1,272,128]{2,1,0:T(8,128)(2,1)S(1)}, u32[]{:S(2)}, u32[]{:S(2)}) collective-permute-start(bf16[1,272,128]{2,1,0:T(8,128)(2,1)S(1)} %get-tuple-element.57), channel_id=1, source_target_pairs={{0,6},{1,7},{2,4},{3,5},{4,2},{5,3},{6,0},{7,1},{8,14},{9,15},{10,... | collective-permute-start | bytes 208904 | tf_op jit(solution)/shard_map/ppermute | solution.py:745
  7.7 5.9 %collective-permute-start.1 = (bf16[1,272,128]{2,1,0:T(8,128)(2,1)S(1)}, bf16[1,272,128]{2,1,0:T(8,128)(2,1)S(1)}, u32[]{:S(2)}, u32[]{:S(2)}) collective-permute-start(bf16[1,272,128]{2,1,0:T(8,128)(2,1)S(1)} %get-tuple-element.57), channel_id=1, source_target_pairs={{0,4},{1,5},{2,6},{3,7},{4,0},{5,1},{6,2},{7,3},{8,12},{9,13},{10,... | collective-permute-start | bytes 208904 | tf_op jit(solution)/shard_map/ppermute | solution.py:745
  7.8 5.9 %collective-permute-start.2 = (bf16[1,272,128]{2,1,0:T(8,128)(2,1)S(1)}, bf16[1,272,128]{2,1,0:T(8,128)(2,1)S(1)}, u32[]{:S(2)}, u32[]{:S(2)}) collective-permute-start(bf16[1,272,128]{2,1,0:T(8,128)(2,1)S(1)} %get-tuple-element.57), channel_id=1, source_target_pairs={{0,2},{1,3},{2,0},{3,1},{4,6},{5,7},{6,4},{7,5},{8,10},{9,11},{10,... | collective-permute-start | bytes 208904 | tf_op jit(solution)/shard_map/ppermute | solution.py:745
  13.7 7.5 %copy-start = (bf16[1024,128]{1,0:T(8,128)(2,1)S(1)}, bf16[1024,128]{1,0:T(8,128)(2,1)}, u32[]{:S(2)}) copy-start(bf16[1024,128]{1,0:T(8,128)(2,1)} %wout_ref.1) | copy-start | bytes 786436
  13.7 5.4 %collective-permute-start.4 = (bf16[4,144,128]{2,1,0:T(8,128)(2,1)S(1)}, bf16[4,144,128]{2,1,0:T(8,128)(2,1)S(1)}, u32[]{:S(2)}, u32[]{:S(2)}) collective-permute-start(bf16[4,144,128]{2,1,0:T(8,128)(2,1)S(1)} %slice.17.near_ref), channel_id=1, source_target_pairs={{0,1},{1,0},{2,3},{3,2},{4,5},{5,4},{6,7},{7,6},{8,9},{9,8},{10,11... | collective-permute-start | bytes 442376 | tf_op jit(solution)/shard_map/ppermute | solution.py:745
  15.3 6.1 %collective-permute-start.5 = (bf16[4,144,128]{2,1,0:T(8,128)(2,1)S(1)}, bf16[4,144,128]{2,1,0:T(8,128)(2,1)S(1)}, u32[]{:S(2)}, u32[]{:S(2)}) collective-permute-start(bf16[4,144,128]{2,1,0:T(8,128)(2,1)S(1)} %slice.17.near_ref), channel_id=1, source_target_pairs={{0,8},{8,0},{1,9},{9,1},{2,10},{10,2},{3,11},{11,3},{4,12},{12,4},... | collective-permute-start | bytes 442376 | tf_op jit(solution)/shard_map/ppermute | solution.py:734
  19.1 2.3 %collective-permute-start.6 = (bf16[4,144,128]{2,1,0:T(8,128)(2,1)S(1)}, bf16[4,144,128]{2,1,0:T(8,128)(2,1)S(1)}, u32[]{:S(2)}, u32[]{:S(2)}) collective-permute-start(bf16[4,144,128]{2,1,0:T(8,128)(2,1)S(1)} %collective-permute-done.4.far_ref), channel_id=1, source_target_pairs={{0,8},{8,0},{1,9},{9,1},{2,10},{10,2},{3,11},{11,3},{4,12},{12,4},... | collective-permute-start | bytes 442376 | tf_op jit(solution)/shard_map/ppermute | solution.py:734
  19.2 6.4 %collective-permute-start.3 = (bf16[4,128,128]{2,1,0:T(8,128)(2,1)S(1)}, bf16[4,128,128]{2,1,0:T(8,128)(2,1)S(1)}, u32[]{:S(2)}, u32[]{:S(2)}) collective-permute-start(bf16[4,128,128]{2,1,0:T(8,128)(2,1)S(1)} %slice.16.near_ref), channel_id=1, source_target_pairs={{0,1},{1,0},{2,3},{3,2},{4,5},{5,4},{6,7},{7,6},{8,9},{9,8},{10,11... | collective-permute-start | bytes 393224 | tf_op jit(solution)/shard_map/ppermute | solution.py:745
  21.0 7.0 %collective-permute-start.7 = (bf16[256,256]{1,0:T(8,128)(2,1)S(1)}, bf16[256,256]{1,0:T(8,128)(2,1)S(1)}, u32[]{:S(2)}, u32[]{:S(2)}) collective-permute-start(bf16[256,256]{1,0:T(8,128)(2,1)S(1)} %get-tuple-element.72.normed_ref), channel_id=1, source_target_pairs={{0,1},{1,0},{2,3},{3,2},{4,5},{5,4},{6,7},{7,6},{8,9},{9,8},{10,11... | collective-permute-start | bytes 393224 | tf_op jit(solution)/shard_map/ppermute | solution.py:745
  21.4 8.0 %collective-permute-start.9 = (bf16[256,256]{1,0:T(8,128)(2,1)S(1)}, bf16[256,256]{1,0:T(8,128)(2,1)S(1)}, u32[]{:S(2)}, u32[]{:S(2)}) collective-permute-start(bf16[256,256]{1,0:T(8,128)(2,1)S(1)} %get-tuple-element.72.normed_ref), channel_id=1, source_target_pairs={{0,8},{8,0},{1,9},{9,1},{2,10},{10,2},{3,11},{11,3},{4,12},{12,4},... | collective-permute-start | bytes 393224 | tf_op jit(solution)/shard_map/ppermute | solution.py:734
  23.6 1.9 %copy-start.1 = (bf16[128,512]{1,0:T(8,128)(2,1)S(1)}, bf16[128,512]{1,0:T(8,128)(2,1)}, u32[]{:S(2)}) copy-start(bf16[128,512]{1,0:T(8,128)(2,1)} %hid_ref.1) | copy-start | bytes 393220
  23.6 1.9 %copy-start.2 = (bf16[512,128]{1,0:T(8,128)(2,1)S(1)}, bf16[512,128]{1,0:T(8,128)(2,1)}, u32[]{:S(2)}) copy-start(bf16[512,128]{1,0:T(8,128)(2,1)} %back_ref.1) | copy-start | bytes 393220
  27.9 1.4 %collective-permute-start.10 = (bf16[256,256]{1,0:T(8,128)(2,1)S(1)}, bf16[256,256]{1,0:T(8,128)(2,1)S(1)}, u32[]{:S(2)}, u32[]{:S(2)}) collective-permute-start(bf16[256,256]{1,0:T(8,128)(2,1)S(1)} %collective-permute-done.7.far_normed_ref), channel_id=1, source_target_pairs={{0,8},{8,0},{1,9},{9,1},{2,10},{10,2},{3,11},{11,3},{4,12},{12,4},... | collective-permute-start | bytes 393224 | tf_op jit(solution)/shard_map/ppermute | solution.py:734
  27.9 1.5 %collective-permute-start.8 = (bf16[512,128]{1,0:T(8,128)(2,1)S(1)}, bf16[512,128]{1,0:T(8,128)(2,1)S(1)}, u32[]{:S(2)}, u32[]{:S(2)}) collective-permute-start(bf16[512,128]{1,0:T(8,128)(2,1)S(1)} %get-tuple-element.73.opm_ref), channel_id=1, source_target_pairs={{0,8},{8,0},{1,9},{9,1},{2,10},{10,2},{3,11},{11,3},{4,12},{12,4},... | collective-permute-start | bytes 393224 | tf_op jit(solution)/shard_map/ppermute | solution.py:734
  31.5 5.1 %collective-permute-start.14 = (bf16[2048,128]{1,0:T(8,128)(2,1)S(1)}, bf16[2048,128]{1,0:T(8,128)(2,1)S(1)}, u32[]{:S(2)}, u32[]{:S(2)}) collective-permute-start(bf16[2048,128]{1,0:T(8,128)(2,1)S(1)} %weight_gradients.1.mine_ref), channel_id=1, source_target_pairs={{0,8},{8,0},{1,9},{9,1},{2,10},{10,2},{3,11},{11,3},{4,12},{12,4},... | collective-permute-start | bytes 1572872 | tf_op jit(solution)/shard_map/ppermute | solution.py:734
  31.9 5.7 %collective-permute-start.11 = (bf16[64,256]{1,0:T(8,128)(2,1)S(1)}, bf16[64,256]{1,0:T(8,128)(2,1)S(1)}, u32[]{:S(2)}, u32[]{:S(2)}) collective-permute-start(bf16[64,256]{1,0:T(8,128)(2,1)S(1)} %get-tuple-element.88), channel_id=1, source_target_pairs={{0,6},{1,7},{2,4},{3,5},{4,2},{5,3},{6,0},{7,1},{8,14},{9,15},{10,... | collective-permute-start | bytes 98312 | tf_op jit(solution)/shard_map/ppermute | solution.py:745
  34.4 4.8 %collective-permute-start.12 = (bf16[64,256]{1,0:T(8,128)(2,1)S(1)}, bf16[64,256]{1,0:T(8,128)(2,1)S(1)}, u32[]{:S(2)}, u32[]{:S(2)}) collective-permute-start(bf16[64,256]{1,0:T(8,128)(2,1)S(1)} %get-tuple-element.88), channel_id=1, source_target_pairs={{0,4},{1,5},{2,6},{3,7},{4,0},{5,1},{6,2},{7,3},{8,12},{9,13},{10,... | collective-permute-start | bytes 98312 | tf_op jit(solution)/shard_map/ppermute | solution.py:745
  34.4 4.8 %collective-permute-start.13 = (bf16[64,256]{1,0:T(8,128)(2,1)S(1)}, bf16[64,256]{1,0:T(8,128)(2,1)S(1)}, u32[]{:S(2)}, u32[]{:S(2)}) collective-permute-start(bf16[64,256]{1,0:T(8,128)(2,1)S(1)} %get-tuple-element.88), channel_id=1, source_target_pairs={{0,2},{1,3},{2,0},{3,1},{4,6},{5,7},{6,4},{7,5},{8,10},{9,11},{10,... | collective-permute-start | bytes 98312 | tf_op jit(solution)/shard_map/ppermute | solution.py:745

commit v8 on v7

--- a/solution.py
+++ b/solution.py
@@ -831,8 +831,6 @@
     near, pair_near = blocks[:, :rows], blocks[:, rows:]
     far = swap_col(near, Y_PARTNER)
     pair_far = swap_col(pair_near, Y_PARTNER)
-    far, normed = lax.optimization_barrier((far, normed))
-    far_normed = swap_col(normed, Y_PARTNER)
     other_near, other_far = swap_depth(near), swap_depth(far)
     sizes = (seqs, res, pair_cols, width)
     orders = (near_order, far_order)
@@ -858,6 +856,8 @@
         compiler_params=params,
         name="outer_products",
     )(ids, near, far, other_near, other_far, wturn)
+    normed, proj_out = lax.optimization_barrier((normed, proj_out))
+    far_normed = swap_col(normed, Y_PARTNER)
     other_near, other_far, proj_out = lax.optimization_barrier((other_near, other_far, proj_out))
     rightt, leftt = pl.pallas_call(
         functools.partial(turn_kernel, sizes, orders),
@@ -974,10 +974,11 @@
         compiler_params=params,
         name="sums_over_depth",
     )(weights, swap_depth(weights))
+    feat = feat.reshape(seqs, res, channels)
     came, feat, dout, dhid, dback = lax.optimization_barrier((came, feat, dout, dhid, dback))
     total = pairwise_sum([block.astype(f32) for block in [part] + came])
     return (
-        feat.reshape(seqs, res, channels),
+        feat,
         couple.reshape(res, pair_cols, pair_width),
         total[:width].T,
         total[width:].T,

time: 40.8 us -> 40.9 us (level)
  starting transfers between devices: 14.8 us -> 15.7 us
  waiting for transfers between devices: 11.3 us -> 10.5 us
    ppermute x9, starting transfers between devices: 13.8 us -> 14.8 us  [swap_col(): lax.ppermute(block, 'col', [(at, at ^ partner) for at in range(count)])]
    ppermute x9, waiting for transfers between devices: 11.2 us -> 10.4 us  [swap_col(): lax.ppermute(block, 'col', [(at, at ^ partner) for at in range(count)])]
  transfers between devices with their start and end apart: 15 -> 15, of which waited for: 6 -> 6; matrix products, arithmetic and copies ran while one was open for 0% -> 2% of each run, Pallas kernels for 20% -> 20%
where the time goes in v8:
time: 40.9 us; the launch traced here: 40.7 us
  starting transfers between devices  15.7 us (38%)
  Pallas kernels  12.1 us (30%)
  waiting for transfers between devices  10.5 us (26%)
  local copies, waits for them, and re-layouts  1.47 us (4%)
  between operations  0.8 us (2%)
    ppermute x9, starting transfers between devices, swap_col(): lax.ppermute(block, 'col', [(at, at ^ partner) for at in range(count)])  14.8 us
    ppermute x9, waiting for transfers between devices, swap_col(): lax.ppermute(block, 'col', [(at, at ^ partner) for at in range(count)])  10.4 us
    pallas_call x1, Pallas kernels, whole_plan(): pl.pallas_call(functools.partial(transition_kernel, sizes, orders), out_s...  2.41 us
    pallas_call x1, Pallas kernels, whole_plan(): pl.pallas_call(functools.partial(outer_kernel, sizes, orders), out_shape=...  2.11 us
    pallas_call x1, Pallas kernels, whole_plan(): pl.pallas_call(functools.partial(projector_kernel, sizes), out_shape=(sha...  2.04 us
    pallas_call x1, Pallas kernels, whole_plan(): pl.pallas_call(pre_kernel, out_shape=(shape((1, rows + 2 * per, pair_widt...  1.91 us
    pallas_call x1, Pallas kernels, whole_plan(): pl.pallas_call(functools.partial(turn_kernel, sizes, orders), out_shape=(...  1.39 us
    pallas_call x1, Pallas kernels, whole_plan(): pl.pallas_call(weights_sum_kernel, out_shape=(shape((outer_width, pair_wi...  1.02 us
  transfers between devices with their start and end apart: 15, of which 6 were waited for; matrix products, arithmetic and copies ran while one was open for 2% of the time, Pallas kernels for 20%

profile of v8, /device:TPU:0, one launch (start us, length us, event | category | flops | bytes accessed | tf_op | source)
XLA Modules:
  0.0 40.7 jit_solution(12769481294171837394)
XLA Ops:
  0.6 0.1 pad_add_fusion.ids_ref
  0.7 1.9 %project.1 = (bf16[1,272,128]{2,1,0:T(8,128)(2,1)S(1)}, f32[1,256]{1,0:T(1,128)S(1)}, bf16[32,256]{1,0:T(8,128)(2,1)S(1)}, bf16[32,256]{1,0:T(8,128)(2,1)S(1)}, ...) custom-call(s32[2]{0:T(128)S(1)} %pad_add_fusion.ids_ref, ...), custom_call_target="tpu_custom_call" | custom-call | tf_op jit(solution)/shard_map/project/pallas_call | solution.py:785
  2.6 5.1 %collective-permute-start = (bf16[1,272,128]{2,1,0:T(8,128)(2,1)S(1)}, bf16[1,272,128]{2,1,0:T(8,128)(2,1)S(1)}, u32[]{:S(2)}, u32[]{:S(2)}) collective-permute-start(bf16[1,272,128]{2,1,0:T(8,128)(2,1)S(1)} %get-tuple-element.57), channel_id=1, source_target_pairs={{0,6},{1,7},{2,4},{3,5},{4,2},{5,3},{6,0},{7,1},{8,14},{9,15},{10,... | collective-permute-start | bytes 208904 | tf_op jit(solution)/shard_map/ppermute | solution.py:745
  7.7 0.0 collective-permute-start.1
  7.8 0.6 %collective-permute-start.2 = (bf16[1,272,128]{2,1,0:T(8,128)(2,1)S(1)}, bf16[1,272,128]{2,1,0:T(8,128)(2,1)S(1)}, u32[]{:S(2)}, u32[]{:S(2)}) collective-permute-start(bf16[1,272,128]{2,1,0:T(8,128)(2,1)S(1)} %get-tuple-element.57), channel_id=1, source_target_pairs={{0,2},{1,3},{2,0},{3,1},{4,6},{5,7},{6,4},{7,5},{8,10},{9,11},{10,... | collective-permute-start | bytes 208904 | tf_op jit(solution)/shard_map/ppermute | solution.py:745
  8.4 2.0 %collective-permute-done = bf16[1,272,128]{2,1,0:T(8,128)(2,1)S(1)} collective-permute-done((bf16[1,272,128]{2,1,0:T(8,128)(2,1)S(1)}, bf16[1,272,128]{2,1,0:T(8,128)(2,1)S(1)}, u32[]{:S(2)}, u32[]{:S(2)}) %collective-permute-start) | collective-permute-done | bytes 69664 | tf_op jit(solution)/shard_map/ppermute | solution.py:745
  10.4 3.2 %collective-permute-done.1 = bf16[1,272,128]{2,1,0:T(8,128)(2,1)S(1)} collective-permute-done((bf16[1,272,128]{2,1,0:T(8,128)(2,1)S(1)}, bf16[1,272,128]{2,1,0:T(8,128)(2,1)S(1)}, u32[]{:S(2)}, u32[]{:S(2)}) %collective-permute-start.1) | collective-permute-done | bytes 69664 | tf_op jit(solution)/shard_map/ppermute | solution.py:745
  13.7 0.0 collective-permute-done.2
  13.7 0.0 copy-start
  13.7 1.6 %collective-permute-start.4 = (bf16[4,144,128]{2,1,0:T(8,128)(2,1)S(1)}, bf16[4,144,128]{2,1,0:T(8,128)(2,1)S(1)}, u32[]{:S(2)}, u32[]{:S(2)}) collective-permute-start(bf16[4,144,128]{2,1,0:T(8,128)(2,1)S(1)} %slice.17.near_ref), channel_id=1, source_target_pairs={{0,1},{1,0},{2,3},{3,2},{4,5},{5,4},{6,7},{7,6},{8,9},{9,8},{10,11... | collective-permute-start | bytes 442376 | tf_op jit(solution)/shard_map/ppermute | solution.py:745
  15.3 0.0 collective-permute-start.5
  15.3 3.8 %collective-permute-done.4.far_ref = bf16[4,144,128]{2,1,0:T(8,128)(2,1)S(1)} collective-permute-done((bf16[4,144,128]{2,1,0:T(8,128)(2,1)S(1)}, bf16[4,144,128]{2,1,0:T(8,128)(2,1)S(1)}, u32[]{:S(2)}, u32[]{:S(2)}) %collective-permute-start.4) | collective-permute-done | bytes 147488 | tf_op jit(solution)/shard_map/ppermute | solution.py:745
  19.1 0.0 collective-permute-start.6
  19.2 1.8 %collective-permute-start.3 = (bf16[4,128,128]{2,1,0:T(8,128)(2,1)S(1)}, bf16[4,128,128]{2,1,0:T(8,128)(2,1)S(1)}, u32[]{:S(2)}, u32[]{:S(2)}) collective-permute-start(bf16[4,128,128]{2,1,0:T(8,128)(2,1)S(1)} %slice.16.near_ref), channel_id=1, source_target_pairs={{0,1},{1,0},{2,3},{3,2},{4,5},{5,4},{6,7},{7,6},{8,9},{9,8},{10,11... | collective-permute-start | bytes 393224 | tf_op jit(solution)/shard_map/ppermute | solution.py:745
  21.0 0.0 copy-done
  21.0 0.1 copy.19
  21.1 0.0 collective-permute-done.5.other_near_ref
  21.1 0.0 collective-permute-done.6.other_far_ref
  21.1 2.1 %outer_products.1 = (bf16[512,1024]{1,0:T(8,128)(2,1)S(1)}, f32[512,128]{1,0:T(8,128)S(1)}, f32[512,128]{1,0:T(8,128)S(1)}, bf16[512,128]{1,0:T(8,128)(2,1)S(1)}, f32[32,128]{1,0:T(8,128)S(1)}) custom-call(s32[2]{0:T(128)S(1)} %pad_add_fusion.ids_ref, bf16[4,144,128]{2,1,0:T(8,128)(2,1)S(1)} %slice.17.near_ref, ...), custom_call_target="tpu_custom_call" | custom-call | tf_op jit(solution)/shard_map/outer_products/pallas_call | solution.py:837
  23.2 0.0 copy-start.1
  23.2 0.0 copy-start.2
  23.2 1.2 %collective-permute-start.7 = (bf16[256,256]{1,0:T(8,128)(2,1)S(1)}, bf16[256,256]{1,0:T(8,128)(2,1)S(1)}, u32[]{:S(2)}, u32[]{:S(2)}) collective-permute-start(bf16[256,256]{1,0:T(8,128)(2,1)S(1)} %get-tuple-element.72.normed_ref), channel_id=1, source_target_pairs={{0,1},{1,0},{2,3},{3,2},{4,5},{5,4},{6,7},{7,6},{8,9},{9,8},{10,11... | collective-permute-start | bytes 393224 | tf_op jit(solution)/shard_map/ppermute | solution.py:745
  24.5 0.0 collective-permute-start.9
  24.5 1.4 %turned.1 = (bf16[1024,128]{1,0:T(8,128)(2,1)S(1)}, bf16[1024,128]{1,0:T(8,128)(2,1)S(1)}) custom-call(s32[2]{0:T(128)S(1)} %pad_add_fusion.ids_ref, bf16[4,144,128]{2,1,0:T(8,128)(2,1)S(1)} %slice.17.near_ref, bf16[4,144,128]{2,1,0:T(8,128)(2,1)S(1)} %collective-permute-done.4.far_ref, bf16[4,144,128]{2,1,0:T(8,128)(2,1)S(1)} %collective-permute-done.5.other_near_ref, ...), custom_call_target="tpu_custom_call" | custom-call | tf_op jit(solution)/shard_map/turned/pallas_call | solution.py:862
  25.9 0.0 collective-permute-done.3.far_ref
  25.9 0.0 copy-done.1
  25.9 0.0 copy-done.2
  25.9 2.4 %transition.1 = (bf16[64,128]{1,0:T(8,128)(2,1)}, bf16[512,128]{1,0:T(8,128)(2,1)S(1)}, bf16[512,128]{1,0:T(8,128)(2,1)S(1)}, bf16[512,512]{1,0:T(8,128)(2,1)S(1...) custom-call(s32[2]{0:T(128)S(1)} %pad_add_fusion.ids_ref, bf16[4,128,128]{2,1,0:T(8,128)(2,1)S(1)} %slice.16.near_ref, ...), custom_call_target="tpu_custom_call" | custom-call | tf_op jit(solution)/shard_map/transition/pallas_call | solution.py:880
  28.3 0.6 %collective-permute-done.7.far_normed_ref = bf16[256,256]{1,0:T(8,128)(2,1)S(1)} collective-permute-done((bf16[256,256]{1,0:T(8,128)(2,1)S(1)}, bf16[256,256]{1,0:T(8,128)(2,1)S(1)}, u32[]{:S(2)}, u32[]{:S(2)}) %collective-permute-start.7) | collective-permute-done | bytes 131104 | tf_op jit(solution)/shard_map/ppermute | solution.py:745
  28.9 0.0 collective-permute-start.10
  28.9 0.5 %collective-permute-start.8 = (bf16[512,128]{1,0:T(8,128)(2,1)S(1)}, bf16[512,128]{1,0:T(8,128)(2,1)S(1)}, u32[]{:S(2)}, u32[]{:S(2)}) collective-permute-start(bf16[512,128]{1,0:T(8,128)(2,1)S(1)} %get-tuple-element.73.opm_ref), channel_id=1, source_target_pairs={{0,8},{8,0},{1,9},{9,1},{2,10},{10,2},{3,11},{11,3},{4,12},{12,4},... | collective-permute-start | bytes 393224 | tf_op jit(solution)/shard_map/ppermute | solution.py:734
  29.4 0.9 %weight_gradients.1.mine_ref = bf16[2048,128]{1,0:T(8,128)(2,1)S(1)} custom-call(bf16[512,1024]{1,0:T(8,128)(2,1)S(1)} %get-tuple-element.75.outer_ref, bf16[512,128]{1,0:T(8,128)(2,1)S(1)} %get-tuple-element.73.opm_ref, bf16[512,128]{1,0:T(8,128)(2,1)S(1)} %get-tuple-element.76.pn_ref, bf16[512,512]{1,0:T(8,128)(2,1)S(1)} %get-tuple-element.77.gh_ref, ...), custom_call_target="tpu_custom_call" | custom-call | tf_op jit(solution)/shard_map/weight_gradients/pallas_call | solution.py:910
  30.4 0.0 collective-permute-done.9.other_normed_ref
  30.4 0.0 collective-permute-done.10.other_far_normed_ref
  30.4 0.1 collective-permute-done.8.other_opm_ref
  30.5 2.0 %projector_parts.1 = (bf16[64,256]{1,0:T(8,128)(2,1)S(1)}, bf16[256,256]{1,0:T(8,128)(2,1)S(1)}) custom-call(s32[2]{0:T(128)S(1)} %pad_add_fusion.ids_ref, bf16[512,128]{1,0:T(8,128)(2,1)S(1)} %get-tuple-element.73.opm_ref, bf16[512,128]{1,0:T(8,128)(2,1)S(1)} %collective-permute-done.8.other_opm_ref, bf16[1024,128]{1,0:T(8,128)(2,1)S(1)} %get-tuple-element.81.rightt_ref, ...), custom_call_target="tpu_custom_call" | custom-call | tf_op jit(solution)/shard_map/projector_parts/pallas_call | solution.py:922
  32.5 0.4 collective-permute-start.14
  32.9 2.3 %collective-permute-start.11 = (bf16[64,256]{1,0:T(8,128)(2,1)S(1)}, bf16[64,256]{1,0:T(8,128)(2,1)S(1)}, u32[]{:S(2)}, u32[]{:S(2)}) collective-permute-start(bf16[64,256]{1,0:T(8,128)(2,1)S(1)} %get-tuple-element.88), channel_id=1, source_target_pairs={{0,6},{1,7},{2,4},{3,5},{4,2},{5,3},{6,0},{7,1},{8,14},{9,15},{10,... | collective-permute-start | bytes 98312 | tf_op jit(solution)/shard_map/ppermute | solution.py:745
  35.2 0.0 collective-permute-start.12
  35.2 2.1 %collective-permute-start.13 = (bf16[64,256]{1,0:T(8,128)(2,1)S(1)}, bf16[64,256]{1,0:T(8,128)(2,1)S(1)}, u32[]{:S(2)}, u32[]{:S(2)}) collective-permute-start(bf16[64,256]{1,0:T(8,128)(2,1)S(1)} %get-tuple-element.88), channel_id=1, source_target_pairs={{0,2},{1,3},{2,0},{3,1},{4,6},{5,7},{6,4},{7,5},{8,10},{9,11},{10,... | collective-permute-start | bytes 98312 | tf_op jit(solution)/shard_map/ppermute | solution.py:745
  37.3 0.3 features.1
  37.6 0.7 %reshape.44 = bf16[64,4,256]{2,1,0:T(4,128)(2,1)} reshape(bf16[256,256]{1,0:T(8,128)(2,1)S(1)} %features.1) | data formatting | bytes 262144 | tf_op jit(solution)/shard_map/reshape | solution.py:977
  38.3 0.0 collective-permute-done.14.other_ref
  38.3 1.0 %sums_over_depth.1 = (f32[1024,128]{1,0:T(8,128)}, f32[128,512]{1,0:T(8,128)}, f32[512,128]{1,0:T(8,128)}) custom-call(bf16[2048,128]{1,0:T(8,128)(2,1)S(1)} %weight_gradients.1.mine_ref, bf16[2048,128]{1,0:T(8,128)(2,1)S(1)} %collective-permute-done.14.other_ref), custom_call_target="tpu_custom_call" | custom-call | tf_op jit(solution)/shard_map/sums_over_depth/pallas_call | solution.py:965
  39.3 0.0 collective-permute-done.11
  39.3 0.7 %collective-permute-done.12 = bf16[64,256]{1,0:T(8,128)(2,1)S(1)} collective-permute-done((bf16[64,256]{1,0:T(8,128)(2,1)S(1)}, bf16[64,256]{1,0:T(8,128)(2,1)S(1)}, u32[]{:S(2)}, u32[]{:S(2)}) %collective-permute-start.12) | collective-permute-done | bytes 32800 | tf_op jit(solution)/shard_map/ppermute | solution.py:745
  40.0 0.0 collective-permute-done.13
  40.0 0.6 %slice_bitcast_fusion = (f32[256,32]{0,1:T(8,128)}, f32[256,32]{0,1:T(8,128)}) fusion(f32[64,256]{1,0:T(8,128)S(1)} %add_add_fusion), kind=kLoop, calls=%fused_computation.2 | loop fusion | bytes 131072 | tf_op jit(solution)/shard_map/transpose | solution.py:984
  (4 shorter events, 0.1 us)
Async XLA Ops:
  2.6 7.8 %collective-permute-start = (bf16[1,272,128]{2,1,0:T(8,128)(2,1)S(1)}, bf16[1,272,128]{2,1,0:T(8,128)(2,1)S(1)}, u32[]{:S(2)}, u32[]{:S(2)}) collective-permute-start(bf16[1,272,128]{2,1,0:T(8,128)(2,1)S(1)} %get-tuple-element.57), channel_id=1, source_target_pairs={{0,6},{1,7},{2,4},{3,5},{4,2},{5,3},{6,0},{7,1},{8,14},{9,15},{10,... | collective-permute-start | bytes 208904 | tf_op jit(solution)/shard_map/ppermute | solution.py:745
  7.7 5.9 %collective-permute-start.1 = (bf16[1,272,128]{2,1,0:T(8,128)(2,1)S(1)}, bf16[1,272,128]{2,1,0:T(8,128)(2,1)S(1)}, u32[]{:S(2)}, u32[]{:S(2)}) collective-permute-start(bf16[1,272,128]{2,1,0:T(8,128)(2,1)S(1)} %get-tuple-element.57), channel_id=1, source_target_pairs={{0,4},{1,5},{2,6},{3,7},{4,0},{5,1},{6,2},{7,3},{8,12},{9,13},{10,... | collective-permute-start | bytes 208904 | tf_op jit(solution)/shard_map/ppermute | solution.py:745
  7.8 5.9 %collective-permute-start.2 = (bf16[1,272,128]{2,1,0:T(8,128)(2,1)S(1)}, bf16[1,272,128]{2,1,0:T(8,128)(2,1)S(1)}, u32[]{:S(2)}, u32[]{:S(2)}) collective-permute-start(bf16[1,272,128]{2,1,0:T(8,128)(2,1)S(1)} %get-tuple-element.57), channel_id=1, source_target_pairs={{0,2},{1,3},{2,0},{3,1},{4,6},{5,7},{6,4},{7,5},{8,10},{9,11},{10,... | collective-permute-start | bytes 208904 | tf_op jit(solution)/shard_map/ppermute | solution.py:745
  13.7 7.3 %copy-start = (bf16[1024,128]{1,0:T(8,128)(2,1)S(1)}, bf16[1024,128]{1,0:T(8,128)(2,1)}, u32[]{:S(2)}) copy-start(bf16[1024,128]{1,0:T(8,128)(2,1)} %wout_ref.1) | copy-start | bytes 786436
  13.7 5.4 %collective-permute-start.4 = (bf16[4,144,128]{2,1,0:T(8,128)(2,1)S(1)}, bf16[4,144,128]{2,1,0:T(8,128)(2,1)S(1)}, u32[]{:S(2)}, u32[]{:S(2)}) collective-permute-start(bf16[4,144,128]{2,1,0:T(8,128)(2,1)S(1)} %slice.17.near_ref), channel_id=1, source_target_pairs={{0,1},{1,0},{2,3},{3,2},{4,5},{5,4},{6,7},{7,6},{8,9},{9,8},{10,11... | collective-permute-start | bytes 442376 | tf_op jit(solution)/shard_map/ppermute | solution.py:745
  15.3 5.8 %collective-permute-start.5 = (bf16[4,144,128]{2,1,0:T(8,128)(2,1)S(1)}, bf16[4,144,128]{2,1,0:T(8,128)(2,1)S(1)}, u32[]{:S(2)}, u32[]{:S(2)}) collective-permute-start(bf16[4,144,128]{2,1,0:T(8,128)(2,1)S(1)} %slice.17.near_ref), channel_id=1, source_target_pairs={{0,8},{8,0},{1,9},{9,1},{2,10},{10,2},{3,11},{11,3},{4,12},{12,4},... | collective-permute-start | bytes 442376 | tf_op jit(solution)/shard_map/ppermute | solution.py:734
  19.1 1.9 %collective-permute-start.6 = (bf16[4,144,128]{2,1,0:T(8,128)(2,1)S(1)}, bf16[4,144,128]{2,1,0:T(8,128)(2,1)S(1)}, u32[]{:S(2)}, u32[]{:S(2)}) collective-permute-start(bf16[4,144,128]{2,1,0:T(8,128)(2,1)S(1)} %collective-permute-done.4.far_ref), channel_id=1, source_target_pairs={{0,8},{8,0},{1,9},{9,1},{2,10},{10,2},{3,11},{11,3},{4,12},{12,4},... | collective-permute-start | bytes 442376 | tf_op jit(solution)/shard_map/ppermute | solution.py:734
  19.2 6.7 %collective-permute-start.3 = (bf16[4,128,128]{2,1,0:T(8,128)(2,1)S(1)}, bf16[4,128,128]{2,1,0:T(8,128)(2,1)S(1)}, u32[]{:S(2)}, u32[]{:S(2)}) collective-permute-start(bf16[4,128,128]{2,1,0:T(8,128)(2,1)S(1)} %slice.16.near_ref), channel_id=1, source_target_pairs={{0,1},{1,0},{2,3},{3,2},{4,5},{5,4},{6,7},{7,6},{8,9},{9,8},{10,11... | collective-permute-start | bytes 393224 | tf_op jit(solution)/shard_map/ppermute | solution.py:745
  23.2 2.7 %copy-start.1 = (bf16[128,512]{1,0:T(8,128)(2,1)S(1)}, bf16[128,512]{1,0:T(8,128)(2,1)}, u32[]{:S(2)}) copy-start(bf16[128,512]{1,0:T(8,128)(2,1)} %hid_ref.1) | copy-start | bytes 393220
  23.2 2.7 %copy-start.2 = (bf16[512,128]{1,0:T(8,128)(2,1)S(1)}, bf16[512,128]{1,0:T(8,128)(2,1)}, u32[]{:S(2)}) copy-start(bf16[512,128]{1,0:T(8,128)(2,1)} %back_ref.1) | copy-start | bytes 393220
  23.2 5.7 %collective-permute-start.7 = (bf16[256,256]{1,0:T(8,128)(2,1)S(1)}, bf16[256,256]{1,0:T(8,128)(2,1)S(1)}, u32[]{:S(2)}, u32[]{:S(2)}) collective-permute-start(bf16[256,256]{1,0:T(8,128)(2,1)S(1)} %get-tuple-element.72.normed_ref), channel_id=1, source_target_pairs={{0,1},{1,0},{2,3},{3,2},{4,5},{5,4},{6,7},{7,6},{8,9},{9,8},{10,11... | collective-permute-start | bytes 393224 | tf_op jit(solution)/shard_map/ppermute | solution.py:745
  24.5 5.9 %collective-permute-start.9 = (bf16[256,256]{1,0:T(8,128)(2,1)S(1)}, bf16[256,256]{1,0:T(8,128)(2,1)S(1)}, u32[]{:S(2)}, u32[]{:S(2)}) collective-permute-start(bf16[256,256]{1,0:T(8,128)(2,1)S(1)} %get-tuple-element.72.normed_ref), channel_id=1, source_target_pairs={{0,8},{8,0},{1,9},{9,1},{2,10},{10,2},{3,11},{11,3},{4,12},{12,4},... | collective-permute-start | bytes 393224 | tf_op jit(solution)/shard_map/ppermute | solution.py:734
  28.9 1.4 %collective-permute-start.10 = (bf16[256,256]{1,0:T(8,128)(2,1)S(1)}, bf16[256,256]{1,0:T(8,128)(2,1)S(1)}, u32[]{:S(2)}, u32[]{:S(2)}) collective-permute-start(bf16[256,256]{1,0:T(8,128)(2,1)S(1)} %collective-permute-done.7.far_normed_ref), channel_id=1, source_target_pairs={{0,8},{8,0},{1,9},{9,1},{2,10},{10,2},{3,11},{11,3},{4,12},{12,4},... | collective-permute-start | bytes 393224 | tf_op jit(solution)/shard_map/ppermute | solution.py:734
  28.9 1.5 %collective-permute-start.8 = (bf16[512,128]{1,0:T(8,128)(2,1)S(1)}, bf16[512,128]{1,0:T(8,128)(2,1)S(1)}, u32[]{:S(2)}, u32[]{:S(2)}) collective-permute-start(bf16[512,128]{1,0:T(8,128)(2,1)S(1)} %get-tuple-element.73.opm_ref), channel_id=1, source_target_pairs={{0,8},{8,0},{1,9},{9,1},{2,10},{10,2},{3,11},{11,3},{4,12},{12,4},... | collective-permute-start | bytes 393224 | tf_op jit(solution)/shard_map/ppermute | solution.py:734
  32.5 5.8 %collective-permute-start.14 = (bf16[2048,128]{1,0:T(8,128)(2,1)S(1)}, bf16[2048,128]{1,0:T(8,128)(2,1)S(1)}, u32[]{:S(2)}, u32[]{:S(2)}) collective-permute-start(bf16[2048,128]{1,0:T(8,128)(2,1)S(1)} %weight_gradients.1.mine_ref), channel_id=1, source_target_pairs={{0,8},{8,0},{1,9},{9,1},{2,10},{10,2},{3,11},{11,3},{4,12},{12,4},... | collective-permute-start | bytes 1572872 | tf_op jit(solution)/shard_map/ppermute | solution.py:734
  32.9 6.4 %collective-permute-start.11 = (bf16[64,256]{1,0:T(8,128)(2,1)S(1)}, bf16[64,256]{1,0:T(8,128)(2,1)S(1)}, u32[]{:S(2)}, u32[]{:S(2)}) collective-permute-start(bf16[64,256]{1,0:T(8,128)(2,1)S(1)} %get-tuple-element.88), channel_id=1, source_target_pairs={{0,6},{1,7},{2,4},{3,5},{4,2},{5,3},{6,0},{7,1},{8,14},{9,15},{10,... | collective-permute-start | bytes 98312 | tf_op jit(solution)/shard_map/ppermute | solution.py:745
  35.2 4.8 %collective-permute-start.12 = (bf16[64,256]{1,0:T(8,128)(2,1)S(1)}, bf16[64,256]{1,0:T(8,128)(2,1)S(1)}, u32[]{:S(2)}, u32[]{:S(2)}) collective-permute-start(bf16[64,256]{1,0:T(8,128)(2,1)S(1)} %get-tuple-element.88), channel_id=1, source_target_pairs={{0,4},{1,5},{2,6},{3,7},{4,0},{5,1},{6,2},{7,3},{8,12},{9,13},{10,... | collective-permute-start | bytes 98312 | tf_op jit(solution)/shard_map/ppermute | solution.py:745
  35.2 4.8 %collective-permute-start.13 = (bf16[64,256]{1,0:T(8,128)(2,1)S(1)}, bf16[64,256]{1,0:T(8,128)(2,1)S(1)}, u32[]{:S(2)}, u32[]{:S(2)}) collective-permute-start(bf16[64,256]{1,0:T(8,128)(2,1)S(1)} %get-tuple-element.88), channel_id=1, source_target_pairs={{0,2},{1,3},{2,0},{3,1},{4,6},{5,7},{6,4},{7,5},{8,10},{9,11},{10,... | collective-permute-start | bytes 98312 | tf_op jit(solution)/shard_map/ppermute | solution.py:745

commit v9 on v8

--- a/solution.py
+++ b/solution.py
@@ -327,8 +327,20 @@
         copy.wait()
     lanes = sent_ref.shape[2]
     group = lanes // res
+    channels = x_ref.shape[2]
+    rows = x_ref[...].astype(jnp.float32).reshape(seqs * res, channels)
+    for at in range(channels // lanes):
+        wide_ref[at] = rows[:, at * lanes : (at + 1) * lanes]
     scaled, inv = norm_pieces(
-        x_ref[...].astype(jnp.float32).reshape(seqs * res, x_ref.shape[2])
+        jnp.concatenate(
+            [
+                jnp.concatenate(
+                    [wide_ref[at, pl.ds(r, seqs, stride=res), :] for r in range(res)], axis=0
+                )
+                for at in range(channels // lanes)
+            ],
+            axis=1,
+        )
     )
     scaled_ref[...] = scaled
     inv_ref[...] = inv
@@ -340,8 +352,6 @@
         (((1,), (1,)), ((), ())),
         preferred_element_type=jnp.float32,
     )
-    for at in range(2):
-        wide_ref[at] = wide[:, at * lanes : (at + 1) * lanes]
     tile_ref[...] = jnp.zeros(tile_ref.shape, jnp.float32)
     mask = maskt_ref[...].astype(jnp.float32)
     tile_ref[0:res, 0:seqs] = mask
@@ -358,11 +368,10 @@
     tile_ref[res : 2 * res, 0 : pmask_ref.shape[1]] = pmask_ref[...].astype(jnp.float32)
     lane_group = lax.broadcasted_iota(jnp.int32, (seqs, lanes), 1) // group
     for at in range(2):
-        both = wide_ref[at, pl.ds(0, seqs, stride=res), :]
+        part = wide[:, at * lanes : (at + 1) * lanes]
+        both = part[0:seqs]
         for r in range(1, res):
-            both = jnp.where(
-                lane_group == r, wide_ref[at, pl.ds(r, seqs, stride=res), :], both
-            )
+            both = jnp.where(lane_group == r, part[r * seqs : (r + 1) * seqs], both)
         sent_ref[0, at * seqs : (at + 1) * seqs, :] = (both * mask_lanes).astype(jnp.bfloat16)
     sent_ref[0, 2 * seqs : first_pair, :] = tile_ref[...].astype(jnp.bfloat16)
 
@@ -441,7 +450,7 @@
             bf16
         )
     ones = jnp.ones((lanes, lanes), bf16)
-    cnt_ref[...] = jnp.dot(cntl_ref[...], ones, preferred_element_type=f32)
+    cnt_ref[...] = 1.0 / jnp.dot(cntl_ref[...], ones, preferred_element_type=f32)
     pm_ref[...] = jnp.dot(pml_ref[...], ones, preferred_element_type=f32).astype(bf16)
 
     for dh in range(width // 4):
@@ -463,39 +472,29 @@
     proj_out_ref[...] = jnp.dot(outer_ref[...], wturn_ref[...], preferred_element_type=f32)
 
 
-def turn_kernel(
-    sizes,
-    orders,
-    ids_ref,
-    near_ref,
-    far_ref,
-    other_near_ref,
-    other_far_ref,
-    rightt_ref,
-    leftt_ref,
-    got_ref,
-    turn_ref,
-):
+def turn_kernel(sizes, ids_ref, mine_ref, other_ref, left_ref, right_ref, got_ref, turn_ref, tmp_ref):
     seqs, res, _, width = sizes
-    depths, cols = got_ref.shape[0], got_ref.shape[1]
+    depths, line = got_ref.shape[0], got_ref.shape[1]
     lanes = res * width
-    residues = res * cols
     me_depth = ids_ref[0]
-    me_col = ids_ref[1]
-    for order, mine, other in zip(orders, (near_ref, far_ref), (other_near_ref, other_far_ref)):
-        for at, partner in enumerate(order):
-            got_ref[me_depth, me_col ^ partner] = mine[at, 0 : 2 * seqs, :]
-            got_ref[1 - me_depth, me_col ^ partner] = other[at, 0 : 2 * seqs, :]
-    for at, out in ((0, leftt_ref), (1, rightt_ref)):
-        for k in range(cols):
+    me_z = ids_ref[1] // 2
+    for at, partner in enumerate((0,) + Z_PARTNERS):
+        z = me_z ^ (partner // 2)
+        got_ref[me_depth, z] = mine_ref[at, 0 : 2 * seqs, :]
+        got_ref[1 - me_depth, z] = other_ref[at, 0 : 2 * seqs, :]
+    for at, out in enumerate((left_ref, right_ref)):
+        for z in range(line):
             block = jnp.concatenate(
-                [got_ref[e, k, at * seqs : (at + 1) * seqs, :] for e in range(depths)], axis=0
+                [got_ref[e, z, at * seqs : (at + 1) * seqs, :] for e in range(depths)], axis=0
             ).astype(jnp.float32)
-            turn_ref[k * lanes : (k + 1) * lanes, :] = block.T
+            turn_ref[z * lanes : (z + 1) * lanes, :] = block.T
         for d in range(width):
-            out[d * residues : (d + 1) * residues, :] = turn_ref[
-                pl.ds(d, residues, stride=width), :
-            ].astype(jnp.bfloat16)
+            tmp_ref[d * line * res : (d + 1) * line * res, :] = turn_ref[
+                pl.ds(d, line * res, stride=width), :
+            ]
+        for z in range(line):
+            rows = slice(z * lanes, (z + 1) * lanes)
+            out[:, rows] = tmp_ref[rows, :].T.astype(jnp.bfloat16)
 
 
 def transition_kernel(
@@ -537,13 +536,15 @@
             )
             for w in range(2)
         ]
-        count = cnt_ref[rows, :]
-        mid = act.astype(f32) + proj_out_ref[rows, :] / count
+        inv_count = cnt_ref[rows, :]
+        mid = act.astype(f32) + proj_out_ref[rows, :] * inv_count
         scaled, inv = norm_pieces(mid)
         normed = (scaled * gain).astype(bf16)
         pn_ref[rows, :] = normed
         pre = jnp.dot(normed, hid_ref[...], preferred_element_type=f32)
-        value, slope = silu_pieces(pre)
+        sigma = 0.5 + 0.5 * jnp.tanh(0.5 * pre)
+        value = pre * sigma
+        slope = sigma + value * (1.0 - sigma)
         hidden_ref[rows, :] = value.astype(bf16)
         masked = grad * pm_ref[rows, :]
         mg_ref[rows, :] = masked
@@ -560,7 +561,7 @@
         )
         gmid = grad.astype(f32) + standardize_adjoint(gsc, scaled, inv)
         gmid_ref[rows, :] = gmid
-        opm_ref[rows, :] = (gmid / count).astype(bf16)
+        opm_ref[rows, :] = (gmid * inv_count).astype(bf16)
     couple_ref[...] = gmid_ref[pl.ds(pl.multiple_of(me_col * per, per), per), :].astype(bf16)
 
 
@@ -569,8 +570,10 @@
     ids_ref,
     opm_ref,
     other_opm_ref,
-    rightt_ref,
-    leftt_ref,
+    left_near_ref,
+    right_near_ref,
+    left_far_ref,
+    right_far_ref,
     wout_ref,
     wturn_ref,
     maskt_ref,
@@ -579,13 +582,15 @@
     other_normed_ref,
     other_far_normed_ref,
     part_ref,
-    spread_ref,
+    grads_ref,
     gf_ref,
     grow_ref,
     gcol_ref,
-    gor_ref,
-    goc_ref,
-    gs_ref,
+    gon_ref,
+    gof_ref,
+    gcn_ref,
+    gcf_ref,
+    tot_ref,
     rows_ref,
 ):
     seqs, res, pair_cols, width = sizes
@@ -593,10 +598,11 @@
     residues = half // pair_cols
     lanes = res * width
     here = 2 * res
+    line = residues // here
+    near = line * res
     me_depth = ids_ref[0]
-    me_col = ids_ref[1]
-    me_y = me_col % 2
-    first_here = (me_col // 2) * here
+    me_z, me_y = ids_ref[1] // 2, ids_ref[1] % 2
+    first_here = me_z * here
     f32, bf16 = jnp.float32, jnp.bfloat16
     gf_ref[me_depth] = opm_ref[...].astype(f32)
     gf_ref[1 - me_depth] = other_opm_ref[...].astype(f32)
@@ -606,24 +612,32 @@
         (me_y, 1 - me_depth, other_normed_ref),
         (1 - me_y, 1 - me_depth, other_far_normed_ref),
     ):
-        rows_ref[y, e] = block[...]
-
-    for il in range(here):
-        for e in range(depths):
-            first = pl.multiple_of((first_here + il) * pair_cols, pair_cols)
-            grow_ref[il * residues + e * pair_cols : il * residues + (e + 1) * pair_cols, :] = (
-                gf_ref[e, pl.ds(first, pair_cols), :].astype(bf16)
-            )
+        for r in range(res):
+            rows_ref[y, r, e] = block[r * seqs : (r + 1) * seqs, :]
+
     my_half = first_here // pair_cols
     my_first = first_here - my_half * pair_cols
-    for jl in range(here):
-        gcol_ref[jl * residues : (jl + 1) * residues, :] = gf_ref[
-            my_half, pl.ds(my_first + jl, residues, stride=pair_cols), :
-        ].astype(bf16)
-    for lhs, weight, out in ((grow_ref, wturn_ref, gor_ref), (gcol_ref, wout_ref, goc_ref)):
+    for at in range(here):
+        for w, y in enumerate((me_y, 1 - me_y)):
+            for z in range(line):
+                to = at * residues + w * near + z * res
+                e, z_low = divmod(z, line // depths)
+                grow_ref[to : to + res, :] = gf_ref[
+                    e, pl.ds((first_here + at) * pair_cols + z_low * here + y * res, res), :
+                ]
+                gcol_ref[to : to + res, :] = gf_ref[
+                    my_half,
+                    pl.ds((z * here + y * res) * pair_cols + my_first + at, res, stride=pair_cols),
+                    :,
+                ]
+    for lhs, weight, outs in (
+        (grow_ref, wturn_ref, (gon_ref, gof_ref)),
+        (gcol_ref, wout_ref, (gcn_ref, gcf_ref)),
+    ):
+        operand = lhs[...].astype(bf16)
         for dh in range(width // 4):
             piece = lax.dot_general(
-                lhs[...],
+                operand,
                 weight[dh * lanes : (dh + 1) * lanes, :],
                 (((1,), (1,)), ((), ())),
                 preferred_element_type=f32,
@@ -637,10 +651,11 @@
                     width,
                 )
                 for dl in range(4):
-                    first = (dh * 4 + dl) * residues
-                    out[first : first + residues, y * lanes : (y + 1) * lanes] = turned[dl].astype(
-                        bf16
-                    )
+                    first = (dh * 4 + dl) * near
+                    for w, out in enumerate(outs):
+                        out[first : first + near, y * lanes : (y + 1) * lanes] = turned[dl][
+                            w * near : (w + 1) * near
+                        ].astype(bf16)
     group = lax.broadcasted_iota(jnp.int32, (here, here * width), 1) // width
     spread = (group == lax.broadcasted_iota(jnp.int32, (here, here * width), 0)).astype(f32)
     mask_lanes = lax.dot_general(
@@ -649,34 +664,30 @@
         (((0,), (0,)), ((), ())),
         preferred_element_type=f32,
     )
-    lane_group = lax.broadcasted_iota(jnp.int32, (seqs, lanes), 1) // width
-    for at, (lhs, rhs) in enumerate(((rightt_ref, gor_ref), (leftt_ref, goc_ref))):
-        total = lax.dot_general(
-            lhs[...], rhs[...], (((0,), (0,)), ((), ())), preferred_element_type=f32
+    for at, (near_lhs, near_rhs, far_lhs, far_rhs) in enumerate(
+        (
+            (right_near_ref, gon_ref, right_far_ref, gof_ref),
+            (left_near_ref, gcn_ref, left_far_ref, gcf_ref),
+        )
+    ):
+        total = jnp.dot(near_lhs[...], near_rhs[...], preferred_element_type=f32) + jnp.dot(
+            far_lhs[...], far_rhs[...], preferred_element_type=f32
         )
         total = (total * mask_lanes).astype(bf16).astype(f32)
+        sums = jnp.zeros((width, rows_ref.shape[4]), f32)
         for y in range(2):
+            block = total[:, y * lanes : (y + 1) * lanes]
             for e in range(depths):
-                block = total[e * seqs : (e + 1) * seqs, y * lanes : (y + 1) * lanes]
-                for r in range(res):
-                    gs_ref[at, y, e, pl.ds(r, seqs, stride=res), :] = jnp.where(
-                        lane_group == r, block, 0.0
-                    )
-    spread_ref[...] = jnp.concatenate(
-        [gs_ref[0, me_y, me_depth], gs_ref[1, me_y, me_depth]], axis=1
-    ).astype(bf16)
-    rows = rows_ref.shape[2]
-    for at in range(2):
-        cross = lax.dot_general(
-            gs_ref[at].reshape(2 * depths * rows, lanes).astype(bf16),
-            rows_ref[...].reshape(2 * depths * rows, rows_ref.shape[3]),
-            (((0,), (0,)), ((), ())),
-            preferred_element_type=f32,
-        )
-        total = cross[:width]
-        for r in range(1, res):
-            total = total + cross[r * width : (r + 1) * width]
-        part_ref[at * width : (at + 1) * width, :] = total.astype(bf16)
+                tot_ref[at, y, e] = block[e * seqs : (e + 1) * seqs]
+            turned = block.T.astype(bf16)
+            for r in range(res):
+                sums = sums + jnp.dot(
+                    turned[r * width : (r + 1) * width],
+                    rows_ref[y, r].reshape(depths * seqs, rows_ref.shape[4]),
+                    preferred_element_type=f32,
+                )
+        part_ref[at * width : (at + 1) * width, :] = sums.astype(bf16)
+        grads_ref[at] = tot_ref[at, me_y, me_depth]
 
 
 def weights_kernel(outer_ref, opm_ref, pn_ref, gh_ref, hidden_ref, mg_ref, out_ref, turn_ref):
@@ -718,16 +729,30 @@
 
 
 def feature_kernel(
-    copies, spread_ref, first_ref, second_ref, scale_ref, scaled_ref, inv_ref, feat_ref
+    sizes, grads_ref, first_ref, second_ref, scale_ref, scaled_ref, inv_ref, feat_ref, rows_ref
 ):
+    seqs, res, _, width = sizes
+    lanes = res * width
+    lane_group = lax.broadcasted_iota(jnp.int32, (seqs, lanes), 1) // width
+    spread = jnp.concatenate(
+        [
+            jnp.concatenate(
+                [jnp.where(lane_group == r, grads_ref[at], 0.0) for r in range(res)], axis=0
+            )
+            for at in range(2)
+        ],
+        axis=1,
+    ).astype(jnp.bfloat16)
     back = jnp.dot(
-        spread_ref[...],
-        wide_projector(first_ref, second_ref, copies),
-        preferred_element_type=jnp.float32,
-    )
-    feat_ref[...] = standardize_adjoint(
-        back * scale_ref[...], scaled_ref[...], inv_ref[...]
-    ).astype(jnp.bfloat16)
+        spread, wide_projector(first_ref, second_ref, res), preferred_element_type=jnp.float32
+    )
+    feat = standardize_adjoint(back * scale_ref[...], scaled_ref[...], inv_ref[...])
+    for at in range(rows_ref.shape[0]):
+        for r in range(res):
+            rows_ref[at, pl.ds(r, seqs, stride=res), :] = feat[
+                r * seqs : (r + 1) * seqs, at * lanes : (at + 1) * lanes
+            ]
+        feat_ref[:, at * lanes : (at + 1) * lanes] = rows_ref[at].astype(jnp.bfloat16)
 
 
 def swap_depth(block):
@@ -771,6 +796,7 @@
     lanes = res * width
     rows = 2 * seqs + MASK_ROWS
     half = residues * pair_cols
+    line = cols // 2
     f32, bf16 = jnp.float32, jnp.bfloat16
     ids = jnp.stack([lax.axis_index("depth"), lax.axis_index("col")]).astype(jnp.int32)
     smem = pl.BlockSpec(memory_space=pltpu.SMEM)
@@ -830,9 +856,28 @@
     )
     near, pair_near = blocks[:, :rows], blocks[:, rows:]
     far = swap_col(near, Y_PARTNER)
+    other_near = swap_depth(near)
+    sizes = (seqs, res, pair_cols, width)
+
+    def turned(mine, other):
+        return pl.pallas_call(
+            functools.partial(turn_kernel, sizes),
+            out_shape=(shape((depths * seqs, line * lanes), bf16),) * 2,
+            in_specs=[smem] + [vmem] * 2,
+            out_specs=[vmem] * 2,
+            scratch_shapes=[
+                pltpu.VMEM((depths, line, 2 * seqs, pair_width), bf16),
+                pltpu.VMEM((line * lanes, depths * seqs), f32),
+                pltpu.VMEM((line * lanes, depths * seqs), f32),
+            ],
+            compiler_params=params,
+            name="turned",
+        )(ids, mine, other)
+
+    left_near, right_near = turned(near, other_near)
+    far, left_near, right_near = lax.optimization_barrier((far, left_near, right_near))
+    other_far = swap_depth(far)
     pair_far = swap_col(pair_near, Y_PARTNER)
-    other_near, other_far = swap_depth(near), swap_depth(far)
-    sizes = (seqs, res, pair_cols, width)
     orders = (near_order, far_order)
     outer, proj_out, cnt, pm, maskt = pl.pallas_call(
         functools.partial(outer_kernel, sizes, orders),
@@ -858,24 +903,10 @@
     )(ids, near, far, other_near, other_far, wturn)
     normed, proj_out = lax.optimization_barrier((normed, proj_out))
     far_normed = swap_col(normed, Y_PARTNER)
-    other_near, other_far, proj_out = lax.optimization_barrier((other_near, other_far, proj_out))
-    rightt, leftt = pl.pallas_call(
-        functools.partial(turn_kernel, sizes, orders),
-        out_shape=(
-            shape((residues * width, depths * seqs), bf16),
-            shape((residues * width, depths * seqs), bf16),
-        ),
-        in_specs=[smem] + [vmem] * 4,
-        out_specs=[vmem] * 2,
-        scratch_shapes=[
-            pltpu.VMEM((depths, cols, 2 * seqs, pair_width), bf16),
-            pltpu.VMEM((residues * width, depths * seqs), f32),
-        ],
-        compiler_params=params,
-        name="turned",
-    )(ids, near, far, other_near, other_far)
-    pair_far, rightt, leftt, proj_out = lax.optimization_barrier(
-        (pair_far, rightt, leftt, proj_out)
+    other_far, proj_out = lax.optimization_barrier((other_far, proj_out))
+    left_far, right_far = turned(far, other_far)
+    pair_far, left_far, right_far, proj_out = lax.optimization_barrier(
+        (pair_far, left_far, right_far, proj_out)
     )
     couple, opm, pn, gh, hidden, mg = pl.pallas_call(
         functools.partial(transition_kernel, sizes, orders),
@@ -919,22 +950,24 @@
     other_opm, other_normed, other_far_normed, weights = lax.optimization_barrier(
         (swap_depth(opm), swap_depth(normed), swap_depth(far_normed), weights)
     )
-    part, spread = pl.pallas_call(
+    part, grads = pl.pallas_call(
         functools.partial(projector_kernel, sizes),
         out_shape=(
             shape((2 * width, channels), bf16),
-            shape((seqs * res, 2 * lanes), bf16),
+            shape((2, seqs, lanes), f32),
         ),
-        in_specs=[smem] + [vmem] * 11,
+        in_specs=[smem] + [vmem] * 13,
         out_specs=[vmem] * 2,
         scratch_shapes=[
             pltpu.VMEM((depths, half, pair_width), f32),
-            pltpu.VMEM((2 * res * residues, pair_width), bf16),
-            pltpu.VMEM((2 * res * residues, pair_width), bf16),
-            pltpu.VMEM((residues * width, 2 * lanes), bf16),
-            pltpu.VMEM((residues * width, 2 * lanes), bf16),
-            pltpu.VMEM((2, 2, depths, seqs * res, lanes), f32),
-            pltpu.VMEM((2, depths, seqs * res, channels), bf16),
+            pltpu.VMEM((2 * res * residues, pair_width), f32),
+            pltpu.VMEM((2 * res * residues, pair_width), f32),
+            pltpu.VMEM((line * lanes, 2 * lanes), bf16),
+            pltpu.VMEM((line * lanes, 2 * lanes), bf16),
+            pltpu.VMEM((line * lanes, 2 * lanes), bf16),
+            pltpu.VMEM((line * lanes, 2 * lanes), bf16),
+            pltpu.VMEM((2, 2, depths, seqs, lanes), f32),
+            pltpu.VMEM((2, res, depths, seqs, channels), bf16),
         ],
         compiler_params=params,
         name="projector_parts",
@@ -942,8 +975,10 @@
         ids,
         opm,
         other_opm,
-        rightt,
-        leftt,
+        left_near,
+        right_near,
+        left_far,
+        right_far,
         output_weight,
         wturn,
         maskt,
@@ -953,13 +988,14 @@
         other_far_normed,
     )
     feat = pl.pallas_call(
-        functools.partial(feature_kernel, res),
+        functools.partial(feature_kernel, sizes),
         out_shape=shape((seqs * res, channels), bf16),
         in_specs=[vmem] * 6,
         out_specs=vmem,
+        scratch_shapes=[pltpu.VMEM((channels // lanes, seqs * res, lanes), f32)],
         compiler_params=params,
         name="features",
-    )(spread, first, second, scale, scaled, inv)
+    )(grads, first, second, scale, scaled, inv)
     part, weights = lax.optimization_barrier((part, weights))
     came = [swap_col(part, partner) for partner in Z_PARTNERS]
     dout, dhid, dback = pl.pallas_call(

time: 40.9 us -> 41.9 us (1.024)
  Pallas kernels: 12.1 us -> 12.8 us
  waiting for transfers between devices: 10.5 us -> 11.1 us
    pallas_call x2 -> x3, Pallas kernels: 1.69 us -> 2.41 us  [the longest x2 2.08 us: turned(): pl.pallas_call(functools.partial(turn_kernel, sizes), out_shape=(shape((d...]
    ppermute x9, waiting for transfers between devices: 10.4 us -> 11 us  [swap_col(): lax.ppermute(block, 'col', [(at, at ^ partner) for at in range(count)])]
  transfers between devices with their start and end apart: 15 -> 15, of which waited for: 6 -> 6; matrix products, arithmetic and copies ran while one was open for 2% -> 2% of each run, Pallas kernels for 20% -> 21%
where the time goes in v9:
time: 41.9 us; the launch traced here: 41.7 us
  starting transfers between devices  15.5 us (37%)
  Pallas kernels  12.8 us (31%)
  waiting for transfers between devices  11.1 us (26%)
  local copies, waits for them, and re-layouts  1.47 us (4%)
  between operations  0.79 us (2%)
    ppermute x9, starting transfers between devices, swap_col(): lax.ppermute(block, 'col', [(at, at ^ partner) for at in range(count)])  14.5 us
    ppermute x9, waiting for transfers between devices, swap_col(): lax.ppermute(block, 'col', [(at, at ^ partner) for at in range(count)])  11 us
    pallas_call x1, Pallas kernels, whole_plan(): pl.pallas_call(functools.partial(transition_kernel, sizes, orders), out_s...  2.41 us
    pallas_call x1, Pallas kernels, whole_plan(): pl.pallas_call(functools.partial(outer_kernel, sizes, orders), out_shape=...  2.12 us
    pallas_call x2, Pallas kernels, turned(): pl.pallas_call(functools.partial(turn_kernel, sizes), out_shape=(shape((d...  2.08 us
    pallas_call x1, Pallas kernels, whole_plan(): pl.pallas_call(functools.partial(projector_kernel, sizes), out_shape=(sha...  1.95 us
    pallas_call x1, Pallas kernels, whole_plan(): pl.pallas_call(pre_kernel, out_shape=(shape((1, rows + 2 * per, pair_widt...  1.93 us
    pallas_call x1, Pallas kernels, whole_plan(): pl.pallas_call(weights_sum_kernel, out_shape=(shape((outer_width, pair_wi...  1.02 us
  transfers between devices with their start and end apart: 15, of which 6 were waited for; matrix products, arithmetic and copies ran while one was open for 2% of the time, Pallas kernels for 21%

profile of v9, /device:TPU:0, one launch (start us, length us, event | category | flops | bytes accessed | tf_op | source)
XLA Modules:
  0.0 41.7 jit_solution(33417154081388781)
XLA Ops:
  0.6 0.1 pad_add_fusion.ids_ref
  0.7 1.9 %project.1 = (bf16[1,272,128]{2,1,0:T(8,128)(2,1)S(1)}, f32[1,256]{1,0:T(1,128)S(1)}, bf16[32,256]{1,0:T(8,128)(2,1)S(1)}, bf16[32,256]{1,0:T(8,128)(2,1)S(1)}, ...) custom-call(s32[2]{0:T(128)S(1)} %pad_add_fusion.ids_ref, ...), custom_call_target="tpu_custom_call" | custom-call | tf_op jit(solution)/shard_map/project/pallas_call | solution.py:811
  2.6 5.1 %collective-permute-start = (bf16[1,272,128]{2,1,0:T(8,128)(2,1)S(1)}, bf16[1,272,128]{2,1,0:T(8,128)(2,1)S(1)}, u32[]{:S(2)}, u32[]{:S(2)}) collective-permute-start(bf16[1,272,128]{2,1,0:T(8,128)(2,1)S(1)} %get-tuple-element.61), channel_id=1, source_target_pairs={{0,6},{1,7},{2,4},{3,5},{4,2},{5,3},{6,0},{7,1},{8,14},{9,15},{10,... | collective-permute-start | bytes 208904 | tf_op jit(solution)/shard_map/ppermute | solution.py:770
  7.8 0.0 collective-permute-start.1
  7.8 0.6 %collective-permute-start.2 = (bf16[1,272,128]{2,1,0:T(8,128)(2,1)S(1)}, bf16[1,272,128]{2,1,0:T(8,128)(2,1)S(1)}, u32[]{:S(2)}, u32[]{:S(2)}) collective-permute-start(bf16[1,272,128]{2,1,0:T(8,128)(2,1)S(1)} %get-tuple-element.61), channel_id=1, source_target_pairs={{0,2},{1,3},{2,0},{3,1},{4,6},{5,7},{6,4},{7,5},{8,10},{9,11},{10,... | collective-permute-start | bytes 208904 | tf_op jit(solution)/shard_map/ppermute | solution.py:770
  8.4 2.0 %collective-permute-done = bf16[1,272,128]{2,1,0:T(8,128)(2,1)S(1)} collective-permute-done((bf16[1,272,128]{2,1,0:T(8,128)(2,1)S(1)}, bf16[1,272,128]{2,1,0:T(8,128)(2,1)S(1)}, u32[]{:S(2)}, u32[]{:S(2)}) %collective-permute-start) | collective-permute-done | bytes 69664 | tf_op jit(solution)/shard_map/ppermute | solution.py:770
  10.4 3.2 %collective-permute-done.1 = bf16[1,272,128]{2,1,0:T(8,128)(2,1)S(1)} collective-permute-done((bf16[1,272,128]{2,1,0:T(8,128)(2,1)S(1)}, bf16[1,272,128]{2,1,0:T(8,128)(2,1)S(1)}, u32[]{:S(2)}, u32[]{:S(2)}) %collective-permute-start.1) | collective-permute-done | bytes 69664 | tf_op jit(solution)/shard_map/ppermute | solution.py:770
  13.7 0.0 collective-permute-done.2
  13.7 0.0 copy-start
  13.7 0.1 collective-permute-start.5
  13.8 1.6 %collective-permute-start.4 = (bf16[4,144,128]{2,1,0:T(8,128)(2,1)S(1)}, bf16[4,144,128]{2,1,0:T(8,128)(2,1)S(1)}, u32[]{:S(2)}, u32[]{:S(2)}) collective-permute-start(bf16[4,144,128]{2,1,0:T(8,128)(2,1)S(1)} %slice.17.mine_ref.near_ref), channel_id=1, source_target_pairs={{0,1},{1,0},{2,3},{3,2},{4,5},{5,4},{6,7},{7,6},{8,9},{9,8},{10,11... | collective-permute-start | bytes 442376 | tf_op jit(solution)/shard_map/ppermute | solution.py:770
  15.4 0.0 collective-permute-done.5.other_ref.other_near_ref
  15.4 1.0 %turned.2 = (bf16[128,512]{1,0:T(8,128)(2,1)S(1)}, bf16[128,512]{1,0:T(8,128)(2,1)S(1)}) custom-call(s32[2]{0:T(128)S(1)} %pad_add_fusion.ids_ref, bf16[4,144,128]{2,1,0:T(8,128)(2,1)S(1)} %slice.17.mine_ref.near_ref, bf16[4,144,128]{2,1,0:T(8,128)(2,1)S(1)} %collective-permute-done.5.other_ref.other_near_ref), custom_call_target="tpu_custom_call" | custom-call | tf_op jit(solution)/shard_map/turned/pallas_call | solution.py:863
  16.5 3.6 %collective-permute-done.4.far_ref.mine_ref = bf16[4,144,128]{2,1,0:T(8,128)(2,1)S(1)} collective-permute-done((bf16[4,144,128]{2,1,0:T(8,128)(2,1)S(1)}, bf16[4,144,128]{2,1,0:T(8,128)(2,1)S(1)}, u32[]{:S(2)}, u32[]{:S(2)}) %collective-permute-start.4) | collective-permute-done | bytes 147488 | tf_op jit(solution)/shard_map/ppermute | solution.py:770
  20.1 0.0 collective-permute-start.6
  20.1 1.6 %collective-permute-start.3 = (bf16[4,128,128]{2,1,0:T(8,128)(2,1)S(1)}, bf16[4,128,128]{2,1,0:T(8,128)(2,1)S(1)}, u32[]{:S(2)}, u32[]{:S(2)}) collective-permute-start(bf16[4,128,128]{2,1,0:T(8,128)(2,1)S(1)} %slice.16.near_ref), channel_id=1, source_target_pairs={{0,1},{1,0},{2,3},{3,2},{4,5},{5,4},{6,7},{7,6},{8,9},{9,8},{10,11... | collective-permute-start | bytes 393224 | tf_op jit(solution)/shard_map/ppermute | solution.py:770
  21.7 0.0 copy-done
  21.7 0.1 copy.19
  21.8 0.0 collective-permute-done.6.other_far_ref.other_ref
  21.8 2.1 %outer_products.1 = (bf16[512,1024]{1,0:T(8,128)(2,1)S(1)}, f32[512,128]{1,0:T(8,128)S(1)}, f32[512,128]{1,0:T(8,128)S(1)}, bf16[512,128]{1,0:T(8,128)(2,1)S(1)}, f32[32,128]{1,0:T(8,128)S(1)}) custom-call(s32[2]{0:T(128)S(1)} %pad_add_fusion.ids_ref, bf16[4,144,128]{2,1,0:T(8,128)(2,1)S(1)} %slice.17.mine_ref.near_ref, ...), custom_call_target="tpu_custom_call" | custom-call | tf_op jit(solution)/shard_map/outer_products/pallas_call | solution.py:882
  23.9 0.0 copy-start.1
  24.0 0.0 copy-start.2
  24.0 1.2 %collective-permute-start.7 = (bf16[256,256]{1,0:T(8,128)(2,1)S(1)}, bf16[256,256]{1,0:T(8,128)(2,1)S(1)}, u32[]{:S(2)}, u32[]{:S(2)}) collective-permute-start(bf16[256,256]{1,0:T(8,128)(2,1)S(1)} %get-tuple-element.78.normed_ref), channel_id=1, source_target_pairs={{0,1},{1,0},{2,3},{3,2},{4,5},{5,4},{6,7},{7,6},{8,9},{9,8},{10,11... | collective-permute-start | bytes 393224 | tf_op jit(solution)/shard_map/ppermute | solution.py:770
  25.2 0.0 collective-permute-start.9
  25.2 1.0 %turned.3 = (bf16[128,512]{1,0:T(8,128)(2,1)S(1)}, bf16[128,512]{1,0:T(8,128)(2,1)S(1)}) custom-call(s32[2]{0:T(128)S(1)} %pad_add_fusion.ids_ref, bf16[4,144,128]{2,1,0:T(8,128)(2,1)S(1)} %collective-permute-done.4.far_ref.mine_ref, bf16[4,144,128]{2,1,0:T(8,128)(2,1)S(1)} %collective-permute-done.6.other_far_ref.other_ref), custom_call_target="tpu_custom_call" | custom-call | tf_op jit(solution)/shard_map/turned/pallas_call | solution.py:863
  26.3 0.0 collective-permute-done.3.far_ref
  26.3 0.0 copy-done.1
  26.3 2.4 %transition.1 = (bf16[64,128]{1,0:T(8,128)(2,1)}, bf16[512,128]{1,0:T(8,128)(2,1)S(1)}, bf16[512,128]{1,0:T(8,128)(2,1)S(1)}, bf16[512,512]{1,0:T(8,128)(2,1)S(1...) custom-call(s32[2]{0:T(128)S(1)} %pad_add_fusion.ids_ref, bf16[4,128,128]{2,1,0:T(8,128)(2,1)S(1)} %slice.16.near_ref, ...), custom_call_target="tpu_custom_call" | custom-call | tf_op jit(solution)/shard_map/transition/pallas_call | solution.py:911
  28.7 1.0 %collective-permute-done.7.far_normed_ref = bf16[256,256]{1,0:T(8,128)(2,1)S(1)} collective-permute-done((bf16[256,256]{1,0:T(8,128)(2,1)S(1)}, bf16[256,256]{1,0:T(8,128)(2,1)S(1)}, u32[]{:S(2)}, u32[]{:S(2)}) %collective-permute-start.7) | collective-permute-done | bytes 131104 | tf_op jit(solution)/shard_map/ppermute | solution.py:770
  29.7 0.0 collective-permute-start.10
  29.7 0.5 %collective-permute-start.8 = (bf16[512,128]{1,0:T(8,128)(2,1)S(1)}, bf16[512,128]{1,0:T(8,128)(2,1)S(1)}, u32[]{:S(2)}, u32[]{:S(2)}) collective-permute-start(bf16[512,128]{1,0:T(8,128)(2,1)S(1)} %get-tuple-element.79.opm_ref), channel_id=1, source_target_pairs={{0,8},{8,0},{1,9},{9,1},{2,10},{10,2},{3,11},{11,3},{4,12},{12,4},... | collective-permute-start | bytes 393224 | tf_op jit(solution)/shard_map/ppermute | solution.py:759
  30.2 0.9 %weight_gradients.1.mine_ref = bf16[2048,128]{1,0:T(8,128)(2,1)S(1)} custom-call(bf16[512,1024]{1,0:T(8,128)(2,1)S(1)} %get-tuple-element.81.outer_ref, bf16[512,128]{1,0:T(8,128)(2,1)S(1)} %get-tuple-element.79.opm_ref, bf16[512,128]{1,0:T(8,128)(2,1)S(1)} %get-tuple-element.82.pn_ref, bf16[512,512]{1,0:T(8,128)(2,1)S(1)} %get-tuple-element.83.gh_ref, ...), custom_call_target="tpu_custom_call" | custom-call | tf_op jit(solution)/shard_map/weight_gradients/pallas_call | solution.py:941
  31.1 0.0 collective-permute-done.9.other_normed_ref
  31.1 0.0 collective-permute-done.10.other_far_normed_ref
  31.1 0.1 collective-permute-done.8.other_opm_ref
  31.2 2.0 %projector_parts.1 = (bf16[64,256]{1,0:T(8,128)(2,1)S(1)}, f32[2,64,128]{2,1,0:T(8,128)S(1)}) custom-call(s32[2]{0:T(128)S(1)} %pad_add_fusion.ids_ref, bf16[512,128]{1,0:T(8,128)(2,1)S(1)} %get-tuple-element.79.opm_ref, bf16[512,128]{1,0:T(8,128)(2,1)S(1)} %collective-permute-done.8.other_opm_ref, bf16[128,512]{1,0:T(8,128)(2,1)S(1)} %get-tuple-element.87.left_near_ref, ...), custom_call_target="tpu_custom_call" | custom-call | tf_op jit(solution)/shard_map/projector_parts/pallas_call | solution.py:953
  33.1 0.3 collective-permute-start.14
  33.5 2.7 %collective-permute-start.11 = (bf16[64,256]{1,0:T(8,128)(2,1)S(1)}, bf16[64,256]{1,0:T(8,128)(2,1)S(1)}, u32[]{:S(2)}, u32[]{:S(2)}) collective-permute-start(bf16[64,256]{1,0:T(8,128)(2,1)S(1)} %get-tuple-element.96), channel_id=1, source_target_pairs={{0,6},{1,7},{2,4},{3,5},{4,2},{5,3},{6,0},{7,1},{8,14},{9,15},{10,... | collective-permute-start | bytes 98312 | tf_op jit(solution)/shard_map/ppermute | solution.py:770
  36.2 0.0 collective-permute-start.12
  36.2 1.7 %collective-permute-start.13 = (bf16[64,256]{1,0:T(8,128)(2,1)S(1)}, bf16[64,256]{1,0:T(8,128)(2,1)S(1)}, u32[]{:S(2)}, u32[]{:S(2)}) collective-permute-start(bf16[64,256]{1,0:T(8,128)(2,1)S(1)} %get-tuple-element.96), channel_id=1, source_target_pairs={{0,2},{1,3},{2,0},{3,1},{4,6},{5,7},{6,4},{7,5},{8,10},{9,11},{10,... | collective-permute-start | bytes 98312 | tf_op jit(solution)/shard_map/ppermute | solution.py:770
  37.9 0.3 features.1
  38.2 0.7 %reshape.44 = bf16[64,4,256]{2,1,0:T(4,128)(2,1)} reshape(bf16[256,256]{1,0:T(8,128)(2,1)S(1)} %features.1) | data formatting | bytes 262144 | tf_op jit(solution)/shard_map/reshape | solution.py:1013
  38.9 0.0 collective-permute-done.14.other_ref
  38.9 1.0 %sums_over_depth.1 = (f32[1024,128]{1,0:T(8,128)}, f32[128,512]{1,0:T(8,128)}, f32[512,128]{1,0:T(8,128)}) custom-call(bf16[2048,128]{1,0:T(8,128)(2,1)S(1)} %weight_gradients.1.mine_ref, bf16[2048,128]{1,0:T(8,128)(2,1)S(1)} %collective-permute-done.14.other_ref), custom_call_target="tpu_custom_call" | custom-call | tf_op jit(solution)/shard_map/sums_over_depth/pallas_call | solution.py:1001
  39.9 0.0 collective-permute-done.11
  39.9 1.1 %collective-permute-done.12 = bf16[64,256]{1,0:T(8,128)(2,1)S(1)} collective-permute-done((bf16[64,256]{1,0:T(8,128)(2,1)S(1)}, bf16[64,256]{1,0:T(8,128)(2,1)S(1)}, u32[]{:S(2)}, u32[]{:S(2)}) %collective-permute-start.12) | collective-permute-done | bytes 32800 | tf_op jit(solution)/shard_map/ppermute | solution.py:770
  41.0 0.0 collective-permute-done.13
  41.1 0.6 %slice_bitcast_fusion = (f32[256,32]{0,1:T(8,128)}, f32[256,32]{0,1:T(8,128)}) fusion(f32[64,256]{1,0:T(8,128)S(1)} %add_add_fusion), kind=kLoop, calls=%fused_computation.2 | loop fusion | bytes 131072 | tf_op jit(solution)/shard_map/transpose | solution.py:1020
  (5 shorter events, 0.1 us)
Async XLA Ops:
  2.6 7.8 %collective-permute-start = (bf16[1,272,128]{2,1,0:T(8,128)(2,1)S(1)}, bf16[1,272,128]{2,1,0:T(8,128)(2,1)S(1)}, u32[]{:S(2)}, u32[]{:S(2)}) collective-permute-start(bf16[1,272,128]{2,1,0:T(8,128)(2,1)S(1)} %get-tuple-element.61), channel_id=1, source_target_pairs={{0,6},{1,7},{2,4},{3,5},{4,2},{5,3},{6,0},{7,1},{8,14},{9,15},{10,... | collective-permute-start | bytes 208904 | tf_op jit(solution)/shard_map/ppermute | solution.py:770
  7.8 5.9 %collective-permute-start.1 = (bf16[1,272,128]{2,1,0:T(8,128)(2,1)S(1)}, bf16[1,272,128]{2,1,0:T(8,128)(2,1)S(1)}, u32[]{:S(2)}, u32[]{:S(2)}) collective-permute-start(bf16[1,272,128]{2,1,0:T(8,128)(2,1)S(1)} %get-tuple-element.61), channel_id=1, source_target_pairs={{0,4},{1,5},{2,6},{3,7},{4,0},{5,1},{6,2},{7,3},{8,12},{9,13},{10,... | collective-permute-start | bytes 208904 | tf_op jit(solution)/shard_map/ppermute | solution.py:770
  7.8 5.9 %collective-permute-start.2 = (bf16[1,272,128]{2,1,0:T(8,128)(2,1)S(1)}, bf16[1,272,128]{2,1,0:T(8,128)(2,1)S(1)}, u32[]{:S(2)}, u32[]{:S(2)}) collective-permute-start(bf16[1,272,128]{2,1,0:T(8,128)(2,1)S(1)} %get-tuple-element.61), channel_id=1, source_target_pairs={{0,2},{1,3},{2,0},{3,1},{4,6},{5,7},{6,4},{7,5},{8,10},{9,11},{10,... | collective-permute-start | bytes 208904 | tf_op jit(solution)/shard_map/ppermute | solution.py:770
  13.7 8.0 %copy-start = (bf16[1024,128]{1,0:T(8,128)(2,1)S(1)}, bf16[1024,128]{1,0:T(8,128)(2,1)}, u32[]{:S(2)}) copy-start(bf16[1024,128]{1,0:T(8,128)(2,1)} %wout_ref.1) | copy-start | bytes 786436
  13.7 1.7 %collective-permute-start.5 = (bf16[4,144,128]{2,1,0:T(8,128)(2,1)S(1)}, bf16[4,144,128]{2,1,0:T(8,128)(2,1)S(1)}, u32[]{:S(2)}, u32[]{:S(2)}) collective-permute-start(bf16[4,144,128]{2,1,0:T(8,128)(2,1)S(1)} %slice.17.mine_ref.near_ref), channel_id=1, source_target_pairs={{0,8},{8,0},{1,9},{9,1},{2,10},{10,2},{3,11},{11,3},{4,12},{12,4},... | collective-permute-start | bytes 442376 | tf_op jit(solution)/shard_map/ppermute | solution.py:759
  13.8 6.3 %collective-permute-start.4 = (bf16[4,144,128]{2,1,0:T(8,128)(2,1)S(1)}, bf16[4,144,128]{2,1,0:T(8,128)(2,1)S(1)}, u32[]{:S(2)}, u32[]{:S(2)}) collective-permute-start(bf16[4,144,128]{2,1,0:T(8,128)(2,1)S(1)} %slice.17.mine_ref.near_ref), channel_id=1, source_target_pairs={{0,1},{1,0},{2,3},{3,2},{4,5},{5,4},{6,7},{7,6},{8,9},{9,8},{10,11... | collective-permute-start | bytes 442376 | tf_op jit(solution)/shard_map/ppermute | solution.py:770
  20.1 1.7 %collective-permute-start.6 = (bf16[4,144,128]{2,1,0:T(8,128)(2,1)S(1)}, bf16[4,144,128]{2,1,0:T(8,128)(2,1)S(1)}, u32[]{:S(2)}, u32[]{:S(2)}) collective-permute-start(bf16[4,144,128]{2,1,0:T(8,128)(2,1)S(1)} %collective-permute-done.4.far_ref.mine_ref), channel_id=1, source_target_pairs={{0,8},{8,0},{1,9},{9,1},{2,10},{10,2},{3,11},{11,3},{4,12},{12,4},... | collective-permute-start | bytes 442376 | tf_op jit(solution)/shard_map/ppermute | solution.py:759
  20.1 6.2 %collective-permute-start.3 = (bf16[4,128,128]{2,1,0:T(8,128)(2,1)S(1)}, bf16[4,128,128]{2,1,0:T(8,128)(2,1)S(1)}, u32[]{:S(2)}, u32[]{:S(2)}) collective-permute-start(bf16[4,128,128]{2,1,0:T(8,128)(2,1)S(1)} %slice.16.near_ref), channel_id=1, source_target_pairs={{0,1},{1,0},{2,3},{3,2},{4,5},{5,4},{6,7},{7,6},{8,9},{9,8},{10,11... | collective-permute-start | bytes 393224 | tf_op jit(solution)/shard_map/ppermute | solution.py:770
  23.9 2.3 %copy-start.1 = (bf16[128,512]{1,0:T(8,128)(2,1)S(1)}, bf16[128,512]{1,0:T(8,128)(2,1)}, u32[]{:S(2)}) copy-start(bf16[128,512]{1,0:T(8,128)(2,1)} %hid_ref.1) | copy-start | bytes 393220
  24.0 2.3 %copy-start.2 = (bf16[512,128]{1,0:T(8,128)(2,1)S(1)}, bf16[512,128]{1,0:T(8,128)(2,1)}, u32[]{:S(2)}) copy-start(bf16[512,128]{1,0:T(8,128)(2,1)} %back_ref.1) | copy-start | bytes 393220
  24.0 5.7 %collective-permute-start.7 = (bf16[256,256]{1,0:T(8,128)(2,1)S(1)}, bf16[256,256]{1,0:T(8,128)(2,1)S(1)}, u32[]{:S(2)}, u32[]{:S(2)}) collective-permute-start(bf16[256,256]{1,0:T(8,128)(2,1)S(1)} %get-tuple-element.78.normed_ref), channel_id=1, source_target_pairs={{0,1},{1,0},{2,3},{3,2},{4,5},{5,4},{6,7},{7,6},{8,9},{9,8},{10,11... | collective-permute-start | bytes 393224 | tf_op jit(solution)/shard_map/ppermute | solution.py:770
  25.2 5.9 %collective-permute-start.9 = (bf16[256,256]{1,0:T(8,128)(2,1)S(1)}, bf16[256,256]{1,0:T(8,128)(2,1)S(1)}, u32[]{:S(2)}, u32[]{:S(2)}) collective-permute-start(bf16[256,256]{1,0:T(8,128)(2,1)S(1)} %get-tuple-element.78.normed_ref), channel_id=1, source_target_pairs={{0,8},{8,0},{1,9},{9,1},{2,10},{10,2},{3,11},{11,3},{4,12},{12,4},... | collective-permute-start | bytes 393224 | tf_op jit(solution)/shard_map/ppermute | solution.py:759
  29.7 1.4 %collective-permute-start.10 = (bf16[256,256]{1,0:T(8,128)(2,1)S(1)}, bf16[256,256]{1,0:T(8,128)(2,1)S(1)}, u32[]{:S(2)}, u32[]{:S(2)}) collective-permute-start(bf16[256,256]{1,0:T(8,128)(2,1)S(1)} %collective-permute-done.7.far_normed_ref), channel_id=1, source_target_pairs={{0,8},{8,0},{1,9},{9,1},{2,10},{10,2},{3,11},{11,3},{4,12},{12,4},... | collective-permute-start | bytes 393224 | tf_op jit(solution)/shard_map/ppermute | solution.py:759
  29.7 1.5 %collective-permute-start.8 = (bf16[512,128]{1,0:T(8,128)(2,1)S(1)}, bf16[512,128]{1,0:T(8,128)(2,1)S(1)}, u32[]{:S(2)}, u32[]{:S(2)}) collective-permute-start(bf16[512,128]{1,0:T(8,128)(2,1)S(1)} %get-tuple-element.79.opm_ref), channel_id=1, source_target_pairs={{0,8},{8,0},{1,9},{9,1},{2,10},{10,2},{3,11},{11,3},{4,12},{12,4},... | collective-permute-start | bytes 393224 | tf_op jit(solution)/shard_map/ppermute | solution.py:759
  33.1 5.8 %collective-permute-start.14 = (bf16[2048,128]{1,0:T(8,128)(2,1)S(1)}, bf16[2048,128]{1,0:T(8,128)(2,1)S(1)}, u32[]{:S(2)}, u32[]{:S(2)}) collective-permute-start(bf16[2048,128]{1,0:T(8,128)(2,1)S(1)} %weight_gradients.1.mine_ref), channel_id=1, source_target_pairs={{0,8},{8,0},{1,9},{9,1},{2,10},{10,2},{3,11},{11,3},{4,12},{12,4},... | collective-permute-start | bytes 1572872 | tf_op jit(solution)/shard_map/ppermute | solution.py:759
  33.5 6.4 %collective-permute-start.11 = (bf16[64,256]{1,0:T(8,128)(2,1)S(1)}, bf16[64,256]{1,0:T(8,128)(2,1)S(1)}, u32[]{:S(2)}, u32[]{:S(2)}) collective-permute-start(bf16[64,256]{1,0:T(8,128)(2,1)S(1)} %get-tuple-element.96), channel_id=1, source_target_pairs={{0,6},{1,7},{2,4},{3,5},{4,2},{5,3},{6,0},{7,1},{8,14},{9,15},{10,... | collective-permute-start | bytes 98312 | tf_op jit(solution)/shard_map/ppermute | solution.py:770
  36.2 4.8 %collective-permute-start.12 = (bf16[64,256]{1,0:T(8,128)(2,1)S(1)}, bf16[64,256]{1,0:T(8,128)(2,1)S(1)}, u32[]{:S(2)}, u32[]{:S(2)}) collective-permute-start(bf16[64,256]{1,0:T(8,128)(2,1)S(1)} %get-tuple-element.96), channel_id=1, source_target_pairs={{0,4},{1,5},{2,6},{3,7},{4,0},{5,1},{6,2},{7,3},{8,12},{9,13},{10,... | collective-permute-start | bytes 98312 | tf_op jit(solution)/shard_map/ppermute | solution.py:770
  36.2 4.8 %collective-permute-start.13 = (bf16[64,256]{1,0:T(8,128)(2,1)S(1)}, bf16[64,256]{1,0:T(8,128)(2,1)S(1)}, u32[]{:S(2)}, u32[]{:S(2)}) collective-permute-start(bf16[64,256]{1,0:T(8,128)(2,1)S(1)} %get-tuple-element.96), channel_id=1, source_target_pairs={{0,2},{1,3},{2,0},{3,1},{4,6},{5,7},{6,4},{7,5},{8,10},{9,11},{10,... | collective-permute-start | bytes 98312 | tf_op jit(solution)/shard_map/ppermute | solution.py:770

commit v10 on v8

--- a/solution.py
+++ b/solution.py
@@ -730,6 +730,17 @@
     ).astype(jnp.bfloat16)
 
 
+def swap_line(block, partners):
+    count = lax.axis_size("col")
+    pairs = [
+        (depth * count + at, depth * count + (at ^ partner))
+        for depth, partner in enumerate(partners)
+        if partner is not None
+        for at in range(count)
+    ]
+    return lax.ppermute(block, ("depth", "col"), pairs)
+
+
 def swap_depth(block):
     return lax.ppermute(block, "depth", [(0, 1), (1, 0)])
 
@@ -828,9 +839,14 @@
     blocks = lax.optimization_barrier(
         jnp.concatenate([sent] + [swap_col(sent, partner) for partner in Z_PARTNERS])
     )
+    half_normed = seqs * res // 2
+    far_normed_a = swap_col(normed[:half_normed], Y_PARTNER)
+    blocks, far_normed_a = lax.optimization_barrier((blocks, far_normed_a))
     near, pair_near = blocks[:, :rows], blocks[:, rows:]
     far = swap_col(near, Y_PARTNER)
     pair_far = swap_col(pair_near, Y_PARTNER)
+    far, normed_b = lax.optimization_barrier((far, normed[half_normed:]))
+    far_normed_b = swap_col(normed_b, Y_PARTNER)
     other_near, other_far = swap_depth(near), swap_depth(far)
     sizes = (seqs, res, pair_cols, width)
     orders = (near_order, far_order)
@@ -856,8 +872,6 @@
         compiler_params=params,
         name="outer_products",
     )(ids, near, far, other_near, other_far, wturn)
-    normed, proj_out = lax.optimization_barrier((normed, proj_out))
-    far_normed = swap_col(normed, Y_PARTNER)
     other_near, other_far, proj_out = lax.optimization_barrier((other_near, other_far, proj_out))
     rightt, leftt = pl.pallas_call(
         functools.partial(turn_kernel, sizes, orders),
@@ -906,7 +920,8 @@
         hidden_weight,
         back_weight,
     )
-    opm, far_normed = lax.optimization_barrier((opm, far_normed))
+    opm, far_normed_b = lax.optimization_barrier((opm, far_normed_b))
+    far_normed = jnp.concatenate([far_normed_a, far_normed_b])
     weights = pl.pallas_call(
         weights_kernel,
         out_shape=shape((outer_width + 2 * hid, pair_width), bf16),
@@ -961,7 +976,6 @@
         name="features",
     )(spread, first, second, scale, scaled, inv)
     part, weights = lax.optimization_barrier((part, weights))
-    came = [swap_col(part, partner) for partner in Z_PARTNERS]
     dout, dhid, dback = pl.pallas_call(
         weights_sum_kernel,
         out_shape=(
@@ -974,9 +988,15 @@
         compiler_params=params,
         name="sums_over_depth",
     )(weights, swap_depth(weights))
+    came_a = swap_line(part, Z_PARTNERS[:2])
+    came_b = swap_line(part, (None, Z_PARTNERS[2]))
     feat = feat.reshape(seqs, res, channels)
-    came, feat, dout, dhid, dback = lax.optimization_barrier((came, feat, dout, dhid, dback))
-    total = pairwise_sum([block.astype(f32) for block in [part] + came])
+    came_a, came_b, feat = lax.optimization_barrier((came_a, came_b, feat))
+    kept = jnp.where(lax.axis_index("depth") == 0, part, came_b)
+    kept = lax.optimization_barrier((kept.astype(f32) + came_a.astype(f32)).astype(bf16))
+    came = swap_depth(kept)
+    came, dout, dhid, dback = lax.optimization_barrier((came, dout, dhid, dback))
+    total = kept.astype(f32) + came.astype(f32)
     return (
         feat,
         couple.reshape(res, pair_cols, pair_width),

time: 40.9 us -> 40 us (0.978)
  waiting for transfers between devices: 10.5 us -> 9.2 us
    ppermute x9 -> x7, starting transfers between devices: 14.8 us -> 11.3 us  [swap_col(): lax.ppermute(block, 'col', [(at, at ^ partner) for at in range(count)])]
    ppermute x0 -> x2, starting transfers between devices: none -> 3.17 us  [swap_line(): return lax.ppermute(block, ('depth', 'col'), pairs)]
    ppermute x9 -> x7, waiting for transfers between devices: 10.4 us -> 7.58 us  [swap_col(): lax.ppermute(block, 'col', [(at, at ^ partner) for at in range(count)])]
    ppermute x0 -> x2, waiting for transfers between devices: none -> 1.52 us  [swap_line(): return lax.ppermute(block, ('depth', 'col'), pairs)]
    ppermute x6 -> x7, starting transfers between devices: 0.91 us -> 1.48 us  [swap_depth(): return lax.ppermute(block, 'depth', [(0, 1), (1, 0)])]
  transfers between devices with their start and end apart: 15 -> 16, of which waited for: 6 -> 6; matrix products, arithmetic and copies ran while one was open for 2% -> 2% of each run, Pallas kernels for 20% -> 21%
where the time goes in v10:
time: 40 us; the launch traced here: 39.7 us
  starting transfers between devices  16 us (40%)
  Pallas kernels  12.1 us (30%)
  waiting for transfers between devices  9.2 us (23%)
  local copies, waits for them, and re-layouts  1.49 us (4%)
  between operations  0.81 us (2%)
    ppermute x7, starting transfers between devices, swap_col(): lax.ppermute(block, 'col', [(at, at ^ partner) for at in range(count)])  11.3 us
    ppermute x7, waiting for transfers between devices, swap_col(): lax.ppermute(block, 'col', [(at, at ^ partner) for at in range(count)])  7.58 us
    ppermute x2, starting transfers between devices, swap_line(): return lax.ppermute(block, ('depth', 'col'), pairs)  3.17 us
    pallas_call x1, Pallas kernels, whole_plan(): pl.pallas_call(functools.partial(transition_kernel, sizes, orders), out_s...  2.41 us
    pallas_call x1, Pallas kernels, whole_plan(): pl.pallas_call(functools.partial(outer_kernel, sizes, orders), out_shape=...  2.11 us
    pallas_call x1, Pallas kernels, whole_plan(): pl.pallas_call(functools.partial(projector_kernel, sizes), out_shape=(sha...  2.03 us
    pallas_call x1, Pallas kernels, whole_plan(): pl.pallas_call(pre_kernel, out_shape=(shape((1, rows + 2 * per, pair_widt...  1.91 us
    ppermute x2, waiting for transfers between devices, swap_line(): return lax.ppermute(block, ('depth', 'col'), pairs)  1.52 us
  transfers between devices with their start and end apart: 16, of which 6 were waited for; matrix products, arithmetic and copies ran while one was open for 2% of the time, Pallas kernels for 21%

profile of v10, /device:TPU:0, one launch (start us, length us, event | category | flops | bytes accessed | tf_op | source)
XLA Modules:
  0.0 39.7 jit_solution(10896076776472936902)
XLA Ops:
  0.6 0.1 pad_add_fusion.ids_ref
  0.7 1.9 %project.1 = (bf16[1,272,128]{2,1,0:T(8,128)(2,1)S(1)}, f32[1,256]{1,0:T(1,128)S(1)}, bf16[32,256]{1,0:T(8,128)(2,1)S(1)}, bf16[32,256]{1,0:T(8,128)(2,1)S(1)}, ...) custom-call(s32[2]{0:T(128)S(1)} %pad_add_fusion.ids_ref, ...), custom_call_target="tpu_custom_call" | custom-call | tf_op jit(solution)/shard_map/project/pallas_call | solution.py:796
  2.6 5.1 %collective-permute-start = (bf16[1,272,128]{2,1,0:T(8,128)(2,1)S(1)}, bf16[1,272,128]{2,1,0:T(8,128)(2,1)S(1)}, u32[]{:S(2)}, u32[]{:S(2)}) collective-permute-start(bf16[1,272,128]{2,1,0:T(8,128)(2,1)S(1)} %get-tuple-element.59), channel_id=1, source_target_pairs={{0,6},{1,7},{2,4},{3,5},{4,2},{5,3},{6,0},{7,1},{8,14},{9,15},{10,... | collective-permute-start | bytes 208904 | tf_op jit(solution)/shard_map/ppermute | solution.py:756
  7.7 0.0 collective-permute-start.1
  7.8 0.6 %collective-permute-start.2 = (bf16[1,272,128]{2,1,0:T(8,128)(2,1)S(1)}, bf16[1,272,128]{2,1,0:T(8,128)(2,1)S(1)}, u32[]{:S(2)}, u32[]{:S(2)}) collective-permute-start(bf16[1,272,128]{2,1,0:T(8,128)(2,1)S(1)} %get-tuple-element.59), channel_id=1, source_target_pairs={{0,2},{1,3},{2,0},{3,1},{4,6},{5,7},{6,4},{7,5},{8,10},{9,11},{10,... | collective-permute-start | bytes 208904 | tf_op jit(solution)/shard_map/ppermute | solution.py:756
  8.4 1.7 %collective-permute-start.3 = (bf16[128,256]{1,0:T(8,128)(2,1)S(1)}, bf16[128,256]{1,0:T(8,128)(2,1)S(1)}, u32[]{:S(2)}, u32[]{:S(2)}) collective-permute-start(bf16[128,256]{1,0:T(8,128)(2,1)S(1)} %get-tuple-element.112), channel_id=1, source_target_pairs={{0,1},{1,0},{2,3},{3,2},{4,5},{5,4},{6,7},{7,6},{8,9},{9,8},{10,11... | collective-permute-start | bytes 196616 | tf_op jit(solution)/shard_map/ppermute | solution.py:756
  10.1 0.3 collective-permute-done
  10.4 3.2 %collective-permute-done.1 = bf16[1,272,128]{2,1,0:T(8,128)(2,1)S(1)} collective-permute-done((bf16[1,272,128]{2,1,0:T(8,128)(2,1)S(1)}, bf16[1,272,128]{2,1,0:T(8,128)(2,1)S(1)}, u32[]{:S(2)}, u32[]{:S(2)}) %collective-permute-start.1) | collective-permute-done | bytes 69664 | tf_op jit(solution)/shard_map/ppermute | solution.py:756
  13.7 0.0 collective-permute-done.2
  13.7 0.0 copy-start
  13.7 0.0 collective-permute-done.3
  13.7 1.6 %collective-permute-start.5 = (bf16[4,144,128]{2,1,0:T(8,128)(2,1)S(1)}, bf16[4,144,128]{2,1,0:T(8,128)(2,1)S(1)}, u32[]{:S(2)}, u32[]{:S(2)}) collective-permute-start(bf16[4,144,128]{2,1,0:T(8,128)(2,1)S(1)} %slice.20.near_ref), channel_id=1, source_target_pairs={{0,1},{1,0},{2,3},{3,2},{4,5},{5,4},{6,7},{7,6},{8,9},{9,8},{10,11... | collective-permute-start | bytes 442376 | tf_op jit(solution)/shard_map/ppermute | solution.py:756
  15.3 0.0 collective-permute-start.6
  15.3 3.8 %collective-permute-done.5.far_ref = bf16[4,144,128]{2,1,0:T(8,128)(2,1)S(1)} collective-permute-done((bf16[4,144,128]{2,1,0:T(8,128)(2,1)S(1)}, bf16[4,144,128]{2,1,0:T(8,128)(2,1)S(1)}, u32[]{:S(2)}, u32[]{:S(2)}) %collective-permute-start.5) | collective-permute-done | bytes 147488 | tf_op jit(solution)/shard_map/ppermute | solution.py:756
  19.2 0.0 collective-permute-start.7
  19.2 1.8 %collective-permute-start.4 = (bf16[4,128,128]{2,1,0:T(8,128)(2,1)S(1)}, bf16[4,128,128]{2,1,0:T(8,128)(2,1)S(1)}, u32[]{:S(2)}, u32[]{:S(2)}) collective-permute-start(bf16[4,128,128]{2,1,0:T(8,128)(2,1)S(1)} %slice.19.near_ref), channel_id=1, source_target_pairs={{0,1},{1,0},{2,3},{3,2},{4,5},{5,4},{6,7},{7,6},{8,9},{9,8},{10,11... | collective-permute-start | bytes 393224 | tf_op jit(solution)/shard_map/ppermute | solution.py:756
  21.0 0.2 collective-permute-start.10
  21.2 0.0 copy-done
  21.2 0.1 copy.19
  21.3 0.4 %collective-permute-start.8 = (bf16[128,256]{1,0:T(8,128)(2,1)S(1)}, bf16[128,256]{1,0:T(8,128)(2,1)S(1)}, u32[]{:S(2)}, u32[]{:S(2)}) collective-permute-start(bf16[128,256]{1,0:T(8,128)(2,1)S(1)} %get-tuple-element.75), channel_id=1, source_target_pairs={{0,1},{1,0},{2,3},{3,2},{4,5},{5,4},{6,7},{7,6},{8,9},{9,8},{10,11... | collective-permute-start | bytes 196616 | tf_op jit(solution)/shard_map/ppermute | solution.py:756
  21.7 0.0 collective-permute-done.6.other_near_ref
  21.7 0.0 collective-permute-done.7.other_far_ref
  21.8 2.1 %outer_products.1 = (bf16[512,1024]{1,0:T(8,128)(2,1)S(1)}, f32[512,128]{1,0:T(8,128)S(1)}, f32[512,128]{1,0:T(8,128)S(1)}, bf16[512,128]{1,0:T(8,128)(2,1)S(1)}, f32[32,128]{1,0:T(8,128)S(1)}) custom-call(s32[2]{0:T(128)S(1)} %pad_add_fusion.ids_ref, bf16[4,144,128]{2,1,0:T(8,128)(2,1)S(1)} %slice.20.near_ref, ...), custom_call_target="tpu_custom_call" | custom-call | tf_op jit(solution)/shard_map/outer_products/pallas_call | solution.py:853
  23.9 0.0 copy-start.1
  23.9 0.0 copy-start.2
  23.9 1.4 %turned.1 = (bf16[1024,128]{1,0:T(8,128)(2,1)S(1)}, bf16[1024,128]{1,0:T(8,128)(2,1)S(1)}) custom-call(s32[2]{0:T(128)S(1)} %pad_add_fusion.ids_ref, bf16[4,144,128]{2,1,0:T(8,128)(2,1)S(1)} %slice.20.near_ref, bf16[4,144,128]{2,1,0:T(8,128)(2,1)S(1)} %collective-permute-done.5.far_ref, bf16[4,144,128]{2,1,0:T(8,128)(2,1)S(1)} %collective-permute-done.6.other_near_ref, ...), custom_call_target="tpu_custom_call" | custom-call | tf_op jit(solution)/shard_map/turned/pallas_call | solution.py:876
  25.3 0.2 collective-permute-done.4.far_ref
  25.5 2.4 %transition.1 = (bf16[64,128]{1,0:T(8,128)(2,1)}, bf16[512,128]{1,0:T(8,128)(2,1)S(1)}, bf16[512,128]{1,0:T(8,128)(2,1)S(1)}, bf16[512,512]{1,0:T(8,128)(2,1)S(1...) custom-call(s32[2]{0:T(128)S(1)} %pad_add_fusion.ids_ref, bf16[4,128,128]{2,1,0:T(8,128)(2,1)S(1)} %slice.19.near_ref, ...), custom_call_target="tpu_custom_call" | custom-call | tf_op jit(solution)/shard_map/transition/pallas_call | solution.py:894
  27.9 0.0 collective-permute-done.8
  28.0 0.1 collective-permute-start.11
  28.0 0.5 %collective-permute-start.9 = (bf16[512,128]{1,0:T(8,128)(2,1)S(1)}, bf16[512,128]{1,0:T(8,128)(2,1)S(1)}, u32[]{:S(2)}, u32[]{:S(2)}) collective-permute-start(bf16[512,128]{1,0:T(8,128)(2,1)S(1)} %get-tuple-element.76.opm_ref), channel_id=1, source_target_pairs={{0,8},{8,0},{1,9},{9,1},{2,10},{10,2},{3,11},{11,3},{4,12},{12,4},... | collective-permute-start | bytes 393224 | tf_op jit(solution)/shard_map/ppermute | solution.py:745
  28.5 0.9 %weight_gradients.1.mine_ref = bf16[2048,128]{1,0:T(8,128)(2,1)S(1)} custom-call(bf16[512,1024]{1,0:T(8,128)(2,1)S(1)} %get-tuple-element.79.outer_ref, bf16[512,128]{1,0:T(8,128)(2,1)S(1)} %get-tuple-element.76.opm_ref, bf16[512,128]{1,0:T(8,128)(2,1)S(1)} %get-tuple-element.80.pn_ref, bf16[512,512]{1,0:T(8,128)(2,1)S(1)} %get-tuple-element.81.gh_ref, ...), custom_call_target="tpu_custom_call" | custom-call | tf_op jit(solution)/shard_map/weight_gradients/pallas_call | solution.py:925
  29.5 0.0 collective-permute-done.10.other_normed_ref
  29.5 0.0 collective-permute-done.11.other_far_normed_ref
  29.5 0.1 collective-permute-done.9.other_opm_ref
  29.6 2.0 %projector_parts.1 = (bf16[64,256]{1,0:T(8,128)(2,1)S(1)}, bf16[256,256]{1,0:T(8,128)(2,1)S(1)}) custom-call(s32[2]{0:T(128)S(1)} %pad_add_fusion.ids_ref, bf16[512,128]{1,0:T(8,128)(2,1)S(1)} %get-tuple-element.76.opm_ref, bf16[512,128]{1,0:T(8,128)(2,1)S(1)} %collective-permute-done.9.other_opm_ref, bf16[1024,128]{1,0:T(8,128)(2,1)S(1)} %get-tuple-element.85.rightt_ref, ...), custom_call_target="tpu_custom_call" | custom-call | tf_op jit(solution)/shard_map/projector_parts/pallas_call | solution.py:937
  31.6 0.4 %collective-permute-start.15 = (bf16[2048,128]{1,0:T(8,128)(2,1)S(1)}, bf16[2048,128]{1,0:T(8,128)(2,1)S(1)}, u32[]{:S(2)}, u32[]{:S(2)}) collective-permute-start(bf16[2048,128]{1,0:T(8,128)(2,1)S(1)} %weight_gradients.1.mine_ref), channel_id=1, source_target_pairs={{0,8},{8,0},{1,9},{9,1},{2,10},{10,2},{3,11},{11,3},{4,12},{12,4},... | collective-permute-start | bytes 1572872 | tf_op jit(solution)/shard_map/ppermute | solution.py:745
  32.0 2.5 %collective-permute-start.12 = (bf16[64,256]{1,0:T(8,128)(2,1)S(1)}, bf16[64,256]{1,0:T(8,128)(2,1)S(1)}, u32[]{:S(2)}, u32[]{:S(2)}) collective-permute-start(bf16[64,256]{1,0:T(8,128)(2,1)S(1)} %get-tuple-element.92), channel_id=1, source_target_pairs={{0,6},{1,7},{2,4},{3,5},{4,2},{5,3},{6,0},{7,1},{8,12},{9,13},{10,... | collective-permute-start | bytes 98312 | tf_op jit(solution)/shard_map/ppermute | solution.py:741
  34.5 0.7 %collective-permute-start.13 = (bf16[64,256]{1,0:T(8,128)(2,1)S(1)}, bf16[64,256]{1,0:T(8,128)(2,1)S(1)}, u32[]{:S(2)}, u32[]{:S(2)}) collective-permute-start(bf16[64,256]{1,0:T(8,128)(2,1)S(1)} %get-tuple-element.92), channel_id=1, source_target_pairs={{8,10},{9,11},{10,8},{11,9},{12,14},{13,15},{14,12},{15,13},{24,26... | collective-permute-start | bytes 98312 | tf_op jit(solution)/shard_map/ppermute | solution.py:741
  35.2 0.3 features.1
  35.5 0.7 %reshape.44 = bf16[64,4,256]{2,1,0:T(4,128)(2,1)} reshape(bf16[256,256]{1,0:T(8,128)(2,1)S(1)} %features.1) | data formatting | bytes 262144 | tf_op jit(solution)/shard_map/reshape | solution.py:993
  36.2 1.5 %collective-permute-done.12 = bf16[64,256]{1,0:T(8,128)(2,1)S(1)} collective-permute-done((bf16[64,256]{1,0:T(8,128)(2,1)S(1)}, bf16[64,256]{1,0:T(8,128)(2,1)S(1)}, u32[]{:S(2)}, u32[]{:S(2)}) %collective-permute-start.12) | collective-permute-done | bytes 32800 | tf_op jit(solution)/shard_map/ppermute | solution.py:741
  37.7 0.0 collective-permute-done.13
  37.8 0.3 collective-permute-start.14
  38.0 0.0 collective-permute-done.15.other_ref
  38.0 1.0 %sums_over_depth.1 = (f32[1024,128]{1,0:T(8,128)}, f32[128,512]{1,0:T(8,128)}, f32[512,128]{1,0:T(8,128)}) custom-call(bf16[2048,128]{1,0:T(8,128)(2,1)S(1)} %weight_gradients.1.mine_ref, bf16[2048,128]{1,0:T(8,128)(2,1)S(1)} %collective-permute-done.15.other_ref), custom_call_target="tpu_custom_call" | custom-call | tf_op jit(solution)/shard_map/sums_over_depth/pallas_call | solution.py:979
  39.0 0.0 collective-permute-done.14
  39.1 0.6 %slice_bitcast_fusion = (f32[256,32]{0,1:T(8,128)}, f32[256,32]{0,1:T(8,128)}) fusion(f32[64,256]{1,0:T(8,128)S(1)} %convert_add_fusion), kind=kLoop, calls=%fused_computation.3 | loop fusion | bytes 131072 | tf_op jit(solution)/shard_map/transpose | solution.py:1004
  (10 shorter events, 0.1 us)
Async XLA Ops:
  2.6 7.8 %collective-permute-start = (bf16[1,272,128]{2,1,0:T(8,128)(2,1)S(1)}, bf16[1,272,128]{2,1,0:T(8,128)(2,1)S(1)}, u32[]{:S(2)}, u32[]{:S(2)}) collective-permute-start(bf16[1,272,128]{2,1,0:T(8,128)(2,1)S(1)} %get-tuple-element.59), channel_id=1, source_target_pairs={{0,6},{1,7},{2,4},{3,5},{4,2},{5,3},{6,0},{7,1},{8,14},{9,15},{10,... | collective-permute-start | bytes 208904 | tf_op jit(solution)/shard_map/ppermute | solution.py:756
  7.7 5.9 %collective-permute-start.1 = (bf16[1,272,128]{2,1,0:T(8,128)(2,1)S(1)}, bf16[1,272,128]{2,1,0:T(8,128)(2,1)S(1)}, u32[]{:S(2)}, u32[]{:S(2)}) collective-permute-start(bf16[1,272,128]{2,1,0:T(8,128)(2,1)S(1)} %get-tuple-element.59), channel_id=1, source_target_pairs={{0,4},{1,5},{2,6},{3,7},{4,0},{5,1},{6,2},{7,3},{8,12},{9,13},{10,... | collective-permute-start | bytes 208904 | tf_op jit(solution)/shard_map/ppermute | solution.py:756
  7.8 5.9 %collective-permute-start.2 = (bf16[1,272,128]{2,1,0:T(8,128)(2,1)S(1)}, bf16[1,272,128]{2,1,0:T(8,128)(2,1)S(1)}, u32[]{:S(2)}, u32[]{:S(2)}) collective-permute-start(bf16[1,272,128]{2,1,0:T(8,128)(2,1)S(1)} %get-tuple-element.59), channel_id=1, source_target_pairs={{0,2},{1,3},{2,0},{3,1},{4,6},{5,7},{6,4},{7,5},{8,10},{9,11},{10,... | collective-permute-start | bytes 208904 | tf_op jit(solution)/shard_map/ppermute | solution.py:756
  8.4 5.3 %collective-permute-start.3 = (bf16[128,256]{1,0:T(8,128)(2,1)S(1)}, bf16[128,256]{1,0:T(8,128)(2,1)S(1)}, u32[]{:S(2)}, u32[]{:S(2)}) collective-permute-start(bf16[128,256]{1,0:T(8,128)(2,1)S(1)} %get-tuple-element.112), channel_id=1, source_target_pairs={{0,1},{1,0},{2,3},{3,2},{4,5},{5,4},{6,7},{7,6},{8,9},{9,8},{10,11... | collective-permute-start | bytes 196616 | tf_op jit(solution)/shard_map/ppermute | solution.py:756
  13.7 7.5 %copy-start = (bf16[1024,128]{1,0:T(8,128)(2,1)S(1)}, bf16[1024,128]{1,0:T(8,128)(2,1)}, u32[]{:S(2)}) copy-start(bf16[1024,128]{1,0:T(8,128)(2,1)} %wout_ref.1) | copy-start | bytes 786436
  13.7 5.4 %collective-permute-start.5 = (bf16[4,144,128]{2,1,0:T(8,128)(2,1)S(1)}, bf16[4,144,128]{2,1,0:T(8,128)(2,1)S(1)}, u32[]{:S(2)}, u32[]{:S(2)}) collective-permute-start(bf16[4,144,128]{2,1,0:T(8,128)(2,1)S(1)} %slice.20.near_ref), channel_id=1, source_target_pairs={{0,1},{1,0},{2,3},{3,2},{4,5},{5,4},{6,7},{7,6},{8,9},{9,8},{10,11... | collective-permute-start | bytes 442376 | tf_op jit(solution)/shard_map/ppermute | solution.py:756
  15.3 6.4 %collective-permute-start.6 = (bf16[4,144,128]{2,1,0:T(8,128)(2,1)S(1)}, bf16[4,144,128]{2,1,0:T(8,128)(2,1)S(1)}, u32[]{:S(2)}, u32[]{:S(2)}) collective-permute-start(bf16[4,144,128]{2,1,0:T(8,128)(2,1)S(1)} %slice.20.near_ref), channel_id=1, source_target_pairs={{0,8},{8,0},{1,9},{9,1},{2,10},{10,2},{3,11},{11,3},{4,12},{12,4},... | collective-permute-start | bytes 442376 | tf_op jit(solution)/shard_map/ppermute | solution.py:745
  19.2 2.6 %collective-permute-start.7 = (bf16[4,144,128]{2,1,0:T(8,128)(2,1)S(1)}, bf16[4,144,128]{2,1,0:T(8,128)(2,1)S(1)}, u32[]{:S(2)}, u32[]{:S(2)}) collective-permute-start(bf16[4,144,128]{2,1,0:T(8,128)(2,1)S(1)} %collective-permute-done.5.far_ref), channel_id=1, source_target_pairs={{0,8},{8,0},{1,9},{9,1},{2,10},{10,2},{3,11},{11,3},{4,12},{12,4},... | collective-permute-start | bytes 442376 | tf_op jit(solution)/shard_map/ppermute | solution.py:745
  19.2 6.4 %collective-permute-start.4 = (bf16[4,128,128]{2,1,0:T(8,128)(2,1)S(1)}, bf16[4,128,128]{2,1,0:T(8,128)(2,1)S(1)}, u32[]{:S(2)}, u32[]{:S(2)}) collective-permute-start(bf16[4,128,128]{2,1,0:T(8,128)(2,1)S(1)} %slice.19.near_ref), channel_id=1, source_target_pairs={{0,1},{1,0},{2,3},{3,2},{4,5},{5,4},{6,7},{7,6},{8,9},{9,8},{10,11... | collective-permute-start | bytes 393224 | tf_op jit(solution)/shard_map/ppermute | solution.py:756
  21.0 8.5 %collective-permute-start.10 = (bf16[256,256]{1,0:T(8,128)(2,1)S(1)}, bf16[256,256]{1,0:T(8,128)(2,1)S(1)}, u32[]{:S(2)}, u32[]{:S(2)}) collective-permute-start(bf16[256,256]{1,0:T(8,128)(2,1)S(1)} %get-tuple-element.60.normed_ref), channel_id=1, source_target_pairs={{0,8},{8,0},{1,9},{9,1},{2,10},{10,2},{3,11},{11,3},{4,12},{12,4},... | collective-permute-start | bytes 393224 | tf_op jit(solution)/shard_map/ppermute | solution.py:745
  21.3 6.6 %collective-permute-start.8 = (bf16[128,256]{1,0:T(8,128)(2,1)S(1)}, bf16[128,256]{1,0:T(8,128)(2,1)S(1)}, u32[]{:S(2)}, u32[]{:S(2)}) collective-permute-start(bf16[128,256]{1,0:T(8,128)(2,1)S(1)} %get-tuple-element.75), channel_id=1, source_target_pairs={{0,1},{1,0},{2,3},{3,2},{4,5},{5,4},{6,7},{7,6},{8,9},{9,8},{10,11... | collective-permute-start | bytes 196616 | tf_op jit(solution)/shard_map/ppermute | solution.py:756
  23.9 1.7 %copy-start.1 = (bf16[128,512]{1,0:T(8,128)(2,1)S(1)}, bf16[128,512]{1,0:T(8,128)(2,1)}, u32[]{:S(2)}) copy-start(bf16[128,512]{1,0:T(8,128)(2,1)} %hid_ref.1) | copy-start | bytes 393220
  23.9 1.6 %copy-start.2 = (bf16[512,128]{1,0:T(8,128)(2,1)S(1)}, bf16[512,128]{1,0:T(8,128)(2,1)}, u32[]{:S(2)}) copy-start(bf16[512,128]{1,0:T(8,128)(2,1)} %back_ref.1) | copy-start | bytes 393220
  28.0 1.5 %collective-permute-start.11 = (bf16[256,256]{1,0:T(8,128)(2,1)S(1)}, bf16[256,256]{1,0:T(8,128)(2,1)S(1)}, u32[]{:S(2)}, u32[]{:S(2)}) collective-permute-start(bf16[256,256]{1,0:T(8,128)(2,1)S(1)} %constant_dynamic-update-slice_fusion.far_normed_ref), channel_id=1, source_target_pairs={{0,8},{8,0},{1,9},{9,1},{2,10},{10,2},{3,11},{11,3},{4,12},{12,4},... | collective-permute-start | bytes 393224 | tf_op jit(solution)/shard_map/ppermute | solution.py:745
  28.0 1.5 %collective-permute-start.9 = (bf16[512,128]{1,0:T(8,128)(2,1)S(1)}, bf16[512,128]{1,0:T(8,128)(2,1)S(1)}, u32[]{:S(2)}, u32[]{:S(2)}) collective-permute-start(bf16[512,128]{1,0:T(8,128)(2,1)S(1)} %get-tuple-element.76.opm_ref), channel_id=1, source_target_pairs={{0,8},{8,0},{1,9},{9,1},{2,10},{10,2},{3,11},{11,3},{4,12},{12,4},... | collective-permute-start | bytes 393224 | tf_op jit(solution)/shard_map/ppermute | solution.py:745
  31.6 6.4 %collective-permute-start.15 = (bf16[2048,128]{1,0:T(8,128)(2,1)S(1)}, bf16[2048,128]{1,0:T(8,128)(2,1)S(1)}, u32[]{:S(2)}, u32[]{:S(2)}) collective-permute-start(bf16[2048,128]{1,0:T(8,128)(2,1)S(1)} %weight_gradients.1.mine_ref), channel_id=1, source_target_pairs={{0,8},{8,0},{1,9},{9,1},{2,10},{10,2},{3,11},{11,3},{4,12},{12,4},... | collective-permute-start | bytes 1572872 | tf_op jit(solution)/shard_map/ppermute | solution.py:745
  32.0 5.7 %collective-permute-start.12 = (bf16[64,256]{1,0:T(8,128)(2,1)S(1)}, bf16[64,256]{1,0:T(8,128)(2,1)S(1)}, u32[]{:S(2)}, u32[]{:S(2)}) collective-permute-start(bf16[64,256]{1,0:T(8,128)(2,1)S(1)} %get-tuple-element.92), channel_id=1, source_target_pairs={{0,6},{1,7},{2,4},{3,5},{4,2},{5,3},{6,0},{7,1},{8,12},{9,13},{10,... | collective-permute-start | bytes 98312 | tf_op jit(solution)/shard_map/ppermute | solution.py:741
  34.5 3.2 %collective-permute-start.13 = (bf16[64,256]{1,0:T(8,128)(2,1)S(1)}, bf16[64,256]{1,0:T(8,128)(2,1)S(1)}, u32[]{:S(2)}, u32[]{:S(2)}) collective-permute-start(bf16[64,256]{1,0:T(8,128)(2,1)S(1)} %get-tuple-element.92), channel_id=1, source_target_pairs={{8,10},{9,11},{10,8},{11,9},{12,14},{13,15},{14,12},{15,13},{24,26... | collective-permute-start | bytes 98312 | tf_op jit(solution)/shard_map/ppermute | solution.py:741
  37.8 1.3 %collective-permute-start.14 = (bf16[64,256]{1,0:T(8,128)(2,1)S(1)}, bf16[64,256]{1,0:T(8,128)(2,1)S(1)}, u32[]{:S(2)}, u32[]{:S(2)}) collective-permute-start(bf16[64,256]{1,0:T(8,128)(2,1)S(1)} %add_convert_fusion), channel_id=1, source_target_pairs={{0,8},{8,0},{1,9},{9,1},{2,10},{10,2},{3,11},{11,3},{4,12},{12,4},... | collective-permute-start | bytes 98312 | tf_op jit(solution)/shard_map/ppermute | solution.py:745

commit v11 on v10

--- a/solution.py
+++ b/solution.py
@@ -444,9 +444,11 @@
     cnt_ref[...] = jnp.dot(cntl_ref[...], ones, preferred_element_type=f32)
     pm_ref[...] = jnp.dot(pml_ref[...], ones, preferred_element_type=f32).astype(bf16)
 
-    for dh in range(width // 4):
+    def outer_step(dh, carry):
+        first_row = pl.multiple_of(dh * 4 * pair_cols, 4 * pair_cols)
+        first_lane = pl.multiple_of(dh * lanes, lanes)
         prod = jnp.dot(
-            mine_ref[dh * 4 * pair_cols : (dh + 1) * 4 * pair_cols, :],
+            mine_ref[pl.ds(first_row, 4 * pair_cols), :],
             leftn_ref[...],
             preferred_element_type=f32,
         )
@@ -457,9 +459,12 @@
             )
             for il in range(res):
                 first = (k * res + il) * pair_cols
-                outer_ref[first : first + pair_cols, dh * lanes : (dh + 1) * lanes] = turned[
+                outer_ref[first : first + pair_cols, pl.ds(first_lane, lanes)] = turned[
                     il
                 ].astype(bf16)
+        return carry
+
+    lax.fori_loop(0, width // 4, outer_step, 0, unroll=2)
     proj_out_ref[...] = jnp.dot(outer_ref[...], wturn_ref[...], preferred_element_type=f32)
 
 
@@ -487,15 +492,22 @@
             got_ref[me_depth, me_col ^ partner] = mine[at, 0 : 2 * seqs, :]
             got_ref[1 - me_depth, me_col ^ partner] = other[at, 0 : 2 * seqs, :]
     for at, out in ((0, leftt_ref), (1, rightt_ref)):
-        for k in range(cols):
+
+        def turn_step(k, carry, at=at):
             block = jnp.concatenate(
                 [got_ref[e, k, at * seqs : (at + 1) * seqs, :] for e in range(depths)], axis=0
             ).astype(jnp.float32)
-            turn_ref[k * lanes : (k + 1) * lanes, :] = block.T
-        for d in range(width):
-            out[d * residues : (d + 1) * residues, :] = turn_ref[
+            turn_ref[pl.ds(pl.multiple_of(k * lanes, lanes), lanes), :] = block.T
+            return carry
+
+        def order_step(d, carry, out=out):
+            out[pl.ds(pl.multiple_of(d * residues, residues), residues), :] = turn_ref[
                 pl.ds(d, residues, stride=width), :
             ].astype(jnp.bfloat16)
+            return carry
+
+        lax.fori_loop(0, cols, turn_step, 0, unroll=2)
+        lax.fori_loop(0, width, order_step, 0, unroll=8)
 
 
 def transition_kernel(
@@ -529,8 +541,8 @@
             pgot_ref[me_col ^ partner] = mine[at]
     gain = gain_ref[...]
     chunk = 2 * per
-    for at in range(cols // 2):
-        rows = slice(at * chunk, (at + 1) * chunk)
+    def chunk_step(at, carry):
+        rows = pl.ds(pl.multiple_of(at * chunk, chunk), chunk)
         act, grad = [
             jnp.concatenate(
                 [pgot_ref[2 * at + b, w * per : (w + 1) * per, :] for b in range(2)], axis=0
@@ -561,6 +573,9 @@
         gmid = grad.astype(f32) + standardize_adjoint(gsc, scaled, inv)
         gmid_ref[rows, :] = gmid
         opm_ref[rows, :] = (gmid / count).astype(bf16)
+        return carry
+
+    lax.fori_loop(0, cols // 2, chunk_step, 0, unroll=2)
     couple_ref[...] = gmid_ref[pl.ds(pl.multiple_of(me_col * per, per), per), :].astype(bf16)
 
 
@@ -620,11 +635,12 @@
         gcol_ref[jl * residues : (jl + 1) * residues, :] = gf_ref[
             my_half, pl.ds(my_first + jl, residues, stride=pair_cols), :
         ].astype(bf16)
-    for lhs, weight, out in ((grow_ref, wturn_ref, gor_ref), (gcol_ref, wout_ref, goc_ref)):
-        for dh in range(width // 4):
+    def outer_gradient_step(dh, carry):
+        first_row = pl.multiple_of(dh * lanes, lanes)
+        for lhs, weight, out in ((grow_ref, wturn_ref, gor_ref), (gcol_ref, wout_ref, goc_ref)):
             piece = lax.dot_general(
                 lhs[...],
-                weight[dh * lanes : (dh + 1) * lanes, :],
+                weight[pl.ds(first_row, lanes), :],
                 (((1,), (1,)), ((), ())),
                 preferred_element_type=f32,
             )
@@ -637,10 +653,13 @@
                     width,
                 )
                 for dl in range(4):
-                    first = (dh * 4 + dl) * residues
-                    out[first : first + residues, y * lanes : (y + 1) * lanes] = turned[dl].astype(
+                    first = pl.multiple_of((dh * 4 + dl) * residues, residues)
+                    out[pl.ds(first, residues), y * lanes : (y + 1) * lanes] = turned[dl].astype(
                         bf16
                     )
+        return carry
+
+    lax.fori_loop(0, width // 4, outer_gradient_step, 0, unroll=2)
     group = lax.broadcasted_iota(jnp.int32, (here, here * width), 1) // width
     spread = (group == lax.broadcasted_iota(jnp.int32, (here, here * width), 0)).astype(f32)
     mask_lanes = lax.dot_general(
@@ -988,8 +1007,8 @@
         compiler_params=params,
         name="sums_over_depth",
     )(weights, swap_depth(weights))
-    came_a = swap_line(part, Z_PARTNERS[:2])
-    came_b = swap_line(part, (None, Z_PARTNERS[2]))
+    came_a = swap_line(part, (Z_PARTNERS[0], Z_PARTNERS[2]))
+    came_b = swap_line(part, (None, Z_PARTNERS[1]))
     feat = feat.reshape(seqs, res, channels)
     came_a, came_b, feat = lax.optimization_barrier((came_a, came_b, feat))
     kept = jnp.where(lax.axis_index("depth") == 0, part, came_b)

time: 40 us -> 42.8 us (1.070)
  Pallas kernels: 12.1 us -> 15 us
    pallas_call x1, Pallas kernels: 2.03 us -> 2.97 us  [whole_plan(): pl.pallas_call(functools.partial(projector_kernel, sizes), out_shape=(sha...]
    pallas_call x1, Pallas kernels: 2.11 us -> 2.98 us  [whole_plan(): pl.pallas_call(functools.partial(outer_kernel, sizes, orders), out_shape=...]
    pallas_call x1, Pallas kernels: 1.39 us -> 2.03 us  [whole_plan(): pl.pallas_call(functools.partial(turn_kernel, sizes, orders), out_shape=(...]
  transfers between devices with their start and end apart: 16 -> 16, of which waited for: 6 -> 5; matrix products, arithmetic and copies ran while one was open for 2% -> 2% of each run, Pallas kernels for 21% -> 24%
where the time goes in v11:
time: 42.8 us; the launch traced here: 42.6 us
  starting transfers between devices  16.1 us (38%)
  Pallas kernels  15 us (35%)
  waiting for transfers between devices  9.02 us (21%)
  local copies, waits for them, and re-layouts  1.49 us (3%)
  between operations  0.83 us (2%)
    ppermute x7, starting transfers between devices, swap_col(): lax.ppermute(block, 'col', [(at, at ^ partner) for at in range(count)])  11.3 us
    ppermute x7, waiting for transfers between devices, swap_col(): lax.ppermute(block, 'col', [(at, at ^ partner) for at in range(count)])  7.35 us
    ppermute x2, starting transfers between devices, swap_line(): return lax.ppermute(block, ('depth', 'col'), pairs)  3.13 us
    pallas_call x1, Pallas kernels, whole_plan(): pl.pallas_call(functools.partial(outer_kernel, sizes, orders), out_shape=...  2.98 us
    pallas_call x1, Pallas kernels, whole_plan(): pl.pallas_call(functools.partial(projector_kernel, sizes), out_shape=(sha...  2.97 us
    pallas_call x1, Pallas kernels, whole_plan(): pl.pallas_call(functools.partial(transition_kernel, sizes, orders), out_s...  2.83 us
    pallas_call x1, Pallas kernels, whole_plan(): pl.pallas_call(functools.partial(turn_kernel, sizes, orders), out_shape=(...  2.03 us
    pallas_call x1, Pallas kernels, whole_plan(): pl.pallas_call(pre_kernel, out_shape=(shape((1, rows + 2 * per, pair_widt...  1.91 us
  transfers between devices with their start and end apart: 16, of which 5 were waited for; matrix products, arithmetic and copies ran while one was open for 2% of the time, Pallas kernels for 24%

profile of v11, /device:TPU:0, one launch (start us, length us, event | category | flops | bytes accessed | tf_op | source)
XLA Modules:
  0.0 42.6 jit_solution(9059539831037996594)
XLA Ops:
  0.6 0.1 pad_add_fusion.ids_ref
  0.7 1.9 %project.1 = (bf16[1,272,128]{2,1,0:T(8,128)(2,1)S(1)}, f32[1,256]{1,0:T(1,128)S(1)}, bf16[32,256]{1,0:T(8,128)(2,1)S(1)}, bf16[32,256]{1,0:T(8,128)(2,1)S(1)}, ...) custom-call(s32[2]{0:T(128)S(1)} %pad_add_fusion.ids_ref, ...), custom_call_target="tpu_custom_call" | custom-call | tf_op jit(solution)/shard_map/project/pallas_call | solution.py:815
  2.6 5.1 %collective-permute-start = (bf16[1,272,128]{2,1,0:T(8,128)(2,1)S(1)}, bf16[1,272,128]{2,1,0:T(8,128)(2,1)S(1)}, u32[]{:S(2)}, u32[]{:S(2)}) collective-permute-start(bf16[1,272,128]{2,1,0:T(8,128)(2,1)S(1)} %get-tuple-element.59), channel_id=1, source_target_pairs={{0,6},{1,7},{2,4},{3,5},{4,2},{5,3},{6,0},{7,1},{8,14},{9,15},{10,... | collective-permute-start | bytes 208904 | tf_op jit(solution)/shard_map/ppermute | solution.py:775
  7.7 0.0 collective-permute-start.1
  7.8 0.6 %collective-permute-start.2 = (bf16[1,272,128]{2,1,0:T(8,128)(2,1)S(1)}, bf16[1,272,128]{2,1,0:T(8,128)(2,1)S(1)}, u32[]{:S(2)}, u32[]{:S(2)}) collective-permute-start(bf16[1,272,128]{2,1,0:T(8,128)(2,1)S(1)} %get-tuple-element.59), channel_id=1, source_target_pairs={{0,2},{1,3},{2,0},{3,1},{4,6},{5,7},{6,4},{7,5},{8,10},{9,11},{10,... | collective-permute-start | bytes 208904 | tf_op jit(solution)/shard_map/ppermute | solution.py:775
  8.4 1.7 %collective-permute-start.3 = (bf16[128,256]{1,0:T(8,128)(2,1)S(1)}, bf16[128,256]{1,0:T(8,128)(2,1)S(1)}, u32[]{:S(2)}, u32[]{:S(2)}) collective-permute-start(bf16[128,256]{1,0:T(8,128)(2,1)S(1)} %get-tuple-element.112), channel_id=1, source_target_pairs={{0,1},{1,0},{2,3},{3,2},{4,5},{5,4},{6,7},{7,6},{8,9},{9,8},{10,11... | collective-permute-start | bytes 196616 | tf_op jit(solution)/shard_map/ppermute | solution.py:775
  10.1 0.3 collective-permute-done
  10.4 3.2 %collective-permute-done.1 = bf16[1,272,128]{2,1,0:T(8,128)(2,1)S(1)} collective-permute-done((bf16[1,272,128]{2,1,0:T(8,128)(2,1)S(1)}, bf16[1,272,128]{2,1,0:T(8,128)(2,1)S(1)}, u32[]{:S(2)}, u32[]{:S(2)}) %collective-permute-start.1) | collective-permute-done | bytes 69664 | tf_op jit(solution)/shard_map/ppermute | solution.py:775
  13.7 0.0 collective-permute-done.2
  13.7 0.0 copy-start
  13.7 0.0 collective-permute-done.3
  13.7 1.6 %collective-permute-start.5 = (bf16[4,144,128]{2,1,0:T(8,128)(2,1)S(1)}, bf16[4,144,128]{2,1,0:T(8,128)(2,1)S(1)}, u32[]{:S(2)}, u32[]{:S(2)}) collective-permute-start(bf16[4,144,128]{2,1,0:T(8,128)(2,1)S(1)} %slice.20.near_ref), channel_id=1, source_target_pairs={{0,1},{1,0},{2,3},{3,2},{4,5},{5,4},{6,7},{7,6},{8,9},{9,8},{10,11... | collective-permute-start | bytes 442376 | tf_op jit(solution)/shard_map/ppermute | solution.py:775
  15.3 0.0 collective-permute-start.6
  15.3 3.8 %collective-permute-done.5.far_ref = bf16[4,144,128]{2,1,0:T(8,128)(2,1)S(1)} collective-permute-done((bf16[4,144,128]{2,1,0:T(8,128)(2,1)S(1)}, bf16[4,144,128]{2,1,0:T(8,128)(2,1)S(1)}, u32[]{:S(2)}, u32[]{:S(2)}) %collective-permute-start.5) | collective-permute-done | bytes 147488 | tf_op jit(solution)/shard_map/ppermute | solution.py:775
  19.2 0.0 collective-permute-start.7
  19.2 1.8 %collective-permute-start.4 = (bf16[4,128,128]{2,1,0:T(8,128)(2,1)S(1)}, bf16[4,128,128]{2,1,0:T(8,128)(2,1)S(1)}, u32[]{:S(2)}, u32[]{:S(2)}) collective-permute-start(bf16[4,128,128]{2,1,0:T(8,128)(2,1)S(1)} %slice.19.near_ref), channel_id=1, source_target_pairs={{0,1},{1,0},{2,3},{3,2},{4,5},{5,4},{6,7},{7,6},{8,9},{9,8},{10,11... | collective-permute-start | bytes 393224 | tf_op jit(solution)/shard_map/ppermute | solution.py:775
  21.0 0.2 collective-permute-start.10
  21.2 0.0 copy-done
  21.2 0.1 copy.19
  21.3 0.4 collective-permute-start.8
  21.7 0.0 collective-permute-done.6.other_near_ref
  21.7 0.0 collective-permute-done.7.other_far_ref
  21.8 3.0 %outer_products.1 = (bf16[512,1024]{1,0:T(8,128)(2,1)S(1)}, f32[512,128]{1,0:T(8,128)S(1)}, f32[512,128]{1,0:T(8,128)S(1)}, bf16[512,128]{1,0:T(8,128)(2,1)S(1)}, f32[32,128]{1,0:T(8,128)S(1)}) custom-call(s32[2]{0:T(128)S(1)} %pad_add_fusion.ids_ref, bf16[4,144,128]{2,1,0:T(8,128)(2,1)S(1)} %slice.20.near_ref, ...), custom_call_target="tpu_custom_call" | custom-call | tf_op jit(solution)/shard_map/outer_products/pallas_call | solution.py:872
  24.7 0.0 copy-start.1
  24.8 0.0 copy-start.2
  24.8 2.0 %turned.1 = (bf16[1024,128]{1,0:T(8,128)(2,1)S(1)}, bf16[1024,128]{1,0:T(8,128)(2,1)S(1)}) custom-call(s32[2]{0:T(128)S(1)} %pad_add_fusion.ids_ref, bf16[4,144,128]{2,1,0:T(8,128)(2,1)S(1)} %slice.20.near_ref, bf16[4,144,128]{2,1,0:T(8,128)(2,1)S(1)} %collective-permute-done.5.far_ref, bf16[4,144,128]{2,1,0:T(8,128)(2,1)S(1)} %collective-permute-done.6.other_near_ref, ...), custom_call_target="tpu_custom_call" | custom-call | tf_op jit(solution)/shard_map/turned/pallas_call | solution.py:895
  26.8 0.0 collective-permute-done.4.far_ref
  26.8 2.8 %transition.1 = (bf16[64,128]{1,0:T(8,128)(2,1)}, bf16[512,128]{1,0:T(8,128)(2,1)S(1)}, bf16[512,128]{1,0:T(8,128)(2,1)S(1)}, bf16[512,512]{1,0:T(8,128)(2,1)S(1...) custom-call(s32[2]{0:T(128)S(1)} %pad_add_fusion.ids_ref, bf16[4,128,128]{2,1,0:T(8,128)(2,1)S(1)} %slice.19.near_ref, ...), custom_call_target="tpu_custom_call" | custom-call | tf_op jit(solution)/shard_map/transition/pallas_call | solution.py:913
  29.7 0.0 collective-permute-done.8
  29.7 0.1 collective-permute-start.11
  29.8 0.5 %collective-permute-start.9 = (bf16[512,128]{1,0:T(8,128)(2,1)S(1)}, bf16[512,128]{1,0:T(8,128)(2,1)S(1)}, u32[]{:S(2)}, u32[]{:S(2)}) collective-permute-start(bf16[512,128]{1,0:T(8,128)(2,1)S(1)} %get-tuple-element.76.opm_ref), channel_id=1, source_target_pairs={{0,8},{8,0},{1,9},{9,1},{2,10},{10,2},{3,11},{11,3},{4,12},{12,4},... | collective-permute-start | bytes 393224 | tf_op jit(solution)/shard_map/ppermute | solution.py:764
  30.3 0.9 %weight_gradients.1.mine_ref = bf16[2048,128]{1,0:T(8,128)(2,1)S(1)} custom-call(bf16[512,1024]{1,0:T(8,128)(2,1)S(1)} %get-tuple-element.79.outer_ref, bf16[512,128]{1,0:T(8,128)(2,1)S(1)} %get-tuple-element.76.opm_ref, bf16[512,128]{1,0:T(8,128)(2,1)S(1)} %get-tuple-element.80.pn_ref, bf16[512,512]{1,0:T(8,128)(2,1)S(1)} %get-tuple-element.81.gh_ref, ...), custom_call_target="tpu_custom_call" | custom-call | tf_op jit(solution)/shard_map/weight_gradients/pallas_call | solution.py:944
  31.2 0.0 collective-permute-done.10.other_normed_ref
  31.2 0.0 collective-permute-done.11.other_far_normed_ref
  31.2 0.1 collective-permute-done.9.other_opm_ref
  31.3 3.0 %projector_parts.1 = (bf16[64,256]{1,0:T(8,128)(2,1)S(1)}, bf16[256,256]{1,0:T(8,128)(2,1)S(1)}) custom-call(s32[2]{0:T(128)S(1)} %pad_add_fusion.ids_ref, bf16[512,128]{1,0:T(8,128)(2,1)S(1)} %get-tuple-element.76.opm_ref, bf16[512,128]{1,0:T(8,128)(2,1)S(1)} %collective-permute-done.9.other_opm_ref, bf16[1024,128]{1,0:T(8,128)(2,1)S(1)} %get-tuple-element.85.rightt_ref, ...), custom_call_target="tpu_custom_call" | custom-call | tf_op jit(solution)/shard_map/projector_parts/pallas_call | solution.py:956
  34.2 0.3 collective-permute-start.15
  34.6 2.5 %collective-permute-start.12 = (bf16[64,256]{1,0:T(8,128)(2,1)S(1)}, bf16[64,256]{1,0:T(8,128)(2,1)S(1)}, u32[]{:S(2)}, u32[]{:S(2)}) collective-permute-start(bf16[64,256]{1,0:T(8,128)(2,1)S(1)} %get-tuple-element.92), channel_id=1, source_target_pairs={{0,6},{1,7},{2,4},{3,5},{4,2},{5,3},{6,0},{7,1},{8,10},{9,11},{10,... | collective-permute-start | bytes 98312 | tf_op jit(solution)/shard_map/ppermute | solution.py:760
  37.1 0.7 %collective-permute-start.13 = (bf16[64,256]{1,0:T(8,128)(2,1)S(1)}, bf16[64,256]{1,0:T(8,128)(2,1)S(1)}, u32[]{:S(2)}, u32[]{:S(2)}) collective-permute-start(bf16[64,256]{1,0:T(8,128)(2,1)S(1)} %get-tuple-element.92), channel_id=1, source_target_pairs={{8,12},{9,13},{10,14},{11,15},{12,8},{13,9},{14,10},{15,11},{24,28... | collective-permute-start | bytes 98312 | tf_op jit(solution)/shard_map/ppermute | solution.py:760
  37.7 0.3 features.1
  38.0 0.7 %reshape.44 = bf16[64,4,256]{2,1,0:T(4,128)(2,1)} reshape(bf16[256,256]{1,0:T(8,128)(2,1)S(1)} %features.1) | data formatting | bytes 262144 | tf_op jit(solution)/shard_map/reshape | solution.py:1012
  38.7 1.6 %collective-permute-done.12 = bf16[64,256]{1,0:T(8,128)(2,1)S(1)} collective-permute-done((bf16[64,256]{1,0:T(8,128)(2,1)S(1)}, bf16[64,256]{1,0:T(8,128)(2,1)S(1)}, u32[]{:S(2)}, u32[]{:S(2)}) %collective-permute-start.12) | collective-permute-done | bytes 32800 | tf_op jit(solution)/shard_map/ppermute | solution.py:760
  40.3 0.0 collective-permute-done.13
  40.3 0.6 %collective-permute-start.14 = (bf16[64,256]{1,0:T(8,128)(2,1)S(1)}, bf16[64,256]{1,0:T(8,128)(2,1)S(1)}, u32[]{:S(2)}, u32[]{:S(2)}) collective-permute-start(bf16[64,256]{1,0:T(8,128)(2,1)S(1)} %add_convert_fusion), channel_id=1, source_target_pairs={{0,8},{8,0},{1,9},{9,1},{2,10},{10,2},{3,11},{11,3},{4,12},{12,4},... | collective-permute-start | bytes 98312 | tf_op jit(solution)/shard_map/ppermute | solution.py:764
  40.9 0.0 collective-permute-done.15.other_ref
  40.9 1.0 %sums_over_depth.1 = (f32[1024,128]{1,0:T(8,128)}, f32[128,512]{1,0:T(8,128)}, f32[512,128]{1,0:T(8,128)}) custom-call(bf16[2048,128]{1,0:T(8,128)(2,1)S(1)} %weight_gradients.1.mine_ref, bf16[2048,128]{1,0:T(8,128)(2,1)S(1)} %collective-permute-done.15.other_ref), custom_call_target="tpu_custom_call" | custom-call | tf_op jit(solution)/shard_map/sums_over_depth/pallas_call | solution.py:998
  41.9 0.0 collective-permute-done.14
  41.9 0.6 %slice_bitcast_fusion = (f32[256,32]{0,1:T(8,128)}, f32[256,32]{0,1:T(8,128)}) fusion(f32[64,256]{1,0:T(8,128)S(1)} %convert_add_fusion), kind=kLoop, calls=%fused_computation.3 | loop fusion | bytes 131072 | tf_op jit(solution)/shard_map/transpose | solution.py:1023
  (10 shorter events, 0.1 us)
Async XLA Ops:
  2.6 7.8 %collective-permute-start = (bf16[1,272,128]{2,1,0:T(8,128)(2,1)S(1)}, bf16[1,272,128]{2,1,0:T(8,128)(2,1)S(1)}, u32[]{:S(2)}, u32[]{:S(2)}) collective-permute-start(bf16[1,272,128]{2,1,0:T(8,128)(2,1)S(1)} %get-tuple-element.59), channel_id=1, source_target_pairs={{0,6},{1,7},{2,4},{3,5},{4,2},{5,3},{6,0},{7,1},{8,14},{9,15},{10,... | collective-permute-start | bytes 208904 | tf_op jit(solution)/shard_map/ppermute | solution.py:775
  7.7 5.9 %collective-permute-start.1 = (bf16[1,272,128]{2,1,0:T(8,128)(2,1)S(1)}, bf16[1,272,128]{2,1,0:T(8,128)(2,1)S(1)}, u32[]{:S(2)}, u32[]{:S(2)}) collective-permute-start(bf16[1,272,128]{2,1,0:T(8,128)(2,1)S(1)} %get-tuple-element.59), channel_id=1, source_target_pairs={{0,4},{1,5},{2,6},{3,7},{4,0},{5,1},{6,2},{7,3},{8,12},{9,13},{10,... | collective-permute-start | bytes 208904 | tf_op jit(solution)/shard_map/ppermute | solution.py:775
  7.8 5.9 %collective-permute-start.2 = (bf16[1,272,128]{2,1,0:T(8,128)(2,1)S(1)}, bf16[1,272,128]{2,1,0:T(8,128)(2,1)S(1)}, u32[]{:S(2)}, u32[]{:S(2)}) collective-permute-start(bf16[1,272,128]{2,1,0:T(8,128)(2,1)S(1)} %get-tuple-element.59), channel_id=1, source_target_pairs={{0,2},{1,3},{2,0},{3,1},{4,6},{5,7},{6,4},{7,5},{8,10},{9,11},{10,... | collective-permute-start | bytes 208904 | tf_op jit(solution)/shard_map/ppermute | solution.py:775
  8.4 5.3 %collective-permute-start.3 = (bf16[128,256]{1,0:T(8,128)(2,1)S(1)}, bf16[128,256]{1,0:T(8,128)(2,1)S(1)}, u32[]{:S(2)}, u32[]{:S(2)}) collective-permute-start(bf16[128,256]{1,0:T(8,128)(2,1)S(1)} %get-tuple-element.112), channel_id=1, source_target_pairs={{0,1},{1,0},{2,3},{3,2},{4,5},{5,4},{6,7},{7,6},{8,9},{9,8},{10,11... | collective-permute-start | bytes 196616 | tf_op jit(solution)/shard_map/ppermute | solution.py:775
  13.7 7.5 %copy-start = (bf16[1024,128]{1,0:T(8,128)(2,1)S(1)}, bf16[1024,128]{1,0:T(8,128)(2,1)}, u32[]{:S(2)}) copy-start(bf16[1024,128]{1,0:T(8,128)(2,1)} %wout_ref.1) | copy-start | bytes 786436
  13.7 5.4 %collective-permute-start.5 = (bf16[4,144,128]{2,1,0:T(8,128)(2,1)S(1)}, bf16[4,144,128]{2,1,0:T(8,128)(2,1)S(1)}, u32[]{:S(2)}, u32[]{:S(2)}) collective-permute-start(bf16[4,144,128]{2,1,0:T(8,128)(2,1)S(1)} %slice.20.near_ref), channel_id=1, source_target_pairs={{0,1},{1,0},{2,3},{3,2},{4,5},{5,4},{6,7},{7,6},{8,9},{9,8},{10,11... | collective-permute-start | bytes 442376 | tf_op jit(solution)/shard_map/ppermute | solution.py:775
  15.3 6.4 %collective-permute-start.6 = (bf16[4,144,128]{2,1,0:T(8,128)(2,1)S(1)}, bf16[4,144,128]{2,1,0:T(8,128)(2,1)S(1)}, u32[]{:S(2)}, u32[]{:S(2)}) collective-permute-start(bf16[4,144,128]{2,1,0:T(8,128)(2,1)S(1)} %slice.20.near_ref), channel_id=1, source_target_pairs={{0,8},{8,0},{1,9},{9,1},{2,10},{10,2},{3,11},{11,3},{4,12},{12,4},... | collective-permute-start | bytes 442376 | tf_op jit(solution)/shard_map/ppermute | solution.py:764
  19.2 2.6 %collective-permute-start.7 = (bf16[4,144,128]{2,1,0:T(8,128)(2,1)S(1)}, bf16[4,144,128]{2,1,0:T(8,128)(2,1)S(1)}, u32[]{:S(2)}, u32[]{:S(2)}) collective-permute-start(bf16[4,144,128]{2,1,0:T(8,128)(2,1)S(1)} %collective-permute-done.5.far_ref), channel_id=1, source_target_pairs={{0,8},{8,0},{1,9},{9,1},{2,10},{10,2},{3,11},{11,3},{4,12},{12,4},... | collective-permute-start | bytes 442376 | tf_op jit(solution)/shard_map/ppermute | solution.py:764
  19.2 7.6 %collective-permute-start.4 = (bf16[4,128,128]{2,1,0:T(8,128)(2,1)S(1)}, bf16[4,128,128]{2,1,0:T(8,128)(2,1)S(1)}, u32[]{:S(2)}, u32[]{:S(2)}) collective-permute-start(bf16[4,128,128]{2,1,0:T(8,128)(2,1)S(1)} %slice.19.near_ref), channel_id=1, source_target_pairs={{0,1},{1,0},{2,3},{3,2},{4,5},{5,4},{6,7},{7,6},{8,9},{9,8},{10,11... | collective-permute-start | bytes 393224 | tf_op jit(solution)/shard_map/ppermute | solution.py:775
  21.0 10.2 %collective-permute-start.10 = (bf16[256,256]{1,0:T(8,128)(2,1)S(1)}, bf16[256,256]{1,0:T(8,128)(2,1)S(1)}, u32[]{:S(2)}, u32[]{:S(2)}) collective-permute-start(bf16[256,256]{1,0:T(8,128)(2,1)S(1)} %get-tuple-element.60.normed_ref), channel_id=1, source_target_pairs={{0,8},{8,0},{1,9},{9,1},{2,10},{10,2},{3,11},{11,3},{4,12},{12,4},... | collective-permute-start | bytes 393224 | tf_op jit(solution)/shard_map/ppermute | solution.py:764
  21.3 8.4 %collective-permute-start.8 = (bf16[128,256]{1,0:T(8,128)(2,1)S(1)}, bf16[128,256]{1,0:T(8,128)(2,1)S(1)}, u32[]{:S(2)}, u32[]{:S(2)}) collective-permute-start(bf16[128,256]{1,0:T(8,128)(2,1)S(1)} %get-tuple-element.75), channel_id=1, source_target_pairs={{0,1},{1,0},{2,3},{3,2},{4,5},{5,4},{6,7},{7,6},{8,9},{9,8},{10,11... | collective-permute-start | bytes 196616 | tf_op jit(solution)/shard_map/ppermute | solution.py:775
  24.7 2.1 %copy-start.1 = (bf16[128,512]{1,0:T(8,128)(2,1)S(1)}, bf16[128,512]{1,0:T(8,128)(2,1)}, u32[]{:S(2)}) copy-start(bf16[128,512]{1,0:T(8,128)(2,1)} %hid_ref.1) | copy-start | bytes 393220
  24.8 2.1 %copy-start.2 = (bf16[512,128]{1,0:T(8,128)(2,1)S(1)}, bf16[512,128]{1,0:T(8,128)(2,1)}, u32[]{:S(2)}) copy-start(bf16[512,128]{1,0:T(8,128)(2,1)} %back_ref.1) | copy-start | bytes 393220
  29.7 1.5 %collective-permute-start.11 = (bf16[256,256]{1,0:T(8,128)(2,1)S(1)}, bf16[256,256]{1,0:T(8,128)(2,1)S(1)}, u32[]{:S(2)}, u32[]{:S(2)}) collective-permute-start(bf16[256,256]{1,0:T(8,128)(2,1)S(1)} %constant_dynamic-update-slice_fusion.far_normed_ref), channel_id=1, source_target_pairs={{0,8},{8,0},{1,9},{9,1},{2,10},{10,2},{3,11},{11,3},{4,12},{12,4},... | collective-permute-start | bytes 393224 | tf_op jit(solution)/shard_map/ppermute | solution.py:764
  29.8 1.5 %collective-permute-start.9 = (bf16[512,128]{1,0:T(8,128)(2,1)S(1)}, bf16[512,128]{1,0:T(8,128)(2,1)S(1)}, u32[]{:S(2)}, u32[]{:S(2)}) collective-permute-start(bf16[512,128]{1,0:T(8,128)(2,1)S(1)} %get-tuple-element.76.opm_ref), channel_id=1, source_target_pairs={{0,8},{8,0},{1,9},{9,1},{2,10},{10,2},{3,11},{11,3},{4,12},{12,4},... | collective-permute-start | bytes 393224 | tf_op jit(solution)/shard_map/ppermute | solution.py:764
  34.2 6.6 %collective-permute-start.15 = (bf16[2048,128]{1,0:T(8,128)(2,1)S(1)}, bf16[2048,128]{1,0:T(8,128)(2,1)S(1)}, u32[]{:S(2)}, u32[]{:S(2)}) collective-permute-start(bf16[2048,128]{1,0:T(8,128)(2,1)S(1)} %weight_gradients.1.mine_ref), channel_id=1, source_target_pairs={{0,8},{8,0},{1,9},{9,1},{2,10},{10,2},{3,11},{11,3},{4,12},{12,4},... | collective-permute-start | bytes 1572872 | tf_op jit(solution)/shard_map/ppermute | solution.py:764
  34.6 5.7 %collective-permute-start.12 = (bf16[64,256]{1,0:T(8,128)(2,1)S(1)}, bf16[64,256]{1,0:T(8,128)(2,1)S(1)}, u32[]{:S(2)}, u32[]{:S(2)}) collective-permute-start(bf16[64,256]{1,0:T(8,128)(2,1)S(1)} %get-tuple-element.92), channel_id=1, source_target_pairs={{0,6},{1,7},{2,4},{3,5},{4,2},{5,3},{6,0},{7,1},{8,10},{9,11},{10,... | collective-permute-start | bytes 98312 | tf_op jit(solution)/shard_map/ppermute | solution.py:760
  37.1 3.2 %collective-permute-start.13 = (bf16[64,256]{1,0:T(8,128)(2,1)S(1)}, bf16[64,256]{1,0:T(8,128)(2,1)S(1)}, u32[]{:S(2)}, u32[]{:S(2)}) collective-permute-start(bf16[64,256]{1,0:T(8,128)(2,1)S(1)} %get-tuple-element.92), channel_id=1, source_target_pairs={{8,12},{9,13},{10,14},{11,15},{12,8},{13,9},{14,10},{15,11},{24,28... | collective-permute-start | bytes 98312 | tf_op jit(solution)/shard_map/ppermute | solution.py:760
  40.3 1.6 %collective-permute-start.14 = (bf16[64,256]{1,0:T(8,128)(2,1)S(1)}, bf16[64,256]{1,0:T(8,128)(2,1)S(1)}, u32[]{:S(2)}, u32[]{:S(2)}) collective-permute-start(bf16[64,256]{1,0:T(8,128)(2,1)S(1)} %add_convert_fusion), channel_id=1, source_target_pairs={{0,8},{8,0},{1,9},{9,1},{2,10},{10,2},{3,11},{11,3},{4,12},{12,4},... | collective-permute-start | bytes 98312 | tf_op jit(solution)/shard_map/ppermute | solution.py:764

commit v12 on v10

--- a/solution.py
+++ b/solution.py
@@ -323,40 +323,43 @@
     ]
     for copy in copies:
         copy.start()
-    for copy in copies:
+    for copy in copies[1:6]:
         copy.wait()
     lanes = sent_ref.shape[2]
     group = lanes // res
-    scaled, inv = norm_pieces(
-        x_ref[...].astype(jnp.float32).reshape(seqs * res, x_ref.shape[2])
-    )
-    scaled_ref[...] = scaled
-    inv_ref[...] = inv
-    normed = (scaled * scale_ref[...]).astype(jnp.bfloat16)
-    normed_ref[...] = normed
-    wide = lax.dot_general(
-        normed,
-        wide_projector(first_ref, second_ref, res),
-        (((1,), (1,)), ((), ())),
-        preferred_element_type=jnp.float32,
-    )
-    for at in range(2):
-        wide_ref[at] = wide[:, at * lanes : (at + 1) * lanes]
     tile_ref[...] = jnp.zeros(tile_ref.shape, jnp.float32)
     mask = maskt_ref[...].astype(jnp.float32)
     tile_ref[0:res, 0:seqs] = mask
     spread = (
         lax.broadcasted_iota(jnp.int32, (MASK_ROWS, lanes), 1) // group
         == lax.broadcasted_iota(jnp.int32, (MASK_ROWS, lanes), 0)
-    ).astype(jnp.float32)
+    ).astype(jnp.bfloat16)
     mask_lanes = lax.dot_general(
-        tile_ref[...], spread, (((0,), (0,)), ((), ())), preferred_element_type=jnp.float32
+        tile_ref[...].astype(jnp.bfloat16),
+        spread,
+        (((0,), (0,)), ((), ())),
+        preferred_element_type=jnp.float32,
     )[:seqs]
     twice = jnp.concatenate([mask] * (lanes // seqs), axis=1)
     here = lax.broadcasted_iota(jnp.int32, (res, lanes), 1) // seqs == ids_ref[0]
     tile_ref[0:res, :] = jnp.where(here, twice, 0.0)
     tile_ref[res : 2 * res, 0 : pmask_ref.shape[1]] = pmask_ref[...].astype(jnp.float32)
+    sent_ref[0, 2 * seqs : first_pair, :] = tile_ref[...].astype(jnp.bfloat16)
     lane_group = lax.broadcasted_iota(jnp.int32, (seqs, lanes), 1) // group
+    projector = wide_projector(first_ref, second_ref, res)
+    copies[0].wait()
+    scaled, inv = norm_pieces(
+        x_ref[...].astype(jnp.float32).reshape(seqs * res, x_ref.shape[2])
+    )
+    normed = (scaled * scale_ref[...]).astype(jnp.bfloat16)
+    wide = lax.dot_general(
+        normed, projector, (((1,), (1,)), ((), ())), preferred_element_type=jnp.float32
+    )
+    for at in range(2):
+        wide_ref[at] = wide[:, at * lanes : (at + 1) * lanes]
+    scaled_ref[...] = scaled
+    inv_ref[...] = inv
+    normed_ref[...] = normed
     for at in range(2):
         both = wide_ref[at, pl.ds(0, seqs, stride=res), :]
         for r in range(1, res):
@@ -364,7 +367,8 @@
                 lane_group == r, wide_ref[at, pl.ds(r, seqs, stride=res), :], both
             )
         sent_ref[0, at * seqs : (at + 1) * seqs, :] = (both * mask_lanes).astype(jnp.bfloat16)
-    sent_ref[0, 2 * seqs : first_pair, :] = tile_ref[...].astype(jnp.bfloat16)
+    for copy in copies[6:]:
+        copy.wait()
 
 
 def outer_kernel(
@@ -460,7 +464,12 @@
                 outer_ref[first : first + pair_cols, dh * lanes : (dh + 1) * lanes] = turned[
                     il
                 ].astype(bf16)
-    proj_out_ref[...] = jnp.dot(outer_ref[...], wturn_ref[...], preferred_element_type=f32)
+        if dh % 2:
+            both = slice((dh - 1) * lanes, (dh + 1) * lanes)
+            added = jnp.dot(outer_ref[:, both], wturn_ref[both, :], preferred_element_type=f32)
+            if dh > 1:
+                added = added + proj_out_ref[...]
+            proj_out_ref[...] = added
 
 
 def turn_kernel(
@@ -620,8 +629,11 @@
         gcol_ref[jl * residues : (jl + 1) * residues, :] = gf_ref[
             my_half, pl.ds(my_first + jl, residues, stride=pair_cols), :
         ].astype(bf16)
-    for lhs, weight, out in ((grow_ref, wturn_ref, gor_ref), (gcol_ref, wout_ref, goc_ref)):
-        for dh in range(width // 4):
+    totals = [None, None]
+    for dh in range(width // 4):
+        for at, (lhs, weight, out, turned_ref) in enumerate(
+            ((grow_ref, wturn_ref, gor_ref, rightt_ref), (gcol_ref, wout_ref, goc_ref, leftt_ref))
+        ):
             piece = lax.dot_general(
                 lhs[...],
                 weight[dh * lanes : (dh + 1) * lanes, :],
@@ -641,6 +653,15 @@
                     out[first : first + residues, y * lanes : (y + 1) * lanes] = turned[dl].astype(
                         bf16
                     )
+            if dh % 2:
+                rows = slice((dh - 1) * 4 * residues, (dh + 1) * 4 * residues)
+                added = lax.dot_general(
+                    turned_ref[rows, :],
+                    out[rows, :],
+                    (((0,), (0,)), ((), ())),
+                    preferred_element_type=f32,
+                )
+                totals[at] = added if totals[at] is None else totals[at] + added
     group = lax.broadcasted_iota(jnp.int32, (here, here * width), 1) // width
     spread = (group == lax.broadcasted_iota(jnp.int32, (here, here * width), 0)).astype(f32)
     mask_lanes = lax.dot_general(
@@ -650,10 +671,7 @@
         preferred_element_type=f32,
     )
     lane_group = lax.broadcasted_iota(jnp.int32, (seqs, lanes), 1) // width
-    for at, (lhs, rhs) in enumerate(((rightt_ref, gor_ref), (leftt_ref, goc_ref))):
-        total = lax.dot_general(
-            lhs[...], rhs[...], (((0,), (0,)), ((), ())), preferred_element_type=f32
-        )
+    for at, total in enumerate(totals):
         total = (total * mask_lanes).astype(bf16).astype(f32)
         for y in range(2):
             for e in range(depths):

time: 40 us -> 40.7 us (1.018)
  Pallas kernels: 12.1 us -> 13.2 us
    pallas_call x1, Pallas kernels: 2.03 us -> 2.7 us  [whole_plan(): pl.pallas_call(functools.partial(projector_kernel, sizes), out_shape=(sha...]
  transfers between devices with their start and end apart: 16 -> 16, of which waited for: 6 -> 5; matrix products, arithmetic and copies ran while one was open for 2% -> 2% of each run, Pallas kernels for 21% -> 21%
where the time goes in v12:
time: 40.7 us; the launch traced here: 40.5 us
  starting transfers between devices  15.9 us (39%)
  Pallas kernels  13.2 us (32%)
  waiting for transfers between devices  9.03 us (22%)
  local copies, waits for them, and re-layouts  1.49 us (4%)
  between operations  0.84 us (2%)
    ppermute x7, starting transfers between devices, swap_col(): lax.ppermute(block, 'col', [(at, at ^ partner) for at in range(count)])  11.3 us
    ppermute x7, waiting for transfers between devices, swap_col(): lax.ppermute(block, 'col', [(at, at ^ partner) for at in range(count)])  7.35 us
    ppermute x2, starting transfers between devices, swap_line(): return lax.ppermute(block, ('depth', 'col'), pairs)  3.13 us
    pallas_call x1, Pallas kernels, whole_plan(): pl.pallas_call(functools.partial(projector_kernel, sizes), out_shape=(sha...  2.7 us
    pallas_call x1, Pallas kernels, whole_plan(): pl.pallas_call(functools.partial(outer_kernel, sizes, orders), out_shape=...  2.43 us
    pallas_call x1, Pallas kernels, whole_plan(): pl.pallas_call(functools.partial(transition_kernel, sizes, orders), out_s...  2.41 us
    pallas_call x1, Pallas kernels, whole_plan(): pl.pallas_call(pre_kernel, out_shape=(shape((1, rows + 2 * per, pair_widt...  2.03 us
    ppermute x2, waiting for transfers between devices, swap_line(): return lax.ppermute(block, ('depth', 'col'), pairs)  1.56 us
  transfers between devices with their start and end apart: 16, of which 5 were waited for; matrix products, arithmetic and copies ran while one was open for 2% of the time, Pallas kernels for 21%

profile of v12, /device:TPU:0, one launch (start us, length us, event | category | flops | bytes accessed | tf_op | source)
XLA Modules:
  0.0 40.5 jit_solution(3140532593166978188)
XLA Ops:
  0.6 0.1 pad_add_fusion.ids_ref
  0.7 2.0 %project.1 = (bf16[1,272,128]{2,1,0:T(8,128)(2,1)S(1)}, f32[1,256]{1,0:T(1,128)S(1)}, bf16[32,256]{1,0:T(8,128)(2,1)S(1)}, bf16[32,256]{1,0:T(8,128)(2,1)S(1)}, ...) custom-call(s32[2]{0:T(128)S(1)} %pad_add_fusion.ids_ref, ...), custom_call_target="tpu_custom_call" | custom-call | tf_op jit(solution)/shard_map/project/pallas_call | solution.py:814
  2.8 5.1 %collective-permute-start = (bf16[1,272,128]{2,1,0:T(8,128)(2,1)S(1)}, bf16[1,272,128]{2,1,0:T(8,128)(2,1)S(1)}, u32[]{:S(2)}, u32[]{:S(2)}) collective-permute-start(bf16[1,272,128]{2,1,0:T(8,128)(2,1)S(1)} %get-tuple-element.59), channel_id=1, source_target_pairs={{0,6},{1,7},{2,4},{3,5},{4,2},{5,3},{6,0},{7,1},{8,14},{9,15},{10,... | collective-permute-start | bytes 208904 | tf_op jit(solution)/shard_map/ppermute | solution.py:774
  7.9 0.0 collective-permute-start.1
  7.9 0.6 %collective-permute-start.2 = (bf16[1,272,128]{2,1,0:T(8,128)(2,1)S(1)}, bf16[1,272,128]{2,1,0:T(8,128)(2,1)S(1)}, u32[]{:S(2)}, u32[]{:S(2)}) collective-permute-start(bf16[1,272,128]{2,1,0:T(8,128)(2,1)S(1)} %get-tuple-element.59), channel_id=1, source_target_pairs={{0,2},{1,3},{2,0},{3,1},{4,6},{5,7},{6,4},{7,5},{8,10},{9,11},{10,... | collective-permute-start | bytes 208904 | tf_op jit(solution)/shard_map/ppermute | solution.py:774
  8.5 1.7 %collective-permute-start.3 = (bf16[128,256]{1,0:T(8,128)(2,1)S(1)}, bf16[128,256]{1,0:T(8,128)(2,1)S(1)}, u32[]{:S(2)}, u32[]{:S(2)}) collective-permute-start(bf16[128,256]{1,0:T(8,128)(2,1)S(1)} %get-tuple-element.112), channel_id=1, source_target_pairs={{0,1},{1,0},{2,3},{3,2},{4,5},{5,4},{6,7},{7,6},{8,9},{9,8},{10,11... | collective-permute-start | bytes 196616 | tf_op jit(solution)/shard_map/ppermute | solution.py:774
  10.3 0.3 collective-permute-done
  10.5 3.2 %collective-permute-done.1 = bf16[1,272,128]{2,1,0:T(8,128)(2,1)S(1)} collective-permute-done((bf16[1,272,128]{2,1,0:T(8,128)(2,1)S(1)}, bf16[1,272,128]{2,1,0:T(8,128)(2,1)S(1)}, u32[]{:S(2)}, u32[]{:S(2)}) %collective-permute-start.1) | collective-permute-done | bytes 69664 | tf_op jit(solution)/shard_map/ppermute | solution.py:774
  13.8 0.0 collective-permute-done.2
  13.8 0.0 copy-start
  13.8 0.0 collective-permute-done.3
  13.9 1.6 %collective-permute-start.5 = (bf16[4,144,128]{2,1,0:T(8,128)(2,1)S(1)}, bf16[4,144,128]{2,1,0:T(8,128)(2,1)S(1)}, u32[]{:S(2)}, u32[]{:S(2)}) collective-permute-start(bf16[4,144,128]{2,1,0:T(8,128)(2,1)S(1)} %slice.20.near_ref), channel_id=1, source_target_pairs={{0,1},{1,0},{2,3},{3,2},{4,5},{5,4},{6,7},{7,6},{8,9},{9,8},{10,11... | collective-permute-start | bytes 442376 | tf_op jit(solution)/shard_map/ppermute | solution.py:774
  15.5 0.0 collective-permute-start.6
  15.5 3.8 %collective-permute-done.5.far_ref = bf16[4,144,128]{2,1,0:T(8,128)(2,1)S(1)} collective-permute-done((bf16[4,144,128]{2,1,0:T(8,128)(2,1)S(1)}, bf16[4,144,128]{2,1,0:T(8,128)(2,1)S(1)}, u32[]{:S(2)}, u32[]{:S(2)}) %collective-permute-start.5) | collective-permute-done | bytes 147488 | tf_op jit(solution)/shard_map/ppermute | solution.py:774
  19.3 0.0 collective-permute-start.7
  19.3 1.8 %collective-permute-start.4 = (bf16[4,128,128]{2,1,0:T(8,128)(2,1)S(1)}, bf16[4,128,128]{2,1,0:T(8,128)(2,1)S(1)}, u32[]{:S(2)}, u32[]{:S(2)}) collective-permute-start(bf16[4,128,128]{2,1,0:T(8,128)(2,1)S(1)} %slice.19.near_ref), channel_id=1, source_target_pairs={{0,1},{1,0},{2,3},{3,2},{4,5},{5,4},{6,7},{7,6},{8,9},{9,8},{10,11... | collective-permute-start | bytes 393224 | tf_op jit(solution)/shard_map/ppermute | solution.py:774
  21.1 0.2 collective-permute-start.10
  21.3 0.0 copy-done
  21.3 0.1 copy.19
  21.4 0.4 %collective-permute-start.8 = (bf16[128,256]{1,0:T(8,128)(2,1)S(1)}, bf16[128,256]{1,0:T(8,128)(2,1)S(1)}, u32[]{:S(2)}, u32[]{:S(2)}) collective-permute-start(bf16[128,256]{1,0:T(8,128)(2,1)S(1)} %get-tuple-element.75), channel_id=1, source_target_pairs={{0,1},{1,0},{2,3},{3,2},{4,5},{5,4},{6,7},{7,6},{8,9},{9,8},{10,11... | collective-permute-start | bytes 196616 | tf_op jit(solution)/shard_map/ppermute | solution.py:774
  21.9 0.0 collective-permute-done.6.other_near_ref
  21.9 0.0 collective-permute-done.7.other_far_ref
  21.9 2.4 %outer_products.1 = (bf16[512,1024]{1,0:T(8,128)(2,1)S(1)}, f32[512,128]{1,0:T(8,128)S(1)}, f32[512,128]{1,0:T(8,128)S(1)}, bf16[512,128]{1,0:T(8,128)(2,1)S(1)}, f32[32,128]{1,0:T(8,128)S(1)}) custom-call(s32[2]{0:T(128)S(1)} %pad_add_fusion.ids_ref, bf16[4,144,128]{2,1,0:T(8,128)(2,1)S(1)} %slice.20.near_ref, ...), custom_call_target="tpu_custom_call" | custom-call | tf_op jit(solution)/shard_map/outer_products/pallas_call | solution.py:871
  24.3 0.0 copy-start.1
  24.3 0.0 copy-start.2
  24.3 1.4 %turned.1 = (bf16[1024,128]{1,0:T(8,128)(2,1)S(1)}, bf16[1024,128]{1,0:T(8,128)(2,1)S(1)}) custom-call(s32[2]{0:T(128)S(1)} %pad_add_fusion.ids_ref, bf16[4,144,128]{2,1,0:T(8,128)(2,1)S(1)} %slice.20.near_ref, bf16[4,144,128]{2,1,0:T(8,128)(2,1)S(1)} %collective-permute-done.5.far_ref, bf16[4,144,128]{2,1,0:T(8,128)(2,1)S(1)} %collective-permute-done.6.other_near_ref, ...), custom_call_target="tpu_custom_call" | custom-call | tf_op jit(solution)/shard_map/turned/pallas_call | solution.py:894
  25.7 0.0 collective-permute-done.4.far_ref
  25.8 2.4 %transition.1 = (bf16[64,128]{1,0:T(8,128)(2,1)}, bf16[512,128]{1,0:T(8,128)(2,1)S(1)}, bf16[512,128]{1,0:T(8,128)(2,1)S(1)}, bf16[512,512]{1,0:T(8,128)(2,1)S(1...) custom-call(s32[2]{0:T(128)S(1)} %pad_add_fusion.ids_ref, bf16[4,128,128]{2,1,0:T(8,128)(2,1)S(1)} %slice.19.near_ref, ...), custom_call_target="tpu_custom_call" | custom-call | tf_op jit(solution)/shard_map/transition/pallas_call | solution.py:912
  28.2 0.0 collective-permute-done.8
  28.2 0.1 collective-permute-start.11
  28.3 0.5 %collective-permute-start.9 = (bf16[512,128]{1,0:T(8,128)(2,1)S(1)}, bf16[512,128]{1,0:T(8,128)(2,1)S(1)}, u32[]{:S(2)}, u32[]{:S(2)}) collective-permute-start(bf16[512,128]{1,0:T(8,128)(2,1)S(1)} %get-tuple-element.76.opm_ref), channel_id=1, source_target_pairs={{0,8},{8,0},{1,9},{9,1},{2,10},{10,2},{3,11},{11,3},{4,12},{12,4},... | collective-permute-start | bytes 393224 | tf_op jit(solution)/shard_map/ppermute | solution.py:763
  28.8 0.9 %weight_gradients.1.mine_ref = bf16[2048,128]{1,0:T(8,128)(2,1)S(1)} custom-call(bf16[512,1024]{1,0:T(8,128)(2,1)S(1)} %get-tuple-element.79.outer_ref, bf16[512,128]{1,0:T(8,128)(2,1)S(1)} %get-tuple-element.76.opm_ref, bf16[512,128]{1,0:T(8,128)(2,1)S(1)} %get-tuple-element.80.pn_ref, bf16[512,512]{1,0:T(8,128)(2,1)S(1)} %get-tuple-element.81.gh_ref, ...), custom_call_target="tpu_custom_call" | custom-call | tf_op jit(solution)/shard_map/weight_gradients/pallas_call | solution.py:943
  29.7 0.0 collective-permute-done.10.other_normed_ref
  29.7 0.0 collective-permute-done.11.other_far_normed_ref
  29.7 0.1 collective-permute-done.9.other_opm_ref
  29.8 2.7 %projector_parts.1 = (bf16[64,256]{1,0:T(8,128)(2,1)S(1)}, bf16[256,256]{1,0:T(8,128)(2,1)S(1)}) custom-call(s32[2]{0:T(128)S(1)} %pad_add_fusion.ids_ref, bf16[512,128]{1,0:T(8,128)(2,1)S(1)} %get-tuple-element.76.opm_ref, bf16[512,128]{1,0:T(8,128)(2,1)S(1)} %collective-permute-done.9.other_opm_ref, bf16[1024,128]{1,0:T(8,128)(2,1)S(1)} %get-tuple-element.85.rightt_ref, ...), custom_call_target="tpu_custom_call" | custom-call | tf_op jit(solution)/shard_map/projector_parts/pallas_call | solution.py:955
  32.5 0.4 collective-permute-start.15
  32.9 2.5 %collective-permute-start.12 = (bf16[64,256]{1,0:T(8,128)(2,1)S(1)}, bf16[64,256]{1,0:T(8,128)(2,1)S(1)}, u32[]{:S(2)}, u32[]{:S(2)}) collective-permute-start(bf16[64,256]{1,0:T(8,128)(2,1)S(1)} %get-tuple-element.92), channel_id=1, source_target_pairs={{0,6},{1,7},{2,4},{3,5},{4,2},{5,3},{6,0},{7,1},{8,12},{9,13},{10,... | collective-permute-start | bytes 98312 | tf_op jit(solution)/shard_map/ppermute | solution.py:759
  35.4 0.7 %collective-permute-start.13 = (bf16[64,256]{1,0:T(8,128)(2,1)S(1)}, bf16[64,256]{1,0:T(8,128)(2,1)S(1)}, u32[]{:S(2)}, u32[]{:S(2)}) collective-permute-start(bf16[64,256]{1,0:T(8,128)(2,1)S(1)} %get-tuple-element.92), channel_id=1, source_target_pairs={{8,10},{9,11},{10,8},{11,9},{12,14},{13,15},{14,12},{15,13},{24,26... | collective-permute-start | bytes 98312 | tf_op jit(solution)/shard_map/ppermute | solution.py:759
  36.0 0.3 features.1
  36.3 0.7 %reshape.44 = bf16[64,4,256]{2,1,0:T(4,128)(2,1)} reshape(bf16[256,256]{1,0:T(8,128)(2,1)S(1)} %features.1) | data formatting | bytes 262144 | tf_op jit(solution)/shard_map/reshape | solution.py:1011
  37.0 1.6 %collective-permute-done.12 = bf16[64,256]{1,0:T(8,128)(2,1)S(1)} collective-permute-done((bf16[64,256]{1,0:T(8,128)(2,1)S(1)}, bf16[64,256]{1,0:T(8,128)(2,1)S(1)}, u32[]{:S(2)}, u32[]{:S(2)}) %collective-permute-start.12) | collective-permute-done | bytes 32800 | tf_op jit(solution)/shard_map/ppermute | solution.py:759
  38.6 0.0 collective-permute-done.13
  38.6 0.2 collective-permute-start.14
  38.9 0.0 collective-permute-done.15.other_ref
  38.9 1.0 %sums_over_depth.1 = (f32[1024,128]{1,0:T(8,128)}, f32[128,512]{1,0:T(8,128)}, f32[512,128]{1,0:T(8,128)}) custom-call(bf16[2048,128]{1,0:T(8,128)(2,1)S(1)} %weight_gradients.1.mine_ref, bf16[2048,128]{1,0:T(8,128)(2,1)S(1)} %collective-permute-done.15.other_ref), custom_call_target="tpu_custom_call" | custom-call | tf_op jit(solution)/shard_map/sums_over_depth/pallas_call | solution.py:997
  39.9 0.0 collective-permute-done.14
  39.9 0.6 %slice_bitcast_fusion = (f32[256,32]{0,1:T(8,128)}, f32[256,32]{0,1:T(8,128)}) fusion(f32[64,256]{1,0:T(8,128)S(1)} %convert_add_fusion), kind=kLoop, calls=%fused_computation.3 | loop fusion | bytes 131072 | tf_op jit(solution)/shard_map/transpose | solution.py:1022
  (10 shorter events, 0.1 us)
Async XLA Ops:
  2.8 7.8 %collective-permute-start = (bf16[1,272,128]{2,1,0:T(8,128)(2,1)S(1)}, bf16[1,272,128]{2,1,0:T(8,128)(2,1)S(1)}, u32[]{:S(2)}, u32[]{:S(2)}) collective-permute-start(bf16[1,272,128]{2,1,0:T(8,128)(2,1)S(1)} %get-tuple-element.59), channel_id=1, source_target_pairs={{0,6},{1,7},{2,4},{3,5},{4,2},{5,3},{6,0},{7,1},{8,14},{9,15},{10,... | collective-permute-start | bytes 208904 | tf_op jit(solution)/shard_map/ppermute | solution.py:774
  7.9 5.9 %collective-permute-start.1 = (bf16[1,272,128]{2,1,0:T(8,128)(2,1)S(1)}, bf16[1,272,128]{2,1,0:T(8,128)(2,1)S(1)}, u32[]{:S(2)}, u32[]{:S(2)}) collective-permute-start(bf16[1,272,128]{2,1,0:T(8,128)(2,1)S(1)} %get-tuple-element.59), channel_id=1, source_target_pairs={{0,4},{1,5},{2,6},{3,7},{4,0},{5,1},{6,2},{7,3},{8,12},{9,13},{10,... | collective-permute-start | bytes 208904 | tf_op jit(solution)/shard_map/ppermute | solution.py:774
  7.9 5.9 %collective-permute-start.2 = (bf16[1,272,128]{2,1,0:T(8,128)(2,1)S(1)}, bf16[1,272,128]{2,1,0:T(8,128)(2,1)S(1)}, u32[]{:S(2)}, u32[]{:S(2)}) collective-permute-start(bf16[1,272,128]{2,1,0:T(8,128)(2,1)S(1)} %get-tuple-element.59), channel_id=1, source_target_pairs={{0,2},{1,3},{2,0},{3,1},{4,6},{5,7},{6,4},{7,5},{8,10},{9,11},{10,... | collective-permute-start | bytes 208904 | tf_op jit(solution)/shard_map/ppermute | solution.py:774
  8.5 5.3 %collective-permute-start.3 = (bf16[128,256]{1,0:T(8,128)(2,1)S(1)}, bf16[128,256]{1,0:T(8,128)(2,1)S(1)}, u32[]{:S(2)}, u32[]{:S(2)}) collective-permute-start(bf16[128,256]{1,0:T(8,128)(2,1)S(1)} %get-tuple-element.112), channel_id=1, source_target_pairs={{0,1},{1,0},{2,3},{3,2},{4,5},{5,4},{6,7},{7,6},{8,9},{9,8},{10,11... | collective-permute-start | bytes 196616 | tf_op jit(solution)/shard_map/ppermute | solution.py:774
  13.8 7.5 %copy-start = (bf16[1024,128]{1,0:T(8,128)(2,1)S(1)}, bf16[1024,128]{1,0:T(8,128)(2,1)}, u32[]{:S(2)}) copy-start(bf16[1024,128]{1,0:T(8,128)(2,1)} %wout_ref.1) | copy-start | bytes 786436
  13.9 5.4 %collective-permute-start.5 = (bf16[4,144,128]{2,1,0:T(8,128)(2,1)S(1)}, bf16[4,144,128]{2,1,0:T(8,128)(2,1)S(1)}, u32[]{:S(2)}, u32[]{:S(2)}) collective-permute-start(bf16[4,144,128]{2,1,0:T(8,128)(2,1)S(1)} %slice.20.near_ref), channel_id=1, source_target_pairs={{0,1},{1,0},{2,3},{3,2},{4,5},{5,4},{6,7},{7,6},{8,9},{9,8},{10,11... | collective-permute-start | bytes 442376 | tf_op jit(solution)/shard_map/ppermute | solution.py:774
  15.5 6.4 %collective-permute-start.6 = (bf16[4,144,128]{2,1,0:T(8,128)(2,1)S(1)}, bf16[4,144,128]{2,1,0:T(8,128)(2,1)S(1)}, u32[]{:S(2)}, u32[]{:S(2)}) collective-permute-start(bf16[4,144,128]{2,1,0:T(8,128)(2,1)S(1)} %slice.20.near_ref), channel_id=1, source_target_pairs={{0,8},{8,0},{1,9},{9,1},{2,10},{10,2},{3,11},{11,3},{4,12},{12,4},... | collective-permute-start | bytes 442376 | tf_op jit(solution)/shard_map/ppermute | solution.py:763
  19.3 2.6 %collective-permute-start.7 = (bf16[4,144,128]{2,1,0:T(8,128)(2,1)S(1)}, bf16[4,144,128]{2,1,0:T(8,128)(2,1)S(1)}, u32[]{:S(2)}, u32[]{:S(2)}) collective-permute-start(bf16[4,144,128]{2,1,0:T(8,128)(2,1)S(1)} %collective-permute-done.5.far_ref), channel_id=1, source_target_pairs={{0,8},{8,0},{1,9},{9,1},{2,10},{10,2},{3,11},{11,3},{4,12},{12,4},... | collective-permute-start | bytes 442376 | tf_op jit(solution)/shard_map/ppermute | solution.py:763
  19.3 6.4 %collective-permute-start.4 = (bf16[4,128,128]{2,1,0:T(8,128)(2,1)S(1)}, bf16[4,128,128]{2,1,0:T(8,128)(2,1)S(1)}, u32[]{:S(2)}, u32[]{:S(2)}) collective-permute-start(bf16[4,128,128]{2,1,0:T(8,128)(2,1)S(1)} %slice.19.near_ref), channel_id=1, source_target_pairs={{0,1},{1,0},{2,3},{3,2},{4,5},{5,4},{6,7},{7,6},{8,9},{9,8},{10,11... | collective-permute-start | bytes 393224 | tf_op jit(solution)/shard_map/ppermute | solution.py:774
  21.1 8.6 %collective-permute-start.10 = (bf16[256,256]{1,0:T(8,128)(2,1)S(1)}, bf16[256,256]{1,0:T(8,128)(2,1)S(1)}, u32[]{:S(2)}, u32[]{:S(2)}) collective-permute-start(bf16[256,256]{1,0:T(8,128)(2,1)S(1)} %get-tuple-element.60.normed_ref), channel_id=1, source_target_pairs={{0,8},{8,0},{1,9},{9,1},{2,10},{10,2},{3,11},{11,3},{4,12},{12,4},... | collective-permute-start | bytes 393224 | tf_op jit(solution)/shard_map/ppermute | solution.py:763
  21.4 6.8 %collective-permute-start.8 = (bf16[128,256]{1,0:T(8,128)(2,1)S(1)}, bf16[128,256]{1,0:T(8,128)(2,1)S(1)}, u32[]{:S(2)}, u32[]{:S(2)}) collective-permute-start(bf16[128,256]{1,0:T(8,128)(2,1)S(1)} %get-tuple-element.75), channel_id=1, source_target_pairs={{0,1},{1,0},{2,3},{3,2},{4,5},{5,4},{6,7},{7,6},{8,9},{9,8},{10,11... | collective-permute-start | bytes 196616 | tf_op jit(solution)/shard_map/ppermute | solution.py:774
  24.3 1.4 %copy-start.1 = (bf16[128,512]{1,0:T(8,128)(2,1)S(1)}, bf16[128,512]{1,0:T(8,128)(2,1)}, u32[]{:S(2)}) copy-start(bf16[128,512]{1,0:T(8,128)(2,1)} %hid_ref.1) | copy-start | bytes 393220
  24.3 1.4 %copy-start.2 = (bf16[512,128]{1,0:T(8,128)(2,1)S(1)}, bf16[512,128]{1,0:T(8,128)(2,1)}, u32[]{:S(2)}) copy-start(bf16[512,128]{1,0:T(8,128)(2,1)} %back_ref.1) | copy-start | bytes 393220
  28.2 1.5 %collective-permute-start.11 = (bf16[256,256]{1,0:T(8,128)(2,1)S(1)}, bf16[256,256]{1,0:T(8,128)(2,1)S(1)}, u32[]{:S(2)}, u32[]{:S(2)}) collective-permute-start(bf16[256,256]{1,0:T(8,128)(2,1)S(1)} %constant_dynamic-update-slice_fusion.far_normed_ref), channel_id=1, source_target_pairs={{0,8},{8,0},{1,9},{9,1},{2,10},{10,2},{3,11},{11,3},{4,12},{12,4},... | collective-permute-start | bytes 393224 | tf_op jit(solution)/shard_map/ppermute | solution.py:763
  28.3 1.5 %collective-permute-start.9 = (bf16[512,128]{1,0:T(8,128)(2,1)S(1)}, bf16[512,128]{1,0:T(8,128)(2,1)S(1)}, u32[]{:S(2)}, u32[]{:S(2)}) collective-permute-start(bf16[512,128]{1,0:T(8,128)(2,1)S(1)} %get-tuple-element.76.opm_ref), channel_id=1, source_target_pairs={{0,8},{8,0},{1,9},{9,1},{2,10},{10,2},{3,11},{11,3},{4,12},{12,4},... | collective-permute-start | bytes 393224 | tf_op jit(solution)/shard_map/ppermute | solution.py:763
  32.5 6.4 %collective-permute-start.15 = (bf16[2048,128]{1,0:T(8,128)(2,1)S(1)}, bf16[2048,128]{1,0:T(8,128)(2,1)S(1)}, u32[]{:S(2)}, u32[]{:S(2)}) collective-permute-start(bf16[2048,128]{1,0:T(8,128)(2,1)S(1)} %weight_gradients.1.mine_ref), channel_id=1, source_target_pairs={{0,8},{8,0},{1,9},{9,1},{2,10},{10,2},{3,11},{11,3},{4,12},{12,4},... | collective-permute-start | bytes 1572872 | tf_op jit(solution)/shard_map/ppermute | solution.py:763
  32.9 5.7 %collective-permute-start.12 = (bf16[64,256]{1,0:T(8,128)(2,1)S(1)}, bf16[64,256]{1,0:T(8,128)(2,1)S(1)}, u32[]{:S(2)}, u32[]{:S(2)}) collective-permute-start(bf16[64,256]{1,0:T(8,128)(2,1)S(1)} %get-tuple-element.92), channel_id=1, source_target_pairs={{0,6},{1,7},{2,4},{3,5},{4,2},{5,3},{6,0},{7,1},{8,12},{9,13},{10,... | collective-permute-start | bytes 98312 | tf_op jit(solution)/shard_map/ppermute | solution.py:759
  35.4 3.2 %collective-permute-start.13 = (bf16[64,256]{1,0:T(8,128)(2,1)S(1)}, bf16[64,256]{1,0:T(8,128)(2,1)S(1)}, u32[]{:S(2)}, u32[]{:S(2)}) collective-permute-start(bf16[64,256]{1,0:T(8,128)(2,1)S(1)} %get-tuple-element.92), channel_id=1, source_target_pairs={{8,10},{9,11},{10,8},{11,9},{12,14},{13,15},{14,12},{15,13},{24,26... | collective-permute-start | bytes 98312 | tf_op jit(solution)/shard_map/ppermute | solution.py:759
  38.6 1.3 %collective-permute-start.14 = (bf16[64,256]{1,0:T(8,128)(2,1)S(1)}, bf16[64,256]{1,0:T(8,128)(2,1)S(1)}, u32[]{:S(2)}, u32[]{:S(2)}) collective-permute-start(bf16[64,256]{1,0:T(8,128)(2,1)S(1)} %add_convert_fusion), channel_id=1, source_target_pairs={{0,8},{8,0},{1,9},{9,1},{2,10},{10,2},{3,11},{11,3},{4,12},{12,4},... | collective-permute-start | bytes 98312 | tf_op jit(solution)/shard_map/ppermute | solution.py:763

commit v13 on v10

--- a/solution.py
+++ b/solution.py
@@ -367,9 +367,16 @@
     sent_ref[0, 2 * seqs : first_pair, :] = tile_ref[...].astype(jnp.bfloat16)
 
 
+def by_owner(ids_ref, z, near_ref, far_ref):
+    step = z ^ (ids_ref[1] // 2)
+    place = (near_ref.shape[0] - step) % near_ref.shape[0]
+    near, far = near_ref[place], far_ref[place]
+    first = ids_ref[1] % 2 == 0
+    return jnp.where(first, near, far), jnp.where(first, far, near)
+
+
 def outer_kernel(
     sizes,
-    orders,
     ids_ref,
     near_ref,
     far_ref,
@@ -381,59 +388,69 @@
     cnt_ref,
     pm_ref,
     maskt_ref,
-    got_ref,
+    rightt_ref,
+    leftt_ref,
     leftn_ref,
     mine_ref,
-    turn_ref,
+    turnl_ref,
+    turnr_ref,
     cntl_ref,
     pml_ref,
 ):
     seqs, res, pair_cols, width = sizes
-    depths, cols = got_ref.shape[0], got_ref.shape[1]
+    line = near_ref.shape[0]
+    cols = 2 * line
     residues = cols * res
     lanes = res * width
-    half_cols = pair_cols // res
     me_depth = ids_ref[0]
-    me_col = ids_ref[1]
+    lower = me_depth == 0
     f32, bf16 = jnp.float32, jnp.bfloat16
 
-    for order, mine, other in zip(orders, (near_ref, far_ref), (other_near_ref, other_far_ref)):
-        for at, partner in enumerate(order):
-            got_ref[me_depth, me_col ^ partner] = mine[at]
-            got_ref[1 - me_depth, me_col ^ partner] = other[at]
-
-    for e in range(depths):
-        for k in range(cols):
-            leftn_ref[e * seqs : (e + 1) * seqs, k * lanes : (k + 1) * lanes] = got_ref[
-                e, k, 0:seqs, :
+    for z in range(line):
+        mine = by_owner(ids_ref, z, near_ref, far_ref)
+        other = by_owner(ids_ref, z, other_near_ref, other_far_ref)
+        for y in range(2):
+            lanes_k = slice((2 * z + y) * lanes, (2 * z + y + 1) * lanes)
+            both = jnp.concatenate(
+                [
+                    jnp.where(lower, mine[y], other[y]),
+                    jnp.where(lower, other[y], mine[y]),
+                ],
+                axis=0,
+            )
+            rows = both.shape[0] // 2
+            left = jnp.concatenate([both[0:seqs], both[rows : rows + seqs]], axis=0)
+            right = jnp.concatenate(
+                [both[seqs : 2 * seqs], both[rows + seqs : rows + 2 * seqs]], axis=0
+            )
+            leftn_ref[:, lanes_k] = left
+            turnl_ref[lanes_k, :] = left.astype(f32).T
+            turnr_ref[lanes_k, :] = right.astype(f32).T
+            tiles = [
+                both[first + 2 * seqs : first + 2 * seqs + MASK_ROWS].astype(f32)
+                for first in (0, rows)
             ]
-    for k in range(half_cols):
-        block = jnp.concatenate(
-            [
-                got_ref[e, me_depth * half_cols + k, seqs : 2 * seqs, :]
-                for e in range(depths)
-            ],
-            axis=0,
-        ).astype(f32)
-        turn_ref[k * lanes : (k + 1) * lanes, :] = block.T
+            maskt_ref[(2 * z + y) * res : (2 * z + y + 1) * res, :] = (
+                tiles[0][0:res] + tiles[1][0:res]
+            )
+            own = mine[y][2 * seqs : 2 * seqs + MASK_ROWS].astype(f32)
+            pair_lane = lax.broadcasted_iota(jnp.int32, (pair_cols, lanes), 1)
+            pair_row = lax.broadcasted_iota(jnp.int32, (pair_cols, lanes), 0)
+            for r in range(res):
+                first = ((2 * z + y) * res + r) * pair_cols
+                pml_ref[first : first + pair_cols, :] = jnp.where(
+                    pair_lane == pair_row, own[res + r : res + r + 1, :], 0.0
+                ).astype(bf16)
     for d in range(width):
-        mine_ref[d * pair_cols : (d + 1) * pair_cols, :] = turn_ref[
-            pl.ds(d, pair_cols, stride=width), :
+        mine_ref[d * pair_cols : (d + 1) * pair_cols, :] = turnr_ref[
+            pl.ds(me_depth * pair_cols * width + d, pair_cols, stride=width), :
         ].astype(bf16)
-
-    base = 2 * seqs
-    pair_lane = lax.broadcasted_iota(jnp.int32, (pair_cols, lanes), 1)
-    pair_row = lax.broadcasted_iota(jnp.int32, (pair_cols, lanes), 0)
-    for k in range(cols):
-        tiles = [got_ref[e, k, base : base + MASK_ROWS, :].astype(f32) for e in range(depths)]
-        maskt_ref[k * res : (k + 1) * res, :] = tiles[0][0:res] + tiles[1][0:res]
-        own = got_ref[me_depth, k, base : base + MASK_ROWS, :].astype(f32)
-        for r in range(res):
-            row = own[res + r : res + r + 1, :]
-            first = (k * res + r) * pair_cols
-            pml_ref[first : first + pair_cols, :] = jnp.where(
-                pair_lane == pair_row, row, 0.0
-            ).astype(bf16)
+    for turned, out in ((turnl_ref, leftt_ref), (turnr_ref, rightt_ref)):
+        for d in range(width):
+            out[d * residues : (d + 1) * residues, :] = turned[
+                pl.ds(d, residues, stride=width), :
+            ].astype(bf16)
+
     maskt = maskt_ref[...]
     cols_mask = maskt_ref[pl.ds(pl.multiple_of(me_depth * pair_cols, pair_cols), pair_cols), :]
     for i in range(residues):
@@ -463,44 +480,8 @@
     proj_out_ref[...] = jnp.dot(outer_ref[...], wturn_ref[...], preferred_element_type=f32)
 
 
-def turn_kernel(
-    sizes,
-    orders,
-    ids_ref,
-    near_ref,
-    far_ref,
-    other_near_ref,
-    other_far_ref,
-    rightt_ref,
-    leftt_ref,
-    got_ref,
-    turn_ref,
-):
-    seqs, res, _, width = sizes
-    depths, cols = got_ref.shape[0], got_ref.shape[1]
-    lanes = res * width
-    residues = res * cols
-    me_depth = ids_ref[0]
-    me_col = ids_ref[1]
-    for order, mine, other in zip(orders, (near_ref, far_ref), (other_near_ref, other_far_ref)):
-        for at, partner in enumerate(order):
-            got_ref[me_depth, me_col ^ partner] = mine[at, 0 : 2 * seqs, :]
-            got_ref[1 - me_depth, me_col ^ partner] = other[at, 0 : 2 * seqs, :]
-    for at, out in ((0, leftt_ref), (1, rightt_ref)):
-        for k in range(cols):
-            block = jnp.concatenate(
-                [got_ref[e, k, at * seqs : (at + 1) * seqs, :] for e in range(depths)], axis=0
-            ).astype(jnp.float32)
-            turn_ref[k * lanes : (k + 1) * lanes, :] = block.T
-        for d in range(width):
-            out[d * residues : (d + 1) * residues, :] = turn_ref[
-                pl.ds(d, residues, stride=width), :
-            ].astype(jnp.bfloat16)
-
-
 def transition_kernel(
     sizes,
-    orders,
     ids_ref,
     near_ref,
     far_ref,
@@ -516,25 +497,20 @@
     gh_ref,
     hidden_ref,
     mg_ref,
-    pgot_ref,
     gmid_ref,
 ):
     seqs, res, pair_cols, width = sizes
     per = res * pair_cols
-    cols = pgot_ref.shape[0]
+    cols = 2 * near_ref.shape[0]
     me_col = ids_ref[1]
     f32, bf16 = jnp.float32, jnp.bfloat16
-    for order, mine in zip(orders, (near_ref, far_ref)):
-        for at, partner in enumerate(order):
-            pgot_ref[me_col ^ partner] = mine[at]
     gain = gain_ref[...]
     chunk = 2 * per
     for at in range(cols // 2):
         rows = slice(at * chunk, (at + 1) * chunk)
+        blocks = by_owner(ids_ref, at, near_ref, far_ref)
         act, grad = [
-            jnp.concatenate(
-                [pgot_ref[2 * at + b, w * per : (w + 1) * per, :] for b in range(2)], axis=0
-            )
+            jnp.concatenate([block[w * per : (w + 1) * per] for block in blocks], axis=0)
             for w in range(2)
         ]
         count = cnt_ref[rows, :]
@@ -589,7 +565,7 @@
     rows_ref,
 ):
     seqs, res, pair_cols, width = sizes
-    depths, half = gf_ref.shape[0], gf_ref.shape[1]
+    depths, half = rows_ref.shape[1], gf_ref.shape[0]
     residues = half // pair_cols
     lanes = res * width
     here = 2 * res
@@ -598,8 +574,8 @@
     me_y = me_col % 2
     first_here = (me_col // 2) * here
     f32, bf16 = jnp.float32, jnp.bfloat16
-    gf_ref[me_depth] = opm_ref[...].astype(f32)
-    gf_ref[1 - me_depth] = other_opm_ref[...].astype(f32)
+    my_half = first_here // pair_cols
+    gf_ref[...] = jnp.where(my_half == me_depth, opm_ref[...], other_opm_ref[...]).astype(f32)
     for y, e, block in (
         (me_y, me_depth, normed_ref),
         (1 - me_y, me_depth, far_normed_ref),
@@ -609,16 +585,14 @@
         rows_ref[y, e] = block[...]
 
     for il in range(here):
-        for e in range(depths):
-            first = pl.multiple_of((first_here + il) * pair_cols, pair_cols)
-            grow_ref[il * residues + e * pair_cols : il * residues + (e + 1) * pair_cols, :] = (
-                gf_ref[e, pl.ds(first, pair_cols), :].astype(bf16)
-            )
-    my_half = first_here // pair_cols
+        first = pl.multiple_of((first_here + il) * pair_cols, pair_cols)
+        for e, block in ((me_depth, opm_ref), (1 - me_depth, other_opm_ref)):
+            to = pl.multiple_of(il * residues + e * pair_cols, pair_cols)
+            grow_ref[pl.ds(to, pair_cols), :] = block[pl.ds(first, pair_cols), :]
     my_first = first_here - my_half * pair_cols
     for jl in range(here):
         gcol_ref[jl * residues : (jl + 1) * residues, :] = gf_ref[
-            my_half, pl.ds(my_first + jl, residues, stride=pair_cols), :
+            pl.ds(my_first + jl, residues, stride=pair_cols), :
         ].astype(bf16)
     for lhs, weight, out in ((grow_ref, wturn_ref, gor_ref), (gcol_ref, wout_ref, goc_ref)):
         for dh in range(width // 4):
@@ -834,8 +808,6 @@
             )
         ],
     )
-    near_order = (0,) + Z_PARTNERS
-    far_order = tuple(at ^ Y_PARTNER for at in near_order)
     blocks = lax.optimization_barrier(
         jnp.concatenate([sent] + [swap_col(sent, partner) for partner in Z_PARTNERS])
     )
@@ -845,54 +817,37 @@
     near, pair_near = blocks[:, :rows], blocks[:, rows:]
     far = swap_col(near, Y_PARTNER)
     pair_far = swap_col(pair_near, Y_PARTNER)
-    far, normed_b = lax.optimization_barrier((far, normed[half_normed:]))
-    far_normed_b = swap_col(normed_b, Y_PARTNER)
     other_near, other_far = swap_depth(near), swap_depth(far)
     sizes = (seqs, res, pair_cols, width)
-    orders = (near_order, far_order)
-    outer, proj_out, cnt, pm, maskt = pl.pallas_call(
-        functools.partial(outer_kernel, sizes, orders),
+    outer, proj_out, cnt, pm, maskt, rightt, leftt = pl.pallas_call(
+        functools.partial(outer_kernel, sizes),
         out_shape=(
             shape((half, outer_width), bf16),
             shape((half, pair_width), f32),
             shape((half, lanes), f32),
             shape((half, lanes), bf16),
             shape((residues, depths * seqs), f32),
+            shape((residues * width, depths * seqs), bf16),
+            shape((residues * width, depths * seqs), bf16),
         ),
         in_specs=[smem] + [vmem] * 5,
-        out_specs=[vmem] * 5,
+        out_specs=[vmem] * 7,
         scratch_shapes=[
-            pltpu.VMEM((depths, cols, rows, pair_width), bf16),
             pltpu.VMEM((depths * seqs, residues * width), bf16),
             pltpu.VMEM((pair_cols * width, depths * seqs), bf16),
-            pltpu.VMEM((pair_cols * width, depths * seqs), f32),
+            pltpu.VMEM((residues * width, depths * seqs), f32),
+            pltpu.VMEM((residues * width, depths * seqs), f32),
             pltpu.VMEM((half, lanes), bf16),
             pltpu.VMEM((half, lanes), bf16),
         ],
         compiler_params=params,
         name="outer_products",
     )(ids, near, far, other_near, other_far, wturn)
-    other_near, other_far, proj_out = lax.optimization_barrier((other_near, other_far, proj_out))
-    rightt, leftt = pl.pallas_call(
-        functools.partial(turn_kernel, sizes, orders),
-        out_shape=(
-            shape((residues * width, depths * seqs), bf16),
-            shape((residues * width, depths * seqs), bf16),
-        ),
-        in_specs=[smem] + [vmem] * 4,
-        out_specs=[vmem] * 2,
-        scratch_shapes=[
-            pltpu.VMEM((depths, cols, 2 * seqs, pair_width), bf16),
-            pltpu.VMEM((residues * width, depths * seqs), f32),
-        ],
-        compiler_params=params,
-        name="turned",
-    )(ids, near, far, other_near, other_far)
-    pair_far, rightt, leftt, proj_out = lax.optimization_barrier(
-        (pair_far, rightt, leftt, proj_out)
-    )
+    normed_b, proj_out = lax.optimization_barrier((normed[half_normed:], proj_out))
+    far_normed_b = swap_col(normed_b, Y_PARTNER)
+    pair_far, proj_out = lax.optimization_barrier((pair_far, proj_out))
     couple, opm, pn, gh, hidden, mg = pl.pallas_call(
-        functools.partial(transition_kernel, sizes, orders),
+        functools.partial(transition_kernel, sizes),
         out_shape=(
             shape((per, pair_width), bf16),
             shape((half, pair_width), bf16),
@@ -904,7 +859,6 @@
         in_specs=[smem] + [vmem] * 8,
         out_specs=[vmem] * 6,
         scratch_shapes=[
-            pltpu.VMEM((cols, 2 * per, pair_width), bf16),
             pltpu.VMEM((half, pair_width), f32),
         ],
         compiler_params=params,
@@ -943,7 +897,7 @@
         in_specs=[smem] + [vmem] * 11,
         out_specs=[vmem] * 2,
         scratch_shapes=[
-            pltpu.VMEM((depths, half, pair_width), f32),
+            pltpu.VMEM((half, pair_width), f32),
             pltpu.VMEM((2 * res * residues, pair_width), bf16),
             pltpu.VMEM((2 * res * residues, pair_width), bf16),
             pltpu.VMEM((residues * width, 2 * lanes), bf16),

time: 40 us -> 40.3 us (level)
  waiting for transfers between devices: 9.2 us -> 10.1 us
  Pallas kernels: 12.1 us -> 11.3 us
    pallas_call x3 -> x2, Pallas kernels: 5.91 us -> 5.1 us  [the longest x1 2.68 us: whole_plan(): pl.pallas_call(functools.partial(outer_kernel, sizes), out_shape=(shape((...]
    ppermute x7, waiting for transfers between devices: 7.58 us -> 8.28 us  [swap_col(): lax.ppermute(block, 'col', [(at, at ^ partner) for at in range(count)])]
    ppermute x7, starting transfers between devices: 11.3 us -> 11.9 us  [swap_col(): lax.ppermute(block, 'col', [(at, at ^ partner) for at in range(count)])]
  transfers between devices with their start and end apart: 16 -> 16, of which waited for: 6 -> 7; matrix products, arithmetic and copies ran while one was open for 2% -> 2% of each run, Pallas kernels for 21% -> 18%
where the time goes in v13:
time: 40.3 us; the launch traced here: 40 us
  starting transfers between devices  16.2 us (40%)
  Pallas kernels  11.3 us (28%)
  waiting for transfers between devices  10.1 us (25%)
  local copies, waits for them, and re-layouts  1.49 us (4%)
  between operations  0.81 us (2%)
    ppermute x7, starting transfers between devices, swap_col(): lax.ppermute(block, 'col', [(at, at ^ partner) for at in range(count)])  11.9 us
    ppermute x7, waiting for transfers between devices, swap_col(): lax.ppermute(block, 'col', [(at, at ^ partner) for at in range(count)])  8.28 us
    ppermute x2, starting transfers between devices, swap_line(): return lax.ppermute(block, ('depth', 'col'), pairs)  2.98 us
    pallas_call x1, Pallas kernels, whole_plan(): pl.pallas_call(functools.partial(outer_kernel, sizes), out_shape=(shape((...  2.68 us
    pallas_call x1, Pallas kernels, whole_plan(): pl.pallas_call(functools.partial(transition_kernel, sizes), out_shape=(sh...  2.42 us
    pallas_call x1, Pallas kernels, whole_plan(): pl.pallas_call(functools.partial(projector_kernel, sizes), out_shape=(sha...  2.05 us
    pallas_call x1, Pallas kernels, whole_plan(): pl.pallas_call(pre_kernel, out_shape=(shape((1, rows + 2 * per, pair_widt...  1.91 us
    ppermute x2, waiting for transfers between devices, swap_line(): return lax.ppermute(block, ('depth', 'col'), pairs)  1.73 us
  transfers between devices with their start and end apart: 16, of which 7 were waited for; matrix products, arithmetic and copies ran while one was open for 2% of the time, Pallas kernels for 18%

profile of v13, /device:TPU:0, one launch (start us, length us, event | category | flops | bytes accessed | tf_op | source)
XLA Modules:
  0.0 40.0 jit_solution(12717048825810693076)
XLA Ops:
  0.6 0.1 pad_add_fusion.ids_ref
  0.7 1.9 %project.1 = (bf16[1,272,128]{2,1,0:T(8,128)(2,1)S(1)}, f32[1,256]{1,0:T(1,128)S(1)}, bf16[32,256]{1,0:T(8,128)(2,1)S(1)}, bf16[32,256]{1,0:T(8,128)(2,1)S(1)}, ...) custom-call(s32[2]{0:T(128)S(1)} %pad_add_fusion.ids_ref, ...), custom_call_target="tpu_custom_call" | custom-call | tf_op jit(solution)/shard_map/project/pallas_call | solution.py:770
  2.6 5.1 %collective-permute-start = (bf16[1,272,128]{2,1,0:T(8,128)(2,1)S(1)}, bf16[1,272,128]{2,1,0:T(8,128)(2,1)S(1)}, u32[]{:S(2)}, u32[]{:S(2)}) collective-permute-start(bf16[1,272,128]{2,1,0:T(8,128)(2,1)S(1)} %get-tuple-element.54), channel_id=1, source_target_pairs={{0,6},{1,7},{2,4},{3,5},{4,2},{5,3},{6,0},{7,1},{8,14},{9,15},{10,... | collective-permute-start | bytes 208904 | tf_op jit(solution)/shard_map/ppermute | solution.py:730
  7.7 0.0 collective-permute-start.1
  7.8 0.6 %collective-permute-start.2 = (bf16[1,272,128]{2,1,0:T(8,128)(2,1)S(1)}, bf16[1,272,128]{2,1,0:T(8,128)(2,1)S(1)}, u32[]{:S(2)}, u32[]{:S(2)}) collective-permute-start(bf16[1,272,128]{2,1,0:T(8,128)(2,1)S(1)} %get-tuple-element.54), channel_id=1, source_target_pairs={{0,2},{1,3},{2,0},{3,1},{4,6},{5,7},{6,4},{7,5},{8,10},{9,11},{10,... | collective-permute-start | bytes 208904 | tf_op jit(solution)/shard_map/ppermute | solution.py:730
  8.4 1.7 %collective-permute-start.3 = (bf16[128,256]{1,0:T(8,128)(2,1)S(1)}, bf16[128,256]{1,0:T(8,128)(2,1)S(1)}, u32[]{:S(2)}, u32[]{:S(2)}) collective-permute-start(bf16[128,256]{1,0:T(8,128)(2,1)S(1)} %get-tuple-element.102), channel_id=1, source_target_pairs={{0,1},{1,0},{2,3},{3,2},{4,5},{5,4},{6,7},{7,6},{8,9},{9,8},{10,11... | collective-permute-start | bytes 196616 | tf_op jit(solution)/shard_map/ppermute | solution.py:730
  10.1 0.3 collective-permute-done
  10.4 3.2 %collective-permute-done.1 = bf16[1,272,128]{2,1,0:T(8,128)(2,1)S(1)} collective-permute-done((bf16[1,272,128]{2,1,0:T(8,128)(2,1)S(1)}, bf16[1,272,128]{2,1,0:T(8,128)(2,1)S(1)}, u32[]{:S(2)}, u32[]{:S(2)}) %collective-permute-start.1) | collective-permute-done | bytes 69664 | tf_op jit(solution)/shard_map/ppermute | solution.py:730
  13.7 0.0 collective-permute-done.2
  13.7 0.0 copy-start
  13.7 0.0 collective-permute-done.3
  13.7 1.6 %collective-permute-start.5 = (bf16[4,144,128]{2,1,0:T(8,128)(2,1)S(1)}, bf16[4,144,128]{2,1,0:T(8,128)(2,1)S(1)}, u32[]{:S(2)}, u32[]{:S(2)}) collective-permute-start(bf16[4,144,128]{2,1,0:T(8,128)(2,1)S(1)} %slice.21.near_ref), channel_id=1, source_target_pairs={{0,1},{1,0},{2,3},{3,2},{4,5},{5,4},{6,7},{7,6},{8,9},{9,8},{10,11... | collective-permute-start | bytes 442376 | tf_op jit(solution)/shard_map/ppermute | solution.py:730
  15.3 0.0 collective-permute-start.6
  15.3 3.8 %collective-permute-done.5.far_ref = bf16[4,144,128]{2,1,0:T(8,128)(2,1)S(1)} collective-permute-done((bf16[4,144,128]{2,1,0:T(8,128)(2,1)S(1)}, bf16[4,144,128]{2,1,0:T(8,128)(2,1)S(1)}, u32[]{:S(2)}, u32[]{:S(2)}) %collective-permute-start.5) | collective-permute-done | bytes 147488 | tf_op jit(solution)/shard_map/ppermute | solution.py:730
  19.2 0.0 collective-permute-start.7
  19.2 1.8 %collective-permute-start.4 = (bf16[4,128,128]{2,1,0:T(8,128)(2,1)S(1)}, bf16[4,128,128]{2,1,0:T(8,128)(2,1)S(1)}, u32[]{:S(2)}, u32[]{:S(2)}) collective-permute-start(bf16[4,128,128]{2,1,0:T(8,128)(2,1)S(1)} %slice.19.near_ref), channel_id=1, source_target_pairs={{0,1},{1,0},{2,3},{3,2},{4,5},{5,4},{6,7},{7,6},{8,9},{9,8},{10,11... | collective-permute-start | bytes 393224 | tf_op jit(solution)/shard_map/ppermute | solution.py:730
  21.0 0.2 collective-permute-start.10
  21.2 0.0 copy-done
  21.2 0.1 copy.19
  21.3 0.0 collective-permute-done.6.other_near_ref
  21.3 0.0 collective-permute-done.7.other_far_ref
  21.3 0.0 copy-start.2
  21.3 2.7 %outer_products.1 = (bf16[512,1024]{1,0:T(8,128)(2,1)S(1)}, f32[512,128]{1,0:T(8,128)S(1)}, f32[512,128]{1,0:T(8,128)S(1)}, bf16[512,128]{1,0:T(8,128)(2,1)S(1)}...) custom-call(s32[2]{0:T(128)S(1)} %pad_add_fusion.ids_ref, ...), custom_call_target="tpu_custom_call" | custom-call | tf_op jit(solution)/shard_map/outer_products/pallas_call | solution.py:822
  24.0 0.0 copy-start.1
  24.0 1.0 %collective-permute-start.8 = (bf16[128,256]{1,0:T(8,128)(2,1)S(1)}, bf16[128,256]{1,0:T(8,128)(2,1)S(1)}, u32[]{:S(2)}, u32[]{:S(2)}) collective-permute-start(bf16[128,256]{1,0:T(8,128)(2,1)S(1)} %get-tuple-element.65), channel_id=1, source_target_pairs={{0,1},{1,0},{2,3},{3,2},{4,5},{5,4},{6,7},{7,6},{8,9},{9,8},{10,11... | collective-permute-start | bytes 196616 | tf_op jit(solution)/shard_map/ppermute | solution.py:730
  25.0 0.1 collective-permute-done.4.far_ref
  25.1 0.0 copy-done.2
  25.1 2.4 %transition.1 = (bf16[64,128]{1,0:T(8,128)(2,1)}, bf16[512,128]{1,0:T(8,128)(2,1)S(1)}, bf16[512,128]{1,0:T(8,128)(2,1)S(1)}, bf16[512,512]{1,0:T(8,128)(2,1)S(1...) custom-call(s32[2]{0:T(128)S(1)} %pad_add_fusion.ids_ref, bf16[4,128,128]{2,1,0:T(8,128)(2,1)S(1)} %slice.19.near_ref, ...), custom_call_target="tpu_custom_call" | custom-call | tf_op jit(solution)/shard_map/transition/pallas_call | solution.py:849
  27.6 0.8 %collective-permute-done.8 = bf16[128,256]{1,0:T(8,128)(2,1)S(1)} collective-permute-done((bf16[128,256]{1,0:T(8,128)(2,1)S(1)}, bf16[128,256]{1,0:T(8,128)(2,1)S(1)}, u32[]{:S(2)}, u32[]{:S(2)}) %collective-permute-start.8) | collective-permute-done | bytes 65568 | tf_op jit(solution)/shard_map/ppermute | solution.py:730
  28.4 0.0 collective-permute-start.11
  28.4 0.5 %collective-permute-start.9 = (bf16[512,128]{1,0:T(8,128)(2,1)S(1)}, bf16[512,128]{1,0:T(8,128)(2,1)S(1)}, u32[]{:S(2)}, u32[]{:S(2)}) collective-permute-start(bf16[512,128]{1,0:T(8,128)(2,1)S(1)} %get-tuple-element.66.opm_ref), channel_id=1, source_target_pairs={{0,8},{8,0},{1,9},{9,1},{2,10},{10,2},{3,11},{11,3},{4,12},{12,4},... | collective-permute-start | bytes 393224 | tf_op jit(solution)/shard_map/ppermute | solution.py:719
  28.9 0.9 %weight_gradients.1.mine_ref = bf16[2048,128]{1,0:T(8,128)(2,1)S(1)} custom-call(bf16[512,1024]{1,0:T(8,128)(2,1)S(1)} %get-tuple-element.69.outer_ref, bf16[512,128]{1,0:T(8,128)(2,1)S(1)} %get-tuple-element.66.opm_ref, bf16[512,128]{1,0:T(8,128)(2,1)S(1)} %get-tuple-element.70.pn_ref, bf16[512,512]{1,0:T(8,128)(2,1)S(1)} %get-tuple-element.71.gh_ref, ...), custom_call_target="tpu_custom_call" | custom-call | tf_op jit(solution)/shard_map/weight_gradients/pallas_call | solution.py:879
  29.8 0.0 collective-permute-done.10.other_normed_ref
  29.9 0.0 collective-permute-done.11.other_far_normed_ref
  29.9 0.1 collective-permute-done.9.other_opm_ref
  29.9 2.0 %projector_parts.1 = (bf16[64,256]{1,0:T(8,128)(2,1)S(1)}, bf16[256,256]{1,0:T(8,128)(2,1)S(1)}) custom-call(s32[2]{0:T(128)S(1)} %pad_add_fusion.ids_ref, bf16[512,128]{1,0:T(8,128)(2,1)S(1)} %get-tuple-element.66.opm_ref, bf16[512,128]{1,0:T(8,128)(2,1)S(1)} %collective-permute-done.9.other_opm_ref, bf16[1024,128]{1,0:T(8,128)(2,1)S(1)} %get-tuple-element.75.rightt_ref, ...), custom_call_target="tpu_custom_call" | custom-call | tf_op jit(solution)/shard_map/projector_parts/pallas_call | solution.py:891
  32.0 0.4 collective-permute-start.15
  32.4 2.3 %collective-permute-start.12 = (bf16[64,256]{1,0:T(8,128)(2,1)S(1)}, bf16[64,256]{1,0:T(8,128)(2,1)S(1)}, u32[]{:S(2)}, u32[]{:S(2)}) collective-permute-start(bf16[64,256]{1,0:T(8,128)(2,1)S(1)} %get-tuple-element.82), channel_id=1, source_target_pairs={{0,6},{1,7},{2,4},{3,5},{4,2},{5,3},{6,0},{7,1},{8,12},{9,13},{10,... | collective-permute-start | bytes 98312 | tf_op jit(solution)/shard_map/ppermute | solution.py:715
  34.7 0.7 %collective-permute-start.13 = (bf16[64,256]{1,0:T(8,128)(2,1)S(1)}, bf16[64,256]{1,0:T(8,128)(2,1)S(1)}, u32[]{:S(2)}, u32[]{:S(2)}) collective-permute-start(bf16[64,256]{1,0:T(8,128)(2,1)S(1)} %get-tuple-element.82), channel_id=1, source_target_pairs={{8,10},{9,11},{10,8},{11,9},{12,14},{13,15},{14,12},{15,13},{24,26... | collective-permute-start | bytes 98312 | tf_op jit(solution)/shard_map/ppermute | solution.py:715
  35.4 0.3 features.1
  35.7 0.7 %reshape.44 = bf16[64,4,256]{2,1,0:T(4,128)(2,1)} reshape(bf16[256,256]{1,0:T(8,128)(2,1)S(1)} %features.1) | data formatting | bytes 262144 | tf_op jit(solution)/shard_map/reshape | solution.py:947
  36.4 1.7 %collective-permute-done.12 = bf16[64,256]{1,0:T(8,128)(2,1)S(1)} collective-permute-done((bf16[64,256]{1,0:T(8,128)(2,1)S(1)}, bf16[64,256]{1,0:T(8,128)(2,1)S(1)}, u32[]{:S(2)}, u32[]{:S(2)}) %collective-permute-start.12) | collective-permute-done | bytes 32800 | tf_op jit(solution)/shard_map/ppermute | solution.py:715
  38.1 0.0 collective-permute-done.13
  38.1 0.2 collective-permute-start.14
  38.3 0.0 collective-permute-done.15.other_ref
  38.4 1.0 %sums_over_depth.1 = (f32[1024,128]{1,0:T(8,128)}, f32[128,512]{1,0:T(8,128)}, f32[512,128]{1,0:T(8,128)}) custom-call(bf16[2048,128]{1,0:T(8,128)(2,1)S(1)} %weight_gradients.1.mine_ref, bf16[2048,128]{1,0:T(8,128)(2,1)S(1)} %collective-permute-done.15.other_ref), custom_call_target="tpu_custom_call" | custom-call | tf_op jit(solution)/shard_map/sums_over_depth/pallas_call | solution.py:933
  39.4 0.0 collective-permute-done.14
  39.4 0.6 %slice_bitcast_fusion = (f32[256,32]{0,1:T(8,128)}, f32[256,32]{0,1:T(8,128)}) fusion(f32[64,256]{1,0:T(8,128)S(1)} %convert_add_fusion), kind=kLoop, calls=%fused_computation.3 | loop fusion | bytes 131072 | tf_op jit(solution)/shard_map/transpose | solution.py:958
  (9 shorter events, 0.1 us)
Async XLA Ops:
  2.6 7.8 %collective-permute-start = (bf16[1,272,128]{2,1,0:T(8,128)(2,1)S(1)}, bf16[1,272,128]{2,1,0:T(8,128)(2,1)S(1)}, u32[]{:S(2)}, u32[]{:S(2)}) collective-permute-start(bf16[1,272,128]{2,1,0:T(8,128)(2,1)S(1)} %get-tuple-element.54), channel_id=1, source_target_pairs={{0,6},{1,7},{2,4},{3,5},{4,2},{5,3},{6,0},{7,1},{8,14},{9,15},{10,... | collective-permute-start | bytes 208904 | tf_op jit(solution)/shard_map/ppermute | solution.py:730
  7.7 5.9 %collective-permute-start.1 = (bf16[1,272,128]{2,1,0:T(8,128)(2,1)S(1)}, bf16[1,272,128]{2,1,0:T(8,128)(2,1)S(1)}, u32[]{:S(2)}, u32[]{:S(2)}) collective-permute-start(bf16[1,272,128]{2,1,0:T(8,128)(2,1)S(1)} %get-tuple-element.54), channel_id=1, source_target_pairs={{0,4},{1,5},{2,6},{3,7},{4,0},{5,1},{6,2},{7,3},{8,12},{9,13},{10,... | collective-permute-start | bytes 208904 | tf_op jit(solution)/shard_map/ppermute | solution.py:730
  7.8 5.9 %collective-permute-start.2 = (bf16[1,272,128]{2,1,0:T(8,128)(2,1)S(1)}, bf16[1,272,128]{2,1,0:T(8,128)(2,1)S(1)}, u32[]{:S(2)}, u32[]{:S(2)}) collective-permute-start(bf16[1,272,128]{2,1,0:T(8,128)(2,1)S(1)} %get-tuple-element.54), channel_id=1, source_target_pairs={{0,2},{1,3},{2,0},{3,1},{4,6},{5,7},{6,4},{7,5},{8,10},{9,11},{10,... | collective-permute-start | bytes 208904 | tf_op jit(solution)/shard_map/ppermute | solution.py:730
  8.4 5.3 %collective-permute-start.3 = (bf16[128,256]{1,0:T(8,128)(2,1)S(1)}, bf16[128,256]{1,0:T(8,128)(2,1)S(1)}, u32[]{:S(2)}, u32[]{:S(2)}) collective-permute-start(bf16[128,256]{1,0:T(8,128)(2,1)S(1)} %get-tuple-element.102), channel_id=1, source_target_pairs={{0,1},{1,0},{2,3},{3,2},{4,5},{5,4},{6,7},{7,6},{8,9},{9,8},{10,11... | collective-permute-start | bytes 196616 | tf_op jit(solution)/shard_map/ppermute | solution.py:730
  13.7 7.5 %copy-start = (bf16[1024,128]{1,0:T(8,128)(2,1)S(1)}, bf16[1024,128]{1,0:T(8,128)(2,1)}, u32[]{:S(2)}) copy-start(bf16[1024,128]{1,0:T(8,128)(2,1)} %wout_ref.1) | copy-start | bytes 786436
  13.7 5.4 %collective-permute-start.5 = (bf16[4,144,128]{2,1,0:T(8,128)(2,1)S(1)}, bf16[4,144,128]{2,1,0:T(8,128)(2,1)S(1)}, u32[]{:S(2)}, u32[]{:S(2)}) collective-permute-start(bf16[4,144,128]{2,1,0:T(8,128)(2,1)S(1)} %slice.21.near_ref), channel_id=1, source_target_pairs={{0,1},{1,0},{2,3},{3,2},{4,5},{5,4},{6,7},{7,6},{8,9},{9,8},{10,11... | collective-permute-start | bytes 442376 | tf_op jit(solution)/shard_map/ppermute | solution.py:730
  15.3 6.0 %collective-permute-start.6 = (bf16[4,144,128]{2,1,0:T(8,128)(2,1)S(1)}, bf16[4,144,128]{2,1,0:T(8,128)(2,1)S(1)}, u32[]{:S(2)}, u32[]{:S(2)}) collective-permute-start(bf16[4,144,128]{2,1,0:T(8,128)(2,1)S(1)} %slice.21.near_ref), channel_id=1, source_target_pairs={{0,8},{8,0},{1,9},{9,1},{2,10},{10,2},{3,11},{11,3},{4,12},{12,4},... | collective-permute-start | bytes 442376 | tf_op jit(solution)/shard_map/ppermute | solution.py:719
  19.2 2.2 %collective-permute-start.7 = (bf16[4,144,128]{2,1,0:T(8,128)(2,1)S(1)}, bf16[4,144,128]{2,1,0:T(8,128)(2,1)S(1)}, u32[]{:S(2)}, u32[]{:S(2)}) collective-permute-start(bf16[4,144,128]{2,1,0:T(8,128)(2,1)S(1)} %collective-permute-done.5.far_ref), channel_id=1, source_target_pairs={{0,8},{8,0},{1,9},{9,1},{2,10},{10,2},{3,11},{11,3},{4,12},{12,4},... | collective-permute-start | bytes 442376 | tf_op jit(solution)/shard_map/ppermute | solution.py:719
  19.2 6.0 %collective-permute-start.4 = (bf16[4,128,128]{2,1,0:T(8,128)(2,1)S(1)}, bf16[4,128,128]{2,1,0:T(8,128)(2,1)S(1)}, u32[]{:S(2)}, u32[]{:S(2)}) collective-permute-start(bf16[4,128,128]{2,1,0:T(8,128)(2,1)S(1)} %slice.19.near_ref), channel_id=1, source_target_pairs={{0,1},{1,0},{2,3},{3,2},{4,5},{5,4},{6,7},{7,6},{8,9},{9,8},{10,11... | collective-permute-start | bytes 393224 | tf_op jit(solution)/shard_map/ppermute | solution.py:730
  21.0 8.9 %collective-permute-start.10 = (bf16[256,256]{1,0:T(8,128)(2,1)S(1)}, bf16[256,256]{1,0:T(8,128)(2,1)S(1)}, u32[]{:S(2)}, u32[]{:S(2)}) collective-permute-start(bf16[256,256]{1,0:T(8,128)(2,1)S(1)} %get-tuple-element.55.normed_ref), channel_id=1, source_target_pairs={{0,8},{8,0},{1,9},{9,1},{2,10},{10,2},{3,11},{11,3},{4,12},{12,4},... | collective-permute-start | bytes 393224 | tf_op jit(solution)/shard_map/ppermute | solution.py:719
  21.3 3.8 %copy-start.2 = (bf16[512,128]{1,0:T(8,128)(2,1)S(1)}, bf16[512,128]{1,0:T(8,128)(2,1)}, u32[]{:S(2)}) copy-start(bf16[512,128]{1,0:T(8,128)(2,1)} %back_ref.1) | copy-start | bytes 393220
  24.0 1.1 %copy-start.1 = (bf16[128,512]{1,0:T(8,128)(2,1)S(1)}, bf16[128,512]{1,0:T(8,128)(2,1)}, u32[]{:S(2)}) copy-start(bf16[128,512]{1,0:T(8,128)(2,1)} %hid_ref.1) | copy-start | bytes 393220
  24.0 4.3 %collective-permute-start.8 = (bf16[128,256]{1,0:T(8,128)(2,1)S(1)}, bf16[128,256]{1,0:T(8,128)(2,1)S(1)}, u32[]{:S(2)}, u32[]{:S(2)}) collective-permute-start(bf16[128,256]{1,0:T(8,128)(2,1)S(1)} %get-tuple-element.65), channel_id=1, source_target_pairs={{0,1},{1,0},{2,3},{3,2},{4,5},{5,4},{6,7},{7,6},{8,9},{9,8},{10,11... | collective-permute-start | bytes 196616 | tf_op jit(solution)/shard_map/ppermute | solution.py:730
  28.4 1.5 %collective-permute-start.11 = (bf16[256,256]{1,0:T(8,128)(2,1)S(1)}, bf16[256,256]{1,0:T(8,128)(2,1)S(1)}, u32[]{:S(2)}, u32[]{:S(2)}) collective-permute-start(bf16[256,256]{1,0:T(8,128)(2,1)S(1)} %constant_dynamic-update-slice_fusion.far_normed_ref), channel_id=1, source_target_pairs={{0,8},{8,0},{1,9},{9,1},{2,10},{10,2},{3,11},{11,3},{4,12},{12,4},... | collective-permute-start | bytes 393224 | tf_op jit(solution)/shard_map/ppermute | solution.py:719
  28.4 1.5 %collective-permute-start.9 = (bf16[512,128]{1,0:T(8,128)(2,1)S(1)}, bf16[512,128]{1,0:T(8,128)(2,1)S(1)}, u32[]{:S(2)}, u32[]{:S(2)}) collective-permute-start(bf16[512,128]{1,0:T(8,128)(2,1)S(1)} %get-tuple-element.66.opm_ref), channel_id=1, source_target_pairs={{0,8},{8,0},{1,9},{9,1},{2,10},{10,2},{3,11},{11,3},{4,12},{12,4},... | collective-permute-start | bytes 393224 | tf_op jit(solution)/shard_map/ppermute | solution.py:719
  32.0 6.4 %collective-permute-start.15 = (bf16[2048,128]{1,0:T(8,128)(2,1)S(1)}, bf16[2048,128]{1,0:T(8,128)(2,1)S(1)}, u32[]{:S(2)}, u32[]{:S(2)}) collective-permute-start(bf16[2048,128]{1,0:T(8,128)(2,1)S(1)} %weight_gradients.1.mine_ref), channel_id=1, source_target_pairs={{0,8},{8,0},{1,9},{9,1},{2,10},{10,2},{3,11},{11,3},{4,12},{12,4},... | collective-permute-start | bytes 1572872 | tf_op jit(solution)/shard_map/ppermute | solution.py:719
  32.4 5.7 %collective-permute-start.12 = (bf16[64,256]{1,0:T(8,128)(2,1)S(1)}, bf16[64,256]{1,0:T(8,128)(2,1)S(1)}, u32[]{:S(2)}, u32[]{:S(2)}) collective-permute-start(bf16[64,256]{1,0:T(8,128)(2,1)S(1)} %get-tuple-element.82), channel_id=1, source_target_pairs={{0,6},{1,7},{2,4},{3,5},{4,2},{5,3},{6,0},{7,1},{8,12},{9,13},{10,... | collective-permute-start | bytes 98312 | tf_op jit(solution)/shard_map/ppermute | solution.py:715
  34.7 3.4 %collective-permute-start.13 = (bf16[64,256]{1,0:T(8,128)(2,1)S(1)}, bf16[64,256]{1,0:T(8,128)(2,1)S(1)}, u32[]{:S(2)}, u32[]{:S(2)}) collective-permute-start(bf16[64,256]{1,0:T(8,128)(2,1)S(1)} %get-tuple-element.82), channel_id=1, source_target_pairs={{8,10},{9,11},{10,8},{11,9},{12,14},{13,15},{14,12},{15,13},{24,26... | collective-permute-start | bytes 98312 | tf_op jit(solution)/shard_map/ppermute | solution.py:715
  38.1 1.3 %collective-permute-start.14 = (bf16[64,256]{1,0:T(8,128)(2,1)S(1)}, bf16[64,256]{1,0:T(8,128)(2,1)S(1)}, u32[]{:S(2)}, u32[]{:S(2)}) collective-permute-start(bf16[64,256]{1,0:T(8,128)(2,1)S(1)} %add_convert_fusion), channel_id=1, source_target_pairs={{0,8},{8,0},{1,9},{9,1},{2,10},{10,2},{3,11},{11,3},{4,12},{12,4},... | collective-permute-start | bytes 98312 | tf_op jit(solution)/shard_map/ppermute | solution.py:719

commit v14 on v13

--- a/solution.py
+++ b/solution.py
@@ -411,6 +411,8 @@
         other = by_owner(ids_ref, z, other_near_ref, other_far_ref)
         for y in range(2):
             lanes_k = slice((2 * z + y) * lanes, (2 * z + y + 1) * lanes)
+            place = y * line + z
+            lanes_p = slice(place * lanes, (place + 1) * lanes)
             both = jnp.concatenate(
                 [
                     jnp.where(lower, mine[y], other[y]),
@@ -423,8 +425,8 @@
             right = jnp.concatenate(
                 [both[seqs : 2 * seqs], both[rows + seqs : rows + 2 * seqs]], axis=0
             )
-            leftn_ref[:, lanes_k] = left
-            turnl_ref[lanes_k, :] = left.astype(f32).T
+            leftn_ref[:, lanes_p] = left
+            turnl_ref[lanes_p, :] = left.astype(f32).T
             turnr_ref[lanes_k, :] = right.astype(f32).T
             tiles = [
                 both[first + 2 * seqs : first + 2 * seqs + MASK_ROWS].astype(f32)
@@ -437,7 +439,7 @@
             pair_lane = lax.broadcasted_iota(jnp.int32, (pair_cols, lanes), 1)
             pair_row = lax.broadcasted_iota(jnp.int32, (pair_cols, lanes), 0)
             for r in range(res):
-                first = ((2 * z + y) * res + r) * pair_cols
+                first = (place * res + r) * pair_cols
                 pml_ref[first : first + pair_cols, :] = jnp.where(
                     pair_lane == pair_row, own[res + r : res + r + 1, :], 0.0
                 ).astype(bf16)
@@ -454,9 +456,9 @@
     maskt = maskt_ref[...]
     cols_mask = maskt_ref[pl.ds(pl.multiple_of(me_depth * pair_cols, pair_cols), pair_cols), :]
     for i in range(residues):
-        cntl_ref[i * pair_cols : (i + 1) * pair_cols, :] = (maskt[i : i + 1, :] * cols_mask).astype(
-            bf16
-        )
+        z, y, r = i // (2 * res), i // res % 2, i % res
+        first = ((y * line + z) * res + r) * pair_cols
+        cntl_ref[first : first + pair_cols, :] = (maskt[i : i + 1, :] * cols_mask).astype(bf16)
     ones = jnp.ones((lanes, lanes), bf16)
     cnt_ref[...] = jnp.dot(cntl_ref[...], ones, preferred_element_type=f32)
     pm_ref[...] = jnp.dot(pml_ref[...], ones, preferred_element_type=f32).astype(bf16)
@@ -482,46 +484,51 @@
 
 def transition_kernel(
     sizes,
+    near,
     ids_ref,
-    near_ref,
-    far_ref,
+    blocks_ref,
     proj_out_ref,
     cnt_ref,
     pm_ref,
     gain_ref,
     hid_ref,
     back_ref,
-    couple_ref,
     opm_ref,
     pn_ref,
     gh_ref,
     hidden_ref,
     mg_ref,
-    gmid_ref,
+    *couple,
 ):
-    seqs, res, pair_cols, width = sizes
+    _, res, pair_cols, _ = sizes
     per = res * pair_cols
-    cols = 2 * near_ref.shape[0]
-    me_col = ids_ref[1]
+    line = blocks_ref.shape[0]
+    me_z, me_y = ids_ref[1] // 2, ids_ref[1] % 2
     f32, bf16 = jnp.float32, jnp.bfloat16
     gain = gain_ref[...]
     chunk = 2 * per
-    for at in range(cols // 2):
+    half = line * per
+    first_row = (me_y if near else 1 - me_y) * half
+    for at in range(line // 2):
         rows = slice(at * chunk, (at + 1) * chunk)
-        blocks = by_owner(ids_ref, at, near_ref, far_ref)
+        there = pl.ds(pl.multiple_of(first_row + at * chunk, chunk), chunk)
+        blocks = [
+            blocks_ref[(line - (z ^ me_z)) % line]
+            for z in (2 * at, 2 * at + 1)
+        ]
         act, grad = [
             jnp.concatenate([block[w * per : (w + 1) * per] for block in blocks], axis=0)
             for w in range(2)
         ]
-        count = cnt_ref[rows, :]
-        mid = act.astype(f32) + proj_out_ref[rows, :] / count
+        count = cnt_ref[there, :]
+        mid = act.astype(f32) + proj_out_ref[there, :] / count
         scaled, inv = norm_pieces(mid)
         normed = (scaled * gain).astype(bf16)
         pn_ref[rows, :] = normed
         pre = jnp.dot(normed, hid_ref[...], preferred_element_type=f32)
         value, slope = silu_pieces(pre)
         hidden_ref[rows, :] = value.astype(bf16)
-        masked = grad * pm_ref[rows, :]
+        masked = grad * pm_ref[there, :]
         mg_ref[rows, :] = masked
         back = lax.dot_general(
             masked, back_ref[...], (((1,), (1,)), ((), ())), preferred_element_type=f32
@@ -535,9 +542,11 @@
             * gain
         )
         gmid = grad.astype(f32) + standardize_adjoint(gsc, scaled, inv)
-        gmid_ref[rows, :] = gmid
         opm_ref[rows, :] = (gmid / count).astype(bf16)
-    couple_ref[...] = gmid_ref[pl.ds(pl.multiple_of(me_col * per, per), per), :].astype(bf16)
+        if near:
+            couple[1][rows, :] = gmid.astype(bf16)
+    if near:
+        couple[0][...] = couple[1][pl.ds(pl.multiple_of(me_z * per, per), per), :]
 
 
 def projector_kernel(
@@ -572,10 +581,16 @@
     me_depth = ids_ref[0]
     me_col = ids_ref[1]
     me_y = me_col % 2
-    first_here = (me_col // 2) * here
+    me_z = me_col // 2
+    first_here = me_z * here
     f32, bf16 = jnp.float32, jnp.bfloat16
     my_half = first_here // pair_cols
-    gf_ref[...] = jnp.where(my_half == me_depth, opm_ref[...], other_opm_ref[...]).astype(f32)
+    mine = jnp.where(my_half == me_depth, opm_ref[...], other_opm_ref[...]).astype(f32)
+    quarter = half // 2
+    for w, y in enumerate((me_y, 1 - me_y)):
+        gf_ref[pl.ds(pl.multiple_of(y * quarter, quarter), quarter), :] = mine[
+            w * quarter : (w + 1) * quarter
+        ]
     for y, e, block in (
         (me_y, me_depth, normed_ref),
         (1 - me_y, me_depth, far_normed_ref),
@@ -584,11 +599,12 @@
     ):
         rows_ref[y, e] = block[...]
 
-    for il in range(here):
-        first = pl.multiple_of((first_here + il) * pair_cols, pair_cols)
-        for e, block in ((me_depth, opm_ref), (1 - me_depth, other_opm_ref)):
-            to = pl.multiple_of(il * residues + e * pair_cols, pair_cols)
-            grow_ref[pl.ds(to, pair_cols), :] = block[pl.ds(first, pair_cols), :]
+    for w, y in enumerate((me_y, 1 - me_y)):
+        for r in range(res):
+            first = pl.multiple_of(w * quarter + (me_z * res + r) * pair_cols, pair_cols)
+            for e, block in ((me_depth, opm_ref), (1 - me_depth, other_opm_ref)):
+                to = pl.multiple_of((y * res + r) * residues + e * pair_cols, pair_cols)
+                grow_ref[pl.ds(to, pair_cols), :] = block[pl.ds(first, pair_cols), :]
     my_first = first_here - my_half * pair_cols
     for jl in range(here):
         gcol_ref[jl * residues : (jl + 1) * residues, :] = gf_ref[
@@ -653,26 +669,36 @@
         part_ref[at * width : (at + 1) * width, :] = total.astype(bf16)
 
 
-def weights_kernel(outer_ref, opm_ref, pn_ref, gh_ref, hidden_ref, mg_ref, out_ref, turn_ref):
-    pair_width, hid = pn_ref.shape[1], gh_ref.shape[1]
+def weights_kernel(ids_ref, outer_ref, *refs):
+    near, far, (out_ref, turn_ref) = refs[0:5], refs[5:10], refs[10:]
+    half, pair_width = near[1].shape
+    hid = near[2].shape[1]
     outer_width = outer_ref.shape[1]
     width = int(outer_width**0.5 + 0.5)
+    me_y = ids_ref[1] % 2
 
     def contract(lhs, rhs):
         return lax.dot_general(
-            lhs[...], rhs[...], (((0,), (0,)), ((), ())), preferred_element_type=jnp.float32
-        )
-
-    turn_ref[...] = contract(outer_ref, opm_ref)
+            lhs, rhs, (((0,), (0,)), ((), ())), preferred_element_type=jnp.float32
+        )
+
+    turn_ref[...] = sum(
+        contract(outer_ref[pl.ds(pl.multiple_of(y * half, half), half), :], refs_y[0][...])
+        for y, refs_y in ((me_y, near), (1 - me_y, far))
+    )
     for c in range(width):
         out_ref[c * width : (c + 1) * width, :] = turn_ref[
             pl.ds(c, width, stride=width), :
         ].astype(jnp.bfloat16)
-    dhid = contract(pn_ref, gh_ref).astype(jnp.bfloat16)
+    dhid = sum(contract(refs_y[1][...], refs_y[2][...]) for refs_y in (near, far))
     for at in range(hid // pair_width):
         first = outer_width + at * pair_width
-        out_ref[first : first + pair_width, :] = dhid[:, at * pair_width : (at + 1) * pair_width]
-    out_ref[outer_width + hid :, :] = contract(hidden_ref, mg_ref).astype(jnp.bfloat16)
+        out_ref[first : first + pair_width, :] = dhid[
+            :, at * pair_width : (at + 1) * pair_width
+        ].astype(jnp.bfloat16)
+    out_ref[outer_width + hid :, :] = sum(
+        contract(refs_y[3][...], refs_y[4][...]) for refs_y in (near, far)
+    ).astype(jnp.bfloat16)
 
 
 def weights_sum_kernel(mine_ref, other_ref, dout_ref, dhid_ref, dback_ref):
@@ -756,6 +782,7 @@
     lanes = res * width
     rows = 2 * seqs + MASK_ROWS
     half = residues * pair_cols
+    line = cols // 2
     f32, bf16 = jnp.float32, jnp.bfloat16
     ids = jnp.stack([lax.axis_index("depth"), lax.axis_index("col")]).astype(jnp.int32)
     smem = pl.BlockSpec(memory_space=pltpu.SMEM)
@@ -811,9 +838,8 @@
     blocks = lax.optimization_barrier(
         jnp.concatenate([sent] + [swap_col(sent, partner) for partner in Z_PARTNERS])
     )
-    half_normed = seqs * res // 2
-    far_normed_a = swap_col(normed[:half_normed], Y_PARTNER)
-    blocks, far_normed_a = lax.optimization_barrier((blocks, far_normed_a))
+    far_normed = swap_col(normed, Y_PARTNER)
+    blocks, far_normed = lax.optimization_barrier((blocks, far_normed))
     near, pair_near = blocks[:, :rows], blocks[:, rows:]
     far = swap_col(near, Y_PARTNER)
     pair_far = swap_col(pair_near, Y_PARTNER)
@@ -843,48 +869,39 @@
         compiler_params=params,
         name="outer_products",
     )(ids, near, far, other_near, other_far, wturn)
-    normed_b, proj_out = lax.optimization_barrier((normed[half_normed:], proj_out))
-    far_normed_b = swap_col(normed_b, Y_PARTNER)
-    pair_far, proj_out = lax.optimization_barrier((pair_far, proj_out))
-    couple, opm, pn, gh, hidden, mg = pl.pallas_call(
-        functools.partial(transition_kernel, sizes),
-        out_shape=(
-            shape((per, pair_width), bf16),
-            shape((half, pair_width), bf16),
-            shape((half, pair_width), bf16),
-            shape((half, hid), bf16),
-            shape((half, hid), bf16),
-            shape((half, pair_width), bf16),
-        ),
-        in_specs=[smem] + [vmem] * 8,
-        out_specs=[vmem] * 6,
-        scratch_shapes=[
-            pltpu.VMEM((half, pair_width), f32),
-        ],
-        compiler_params=params,
-        name="transition",
-    )(
-        ids,
-        pair_near,
-        pair_far,
-        proj_out,
-        cnt,
-        pm,
-        gain,
-        hidden_weight,
-        back_weight,
-    )
-    opm, far_normed_b = lax.optimization_barrier((opm, far_normed_b))
-    far_normed = jnp.concatenate([far_normed_a, far_normed_b])
+
+    def transition(near, blocks):
+        rows_out = line * per
+        return pl.pallas_call(
+            functools.partial(transition_kernel, sizes, near),
+            out_shape=(
+                shape((rows_out, pair_width), bf16),
+                shape((rows_out, pair_width), bf16),
+                shape((rows_out, hid), bf16),
+                shape((rows_out, hid), bf16),
+                shape((rows_out, pair_width), bf16),
+            )
+            + ((shape((per, pair_width), bf16),) if near else ()),
+            in_specs=[smem] + [vmem] * 7,
+            out_specs=[vmem] * (6 if near else 5),
+            scratch_shapes=[pltpu.VMEM((rows_out, pair_width), bf16)] if near else [],
+            compiler_params=params,
+            name="transition",
+        )(ids, blocks, proj_out, cnt, pm, gain, hidden_weight, back_weight)
+
+    *near_arrays, couple = transition(True, pair_near)
+    pair_far, near_arrays = lax.optimization_barrier((pair_far, near_arrays))
+    far_arrays = transition(False, pair_far)
+    opm = jnp.concatenate([near_arrays[0], far_arrays[0]])
     weights = pl.pallas_call(
         weights_kernel,
         out_shape=shape((outer_width + 2 * hid, pair_width), bf16),
-        in_specs=[vmem] * 6,
+        in_specs=[smem] + [vmem] * 11,
         out_specs=vmem,
         scratch_shapes=[pltpu.VMEM((outer_width, pair_width), f32)],
         compiler_params=params,
         name="weight_gradients",
-    )(outer, opm, pn, gh, hidden, mg)
+    )(ids, outer, *near_arrays, *far_arrays)
     other_opm, other_normed, other_far_normed, weights = lax.optimization_barrier(
         (swap_depth(opm), swap_depth(normed), swap_depth(far_normed), weights)
     )

time: 40.3 us -> 40.5 us (level)
  Pallas kernels: 11.3 us -> 12.9 us
  waiting for transfers between devices: 10.1 us -> 8.52 us
    ppermute x7 -> x6, starting transfers between devices: 11.9 us -> 10.8 us  [swap_col(): lax.ppermute(block, 'col', [(at, at ^ partner) for at in range(count)])]
    pallas_call x1 -> x2, Pallas kernels: 2.42 us -> 3.36 us  [transition(): pl.pallas_call(functools.partial(transition_kernel, sizes, near), out_sha...]
    ppermute x7 -> x6, waiting for transfers between devices: 8.28 us -> 7.43 us  [swap_col(): lax.ppermute(block, 'col', [(at, at ^ partner) for at in range(count)])]
    ppermute x2, waiting for transfers between devices: 1.73 us -> 1.08 us  [swap_line(): return lax.ppermute(block, ('depth', 'col'), pairs)]
    ppermute x2, starting transfers between devices: 2.98 us -> 3.62 us  [swap_line(): return lax.ppermute(block, ('depth', 'col'), pairs)]
    ppermute x7, starting transfers between devices: 1.34 us -> 1.94 us  [swap_depth(): return lax.ppermute(block, 'depth', [(0, 1), (1, 0)])]
    pallas_call x1, Pallas kernels: 0.92 us -> 1.47 us  [whole_plan(): pl.pallas_call(weights_kernel, out_shape=shape((outer_width + 2 * hid, pa...]
  transfers between devices with their start and end apart: 16 -> 15, of which waited for: 7 -> 4; matrix products, arithmetic and copies ran while one was open for 2% -> 2% of each run, Pallas kernels for 18% -> 22%
where the time goes in v14:
time: 40.5 us; the launch traced here: 40.3 us
  starting transfers between devices  16.4 us (40%)
  Pallas kernels  12.9 us (32%)
  waiting for transfers between devices  8.52 us (21%)
  local copies, waits for them, and re-layouts  1.49 us (4%)
  between operations  0.82 us (2%)
    ppermute x6, starting transfers between devices, swap_col(): lax.ppermute(block, 'col', [(at, at ^ partner) for at in range(count)])  10.8 us
    ppermute x6, waiting for transfers between devices, swap_col(): lax.ppermute(block, 'col', [(at, at ^ partner) for at in range(count)])  7.43 us
    ppermute x2, starting transfers between devices, swap_line(): return lax.ppermute(block, ('depth', 'col'), pairs)  3.62 us
    pallas_call x2, Pallas kernels, transition(): pl.pallas_call(functools.partial(transition_kernel, sizes, near), out_sha...  3.36 us
    pallas_call x1, Pallas kernels, whole_plan(): pl.pallas_call(functools.partial(outer_kernel, sizes), out_shape=(shape((...  2.82 us
    pallas_call x1, Pallas kernels, whole_plan(): pl.pallas_call(functools.partial(projector_kernel, sizes), out_shape=(sha...  2.06 us
    ppermute x7, starting transfers between devices, swap_depth(): return lax.ppermute(block, 'depth', [(0, 1), (1, 0)])  1.94 us
    pallas_call x1, Pallas kernels, whole_plan(): pl.pallas_call(pre_kernel, out_shape=(shape((1, rows + 2 * per, pair_widt...  1.91 us
  transfers between devices with their start and end apart: 15, of which 4 were waited for; matrix products, arithmetic and copies ran while one was open for 2% of the time, Pallas kernels for 22%

profile of v14, /device:TPU:0, one launch (start us, length us, event | category | flops | bytes accessed | tf_op | source)
XLA Modules:
  0.0 40.3 jit_solution(14852885826099947471)
XLA Ops:
  0.6 0.1 pad_add_fusion.ids_ref
  0.7 1.9 %project.1 = (bf16[1,272,128]{2,1,0:T(8,128)(2,1)S(1)}, f32[1,256]{1,0:T(1,128)S(1)}, bf16[32,256]{1,0:T(8,128)(2,1)S(1)}, bf16[32,256]{1,0:T(8,128)(2,1)S(1)}, ...) custom-call(s32[2]{0:T(128)S(1)} %pad_add_fusion.ids_ref, ...), custom_call_target="tpu_custom_call" | custom-call | tf_op jit(solution)/shard_map/project/pallas_call | solution.py:797
  2.6 5.1 %collective-permute-start = (bf16[1,272,128]{2,1,0:T(8,128)(2,1)S(1)}, bf16[1,272,128]{2,1,0:T(8,128)(2,1)S(1)}, u32[]{:S(2)}, u32[]{:S(2)}) collective-permute-start(bf16[1,272,128]{2,1,0:T(8,128)(2,1)S(1)} %get-tuple-element.59), channel_id=1, source_target_pairs={{0,6},{1,7},{2,4},{3,5},{4,2},{5,3},{6,0},{7,1},{8,14},{9,15},{10,... | collective-permute-start | bytes 208904 | tf_op jit(solution)/shard_map/ppermute | solution.py:756
  7.7 0.0 collective-permute-start.1
  7.8 0.6 %collective-permute-start.2 = (bf16[1,272,128]{2,1,0:T(8,128)(2,1)S(1)}, bf16[1,272,128]{2,1,0:T(8,128)(2,1)S(1)}, u32[]{:S(2)}, u32[]{:S(2)}) collective-permute-start(bf16[1,272,128]{2,1,0:T(8,128)(2,1)S(1)} %get-tuple-element.59), channel_id=1, source_target_pairs={{0,2},{1,3},{2,0},{3,1},{4,6},{5,7},{6,4},{7,5},{8,10},{9,11},{10,... | collective-permute-start | bytes 208904 | tf_op jit(solution)/shard_map/ppermute | solution.py:756
  8.4 1.7 %collective-permute-start.3 = (bf16[256,256]{1,0:T(8,128)(2,1)S(1)}, bf16[256,256]{1,0:T(8,128)(2,1)S(1)}, u32[]{:S(2)}, u32[]{:S(2)}) collective-permute-start(bf16[256,256]{1,0:T(8,128)(2,1)S(1)} %get-tuple-element.60.normed_ref), channel_id=1, source_target_pairs={{0,1},{1,0},{2,3},{3,2},{4,5},{5,4},{6,7},{7,6},{8,9},{9,8},{10,11... | collective-permute-start | bytes 393224 | tf_op jit(solution)/shard_map/ppermute | solution.py:756
  10.1 0.4 collective-permute-done
  10.4 3.2 %collective-permute-done.1 = bf16[1,272,128]{2,1,0:T(8,128)(2,1)S(1)} collective-permute-done((bf16[1,272,128]{2,1,0:T(8,128)(2,1)S(1)}, bf16[1,272,128]{2,1,0:T(8,128)(2,1)S(1)}, u32[]{:S(2)}, u32[]{:S(2)}) %collective-permute-start.1) | collective-permute-done | bytes 69664 | tf_op jit(solution)/shard_map/ppermute | solution.py:756
  13.7 0.0 collective-permute-done.2
  13.7 0.0 copy-start
  13.7 0.0 collective-permute-done.3.far_normed_ref
  13.7 1.6 %collective-permute-start.5 = (bf16[4,144,128]{2,1,0:T(8,128)(2,1)S(1)}, bf16[4,144,128]{2,1,0:T(8,128)(2,1)S(1)}, u32[]{:S(2)}, u32[]{:S(2)}) collective-permute-start(bf16[4,144,128]{2,1,0:T(8,128)(2,1)S(1)} %slice.13.near_ref), channel_id=1, source_target_pairs={{0,1},{1,0},{2,3},{3,2},{4,5},{5,4},{6,7},{7,6},{8,9},{9,8},{10,11... | collective-permute-start | bytes 442376 | tf_op jit(solution)/shard_map/ppermute | solution.py:756
  15.3 0.0 collective-permute-start.6
  15.3 3.8 %collective-permute-done.5.far_ref = bf16[4,144,128]{2,1,0:T(8,128)(2,1)S(1)} collective-permute-done((bf16[4,144,128]{2,1,0:T(8,128)(2,1)S(1)}, bf16[4,144,128]{2,1,0:T(8,128)(2,1)S(1)}, u32[]{:S(2)}, u32[]{:S(2)}) %collective-permute-start.5) | collective-permute-done | bytes 147488 | tf_op jit(solution)/shard_map/ppermute | solution.py:756
  19.2 0.0 collective-permute-start.7
  19.2 1.8 %collective-permute-start.4 = (bf16[4,128,128]{2,1,0:T(8,128)(2,1)S(1)}, bf16[4,128,128]{2,1,0:T(8,128)(2,1)S(1)}, u32[]{:S(2)}, u32[]{:S(2)}) collective-permute-start(bf16[4,128,128]{2,1,0:T(8,128)(2,1)S(1)} %slice.12.blocks_ref), channel_id=1, source_target_pairs={{0,1},{1,0},{2,3},{3,2},{4,5},{5,4},{6,7},{7,6},{8,9},{9,8},{10,11... | collective-permute-start | bytes 393224 | tf_op jit(solution)/shard_map/ppermute | solution.py:756
  21.0 0.2 collective-permute-start.9
  21.2 0.0 copy-done
  21.2 0.1 copy.19
  21.3 0.3 collective-permute-start.10
  21.7 0.0 collective-permute-done.6.other_near_ref
  21.7 0.0 collective-permute-done.7.other_far_ref
  21.7 0.0 copy-start.1
  21.7 0.0 copy-start.2
  21.7 2.8 %outer_products.1 = (bf16[512,1024]{1,0:T(8,128)(2,1)S(1)}, f32[512,128]{1,0:T(8,128)S(1)}, f32[512,128]{1,0:T(8,128)S(1)}, bf16[512,128]{1,0:T(8,128)(2,1)S(1)}...) custom-call(s32[2]{0:T(128)S(1)} %pad_add_fusion.ids_ref, ...), custom_call_target="tpu_custom_call" | custom-call | tf_op jit(solution)/shard_map/outer_products/pallas_call | solution.py:848
  24.5 0.0 copy-done.1
  24.5 0.0 copy-done.2
  24.5 2.0 %transition.2 = (bf16[256,128]{1,0:T(8,128)(2,1)S(1)}, bf16[256,128]{1,0:T(8,128)(2,1)S(1)}, bf16[256,512]{1,0:T(8,128)(2,1)S(1)}, bf16[256,512]{1,0:T(8,128)(2,...) custom-call(s32[2]{0:T(128)S(1)} %pad_add_fusion.ids_ref, bf16[4,128,128]{2,1,0:T(8,128)(2,1)S(1)} %slice.12.blocks_ref, ...), custom_call_target="tpu_custom_call" | custom-call | tf_op jit(solution)/shard_map/transition/pallas_call | solution.py:875
  26.5 0.0 collective-permute-done.4.blocks_ref
  26.5 1.4 %transition.3 = (bf16[256,128]{1,0:T(8,128)(2,1)S(1)}, bf16[256,128]{1,0:T(8,128)(2,1)S(1)}, bf16[256,512]{1,0:T(8,128)(2,1)S(1)}, bf16[256,512]{1,0:T(8,128)(2,1)S(1)}, bf16[256,128]{1,0:T(8,128)(2,1)S(1)}) custom-call(s32[2]{0:T(128)S(1)} %pad_add_fusion.ids_ref, bf16[4,128,128]{2,1,0:T(8,128)(2,1)S(1)} %collective-permute-done.4.blocks_ref, ...), custom_call_target="tpu_custom_call" | custom-call | tf_op jit(solution)/shard_map/transition/pallas_call | solution.py:875
  27.9 0.3 collective-permute-start.8
  28.2 1.5 %weight_gradients.1.mine_ref = bf16[2048,128]{1,0:T(8,128)(2,1)S(1)} custom-call(s32[2]{0:T(128)S(1)} %pad_add_fusion.ids_ref, bf16[512,1024]{1,0:T(8,128)(2,1)S(1)} %get-tuple-element.75.outer_ref, bf16[256,128]{1,0:T(8,128)(2,1)S(1)} %get-tuple-element.71.refs_0_, bf16[256,128]{1,0:T(8,128)(2,1)S(1)} %get-tuple-element.76.refs_1_, ...), custom_call_target="tpu_custom_call" | custom-call | tf_op jit(solution)/shard_map/weight_gradients/pallas_call | solution.py:896
  29.7 0.0 collective-permute-done.9.other_normed_ref
  29.7 0.0 collective-permute-done.10.other_far_normed_ref
  29.7 0.0 collective-permute-done.8.other_opm_ref
  29.7 2.1 %projector_parts.1 = (bf16[64,256]{1,0:T(8,128)(2,1)S(1)}, bf16[256,256]{1,0:T(8,128)(2,1)S(1)}) custom-call(s32[2]{0:T(128)S(1)} %pad_add_fusion.ids_ref, bf16[512,128]{1,0:T(8,128)(2,1)S(1)} %constant_dynamic-update-slice_fusion.opm_ref, bf16[512,128]{1,0:T(8,128)(2,1)S(1)} %collective-permute-done.8.other_opm_ref, ...), custom_call_target="tpu_custom_call" | custom-call | tf_op jit(solution)/shard_map/projector_parts/pallas_call | solution.py:908
  31.8 0.3 collective-permute-start.14
  32.1 3.0 %collective-permute-start.11 = (bf16[64,256]{1,0:T(8,128)(2,1)S(1)}, bf16[64,256]{1,0:T(8,128)(2,1)S(1)}, u32[]{:S(2)}, u32[]{:S(2)}) collective-permute-start(bf16[64,256]{1,0:T(8,128)(2,1)S(1)} %get-tuple-element.92), channel_id=1, source_target_pairs={{0,6},{1,7},{2,4},{3,5},{4,2},{5,3},{6,0},{7,1},{8,12},{9,13},{10,... | collective-permute-start | bytes 98312 | tf_op jit(solution)/shard_map/ppermute | solution.py:741
  35.1 0.7 %collective-permute-start.12 = (bf16[64,256]{1,0:T(8,128)(2,1)S(1)}, bf16[64,256]{1,0:T(8,128)(2,1)S(1)}, u32[]{:S(2)}, u32[]{:S(2)}) collective-permute-start(bf16[64,256]{1,0:T(8,128)(2,1)S(1)} %get-tuple-element.92), channel_id=1, source_target_pairs={{8,10},{9,11},{10,8},{11,9},{12,14},{13,15},{14,12},{15,13},{24,26... | collective-permute-start | bytes 98312 | tf_op jit(solution)/shard_map/ppermute | solution.py:741
  35.8 0.3 features.1
  36.1 0.7 %reshape.44 = bf16[64,4,256]{2,1,0:T(4,128)(2,1)} reshape(bf16[256,256]{1,0:T(8,128)(2,1)S(1)} %features.1) | data formatting | bytes 262144 | tf_op jit(solution)/shard_map/reshape | solution.py:964
  36.8 1.1 %collective-permute-done.11 = bf16[64,256]{1,0:T(8,128)(2,1)S(1)} collective-permute-done((bf16[64,256]{1,0:T(8,128)(2,1)S(1)}, bf16[64,256]{1,0:T(8,128)(2,1)S(1)}, u32[]{:S(2)}, u32[]{:S(2)}) %collective-permute-start.11) | collective-permute-done | bytes 32800 | tf_op jit(solution)/shard_map/ppermute | solution.py:741
  37.9 0.0 collective-permute-done.12
  37.9 0.7 %collective-permute-start.13 = (bf16[64,256]{1,0:T(8,128)(2,1)S(1)}, bf16[64,256]{1,0:T(8,128)(2,1)S(1)}, u32[]{:S(2)}, u32[]{:S(2)}) collective-permute-start(bf16[64,256]{1,0:T(8,128)(2,1)S(1)} %add_convert_fusion), channel_id=1, source_target_pairs={{0,8},{8,0},{1,9},{9,1},{2,10},{10,2},{3,11},{11,3},{4,12},{12,4},... | collective-permute-start | bytes 98312 | tf_op jit(solution)/shard_map/ppermute | solution.py:745
  38.6 0.0 collective-permute-done.14.other_ref
  38.6 1.0 %sums_over_depth.1 = (f32[1024,128]{1,0:T(8,128)}, f32[128,512]{1,0:T(8,128)}, f32[512,128]{1,0:T(8,128)}) custom-call(bf16[2048,128]{1,0:T(8,128)(2,1)S(1)} %weight_gradients.1.mine_ref, bf16[2048,128]{1,0:T(8,128)(2,1)S(1)} %collective-permute-done.14.other_ref), custom_call_target="tpu_custom_call" | custom-call | tf_op jit(solution)/shard_map/sums_over_depth/pallas_call | solution.py:950
  39.6 0.0 collective-permute-done.13
  39.6 0.6 %slice_bitcast_fusion = (f32[256,32]{0,1:T(8,128)}, f32[256,32]{0,1:T(8,128)}) fusion(f32[64,256]{1,0:T(8,128)S(1)} %convert_add_fusion), kind=kLoop, calls=%fused_computation.3 | loop fusion | bytes 131072 | tf_op jit(solution)/shard_map/transpose | solution.py:975
  (7 shorter events, 0.1 us)
Async XLA Ops:
  2.6 7.8 %collective-permute-start = (bf16[1,272,128]{2,1,0:T(8,128)(2,1)S(1)}, bf16[1,272,128]{2,1,0:T(8,128)(2,1)S(1)}, u32[]{:S(2)}, u32[]{:S(2)}) collective-permute-start(bf16[1,272,128]{2,1,0:T(8,128)(2,1)S(1)} %get-tuple-element.59), channel_id=1, source_target_pairs={{0,6},{1,7},{2,4},{3,5},{4,2},{5,3},{6,0},{7,1},{8,14},{9,15},{10,... | collective-permute-start | bytes 208904 | tf_op jit(solution)/shard_map/ppermute | solution.py:756
  7.7 5.9 %collective-permute-start.1 = (bf16[1,272,128]{2,1,0:T(8,128)(2,1)S(1)}, bf16[1,272,128]{2,1,0:T(8,128)(2,1)S(1)}, u32[]{:S(2)}, u32[]{:S(2)}) collective-permute-start(bf16[1,272,128]{2,1,0:T(8,128)(2,1)S(1)} %get-tuple-element.59), channel_id=1, source_target_pairs={{0,4},{1,5},{2,6},{3,7},{4,0},{5,1},{6,2},{7,3},{8,12},{9,13},{10,... | collective-permute-start | bytes 208904 | tf_op jit(solution)/shard_map/ppermute | solution.py:756
  7.8 5.9 %collective-permute-start.2 = (bf16[1,272,128]{2,1,0:T(8,128)(2,1)S(1)}, bf16[1,272,128]{2,1,0:T(8,128)(2,1)S(1)}, u32[]{:S(2)}, u32[]{:S(2)}) collective-permute-start(bf16[1,272,128]{2,1,0:T(8,128)(2,1)S(1)} %get-tuple-element.59), channel_id=1, source_target_pairs={{0,2},{1,3},{2,0},{3,1},{4,6},{5,7},{6,4},{7,5},{8,10},{9,11},{10,... | collective-permute-start | bytes 208904 | tf_op jit(solution)/shard_map/ppermute | solution.py:756
  8.4 5.3 %collective-permute-start.3 = (bf16[256,256]{1,0:T(8,128)(2,1)S(1)}, bf16[256,256]{1,0:T(8,128)(2,1)S(1)}, u32[]{:S(2)}, u32[]{:S(2)}) collective-permute-start(bf16[256,256]{1,0:T(8,128)(2,1)S(1)} %get-tuple-element.60.normed_ref), channel_id=1, source_target_pairs={{0,1},{1,0},{2,3},{3,2},{4,5},{5,4},{6,7},{7,6},{8,9},{9,8},{10,11... | collective-permute-start | bytes 393224 | tf_op jit(solution)/shard_map/ppermute | solution.py:756
  13.7 7.5 %copy-start = (bf16[1024,128]{1,0:T(8,128)(2,1)S(1)}, bf16[1024,128]{1,0:T(8,128)(2,1)}, u32[]{:S(2)}) copy-start(bf16[1024,128]{1,0:T(8,128)(2,1)} %wout_ref.1) | copy-start | bytes 786436
  13.7 5.4 %collective-permute-start.5 = (bf16[4,144,128]{2,1,0:T(8,128)(2,1)S(1)}, bf16[4,144,128]{2,1,0:T(8,128)(2,1)S(1)}, u32[]{:S(2)}, u32[]{:S(2)}) collective-permute-start(bf16[4,144,128]{2,1,0:T(8,128)(2,1)S(1)} %slice.13.near_ref), channel_id=1, source_target_pairs={{0,1},{1,0},{2,3},{3,2},{4,5},{5,4},{6,7},{7,6},{8,9},{9,8},{10,11... | collective-permute-start | bytes 442376 | tf_op jit(solution)/shard_map/ppermute | solution.py:756
  15.3 6.3 %collective-permute-start.6 = (bf16[4,144,128]{2,1,0:T(8,128)(2,1)S(1)}, bf16[4,144,128]{2,1,0:T(8,128)(2,1)S(1)}, u32[]{:S(2)}, u32[]{:S(2)}) collective-permute-start(bf16[4,144,128]{2,1,0:T(8,128)(2,1)S(1)} %slice.13.near_ref), channel_id=1, source_target_pairs={{0,8},{8,0},{1,9},{9,1},{2,10},{10,2},{3,11},{11,3},{4,12},{12,4},... | collective-permute-start | bytes 442376 | tf_op jit(solution)/shard_map/ppermute | solution.py:745
  19.2 2.5 %collective-permute-start.7 = (bf16[4,144,128]{2,1,0:T(8,128)(2,1)S(1)}, bf16[4,144,128]{2,1,0:T(8,128)(2,1)S(1)}, u32[]{:S(2)}, u32[]{:S(2)}) collective-permute-start(bf16[4,144,128]{2,1,0:T(8,128)(2,1)S(1)} %collective-permute-done.5.far_ref), channel_id=1, source_target_pairs={{0,8},{8,0},{1,9},{9,1},{2,10},{10,2},{3,11},{11,3},{4,12},{12,4},... | collective-permute-start | bytes 442376 | tf_op jit(solution)/shard_map/ppermute | solution.py:745
  19.2 7.3 %collective-permute-start.4 = (bf16[4,128,128]{2,1,0:T(8,128)(2,1)S(1)}, bf16[4,128,128]{2,1,0:T(8,128)(2,1)S(1)}, u32[]{:S(2)}, u32[]{:S(2)}) collective-permute-start(bf16[4,128,128]{2,1,0:T(8,128)(2,1)S(1)} %slice.12.blocks_ref), channel_id=1, source_target_pairs={{0,1},{1,0},{2,3},{3,2},{4,5},{5,4},{6,7},{7,6},{8,9},{9,8},{10,11... | collective-permute-start | bytes 393224 | tf_op jit(solution)/shard_map/ppermute | solution.py:756
  21.0 8.7 %collective-permute-start.9 = (bf16[256,256]{1,0:T(8,128)(2,1)S(1)}, bf16[256,256]{1,0:T(8,128)(2,1)S(1)}, u32[]{:S(2)}, u32[]{:S(2)}) collective-permute-start(bf16[256,256]{1,0:T(8,128)(2,1)S(1)} %get-tuple-element.60.normed_ref), channel_id=1, source_target_pairs={{0,8},{8,0},{1,9},{9,1},{2,10},{10,2},{3,11},{11,3},{4,12},{12,4},... | collective-permute-start | bytes 393224 | tf_op jit(solution)/shard_map/ppermute | solution.py:745
  21.3 8.4 %collective-permute-start.10 = (bf16[256,256]{1,0:T(8,128)(2,1)S(1)}, bf16[256,256]{1,0:T(8,128)(2,1)S(1)}, u32[]{:S(2)}, u32[]{:S(2)}) collective-permute-start(bf16[256,256]{1,0:T(8,128)(2,1)S(1)} %collective-permute-done.3.far_normed_ref), channel_id=1, source_target_pairs={{0,8},{8,0},{1,9},{9,1},{2,10},{10,2},{3,11},{11,3},{4,12},{12,4},... | collective-permute-start | bytes 393224 | tf_op jit(solution)/shard_map/ppermute | solution.py:745
  21.7 2.8 %copy-start.1 = (bf16[128,512]{1,0:T(8,128)(2,1)S(1)}, bf16[128,512]{1,0:T(8,128)(2,1)}, u32[]{:S(2)}) copy-start(bf16[128,512]{1,0:T(8,128)(2,1)} %hid_ref.3) | copy-start | bytes 393220
  21.7 2.9 %copy-start.2 = (bf16[512,128]{1,0:T(8,128)(2,1)S(1)}, bf16[512,128]{1,0:T(8,128)(2,1)}, u32[]{:S(2)}) copy-start(bf16[512,128]{1,0:T(8,128)(2,1)} %back_ref.3) | copy-start | bytes 393220
  27.9 1.8 %collective-permute-start.8 = (bf16[512,128]{1,0:T(8,128)(2,1)S(1)}, bf16[512,128]{1,0:T(8,128)(2,1)S(1)}, u32[]{:S(2)}, u32[]{:S(2)}) collective-permute-start(bf16[512,128]{1,0:T(8,128)(2,1)S(1)} %constant_dynamic-update-slice_fusion.opm_ref), channel_id=1, source_target_pairs={{0,8},{8,0},{1,9},{9,1},{2,10},{10,2},{3,11},{11,3},{4,12},{12,4},... | collective-permute-start | bytes 393224 | tf_op jit(solution)/shard_map/ppermute | solution.py:745
  31.8 6.8 %collective-permute-start.14 = (bf16[2048,128]{1,0:T(8,128)(2,1)S(1)}, bf16[2048,128]{1,0:T(8,128)(2,1)S(1)}, u32[]{:S(2)}, u32[]{:S(2)}) collective-permute-start(bf16[2048,128]{1,0:T(8,128)(2,1)S(1)} %weight_gradients.1.mine_ref), channel_id=1, source_target_pairs={{0,8},{8,0},{1,9},{9,1},{2,10},{10,2},{3,11},{11,3},{4,12},{12,4},... | collective-permute-start | bytes 1572872 | tf_op jit(solution)/shard_map/ppermute | solution.py:745
  32.1 5.7 %collective-permute-start.11 = (bf16[64,256]{1,0:T(8,128)(2,1)S(1)}, bf16[64,256]{1,0:T(8,128)(2,1)S(1)}, u32[]{:S(2)}, u32[]{:S(2)}) collective-permute-start(bf16[64,256]{1,0:T(8,128)(2,1)S(1)} %get-tuple-element.92), channel_id=1, source_target_pairs={{0,6},{1,7},{2,4},{3,5},{4,2},{5,3},{6,0},{7,1},{8,12},{9,13},{10,... | collective-permute-start | bytes 98312 | tf_op jit(solution)/shard_map/ppermute | solution.py:741
  35.1 2.7 %collective-permute-start.12 = (bf16[64,256]{1,0:T(8,128)(2,1)S(1)}, bf16[64,256]{1,0:T(8,128)(2,1)S(1)}, u32[]{:S(2)}, u32[]{:S(2)}) collective-permute-start(bf16[64,256]{1,0:T(8,128)(2,1)S(1)} %get-tuple-element.92), channel_id=1, source_target_pairs={{8,10},{9,11},{10,8},{11,9},{12,14},{13,15},{14,12},{15,13},{24,26... | collective-permute-start | bytes 98312 | tf_op jit(solution)/shard_map/ppermute | solution.py:741
  37.9 1.8 %collective-permute-start.13 = (bf16[64,256]{1,0:T(8,128)(2,1)S(1)}, bf16[64,256]{1,0:T(8,128)(2,1)S(1)}, u32[]{:S(2)}, u32[]{:S(2)}) collective-permute-start(bf16[64,256]{1,0:T(8,128)(2,1)S(1)} %add_convert_fusion), channel_id=1, source_target_pairs={{0,8},{8,0},{1,9},{9,1},{2,10},{10,2},{3,11},{11,3},{4,12},{12,4},... | collective-permute-start | bytes 98312 | tf_op jit(solution)/shard_map/ppermute | solution.py:745

commit v15 on v13

--- a/solution.py
+++ b/solution.py
@@ -692,7 +692,16 @@
 
 
 def feature_kernel(
-    copies, spread_ref, first_ref, second_ref, scale_ref, scaled_ref, inv_ref, feat_ref
+    copies,
+    spread_ref,
+    first_ref,
+    second_ref,
+    scale_ref,
+    scaled_ref,
+    inv_ref,
+    held_ref,
+    feat_ref,
+    couple_ref,
 ):
     back = jnp.dot(
         spread_ref[...],
@@ -702,6 +711,7 @@
     feat_ref[...] = standardize_adjoint(
         back * scale_ref[...], scaled_ref[...], inv_ref[...]
     ).astype(jnp.bfloat16)
+    couple_ref[...] = held_ref[...]
 
 
 def swap_line(block, partners):
@@ -811,8 +821,8 @@
     blocks = lax.optimization_barrier(
         jnp.concatenate([sent] + [swap_col(sent, partner) for partner in Z_PARTNERS])
     )
-    half_normed = seqs * res // 2
-    far_normed_a = swap_col(normed[:half_normed], Y_PARTNER)
+    early_rows = seqs * res * 3 // 4
+    far_normed_a = swap_col(normed[:early_rows], Y_PARTNER)
     blocks, far_normed_a = lax.optimization_barrier((blocks, far_normed_a))
     near, pair_near = blocks[:, :rows], blocks[:, rows:]
     far = swap_col(near, Y_PARTNER)
@@ -843,10 +853,10 @@
         compiler_params=params,
         name="outer_products",
     )(ids, near, far, other_near, other_far, wturn)
-    normed_b, proj_out = lax.optimization_barrier((normed[half_normed:], proj_out))
+    normed_b, proj_out = lax.optimization_barrier((normed[early_rows:], proj_out))
     far_normed_b = swap_col(normed_b, Y_PARTNER)
     pair_far, proj_out = lax.optimization_barrier((pair_far, proj_out))
-    couple, opm, pn, gh, hidden, mg = pl.pallas_call(
+    held, opm, pn, gh, hidden, mg = pl.pallas_call(
         functools.partial(transition_kernel, sizes),
         out_shape=(
             shape((per, pair_width), bf16),
@@ -921,14 +931,14 @@
         other_normed,
         other_far_normed,
     )
-    feat = pl.pallas_call(
+    feat, couple = pl.pallas_call(
         functools.partial(feature_kernel, res),
-        out_shape=shape((seqs * res, channels), bf16),
-        in_specs=[vmem] * 6,
-        out_specs=vmem,
+        out_shape=(shape((seqs * res, channels), bf16), shape((per, pair_width), bf16)),
+        in_specs=[vmem] * 7,
+        out_specs=[vmem] * 2,
         compiler_params=params,
         name="features",
-    )(spread, first, second, scale, scaled, inv)
+    )(spread, first, second, scale, scaled, inv, held)
     part, weights = lax.optimization_barrier((part, weights))
     dout, dhid, dback = pl.pallas_call(
         weights_sum_kernel,
@@ -945,7 +955,7 @@
     came_a = swap_line(part, Z_PARTNERS[:2])
     came_b = swap_line(part, (None, Z_PARTNERS[2]))
     feat = feat.reshape(seqs, res, channels)
-    came_a, came_b, feat = lax.optimization_barrier((came_a, came_b, feat))
+    came_a, came_b, feat, couple = lax.optimization_barrier((came_a, came_b, feat, couple))
     kept = jnp.where(lax.axis_index("depth") == 0, part, came_b)
     kept = lax.optimization_barrier((kept.astype(f32) + came_a.astype(f32)).astype(bf16))
     came = swap_depth(kept)

time: 40.3 us -> 40.3 us (level)
  starting transfers between devices: 16.2 us -> 17 us
  waiting for transfers between devices: 10.1 us -> 9.45 us
    ppermute x2, waiting for transfers between devices: 1.73 us -> 0.84 us  [swap_line(): return lax.ppermute(block, ('depth', 'col'), pairs)]
    pallas_call x1, Pallas kernels: 2.42 us -> 1.81 us  [whole_plan(): pl.pallas_call(functools.partial(transition_kernel, sizes), out_shape=(sh...]
    pallas_call x1, Pallas kernels: 0.31 us -> 0.85 us  [whole_plan(): pl.pallas_call(functools.partial(feature_kernel, res), out_shape=(shape((...]
    ppermute x7, starting transfers between devices: 1.34 us -> 1.79 us  [swap_depth(): return lax.ppermute(block, 'depth', [(0, 1), (1, 0)])]
where the time goes in v15:
time: 40.3 us; the launch traced here: 40.1 us
  starting transfers between devices  17 us (42%)
  Pallas kernels  11.2 us (28%)
  waiting for transfers between devices  9.45 us (23%)
  local copies, waits for them, and re-layouts  1.49 us (4%)
  between operations  0.8 us (2%)
    ppermute x7, starting transfers between devices, swap_col(): lax.ppermute(block, 'col', [(at, at ^ partner) for at in range(count)])  11.9 us
    ppermute x7, waiting for transfers between devices, swap_col(): lax.ppermute(block, 'col', [(at, at ^ partner) for at in range(count)])  8.52 us
    ppermute x2, starting transfers between devices, swap_line(): return lax.ppermute(block, ('depth', 'col'), pairs)  3.33 us
    pallas_call x1, Pallas kernels, whole_plan(): pl.pallas_call(functools.partial(outer_kernel, sizes), out_shape=(shape((...  2.68 us
    pallas_call x1, Pallas kernels, whole_plan(): pl.pallas_call(functools.partial(projector_kernel, sizes), out_shape=(sha...  2.05 us
    pallas_call x1, Pallas kernels, whole_plan(): pl.pallas_call(pre_kernel, out_shape=(shape((1, rows + 2 * per, pair_widt...  1.91 us
    pallas_call x1, Pallas kernels, whole_plan(): pl.pallas_call(functools.partial(transition_kernel, sizes), out_shape=(sh...  1.81 us
    ppermute x7, starting transfers between devices, swap_depth(): return lax.ppermute(block, 'depth', [(0, 1), (1, 0)])  1.79 us
  transfers between devices with their start and end apart: 16, of which 7 were waited for; matrix products, arithmetic and copies ran while one was open for 2% of the time, Pallas kernels for 18%

profile of v15, /device:TPU:0, one launch (start us, length us, event | category | flops | bytes accessed | tf_op | source)
XLA Modules:
  0.0 40.1 jit_solution(2893044373055078255)
XLA Ops:
  0.6 0.1 pad_add_fusion.ids_ref
  0.7 1.9 %project.1 = (bf16[1,272,128]{2,1,0:T(8,128)(2,1)S(1)}, f32[1,256]{1,0:T(1,128)S(1)}, bf16[32,256]{1,0:T(8,128)(2,1)S(1)}, bf16[32,256]{1,0:T(8,128)(2,1)S(1)}, ...) custom-call(s32[2]{0:T(128)S(1)} %pad_add_fusion.ids_ref, ...), custom_call_target="tpu_custom_call" | custom-call | tf_op jit(solution)/shard_map/project/pallas_call | solution.py:780
  2.6 5.1 %collective-permute-start = (bf16[1,272,128]{2,1,0:T(8,128)(2,1)S(1)}, bf16[1,272,128]{2,1,0:T(8,128)(2,1)S(1)}, u32[]{:S(2)}, u32[]{:S(2)}) collective-permute-start(bf16[1,272,128]{2,1,0:T(8,128)(2,1)S(1)} %get-tuple-element.57), channel_id=1, source_target_pairs={{0,6},{1,7},{2,4},{3,5},{4,2},{5,3},{6,0},{7,1},{8,14},{9,15},{10,... | collective-permute-start | bytes 208904 | tf_op jit(solution)/shard_map/ppermute | solution.py:740
  7.7 0.0 collective-permute-start.1
  7.8 0.6 %collective-permute-start.2 = (bf16[1,272,128]{2,1,0:T(8,128)(2,1)S(1)}, bf16[1,272,128]{2,1,0:T(8,128)(2,1)S(1)}, u32[]{:S(2)}, u32[]{:S(2)}) collective-permute-start(bf16[1,272,128]{2,1,0:T(8,128)(2,1)S(1)} %get-tuple-element.57), channel_id=1, source_target_pairs={{0,2},{1,3},{2,0},{3,1},{4,6},{5,7},{6,4},{7,5},{8,10},{9,11},{10,... | collective-permute-start | bytes 208904 | tf_op jit(solution)/shard_map/ppermute | solution.py:740
  8.4 1.7 %collective-permute-start.3 = (bf16[192,256]{1,0:T(8,128)(2,1)S(1)}, bf16[192,256]{1,0:T(8,128)(2,1)S(1)}, u32[]{:S(2)}, u32[]{:S(2)}) collective-permute-start(bf16[192,256]{1,0:T(8,128)(2,1)S(1)} %slice.18), channel_id=1, source_target_pairs={{0,1},{1,0},{2,3},{3,2},{4,5},{5,4},{6,7},{7,6},{8,9},{9,8},{10,11... | collective-permute-start | bytes 294920 | tf_op jit(solution)/shard_map/ppermute | solution.py:740
  10.1 0.3 collective-permute-done
  10.4 3.2 %collective-permute-done.1 = bf16[1,272,128]{2,1,0:T(8,128)(2,1)S(1)} collective-permute-done((bf16[1,272,128]{2,1,0:T(8,128)(2,1)S(1)}, bf16[1,272,128]{2,1,0:T(8,128)(2,1)S(1)}, u32[]{:S(2)}, u32[]{:S(2)}) %collective-permute-start.1) | collective-permute-done | bytes 69664 | tf_op jit(solution)/shard_map/ppermute | solution.py:740
  13.7 0.0 collective-permute-done.2
  13.7 0.0 copy-start
  13.7 0.0 collective-permute-done.3
  13.7 1.6 %collective-permute-start.5 = (bf16[4,144,128]{2,1,0:T(8,128)(2,1)S(1)}, bf16[4,144,128]{2,1,0:T(8,128)(2,1)S(1)}, u32[]{:S(2)}, u32[]{:S(2)}) collective-permute-start(bf16[4,144,128]{2,1,0:T(8,128)(2,1)S(1)} %slice.21.near_ref), channel_id=1, source_target_pairs={{0,1},{1,0},{2,3},{3,2},{4,5},{5,4},{6,7},{7,6},{8,9},{9,8},{10,11... | collective-permute-start | bytes 442376 | tf_op jit(solution)/shard_map/ppermute | solution.py:740
  15.3 0.0 collective-permute-start.6
  15.3 3.8 %collective-permute-done.5.far_ref = bf16[4,144,128]{2,1,0:T(8,128)(2,1)S(1)} collective-permute-done((bf16[4,144,128]{2,1,0:T(8,128)(2,1)S(1)}, bf16[4,144,128]{2,1,0:T(8,128)(2,1)S(1)}, u32[]{:S(2)}, u32[]{:S(2)}) %collective-permute-start.5) | collective-permute-done | bytes 147488 | tf_op jit(solution)/shard_map/ppermute | solution.py:740
  19.2 0.0 collective-permute-start.7
  19.2 1.8 %collective-permute-start.4 = (bf16[4,128,128]{2,1,0:T(8,128)(2,1)S(1)}, bf16[4,128,128]{2,1,0:T(8,128)(2,1)S(1)}, u32[]{:S(2)}, u32[]{:S(2)}) collective-permute-start(bf16[4,128,128]{2,1,0:T(8,128)(2,1)S(1)} %slice.19.near_ref), channel_id=1, source_target_pairs={{0,1},{1,0},{2,3},{3,2},{4,5},{5,4},{6,7},{7,6},{8,9},{9,8},{10,11... | collective-permute-start | bytes 393224 | tf_op jit(solution)/shard_map/ppermute | solution.py:740
  21.0 0.2 collective-permute-start.10
  21.2 0.0 copy-done
  21.2 0.1 copy.19
  21.3 0.0 collective-permute-done.6.other_near_ref
  21.3 0.0 collective-permute-done.7.other_far_ref
  21.3 0.0 copy-start.2
  21.3 2.7 %outer_products.1 = (bf16[512,1024]{1,0:T(8,128)(2,1)S(1)}, f32[512,128]{1,0:T(8,128)S(1)}, f32[512,128]{1,0:T(8,128)S(1)}, bf16[512,128]{1,0:T(8,128)(2,1)S(1)}...) custom-call(s32[2]{0:T(128)S(1)} %pad_add_fusion.ids_ref, ...), custom_call_target="tpu_custom_call" | custom-call | tf_op jit(solution)/shard_map/outer_products/pallas_call | solution.py:832
  24.0 0.0 copy-start.1
  24.0 1.0 %collective-permute-start.8 = (bf16[64,256]{1,0:T(8,128)(2,1)S(1)}, bf16[64,256]{1,0:T(8,128)(2,1)S(1)}, u32[]{:S(2)}, u32[]{:S(2)}) collective-permute-start(bf16[64,256]{1,0:T(8,128)(2,1)S(1)} %slice.20), channel_id=1, source_target_pairs={{0,1},{1,0},{2,3},{3,2},{4,5},{5,4},{6,7},{7,6},{8,9},{9,8},{10,11... | collective-permute-start | bytes 98312 | tf_op jit(solution)/shard_map/ppermute | solution.py:740
  25.0 0.1 collective-permute-done.4.far_ref
  25.1 0.0 copy-done.2
  25.1 1.8 %transition.1 = (bf16[64,128]{1,0:T(8,128)(2,1)S(1)}, bf16[512,128]{1,0:T(8,128)(2,1)S(1)}, bf16[512,128]{1,0:T(8,128)(2,1)S(1)}, bf16[512,512]{1,0:T(8,128)(2,1...) custom-call(s32[2]{0:T(128)S(1)} %pad_add_fusion.ids_ref, bf16[4,128,128]{2,1,0:T(8,128)(2,1)S(1)} %slice.19.near_ref, ...), custom_call_target="tpu_custom_call" | custom-call | tf_op jit(solution)/shard_map/transition/pallas_call | solution.py:859
  27.0 1.1 %collective-permute-done.8 = bf16[64,256]{1,0:T(8,128)(2,1)S(1)} collective-permute-done((bf16[64,256]{1,0:T(8,128)(2,1)S(1)}, bf16[64,256]{1,0:T(8,128)(2,1)S(1)}, u32[]{:S(2)}, u32[]{:S(2)}) %collective-permute-start.8) | collective-permute-done | bytes 32800 | tf_op jit(solution)/shard_map/ppermute | solution.py:740
  28.0 0.0 collective-permute-start.11
  28.0 0.5 %collective-permute-start.9 = (bf16[512,128]{1,0:T(8,128)(2,1)S(1)}, bf16[512,128]{1,0:T(8,128)(2,1)S(1)}, u32[]{:S(2)}, u32[]{:S(2)}) collective-permute-start(bf16[512,128]{1,0:T(8,128)(2,1)S(1)} %get-tuple-element.69.opm_ref), channel_id=1, source_target_pairs={{0,8},{8,0},{1,9},{9,1},{2,10},{10,2},{3,11},{11,3},{4,12},{12,4},... | collective-permute-start | bytes 393224 | tf_op jit(solution)/shard_map/ppermute | solution.py:729
  28.5 0.9 %weight_gradients.1.mine_ref = bf16[2048,128]{1,0:T(8,128)(2,1)S(1)} custom-call(bf16[512,1024]{1,0:T(8,128)(2,1)S(1)} %get-tuple-element.72.outer_ref, bf16[512,128]{1,0:T(8,128)(2,1)S(1)} %get-tuple-element.69.opm_ref, bf16[512,128]{1,0:T(8,128)(2,1)S(1)} %get-tuple-element.73.pn_ref, bf16[512,512]{1,0:T(8,128)(2,1)S(1)} %get-tuple-element.74.gh_ref, ...), custom_call_target="tpu_custom_call" | custom-call | tf_op jit(solution)/shard_map/weight_gradients/pallas_call | solution.py:889
  29.5 0.0 collective-permute-done.10.other_normed_ref
  29.5 0.0 collective-permute-done.11.other_far_normed_ref
  29.5 0.1 collective-permute-done.9.other_opm_ref
  29.6 2.0 %projector_parts.1 = (bf16[64,256]{1,0:T(8,128)(2,1)S(1)}, bf16[256,256]{1,0:T(8,128)(2,1)S(1)}) custom-call(s32[2]{0:T(128)S(1)} %pad_add_fusion.ids_ref, bf16[512,128]{1,0:T(8,128)(2,1)S(1)} %get-tuple-element.69.opm_ref, bf16[512,128]{1,0:T(8,128)(2,1)S(1)} %collective-permute-done.9.other_opm_ref, bf16[1024,128]{1,0:T(8,128)(2,1)S(1)} %get-tuple-element.78.rightt_ref, ...), custom_call_target="tpu_custom_call" | custom-call | tf_op jit(solution)/shard_map/projector_parts/pallas_call | solution.py:901
  31.6 0.4 collective-permute-start.15
  32.0 2.7 %collective-permute-start.12 = (bf16[64,256]{1,0:T(8,128)(2,1)S(1)}, bf16[64,256]{1,0:T(8,128)(2,1)S(1)}, u32[]{:S(2)}, u32[]{:S(2)}) collective-permute-start(bf16[64,256]{1,0:T(8,128)(2,1)S(1)} %get-tuple-element.85), channel_id=1, source_target_pairs={{0,6},{1,7},{2,4},{3,5},{4,2},{5,3},{6,0},{7,1},{8,12},{9,13},{10,... | collective-permute-start | bytes 98312 | tf_op jit(solution)/shard_map/ppermute | solution.py:725
  34.7 0.7 %collective-permute-start.13 = (bf16[64,256]{1,0:T(8,128)(2,1)S(1)}, bf16[64,256]{1,0:T(8,128)(2,1)S(1)}, u32[]{:S(2)}, u32[]{:S(2)}) collective-permute-start(bf16[64,256]{1,0:T(8,128)(2,1)S(1)} %get-tuple-element.85), channel_id=1, source_target_pairs={{8,10},{9,11},{10,8},{11,9},{12,14},{13,15},{14,12},{15,13},{24,26... | collective-permute-start | bytes 98312 | tf_op jit(solution)/shard_map/ppermute | solution.py:725
  35.4 0.8 %features.1 = (bf16[256,256]{1,0:T(8,128)(2,1)S(1)}, bf16[64,128]{1,0:T(8,128)(2,1)}) custom-call(bf16[256,256]{1,0:T(8,128)(2,1)S(1)} %get-tuple-element.86.spread_ref, bf16[32,256]{1,0:T(8,128)(2,1)S(1)} %get-tuple-element.87.first_ref, bf16[32,256]{1,0:T(8,128)(2,1)S(1)} %get-tuple-element.88.second_ref, f32[1,256]{1,0:T(1,128)S(1)} %get-tuple-element.89.scale_ref, ...), custom_call_target="tpu_custom_call" | custom-call | tf_op jit(solution)/shard_map/features/pallas_call | solution.py:934
  36.2 0.7 %reshape.44 = bf16[64,4,256]{2,1,0:T(4,128)(2,1)} reshape(bf16[256,256]{1,0:T(8,128)(2,1)S(1)} %get-tuple-element.93) | data formatting | bytes 262144 | tf_op jit(solution)/shard_map/reshape | solution.py:957
  36.9 0.8 %collective-permute-done.12 = bf16[64,256]{1,0:T(8,128)(2,1)S(1)} collective-permute-done((bf16[64,256]{1,0:T(8,128)(2,1)S(1)}, bf16[64,256]{1,0:T(8,128)(2,1)S(1)}, u32[]{:S(2)}, u32[]{:S(2)}) %collective-permute-start.12) | collective-permute-done | bytes 32800 | tf_op jit(solution)/shard_map/ppermute | solution.py:725
  37.7 0.0 collective-permute-done.13
  37.7 0.7 %collective-permute-start.14 = (bf16[64,256]{1,0:T(8,128)(2,1)S(1)}, bf16[64,256]{1,0:T(8,128)(2,1)S(1)}, u32[]{:S(2)}, u32[]{:S(2)}) collective-permute-start(bf16[64,256]{1,0:T(8,128)(2,1)S(1)} %add_convert_fusion), channel_id=1, source_target_pairs={{0,8},{8,0},{1,9},{9,1},{2,10},{10,2},{3,11},{11,3},{4,12},{12,4},... | collective-permute-start | bytes 98312 | tf_op jit(solution)/shard_map/ppermute | solution.py:729
  38.4 0.0 collective-permute-done.15.other_ref
  38.4 1.0 %sums_over_depth.1 = (f32[1024,128]{1,0:T(8,128)}, f32[128,512]{1,0:T(8,128)}, f32[512,128]{1,0:T(8,128)}) custom-call(bf16[2048,128]{1,0:T(8,128)(2,1)S(1)} %weight_gradients.1.mine_ref, bf16[2048,128]{1,0:T(8,128)(2,1)S(1)} %collective-permute-done.15.other_ref), custom_call_target="tpu_custom_call" | custom-call | tf_op jit(solution)/shard_map/sums_over_depth/pallas_call | solution.py:943
  39.4 0.0 collective-permute-done.14
  39.4 0.6 %slice_bitcast_fusion = (f32[256,32]{0,1:T(8,128)}, f32[256,32]{0,1:T(8,128)}) fusion(f32[64,256]{1,0:T(8,128)S(1)} %convert_add_fusion), kind=kLoop, calls=%fused_computation.3 | loop fusion | bytes 131072 | tf_op jit(solution)/shard_map/transpose | solution.py:968
  (10 shorter events, 0.1 us)
Async XLA Ops:
  2.6 7.8 %collective-permute-start = (bf16[1,272,128]{2,1,0:T(8,128)(2,1)S(1)}, bf16[1,272,128]{2,1,0:T(8,128)(2,1)S(1)}, u32[]{:S(2)}, u32[]{:S(2)}) collective-permute-start(bf16[1,272,128]{2,1,0:T(8,128)(2,1)S(1)} %get-tuple-element.57), channel_id=1, source_target_pairs={{0,6},{1,7},{2,4},{3,5},{4,2},{5,3},{6,0},{7,1},{8,14},{9,15},{10,... | collective-permute-start | bytes 208904 | tf_op jit(solution)/shard_map/ppermute | solution.py:740
  7.7 5.9 %collective-permute-start.1 = (bf16[1,272,128]{2,1,0:T(8,128)(2,1)S(1)}, bf16[1,272,128]{2,1,0:T(8,128)(2,1)S(1)}, u32[]{:S(2)}, u32[]{:S(2)}) collective-permute-start(bf16[1,272,128]{2,1,0:T(8,128)(2,1)S(1)} %get-tuple-element.57), channel_id=1, source_target_pairs={{0,4},{1,5},{2,6},{3,7},{4,0},{5,1},{6,2},{7,3},{8,12},{9,13},{10,... | collective-permute-start | bytes 208904 | tf_op jit(solution)/shard_map/ppermute | solution.py:740
  7.8 5.9 %collective-permute-start.2 = (bf16[1,272,128]{2,1,0:T(8,128)(2,1)S(1)}, bf16[1,272,128]{2,1,0:T(8,128)(2,1)S(1)}, u32[]{:S(2)}, u32[]{:S(2)}) collective-permute-start(bf16[1,272,128]{2,1,0:T(8,128)(2,1)S(1)} %get-tuple-element.57), channel_id=1, source_target_pairs={{0,2},{1,3},{2,0},{3,1},{4,6},{5,7},{6,4},{7,5},{8,10},{9,11},{10,... | collective-permute-start | bytes 208904 | tf_op jit(solution)/shard_map/ppermute | solution.py:740
  8.4 5.3 %collective-permute-start.3 = (bf16[192,256]{1,0:T(8,128)(2,1)S(1)}, bf16[192,256]{1,0:T(8,128)(2,1)S(1)}, u32[]{:S(2)}, u32[]{:S(2)}) collective-permute-start(bf16[192,256]{1,0:T(8,128)(2,1)S(1)} %slice.18), channel_id=1, source_target_pairs={{0,1},{1,0},{2,3},{3,2},{4,5},{5,4},{6,7},{7,6},{8,9},{9,8},{10,11... | collective-permute-start | bytes 294920 | tf_op jit(solution)/shard_map/ppermute | solution.py:740
  13.7 7.5 %copy-start = (bf16[1024,128]{1,0:T(8,128)(2,1)S(1)}, bf16[1024,128]{1,0:T(8,128)(2,1)}, u32[]{:S(2)}) copy-start(bf16[1024,128]{1,0:T(8,128)(2,1)} %wout_ref.1) | copy-start | bytes 786436
  13.7 5.4 %collective-permute-start.5 = (bf16[4,144,128]{2,1,0:T(8,128)(2,1)S(1)}, bf16[4,144,128]{2,1,0:T(8,128)(2,1)S(1)}, u32[]{:S(2)}, u32[]{:S(2)}) collective-permute-start(bf16[4,144,128]{2,1,0:T(8,128)(2,1)S(1)} %slice.21.near_ref), channel_id=1, source_target_pairs={{0,1},{1,0},{2,3},{3,2},{4,5},{5,4},{6,7},{7,6},{8,9},{9,8},{10,11... | collective-permute-start | bytes 442376 | tf_op jit(solution)/shard_map/ppermute | solution.py:740
  15.3 6.0 %collective-permute-start.6 = (bf16[4,144,128]{2,1,0:T(8,128)(2,1)S(1)}, bf16[4,144,128]{2,1,0:T(8,128)(2,1)S(1)}, u32[]{:S(2)}, u32[]{:S(2)}) collective-permute-start(bf16[4,144,128]{2,1,0:T(8,128)(2,1)S(1)} %slice.21.near_ref), channel_id=1, source_target_pairs={{0,8},{8,0},{1,9},{9,1},{2,10},{10,2},{3,11},{11,3},{4,12},{12,4},... | collective-permute-start | bytes 442376 | tf_op jit(solution)/shard_map/ppermute | solution.py:729
  19.2 2.2 %collective-permute-start.7 = (bf16[4,144,128]{2,1,0:T(8,128)(2,1)S(1)}, bf16[4,144,128]{2,1,0:T(8,128)(2,1)S(1)}, u32[]{:S(2)}, u32[]{:S(2)}) collective-permute-start(bf16[4,144,128]{2,1,0:T(8,128)(2,1)S(1)} %collective-permute-done.5.far_ref), channel_id=1, source_target_pairs={{0,8},{8,0},{1,9},{9,1},{2,10},{10,2},{3,11},{11,3},{4,12},{12,4},... | collective-permute-start | bytes 442376 | tf_op jit(solution)/shard_map/ppermute | solution.py:729
  19.2 6.0 %collective-permute-start.4 = (bf16[4,128,128]{2,1,0:T(8,128)(2,1)S(1)}, bf16[4,128,128]{2,1,0:T(8,128)(2,1)S(1)}, u32[]{:S(2)}, u32[]{:S(2)}) collective-permute-start(bf16[4,128,128]{2,1,0:T(8,128)(2,1)S(1)} %slice.19.near_ref), channel_id=1, source_target_pairs={{0,1},{1,0},{2,3},{3,2},{4,5},{5,4},{6,7},{7,6},{8,9},{9,8},{10,11... | collective-permute-start | bytes 393224 | tf_op jit(solution)/shard_map/ppermute | solution.py:740
  21.0 8.5 %collective-permute-start.10 = (bf16[256,256]{1,0:T(8,128)(2,1)S(1)}, bf16[256,256]{1,0:T(8,128)(2,1)S(1)}, u32[]{:S(2)}, u32[]{:S(2)}) collective-permute-start(bf16[256,256]{1,0:T(8,128)(2,1)S(1)} %get-tuple-element.58.normed_ref), channel_id=1, source_target_pairs={{0,8},{8,0},{1,9},{9,1},{2,10},{10,2},{3,11},{11,3},{4,12},{12,4},... | collective-permute-start | bytes 393224 | tf_op jit(solution)/shard_map/ppermute | solution.py:729
  21.3 3.8 %copy-start.2 = (bf16[512,128]{1,0:T(8,128)(2,1)S(1)}, bf16[512,128]{1,0:T(8,128)(2,1)}, u32[]{:S(2)}) copy-start(bf16[512,128]{1,0:T(8,128)(2,1)} %back_ref.1) | copy-start | bytes 393220
  24.0 1.1 %copy-start.1 = (bf16[128,512]{1,0:T(8,128)(2,1)S(1)}, bf16[128,512]{1,0:T(8,128)(2,1)}, u32[]{:S(2)}) copy-start(bf16[128,512]{1,0:T(8,128)(2,1)} %hid_ref.1) | copy-start | bytes 393220
  24.0 4.0 %collective-permute-start.8 = (bf16[64,256]{1,0:T(8,128)(2,1)S(1)}, bf16[64,256]{1,0:T(8,128)(2,1)S(1)}, u32[]{:S(2)}, u32[]{:S(2)}) collective-permute-start(bf16[64,256]{1,0:T(8,128)(2,1)S(1)} %slice.20), channel_id=1, source_target_pairs={{0,1},{1,0},{2,3},{3,2},{4,5},{5,4},{6,7},{7,6},{8,9},{9,8},{10,11... | collective-permute-start | bytes 98312 | tf_op jit(solution)/shard_map/ppermute | solution.py:740
  28.0 1.5 %collective-permute-start.11 = (bf16[256,256]{1,0:T(8,128)(2,1)S(1)}, bf16[256,256]{1,0:T(8,128)(2,1)S(1)}, u32[]{:S(2)}, u32[]{:S(2)}) collective-permute-start(bf16[256,256]{1,0:T(8,128)(2,1)S(1)} %constant_dynamic-update-slice_fusion.far_normed_ref), channel_id=1, source_target_pairs={{0,8},{8,0},{1,9},{9,1},{2,10},{10,2},{3,11},{11,3},{4,12},{12,4},... | collective-permute-start | bytes 393224 | tf_op jit(solution)/shard_map/ppermute | solution.py:729
  28.0 1.5 %collective-permute-start.9 = (bf16[512,128]{1,0:T(8,128)(2,1)S(1)}, bf16[512,128]{1,0:T(8,128)(2,1)S(1)}, u32[]{:S(2)}, u32[]{:S(2)}) collective-permute-start(bf16[512,128]{1,0:T(8,128)(2,1)S(1)} %get-tuple-element.69.opm_ref), channel_id=1, source_target_pairs={{0,8},{8,0},{1,9},{9,1},{2,10},{10,2},{3,11},{11,3},{4,12},{12,4},... | collective-permute-start | bytes 393224 | tf_op jit(solution)/shard_map/ppermute | solution.py:729
  31.6 6.8 %collective-permute-start.15 = (bf16[2048,128]{1,0:T(8,128)(2,1)S(1)}, bf16[2048,128]{1,0:T(8,128)(2,1)S(1)}, u32[]{:S(2)}, u32[]{:S(2)}) collective-permute-start(bf16[2048,128]{1,0:T(8,128)(2,1)S(1)} %weight_gradients.1.mine_ref), channel_id=1, source_target_pairs={{0,8},{8,0},{1,9},{9,1},{2,10},{10,2},{3,11},{11,3},{4,12},{12,4},... | collective-permute-start | bytes 1572872 | tf_op jit(solution)/shard_map/ppermute | solution.py:729
  32.0 5.7 %collective-permute-start.12 = (bf16[64,256]{1,0:T(8,128)(2,1)S(1)}, bf16[64,256]{1,0:T(8,128)(2,1)S(1)}, u32[]{:S(2)}, u32[]{:S(2)}) collective-permute-start(bf16[64,256]{1,0:T(8,128)(2,1)S(1)} %get-tuple-element.85), channel_id=1, source_target_pairs={{0,6},{1,7},{2,4},{3,5},{4,2},{5,3},{6,0},{7,1},{8,12},{9,13},{10,... | collective-permute-start | bytes 98312 | tf_op jit(solution)/shard_map/ppermute | solution.py:725
  34.7 3.0 %collective-permute-start.13 = (bf16[64,256]{1,0:T(8,128)(2,1)S(1)}, bf16[64,256]{1,0:T(8,128)(2,1)S(1)}, u32[]{:S(2)}, u32[]{:S(2)}) collective-permute-start(bf16[64,256]{1,0:T(8,128)(2,1)S(1)} %get-tuple-element.85), channel_id=1, source_target_pairs={{8,10},{9,11},{10,8},{11,9},{12,14},{13,15},{14,12},{15,13},{24,26... | collective-permute-start | bytes 98312 | tf_op jit(solution)/shard_map/ppermute | solution.py:725
  37.7 1.7 %collective-permute-start.14 = (bf16[64,256]{1,0:T(8,128)(2,1)S(1)}, bf16[64,256]{1,0:T(8,128)(2,1)S(1)}, u32[]{:S(2)}, u32[]{:S(2)}) collective-permute-start(bf16[64,256]{1,0:T(8,128)(2,1)S(1)} %add_convert_fusion), channel_id=1, source_target_pairs={{0,8},{8,0},{1,9},{9,1},{2,10},{10,2},{3,11},{11,3},{4,12},{12,4},... | collective-permute-start | bytes 98312 | tf_op jit(solution)/shard_map/ppermute | solution.py:729

commit v16 on v15

--- a/solution.py
+++ b/solution.py
@@ -821,9 +821,8 @@
     blocks = lax.optimization_barrier(
         jnp.concatenate([sent] + [swap_col(sent, partner) for partner in Z_PARTNERS])
     )
-    early_rows = seqs * res * 3 // 4
-    far_normed_a = swap_col(normed[:early_rows], Y_PARTNER)
-    blocks, far_normed_a = lax.optimization_barrier((blocks, far_normed_a))
+    far_normed = swap_col(normed, Y_PARTNER)
+    blocks, far_normed = lax.optimization_barrier((blocks, far_normed))
     near, pair_near = blocks[:, :rows], blocks[:, rows:]
     far = swap_col(near, Y_PARTNER)
     pair_far = swap_col(pair_near, Y_PARTNER)
@@ -853,9 +852,11 @@
         compiler_params=params,
         name="outer_products",
     )(ids, near, far, other_near, other_far, wturn)
-    normed_b, proj_out = lax.optimization_barrier((normed[early_rows:], proj_out))
-    far_normed_b = swap_col(normed_b, Y_PARTNER)
-    pair_far, proj_out = lax.optimization_barrier((pair_far, proj_out))
+    normed_again, far_again, proj_out = lax.optimization_barrier((normed, far_normed, proj_out))
+    other_normed, other_far_normed = swap_depth(normed_again), swap_depth(far_again)
+    pair_far, proj_out, other_normed, other_far_normed = lax.optimization_barrier(
+        (pair_far, proj_out, other_normed, other_far_normed)
+    )
     held, opm, pn, gh, hidden, mg = pl.pallas_call(
         functools.partial(transition_kernel, sizes),
         out_shape=(
@@ -884,8 +885,6 @@
         hidden_weight,
         back_weight,
     )
-    opm, far_normed_b = lax.optimization_barrier((opm, far_normed_b))
-    far_normed = jnp.concatenate([far_normed_a, far_normed_b])
     weights = pl.pallas_call(
         weights_kernel,
         out_shape=shape((outer_width + 2 * hid, pair_width), bf16),
@@ -895,9 +894,7 @@
         compiler_params=params,
         name="weight_gradients",
     )(outer, opm, pn, gh, hidden, mg)
-    other_opm, other_normed, other_far_normed, weights = lax.optimization_barrier(
-        (swap_depth(opm), swap_depth(normed), swap_depth(far_normed), weights)
-    )
+    other_opm, weights = lax.optimization_barrier((swap_depth(opm), weights))
     part, spread = pl.pallas_call(
         functools.partial(projector_kernel, sizes),
         out_shape=(

time: 40.3 us -> 40.5 us (level)
  waiting for transfers between devices: 9.45 us -> 11.6 us
  starting transfers between devices: 17 us -> 15.1 us
    ppermute x7 -> x6, starting transfers between devices: 11.9 us -> 10.6 us  [swap_col(): lax.ppermute(block, 'col', [(at, at ^ partner) for at in range(count)])]
    ppermute x2, waiting for transfers between devices: 0.84 us -> 2.02 us  [swap_line(): return lax.ppermute(block, ('depth', 'col'), pairs)]
    ppermute x7 -> x6, waiting for transfers between devices: 8.52 us -> 9.19 us  [swap_col(): lax.ppermute(block, 'col', [(at, at ^ partner) for at in range(count)])]
    ppermute x7, starting transfers between devices: 1.79 us -> 1.24 us  [swap_depth(): return lax.ppermute(block, 'depth', [(0, 1), (1, 0)])]
  transfers between devices with their start and end apart: 16 -> 15, of which waited for: 7 -> 7; matrix products, arithmetic and copies ran while one was open for 2% -> 2% of each run, Pallas kernels for 18% -> 14%
where the time goes in v16:
time: 40.5 us; the launch traced here: 40.2 us
  starting transfers between devices  15.1 us (37%)
  waiting for transfers between devices  11.6 us (29%)
  Pallas kernels  11.2 us (28%)
  local copies, waits for them, and re-layouts  1.46 us (4%)
  between operations  0.77 us (2%)
    ppermute x6, starting transfers between devices, swap_col(): lax.ppermute(block, 'col', [(at, at ^ partner) for at in range(count)])  10.6 us
    ppermute x6, waiting for transfers between devices, swap_col(): lax.ppermute(block, 'col', [(at, at ^ partner) for at in range(count)])  9.19 us
    ppermute x2, starting transfers between devices, swap_line(): return lax.ppermute(block, ('depth', 'col'), pairs)  3.23 us
    pallas_call x1, Pallas kernels, whole_plan(): pl.pallas_call(functools.partial(outer_kernel, sizes), out_shape=(shape((...  2.68 us
    pallas_call x1, Pallas kernels, whole_plan(): pl.pallas_call(functools.partial(projector_kernel, sizes), out_shape=(sha...  2.05 us
    ppermute x2, waiting for transfers between devices, swap_line(): return lax.ppermute(block, ('depth', 'col'), pairs)  2.02 us
    pallas_call x1, Pallas kernels, whole_plan(): pl.pallas_call(pre_kernel, out_shape=(shape((1, rows + 2 * per, pair_widt...  1.91 us
    pallas_call x1, Pallas kernels, whole_plan(): pl.pallas_call(functools.partial(transition_kernel, sizes), out_shape=(sh...  1.81 us
  transfers between devices with their start and end apart: 15, of which 7 were waited for; matrix products, arithmetic and copies ran while one was open for 2% of the time, Pallas kernels for 14%

profile of v16, /device:TPU:0, one launch (start us, length us, event | category | flops | bytes accessed | tf_op | source)
XLA Modules:
  0.0 40.2 jit_solution(17159603506141594257)
XLA Ops:
  0.6 0.1 pad_add_fusion.ids_ref
  0.7 1.9 %project.1 = (bf16[1,272,128]{2,1,0:T(8,128)(2,1)S(1)}, f32[1,256]{1,0:T(1,128)S(1)}, bf16[32,256]{1,0:T(8,128)(2,1)S(1)}, bf16[32,256]{1,0:T(8,128)(2,1)S(1)}, ...) custom-call(s32[2]{0:T(128)S(1)} %pad_add_fusion.ids_ref, ...), custom_call_target="tpu_custom_call" | custom-call | tf_op jit(solution)/shard_map/project/pallas_call | solution.py:780
  2.6 3.1 %collective-permute-start.2 = (bf16[1,272,128]{2,1,0:T(8,128)(2,1)S(1)}, bf16[1,272,128]{2,1,0:T(8,128)(2,1)S(1)}, u32[]{:S(2)}, u32[]{:S(2)}) collective-permute-start(bf16[1,272,128]{2,1,0:T(8,128)(2,1)S(1)} %get-tuple-element.56), channel_id=1, source_target_pairs={{0,2},{1,3},{2,0},{3,1},{4,6},{5,7},{6,4},{7,5},{8,10},{9,11},{10,... | collective-permute-start | bytes 208904 | tf_op jit(solution)/shard_map/ppermute | solution.py:740
  5.7 2.6 %collective-permute-start.1 = (bf16[1,272,128]{2,1,0:T(8,128)(2,1)S(1)}, bf16[1,272,128]{2,1,0:T(8,128)(2,1)S(1)}, u32[]{:S(2)}, u32[]{:S(2)}) collective-permute-start(bf16[1,272,128]{2,1,0:T(8,128)(2,1)S(1)} %get-tuple-element.56), channel_id=1, source_target_pairs={{0,4},{1,5},{2,6},{3,7},{4,0},{5,1},{6,2},{7,3},{8,12},{9,13},{10,... | collective-permute-start | bytes 208904 | tf_op jit(solution)/shard_map/ppermute | solution.py:740
  8.3 0.0 collective-permute-start
  8.3 1.7 %collective-permute-start.3 = (bf16[256,256]{1,0:T(8,128)(2,1)S(1)}, bf16[256,256]{1,0:T(8,128)(2,1)S(1)}, u32[]{:S(2)}, u32[]{:S(2)}) collective-permute-start(bf16[256,256]{1,0:T(8,128)(2,1)S(1)} %get-tuple-element.62.normed_ref), channel_id=1, source_target_pairs={{0,1},{1,0},{2,3},{3,2},{4,5},{5,4},{6,7},{7,6},{8,9},{9,8},{10,11... | collective-permute-start | bytes 393224 | tf_op jit(solution)/shard_map/ppermute | solution.py:740
  10.1 0.0 collective-permute-done.2
  10.1 3.2 %collective-permute-done.1 = bf16[1,272,128]{2,1,0:T(8,128)(2,1)S(1)} collective-permute-done((bf16[1,272,128]{2,1,0:T(8,128)(2,1)S(1)}, bf16[1,272,128]{2,1,0:T(8,128)(2,1)S(1)}, u32[]{:S(2)}, u32[]{:S(2)}) %collective-permute-start.1) | collective-permute-done | bytes 69664 | tf_op jit(solution)/shard_map/ppermute | solution.py:740
  13.2 1.3 %collective-permute-done = bf16[1,272,128]{2,1,0:T(8,128)(2,1)S(1)} collective-permute-done((bf16[1,272,128]{2,1,0:T(8,128)(2,1)S(1)}, bf16[1,272,128]{2,1,0:T(8,128)(2,1)S(1)}, u32[]{:S(2)}, u32[]{:S(2)}) %collective-permute-start) | collective-permute-done | bytes 69664 | tf_op jit(solution)/shard_map/ppermute | solution.py:740
  14.6 0.0 copy-start
  14.6 0.0 collective-permute-done.3.far_normed_ref
  14.6 1.6 %collective-permute-start.5 = (bf16[4,144,128]{2,1,0:T(8,128)(2,1)S(1)}, bf16[4,144,128]{2,1,0:T(8,128)(2,1)S(1)}, u32[]{:S(2)}, u32[]{:S(2)}) collective-permute-start(bf16[4,144,128]{2,1,0:T(8,128)(2,1)S(1)} %slice.13.near_ref), channel_id=1, source_target_pairs={{0,1},{1,0},{2,3},{3,2},{4,5},{5,4},{6,7},{7,6},{8,9},{9,8},{10,11... | collective-permute-start | bytes 442376 | tf_op jit(solution)/shard_map/ppermute | solution.py:740
  16.2 0.0 collective-permute-start.6
  16.2 3.6 %collective-permute-done.5.far_ref = bf16[4,144,128]{2,1,0:T(8,128)(2,1)S(1)} collective-permute-done((bf16[4,144,128]{2,1,0:T(8,128)(2,1)S(1)}, bf16[4,144,128]{2,1,0:T(8,128)(2,1)S(1)}, u32[]{:S(2)}, u32[]{:S(2)}) %collective-permute-start.5) | collective-permute-done | bytes 147488 | tf_op jit(solution)/shard_map/ppermute | solution.py:740
  19.8 0.0 collective-permute-start.7
  19.8 0.0 copy-done
  19.8 0.1 copy.19
  19.9 1.6 %collective-permute-start.4 = (bf16[4,128,128]{2,1,0:T(8,128)(2,1)S(1)}, bf16[4,128,128]{2,1,0:T(8,128)(2,1)S(1)}, u32[]{:S(2)}, u32[]{:S(2)}) collective-permute-start(bf16[4,128,128]{2,1,0:T(8,128)(2,1)S(1)} %slice.12.near_ref), channel_id=1, source_target_pairs={{0,1},{1,0},{2,3},{3,2},{4,5},{5,4},{6,7},{7,6},{8,9},{9,8},{10,11... | collective-permute-start | bytes 393224 | tf_op jit(solution)/shard_map/ppermute | solution.py:740
  21.5 0.0 collective-permute-done.6.other_near_ref
  21.5 0.0 collective-permute-done.7.other_far_ref
  21.5 0.0 copy-start.1
  21.5 0.0 copy-start.2
  21.6 2.7 %outer_products.1 = (bf16[512,1024]{1,0:T(8,128)(2,1)S(1)}, f32[512,128]{1,0:T(8,128)S(1)}, f32[512,128]{1,0:T(8,128)S(1)}, bf16[512,128]{1,0:T(8,128)(2,1)S(1)}...) custom-call(s32[2]{0:T(128)S(1)} %pad_add_fusion.ids_ref, ...), custom_call_target="tpu_custom_call" | custom-call | tf_op jit(solution)/shard_map/outer_products/pallas_call | solution.py:831
  24.2 0.3 collective-permute-start.8
  24.5 0.3 collective-permute-start.9
  24.8 1.1 %collective-permute-done.4.far_ref = bf16[4,128,128]{2,1,0:T(8,128)(2,1)S(1)} collective-permute-done((bf16[4,128,128]{2,1,0:T(8,128)(2,1)S(1)}, bf16[4,128,128]{2,1,0:T(8,128)(2,1)S(1)}, u32[]{:S(2)}, u32[]{:S(2)}) %collective-permute-start.4) | collective-permute-done | bytes 131104 | tf_op jit(solution)/shard_map/ppermute | solution.py:740
  25.9 0.0 collective-permute-done.8.other_normed_ref
  25.9 0.0 collective-permute-done.9.other_far_normed_ref
  25.9 0.0 copy-done.1
  25.9 0.0 copy-done.2
  25.9 1.8 %transition.1 = (bf16[64,128]{1,0:T(8,128)(2,1)S(1)}, bf16[512,128]{1,0:T(8,128)(2,1)S(1)}, bf16[512,128]{1,0:T(8,128)(2,1)S(1)}, bf16[512,512]{1,0:T(8,128)(2,1...) custom-call(s32[2]{0:T(128)S(1)} %pad_add_fusion.ids_ref, bf16[4,128,128]{2,1,0:T(8,128)(2,1)S(1)} %slice.12.near_ref, ...), custom_call_target="tpu_custom_call" | custom-call | tf_op jit(solution)/shard_map/transition/pallas_call | solution.py:860
  27.8 0.3 collective-permute-start.10
  28.1 0.9 %weight_gradients.1.mine_ref = bf16[2048,128]{1,0:T(8,128)(2,1)S(1)} custom-call(bf16[512,1024]{1,0:T(8,128)(2,1)S(1)} %get-tuple-element.70.outer_ref, bf16[512,128]{1,0:T(8,128)(2,1)S(1)} %get-tuple-element.69.opm_ref, bf16[512,128]{1,0:T(8,128)(2,1)S(1)} %get-tuple-element.71.pn_ref, bf16[512,512]{1,0:T(8,128)(2,1)S(1)} %get-tuple-element.72.gh_ref, ...), custom_call_target="tpu_custom_call" | custom-call | tf_op jit(solution)/shard_map/weight_gradients/pallas_call | solution.py:888
  29.0 0.2 collective-permute-done.10.other_opm_ref
  29.2 2.0 %projector_parts.1 = (bf16[64,256]{1,0:T(8,128)(2,1)S(1)}, bf16[256,256]{1,0:T(8,128)(2,1)S(1)}) custom-call(s32[2]{0:T(128)S(1)} %pad_add_fusion.ids_ref, bf16[512,128]{1,0:T(8,128)(2,1)S(1)} %get-tuple-element.69.opm_ref, bf16[512,128]{1,0:T(8,128)(2,1)S(1)} %collective-permute-done.10.other_opm_ref, bf16[1024,128]{1,0:T(8,128)(2,1)S(1)} %get-tuple-element.76.rightt_ref, ...), custom_call_target="tpu_custom_call" | custom-call | tf_op jit(solution)/shard_map/projector_parts/pallas_call | solution.py:898
  31.2 0.3 collective-permute-start.14
  31.5 0.7 %collective-permute-start.12 = (bf16[64,256]{1,0:T(8,128)(2,1)S(1)}, bf16[64,256]{1,0:T(8,128)(2,1)S(1)}, u32[]{:S(2)}, u32[]{:S(2)}) collective-permute-start(bf16[64,256]{1,0:T(8,128)(2,1)S(1)} %get-tuple-element.83), channel_id=1, source_target_pairs={{8,10},{9,11},{10,8},{11,9},{12,14},{13,15},{14,12},{15,13},{24,26... | collective-permute-start | bytes 98312 | tf_op jit(solution)/shard_map/ppermute | solution.py:725
  32.2 2.6 %collective-permute-start.11 = (bf16[64,256]{1,0:T(8,128)(2,1)S(1)}, bf16[64,256]{1,0:T(8,128)(2,1)S(1)}, u32[]{:S(2)}, u32[]{:S(2)}) collective-permute-start(bf16[64,256]{1,0:T(8,128)(2,1)S(1)} %get-tuple-element.83), channel_id=1, source_target_pairs={{0,6},{1,7},{2,4},{3,5},{4,2},{5,3},{6,0},{7,1},{8,12},{9,13},{10,... | collective-permute-start | bytes 98312 | tf_op jit(solution)/shard_map/ppermute | solution.py:725
  34.8 0.8 %features.1 = (bf16[256,256]{1,0:T(8,128)(2,1)S(1)}, bf16[64,128]{1,0:T(8,128)(2,1)}) custom-call(bf16[256,256]{1,0:T(8,128)(2,1)S(1)} %get-tuple-element.84.spread_ref, bf16[32,256]{1,0:T(8,128)(2,1)S(1)} %get-tuple-element.85.first_ref, bf16[32,256]{1,0:T(8,128)(2,1)S(1)} %get-tuple-element.86.second_ref, f32[1,256]{1,0:T(1,128)S(1)} %get-tuple-element.87.scale_ref, ...), custom_call_target="tpu_custom_call" | custom-call | tf_op jit(solution)/shard_map/features/pallas_call | solution.py:931
  35.6 0.7 %reshape.44 = bf16[64,4,256]{2,1,0:T(4,128)(2,1)} reshape(bf16[256,256]{1,0:T(8,128)(2,1)S(1)} %get-tuple-element.91) | data formatting | bytes 262144 | tf_op jit(solution)/shard_map/reshape | solution.py:954
  36.3 0.0 collective-permute-done.12
  36.3 2.0 %collective-permute-done.11 = bf16[64,256]{1,0:T(8,128)(2,1)S(1)} collective-permute-done((bf16[64,256]{1,0:T(8,128)(2,1)S(1)}, bf16[64,256]{1,0:T(8,128)(2,1)S(1)}, u32[]{:S(2)}, u32[]{:S(2)}) %collective-permute-start.11) | collective-permute-done | bytes 32800 | tf_op jit(solution)/shard_map/ppermute | solution.py:725
  38.3 0.1 collective-permute-start.13
  38.4 0.0 collective-permute-done.14.other_ref
  38.4 1.0 %sums_over_depth.1 = (f32[1024,128]{1,0:T(8,128)}, f32[128,512]{1,0:T(8,128)}, f32[512,128]{1,0:T(8,128)}) custom-call(bf16[2048,128]{1,0:T(8,128)(2,1)S(1)} %weight_gradients.1.mine_ref, bf16[2048,128]{1,0:T(8,128)(2,1)S(1)} %collective-permute-done.14.other_ref), custom_call_target="tpu_custom_call" | custom-call | tf_op jit(solution)/shard_map/sums_over_depth/pallas_call | solution.py:940
  39.4 0.2 collective-permute-done.13
  39.6 0.6 %slice_bitcast_fusion = (f32[256,32]{0,1:T(8,128)}, f32[256,32]{0,1:T(8,128)}) fusion(f32[64,256]{1,0:T(8,128)S(1)} %convert_add_fusion), kind=kLoop, calls=%fused_computation.3 | loop fusion | bytes 131072 | tf_op jit(solution)/shard_map/transpose | solution.py:965
  (5 shorter events, 0.1 us)
Async XLA Ops:
  2.6 7.4 %collective-permute-start.2 = (bf16[1,272,128]{2,1,0:T(8,128)(2,1)S(1)}, bf16[1,272,128]{2,1,0:T(8,128)(2,1)S(1)}, u32[]{:S(2)}, u32[]{:S(2)}) collective-permute-start(bf16[1,272,128]{2,1,0:T(8,128)(2,1)S(1)} %get-tuple-element.56), channel_id=1, source_target_pairs={{0,2},{1,3},{2,0},{3,1},{4,6},{5,7},{6,4},{7,5},{8,10},{9,11},{10,... | collective-permute-start | bytes 208904 | tf_op jit(solution)/shard_map/ppermute | solution.py:740
  5.7 7.5 %collective-permute-start.1 = (bf16[1,272,128]{2,1,0:T(8,128)(2,1)S(1)}, bf16[1,272,128]{2,1,0:T(8,128)(2,1)S(1)}, u32[]{:S(2)}, u32[]{:S(2)}) collective-permute-start(bf16[1,272,128]{2,1,0:T(8,128)(2,1)S(1)} %get-tuple-element.56), channel_id=1, source_target_pairs={{0,4},{1,5},{2,6},{3,7},{4,0},{5,1},{6,2},{7,3},{8,12},{9,13},{10,... | collective-permute-start | bytes 208904 | tf_op jit(solution)/shard_map/ppermute | solution.py:740
  8.3 6.2 %collective-permute-start = (bf16[1,272,128]{2,1,0:T(8,128)(2,1)S(1)}, bf16[1,272,128]{2,1,0:T(8,128)(2,1)S(1)}, u32[]{:S(2)}, u32[]{:S(2)}) collective-permute-start(bf16[1,272,128]{2,1,0:T(8,128)(2,1)S(1)} %get-tuple-element.56), channel_id=1, source_target_pairs={{0,6},{1,7},{2,4},{3,5},{4,2},{5,3},{6,0},{7,1},{8,14},{9,15},{10,... | collective-permute-start | bytes 208904 | tf_op jit(solution)/shard_map/ppermute | solution.py:740
  8.3 6.3 %collective-permute-start.3 = (bf16[256,256]{1,0:T(8,128)(2,1)S(1)}, bf16[256,256]{1,0:T(8,128)(2,1)S(1)}, u32[]{:S(2)}, u32[]{:S(2)}) collective-permute-start(bf16[256,256]{1,0:T(8,128)(2,1)S(1)} %get-tuple-element.62.normed_ref), channel_id=1, source_target_pairs={{0,1},{1,0},{2,3},{3,2},{4,5},{5,4},{6,7},{7,6},{8,9},{9,8},{10,11... | collective-permute-start | bytes 393224 | tf_op jit(solution)/shard_map/ppermute | solution.py:740
  14.6 5.3 %copy-start = (bf16[1024,128]{1,0:T(8,128)(2,1)S(1)}, bf16[1024,128]{1,0:T(8,128)(2,1)}, u32[]{:S(2)}) copy-start(bf16[1024,128]{1,0:T(8,128)(2,1)} %wout_ref.1) | copy-start | bytes 786436
  14.6 5.2 %collective-permute-start.5 = (bf16[4,144,128]{2,1,0:T(8,128)(2,1)S(1)}, bf16[4,144,128]{2,1,0:T(8,128)(2,1)S(1)}, u32[]{:S(2)}, u32[]{:S(2)}) collective-permute-start(bf16[4,144,128]{2,1,0:T(8,128)(2,1)S(1)} %slice.13.near_ref), channel_id=1, source_target_pairs={{0,1},{1,0},{2,3},{3,2},{4,5},{5,4},{6,7},{7,6},{8,9},{9,8},{10,11... | collective-permute-start | bytes 442376 | tf_op jit(solution)/shard_map/ppermute | solution.py:740
  16.2 5.3 %collective-permute-start.6 = (bf16[4,144,128]{2,1,0:T(8,128)(2,1)S(1)}, bf16[4,144,128]{2,1,0:T(8,128)(2,1)S(1)}, u32[]{:S(2)}, u32[]{:S(2)}) collective-permute-start(bf16[4,144,128]{2,1,0:T(8,128)(2,1)S(1)} %slice.13.near_ref), channel_id=1, source_target_pairs={{0,8},{8,0},{1,9},{9,1},{2,10},{10,2},{3,11},{11,3},{4,12},{12,4},... | collective-permute-start | bytes 442376 | tf_op jit(solution)/shard_map/ppermute | solution.py:729
  19.8 1.7 %collective-permute-start.7 = (bf16[4,144,128]{2,1,0:T(8,128)(2,1)S(1)}, bf16[4,144,128]{2,1,0:T(8,128)(2,1)S(1)}, u32[]{:S(2)}, u32[]{:S(2)}) collective-permute-start(bf16[4,144,128]{2,1,0:T(8,128)(2,1)S(1)} %collective-permute-done.5.far_ref), channel_id=1, source_target_pairs={{0,8},{8,0},{1,9},{9,1},{2,10},{10,2},{3,11},{11,3},{4,12},{12,4},... | collective-permute-start | bytes 442376 | tf_op jit(solution)/shard_map/ppermute | solution.py:729
  19.9 6.0 %collective-permute-start.4 = (bf16[4,128,128]{2,1,0:T(8,128)(2,1)S(1)}, bf16[4,128,128]{2,1,0:T(8,128)(2,1)S(1)}, u32[]{:S(2)}, u32[]{:S(2)}) collective-permute-start(bf16[4,128,128]{2,1,0:T(8,128)(2,1)S(1)} %slice.12.near_ref), channel_id=1, source_target_pairs={{0,1},{1,0},{2,3},{3,2},{4,5},{5,4},{6,7},{7,6},{8,9},{9,8},{10,11... | collective-permute-start | bytes 393224 | tf_op jit(solution)/shard_map/ppermute | solution.py:740
  21.5 4.4 %copy-start.1 = (bf16[128,512]{1,0:T(8,128)(2,1)S(1)}, bf16[128,512]{1,0:T(8,128)(2,1)}, u32[]{:S(2)}) copy-start(bf16[128,512]{1,0:T(8,128)(2,1)} %hid_ref.1) | copy-start | bytes 393220
  21.5 4.4 %copy-start.2 = (bf16[512,128]{1,0:T(8,128)(2,1)S(1)}, bf16[512,128]{1,0:T(8,128)(2,1)}, u32[]{:S(2)}) copy-start(bf16[512,128]{1,0:T(8,128)(2,1)} %back_ref.1) | copy-start | bytes 393220
  24.2 1.7 %collective-permute-start.8 = (bf16[256,256]{1,0:T(8,128)(2,1)S(1)}, bf16[256,256]{1,0:T(8,128)(2,1)S(1)}, u32[]{:S(2)}, u32[]{:S(2)}) collective-permute-start(bf16[256,256]{1,0:T(8,128)(2,1)S(1)} %get-tuple-element.62.normed_ref), channel_id=1, source_target_pairs={{0,8},{8,0},{1,9},{9,1},{2,10},{10,2},{3,11},{11,3},{4,12},{12,4},... | collective-permute-start | bytes 393224 | tf_op jit(solution)/shard_map/ppermute | solution.py:729
  24.5 1.4 %collective-permute-start.9 = (bf16[256,256]{1,0:T(8,128)(2,1)S(1)}, bf16[256,256]{1,0:T(8,128)(2,1)S(1)}, u32[]{:S(2)}, u32[]{:S(2)}) collective-permute-start(bf16[256,256]{1,0:T(8,128)(2,1)S(1)} %collective-permute-done.3.far_normed_ref), channel_id=1, source_target_pairs={{0,8},{8,0},{1,9},{9,1},{2,10},{10,2},{3,11},{11,3},{4,12},{12,4},... | collective-permute-start | bytes 393224 | tf_op jit(solution)/shard_map/ppermute | solution.py:729
  27.8 1.4 %collective-permute-start.10 = (bf16[512,128]{1,0:T(8,128)(2,1)S(1)}, bf16[512,128]{1,0:T(8,128)(2,1)S(1)}, u32[]{:S(2)}, u32[]{:S(2)}) collective-permute-start(bf16[512,128]{1,0:T(8,128)(2,1)S(1)} %get-tuple-element.69.opm_ref), channel_id=1, source_target_pairs={{0,8},{8,0},{1,9},{9,1},{2,10},{10,2},{3,11},{11,3},{4,12},{12,4},... | collective-permute-start | bytes 393224 | tf_op jit(solution)/shard_map/ppermute | solution.py:729
  31.2 7.2 %collective-permute-start.14 = (bf16[2048,128]{1,0:T(8,128)(2,1)S(1)}, bf16[2048,128]{1,0:T(8,128)(2,1)S(1)}, u32[]{:S(2)}, u32[]{:S(2)}) collective-permute-start(bf16[2048,128]{1,0:T(8,128)(2,1)S(1)} %weight_gradients.1.mine_ref), channel_id=1, source_target_pairs={{0,8},{8,0},{1,9},{9,1},{2,10},{10,2},{3,11},{11,3},{4,12},{12,4},... | collective-permute-start | bytes 1572872 | tf_op jit(solution)/shard_map/ppermute | solution.py:729
  31.5 4.8 %collective-permute-start.12 = (bf16[64,256]{1,0:T(8,128)(2,1)S(1)}, bf16[64,256]{1,0:T(8,128)(2,1)S(1)}, u32[]{:S(2)}, u32[]{:S(2)}) collective-permute-start(bf16[64,256]{1,0:T(8,128)(2,1)S(1)} %get-tuple-element.83), channel_id=1, source_target_pairs={{8,10},{9,11},{10,8},{11,9},{12,14},{13,15},{14,12},{15,13},{24,26... | collective-permute-start | bytes 98312 | tf_op jit(solution)/shard_map/ppermute | solution.py:725
  32.2 6.1 %collective-permute-start.11 = (bf16[64,256]{1,0:T(8,128)(2,1)S(1)}, bf16[64,256]{1,0:T(8,128)(2,1)S(1)}, u32[]{:S(2)}, u32[]{:S(2)}) collective-permute-start(bf16[64,256]{1,0:T(8,128)(2,1)S(1)} %get-tuple-element.83), channel_id=1, source_target_pairs={{0,6},{1,7},{2,4},{3,5},{4,2},{5,3},{6,0},{7,1},{8,12},{9,13},{10,... | collective-permute-start | bytes 98312 | tf_op jit(solution)/shard_map/ppermute | solution.py:725
  38.3 1.3 %collective-permute-start.13 = (bf16[64,256]{1,0:T(8,128)(2,1)S(1)}, bf16[64,256]{1,0:T(8,128)(2,1)S(1)}, u32[]{:S(2)}, u32[]{:S(2)}) collective-permute-start(bf16[64,256]{1,0:T(8,128)(2,1)S(1)} %add_convert_fusion), channel_id=1, source_target_pairs={{0,8},{8,0},{1,9},{9,1},{2,10},{10,2},{3,11},{11,3},{4,12},{12,4},... | collective-permute-start | bytes 98312 | tf_op jit(solution)/shard_map/ppermute | solution.py:729

commit v17 on v16

--- a/solution.py
+++ b/solution.py
@@ -245,7 +245,7 @@
 
 FEW_RESIDUES = 32
 MASK_ROWS = 16
-Z_PARTNERS = (6, 4, 2)
+Z_PARTNERS = (2, 4, 6)
 Y_PARTNER = 1
 
 
@@ -369,8 +369,7 @@
 
 def by_owner(ids_ref, z, near_ref, far_ref):
     step = z ^ (ids_ref[1] // 2)
-    place = (near_ref.shape[0] - step) % near_ref.shape[0]
-    near, far = near_ref[place], far_ref[place]
+    near, far = near_ref[step], far_ref[step]
     first = ids_ref[1] % 2 == 0
     return jnp.where(first, near, far), jnp.where(first, far, near)
 
@@ -949,10 +948,10 @@
         compiler_params=params,
         name="sums_over_depth",
     )(weights, swap_depth(weights))
-    came_a = swap_line(part, Z_PARTNERS[:2])
-    came_b = swap_line(part, (None, Z_PARTNERS[2]))
+    came_b = swap_line(part, (None, Z_PARTNERS[0]))
+    came_a = swap_line(part, (Z_PARTNERS[2], Z_PARTNERS[1]))
     feat = feat.reshape(seqs, res, channels)
-    came_a, came_b, feat, couple = lax.optimization_barrier((came_a, came_b, feat, couple))
+    came_b, came_a, feat, couple = lax.optimization_barrier((came_b, came_a, feat, couple))
     kept = jnp.where(lax.axis_index("depth") == 0, part, came_b)
     kept = lax.optimization_barrier((kept.astype(f32) + came_a.astype(f32)).astype(bf16))
     came = swap_depth(kept)

time: 40.5 us -> 39.8 us (0.983)
  waiting for transfers between devices: 11.6 us -> 9.19 us
  starting transfers between devices: 15.1 us -> 16.8 us
    ppermute x2, waiting for transfers between devices: 2.02 us -> 0.56 us  [swap_line(): return lax.ppermute(block, ('depth', 'col'), pairs)]
    ppermute x7, starting transfers between devices: 1.24 us -> 2.34 us  [swap_depth(): return lax.ppermute(block, 'depth', [(0, 1), (1, 0)])]
    ppermute x6, waiting for transfers between devices: 9.19 us -> 8.32 us  [swap_col(): lax.ppermute(block, 'col', [(at, at ^ partner) for at in range(count)])]
where the time goes in v17:
time: 39.8 us; the launch traced here: 39.5 us
  starting transfers between devices  16.8 us (42%)
  Pallas kernels  11.2 us (28%)
  waiting for transfers between devices  9.19 us (23%)
  local copies, waits for them, and re-layouts  1.46 us (4%)
  between operations  0.76 us (2%)
    ppermute x6, starting transfers between devices, swap_col(): lax.ppermute(block, 'col', [(at, at ^ partner) for at in range(count)])  10.8 us
    ppermute x6, waiting for transfers between devices, swap_col(): lax.ppermute(block, 'col', [(at, at ^ partner) for at in range(count)])  8.32 us
    ppermute x2, starting transfers between devices, swap_line(): return lax.ppermute(block, ('depth', 'col'), pairs)  3.61 us
    pallas_call x1, Pallas kernels, whole_plan(): pl.pallas_call(functools.partial(outer_kernel, sizes), out_shape=(shape((...  2.67 us
    ppermute x7, starting transfers between devices, swap_depth(): return lax.ppermute(block, 'depth', [(0, 1), (1, 0)])  2.34 us
    pallas_call x1, Pallas kernels, whole_plan(): pl.pallas_call(functools.partial(projector_kernel, sizes), out_shape=(sha...  2.05 us
    pallas_call x1, Pallas kernels, whole_plan(): pl.pallas_call(pre_kernel, out_shape=(shape((1, rows + 2 * per, pair_widt...  1.91 us
    pallas_call x1, Pallas kernels, whole_plan(): pl.pallas_call(functools.partial(transition_kernel, sizes), out_shape=(sh...  1.81 us
  transfers between devices with their start and end apart: 15, of which 7 were waited for; matrix products, arithmetic and copies ran while one was open for 2% of the time, Pallas kernels for 14%

profile of v17, /device:TPU:0, one launch (start us, length us, event | category | flops | bytes accessed | tf_op | source)
XLA Modules:
  0.0 39.5 jit_solution(5573211869475923680)
XLA Ops:
  0.6 0.1 pad_add_fusion.ids_ref
  0.7 1.9 %project.1 = (bf16[1,272,128]{2,1,0:T(8,128)(2,1)S(1)}, f32[1,256]{1,0:T(1,128)S(1)}, bf16[32,256]{1,0:T(8,128)(2,1)S(1)}, bf16[32,256]{1,0:T(8,128)(2,1)S(1)}, ...) custom-call(s32[2]{0:T(128)S(1)} %pad_add_fusion.ids_ref, ...), custom_call_target="tpu_custom_call" | custom-call | tf_op jit(solution)/shard_map/project/pallas_call | solution.py:779
  2.6 5.1 %collective-permute-start.2 = (bf16[1,272,128]{2,1,0:T(8,128)(2,1)S(1)}, bf16[1,272,128]{2,1,0:T(8,128)(2,1)S(1)}, u32[]{:S(2)}, u32[]{:S(2)}) collective-permute-start(bf16[1,272,128]{2,1,0:T(8,128)(2,1)S(1)} %get-tuple-element.56), channel_id=1, source_target_pairs={{0,6},{1,7},{2,4},{3,5},{4,2},{5,3},{6,0},{7,1},{8,14},{9,15},{10,... | collective-permute-start | bytes 208904 | tf_op jit(solution)/shard_map/ppermute | solution.py:739
  7.7 0.0 collective-permute-start.1
  7.8 0.6 %collective-permute-start = (bf16[1,272,128]{2,1,0:T(8,128)(2,1)S(1)}, bf16[1,272,128]{2,1,0:T(8,128)(2,1)S(1)}, u32[]{:S(2)}, u32[]{:S(2)}) collective-permute-start(bf16[1,272,128]{2,1,0:T(8,128)(2,1)S(1)} %get-tuple-element.56), channel_id=1, source_target_pairs={{0,2},{1,3},{2,0},{3,1},{4,6},{5,7},{6,4},{7,5},{8,10},{9,11},{10,... | collective-permute-start | bytes 208904 | tf_op jit(solution)/shard_map/ppermute | solution.py:739
  8.4 1.7 %collective-permute-start.3 = (bf16[256,256]{1,0:T(8,128)(2,1)S(1)}, bf16[256,256]{1,0:T(8,128)(2,1)S(1)}, u32[]{:S(2)}, u32[]{:S(2)}) collective-permute-start(bf16[256,256]{1,0:T(8,128)(2,1)S(1)} %get-tuple-element.62.normed_ref), channel_id=1, source_target_pairs={{0,1},{1,0},{2,3},{3,2},{4,5},{5,4},{6,7},{7,6},{8,9},{9,8},{10,11... | collective-permute-start | bytes 393224 | tf_op jit(solution)/shard_map/ppermute | solution.py:739
  10.1 0.4 collective-permute-done.2
  10.4 3.2 %collective-permute-done.1 = bf16[1,272,128]{2,1,0:T(8,128)(2,1)S(1)} collective-permute-done((bf16[1,272,128]{2,1,0:T(8,128)(2,1)S(1)}, bf16[1,272,128]{2,1,0:T(8,128)(2,1)S(1)}, u32[]{:S(2)}, u32[]{:S(2)}) %collective-permute-start.1) | collective-permute-done | bytes 69664 | tf_op jit(solution)/shard_map/ppermute | solution.py:739
  13.7 0.0 collective-permute-done
  13.7 0.0 copy-start
  13.7 0.0 collective-permute-done.3.far_normed_ref
  13.7 1.6 %collective-permute-start.5 = (bf16[4,144,128]{2,1,0:T(8,128)(2,1)S(1)}, bf16[4,144,128]{2,1,0:T(8,128)(2,1)S(1)}, u32[]{:S(2)}, u32[]{:S(2)}) collective-permute-start(bf16[4,144,128]{2,1,0:T(8,128)(2,1)S(1)} %slice.13.near_ref), channel_id=1, source_target_pairs={{0,1},{1,0},{2,3},{3,2},{4,5},{5,4},{6,7},{7,6},{8,9},{9,8},{10,11... | collective-permute-start | bytes 442376 | tf_op jit(solution)/shard_map/ppermute | solution.py:739
  15.3 0.0 collective-permute-start.6
  15.3 3.8 %collective-permute-done.5.far_ref = bf16[4,144,128]{2,1,0:T(8,128)(2,1)S(1)} collective-permute-done((bf16[4,144,128]{2,1,0:T(8,128)(2,1)S(1)}, bf16[4,144,128]{2,1,0:T(8,128)(2,1)S(1)}, u32[]{:S(2)}, u32[]{:S(2)}) %collective-permute-start.5) | collective-permute-done | bytes 147488 | tf_op jit(solution)/shard_map/ppermute | solution.py:739
  19.2 0.0 collective-permute-start.7
  19.2 0.0 copy-done
  19.2 0.1 copy.19
  19.3 1.8 %collective-permute-start.4 = (bf16[4,128,128]{2,1,0:T(8,128)(2,1)S(1)}, bf16[4,128,128]{2,1,0:T(8,128)(2,1)S(1)}, u32[]{:S(2)}, u32[]{:S(2)}) collective-permute-start(bf16[4,128,128]{2,1,0:T(8,128)(2,1)S(1)} %slice.12.near_ref), channel_id=1, source_target_pairs={{0,1},{1,0},{2,3},{3,2},{4,5},{5,4},{6,7},{7,6},{8,9},{9,8},{10,11... | collective-permute-start | bytes 393224 | tf_op jit(solution)/shard_map/ppermute | solution.py:739
  21.1 0.0 collective-permute-done.6.other_near_ref
  21.1 0.0 collective-permute-done.7.other_far_ref
  21.1 0.0 copy-start.1
  21.1 0.0 copy-start.2
  21.1 2.7 %outer_products.1 = (bf16[512,1024]{1,0:T(8,128)(2,1)S(1)}, f32[512,128]{1,0:T(8,128)S(1)}, f32[512,128]{1,0:T(8,128)S(1)}, bf16[512,128]{1,0:T(8,128)(2,1)S(1)}...) custom-call(s32[2]{0:T(128)S(1)} %pad_add_fusion.ids_ref, ...), custom_call_target="tpu_custom_call" | custom-call | tf_op jit(solution)/shard_map/outer_products/pallas_call | solution.py:830
  23.8 0.3 collective-permute-start.8
  24.1 0.3 collective-permute-start.9
  24.4 0.9 %collective-permute-done.4.far_ref = bf16[4,128,128]{2,1,0:T(8,128)(2,1)S(1)} collective-permute-done((bf16[4,128,128]{2,1,0:T(8,128)(2,1)S(1)}, bf16[4,128,128]{2,1,0:T(8,128)(2,1)S(1)}, u32[]{:S(2)}, u32[]{:S(2)}) %collective-permute-start.4) | collective-permute-done | bytes 131104 | tf_op jit(solution)/shard_map/ppermute | solution.py:739
  25.3 0.0 collective-permute-done.8.other_normed_ref
  25.3 0.2 collective-permute-done.9.other_far_normed_ref
  25.4 0.0 copy-done.1
  25.4 0.0 copy-done.2
  25.4 1.8 %transition.1 = (bf16[64,128]{1,0:T(8,128)(2,1)S(1)}, bf16[512,128]{1,0:T(8,128)(2,1)S(1)}, bf16[512,128]{1,0:T(8,128)(2,1)S(1)}, bf16[512,512]{1,0:T(8,128)(2,1...) custom-call(s32[2]{0:T(128)S(1)} %pad_add_fusion.ids_ref, bf16[4,128,128]{2,1,0:T(8,128)(2,1)S(1)} %slice.12.near_ref, ...), custom_call_target="tpu_custom_call" | custom-call | tf_op jit(solution)/shard_map/transition/pallas_call | solution.py:859
  27.2 0.4 collective-permute-start.10
  27.6 0.9 %weight_gradients.1.mine_ref = bf16[2048,128]{1,0:T(8,128)(2,1)S(1)} custom-call(bf16[512,1024]{1,0:T(8,128)(2,1)S(1)} %get-tuple-element.70.outer_ref, bf16[512,128]{1,0:T(8,128)(2,1)S(1)} %get-tuple-element.69.opm_ref, bf16[512,128]{1,0:T(8,128)(2,1)S(1)} %get-tuple-element.71.pn_ref, bf16[512,512]{1,0:T(8,128)(2,1)S(1)} %get-tuple-element.72.gh_ref, ...), custom_call_target="tpu_custom_call" | custom-call | tf_op jit(solution)/shard_map/weight_gradients/pallas_call | solution.py:887
  28.5 0.1 collective-permute-done.10.other_opm_ref
  28.7 2.0 %projector_parts.1 = (bf16[64,256]{1,0:T(8,128)(2,1)S(1)}, bf16[256,256]{1,0:T(8,128)(2,1)S(1)}) custom-call(s32[2]{0:T(128)S(1)} %pad_add_fusion.ids_ref, bf16[512,128]{1,0:T(8,128)(2,1)S(1)} %get-tuple-element.69.opm_ref, bf16[512,128]{1,0:T(8,128)(2,1)S(1)} %collective-permute-done.10.other_opm_ref, bf16[1024,128]{1,0:T(8,128)(2,1)S(1)} %get-tuple-element.76.rightt_ref, ...), custom_call_target="tpu_custom_call" | custom-call | tf_op jit(solution)/shard_map/projector_parts/pallas_call | solution.py:897
  30.7 0.4 collective-permute-start.14
  31.1 3.0 %collective-permute-start.12 = (bf16[64,256]{1,0:T(8,128)(2,1)S(1)}, bf16[64,256]{1,0:T(8,128)(2,1)S(1)}, u32[]{:S(2)}, u32[]{:S(2)}) collective-permute-start(bf16[64,256]{1,0:T(8,128)(2,1)S(1)} %get-tuple-element.83), channel_id=1, source_target_pairs={{0,6},{1,7},{2,4},{3,5},{4,2},{5,3},{6,0},{7,1},{8,12},{9,13},{10,... | collective-permute-start | bytes 98312 | tf_op jit(solution)/shard_map/ppermute | solution.py:724
  34.0 0.7 %collective-permute-start.11 = (bf16[64,256]{1,0:T(8,128)(2,1)S(1)}, bf16[64,256]{1,0:T(8,128)(2,1)S(1)}, u32[]{:S(2)}, u32[]{:S(2)}) collective-permute-start(bf16[64,256]{1,0:T(8,128)(2,1)S(1)} %get-tuple-element.83), channel_id=1, source_target_pairs={{8,10},{9,11},{10,8},{11,9},{12,14},{13,15},{14,12},{15,13},{24,26... | collective-permute-start | bytes 98312 | tf_op jit(solution)/shard_map/ppermute | solution.py:724
  34.7 0.8 %features.1 = (bf16[256,256]{1,0:T(8,128)(2,1)S(1)}, bf16[64,128]{1,0:T(8,128)(2,1)}) custom-call(bf16[256,256]{1,0:T(8,128)(2,1)S(1)} %get-tuple-element.84.spread_ref, bf16[32,256]{1,0:T(8,128)(2,1)S(1)} %get-tuple-element.85.first_ref, bf16[32,256]{1,0:T(8,128)(2,1)S(1)} %get-tuple-element.86.second_ref, f32[1,256]{1,0:T(1,128)S(1)} %get-tuple-element.87.scale_ref, ...), custom_call_target="tpu_custom_call" | custom-call | tf_op jit(solution)/shard_map/features/pallas_call | solution.py:930
  35.5 0.7 %reshape.44 = bf16[64,4,256]{2,1,0:T(4,128)(2,1)} reshape(bf16[256,256]{1,0:T(8,128)(2,1)S(1)} %get-tuple-element.91) | data formatting | bytes 262144 | tf_op jit(solution)/shard_map/reshape | solution.py:953
  36.2 0.6 %collective-permute-done.12 = bf16[64,256]{1,0:T(8,128)(2,1)S(1)} collective-permute-done((bf16[64,256]{1,0:T(8,128)(2,1)S(1)}, bf16[64,256]{1,0:T(8,128)(2,1)S(1)}, u32[]{:S(2)}, u32[]{:S(2)}) %collective-permute-start.12) | collective-permute-done | bytes 32800 | tf_op jit(solution)/shard_map/ppermute | solution.py:724
  36.8 0.0 collective-permute-done.11
  36.8 1.0 %collective-permute-start.13 = (bf16[64,256]{1,0:T(8,128)(2,1)S(1)}, bf16[64,256]{1,0:T(8,128)(2,1)S(1)}, u32[]{:S(2)}, u32[]{:S(2)}) collective-permute-start(bf16[64,256]{1,0:T(8,128)(2,1)S(1)} %add_convert_fusion), channel_id=1, source_target_pairs={{0,8},{8,0},{1,9},{9,1},{2,10},{10,2},{3,11},{11,3},{4,12},{12,4},... | collective-permute-start | bytes 98312 | tf_op jit(solution)/shard_map/ppermute | solution.py:728
  37.9 0.0 collective-permute-done.14.other_ref
  37.9 1.0 %sums_over_depth.1 = (f32[1024,128]{1,0:T(8,128)}, f32[128,512]{1,0:T(8,128)}, f32[512,128]{1,0:T(8,128)}) custom-call(bf16[2048,128]{1,0:T(8,128)(2,1)S(1)} %weight_gradients.1.mine_ref, bf16[2048,128]{1,0:T(8,128)(2,1)S(1)} %collective-permute-done.14.other_ref), custom_call_target="tpu_custom_call" | custom-call | tf_op jit(solution)/shard_map/sums_over_depth/pallas_call | solution.py:939
  38.9 0.0 collective-permute-done.13
  38.9 0.6 %slice_bitcast_fusion = (f32[256,32]{0,1:T(8,128)}, f32[256,32]{0,1:T(8,128)}) fusion(f32[64,256]{1,0:T(8,128)S(1)} %convert_add_fusion), kind=kLoop, calls=%fused_computation.3 | loop fusion | bytes 131072 | tf_op jit(solution)/shard_map/transpose | solution.py:964
  (5 shorter events, 0.1 us)
Async XLA Ops:
  2.6 7.8 %collective-permute-start.2 = (bf16[1,272,128]{2,1,0:T(8,128)(2,1)S(1)}, bf16[1,272,128]{2,1,0:T(8,128)(2,1)S(1)}, u32[]{:S(2)}, u32[]{:S(2)}) collective-permute-start(bf16[1,272,128]{2,1,0:T(8,128)(2,1)S(1)} %get-tuple-element.56), channel_id=1, source_target_pairs={{0,6},{1,7},{2,4},{3,5},{4,2},{5,3},{6,0},{7,1},{8,14},{9,15},{10,... | collective-permute-start | bytes 208904 | tf_op jit(solution)/shard_map/ppermute | solution.py:739
  7.7 5.9 %collective-permute-start.1 = (bf16[1,272,128]{2,1,0:T(8,128)(2,1)S(1)}, bf16[1,272,128]{2,1,0:T(8,128)(2,1)S(1)}, u32[]{:S(2)}, u32[]{:S(2)}) collective-permute-start(bf16[1,272,128]{2,1,0:T(8,128)(2,1)S(1)} %get-tuple-element.56), channel_id=1, source_target_pairs={{0,4},{1,5},{2,6},{3,7},{4,0},{5,1},{6,2},{7,3},{8,12},{9,13},{10,... | collective-permute-start | bytes 208904 | tf_op jit(solution)/shard_map/ppermute | solution.py:739
  7.8 5.9 %collective-permute-start = (bf16[1,272,128]{2,1,0:T(8,128)(2,1)S(1)}, bf16[1,272,128]{2,1,0:T(8,128)(2,1)S(1)}, u32[]{:S(2)}, u32[]{:S(2)}) collective-permute-start(bf16[1,272,128]{2,1,0:T(8,128)(2,1)S(1)} %get-tuple-element.56), channel_id=1, source_target_pairs={{0,2},{1,3},{2,0},{3,1},{4,6},{5,7},{6,4},{7,5},{8,10},{9,11},{10,... | collective-permute-start | bytes 208904 | tf_op jit(solution)/shard_map/ppermute | solution.py:739
  8.4 5.3 %collective-permute-start.3 = (bf16[256,256]{1,0:T(8,128)(2,1)S(1)}, bf16[256,256]{1,0:T(8,128)(2,1)S(1)}, u32[]{:S(2)}, u32[]{:S(2)}) collective-permute-start(bf16[256,256]{1,0:T(8,128)(2,1)S(1)} %get-tuple-element.62.normed_ref), channel_id=1, source_target_pairs={{0,1},{1,0},{2,3},{3,2},{4,5},{5,4},{6,7},{7,6},{8,9},{9,8},{10,11... | collective-permute-start | bytes 393224 | tf_op jit(solution)/shard_map/ppermute | solution.py:739
  13.7 5.5 %copy-start = (bf16[1024,128]{1,0:T(8,128)(2,1)S(1)}, bf16[1024,128]{1,0:T(8,128)(2,1)}, u32[]{:S(2)}) copy-start(bf16[1024,128]{1,0:T(8,128)(2,1)} %wout_ref.1) | copy-start | bytes 786436
  13.7 5.4 %collective-permute-start.5 = (bf16[4,144,128]{2,1,0:T(8,128)(2,1)S(1)}, bf16[4,144,128]{2,1,0:T(8,128)(2,1)S(1)}, u32[]{:S(2)}, u32[]{:S(2)}) collective-permute-start(bf16[4,144,128]{2,1,0:T(8,128)(2,1)S(1)} %slice.13.near_ref), channel_id=1, source_target_pairs={{0,1},{1,0},{2,3},{3,2},{4,5},{5,4},{6,7},{7,6},{8,9},{9,8},{10,11... | collective-permute-start | bytes 442376 | tf_op jit(solution)/shard_map/ppermute | solution.py:739
  15.3 5.8 %collective-permute-start.6 = (bf16[4,144,128]{2,1,0:T(8,128)(2,1)S(1)}, bf16[4,144,128]{2,1,0:T(8,128)(2,1)S(1)}, u32[]{:S(2)}, u32[]{:S(2)}) collective-permute-start(bf16[4,144,128]{2,1,0:T(8,128)(2,1)S(1)} %slice.13.near_ref), channel_id=1, source_target_pairs={{0,8},{8,0},{1,9},{9,1},{2,10},{10,2},{3,11},{11,3},{4,12},{12,4},... | collective-permute-start | bytes 442376 | tf_op jit(solution)/shard_map/ppermute | solution.py:728
  19.2 1.9 %collective-permute-start.7 = (bf16[4,144,128]{2,1,0:T(8,128)(2,1)S(1)}, bf16[4,144,128]{2,1,0:T(8,128)(2,1)S(1)}, u32[]{:S(2)}, u32[]{:S(2)}) collective-permute-start(bf16[4,144,128]{2,1,0:T(8,128)(2,1)S(1)} %collective-permute-done.5.far_ref), channel_id=1, source_target_pairs={{0,8},{8,0},{1,9},{9,1},{2,10},{10,2},{3,11},{11,3},{4,12},{12,4},... | collective-permute-start | bytes 442376 | tf_op jit(solution)/shard_map/ppermute | solution.py:728
  19.3 6.0 %collective-permute-start.4 = (bf16[4,128,128]{2,1,0:T(8,128)(2,1)S(1)}, bf16[4,128,128]{2,1,0:T(8,128)(2,1)S(1)}, u32[]{:S(2)}, u32[]{:S(2)}) collective-permute-start(bf16[4,128,128]{2,1,0:T(8,128)(2,1)S(1)} %slice.12.near_ref), channel_id=1, source_target_pairs={{0,1},{1,0},{2,3},{3,2},{4,5},{5,4},{6,7},{7,6},{8,9},{9,8},{10,11... | collective-permute-start | bytes 393224 | tf_op jit(solution)/shard_map/ppermute | solution.py:739
  21.1 4.3 %copy-start.1 = (bf16[128,512]{1,0:T(8,128)(2,1)S(1)}, bf16[128,512]{1,0:T(8,128)(2,1)}, u32[]{:S(2)}) copy-start(bf16[128,512]{1,0:T(8,128)(2,1)} %hid_ref.1) | copy-start | bytes 393220
  21.1 4.3 %copy-start.2 = (bf16[512,128]{1,0:T(8,128)(2,1)S(1)}, bf16[512,128]{1,0:T(8,128)(2,1)}, u32[]{:S(2)}) copy-start(bf16[512,128]{1,0:T(8,128)(2,1)} %back_ref.1) | copy-start | bytes 393220
  23.8 1.5 %collective-permute-start.8 = (bf16[256,256]{1,0:T(8,128)(2,1)S(1)}, bf16[256,256]{1,0:T(8,128)(2,1)S(1)}, u32[]{:S(2)}, u32[]{:S(2)}) collective-permute-start(bf16[256,256]{1,0:T(8,128)(2,1)S(1)} %get-tuple-element.62.normed_ref), channel_id=1, source_target_pairs={{0,8},{8,0},{1,9},{9,1},{2,10},{10,2},{3,11},{11,3},{4,12},{12,4},... | collective-permute-start | bytes 393224 | tf_op jit(solution)/shard_map/ppermute | solution.py:728
  24.1 1.3 %collective-permute-start.9 = (bf16[256,256]{1,0:T(8,128)(2,1)S(1)}, bf16[256,256]{1,0:T(8,128)(2,1)S(1)}, u32[]{:S(2)}, u32[]{:S(2)}) collective-permute-start(bf16[256,256]{1,0:T(8,128)(2,1)S(1)} %collective-permute-done.3.far_normed_ref), channel_id=1, source_target_pairs={{0,8},{8,0},{1,9},{9,1},{2,10},{10,2},{3,11},{11,3},{4,12},{12,4},... | collective-permute-start | bytes 393224 | tf_op jit(solution)/shard_map/ppermute | solution.py:728
  27.2 1.4 %collective-permute-start.10 = (bf16[512,128]{1,0:T(8,128)(2,1)S(1)}, bf16[512,128]{1,0:T(8,128)(2,1)S(1)}, u32[]{:S(2)}, u32[]{:S(2)}) collective-permute-start(bf16[512,128]{1,0:T(8,128)(2,1)S(1)} %get-tuple-element.69.opm_ref), channel_id=1, source_target_pairs={{0,8},{8,0},{1,9},{9,1},{2,10},{10,2},{3,11},{11,3},{4,12},{12,4},... | collective-permute-start | bytes 393224 | tf_op jit(solution)/shard_map/ppermute | solution.py:728
  30.7 7.1 %collective-permute-start.14 = (bf16[2048,128]{1,0:T(8,128)(2,1)S(1)}, bf16[2048,128]{1,0:T(8,128)(2,1)S(1)}, u32[]{:S(2)}, u32[]{:S(2)}) collective-permute-start(bf16[2048,128]{1,0:T(8,128)(2,1)S(1)} %weight_gradients.1.mine_ref), channel_id=1, source_target_pairs={{0,8},{8,0},{1,9},{9,1},{2,10},{10,2},{3,11},{11,3},{4,12},{12,4},... | collective-permute-start | bytes 1572872 | tf_op jit(solution)/shard_map/ppermute | solution.py:728
  31.1 5.7 %collective-permute-start.12 = (bf16[64,256]{1,0:T(8,128)(2,1)S(1)}, bf16[64,256]{1,0:T(8,128)(2,1)S(1)}, u32[]{:S(2)}, u32[]{:S(2)}) collective-permute-start(bf16[64,256]{1,0:T(8,128)(2,1)S(1)} %get-tuple-element.83), channel_id=1, source_target_pairs={{0,6},{1,7},{2,4},{3,5},{4,2},{5,3},{6,0},{7,1},{8,12},{9,13},{10,... | collective-permute-start | bytes 98312 | tf_op jit(solution)/shard_map/ppermute | solution.py:724
  34.0 2.8 %collective-permute-start.11 = (bf16[64,256]{1,0:T(8,128)(2,1)S(1)}, bf16[64,256]{1,0:T(8,128)(2,1)S(1)}, u32[]{:S(2)}, u32[]{:S(2)}) collective-permute-start(bf16[64,256]{1,0:T(8,128)(2,1)S(1)} %get-tuple-element.83), channel_id=1, source_target_pairs={{8,10},{9,11},{10,8},{11,9},{12,14},{13,15},{14,12},{15,13},{24,26... | collective-permute-start | bytes 98312 | tf_op jit(solution)/shard_map/ppermute | solution.py:724
  36.8 2.1 %collective-permute-start.13 = (bf16[64,256]{1,0:T(8,128)(2,1)S(1)}, bf16[64,256]{1,0:T(8,128)(2,1)S(1)}, u32[]{:S(2)}, u32[]{:S(2)}) collective-permute-start(bf16[64,256]{1,0:T(8,128)(2,1)S(1)} %add_convert_fusion), channel_id=1, source_target_pairs={{0,8},{8,0},{1,9},{9,1},{2,10},{10,2},{3,11},{11,3},{4,12},{12,4},... | collective-permute-start | bytes 98312 | tf_op jit(solution)/shard_map/ppermute | solution.py:728

commit v18 on v17

--- a/solution.py
+++ b/solution.py
@@ -674,23 +674,7 @@
     out_ref[outer_width + hid :, :] = contract(hidden_ref, mg_ref).astype(jnp.bfloat16)
 
 
-def weights_sum_kernel(mine_ref, other_ref, dout_ref, dhid_ref, dback_ref):
-    pair_width, hid = dhid_ref.shape
-    outer_width = dout_ref.shape[0]
-
-    def added(first, count):
-        rows = slice(first, first + count)
-        return mine_ref[rows, :].astype(jnp.float32) + other_ref[rows, :].astype(jnp.float32)
-
-    dout_ref[...] = added(0, outer_width)
-    for at in range(hid // pair_width):
-        dhid_ref[:, at * pair_width : (at + 1) * pair_width] = added(
-            outer_width + at * pair_width, pair_width
-        )
-    dback_ref[...] = added(outer_width + hid, hid)
-
-
-def feature_kernel(
+def finish_kernel(
     copies,
     spread_ref,
     first_ref,
@@ -699,18 +683,35 @@
     scaled_ref,
     inv_ref,
     held_ref,
+    mine_ref,
+    other_ref,
     feat_ref,
     couple_ref,
+    dout_ref,
+    dhid_ref,
+    dback_ref,
 ):
     back = jnp.dot(
         spread_ref[...],
         wide_projector(first_ref, second_ref, copies),
         preferred_element_type=jnp.float32,
     )
-    feat_ref[...] = standardize_adjoint(
-        back * scale_ref[...], scaled_ref[...], inv_ref[...]
-    ).astype(jnp.bfloat16)
+    feat = standardize_adjoint(back * scale_ref[...], scaled_ref[...], inv_ref[...])
+    feat_ref[...] = feat.reshape(feat_ref.shape).astype(jnp.bfloat16)
     couple_ref[...] = held_ref[...]
+    pair_width, hid = dhid_ref.shape
+    outer_width = dout_ref.shape[0]
+
+    def added(first, count):
+        rows = slice(first, first + count)
+        return mine_ref[rows, :].astype(jnp.float32) + other_ref[rows, :].astype(jnp.float32)
+
+    dout_ref[...] = added(0, outer_width)
+    for at in range(hid // pair_width):
+        dhid_ref[:, at * pair_width : (at + 1) * pair_width] = added(
+            outer_width + at * pair_width, pair_width
+        )
+    dback_ref[...] = added(outer_width + hid, hid)
 
 
 def swap_line(block, partners):
@@ -927,35 +928,30 @@
         other_normed,
         other_far_normed,
     )
-    feat, couple = pl.pallas_call(
-        functools.partial(feature_kernel, res),
-        out_shape=(shape((seqs * res, channels), bf16), shape((per, pair_width), bf16)),
-        in_specs=[vmem] * 7,
-        out_specs=[vmem] * 2,
-        compiler_params=params,
-        name="features",
-    )(spread, first, second, scale, scaled, inv, held)
     part, weights = lax.optimization_barrier((part, weights))
-    dout, dhid, dback = pl.pallas_call(
-        weights_sum_kernel,
+    feat, couple, dout, dhid, dback = pl.pallas_call(
+        functools.partial(finish_kernel, res),
         out_shape=(
+            shape((seqs, res, channels), bf16),
+            shape((per, pair_width), bf16),
             shape((outer_width, pair_width), f32),
             shape((pair_width, hid), f32),
             shape((hid, pair_width), f32),
         ),
-        in_specs=[vmem] * 2,
-        out_specs=[vmem] * 3,
+        in_specs=[vmem] * 9,
+        out_specs=[vmem] * 5,
         compiler_params=params,
-        name="sums_over_depth",
-    )(weights, swap_depth(weights))
+        name="finish",
+    )(spread, first, second, scale, scaled, inv, held, weights, swap_depth(weights))
     came_b = swap_line(part, (None, Z_PARTNERS[0]))
     came_a = swap_line(part, (Z_PARTNERS[2], Z_PARTNERS[1]))
-    feat = feat.reshape(seqs, res, channels)
-    came_b, came_a, feat, couple = lax.optimization_barrier((came_b, came_a, feat, couple))
+    came_b, came_a = lax.optimization_barrier((came_b, came_a))
     kept = jnp.where(lax.axis_index("depth") == 0, part, came_b)
     kept = lax.optimization_barrier((kept.astype(f32) + came_a.astype(f32)).astype(bf16))
     came = swap_depth(kept)
-    came, dout, dhid, dback = lax.optimization_barrier((came, dout, dhid, dback))
+    came, feat, couple, dout, dhid, dback = lax.optimization_barrier(
+        (came, feat, couple, dout, dhid, dback)
+    )
     total = kept.astype(f32) + came.astype(f32)
     return (
         feat,

time: 39.8 us -> 39.8 us (level)
  waiting for transfers between devices: 9.19 us -> 10.7 us
  local copies, waits for them, and re-layouts: 1.46 us -> 0.77 us
  Pallas kernels: 11.2 us -> 10.7 us
    ppermute x2, waiting for transfers between devices: 0.56 us -> 2.09 us  [swap_line(): return lax.ppermute(block, ('depth', 'col'), pairs)]
    reshape x1 -> x0, local copies, waits for them, and re-layouts: 0.69 us -> none  [whole_plan(): feat = feat.reshape(seqs, res, channels)]
    pallas_call x2 -> x1, Pallas kernels: 1.86 us -> 1.32 us  [whole_plan(): pl.pallas_call(functools.partial(finish_kernel, res), out_shape=(shape((s...]
  transfers between devices with their start and end apart: 15 -> 15, of which waited for: 7 -> 7; matrix products, arithmetic and copies ran while one was open for 2% -> 0% of each run, Pallas kernels for 14% -> 12%
where the time goes in v18:
time: 39.8 us; the launch traced here: 39.6 us
  starting transfers between devices  16.5 us (41%)
  Pallas kernels  10.7 us (27%)
  waiting for transfers between devices  10.7 us (27%)
  local copies, waits for them, and re-layouts  0.77 us (2%)
  between operations  0.76 us (2%)
    ppermute x6, starting transfers between devices, swap_col(): lax.ppermute(block, 'col', [(at, at ^ partner) for at in range(count)])  10.8 us
    ppermute x6, waiting for transfers between devices, swap_col(): lax.ppermute(block, 'col', [(at, at ^ partner) for at in range(count)])  8.32 us
    ppermute x2, starting transfers between devices, swap_line(): return lax.ppermute(block, ('depth', 'col'), pairs)  3.61 us
    pallas_call x1, Pallas kernels, whole_plan(): pl.pallas_call(functools.partial(outer_kernel, sizes), out_shape=(shape((...  2.67 us
    ppermute x2, waiting for transfers between devices, swap_line(): return lax.ppermute(block, ('depth', 'col'), pairs)  2.09 us
    ppermute x7, starting transfers between devices, swap_depth(): return lax.ppermute(block, 'depth', [(0, 1), (1, 0)])  2.07 us
    pallas_call x1, Pallas kernels, whole_plan(): pl.pallas_call(functools.partial(projector_kernel, sizes), out_shape=(sha...  2.05 us
    pallas_call x1, Pallas kernels, whole_plan(): pl.pallas_call(pre_kernel, out_shape=(shape((1, rows + 2 * per, pair_widt...  1.91 us
  transfers between devices with their start and end apart: 15, of which 7 were waited for; matrix products, arithmetic and copies ran while one was open for 0% of the time, Pallas kernels for 12%

profile of v18, /device:TPU:0, one launch (start us, length us, event | category | flops | bytes accessed | tf_op | source)
XLA Modules:
  0.0 39.6 jit_solution(2991054651454589792)
XLA Ops:
  0.6 0.1 pad_add_fusion.ids_ref
  0.7 1.9 %project.1 = (bf16[1,272,128]{2,1,0:T(8,128)(2,1)S(1)}, f32[1,256]{1,0:T(1,128)S(1)}, bf16[32,256]{1,0:T(8,128)(2,1)S(1)}, bf16[32,256]{1,0:T(8,128)(2,1)S(1)}, ...) custom-call(s32[2]{0:T(128)S(1)} %pad_add_fusion.ids_ref, ...), custom_call_target="tpu_custom_call" | custom-call | tf_op jit(solution)/shard_map/project/pallas_call | solution.py:780
  2.6 5.1 %collective-permute-start.2 = (bf16[1,272,128]{2,1,0:T(8,128)(2,1)S(1)}, bf16[1,272,128]{2,1,0:T(8,128)(2,1)S(1)}, u32[]{:S(2)}, u32[]{:S(2)}) collective-permute-start(bf16[1,272,128]{2,1,0:T(8,128)(2,1)S(1)} %get-tuple-element.56), channel_id=1, source_target_pairs={{0,6},{1,7},{2,4},{3,5},{4,2},{5,3},{6,0},{7,1},{8,14},{9,15},{10,... | collective-permute-start | bytes 208904 | tf_op jit(solution)/shard_map/ppermute | solution.py:740
  7.7 0.0 collective-permute-start.1
  7.8 0.6 %collective-permute-start = (bf16[1,272,128]{2,1,0:T(8,128)(2,1)S(1)}, bf16[1,272,128]{2,1,0:T(8,128)(2,1)S(1)}, u32[]{:S(2)}, u32[]{:S(2)}) collective-permute-start(bf16[1,272,128]{2,1,0:T(8,128)(2,1)S(1)} %get-tuple-element.56), channel_id=1, source_target_pairs={{0,2},{1,3},{2,0},{3,1},{4,6},{5,7},{6,4},{7,5},{8,10},{9,11},{10,... | collective-permute-start | bytes 208904 | tf_op jit(solution)/shard_map/ppermute | solution.py:740
  8.4 1.7 %collective-permute-start.3 = (bf16[256,256]{1,0:T(8,128)(2,1)S(1)}, bf16[256,256]{1,0:T(8,128)(2,1)S(1)}, u32[]{:S(2)}, u32[]{:S(2)}) collective-permute-start(bf16[256,256]{1,0:T(8,128)(2,1)S(1)} %get-tuple-element.62.normed_ref), channel_id=1, source_target_pairs={{0,1},{1,0},{2,3},{3,2},{4,5},{5,4},{6,7},{7,6},{8,9},{9,8},{10,11... | collective-permute-start | bytes 393224 | tf_op jit(solution)/shard_map/ppermute | solution.py:740
  10.1 0.4 collective-permute-done.2
  10.4 3.2 %collective-permute-done.1 = bf16[1,272,128]{2,1,0:T(8,128)(2,1)S(1)} collective-permute-done((bf16[1,272,128]{2,1,0:T(8,128)(2,1)S(1)}, bf16[1,272,128]{2,1,0:T(8,128)(2,1)S(1)}, u32[]{:S(2)}, u32[]{:S(2)}) %collective-permute-start.1) | collective-permute-done | bytes 69664 | tf_op jit(solution)/shard_map/ppermute | solution.py:740
  13.7 0.0 collective-permute-done
  13.7 0.0 copy-start
  13.7 0.0 collective-permute-done.3.far_normed_ref
  13.7 1.6 %collective-permute-start.5 = (bf16[4,144,128]{2,1,0:T(8,128)(2,1)S(1)}, bf16[4,144,128]{2,1,0:T(8,128)(2,1)S(1)}, u32[]{:S(2)}, u32[]{:S(2)}) collective-permute-start(bf16[4,144,128]{2,1,0:T(8,128)(2,1)S(1)} %slice.13.near_ref), channel_id=1, source_target_pairs={{0,1},{1,0},{2,3},{3,2},{4,5},{5,4},{6,7},{7,6},{8,9},{9,8},{10,11... | collective-permute-start | bytes 442376 | tf_op jit(solution)/shard_map/ppermute | solution.py:740
  15.3 0.0 collective-permute-start.6
  15.3 3.8 %collective-permute-done.5.far_ref = bf16[4,144,128]{2,1,0:T(8,128)(2,1)S(1)} collective-permute-done((bf16[4,144,128]{2,1,0:T(8,128)(2,1)S(1)}, bf16[4,144,128]{2,1,0:T(8,128)(2,1)S(1)}, u32[]{:S(2)}, u32[]{:S(2)}) %collective-permute-start.5) | collective-permute-done | bytes 147488 | tf_op jit(solution)/shard_map/ppermute | solution.py:740
  19.2 0.0 collective-permute-start.7
  19.2 0.0 copy-done
  19.2 0.1 copy.19
  19.3 1.8 %collective-permute-start.4 = (bf16[4,128,128]{2,1,0:T(8,128)(2,1)S(1)}, bf16[4,128,128]{2,1,0:T(8,128)(2,1)S(1)}, u32[]{:S(2)}, u32[]{:S(2)}) collective-permute-start(bf16[4,128,128]{2,1,0:T(8,128)(2,1)S(1)} %slice.12.near_ref), channel_id=1, source_target_pairs={{0,1},{1,0},{2,3},{3,2},{4,5},{5,4},{6,7},{7,6},{8,9},{9,8},{10,11... | collective-permute-start | bytes 393224 | tf_op jit(solution)/shard_map/ppermute | solution.py:740
  21.1 0.0 collective-permute-done.6.other_near_ref
  21.1 0.0 collective-permute-done.7.other_far_ref
  21.1 0.0 copy-start.1
  21.1 0.0 copy-start.2
  21.1 2.7 %outer_products.1 = (bf16[512,1024]{1,0:T(8,128)(2,1)S(1)}, f32[512,128]{1,0:T(8,128)S(1)}, f32[512,128]{1,0:T(8,128)S(1)}, bf16[512,128]{1,0:T(8,128)(2,1)S(1)}...) custom-call(s32[2]{0:T(128)S(1)} %pad_add_fusion.ids_ref, ...), custom_call_target="tpu_custom_call" | custom-call | tf_op jit(solution)/shard_map/outer_products/pallas_call | solution.py:831
  23.8 0.3 collective-permute-start.8
  24.1 0.3 collective-permute-start.9
  24.4 0.9 %collective-permute-done.4.far_ref = bf16[4,128,128]{2,1,0:T(8,128)(2,1)S(1)} collective-permute-done((bf16[4,128,128]{2,1,0:T(8,128)(2,1)S(1)}, bf16[4,128,128]{2,1,0:T(8,128)(2,1)S(1)}, u32[]{:S(2)}, u32[]{:S(2)}) %collective-permute-start.4) | collective-permute-done | bytes 131104 | tf_op jit(solution)/shard_map/ppermute | solution.py:740
  25.3 0.0 collective-permute-done.8.other_normed_ref
  25.3 0.2 collective-permute-done.9.other_far_normed_ref
  25.4 0.0 copy-done.1
  25.4 0.0 copy-done.2
  25.4 1.8 %transition.1 = (bf16[64,128]{1,0:T(8,128)(2,1)S(1)}, bf16[512,128]{1,0:T(8,128)(2,1)S(1)}, bf16[512,128]{1,0:T(8,128)(2,1)S(1)}, bf16[512,512]{1,0:T(8,128)(2,1...) custom-call(s32[2]{0:T(128)S(1)} %pad_add_fusion.ids_ref, bf16[4,128,128]{2,1,0:T(8,128)(2,1)S(1)} %slice.12.near_ref, ...), custom_call_target="tpu_custom_call" | custom-call | tf_op jit(solution)/shard_map/transition/pallas_call | solution.py:860
  27.2 0.4 collective-permute-start.10
  27.6 0.9 %weight_gradients.1.mine_ref = bf16[2048,128]{1,0:T(8,128)(2,1)S(1)} custom-call(bf16[512,1024]{1,0:T(8,128)(2,1)S(1)} %get-tuple-element.70.outer_ref, bf16[512,128]{1,0:T(8,128)(2,1)S(1)} %get-tuple-element.69.opm_ref, bf16[512,128]{1,0:T(8,128)(2,1)S(1)} %get-tuple-element.71.pn_ref, bf16[512,512]{1,0:T(8,128)(2,1)S(1)} %get-tuple-element.72.gh_ref, ...), custom_call_target="tpu_custom_call" | custom-call | tf_op jit(solution)/shard_map/weight_gradients/pallas_call | solution.py:888
  28.5 0.1 collective-permute-done.10.other_opm_ref
  28.7 2.0 %projector_parts.1 = (bf16[64,256]{1,0:T(8,128)(2,1)S(1)}, bf16[256,256]{1,0:T(8,128)(2,1)S(1)}) custom-call(s32[2]{0:T(128)S(1)} %pad_add_fusion.ids_ref, bf16[512,128]{1,0:T(8,128)(2,1)S(1)} %get-tuple-element.69.opm_ref, bf16[512,128]{1,0:T(8,128)(2,1)S(1)} %collective-permute-done.10.other_opm_ref, bf16[1024,128]{1,0:T(8,128)(2,1)S(1)} %get-tuple-element.76.rightt_ref, ...), custom_call_target="tpu_custom_call" | custom-call | tf_op jit(solution)/shard_map/projector_parts/pallas_call | solution.py:898
  30.7 0.4 collective-permute-start.14
  31.1 3.0 %collective-permute-start.12 = (bf16[64,256]{1,0:T(8,128)(2,1)S(1)}, bf16[64,256]{1,0:T(8,128)(2,1)S(1)}, u32[]{:S(2)}, u32[]{:S(2)}) collective-permute-start(bf16[64,256]{1,0:T(8,128)(2,1)S(1)} %get-tuple-element.83), channel_id=1, source_target_pairs={{0,6},{1,7},{2,4},{3,5},{4,2},{5,3},{6,0},{7,1},{8,12},{9,13},{10,... | collective-permute-start | bytes 98312 | tf_op jit(solution)/shard_map/ppermute | solution.py:725
  34.0 0.7 %collective-permute-start.11 = (bf16[64,256]{1,0:T(8,128)(2,1)S(1)}, bf16[64,256]{1,0:T(8,128)(2,1)S(1)}, u32[]{:S(2)}, u32[]{:S(2)}) collective-permute-start(bf16[64,256]{1,0:T(8,128)(2,1)S(1)} %get-tuple-element.83), channel_id=1, source_target_pairs={{8,10},{9,11},{10,8},{11,9},{12,14},{13,15},{14,12},{15,13},{24,26... | collective-permute-start | bytes 98312 | tf_op jit(solution)/shard_map/ppermute | solution.py:725
  34.7 2.1 %collective-permute-done.12 = bf16[64,256]{1,0:T(8,128)(2,1)S(1)} collective-permute-done((bf16[64,256]{1,0:T(8,128)(2,1)S(1)}, bf16[64,256]{1,0:T(8,128)(2,1)S(1)}, u32[]{:S(2)}, u32[]{:S(2)}) %collective-permute-start.12) | collective-permute-done | bytes 32800 | tf_op jit(solution)/shard_map/ppermute | solution.py:725
  36.8 0.0 collective-permute-done.11
  36.8 0.8 %collective-permute-start.13 = (bf16[64,256]{1,0:T(8,128)(2,1)S(1)}, bf16[64,256]{1,0:T(8,128)(2,1)S(1)}, u32[]{:S(2)}, u32[]{:S(2)}) collective-permute-start(bf16[64,256]{1,0:T(8,128)(2,1)S(1)} %add_convert_fusion), channel_id=1, source_target_pairs={{0,8},{8,0},{1,9},{9,1},{2,10},{10,2},{3,11},{11,3},{4,12},{12,4},... | collective-permute-start | bytes 98312 | tf_op jit(solution)/shard_map/ppermute | solution.py:729
  37.6 0.0 collective-permute-done.14.other_ref
  37.6 1.3 %finish.1 = (bf16[64,4,256]{2,1,0:T(4,128)(2,1)}, bf16[64,128]{1,0:T(8,128)(2,1)}, f32[1024,128]{1,0:T(8,128)}, f32[128,512]{1,0:T(8,128)}, f32[512,128]{1,0:T(8,128)}) custom-call(bf16[256,256]{1,0:T(8,128)(2,1)S(1)} %get-tuple-element.86.spread_ref, bf16[32,256]{1,0:T(8,128)(2,1)S(1)} %get-tuple-element.87.first_ref, ...), custom_call_target="tpu_custom_call" | custom-call | tf_op jit(solution)/shard_map/finish/pallas_call | solution.py:932
  38.9 0.0 collective-permute-done.13
  38.9 0.6 %slice_bitcast_fusion = (f32[256,32]{0,1:T(8,128)}, f32[256,32]{0,1:T(8,128)}) fusion(f32[64,256]{1,0:T(8,128)S(1)} %convert_add_fusion), kind=kLoop, calls=%fused_computation.3 | loop fusion | bytes 131072 | tf_op jit(solution)/shard_map/transpose | solution.py:960
  (5 shorter events, 0.1 us)
Async XLA Ops:
  2.6 7.8 %collective-permute-start.2 = (bf16[1,272,128]{2,1,0:T(8,128)(2,1)S(1)}, bf16[1,272,128]{2,1,0:T(8,128)(2,1)S(1)}, u32[]{:S(2)}, u32[]{:S(2)}) collective-permute-start(bf16[1,272,128]{2,1,0:T(8,128)(2,1)S(1)} %get-tuple-element.56), channel_id=1, source_target_pairs={{0,6},{1,7},{2,4},{3,5},{4,2},{5,3},{6,0},{7,1},{8,14},{9,15},{10,... | collective-permute-start | bytes 208904 | tf_op jit(solution)/shard_map/ppermute | solution.py:740
  7.7 5.9 %collective-permute-start.1 = (bf16[1,272,128]{2,1,0:T(8,128)(2,1)S(1)}, bf16[1,272,128]{2,1,0:T(8,128)(2,1)S(1)}, u32[]{:S(2)}, u32[]{:S(2)}) collective-permute-start(bf16[1,272,128]{2,1,0:T(8,128)(2,1)S(1)} %get-tuple-element.56), channel_id=1, source_target_pairs={{0,4},{1,5},{2,6},{3,7},{4,0},{5,1},{6,2},{7,3},{8,12},{9,13},{10,... | collective-permute-start | bytes 208904 | tf_op jit(solution)/shard_map/ppermute | solution.py:740
  7.8 5.9 %collective-permute-start = (bf16[1,272,128]{2,1,0:T(8,128)(2,1)S(1)}, bf16[1,272,128]{2,1,0:T(8,128)(2,1)S(1)}, u32[]{:S(2)}, u32[]{:S(2)}) collective-permute-start(bf16[1,272,128]{2,1,0:T(8,128)(2,1)S(1)} %get-tuple-element.56), channel_id=1, source_target_pairs={{0,2},{1,3},{2,0},{3,1},{4,6},{5,7},{6,4},{7,5},{8,10},{9,11},{10,... | collective-permute-start | bytes 208904 | tf_op jit(solution)/shard_map/ppermute | solution.py:740
  8.4 5.3 %collective-permute-start.3 = (bf16[256,256]{1,0:T(8,128)(2,1)S(1)}, bf16[256,256]{1,0:T(8,128)(2,1)S(1)}, u32[]{:S(2)}, u32[]{:S(2)}) collective-permute-start(bf16[256,256]{1,0:T(8,128)(2,1)S(1)} %get-tuple-element.62.normed_ref), channel_id=1, source_target_pairs={{0,1},{1,0},{2,3},{3,2},{4,5},{5,4},{6,7},{7,6},{8,9},{9,8},{10,11... | collective-permute-start | bytes 393224 | tf_op jit(solution)/shard_map/ppermute | solution.py:740
  13.7 5.5 %copy-start = (bf16[1024,128]{1,0:T(8,128)(2,1)S(1)}, bf16[1024,128]{1,0:T(8,128)(2,1)}, u32[]{:S(2)}) copy-start(bf16[1024,128]{1,0:T(8,128)(2,1)} %wout_ref.1) | copy-start | bytes 786436
  13.7 5.4 %collective-permute-start.5 = (bf16[4,144,128]{2,1,0:T(8,128)(2,1)S(1)}, bf16[4,144,128]{2,1,0:T(8,128)(2,1)S(1)}, u32[]{:S(2)}, u32[]{:S(2)}) collective-permute-start(bf16[4,144,128]{2,1,0:T(8,128)(2,1)S(1)} %slice.13.near_ref), channel_id=1, source_target_pairs={{0,1},{1,0},{2,3},{3,2},{4,5},{5,4},{6,7},{7,6},{8,9},{9,8},{10,11... | collective-permute-start | bytes 442376 | tf_op jit(solution)/shard_map/ppermute | solution.py:740
  15.3 5.8 %collective-permute-start.6 = (bf16[4,144,128]{2,1,0:T(8,128)(2,1)S(1)}, bf16[4,144,128]{2,1,0:T(8,128)(2,1)S(1)}, u32[]{:S(2)}, u32[]{:S(2)}) collective-permute-start(bf16[4,144,128]{2,1,0:T(8,128)(2,1)S(1)} %slice.13.near_ref), channel_id=1, source_target_pairs={{0,8},{8,0},{1,9},{9,1},{2,10},{10,2},{3,11},{11,3},{4,12},{12,4},... | collective-permute-start | bytes 442376 | tf_op jit(solution)/shard_map/ppermute | solution.py:729
  19.2 1.9 %collective-permute-start.7 = (bf16[4,144,128]{2,1,0:T(8,128)(2,1)S(1)}, bf16[4,144,128]{2,1,0:T(8,128)(2,1)S(1)}, u32[]{:S(2)}, u32[]{:S(2)}) collective-permute-start(bf16[4,144,128]{2,1,0:T(8,128)(2,1)S(1)} %collective-permute-done.5.far_ref), channel_id=1, source_target_pairs={{0,8},{8,0},{1,9},{9,1},{2,10},{10,2},{3,11},{11,3},{4,12},{12,4},... | collective-permute-start | bytes 442376 | tf_op jit(solution)/shard_map/ppermute | solution.py:729
  19.3 6.0 %collective-permute-start.4 = (bf16[4,128,128]{2,1,0:T(8,128)(2,1)S(1)}, bf16[4,128,128]{2,1,0:T(8,128)(2,1)S(1)}, u32[]{:S(2)}, u32[]{:S(2)}) collective-permute-start(bf16[4,128,128]{2,1,0:T(8,128)(2,1)S(1)} %slice.12.near_ref), channel_id=1, source_target_pairs={{0,1},{1,0},{2,3},{3,2},{4,5},{5,4},{6,7},{7,6},{8,9},{9,8},{10,11... | collective-permute-start | bytes 393224 | tf_op jit(solution)/shard_map/ppermute | solution.py:740
  21.1 4.3 %copy-start.1 = (bf16[128,512]{1,0:T(8,128)(2,1)S(1)}, bf16[128,512]{1,0:T(8,128)(2,1)}, u32[]{:S(2)}) copy-start(bf16[128,512]{1,0:T(8,128)(2,1)} %hid_ref.1) | copy-start | bytes 393220
  21.1 4.3 %copy-start.2 = (bf16[512,128]{1,0:T(8,128)(2,1)S(1)}, bf16[512,128]{1,0:T(8,128)(2,1)}, u32[]{:S(2)}) copy-start(bf16[512,128]{1,0:T(8,128)(2,1)} %back_ref.1) | copy-start | bytes 393220
  23.8 1.5 %collective-permute-start.8 = (bf16[256,256]{1,0:T(8,128)(2,1)S(1)}, bf16[256,256]{1,0:T(8,128)(2,1)S(1)}, u32[]{:S(2)}, u32[]{:S(2)}) collective-permute-start(bf16[256,256]{1,0:T(8,128)(2,1)S(1)} %get-tuple-element.62.normed_ref), channel_id=1, source_target_pairs={{0,8},{8,0},{1,9},{9,1},{2,10},{10,2},{3,11},{11,3},{4,12},{12,4},... | collective-permute-start | bytes 393224 | tf_op jit(solution)/shard_map/ppermute | solution.py:729
  24.1 1.3 %collective-permute-start.9 = (bf16[256,256]{1,0:T(8,128)(2,1)S(1)}, bf16[256,256]{1,0:T(8,128)(2,1)S(1)}, u32[]{:S(2)}, u32[]{:S(2)}) collective-permute-start(bf16[256,256]{1,0:T(8,128)(2,1)S(1)} %collective-permute-done.3.far_normed_ref), channel_id=1, source_target_pairs={{0,8},{8,0},{1,9},{9,1},{2,10},{10,2},{3,11},{11,3},{4,12},{12,4},... | collective-permute-start | bytes 393224 | tf_op jit(solution)/shard_map/ppermute | solution.py:729
  27.2 1.4 %collective-permute-start.10 = (bf16[512,128]{1,0:T(8,128)(2,1)S(1)}, bf16[512,128]{1,0:T(8,128)(2,1)S(1)}, u32[]{:S(2)}, u32[]{:S(2)}) collective-permute-start(bf16[512,128]{1,0:T(8,128)(2,1)S(1)} %get-tuple-element.69.opm_ref), channel_id=1, source_target_pairs={{0,8},{8,0},{1,9},{9,1},{2,10},{10,2},{3,11},{11,3},{4,12},{12,4},... | collective-permute-start | bytes 393224 | tf_op jit(solution)/shard_map/ppermute | solution.py:729
  30.7 6.9 %collective-permute-start.14 = (bf16[2048,128]{1,0:T(8,128)(2,1)S(1)}, bf16[2048,128]{1,0:T(8,128)(2,1)S(1)}, u32[]{:S(2)}, u32[]{:S(2)}) collective-permute-start(bf16[2048,128]{1,0:T(8,128)(2,1)S(1)} %weight_gradients.1.mine_ref), channel_id=1, source_target_pairs={{0,8},{8,0},{1,9},{9,1},{2,10},{10,2},{3,11},{11,3},{4,12},{12,4},... | collective-permute-start | bytes 1572872 | tf_op jit(solution)/shard_map/ppermute | solution.py:729
  31.1 5.7 %collective-permute-start.12 = (bf16[64,256]{1,0:T(8,128)(2,1)S(1)}, bf16[64,256]{1,0:T(8,128)(2,1)S(1)}, u32[]{:S(2)}, u32[]{:S(2)}) collective-permute-start(bf16[64,256]{1,0:T(8,128)(2,1)S(1)} %get-tuple-element.83), channel_id=1, source_target_pairs={{0,6},{1,7},{2,4},{3,5},{4,2},{5,3},{6,0},{7,1},{8,12},{9,13},{10,... | collective-permute-start | bytes 98312 | tf_op jit(solution)/shard_map/ppermute | solution.py:725
  34.0 2.8 %collective-permute-start.11 = (bf16[64,256]{1,0:T(8,128)(2,1)S(1)}, bf16[64,256]{1,0:T(8,128)(2,1)S(1)}, u32[]{:S(2)}, u32[]{:S(2)}) collective-permute-start(bf16[64,256]{1,0:T(8,128)(2,1)S(1)} %get-tuple-element.83), channel_id=1, source_target_pairs={{8,10},{9,11},{10,8},{11,9},{12,14},{13,15},{14,12},{15,13},{24,26... | collective-permute-start | bytes 98312 | tf_op jit(solution)/shard_map/ppermute | solution.py:725
  36.8 2.1 %collective-permute-start.13 = (bf16[64,256]{1,0:T(8,128)(2,1)S(1)}, bf16[64,256]{1,0:T(8,128)(2,1)S(1)}, u32[]{:S(2)}, u32[]{:S(2)}) collective-permute-start(bf16[64,256]{1,0:T(8,128)(2,1)S(1)} %add_convert_fusion), channel_id=1, source_target_pairs={{0,8},{8,0},{1,9},{9,1},{2,10},{10,2},{3,11},{11,3},{4,12},{12,4},... | collective-permute-start | bytes 98312 | tf_op jit(solution)/shard_map/ppermute | solution.py:729

commit v19 on v17

--- a/solution.py
+++ b/solution.py
@@ -707,21 +707,9 @@
         wide_projector(first_ref, second_ref, copies),
         preferred_element_type=jnp.float32,
     )
-    feat_ref[...] = standardize_adjoint(
-        back * scale_ref[...], scaled_ref[...], inv_ref[...]
-    ).astype(jnp.bfloat16)
+    feat = standardize_adjoint(back * scale_ref[...], scaled_ref[...], inv_ref[...])
+    feat_ref[...] = feat.reshape(feat_ref.shape).astype(jnp.bfloat16)
     couple_ref[...] = held_ref[...]
-
-
-def swap_line(block, partners):
-    count = lax.axis_size("col")
-    pairs = [
-        (depth * count + at, depth * count + (at ^ partner))
-        for depth, partner in enumerate(partners)
-        if partner is not None
-        for at in range(count)
-    ]
-    return lax.ppermute(block, ("depth", "col"), pairs)
 
 
 def swap_depth(block):
@@ -929,7 +917,7 @@
     )
     feat, couple = pl.pallas_call(
         functools.partial(feature_kernel, res),
-        out_shape=(shape((seqs * res, channels), bf16), shape((per, pair_width), bf16)),
+        out_shape=(shape((seqs, res, channels), bf16), shape((per, pair_width), bf16)),
         in_specs=[vmem] * 7,
         out_specs=[vmem] * 2,
         compiler_params=params,
@@ -948,13 +936,10 @@
         compiler_params=params,
         name="sums_over_depth",
     )(weights, swap_depth(weights))
-    came_b = swap_line(part, (None, Z_PARTNERS[0]))
-    came_a = swap_line(part, (Z_PARTNERS[2], Z_PARTNERS[1]))
-    feat = feat.reshape(seqs, res, channels)
-    came_b, came_a, feat, couple = lax.optimization_barrier((came_b, came_a, feat, couple))
-    kept = jnp.where(lax.axis_index("depth") == 0, part, came_b)
-    kept = lax.optimization_barrier((kept.astype(f32) + came_a.astype(f32)).astype(bf16))
-    came = swap_depth(kept)
+    came = swap_col(part, Z_PARTNERS[1])
+    came, feat, couple = lax.optimization_barrier((came, feat, couple))
+    kept = lax.optimization_barrier((part.astype(f32) + came.astype(f32)).astype(bf16))
+    came = swap_col(kept, Z_PARTNERS[0])
     came, dout, dhid, dback = lax.optimization_barrier((came, dout, dhid, dback))
     total = kept.astype(f32) + came.astype(f32)
     return (

time: 39.8 us -> 41.1 us (1.033)
  waiting for transfers between devices: 9.19 us -> 13.9 us
  starting transfers between devices: 16.8 us -> 14 us
  local copies, waits for them, and re-layouts: 1.46 us -> 0.77 us
    ppermute x6 -> x8, waiting for transfers between devices: 8.32 us -> 13.5 us  [swap_col(): lax.ppermute(block, 'col', [(at, at ^ partner) for at in range(count)])]
    ppermute x2 -> x0, starting transfers between devices: 3.61 us -> none  [swap_line(): return lax.ppermute(block, ('depth', 'col'), pairs)]
    ppermute x6 -> x8, starting transfers between devices: 10.8 us -> 12.7 us  [swap_col(): lax.ppermute(block, 'col', [(at, at ^ partner) for at in range(count)])]
    ppermute x7 -> x6, starting transfers between devices: 2.34 us -> 1.28 us  [swap_depth(): return lax.ppermute(block, 'depth', [(0, 1), (1, 0)])]
    reshape x1 -> x0, local copies, waits for them, and re-layouts: 0.69 us -> none  [whole_plan(): feat = feat.reshape(seqs, res, channels)]
    ppermute x2 -> x0, waiting for transfers between devices: 0.56 us -> none  [swap_line(): return lax.ppermute(block, ('depth', 'col'), pairs)]
  transfers between devices with their start and end apart: 15 -> 14, of which waited for: 7 -> 8; matrix products, arithmetic and copies ran while one was open for 2% -> 0% of each run, Pallas kernels for 14% -> 14%
where the time goes in v19:
time: 41.1 us; the launch traced here: 40.9 us
  starting transfers between devices  14 us (34%)
  waiting for transfers between devices  13.9 us (34%)
  Pallas kernels  11.4 us (28%)
  local copies, waits for them, and re-layouts  0.77 us (2%)
  between operations  0.75 us (2%)
    ppermute x8, waiting for transfers between devices, swap_col(): lax.ppermute(block, 'col', [(at, at ^ partner) for at in range(count)])  13.5 us
    ppermute x8, starting transfers between devices, swap_col(): lax.ppermute(block, 'col', [(at, at ^ partner) for at in range(count)])  12.7 us
    pallas_call x1, Pallas kernels, whole_plan(): pl.pallas_call(functools.partial(outer_kernel, sizes), out_shape=(shape((...  2.67 us
    pallas_call x1, Pallas kernels, whole_plan(): pl.pallas_call(functools.partial(projector_kernel, sizes), out_shape=(sha...  2.05 us
    pallas_call x1, Pallas kernels, whole_plan(): pl.pallas_call(pre_kernel, out_shape=(shape((1, rows + 2 * per, pair_widt...  1.91 us
    pallas_call x1, Pallas kernels, whole_plan(): pl.pallas_call(functools.partial(transition_kernel, sizes), out_shape=(sh...  1.81 us
    ppermute x6, starting transfers between devices, swap_depth(): return lax.ppermute(block, 'depth', [(0, 1), (1, 0)])  1.28 us
    pallas_call x1, Pallas kernels, whole_plan(): pl.pallas_call(weights_sum_kernel, out_shape=(shape((outer_width, pair_wi...  1.02 us
  transfers between devices with their start and end apart: 14, of which 8 were waited for; matrix products, arithmetic and copies ran while one was open for 0% of the time, Pallas kernels for 14%

profile of v19, /device:TPU:0, one launch (start us, length us, event | category | flops | bytes accessed | tf_op | source)
XLA Modules:
  0.0 40.9 jit_solution(3537760768659328294)
XLA Ops:
  0.6 0.1 pad_add_fusion.ids_ref
  0.7 1.9 %project.1 = (bf16[1,272,128]{2,1,0:T(8,128)(2,1)S(1)}, f32[1,256]{1,0:T(1,128)S(1)}, bf16[32,256]{1,0:T(8,128)(2,1)S(1)}, bf16[32,256]{1,0:T(8,128)(2,1)S(1)}, ...) custom-call(s32[2]{0:T(128)S(1)} %pad_add_fusion.ids_ref, ...), custom_call_target="tpu_custom_call" | custom-call | tf_op jit(solution)/shard_map/project/pallas_call | solution.py:767
  2.6 5.1 %collective-permute-start.2 = (bf16[1,272,128]{2,1,0:T(8,128)(2,1)S(1)}, bf16[1,272,128]{2,1,0:T(8,128)(2,1)S(1)}, u32[]{:S(2)}, u32[]{:S(2)}) collective-permute-start(bf16[1,272,128]{2,1,0:T(8,128)(2,1)S(1)} %get-tuple-element.55), channel_id=1, source_target_pairs={{0,6},{1,7},{2,4},{3,5},{4,2},{5,3},{6,0},{7,1},{8,14},{9,15},{10,... | collective-permute-start | bytes 208904 | tf_op jit(solution)/shard_map/ppermute | solution.py:727
  7.7 0.0 collective-permute-start.1
  7.8 0.6 %collective-permute-start = (bf16[1,272,128]{2,1,0:T(8,128)(2,1)S(1)}, bf16[1,272,128]{2,1,0:T(8,128)(2,1)S(1)}, u32[]{:S(2)}, u32[]{:S(2)}) collective-permute-start(bf16[1,272,128]{2,1,0:T(8,128)(2,1)S(1)} %get-tuple-element.55), channel_id=1, source_target_pairs={{0,2},{1,3},{2,0},{3,1},{4,6},{5,7},{6,4},{7,5},{8,10},{9,11},{10,... | collective-permute-start | bytes 208904 | tf_op jit(solution)/shard_map/ppermute | solution.py:727
  8.4 1.7 %collective-permute-start.3 = (bf16[256,256]{1,0:T(8,128)(2,1)S(1)}, bf16[256,256]{1,0:T(8,128)(2,1)S(1)}, u32[]{:S(2)}, u32[]{:S(2)}) collective-permute-start(bf16[256,256]{1,0:T(8,128)(2,1)S(1)} %get-tuple-element.61.normed_ref), channel_id=1, source_target_pairs={{0,1},{1,0},{2,3},{3,2},{4,5},{5,4},{6,7},{7,6},{8,9},{9,8},{10,11... | collective-permute-start | bytes 393224 | tf_op jit(solution)/shard_map/ppermute | solution.py:727
  10.1 0.4 collective-permute-done.2
  10.4 3.2 %collective-permute-done.1 = bf16[1,272,128]{2,1,0:T(8,128)(2,1)S(1)} collective-permute-done((bf16[1,272,128]{2,1,0:T(8,128)(2,1)S(1)}, bf16[1,272,128]{2,1,0:T(8,128)(2,1)S(1)}, u32[]{:S(2)}, u32[]{:S(2)}) %collective-permute-start.1) | collective-permute-done | bytes 69664 | tf_op jit(solution)/shard_map/ppermute | solution.py:727
  13.7 0.0 collective-permute-done
  13.7 0.0 copy-start
  13.7 0.0 collective-permute-done.3.far_normed_ref
  13.7 1.6 %collective-permute-start.5 = (bf16[4,144,128]{2,1,0:T(8,128)(2,1)S(1)}, bf16[4,144,128]{2,1,0:T(8,128)(2,1)S(1)}, u32[]{:S(2)}, u32[]{:S(2)}) collective-permute-start(bf16[4,144,128]{2,1,0:T(8,128)(2,1)S(1)} %slice.13.near_ref), channel_id=1, source_target_pairs={{0,1},{1,0},{2,3},{3,2},{4,5},{5,4},{6,7},{7,6},{8,9},{9,8},{10,11... | collective-permute-start | bytes 442376 | tf_op jit(solution)/shard_map/ppermute | solution.py:727
  15.3 0.0 collective-permute-start.6
  15.3 3.8 %collective-permute-done.5.far_ref = bf16[4,144,128]{2,1,0:T(8,128)(2,1)S(1)} collective-permute-done((bf16[4,144,128]{2,1,0:T(8,128)(2,1)S(1)}, bf16[4,144,128]{2,1,0:T(8,128)(2,1)S(1)}, u32[]{:S(2)}, u32[]{:S(2)}) %collective-permute-start.5) | collective-permute-done | bytes 147488 | tf_op jit(solution)/shard_map/ppermute | solution.py:727
  19.2 0.0 collective-permute-start.7
  19.2 0.0 copy-done
  19.2 0.1 copy.19
  19.3 1.8 %collective-permute-start.4 = (bf16[4,128,128]{2,1,0:T(8,128)(2,1)S(1)}, bf16[4,128,128]{2,1,0:T(8,128)(2,1)S(1)}, u32[]{:S(2)}, u32[]{:S(2)}) collective-permute-start(bf16[4,128,128]{2,1,0:T(8,128)(2,1)S(1)} %slice.12.near_ref), channel_id=1, source_target_pairs={{0,1},{1,0},{2,3},{3,2},{4,5},{5,4},{6,7},{7,6},{8,9},{9,8},{10,11... | collective-permute-start | bytes 393224 | tf_op jit(solution)/shard_map/ppermute | solution.py:727
  21.1 0.0 collective-permute-done.6.other_near_ref
  21.1 0.0 collective-permute-done.7.other_far_ref
  21.1 0.0 copy-start.1
  21.1 0.0 copy-start.2
  21.1 2.7 %outer_products.1 = (bf16[512,1024]{1,0:T(8,128)(2,1)S(1)}, f32[512,128]{1,0:T(8,128)S(1)}, f32[512,128]{1,0:T(8,128)S(1)}, bf16[512,128]{1,0:T(8,128)(2,1)S(1)}...) custom-call(s32[2]{0:T(128)S(1)} %pad_add_fusion.ids_ref, ...), custom_call_target="tpu_custom_call" | custom-call | tf_op jit(solution)/shard_map/outer_products/pallas_call | solution.py:818
  23.8 0.3 collective-permute-start.8
  24.1 0.3 collective-permute-start.9
  24.4 0.9 %collective-permute-done.4.far_ref = bf16[4,128,128]{2,1,0:T(8,128)(2,1)S(1)} collective-permute-done((bf16[4,128,128]{2,1,0:T(8,128)(2,1)S(1)}, bf16[4,128,128]{2,1,0:T(8,128)(2,1)S(1)}, u32[]{:S(2)}, u32[]{:S(2)}) %collective-permute-start.4) | collective-permute-done | bytes 131104 | tf_op jit(solution)/shard_map/ppermute | solution.py:727
  25.3 0.0 collective-permute-done.8.other_normed_ref
  25.3 0.2 collective-permute-done.9.other_far_normed_ref
  25.4 0.0 copy-done.1
  25.4 0.0 copy-done.2
  25.4 1.8 %transition.1 = (bf16[64,128]{1,0:T(8,128)(2,1)S(1)}, bf16[512,128]{1,0:T(8,128)(2,1)S(1)}, bf16[512,128]{1,0:T(8,128)(2,1)S(1)}, bf16[512,512]{1,0:T(8,128)(2,1...) custom-call(s32[2]{0:T(128)S(1)} %pad_add_fusion.ids_ref, bf16[4,128,128]{2,1,0:T(8,128)(2,1)S(1)} %slice.12.near_ref, ...), custom_call_target="tpu_custom_call" | custom-call | tf_op jit(solution)/shard_map/transition/pallas_call | solution.py:847
  27.3 0.4 collective-permute-start.10
  27.6 0.9 %weight_gradients.1.mine_ref = bf16[2048,128]{1,0:T(8,128)(2,1)S(1)} custom-call(bf16[512,1024]{1,0:T(8,128)(2,1)S(1)} %get-tuple-element.69.outer_ref, bf16[512,128]{1,0:T(8,128)(2,1)S(1)} %get-tuple-element.68.opm_ref, bf16[512,128]{1,0:T(8,128)(2,1)S(1)} %get-tuple-element.70.pn_ref, bf16[512,512]{1,0:T(8,128)(2,1)S(1)} %get-tuple-element.71.gh_ref, ...), custom_call_target="tpu_custom_call" | custom-call | tf_op jit(solution)/shard_map/weight_gradients/pallas_call | solution.py:875
  28.5 0.1 collective-permute-done.10.other_opm_ref
  28.7 2.1 %projector_parts.1 = (bf16[64,256]{1,0:T(8,128)(2,1)S(1)}, bf16[256,256]{1,0:T(8,128)(2,1)S(1)}) custom-call(s32[2]{0:T(128)S(1)} %pad_add_fusion.ids_ref, bf16[512,128]{1,0:T(8,128)(2,1)S(1)} %get-tuple-element.68.opm_ref, bf16[512,128]{1,0:T(8,128)(2,1)S(1)} %collective-permute-done.10.other_opm_ref, bf16[1024,128]{1,0:T(8,128)(2,1)S(1)} %get-tuple-element.75.rightt_ref, ...), custom_call_target="tpu_custom_call" | custom-call | tf_op jit(solution)/shard_map/projector_parts/pallas_call | solution.py:885
  30.7 0.4 collective-permute-start.13
  31.1 1.5 %collective-permute-start.11 = (bf16[64,256]{1,0:T(8,128)(2,1)S(1)}, bf16[64,256]{1,0:T(8,128)(2,1)S(1)}, u32[]{:S(2)}, u32[]{:S(2)}) collective-permute-start(bf16[64,256]{1,0:T(8,128)(2,1)S(1)} %get-tuple-element.82), channel_id=1, source_target_pairs={{0,4},{1,5},{2,6},{3,7},{4,0},{5,1},{6,2},{7,3},{8,12},{9,13},{10,... | collective-permute-start | bytes 98312 | tf_op jit(solution)/shard_map/ppermute | solution.py:727
  32.6 1.0 %features.1 = (bf16[64,4,256]{2,1,0:T(4,128)(2,1)}, bf16[64,128]{1,0:T(8,128)(2,1)}) custom-call(bf16[256,256]{1,0:T(8,128)(2,1)S(1)} %get-tuple-element.83.spread_ref, bf16[32,256]{1,0:T(8,128)(2,1)S(1)} %get-tuple-element.84.first_ref, bf16[32,256]{1,0:T(8,128)(2,1)S(1)} %get-tuple-element.85.second_ref, f32[1,256]{1,0:T(1,128)S(1)} %get-tuple-element.86.scale_ref, ...), custom_call_target="tpu_custom_call" | custom-call | tf_op jit(solution)/shard_map/features/pallas_call | solution.py:918
  33.5 2.7 %collective-permute-done.11 = bf16[64,256]{1,0:T(8,128)(2,1)S(1)} collective-permute-done((bf16[64,256]{1,0:T(8,128)(2,1)S(1)}, bf16[64,256]{1,0:T(8,128)(2,1)S(1)}, u32[]{:S(2)}, u32[]{:S(2)}) %collective-permute-start.11) | collective-permute-done | bytes 32800 | tf_op jit(solution)/shard_map/ppermute | solution.py:727
  36.3 0.4 %collective-permute-start.12 = (bf16[64,256]{1,0:T(8,128)(2,1)S(1)}, bf16[64,256]{1,0:T(8,128)(2,1)S(1)}, u32[]{:S(2)}, u32[]{:S(2)}) collective-permute-start(bf16[64,256]{1,0:T(8,128)(2,1)S(1)} %add_convert_fusion), channel_id=1, source_target_pairs={{0,2},{1,3},{2,0},{3,1},{4,6},{5,7},{6,4},{7,5},{8,10},{9,11},{10,... | collective-permute-start | bytes 98312 | tf_op jit(solution)/shard_map/ppermute | solution.py:727
  36.7 0.0 collective-permute-done.13.other_ref
  36.7 1.0 %sums_over_depth.1 = (f32[1024,128]{1,0:T(8,128)}, f32[128,512]{1,0:T(8,128)}, f32[512,128]{1,0:T(8,128)}) custom-call(bf16[2048,128]{1,0:T(8,128)(2,1)S(1)} %weight_gradients.1.mine_ref, bf16[2048,128]{1,0:T(8,128)(2,1)S(1)} %collective-permute-done.13.other_ref), custom_call_target="tpu_custom_call" | custom-call | tf_op jit(solution)/shard_map/sums_over_depth/pallas_call | solution.py:927
  37.7 2.5 %collective-permute-done.12 = bf16[64,256]{1,0:T(8,128)(2,1)S(1)} collective-permute-done((bf16[64,256]{1,0:T(8,128)(2,1)S(1)}, bf16[64,256]{1,0:T(8,128)(2,1)S(1)}, u32[]{:S(2)}, u32[]{:S(2)}) %collective-permute-start.12) | collective-permute-done | bytes 32800 | tf_op jit(solution)/shard_map/ppermute | solution.py:727
  40.2 0.6 %slice_bitcast_fusion = (f32[256,32]{0,1:T(8,128)}, f32[256,32]{0,1:T(8,128)}) fusion(f32[64,256]{1,0:T(8,128)S(1)} %convert_add_fusion), kind=kLoop, calls=%fused_computation.3 | loop fusion | bytes 131072 | tf_op jit(solution)/shard_map/transpose | solution.py:949
  (5 shorter events, 0.1 us)
Async XLA Ops:
  2.6 7.8 %collective-permute-start.2 = (bf16[1,272,128]{2,1,0:T(8,128)(2,1)S(1)}, bf16[1,272,128]{2,1,0:T(8,128)(2,1)S(1)}, u32[]{:S(2)}, u32[]{:S(2)}) collective-permute-start(bf16[1,272,128]{2,1,0:T(8,128)(2,1)S(1)} %get-tuple-element.55), channel_id=1, source_target_pairs={{0,6},{1,7},{2,4},{3,5},{4,2},{5,3},{6,0},{7,1},{8,14},{9,15},{10,... | collective-permute-start | bytes 208904 | tf_op jit(solution)/shard_map/ppermute | solution.py:727
  7.7 5.9 %collective-permute-start.1 = (bf16[1,272,128]{2,1,0:T(8,128)(2,1)S(1)}, bf16[1,272,128]{2,1,0:T(8,128)(2,1)S(1)}, u32[]{:S(2)}, u32[]{:S(2)}) collective-permute-start(bf16[1,272,128]{2,1,0:T(8,128)(2,1)S(1)} %get-tuple-element.55), channel_id=1, source_target_pairs={{0,4},{1,5},{2,6},{3,7},{4,0},{5,1},{6,2},{7,3},{8,12},{9,13},{10,... | collective-permute-start | bytes 208904 | tf_op jit(solution)/shard_map/ppermute | solution.py:727
  7.8 5.9 %collective-permute-start = (bf16[1,272,128]{2,1,0:T(8,128)(2,1)S(1)}, bf16[1,272,128]{2,1,0:T(8,128)(2,1)S(1)}, u32[]{:S(2)}, u32[]{:S(2)}) collective-permute-start(bf16[1,272,128]{2,1,0:T(8,128)(2,1)S(1)} %get-tuple-element.55), channel_id=1, source_target_pairs={{0,2},{1,3},{2,0},{3,1},{4,6},{5,7},{6,4},{7,5},{8,10},{9,11},{10,... | collective-permute-start | bytes 208904 | tf_op jit(solution)/shard_map/ppermute | solution.py:727
  8.4 5.3 %collective-permute-start.3 = (bf16[256,256]{1,0:T(8,128)(2,1)S(1)}, bf16[256,256]{1,0:T(8,128)(2,1)S(1)}, u32[]{:S(2)}, u32[]{:S(2)}) collective-permute-start(bf16[256,256]{1,0:T(8,128)(2,1)S(1)} %get-tuple-element.61.normed_ref), channel_id=1, source_target_pairs={{0,1},{1,0},{2,3},{3,2},{4,5},{5,4},{6,7},{7,6},{8,9},{9,8},{10,11... | collective-permute-start | bytes 393224 | tf_op jit(solution)/shard_map/ppermute | solution.py:727
  13.7 5.5 %copy-start = (bf16[1024,128]{1,0:T(8,128)(2,1)S(1)}, bf16[1024,128]{1,0:T(8,128)(2,1)}, u32[]{:S(2)}) copy-start(bf16[1024,128]{1,0:T(8,128)(2,1)} %wout_ref.1) | copy-start | bytes 786436
  13.7 5.4 %collective-permute-start.5 = (bf16[4,144,128]{2,1,0:T(8,128)(2,1)S(1)}, bf16[4,144,128]{2,1,0:T(8,128)(2,1)S(1)}, u32[]{:S(2)}, u32[]{:S(2)}) collective-permute-start(bf16[4,144,128]{2,1,0:T(8,128)(2,1)S(1)} %slice.13.near_ref), channel_id=1, source_target_pairs={{0,1},{1,0},{2,3},{3,2},{4,5},{5,4},{6,7},{7,6},{8,9},{9,8},{10,11... | collective-permute-start | bytes 442376 | tf_op jit(solution)/shard_map/ppermute | solution.py:727
  15.3 5.8 %collective-permute-start.6 = (bf16[4,144,128]{2,1,0:T(8,128)(2,1)S(1)}, bf16[4,144,128]{2,1,0:T(8,128)(2,1)S(1)}, u32[]{:S(2)}, u32[]{:S(2)}) collective-permute-start(bf16[4,144,128]{2,1,0:T(8,128)(2,1)S(1)} %slice.13.near_ref), channel_id=1, source_target_pairs={{0,8},{8,0},{1,9},{9,1},{2,10},{10,2},{3,11},{11,3},{4,12},{12,4},... | collective-permute-start | bytes 442376 | tf_op jit(solution)/shard_map/ppermute | solution.py:716
  19.2 1.9 %collective-permute-start.7 = (bf16[4,144,128]{2,1,0:T(8,128)(2,1)S(1)}, bf16[4,144,128]{2,1,0:T(8,128)(2,1)S(1)}, u32[]{:S(2)}, u32[]{:S(2)}) collective-permute-start(bf16[4,144,128]{2,1,0:T(8,128)(2,1)S(1)} %collective-permute-done.5.far_ref), channel_id=1, source_target_pairs={{0,8},{8,0},{1,9},{9,1},{2,10},{10,2},{3,11},{11,3},{4,12},{12,4},... | collective-permute-start | bytes 442376 | tf_op jit(solution)/shard_map/ppermute | solution.py:716
  19.3 6.0 %collective-permute-start.4 = (bf16[4,128,128]{2,1,0:T(8,128)(2,1)S(1)}, bf16[4,128,128]{2,1,0:T(8,128)(2,1)S(1)}, u32[]{:S(2)}, u32[]{:S(2)}) collective-permute-start(bf16[4,128,128]{2,1,0:T(8,128)(2,1)S(1)} %slice.12.near_ref), channel_id=1, source_target_pairs={{0,1},{1,0},{2,3},{3,2},{4,5},{5,4},{6,7},{7,6},{8,9},{9,8},{10,11... | collective-permute-start | bytes 393224 | tf_op jit(solution)/shard_map/ppermute | solution.py:727
  21.1 4.3 %copy-start.1 = (bf16[128,512]{1,0:T(8,128)(2,1)S(1)}, bf16[128,512]{1,0:T(8,128)(2,1)}, u32[]{:S(2)}) copy-start(bf16[128,512]{1,0:T(8,128)(2,1)} %hid_ref.1) | copy-start | bytes 393220
  21.1 4.3 %copy-start.2 = (bf16[512,128]{1,0:T(8,128)(2,1)S(1)}, bf16[512,128]{1,0:T(8,128)(2,1)}, u32[]{:S(2)}) copy-start(bf16[512,128]{1,0:T(8,128)(2,1)} %back_ref.1) | copy-start | bytes 393220
  23.8 1.5 %collective-permute-start.8 = (bf16[256,256]{1,0:T(8,128)(2,1)S(1)}, bf16[256,256]{1,0:T(8,128)(2,1)S(1)}, u32[]{:S(2)}, u32[]{:S(2)}) collective-permute-start(bf16[256,256]{1,0:T(8,128)(2,1)S(1)} %get-tuple-element.61.normed_ref), channel_id=1, source_target_pairs={{0,8},{8,0},{1,9},{9,1},{2,10},{10,2},{3,11},{11,3},{4,12},{12,4},... | collective-permute-start | bytes 393224 | tf_op jit(solution)/shard_map/ppermute | solution.py:716
  24.1 1.3 %collective-permute-start.9 = (bf16[256,256]{1,0:T(8,128)(2,1)S(1)}, bf16[256,256]{1,0:T(8,128)(2,1)S(1)}, u32[]{:S(2)}, u32[]{:S(2)}) collective-permute-start(bf16[256,256]{1,0:T(8,128)(2,1)S(1)} %collective-permute-done.3.far_normed_ref), channel_id=1, source_target_pairs={{0,8},{8,0},{1,9},{9,1},{2,10},{10,2},{3,11},{11,3},{4,12},{12,4},... | collective-permute-start | bytes 393224 | tf_op jit(solution)/shard_map/ppermute | solution.py:716
  27.3 1.4 %collective-permute-start.10 = (bf16[512,128]{1,0:T(8,128)(2,1)S(1)}, bf16[512,128]{1,0:T(8,128)(2,1)S(1)}, u32[]{:S(2)}, u32[]{:S(2)}) collective-permute-start(bf16[512,128]{1,0:T(8,128)(2,1)S(1)} %get-tuple-element.68.opm_ref), channel_id=1, source_target_pairs={{0,8},{8,0},{1,9},{9,1},{2,10},{10,2},{3,11},{11,3},{4,12},{12,4},... | collective-permute-start | bytes 393224 | tf_op jit(solution)/shard_map/ppermute | solution.py:716
  30.7 6.0 %collective-permute-start.13 = (bf16[2048,128]{1,0:T(8,128)(2,1)S(1)}, bf16[2048,128]{1,0:T(8,128)(2,1)S(1)}, u32[]{:S(2)}, u32[]{:S(2)}) collective-permute-start(bf16[2048,128]{1,0:T(8,128)(2,1)S(1)} %weight_gradients.1.mine_ref), channel_id=1, source_target_pairs={{0,8},{8,0},{1,9},{9,1},{2,10},{10,2},{3,11},{11,3},{4,12},{12,4},... | collective-permute-start | bytes 1572872 | tf_op jit(solution)/shard_map/ppermute | solution.py:716
  31.1 5.2 %collective-permute-start.11 = (bf16[64,256]{1,0:T(8,128)(2,1)S(1)}, bf16[64,256]{1,0:T(8,128)(2,1)S(1)}, u32[]{:S(2)}, u32[]{:S(2)}) collective-permute-start(bf16[64,256]{1,0:T(8,128)(2,1)S(1)} %get-tuple-element.82), channel_id=1, source_target_pairs={{0,4},{1,5},{2,6},{3,7},{4,0},{5,1},{6,2},{7,3},{8,12},{9,13},{10,... | collective-permute-start | bytes 98312 | tf_op jit(solution)/shard_map/ppermute | solution.py:727
  36.3 4.0 %collective-permute-start.12 = (bf16[64,256]{1,0:T(8,128)(2,1)S(1)}, bf16[64,256]{1,0:T(8,128)(2,1)S(1)}, u32[]{:S(2)}, u32[]{:S(2)}) collective-permute-start(bf16[64,256]{1,0:T(8,128)(2,1)S(1)} %add_convert_fusion), channel_id=1, source_target_pairs={{0,2},{1,3},{2,0},{3,1},{4,6},{5,7},{6,4},{7,5},{8,10},{9,11},{10,... | collective-permute-start | bytes 98312 | tf_op jit(solution)/shard_map/ppermute | solution.py:727

commit v20 on v17

--- a/solution.py
+++ b/solution.py
@@ -707,9 +707,8 @@
         wide_projector(first_ref, second_ref, copies),
         preferred_element_type=jnp.float32,
     )
-    feat_ref[...] = standardize_adjoint(
-        back * scale_ref[...], scaled_ref[...], inv_ref[...]
-    ).astype(jnp.bfloat16)
+    feat = standardize_adjoint(back * scale_ref[...], scaled_ref[...], inv_ref[...])
+    feat_ref[...] = feat.reshape(feat_ref.shape).astype(jnp.bfloat16)
     couple_ref[...] = held_ref[...]
 
 
@@ -929,7 +928,7 @@
     )
     feat, couple = pl.pallas_call(
         functools.partial(feature_kernel, res),
-        out_shape=(shape((seqs * res, channels), bf16), shape((per, pair_width), bf16)),
+        out_shape=(shape((seqs, res, channels), bf16), shape((per, pair_width), bf16)),
         in_specs=[vmem] * 7,
         out_specs=[vmem] * 2,
         compiler_params=params,
@@ -950,7 +949,6 @@
     )(weights, swap_depth(weights))
     came_b = swap_line(part, (None, Z_PARTNERS[0]))
     came_a = swap_line(part, (Z_PARTNERS[2], Z_PARTNERS[1]))
-    feat = feat.reshape(seqs, res, channels)
     came_b, came_a, feat, couple = lax.optimization_barrier((came_b, came_a, feat, couple))
     kept = jnp.where(lax.axis_index("depth") == 0, part, came_b)
     kept = lax.optimization_barrier((kept.astype(f32) + came_a.astype(f32)).astype(bf16))

time: 39.8 us -> 39.5 us (level)
  local copies, waits for them, and re-layouts: 1.46 us -> 0.77 us
  waiting for transfers between devices: 9.19 us -> 9.75 us
    reshape x1 -> x0, local copies, waits for them, and re-layouts: 0.69 us -> none  [whole_plan(): feat = feat.reshape(seqs, res, channels)]
    ppermute x2, waiting for transfers between devices: 0.56 us -> 1.12 us  [swap_line(): return lax.ppermute(block, ('depth', 'col'), pairs)]
  transfers between devices with their start and end apart: 15 -> 15, of which waited for: 7 -> 7; matrix products, arithmetic and copies ran while one was open for 2% -> 0% of each run, Pallas kernels for 14% -> 14%
where the time goes in v20:
time: 39.5 us; the launch traced here: 39.3 us
  starting transfers between devices  16.5 us (42%)
  Pallas kernels  11.3 us (29%)
  waiting for transfers between devices  9.75 us (25%)
  local copies, waits for them, and re-layouts  0.77 us (2%)
  between operations  0.76 us (2%)
    ppermute x6, starting transfers between devices, swap_col(): lax.ppermute(block, 'col', [(at, at ^ partner) for at in range(count)])  10.8 us
    ppermute x6, waiting for transfers between devices, swap_col(): lax.ppermute(block, 'col', [(at, at ^ partner) for at in range(count)])  8.32 us
    ppermute x2, starting transfers between devices, swap_line(): return lax.ppermute(block, ('depth', 'col'), pairs)  3.61 us
    pallas_call x1, Pallas kernels, whole_plan(): pl.pallas_call(functools.partial(outer_kernel, sizes), out_shape=(shape((...  2.67 us
    ppermute x7, starting transfers between devices, swap_depth(): return lax.ppermute(block, 'depth', [(0, 1), (1, 0)])  2.07 us
    pallas_call x1, Pallas kernels, whole_plan(): pl.pallas_call(functools.partial(projector_kernel, sizes), out_shape=(sha...  2.05 us
    pallas_call x1, Pallas kernels, whole_plan(): pl.pallas_call(pre_kernel, out_shape=(shape((1, rows + 2 * per, pair_widt...  1.91 us
    pallas_call x1, Pallas kernels, whole_plan(): pl.pallas_call(functools.partial(transition_kernel, sizes), out_shape=(sh...  1.81 us
  transfers between devices with their start and end apart: 15, of which 7 were waited for; matrix products, arithmetic and copies ran while one was open for 0% of the time, Pallas kernels for 14%

profile of v20, /device:TPU:0, one launch (start us, length us, event | category | flops | bytes accessed | tf_op | source)
XLA Modules:
  0.0 39.3 jit_solution(11551363214112452978)
XLA Ops:
  0.6 0.1 pad_add_fusion.ids_ref
  0.7 1.9 %project.1 = (bf16[1,272,128]{2,1,0:T(8,128)(2,1)S(1)}, f32[1,256]{1,0:T(1,128)S(1)}, bf16[32,256]{1,0:T(8,128)(2,1)S(1)}, bf16[32,256]{1,0:T(8,128)(2,1)S(1)}, ...) custom-call(s32[2]{0:T(128)S(1)} %pad_add_fusion.ids_ref, ...), custom_call_target="tpu_custom_call" | custom-call | tf_op jit(solution)/shard_map/project/pallas_call | solution.py:778
  2.6 5.1 %collective-permute-start.2 = (bf16[1,272,128]{2,1,0:T(8,128)(2,1)S(1)}, bf16[1,272,128]{2,1,0:T(8,128)(2,1)S(1)}, u32[]{:S(2)}, u32[]{:S(2)}) collective-permute-start(bf16[1,272,128]{2,1,0:T(8,128)(2,1)S(1)} %get-tuple-element.56), channel_id=1, source_target_pairs={{0,6},{1,7},{2,4},{3,5},{4,2},{5,3},{6,0},{7,1},{8,14},{9,15},{10,... | collective-permute-start | bytes 208904 | tf_op jit(solution)/shard_map/ppermute | solution.py:738
  7.7 0.0 collective-permute-start.1
  7.8 0.6 %collective-permute-start = (bf16[1,272,128]{2,1,0:T(8,128)(2,1)S(1)}, bf16[1,272,128]{2,1,0:T(8,128)(2,1)S(1)}, u32[]{:S(2)}, u32[]{:S(2)}) collective-permute-start(bf16[1,272,128]{2,1,0:T(8,128)(2,1)S(1)} %get-tuple-element.56), channel_id=1, source_target_pairs={{0,2},{1,3},{2,0},{3,1},{4,6},{5,7},{6,4},{7,5},{8,10},{9,11},{10,... | collective-permute-start | bytes 208904 | tf_op jit(solution)/shard_map/ppermute | solution.py:738
  8.4 1.7 %collective-permute-start.3 = (bf16[256,256]{1,0:T(8,128)(2,1)S(1)}, bf16[256,256]{1,0:T(8,128)(2,1)S(1)}, u32[]{:S(2)}, u32[]{:S(2)}) collective-permute-start(bf16[256,256]{1,0:T(8,128)(2,1)S(1)} %get-tuple-element.62.normed_ref), channel_id=1, source_target_pairs={{0,1},{1,0},{2,3},{3,2},{4,5},{5,4},{6,7},{7,6},{8,9},{9,8},{10,11... | collective-permute-start | bytes 393224 | tf_op jit(solution)/shard_map/ppermute | solution.py:738
  10.1 0.4 collective-permute-done.2
  10.4 3.2 %collective-permute-done.1 = bf16[1,272,128]{2,1,0:T(8,128)(2,1)S(1)} collective-permute-done((bf16[1,272,128]{2,1,0:T(8,128)(2,1)S(1)}, bf16[1,272,128]{2,1,0:T(8,128)(2,1)S(1)}, u32[]{:S(2)}, u32[]{:S(2)}) %collective-permute-start.1) | collective-permute-done | bytes 69664 | tf_op jit(solution)/shard_map/ppermute | solution.py:738
  13.7 0.0 collective-permute-done
  13.7 0.0 copy-start
  13.7 0.0 collective-permute-done.3.far_normed_ref
  13.7 1.6 %collective-permute-start.5 = (bf16[4,144,128]{2,1,0:T(8,128)(2,1)S(1)}, bf16[4,144,128]{2,1,0:T(8,128)(2,1)S(1)}, u32[]{:S(2)}, u32[]{:S(2)}) collective-permute-start(bf16[4,144,128]{2,1,0:T(8,128)(2,1)S(1)} %slice.13.near_ref), channel_id=1, source_target_pairs={{0,1},{1,0},{2,3},{3,2},{4,5},{5,4},{6,7},{7,6},{8,9},{9,8},{10,11... | collective-permute-start | bytes 442376 | tf_op jit(solution)/shard_map/ppermute | solution.py:738
  15.3 0.0 collective-permute-start.6
  15.3 3.8 %collective-permute-done.5.far_ref = bf16[4,144,128]{2,1,0:T(8,128)(2,1)S(1)} collective-permute-done((bf16[4,144,128]{2,1,0:T(8,128)(2,1)S(1)}, bf16[4,144,128]{2,1,0:T(8,128)(2,1)S(1)}, u32[]{:S(2)}, u32[]{:S(2)}) %collective-permute-start.5) | collective-permute-done | bytes 147488 | tf_op jit(solution)/shard_map/ppermute | solution.py:738
  19.2 0.0 collective-permute-start.7
  19.2 0.0 copy-done
  19.2 0.1 copy.19
  19.3 1.8 %collective-permute-start.4 = (bf16[4,128,128]{2,1,0:T(8,128)(2,1)S(1)}, bf16[4,128,128]{2,1,0:T(8,128)(2,1)S(1)}, u32[]{:S(2)}, u32[]{:S(2)}) collective-permute-start(bf16[4,128,128]{2,1,0:T(8,128)(2,1)S(1)} %slice.12.near_ref), channel_id=1, source_target_pairs={{0,1},{1,0},{2,3},{3,2},{4,5},{5,4},{6,7},{7,6},{8,9},{9,8},{10,11... | collective-permute-start | bytes 393224 | tf_op jit(solution)/shard_map/ppermute | solution.py:738
  21.1 0.0 collective-permute-done.6.other_near_ref
  21.1 0.0 collective-permute-done.7.other_far_ref
  21.1 0.0 copy-start.1
  21.1 0.0 copy-start.2
  21.1 2.7 %outer_products.1 = (bf16[512,1024]{1,0:T(8,128)(2,1)S(1)}, f32[512,128]{1,0:T(8,128)S(1)}, f32[512,128]{1,0:T(8,128)S(1)}, bf16[512,128]{1,0:T(8,128)(2,1)S(1)}...) custom-call(s32[2]{0:T(128)S(1)} %pad_add_fusion.ids_ref, ...), custom_call_target="tpu_custom_call" | custom-call | tf_op jit(solution)/shard_map/outer_products/pallas_call | solution.py:829
  23.8 0.3 collective-permute-start.8
  24.1 0.3 collective-permute-start.9
  24.4 0.9 %collective-permute-done.4.far_ref = bf16[4,128,128]{2,1,0:T(8,128)(2,1)S(1)} collective-permute-done((bf16[4,128,128]{2,1,0:T(8,128)(2,1)S(1)}, bf16[4,128,128]{2,1,0:T(8,128)(2,1)S(1)}, u32[]{:S(2)}, u32[]{:S(2)}) %collective-permute-start.4) | collective-permute-done | bytes 131104 | tf_op jit(solution)/shard_map/ppermute | solution.py:738
  25.3 0.0 collective-permute-done.8.other_normed_ref
  25.3 0.2 collective-permute-done.9.other_far_normed_ref
  25.4 0.0 copy-done.1
  25.4 0.0 copy-done.2
  25.4 1.8 %transition.1 = (bf16[64,128]{1,0:T(8,128)(2,1)S(1)}, bf16[512,128]{1,0:T(8,128)(2,1)S(1)}, bf16[512,128]{1,0:T(8,128)(2,1)S(1)}, bf16[512,512]{1,0:T(8,128)(2,1...) custom-call(s32[2]{0:T(128)S(1)} %pad_add_fusion.ids_ref, bf16[4,128,128]{2,1,0:T(8,128)(2,1)S(1)} %slice.12.near_ref, ...), custom_call_target="tpu_custom_call" | custom-call | tf_op jit(solution)/shard_map/transition/pallas_call | solution.py:858
  27.2 0.4 collective-permute-start.10
  27.6 0.9 %weight_gradients.1.mine_ref = bf16[2048,128]{1,0:T(8,128)(2,1)S(1)} custom-call(bf16[512,1024]{1,0:T(8,128)(2,1)S(1)} %get-tuple-element.70.outer_ref, bf16[512,128]{1,0:T(8,128)(2,1)S(1)} %get-tuple-element.69.opm_ref, bf16[512,128]{1,0:T(8,128)(2,1)S(1)} %get-tuple-element.71.pn_ref, bf16[512,512]{1,0:T(8,128)(2,1)S(1)} %get-tuple-element.72.gh_ref, ...), custom_call_target="tpu_custom_call" | custom-call | tf_op jit(solution)/shard_map/weight_gradients/pallas_call | solution.py:886
  28.5 0.1 collective-permute-done.10.other_opm_ref
  28.7 2.0 %projector_parts.1 = (bf16[64,256]{1,0:T(8,128)(2,1)S(1)}, bf16[256,256]{1,0:T(8,128)(2,1)S(1)}) custom-call(s32[2]{0:T(128)S(1)} %pad_add_fusion.ids_ref, bf16[512,128]{1,0:T(8,128)(2,1)S(1)} %get-tuple-element.69.opm_ref, bf16[512,128]{1,0:T(8,128)(2,1)S(1)} %collective-permute-done.10.other_opm_ref, bf16[1024,128]{1,0:T(8,128)(2,1)S(1)} %get-tuple-element.76.rightt_ref, ...), custom_call_target="tpu_custom_call" | custom-call | tf_op jit(solution)/shard_map/projector_parts/pallas_call | solution.py:896
  30.7 0.4 collective-permute-start.14
  31.1 3.0 %collective-permute-start.12 = (bf16[64,256]{1,0:T(8,128)(2,1)S(1)}, bf16[64,256]{1,0:T(8,128)(2,1)S(1)}, u32[]{:S(2)}, u32[]{:S(2)}) collective-permute-start(bf16[64,256]{1,0:T(8,128)(2,1)S(1)} %get-tuple-element.83), channel_id=1, source_target_pairs={{0,6},{1,7},{2,4},{3,5},{4,2},{5,3},{6,0},{7,1},{8,12},{9,13},{10,... | collective-permute-start | bytes 98312 | tf_op jit(solution)/shard_map/ppermute | solution.py:723
  34.0 0.7 %collective-permute-start.11 = (bf16[64,256]{1,0:T(8,128)(2,1)S(1)}, bf16[64,256]{1,0:T(8,128)(2,1)S(1)}, u32[]{:S(2)}, u32[]{:S(2)}) collective-permute-start(bf16[64,256]{1,0:T(8,128)(2,1)S(1)} %get-tuple-element.83), channel_id=1, source_target_pairs={{8,10},{9,11},{10,8},{11,9},{12,14},{13,15},{14,12},{15,13},{24,26... | collective-permute-start | bytes 98312 | tf_op jit(solution)/shard_map/ppermute | solution.py:723
  34.7 1.0 %features.1 = (bf16[64,4,256]{2,1,0:T(4,128)(2,1)}, bf16[64,128]{1,0:T(8,128)(2,1)}) custom-call(bf16[256,256]{1,0:T(8,128)(2,1)S(1)} %get-tuple-element.84.spread_ref, bf16[32,256]{1,0:T(8,128)(2,1)S(1)} %get-tuple-element.85.first_ref, bf16[32,256]{1,0:T(8,128)(2,1)S(1)} %get-tuple-element.86.second_ref, f32[1,256]{1,0:T(1,128)S(1)} %get-tuple-element.87.scale_ref, ...), custom_call_target="tpu_custom_call" | custom-call | tf_op jit(solution)/shard_map/features/pallas_call | solution.py:929
  35.7 1.1 %collective-permute-done.12 = bf16[64,256]{1,0:T(8,128)(2,1)S(1)} collective-permute-done((bf16[64,256]{1,0:T(8,128)(2,1)S(1)}, bf16[64,256]{1,0:T(8,128)(2,1)S(1)}, u32[]{:S(2)}, u32[]{:S(2)}) %collective-permute-start.12) | collective-permute-done | bytes 32800 | tf_op jit(solution)/shard_map/ppermute | solution.py:723
  36.8 0.0 collective-permute-done.11
  36.8 0.8 %collective-permute-start.13 = (bf16[64,256]{1,0:T(8,128)(2,1)S(1)}, bf16[64,256]{1,0:T(8,128)(2,1)S(1)}, u32[]{:S(2)}, u32[]{:S(2)}) collective-permute-start(bf16[64,256]{1,0:T(8,128)(2,1)S(1)} %add_convert_fusion), channel_id=1, source_target_pairs={{0,8},{8,0},{1,9},{9,1},{2,10},{10,2},{3,11},{11,3},{4,12},{12,4},... | collective-permute-start | bytes 98312 | tf_op jit(solution)/shard_map/ppermute | solution.py:727
  37.6 0.0 collective-permute-done.14.other_ref
  37.6 1.0 %sums_over_depth.1 = (f32[1024,128]{1,0:T(8,128)}, f32[128,512]{1,0:T(8,128)}, f32[512,128]{1,0:T(8,128)}) custom-call(bf16[2048,128]{1,0:T(8,128)(2,1)S(1)} %weight_gradients.1.mine_ref, bf16[2048,128]{1,0:T(8,128)(2,1)S(1)} %collective-permute-done.14.other_ref), custom_call_target="tpu_custom_call" | custom-call | tf_op jit(solution)/shard_map/sums_over_depth/pallas_call | solution.py:938
  38.6 0.0 collective-permute-done.13
  38.6 0.6 %slice_bitcast_fusion = (f32[256,32]{0,1:T(8,128)}, f32[256,32]{0,1:T(8,128)}) fusion(f32[64,256]{1,0:T(8,128)S(1)} %convert_add_fusion), kind=kLoop, calls=%fused_computation.3 | loop fusion | bytes 131072 | tf_op jit(solution)/shard_map/transpose | solution.py:962
  (5 shorter events, 0.1 us)
Async XLA Ops:
  2.6 7.8 %collective-permute-start.2 = (bf16[1,272,128]{2,1,0:T(8,128)(2,1)S(1)}, bf16[1,272,128]{2,1,0:T(8,128)(2,1)S(1)}, u32[]{:S(2)}, u32[]{:S(2)}) collective-permute-start(bf16[1,272,128]{2,1,0:T(8,128)(2,1)S(1)} %get-tuple-element.56), channel_id=1, source_target_pairs={{0,6},{1,7},{2,4},{3,5},{4,2},{5,3},{6,0},{7,1},{8,14},{9,15},{10,... | collective-permute-start | bytes 208904 | tf_op jit(solution)/shard_map/ppermute | solution.py:738
  7.7 5.9 %collective-permute-start.1 = (bf16[1,272,128]{2,1,0:T(8,128)(2,1)S(1)}, bf16[1,272,128]{2,1,0:T(8,128)(2,1)S(1)}, u32[]{:S(2)}, u32[]{:S(2)}) collective-permute-start(bf16[1,272,128]{2,1,0:T(8,128)(2,1)S(1)} %get-tuple-element.56), channel_id=1, source_target_pairs={{0,4},{1,5},{2,6},{3,7},{4,0},{5,1},{6,2},{7,3},{8,12},{9,13},{10,... | collective-permute-start | bytes 208904 | tf_op jit(solution)/shard_map/ppermute | solution.py:738
  7.8 5.9 %collective-permute-start = (bf16[1,272,128]{2,1,0:T(8,128)(2,1)S(1)}, bf16[1,272,128]{2,1,0:T(8,128)(2,1)S(1)}, u32[]{:S(2)}, u32[]{:S(2)}) collective-permute-start(bf16[1,272,128]{2,1,0:T(8,128)(2,1)S(1)} %get-tuple-element.56), channel_id=1, source_target_pairs={{0,2},{1,3},{2,0},{3,1},{4,6},{5,7},{6,4},{7,5},{8,10},{9,11},{10,... | collective-permute-start | bytes 208904 | tf_op jit(solution)/shard_map/ppermute | solution.py:738
  8.4 5.3 %collective-permute-start.3 = (bf16[256,256]{1,0:T(8,128)(2,1)S(1)}, bf16[256,256]{1,0:T(8,128)(2,1)S(1)}, u32[]{:S(2)}, u32[]{:S(2)}) collective-permute-start(bf16[256,256]{1,0:T(8,128)(2,1)S(1)} %get-tuple-element.62.normed_ref), channel_id=1, source_target_pairs={{0,1},{1,0},{2,3},{3,2},{4,5},{5,4},{6,7},{7,6},{8,9},{9,8},{10,11... | collective-permute-start | bytes 393224 | tf_op jit(solution)/shard_map/ppermute | solution.py:738
  13.7 5.5 %copy-start = (bf16[1024,128]{1,0:T(8,128)(2,1)S(1)}, bf16[1024,128]{1,0:T(8,128)(2,1)}, u32[]{:S(2)}) copy-start(bf16[1024,128]{1,0:T(8,128)(2,1)} %wout_ref.1) | copy-start | bytes 786436
  13.7 5.4 %collective-permute-start.5 = (bf16[4,144,128]{2,1,0:T(8,128)(2,1)S(1)}, bf16[4,144,128]{2,1,0:T(8,128)(2,1)S(1)}, u32[]{:S(2)}, u32[]{:S(2)}) collective-permute-start(bf16[4,144,128]{2,1,0:T(8,128)(2,1)S(1)} %slice.13.near_ref), channel_id=1, source_target_pairs={{0,1},{1,0},{2,3},{3,2},{4,5},{5,4},{6,7},{7,6},{8,9},{9,8},{10,11... | collective-permute-start | bytes 442376 | tf_op jit(solution)/shard_map/ppermute | solution.py:738
  15.3 5.8 %collective-permute-start.6 = (bf16[4,144,128]{2,1,0:T(8,128)(2,1)S(1)}, bf16[4,144,128]{2,1,0:T(8,128)(2,1)S(1)}, u32[]{:S(2)}, u32[]{:S(2)}) collective-permute-start(bf16[4,144,128]{2,1,0:T(8,128)(2,1)S(1)} %slice.13.near_ref), channel_id=1, source_target_pairs={{0,8},{8,0},{1,9},{9,1},{2,10},{10,2},{3,11},{11,3},{4,12},{12,4},... | collective-permute-start | bytes 442376 | tf_op jit(solution)/shard_map/ppermute | solution.py:727
  19.2 1.9 %collective-permute-start.7 = (bf16[4,144,128]{2,1,0:T(8,128)(2,1)S(1)}, bf16[4,144,128]{2,1,0:T(8,128)(2,1)S(1)}, u32[]{:S(2)}, u32[]{:S(2)}) collective-permute-start(bf16[4,144,128]{2,1,0:T(8,128)(2,1)S(1)} %collective-permute-done.5.far_ref), channel_id=1, source_target_pairs={{0,8},{8,0},{1,9},{9,1},{2,10},{10,2},{3,11},{11,3},{4,12},{12,4},... | collective-permute-start | bytes 442376 | tf_op jit(solution)/shard_map/ppermute | solution.py:727
  19.3 6.0 %collective-permute-start.4 = (bf16[4,128,128]{2,1,0:T(8,128)(2,1)S(1)}, bf16[4,128,128]{2,1,0:T(8,128)(2,1)S(1)}, u32[]{:S(2)}, u32[]{:S(2)}) collective-permute-start(bf16[4,128,128]{2,1,0:T(8,128)(2,1)S(1)} %slice.12.near_ref), channel_id=1, source_target_pairs={{0,1},{1,0},{2,3},{3,2},{4,5},{5,4},{6,7},{7,6},{8,9},{9,8},{10,11... | collective-permute-start | bytes 393224 | tf_op jit(solution)/shard_map/ppermute | solution.py:738
  21.1 4.3 %copy-start.1 = (bf16[128,512]{1,0:T(8,128)(2,1)S(1)}, bf16[128,512]{1,0:T(8,128)(2,1)}, u32[]{:S(2)}) copy-start(bf16[128,512]{1,0:T(8,128)(2,1)} %hid_ref.1) | copy-start | bytes 393220
  21.1 4.3 %copy-start.2 = (bf16[512,128]{1,0:T(8,128)(2,1)S(1)}, bf16[512,128]{1,0:T(8,128)(2,1)}, u32[]{:S(2)}) copy-start(bf16[512,128]{1,0:T(8,128)(2,1)} %back_ref.1) | copy-start | bytes 393220
  23.8 1.5 %collective-permute-start.8 = (bf16[256,256]{1,0:T(8,128)(2,1)S(1)}, bf16[256,256]{1,0:T(8,128)(2,1)S(1)}, u32[]{:S(2)}, u32[]{:S(2)}) collective-permute-start(bf16[256,256]{1,0:T(8,128)(2,1)S(1)} %get-tuple-element.62.normed_ref), channel_id=1, source_target_pairs={{0,8},{8,0},{1,9},{9,1},{2,10},{10,2},{3,11},{11,3},{4,12},{12,4},... | collective-permute-start | bytes 393224 | tf_op jit(solution)/shard_map/ppermute | solution.py:727
  24.1 1.3 %collective-permute-start.9 = (bf16[256,256]{1,0:T(8,128)(2,1)S(1)}, bf16[256,256]{1,0:T(8,128)(2,1)S(1)}, u32[]{:S(2)}, u32[]{:S(2)}) collective-permute-start(bf16[256,256]{1,0:T(8,128)(2,1)S(1)} %collective-permute-done.3.far_normed_ref), channel_id=1, source_target_pairs={{0,8},{8,0},{1,9},{9,1},{2,10},{10,2},{3,11},{11,3},{4,12},{12,4},... | collective-permute-start | bytes 393224 | tf_op jit(solution)/shard_map/ppermute | solution.py:727
  27.2 1.4 %collective-permute-start.10 = (bf16[512,128]{1,0:T(8,128)(2,1)S(1)}, bf16[512,128]{1,0:T(8,128)(2,1)S(1)}, u32[]{:S(2)}, u32[]{:S(2)}) collective-permute-start(bf16[512,128]{1,0:T(8,128)(2,1)S(1)} %get-tuple-element.69.opm_ref), channel_id=1, source_target_pairs={{0,8},{8,0},{1,9},{9,1},{2,10},{10,2},{3,11},{11,3},{4,12},{12,4},... | collective-permute-start | bytes 393224 | tf_op jit(solution)/shard_map/ppermute | solution.py:727
  30.7 6.9 %collective-permute-start.14 = (bf16[2048,128]{1,0:T(8,128)(2,1)S(1)}, bf16[2048,128]{1,0:T(8,128)(2,1)S(1)}, u32[]{:S(2)}, u32[]{:S(2)}) collective-permute-start(bf16[2048,128]{1,0:T(8,128)(2,1)S(1)} %weight_gradients.1.mine_ref), channel_id=1, source_target_pairs={{0,8},{8,0},{1,9},{9,1},{2,10},{10,2},{3,11},{11,3},{4,12},{12,4},... | collective-permute-start | bytes 1572872 | tf_op jit(solution)/shard_map/ppermute | solution.py:727
  31.1 5.7 %collective-permute-start.12 = (bf16[64,256]{1,0:T(8,128)(2,1)S(1)}, bf16[64,256]{1,0:T(8,128)(2,1)S(1)}, u32[]{:S(2)}, u32[]{:S(2)}) collective-permute-start(bf16[64,256]{1,0:T(8,128)(2,1)S(1)} %get-tuple-element.83), channel_id=1, source_target_pairs={{0,6},{1,7},{2,4},{3,5},{4,2},{5,3},{6,0},{7,1},{8,12},{9,13},{10,... | collective-permute-start | bytes 98312 | tf_op jit(solution)/shard_map/ppermute | solution.py:723
  34.0 2.8 %collective-permute-start.11 = (bf16[64,256]{1,0:T(8,128)(2,1)S(1)}, bf16[64,256]{1,0:T(8,128)(2,1)S(1)}, u32[]{:S(2)}, u32[]{:S(2)}) collective-permute-start(bf16[64,256]{1,0:T(8,128)(2,1)S(1)} %get-tuple-element.83), channel_id=1, source_target_pairs={{8,10},{9,11},{10,8},{11,9},{12,14},{13,15},{14,12},{15,13},{24,26... | collective-permute-start | bytes 98312 | tf_op jit(solution)/shard_map/ppermute | solution.py:723
  36.8 1.8 %collective-permute-start.13 = (bf16[64,256]{1,0:T(8,128)(2,1)S(1)}, bf16[64,256]{1,0:T(8,128)(2,1)S(1)}, u32[]{:S(2)}, u32[]{:S(2)}) collective-permute-start(bf16[64,256]{1,0:T(8,128)(2,1)S(1)} %add_convert_fusion), channel_id=1, source_target_pairs={{0,8},{8,0},{1,9},{9,1},{2,10},{10,2},{3,11},{11,3},{4,12},{12,4},... | collective-permute-start | bytes 98312 | tf_op jit(solution)/shard_map/ppermute | solution.py:727

commit v21 on v20

--- a/solution.py
+++ b/solution.py
@@ -552,7 +552,6 @@
     normed_ref,
     far_normed_ref,
     other_normed_ref,
-    other_far_normed_ref,
     part_ref,
     spread_ref,
     gf_ref,
@@ -575,13 +574,11 @@
     f32, bf16 = jnp.float32, jnp.bfloat16
     my_half = first_here // pair_cols
     gf_ref[...] = jnp.where(my_half == me_depth, opm_ref[...], other_opm_ref[...]).astype(f32)
-    for y, e, block in (
-        (me_y, me_depth, normed_ref),
-        (1 - me_y, me_depth, far_normed_ref),
-        (me_y, 1 - me_depth, other_normed_ref),
-        (1 - me_y, 1 - me_depth, other_far_normed_ref),
-    ):
-        rows_ref[y, e] = block[...]
+    rows = rows_ref.shape[2]
+    rows_ref[me_y, me_depth] = normed_ref[...]
+    rows_ref[1 - me_y, me_depth] = far_normed_ref[...]
+    rows_ref[me_y, 1 - me_depth] = other_normed_ref[0:rows, :]
+    rows_ref[1 - me_y, 1 - me_depth] = other_normed_ref[rows:, :]
 
     for il in range(here):
         first = pl.multiple_of((first_here + il) * pair_cols, pair_cols)
@@ -850,11 +847,8 @@
         compiler_params=params,
         name="outer_products",
     )(ids, near, far, other_near, other_far, wturn)
-    normed_again, far_again, proj_out = lax.optimization_barrier((normed, far_normed, proj_out))
-    other_normed, other_far_normed = swap_depth(normed_again), swap_depth(far_again)
-    pair_far, proj_out, other_normed, other_far_normed = lax.optimization_barrier(
-        (pair_far, proj_out, other_normed, other_far_normed)
-    )
+    other_normed = swap_depth(jnp.concatenate([normed, far_normed]))
+    pair_far, proj_out, other_normed = lax.optimization_barrier((pair_far, proj_out, other_normed))
     held, opm, pn, gh, hidden, mg = pl.pallas_call(
         functools.partial(transition_kernel, sizes),
         out_shape=(
@@ -899,7 +893,7 @@
             shape((2 * width, channels), bf16),
             shape((seqs * res, 2 * lanes), bf16),
         ),
-        in_specs=[smem] + [vmem] * 11,
+        in_specs=[smem] + [vmem] * 10,
         out_specs=[vmem] * 2,
         scratch_shapes=[
             pltpu.VMEM((half, pair_width), f32),
@@ -924,7 +918,6 @@
         normed,
         far_normed,
         other_normed,
-        other_far_normed,
     )
     feat, couple = pl.pallas_call(
         functools.partial(feature_kernel, res),

time: 39.5 us -> 39.4 us (level)
    ppermute x7 -> x6, starting transfers between devices: 2.07 us -> 1.95 us  [swap_depth(): return lax.ppermute(block, 'depth', [(0, 1), (1, 0)])]
  transfers between devices with their start and end apart: 15 -> 14, of which waited for: 7 -> 6; matrix products, arithmetic and copies ran while one was open for 0% -> 0% of each run, Pallas kernels for 14% -> 14%
where the time goes in v21:
time: 39.4 us; the launch traced here: 39.1 us
  starting transfers between devices  16.6 us (42%)
  Pallas kernels  11.4 us (29%)
  waiting for transfers between devices  9.46 us (24%)
  between operations  0.8 us (2%)
  local copies, waits for them, and re-layouts  0.78 us (2%)
    ppermute x6, starting transfers between devices, swap_col(): lax.ppermute(block, 'col', [(at, at ^ partner) for at in range(count)])  10.8 us
    ppermute x6, waiting for transfers between devices, swap_col(): lax.ppermute(block, 'col', [(at, at ^ partner) for at in range(count)])  8.16 us
    ppermute x2, starting transfers between devices, swap_line(): return lax.ppermute(block, ('depth', 'col'), pairs)  3.83 us
    pallas_call x1, Pallas kernels, whole_plan(): pl.pallas_call(functools.partial(outer_kernel, sizes), out_shape=(shape((...  2.67 us
    pallas_call x1, Pallas kernels, whole_plan(): pl.pallas_call(functools.partial(projector_kernel, sizes), out_shape=(sha...  2.05 us
    ppermute x6, starting transfers between devices, swap_depth(): return lax.ppermute(block, 'depth', [(0, 1), (1, 0)])  1.95 us
    pallas_call x1, Pallas kernels, whole_plan(): pl.pallas_call(pre_kernel, out_shape=(shape((1, rows + 2 * per, pair_widt...  1.91 us
    pallas_call x1, Pallas kernels, whole_plan(): pl.pallas_call(functools.partial(transition_kernel, sizes), out_shape=(sh...  1.82 us
  transfers between devices with their start and end apart: 14, of which 6 were waited for; matrix products, arithmetic and copies ran while one was open for 0% of the time, Pallas kernels for 14%

profile of v21, /device:TPU:0, one launch (start us, length us, event | category | flops | bytes accessed | tf_op | source)
XLA Modules:
  0.0 39.1 jit_solution(18305831443992535806)
XLA Ops:
  0.6 0.1 pad_add_fusion.ids_ref
  0.7 1.9 %project.1 = (bf16[1,272,128]{2,1,0:T(8,128)(2,1)S(1)}, f32[1,256]{1,0:T(1,128)S(1)}, bf16[32,256]{1,0:T(8,128)(2,1)S(1)}, bf16[32,256]{1,0:T(8,128)(2,1)S(1)}, ...) custom-call(s32[2]{0:T(128)S(1)} %pad_add_fusion.ids_ref, ...), custom_call_target="tpu_custom_call" | custom-call | tf_op jit(solution)/shard_map/project/pallas_call | solution.py:775
  2.6 5.1 %collective-permute-start.2 = (bf16[1,272,128]{2,1,0:T(8,128)(2,1)S(1)}, bf16[1,272,128]{2,1,0:T(8,128)(2,1)S(1)}, u32[]{:S(2)}, u32[]{:S(2)}) collective-permute-start(bf16[1,272,128]{2,1,0:T(8,128)(2,1)S(1)} %get-tuple-element.52), channel_id=1, source_target_pairs={{0,6},{1,7},{2,4},{3,5},{4,2},{5,3},{6,0},{7,1},{8,14},{9,15},{10,... | collective-permute-start | bytes 208904 | tf_op jit(solution)/shard_map/ppermute | solution.py:735
  7.7 0.0 collective-permute-start.1
  7.8 0.6 %collective-permute-start = (bf16[1,272,128]{2,1,0:T(8,128)(2,1)S(1)}, bf16[1,272,128]{2,1,0:T(8,128)(2,1)S(1)}, u32[]{:S(2)}, u32[]{:S(2)}) collective-permute-start(bf16[1,272,128]{2,1,0:T(8,128)(2,1)S(1)} %get-tuple-element.52), channel_id=1, source_target_pairs={{0,2},{1,3},{2,0},{3,1},{4,6},{5,7},{6,4},{7,5},{8,10},{9,11},{10,... | collective-permute-start | bytes 208904 | tf_op jit(solution)/shard_map/ppermute | solution.py:735
  8.4 1.7 %collective-permute-start.3 = (bf16[256,256]{1,0:T(8,128)(2,1)S(1)}, bf16[256,256]{1,0:T(8,128)(2,1)S(1)}, u32[]{:S(2)}, u32[]{:S(2)}) collective-permute-start(bf16[256,256]{1,0:T(8,128)(2,1)S(1)} %get-tuple-element.53.normed_ref), channel_id=1, source_target_pairs={{0,1},{1,0},{2,3},{3,2},{4,5},{5,4},{6,7},{7,6},{8,9},{9,8},{10,11... | collective-permute-start | bytes 393224 | tf_op jit(solution)/shard_map/ppermute | solution.py:735
  10.1 0.4 collective-permute-done.2
  10.4 3.2 %collective-permute-done.1 = bf16[1,272,128]{2,1,0:T(8,128)(2,1)S(1)} collective-permute-done((bf16[1,272,128]{2,1,0:T(8,128)(2,1)S(1)}, bf16[1,272,128]{2,1,0:T(8,128)(2,1)S(1)}, u32[]{:S(2)}, u32[]{:S(2)}) %collective-permute-start.1) | collective-permute-done | bytes 69664 | tf_op jit(solution)/shard_map/ppermute | solution.py:735
  13.7 0.0 collective-permute-done
  13.7 0.0 collective-permute-done.3.far_normed_ref
  13.7 1.6 %collective-permute-start.5 = (bf16[4,144,128]{2,1,0:T(8,128)(2,1)S(1)}, bf16[4,144,128]{2,1,0:T(8,128)(2,1)S(1)}, u32[]{:S(2)}, u32[]{:S(2)}) collective-permute-start(bf16[4,144,128]{2,1,0:T(8,128)(2,1)S(1)} %slice.13.near_ref), channel_id=1, source_target_pairs={{0,1},{1,0},{2,3},{3,2},{4,5},{5,4},{6,7},{7,6},{8,9},{9,8},{10,11... | collective-permute-start | bytes 442376 | tf_op jit(solution)/shard_map/ppermute | solution.py:735
  15.3 0.0 copy-start
  15.4 0.1 collective-permute-start.8
  15.4 0.5 %collective-permute-start.6 = (bf16[4,144,128]{2,1,0:T(8,128)(2,1)S(1)}, bf16[4,144,128]{2,1,0:T(8,128)(2,1)S(1)}, u32[]{:S(2)}, u32[]{:S(2)}) collective-permute-start(bf16[4,144,128]{2,1,0:T(8,128)(2,1)S(1)} %slice.13.near_ref), channel_id=1, source_target_pairs={{0,8},{8,0},{1,9},{9,1},{2,10},{10,2},{3,11},{11,3},{4,12},{12,4},... | collective-permute-start | bytes 442376 | tf_op jit(solution)/shard_map/ppermute | solution.py:724
  15.9 3.2 %collective-permute-done.5.far_ref = bf16[4,144,128]{2,1,0:T(8,128)(2,1)S(1)} collective-permute-done((bf16[4,144,128]{2,1,0:T(8,128)(2,1)S(1)}, bf16[4,144,128]{2,1,0:T(8,128)(2,1)S(1)}, u32[]{:S(2)}, u32[]{:S(2)}) %collective-permute-start.5) | collective-permute-done | bytes 147488 | tf_op jit(solution)/shard_map/ppermute | solution.py:735
  19.1 0.0 collective-permute-start.7
  19.2 1.8 %collective-permute-start.4 = (bf16[4,128,128]{2,1,0:T(8,128)(2,1)S(1)}, bf16[4,128,128]{2,1,0:T(8,128)(2,1)S(1)}, u32[]{:S(2)}, u32[]{:S(2)}) collective-permute-start(bf16[4,128,128]{2,1,0:T(8,128)(2,1)S(1)} %slice.12.near_ref), channel_id=1, source_target_pairs={{0,1},{1,0},{2,3},{3,2},{4,5},{5,4},{6,7},{7,6},{8,9},{9,8},{10,11... | collective-permute-start | bytes 393224 | tf_op jit(solution)/shard_map/ppermute | solution.py:735
  21.0 0.0 copy-done
  21.0 0.1 copy.19
  21.1 0.0 collective-permute-done.6.other_near_ref
  21.1 0.0 collective-permute-done.7.other_far_ref
  21.1 0.0 copy-start.1
  21.1 0.0 copy-start.2
  21.1 2.7 %outer_products.1 = (bf16[512,1024]{1,0:T(8,128)(2,1)S(1)}, f32[512,128]{1,0:T(8,128)S(1)}, f32[512,128]{1,0:T(8,128)S(1)}, bf16[512,128]{1,0:T(8,128)(2,1)S(1)}...) custom-call(s32[2]{0:T(128)S(1)} %pad_add_fusion.ids_ref, ...), custom_call_target="tpu_custom_call" | custom-call | tf_op jit(solution)/shard_map/outer_products/pallas_call | solution.py:826
  23.8 1.3 %collective-permute-done.4.far_ref = bf16[4,128,128]{2,1,0:T(8,128)(2,1)S(1)} collective-permute-done((bf16[4,128,128]{2,1,0:T(8,128)(2,1)S(1)}, bf16[4,128,128]{2,1,0:T(8,128)(2,1)S(1)}, u32[]{:S(2)}, u32[]{:S(2)}) %collective-permute-start.4) | collective-permute-done | bytes 131104 | tf_op jit(solution)/shard_map/ppermute | solution.py:735
  25.1 0.0 collective-permute-done.8.other_normed_ref
  25.1 0.0 copy-done.1
  25.1 0.0 copy-done.2
  25.1 1.8 %transition.1 = (bf16[64,128]{1,0:T(8,128)(2,1)S(1)}, bf16[512,128]{1,0:T(8,128)(2,1)S(1)}, bf16[512,128]{1,0:T(8,128)(2,1)S(1)}, bf16[512,512]{1,0:T(8,128)(2,1...) custom-call(s32[2]{0:T(128)S(1)} %pad_add_fusion.ids_ref, bf16[4,128,128]{2,1,0:T(8,128)(2,1)S(1)} %slice.12.near_ref, ...), custom_call_target="tpu_custom_call" | custom-call | tf_op jit(solution)/shard_map/transition/pallas_call | solution.py:852
  27.0 0.1 collective-permute-start.9
  27.0 0.9 %weight_gradients.1.mine_ref = bf16[2048,128]{1,0:T(8,128)(2,1)S(1)} custom-call(bf16[512,1024]{1,0:T(8,128)(2,1)S(1)} %get-tuple-element.63.outer_ref, bf16[512,128]{1,0:T(8,128)(2,1)S(1)} %get-tuple-element.62.opm_ref, bf16[512,128]{1,0:T(8,128)(2,1)S(1)} %get-tuple-element.64.pn_ref, bf16[512,512]{1,0:T(8,128)(2,1)S(1)} %get-tuple-element.65.gh_ref, ...), custom_call_target="tpu_custom_call" | custom-call | tf_op jit(solution)/shard_map/weight_gradients/pallas_call | solution.py:880
  28.0 0.4 %collective-permute-done.9.other_opm_ref = bf16[512,128]{1,0:T(8,128)(2,1)S(1)} collective-permute-done((bf16[512,128]{1,0:T(8,128)(2,1)S(1)}, bf16[512,128]{1,0:T(8,128)(2,1)S(1)}, u32[]{:S(2)}, u32[]{:S(2)}) %collective-permute-start.9) | collective-permute-done | bytes 131104 | tf_op jit(solution)/shard_map/ppermute | solution.py:724
  28.4 2.0 %projector_parts.1 = (bf16[64,256]{1,0:T(8,128)(2,1)S(1)}, bf16[256,256]{1,0:T(8,128)(2,1)S(1)}) custom-call(s32[2]{0:T(128)S(1)} %pad_add_fusion.ids_ref, bf16[512,128]{1,0:T(8,128)(2,1)S(1)} %get-tuple-element.62.opm_ref, bf16[512,128]{1,0:T(8,128)(2,1)S(1)} %collective-permute-done.9.other_opm_ref, bf16[1024,128]{1,0:T(8,128)(2,1)S(1)} %get-tuple-element.69.rightt_ref, ...), custom_call_target="tpu_custom_call" | custom-call | tf_op jit(solution)/shard_map/projector_parts/pallas_call | solution.py:890
  30.4 0.2 collective-permute-start.13
  30.6 3.2 %collective-permute-start.11 = (bf16[64,256]{1,0:T(8,128)(2,1)S(1)}, bf16[64,256]{1,0:T(8,128)(2,1)S(1)}, u32[]{:S(2)}, u32[]{:S(2)}) collective-permute-start(bf16[64,256]{1,0:T(8,128)(2,1)S(1)} %get-tuple-element.75), channel_id=1, source_target_pairs={{0,6},{1,7},{2,4},{3,5},{4,2},{5,3},{6,0},{7,1},{8,12},{9,13},{10,... | collective-permute-start | bytes 98312 | tf_op jit(solution)/shard_map/ppermute | solution.py:720
  33.8 0.7 %collective-permute-start.10 = (bf16[64,256]{1,0:T(8,128)(2,1)S(1)}, bf16[64,256]{1,0:T(8,128)(2,1)S(1)}, u32[]{:S(2)}, u32[]{:S(2)}) collective-permute-start(bf16[64,256]{1,0:T(8,128)(2,1)S(1)} %get-tuple-element.75), channel_id=1, source_target_pairs={{8,10},{9,11},{10,8},{11,9},{12,14},{13,15},{14,12},{15,13},{24,26... | collective-permute-start | bytes 98312 | tf_op jit(solution)/shard_map/ppermute | solution.py:720
  34.5 1.0 %features.1 = (bf16[64,4,256]{2,1,0:T(4,128)(2,1)}, bf16[64,128]{1,0:T(8,128)(2,1)}) custom-call(bf16[256,256]{1,0:T(8,128)(2,1)S(1)} %get-tuple-element.76.spread_ref, bf16[32,256]{1,0:T(8,128)(2,1)S(1)} %get-tuple-element.77.first_ref, bf16[32,256]{1,0:T(8,128)(2,1)S(1)} %get-tuple-element.78.second_ref, f32[1,256]{1,0:T(1,128)S(1)} %get-tuple-element.79.scale_ref, ...), custom_call_target="tpu_custom_call" | custom-call | tf_op jit(solution)/shard_map/features/pallas_call | solution.py:922
  35.5 0.9 %collective-permute-done.11 = bf16[64,256]{1,0:T(8,128)(2,1)S(1)} collective-permute-done((bf16[64,256]{1,0:T(8,128)(2,1)S(1)}, bf16[64,256]{1,0:T(8,128)(2,1)S(1)}, u32[]{:S(2)}, u32[]{:S(2)}) %collective-permute-start.11) | collective-permute-done | bytes 32800 | tf_op jit(solution)/shard_map/ppermute | solution.py:720
  36.4 0.0 collective-permute-done.10
  36.4 1.1 %collective-permute-start.12 = (bf16[64,256]{1,0:T(8,128)(2,1)S(1)}, bf16[64,256]{1,0:T(8,128)(2,1)S(1)}, u32[]{:S(2)}, u32[]{:S(2)}) collective-permute-start(bf16[64,256]{1,0:T(8,128)(2,1)S(1)} %add_convert_fusion), channel_id=1, source_target_pairs={{0,8},{8,0},{1,9},{9,1},{2,10},{10,2},{3,11},{11,3},{4,12},{12,4},... | collective-permute-start | bytes 98312 | tf_op jit(solution)/shard_map/ppermute | solution.py:724
  37.5 0.0 collective-permute-done.13.other_ref
  37.5 1.0 %sums_over_depth.1 = (f32[1024,128]{1,0:T(8,128)}, f32[128,512]{1,0:T(8,128)}, f32[512,128]{1,0:T(8,128)}) custom-call(bf16[2048,128]{1,0:T(8,128)(2,1)S(1)} %weight_gradients.1.mine_ref, bf16[2048,128]{1,0:T(8,128)(2,1)S(1)} %collective-permute-done.13.other_ref), custom_call_target="tpu_custom_call" | custom-call | tf_op jit(solution)/shard_map/sums_over_depth/pallas_call | solution.py:931
  38.5 0.0 collective-permute-done.12
  38.5 0.6 %slice_bitcast_fusion = (f32[256,32]{0,1:T(8,128)}, f32[256,32]{0,1:T(8,128)}) fusion(f32[64,256]{1,0:T(8,128)S(1)} %convert_add_fusion), kind=kLoop, calls=%fused_computation.4 | loop fusion | bytes 131072 | tf_op jit(solution)/shard_map/transpose | solution.py:955
  (6 shorter events, 0.1 us)
Async XLA Ops:
  2.6 7.8 %collective-permute-start.2 = (bf16[1,272,128]{2,1,0:T(8,128)(2,1)S(1)}, bf16[1,272,128]{2,1,0:T(8,128)(2,1)S(1)}, u32[]{:S(2)}, u32[]{:S(2)}) collective-permute-start(bf16[1,272,128]{2,1,0:T(8,128)(2,1)S(1)} %get-tuple-element.52), channel_id=1, source_target_pairs={{0,6},{1,7},{2,4},{3,5},{4,2},{5,3},{6,0},{7,1},{8,14},{9,15},{10,... | collective-permute-start | bytes 208904 | tf_op jit(solution)/shard_map/ppermute | solution.py:735
  7.7 5.9 %collective-permute-start.1 = (bf16[1,272,128]{2,1,0:T(8,128)(2,1)S(1)}, bf16[1,272,128]{2,1,0:T(8,128)(2,1)S(1)}, u32[]{:S(2)}, u32[]{:S(2)}) collective-permute-start(bf16[1,272,128]{2,1,0:T(8,128)(2,1)S(1)} %get-tuple-element.52), channel_id=1, source_target_pairs={{0,4},{1,5},{2,6},{3,7},{4,0},{5,1},{6,2},{7,3},{8,12},{9,13},{10,... | collective-permute-start | bytes 208904 | tf_op jit(solution)/shard_map/ppermute | solution.py:735
  7.8 5.9 %collective-permute-start = (bf16[1,272,128]{2,1,0:T(8,128)(2,1)S(1)}, bf16[1,272,128]{2,1,0:T(8,128)(2,1)S(1)}, u32[]{:S(2)}, u32[]{:S(2)}) collective-permute-start(bf16[1,272,128]{2,1,0:T(8,128)(2,1)S(1)} %get-tuple-element.52), channel_id=1, source_target_pairs={{0,2},{1,3},{2,0},{3,1},{4,6},{5,7},{6,4},{7,5},{8,10},{9,11},{10,... | collective-permute-start | bytes 208904 | tf_op jit(solution)/shard_map/ppermute | solution.py:735
  8.4 5.3 %collective-permute-start.3 = (bf16[256,256]{1,0:T(8,128)(2,1)S(1)}, bf16[256,256]{1,0:T(8,128)(2,1)S(1)}, u32[]{:S(2)}, u32[]{:S(2)}) collective-permute-start(bf16[256,256]{1,0:T(8,128)(2,1)S(1)} %get-tuple-element.53.normed_ref), channel_id=1, source_target_pairs={{0,1},{1,0},{2,3},{3,2},{4,5},{5,4},{6,7},{7,6},{8,9},{9,8},{10,11... | collective-permute-start | bytes 393224 | tf_op jit(solution)/shard_map/ppermute | solution.py:735
  13.7 5.4 %collective-permute-start.5 = (bf16[4,144,128]{2,1,0:T(8,128)(2,1)S(1)}, bf16[4,144,128]{2,1,0:T(8,128)(2,1)S(1)}, u32[]{:S(2)}, u32[]{:S(2)}) collective-permute-start(bf16[4,144,128]{2,1,0:T(8,128)(2,1)S(1)} %slice.13.near_ref), channel_id=1, source_target_pairs={{0,1},{1,0},{2,3},{3,2},{4,5},{5,4},{6,7},{7,6},{8,9},{9,8},{10,11... | collective-permute-start | bytes 442376 | tf_op jit(solution)/shard_map/ppermute | solution.py:735
  15.3 5.6 %copy-start = (bf16[1024,128]{1,0:T(8,128)(2,1)S(1)}, bf16[1024,128]{1,0:T(8,128)(2,1)}, u32[]{:S(2)}) copy-start(bf16[1024,128]{1,0:T(8,128)(2,1)} %wout_ref.1) | copy-start | bytes 786436
  15.4 9.8 %collective-permute-start.8 = (bf16[512,256]{1,0:T(8,128)(2,1)S(1)}, bf16[512,256]{1,0:T(8,128)(2,1)S(1)}, u32[]{:S(2)}, u32[]{:S(2)}) collective-permute-start(bf16[512,256]{1,0:T(8,128)(2,1)S(1)} %pad_maximum_fusion.1), channel_id=1, source_target_pairs={{0,8},{8,0},{1,9},{9,1},{2,10},{10,2},{3,11},{11,3},{4,12},{12,4},... | collective-permute-start | bytes 786440 | tf_op jit(solution)/shard_map/ppermute | solution.py:724
  15.4 5.6 %collective-permute-start.6 = (bf16[4,144,128]{2,1,0:T(8,128)(2,1)S(1)}, bf16[4,144,128]{2,1,0:T(8,128)(2,1)S(1)}, u32[]{:S(2)}, u32[]{:S(2)}) collective-permute-start(bf16[4,144,128]{2,1,0:T(8,128)(2,1)S(1)} %slice.13.near_ref), channel_id=1, source_target_pairs={{0,8},{8,0},{1,9},{9,1},{2,10},{10,2},{3,11},{11,3},{4,12},{12,4},... | collective-permute-start | bytes 442376 | tf_op jit(solution)/shard_map/ppermute | solution.py:724
  19.1 1.9 %collective-permute-start.7 = (bf16[4,144,128]{2,1,0:T(8,128)(2,1)S(1)}, bf16[4,144,128]{2,1,0:T(8,128)(2,1)S(1)}, u32[]{:S(2)}, u32[]{:S(2)}) collective-permute-start(bf16[4,144,128]{2,1,0:T(8,128)(2,1)S(1)} %collective-permute-done.5.far_ref), channel_id=1, source_target_pairs={{0,8},{8,0},{1,9},{9,1},{2,10},{10,2},{3,11},{11,3},{4,12},{12,4},... | collective-permute-start | bytes 442376 | tf_op jit(solution)/shard_map/ppermute | solution.py:724
  19.2 6.0 %collective-permute-start.4 = (bf16[4,128,128]{2,1,0:T(8,128)(2,1)S(1)}, bf16[4,128,128]{2,1,0:T(8,128)(2,1)S(1)}, u32[]{:S(2)}, u32[]{:S(2)}) collective-permute-start(bf16[4,128,128]{2,1,0:T(8,128)(2,1)S(1)} %slice.12.near_ref), channel_id=1, source_target_pairs={{0,1},{1,0},{2,3},{3,2},{4,5},{5,4},{6,7},{7,6},{8,9},{9,8},{10,11... | collective-permute-start | bytes 393224 | tf_op jit(solution)/shard_map/ppermute | solution.py:735
  21.1 4.0 %copy-start.1 = (bf16[128,512]{1,0:T(8,128)(2,1)S(1)}, bf16[128,512]{1,0:T(8,128)(2,1)}, u32[]{:S(2)}) copy-start(bf16[128,512]{1,0:T(8,128)(2,1)} %hid_ref.1) | copy-start | bytes 393220
  21.1 4.0 %copy-start.2 = (bf16[512,128]{1,0:T(8,128)(2,1)S(1)}, bf16[512,128]{1,0:T(8,128)(2,1)}, u32[]{:S(2)}) copy-start(bf16[512,128]{1,0:T(8,128)(2,1)} %back_ref.1) | copy-start | bytes 393220
  27.0 1.4 %collective-permute-start.9 = (bf16[512,128]{1,0:T(8,128)(2,1)S(1)}, bf16[512,128]{1,0:T(8,128)(2,1)S(1)}, u32[]{:S(2)}, u32[]{:S(2)}) collective-permute-start(bf16[512,128]{1,0:T(8,128)(2,1)S(1)} %get-tuple-element.62.opm_ref), channel_id=1, source_target_pairs={{0,8},{8,0},{1,9},{9,1},{2,10},{10,2},{3,11},{11,3},{4,12},{12,4},... | collective-permute-start | bytes 393224 | tf_op jit(solution)/shard_map/ppermute | solution.py:724
  30.4 7.0 %collective-permute-start.13 = (bf16[2048,128]{1,0:T(8,128)(2,1)S(1)}, bf16[2048,128]{1,0:T(8,128)(2,1)S(1)}, u32[]{:S(2)}, u32[]{:S(2)}) collective-permute-start(bf16[2048,128]{1,0:T(8,128)(2,1)S(1)} %weight_gradients.1.mine_ref), channel_id=1, source_target_pairs={{0,8},{8,0},{1,9},{9,1},{2,10},{10,2},{3,11},{11,3},{4,12},{12,4},... | collective-permute-start | bytes 1572872 | tf_op jit(solution)/shard_map/ppermute | solution.py:724
  30.6 5.7 %collective-permute-start.11 = (bf16[64,256]{1,0:T(8,128)(2,1)S(1)}, bf16[64,256]{1,0:T(8,128)(2,1)S(1)}, u32[]{:S(2)}, u32[]{:S(2)}) collective-permute-start(bf16[64,256]{1,0:T(8,128)(2,1)S(1)} %get-tuple-element.75), channel_id=1, source_target_pairs={{0,6},{1,7},{2,4},{3,5},{4,2},{5,3},{6,0},{7,1},{8,12},{9,13},{10,... | collective-permute-start | bytes 98312 | tf_op jit(solution)/shard_map/ppermute | solution.py:720
  33.8 2.5 %collective-permute-start.10 = (bf16[64,256]{1,0:T(8,128)(2,1)S(1)}, bf16[64,256]{1,0:T(8,128)(2,1)S(1)}, u32[]{:S(2)}, u32[]{:S(2)}) collective-permute-start(bf16[64,256]{1,0:T(8,128)(2,1)S(1)} %get-tuple-element.75), channel_id=1, source_target_pairs={{8,10},{9,11},{10,8},{11,9},{12,14},{13,15},{14,12},{15,13},{24,26... | collective-permute-start | bytes 98312 | tf_op jit(solution)/shard_map/ppermute | solution.py:720
  36.4 2.1 %collective-permute-start.12 = (bf16[64,256]{1,0:T(8,128)(2,1)S(1)}, bf16[64,256]{1,0:T(8,128)(2,1)S(1)}, u32[]{:S(2)}, u32[]{:S(2)}) collective-permute-start(bf16[64,256]{1,0:T(8,128)(2,1)S(1)} %add_convert_fusion), channel_id=1, source_target_pairs={{0,8},{8,0},{1,9},{9,1},{2,10},{10,2},{3,11},{11,3},{4,12},{12,4},... | collective-permute-start | bytes 98312 | tf_op jit(solution)/shard_map/ppermute | solution.py:724
